TPU v7x, 32 devices: a whole 2x2x4 slice. The times are simulated.
32 devices in a mesh: blk: 8 (over z, y), rows: 4 (over x, core).
Axes of the slice: x: 2, y: 2, z: 4, core: 2. Of those that a mesh axis runs over, the one named last changes fastest.
Arguments:
- fine_blocks: bfloat16 [4, 8, 8, 8, 128, 128], P('rows', 'blk'), may hold values from -0.5 to 0.5
- block_rows: int32 [4, 8, 8, 8], P('rows', 'blk'), may hold values from 0 to 15
- block_cols: int32 [4, 8, 8, 8], P('rows', 'blk'), may hold values from 0 to 15
- block_counts: int32 [4, 8, 8], P('rows', 'blk'), may hold values from 1 to 8, 36 in all within a row
- prolong_blocks: bfloat16 [4, 128, 128, 384], P('rows', 'blk'), may hold values from -1.1953125 to 1.1953125
- prolong_mask: int32 [4, 128, 3], P('rows', 'blk'), may hold values 0 or 1
Outputs:
- coarse_blocks: float32 [4, 8, 128, 8, 5, 128], P('rows', 'blk')
Inputs may be any that keep to these rules, and one draw needn't show every extreme that they name: `block_counts`: the 8 counts of one device sum to 36, and one of them is 8.
All inputs are finite; a program needn't handle non-finite values. No bound on the sum of `prolong_mask` on one device may be relied on, other than what follows from the above.
Results may differ from a plain program's by a relative error of at most 0.004.
Values may be sent and summed in bfloat16 or wider, within the bound.
No kernel may reach another device: no remote copies, remote signals or barrier semaphores. Data moves between devices by JAX's collectives and lax.ppermute only.
A program may use at most 128 MiB of HBM per device.

v0:
```python
import jax
import jax.numpy as jnp
from jax import lax
from jax.sharding import PartitionSpec as P


def padded_2(array, sides, width):
    for axis, dim in sides:
        size, length = (lax.axis_size(axis), array.shape[dim])
        up = [(i, (i + 1) % size) for i in range(size - 1)]
        down = [(j, i) for i, j in up]
        last = lax.slice_in_dim(array, length - width, length, axis=dim)
        initial = lax.slice_in_dim(array, 0, width, axis=dim)
        before = lax.ppermute(last, axis, up)
        after = lax.ppermute(initial, axis, down)
        array = jnp.concatenate([before, array, after], axis=dim)
    return array


def per_device(fine_blocks, block_rows, block_cols, block_counts, prolong_blocks, prolong_mask):
    matrix = fine_blocks[0, 0]
    slot_rows = block_rows[0, 0]
    slot_cols = block_cols[0, 0]
    slot_counts = block_counts[0, 0]
    prolong = prolong_blocks[0]
    pattern = prolong_mask[0]
    shard_rows, pore_count, prolong_width = prolong.shape
    coarse_width = prolong_width // 3
    slot_total = matrix.shape[1]
    panels = lax.axis_size("blk")
    groups = lax.axis_size("rows")
    group_index = lax.axis_index("rows")
    offsets = group_index + jnp.arange(3, dtype=jnp.int32) - 1
    keeper = (pattern == 1) & (offsets[None, :] >= 0) & (offsets[None, :] < groups)
    masked = (
        prolong.reshape(shard_rows, pore_count, 3, coarse_width)
        * keeper[:, None, :, None].astype(jnp.bfloat16)
    ).reshape(shard_rows, pore_count, prolong_width)
    row_ids = jnp.arange(shard_rows, dtype=jnp.int32)
    slot_ids = jnp.arange(slot_total, dtype=jnp.int32)

    def row_products(peer_index, panel_rows):
        local_block_list = lax.dynamic_index_in_dim(matrix, peer_index, 0, keepdims=False)
        rows_here = lax.dynamic_index_in_dim(slot_rows, peer_index, 0, keepdims=False)
        cols_here = lax.dynamic_index_in_dim(slot_cols, peer_index, 0, keepdims=False)
        count_here = lax.dynamic_index_in_dim(slot_counts, peer_index, 0, keepdims=False)
        chosen_entries = jnp.take(panel_rows, cols_here, axis=0)
        block_products = jnp.einsum(
            "wju,wul->wjl", local_block_list, chosen_entries, preferred_element_type=jnp.float32
        )
        selector_mask = (
            (rows_here[:, None] == row_ids[None, :]) & (slot_ids < count_here)[:, None]
        ).astype(jnp.float32)
        reduced_sums = jnp.einsum(
            "pr,pwy->rwy", selector_mask, block_products, precision=lax.Precision.HIGHEST
        )
        return reduced_sums.astype(jnp.bfloat16)

    def store_slab(current, slab, peer_index):
        return lax.dynamic_update_index_in_dim(current, slab, peer_index, 0)

    start_rows = jnp.zeros((panels, shard_rows, pore_count, prolong_width), jnp.bfloat16)
    panel_rows = lax.all_gather(masked, "blk", axis=0, tiled=True)
    shard_total = panel_rows.shape[0] // shard_rows

    def one_shard(shard_step, current):
        present_row_count = lax.dynamic_slice_in_dim(
            panel_rows, shard_step * shard_rows, shard_rows, 0
        )
        return store_slab(current, row_products(shard_step, present_row_count), shard_step)

    collected = lax.fori_loop(0, shard_total, one_shard, start_rows)
    partial_value = jnp.einsum(
        "ixe,pixf->epf", masked, collected, preferred_element_type=jnp.float32
    )
    shares = partial_value.astype(jnp.bfloat16).reshape(3, coarse_width, panels, 3, coarse_width)
    padded = padded_2(shares, (("rows", 0),), 1)
    own_part = padded[2].astype(jnp.float32)
    from_lower = padded[0].astype(jnp.float32)
    from_upper = padded[4].astype(jnp.float32)
    coarse = jnp.pad(own_part, ((0, 0), (0, 0), (1, 1), (0, 0)))
    coarse = coarse + jnp.pad(from_lower, ((0, 0), (0, 0), (0, 2), (0, 0)))
    coarse = coarse + jnp.pad(from_upper, ((0, 0), (0, 0), (2, 0), (0, 0)))
    return coarse[None, None]


def solution(mesh):
    in_specs = (
        P("rows", "blk", None, None, None, None),
        P("rows", "blk", None, None),
        P("rows", "blk", None, None),
        P("rows", "blk", None),
        P("rows", "blk", None, None),
        P("rows", "blk", None),
    )
    out_specs = P("rows", "blk", None, None, None, None)
    return jax.shard_map(
        per_device, mesh=mesh, in_specs=in_specs, out_specs=out_specs, check_vma=False
    )
```

profile of v0, /device:TPU:1, one launch (start us, length us, event | category | flops | bytes accessed | tf_op | source)
XLA Modules:
  0.0 322.5 jit_solution(2868464447715926716)
XLA Ops:
  7.5 2.7 bitcast_multiply_fusion
  10.3 178.3 %all-gather.2.cloned.1.call-done = bf16[128,128,384]{2,1,0:T(8,128)(2,1)} async-done(((bf16[16,128,384]{2,1,0:T(8,128)(2,1)}), bf16[128,128,384]{2,1,0:T(8,128)(2,1)}) %all-gather.2.cloned.1.call-update) | async-done | bytes 12582928 | tf_op jit(solution)/shard_map/all_gather | solution.py:63
  188.5 94.5 %while.14 = (s32[]{:T(128)}, bf16[8,16,128,384]{2,3,1,0:T(8,128)(2,1)}, s32[8,8]{1,0:T(8,128)}, s32[8]{0:T(128)S(1)}, bf16[8,8,128,128]{3,2,1,0:T(8,128)(2,1)}, ...) while((s32[]{:T(128)}, ...), condition=%wide.region_1.2_spmd.clone, body=%wide.region_0.1_spmd.clone.sunk | while | flops 177341792 | bytes 16782812 | solution.py:72
  188.5 1.6 constant_dynamic-slice_fusion.4
  190.8 0.7 gather_fusion
  192.3 1.4 fusion.43
  195.7 2.2 fusion.45
  197.9 1.2 copy.41
  199.1 1.3 constant_dynamic-update-slice_fusion.2
  200.4 1.6 constant_dynamic-slice_fusion.4
  202.7 0.7 gather_fusion
  203.4 0.7 compare_and_fusion.2
  204.1 1.4 fusion.43
  207.5 2.2 fusion.45
  209.7 1.2 copy.41
  210.9 1.3 constant_dynamic-update-slice_fusion.2
  212.2 1.6 constant_dynamic-slice_fusion.4
  214.5 0.7 gather_fusion
  215.2 0.7 compare_and_fusion.2
  215.9 1.4 fusion.43
  219.3 2.2 fusion.45
  221.5 1.2 copy.41
  222.7 1.3 constant_dynamic-update-slice_fusion.2
  223.9 1.6 constant_dynamic-slice_fusion.4
  226.2 0.7 gather_fusion
  227.0 0.7 compare_and_fusion.2
  227.7 1.4 fusion.43
  231.1 2.2 fusion.45
  233.3 1.2 copy.41
  234.5 1.3 constant_dynamic-update-slice_fusion.2
  235.8 1.6 constant_dynamic-slice_fusion.4
  238.1 0.7 gather_fusion
  239.5 1.4 fusion.43
  243.0 2.2 fusion.45
  245.1 1.2 copy.41
  246.3 1.3 constant_dynamic-update-slice_fusion.2
  247.6 1.6 constant_dynamic-slice_fusion.4
  249.9 0.7 gather_fusion
  250.6 0.7 compare_and_fusion.2
  251.3 1.4 fusion.43
  254.8 2.2 fusion.45
  256.9 1.2 copy.41
  258.1 1.3 constant_dynamic-update-slice_fusion.2
  259.4 1.6 constant_dynamic-slice_fusion.4
  261.7 0.7 gather_fusion
  262.4 0.7 compare_and_fusion.2
  263.1 1.4 fusion.43
  266.5 2.2 fusion.45
  268.7 1.2 copy.41
  269.9 1.3 constant_dynamic-update-slice_fusion.2
  271.2 1.6 constant_dynamic-slice_fusion.4
  273.5 0.7 gather_fusion
  275.0 1.4 fusion.43
  278.4 2.2 fusion.45
  280.6 1.2 copy.41
  281.8 1.3 constant_dynamic-update-slice_fusion.2
  283.1 10.1 %bitcast_convert_fusion = bf16[384,8,384]{0,2,1:T(8,128)(2,1)S(1)} fusion(bf16[8,16,128,384]{2,3,1,0:T(8,128)(2,1)} %get-tuple-element.159, bf16[16,128,384]{2,1,0:T(8,128)(2,1)} %bitcast_multiply_fusion), kind=kOutput, calls=%fused_computation.30 | convolution fusion | flops 4833017856 | bytes 16515072 | tf_op jit(solution)/shard_map/ixe,pixf->epf/dot_general | solution.py:73
  293.8 1.3 copy.21
  295.1 4.1 %collective-permute-start = (bf16[1,128,8,3,128]{4,2,3,1,0:T(8,128)(2,1)}, bf16[1,128,8,3,128]{4,2,3,1,0:T(8,128)(2,1)S(1)}, u32[]{:S(2)}, u32[]{:S(2)}) collective-permute-start(bf16[1,128,8,3,128]{4,2,3,1,0:T(8,128)(2,1)} %copy.21), channel_id=1, source_target_pairs={{0,1},{1,2},{2,3},{4,5},{5,6},{6,7},{8,9},{9,10},{10,11},{12,13},{... | collective-permute-start | bytes 2359304 | tf_op jit(solution)/shard_map/ppermute | solution.py:14
  299.1 1.3 copy.22
  300.4 1.9 collective-permute-start.1
  302.8 5.6 %collective-permute-done = bf16[1,128,8,3,128]{4,2,3,1,0:T(8,128)(2,1)S(1)} collective-permute-done((bf16[1,128,8,3,128]{4,2,3,1,0:T(8,128)(2,1)}, bf16[1,128,8,3,128]{4,2,3,1,0:T(8,128)(2,1)S(1)}, u32[]{:S(2)}, u32[]{:S(2)}) %collective-permute-start) | collective-permute-done | bytes 786464 | tf_op jit(solution)/shard_map/ppermute | solution.py:14
  308.4 5.5 %collective-permute-done.1 = bf16[1,128,8,3,128]{4,2,3,1,0:T(8,128)(2,1)S(1)} collective-permute-done((bf16[1,128,8,3,128]{4,2,3,1,0:T(8,128)(2,1)}, bf16[1,128,8,3,128]{4,2,3,1,0:T(8,128)(2,1)S(1)}, u32[]{:S(2)}, u32[]{:S(2)}) %collective-permute-start.1) | collective-permute-done | bytes 786464 | tf_op jit(solution)/shard_map/ppermute | solution.py:15
  313.9 1.7 add_bitcast_fusion
  (56 shorter events, 26.1 us)
Async XLA Ops:
  6.5 182.0 %all-gather.2.cloned.1.call-start = ((), (), s32[]{:S(2)}) async-start(), calls=%async_computation | async-start | bytes 14155776 | tf_op jit(solution)/shard_map/all_gather | solution.py:63
  7.5 181.0 %copy-start = (s32[1,1,8]{2,1,0:T(1,128)S(1)}, s32[1,1,8]{2,1,0:T(1,128)}, u32[]{:S(2)}) copy-start(s32[1,1,8]{2,1,0:T(1,128)} %param.11) | copy-start | bytes 100
  295.1 13.3 %collective-permute-start = (bf16[1,128,8,3,128]{4,2,3,1,0:T(8,128)(2,1)}, bf16[1,128,8,3,128]{4,2,3,1,0:T(8,128)(2,1)S(1)}, u32[]{:S(2)}, u32[]{:S(2)}) collective-permute-start(bf16[1,128,8,3,128]{4,2,3,1,0:T(8,128)(2,1)} %copy.21), channel_id=1, source_target_pairs={{0,1},{1,2},{2,3},{4,5},{5,6},{6,7},{8,9},{9,10},{10,11},{12,13},{... | collective-permute-start | bytes 2359304 | tf_op jit(solution)/shard_map/ppermute | solution.py:14
  300.4 13.5 %collective-permute-start.1 = (bf16[1,128,8,3,128]{4,2,3,1,0:T(8,128)(2,1)}, bf16[1,128,8,3,128]{4,2,3,1,0:T(8,128)(2,1)S(1)}, u32[]{:S(2)}, u32[]{:S(2)}) collective-permute-start(bf16[1,128,8,3,128]{4,2,3,1,0:T(8,128)(2,1)} %copy.22), channel_id=1, source_target_pairs={{1,0},{2,1},{3,2},{5,4},{6,5},{7,6},{9,8},{10,9},{11,10},{13,12},{... | collective-permute-start | bytes 2359304 | tf_op jit(solution)/shard_map/ppermute | solution.py:15
Sparse Core Ops, SparseCore 0:
  10.4 178.0 all-gather.1
where the time goes:
time: 324 us; the launch traced here: 322 us
  waiting for transfers between devices  189 us (58%)
  local copies, waits for them, and re-layouts  52.7 us (16%)
  matrix products  38.6 us (12%)
  other arithmetic  22 us (7%)
  between operations  13.5 us (4%)
  starting transfers between devices  5.97 us (2%)
    all_gather x1, waiting for transfers between devices, per_device(): panel_rows = lax.all_gather(masked, 'blk', axis=0, tiled=True)  178 us
    dynamic_update_slice x16, local copies, waits for them, and re-layouts, store_slab(): return lax.dynamic_update_index_in_dim(current, slab, peer_index, 0)  19.6 us
    dot_general x8, matrix products, row_products(): jnp.einsum('pr,pwy->rwy', selector_mask, block_products, precision=lax.Pr...  17.4 us
    dynamic_slice x8, local copies, waits for them, and re-layouts, one_shard(): lax.dynamic_slice_in_dim(panel_rows, shard_step * shard_rows, shard_rows, 0)  12.7 us
    dot_general x8, matrix products, row_products(): jnp.einsum('wju,wul->wjl', local_block_list, chosen_entries, preferred_el...  11.1 us
    dot_general x1, matrix products, per_device(): jnp.einsum('ixe,pixf->epf', masked, collected, preferred_element_type=jnp...  10.1 us
  transfers between devices with their start and end apart: 3, of which 3 were waited for; matrix products, arithmetic and copies ran while one was open for 1% of the time, Pallas kernels for 0%

commit v1 on v0

v1 whole, which is shorter than its diff:
```python
import functools
import jax
import jax.numpy as jnp
from jax import lax
from jax.experimental import pallas as pl
from jax.experimental.pallas import tpu as pltpu
from jax.sharding import PartitionSpec as P

VMEM_LIMIT = 28 * 1024 * 1024


def grid_of(panels):
    columns = max(d for d in range(1, panels + 1) if panels % d == 0 and d * d <= panels)
    return panels // columns, columns


def pack_kernel(info, mask, prolong, head, tail, turned):
    step = pl.program_id(0)
    group, groups, turn = info[0], info[1], info[2]
    rows = prolong.shape[0]
    width = head.shape[-1]
    for i in range(rows):
        row = step * rows + i
        blocks = []
        for e in range(3):
            candidate = group + e - 1
            keep = (mask[3 * row + e] == 1) & (candidate >= 0) & (candidate < groups)
            block = prolong[i, :, e * width:(e + 1) * width]
            blocks.append(block * jnp.where(keep, 1.0, 0.0).astype(block.dtype))
        packed = [jnp.where(turn == 1, blocks[(k + 1) % 3], blocks[k]) for k in range(3)]
        head[i, 0] = packed[0]
        head[i, 1] = packed[1]
        tail[i] = packed[2]
        for k in range(3):
            turned[i, k * width:(k + 1) * width, :] = packed[k].T


def pack(info, mask, prolong):
    rows, pores, width3 = prolong.shape
    width = width3 // 3
    step = 4 if rows % 4 == 0 else rows
    kind = prolong.dtype
    return pl.pallas_call(
        pack_kernel,
        grid_spec=pltpu.PrefetchScalarGridSpec(
            num_scalar_prefetch=2,
            grid=(rows // step,),
            in_specs=[pl.BlockSpec((step, pores, width3), lambda i, *_: (i, 0, 0))],
            out_specs=[
                pl.BlockSpec((step, 2, pores, width), lambda i, *_: (i, 0, 0, 0)),
                pl.BlockSpec((step, pores, width), lambda i, *_: (i, 0, 0)),
                pl.BlockSpec((step, width3, pores), lambda i, *_: (i, 0, 0)),
            ],
        ),
        out_shape=[
            jax.ShapeDtypeStruct((rows, 2, pores, width), kind),
            jax.ShapeDtypeStruct((rows, pores, width), kind),
            jax.ShapeDtypeStruct((rows, width3, pores), kind),
        ],
        compiler_params=pltpu.CompilerParams(vmem_limit_bytes=VMEM_LIMIT),
        cost_estimate=pl.CostEstimate(flops=0, bytes_accessed=8 * 2 ** 20, transcendentals=0),
        name="pack_rows",
    )(info, mask, prolong)


def stage_kernel(layout, scalars, slot_rows, slot_cols, turned, *refs):
    slots = len(layout)
    sources = sum(len(s) for s in layout)
    matrix = refs[:slots]
    heads = refs[slots:slots + sources]
    tails = refs[slots + sources:slots + 2 * sources]
    own, up, down, total = refs[slots + 2 * sources:]
    cap = matrix[0].shape[1]
    pores = matrix[0].shape[2]
    width = tails[0].shape[-1]
    turn = scalars[0]
    at = 0
    for slot, kinds in enumerate(layout):
        panel = scalars[1 + slot]
        total[...] = jnp.zeros_like(total)
        for whole in kinds:
            live = scalars[1 + slots + at]
            head, tail = heads[at], tails[at]

            def product(entry, whole=whole, head=head, tail=tail, slot=slot, panel=panel):
                pick = slot_cols[panel * cap + entry] if whole else entry
                right = jnp.concatenate([head[pick, 0], head[pick, 1], tail[pick]], axis=1)
                return jnp.dot(matrix[slot][0, entry], right, preferred_element_type=jnp.float32)

            def add(left, value):
                result = jnp.dot(left, value, preferred_element_type=jnp.float32)
                for k in range(3):
                    total[k] += result[:, k * width:(k + 1) * width]

            def two(u, carry, product=product, panel=panel):
                first, second = 2 * u, 2 * u + 1
                left = jnp.concatenate(
                    [turned[slot_rows[panel * cap + first]], turned[slot_rows[panel * cap + second]]], axis=1)
                value = jnp.concatenate([product(first), product(second)], axis=0).astype(jnp.bfloat16)
                add(left, value)
                return carry

            lax.fori_loop(0, live // 2, two, 0)

            @pl.when(live % 2 == 1)
            def _(live=live, product=product, panel=panel):
                entry = live - 1
                add(turned[slot_rows[panel * cap + entry]], product(entry).astype(jnp.bfloat16))

            at += 1
        for f in range(3):
            k = jnp.where(turn == 1, (f + 2) % 3, f)
            own[slot, f] = total[k, pl.ds(pl.multiple_of((1 - turn) * width, width), width), :].astype(own.dtype)
            up[slot, f] = total[k, pl.ds(pl.multiple_of((2 - turn) * width, width), width), :].astype(up.dtype)
            down[slot, f] = total[k, 0:width, :].astype(down.dtype)


def stage(layout, scalars, slot_rows, slot_cols, turned, matrix, heads, tails):
    slots = len(layout)
    panels, cap, pores, _ = matrix.shape
    width3 = turned.shape[1]
    width = width3 // 3

    def whole_spec(x):
        return pl.BlockSpec(x.shape, lambda i, *_, n=x.ndim: (0,) * n)

    matrix_specs = [
        pl.BlockSpec((1, cap, pores, pores), lambda i, s, *_, j=j: (s[1 + j], 0, 0, 0)) for j in range(slots)]
    out = jax.ShapeDtypeStruct((slots, 3, width, width), jnp.bfloat16)
    flops = 2 * slots * 5 * (pores * pores * width3 + width3 * width3 * pores)
    size = sum(2 * x.size for x in (*heads, *tails)) + 2 * turned.size + 2 * slots * cap * pores * pores
    return pl.pallas_call(
        functools.partial(stage_kernel, layout),
        grid_spec=pltpu.PrefetchScalarGridSpec(
            num_scalar_prefetch=3,
            grid=(1,),
            in_specs=[whole_spec(turned), *matrix_specs, *map(whole_spec, heads), *map(whole_spec, tails)],
            out_specs=[pl.BlockSpec(out.shape, lambda i, *_: (0, 0, 0, 0))] * 3,
            scratch_shapes=[pltpu.VMEM((3, width3, width), jnp.float32)],
        ),
        out_shape=[out] * 3,
        compiler_params=pltpu.CompilerParams(vmem_limit_bytes=VMEM_LIMIT),
        cost_estimate=pl.CostEstimate(flops=flops, bytes_accessed=size, transcendentals=0),
        name="stage_products",
    )(scalars, slot_rows, slot_cols, turned, *([matrix] * slots), *heads, *tails)


def assemble_kernel(counts, panels, info, *refs):
    out = refs[-1]
    total = sum(counts)
    rows = refs[0].shape[2]
    pitch = 5 * panels
    at = 0
    for index, slots in enumerate(counts):
        own, lower, upper = refs[3 * index:3 * index + 3]
        for slot in range(slots):
            @pl.when(info[total + at] == 1)
            def _(slot=slot, own=own, lower=lower, upper=upper, at=at):
                panel = info[at]
                for d in range(5):
                    terms = []
                    if 0 <= d - 1 < 3:
                        terms.append(own[slot, d - 1].astype(jnp.float32))
                    if d < 3:
                        terms.append(lower[slot, d].astype(jnp.float32))
                    if 0 <= d - 2 < 3:
                        terms.append(upper[slot, d - 2].astype(jnp.float32))
                    out[pl.ds(d * panels + panel, rows, stride=pitch), :] = functools.reduce(jnp.add, terms)
            at += 1


def assemble(info, pieces, panels):
    counts = tuple(own.shape[0] for own, _, _ in pieces)
    width = pieces[0][0].shape[-1]
    rows = width // 4
    specs = [
        pl.BlockSpec((x.shape[0], 3, rows, width), lambda i, *_: (0, 0, i, 0)) for piece in pieces for x in piece]
    flat = [x for piece in pieces for x in piece]
    result = pl.pallas_call(
        functools.partial(assemble_kernel, counts, panels),
        grid_spec=pltpu.PrefetchScalarGridSpec(
            num_scalar_prefetch=1,
            grid=(width // rows,),
            in_specs=specs,
            out_specs=pl.BlockSpec((rows * 5 * panels, width), lambda i, *_: (i, 0)),
        ),
        out_shape=jax.ShapeDtypeStruct((width * 5 * panels, width), jnp.float32),
        compiler_params=pltpu.CompilerParams(vmem_limit_bytes=VMEM_LIMIT),
        cost_estimate=pl.CostEstimate(flops=0, bytes_accessed=8 * 2 ** 20, transcendentals=0),
        name="assemble_coarse",
    )(info, *flat)
    return result.reshape(width, 5, panels, width).transpose(0, 2, 1, 3)


def per_device(fine_blocks, block_rows, block_cols, block_counts, prolong_blocks, prolong_mask):
    matrix = fine_blocks[0, 0]
    rows_list = block_rows[0, 0]
    cols_list = block_cols[0, 0]
    count_list = block_counts[0, 0]
    prolong = prolong_blocks[0]
    panels = lax.axis_size("blk")
    groups = lax.axis_size("rows")
    lines, columns = grid_of(panels)
    group = lax.axis_index("rows")
    place = lax.axis_index("blk")
    z, y = place // columns, place % columns
    turn = (group == 0).astype(jnp.int32)
    flat_rows, flat_cols = rows_list.reshape(-1), cols_list.reshape(-1)

    every = range(groups)
    inner = range(1, groups - 1)

    def move(x, pairs, members):
        perm = [(a * groups + g, b * groups + g) for g in members for a, b in pairs]
        if not perm:
            return jnp.zeros_like(x)
        return lax.ppermute(x, ("blk", "rows"), perm)

    def move_both(pair, pairs):
        return move(pair[0], pairs, every), move(pair[1], pairs, inner)

    def line_pairs(s, sign):
        return [(h * columns + c, (h + sign) * columns + c)
                for h in range(lines) for c in range(columns)
                if 0 <= h + sign < lines and 0 <= h + sign - sign * s < lines]

    def across_pairs(shift, present):
        return [(h * columns + c, h * columns + (c + shift) % columns)
                for h in range(lines) if present(h) for c in range(columns)]

    served = [move(cols_list, [(b, a) for a, b in across_pairs(shift, lambda h: True)], every)
              for shift in range(1, columns)]

    info = jnp.stack([group, jnp.int32(groups), turn]).astype(jnp.int32)
    head, tail, turned = pack(info, prolong_mask[0].reshape(-1), prolong)
    own = (head, tail)

    def has(s, sign):
        source = z + sign * s
        return (source >= 0) & (source < lines)

    def picked(pair, line, shift):
        wanted = lax.dynamic_index_in_dim(served[shift - 1], jnp.clip(line, 0, lines - 1) * columns + y, 0, False)
        return tuple(x.at[wanted].get(mode="promise_in_bounds") for x in pair)

    def entry(line, shift):
        return jnp.clip(line, 0, lines - 1) * columns + (y - shift) % columns

    merged = [2 * s > lines - 1 for s in range(lines)]
    received = [[(z, jnp.bool_(True), [(own, jnp.bool_(True))])]]
    below, above = own, own
    crossing = []
    pieces, slot_panels, slot_present = [], [], []
    for s in range(lines + 1):
        if 0 < s < lines:
            below = move_both(below, line_pairs(s, 1))
            above = move_both(above, line_pairs(s, -1))
            has_below, has_above = has(s, -1), has(s, 1)
            if merged[s]:
                line = jnp.where(has_below, z - s, z + s)
                received.append([(line, has_below | has_above, [(below, has_below), (above, has_above)])])
            else:
                received.append([(z - s, has_below, [(below, has_below)]), (z + s, has_above, [(above, has_above)])])
        work = []
        if s < lines:
            work += [(entry(line, 0), there, [(p, ok, True) for p, ok in sources])
                     for line, there, sources in received[s]]
        if s > 0:
            work += crossing
        crossing = []
        if s < lines:
            for shift in range(1, columns):
                for index, (line, there, sources) in enumerate(received[s]):
                    pair = picked(sources[0][0], line, shift)
                    if len(sources) == 2:
                        other = picked(sources[1][0], line, shift)
                        pair = tuple(jnp.where(sources[0][1], a, b) for a, b in zip(pair, other))
                    if s == 0:
                        present = lambda h: True
                    elif merged[s]:
                        present = lambda h: 0 <= h - s or h + s < lines
                    else:
                        present = (lambda h: 0 <= h - s) if index == 0 else (lambda h: h + s < lines)
                    crossing.append((entry(line, shift), there,
                                     [(move_both(pair, across_pairs(shift, present)), there, False)]))
        if not work:
            continue
        layout = tuple(tuple(whole for _, _, whole in sources) for _, _, sources in work)
        panel_of = [panel for panel, _, _ in work]
        lives = [jnp.where(ok, count_list[panel], 0) for panel, _, sources in work for _, ok, _ in sources]
        scalars = jnp.stack([turn, *panel_of, *lives]).astype(jnp.int32)
        heads = [pair[0] for _, _, sources in work for pair, _, _ in sources]
        tails = [pair[1] for _, _, sources in work for pair, _, _ in sources]
        mine, up, down = stage(layout, scalars, flat_rows, flat_cols, turned, matrix, heads, tails)
        lower = lax.ppermute(up, "rows", [(g, g + 1) for g in range(groups - 1)])
        upper = lax.ppermute(down, "rows", [(g + 1, g) for g in range(groups - 1)])
        pieces.append((mine, lower, upper))
        slot_panels += panel_of
        slot_present += [there.astype(jnp.int32) for _, there, _ in work]
    where = jnp.stack([*slot_panels, *slot_present]).astype(jnp.int32)
    return assemble(where, pieces, panels)[None, None]


def solution(mesh):
    in_specs = (
        P("rows", "blk", None, None, None, None),
        P("rows", "blk", None, None),
        P("rows", "blk", None, None),
        P("rows", "blk", None),
        P("rows", "blk", None, None),
        P("rows", "blk", None),
    )
    out_specs = P("rows", "blk", None, None, None, None)
    return jax.shard_map(
        per_device, mesh=mesh, in_specs=in_specs, out_specs=out_specs, check_vma=False
    )
```

time: 324 us -> 225 us (0.69)
  the two profiles are of different devices: /device:TPU:1 before, /device:TPU:21 now
where the time goes in v1:
time: 225 us; the launch traced here: 223 us
  starting transfers between devices  86.1 us (38%)
  local copies, waits for them, and re-layouts  50.6 us (22%)
  waiting for transfers between devices  39.7 us (18%)
  Pallas kernels  29.5 us (13%)
  other arithmetic  10.3 us (5%)
  between operations  6.62 us (3%)
    ppermute x23, starting transfers between devices, move(): return lax.ppermute(x, ('blk', 'rows'), perm)  55.3 us
    ppermute x23, waiting for transfers between devices, move(): return lax.ppermute(x, ('blk', 'rows'), perm)  32.2 us
    gather x14, local copies, waits for them, and re-layouts, picked(): return tuple((x.at[wanted].get(mode='promise_in_bounds') for x in pair))  28.6 us
    pallas_call x5, Pallas kernels, stage(): pl.pallas_call(functools.partial(stage_kernel, layout), grid_spec=pltpu.P...  22.6 us
    ppermute x5, starting transfers between devices, per_device(): lower = lax.ppermute(up, 'rows', [(g, g + 1) for g in range(groups - 1)])  21.2 us
    unnamed x57, local copies, waits for them, and re-layouts  17.5 us
    ppermute x5, starting transfers between devices, per_device(): upper = lax.ppermute(down, 'rows', [(g + 1, g) for g in range(groups - 1)])  9.58 us
    ppermute x5, waiting for transfers between devices, per_device(): upper = lax.ppermute(down, 'rows', [(g + 1, g) for g in range(groups - 1)])  7.47 us
  transfers between devices with their start and end apart: 33, of which 4 were waited for; matrix products, arithmetic and copies ran while one was open for 18% of the time, Pallas kernels for 10%

profile of v1, /device:TPU:21, one launch (start us, length us, event | category | flops | bytes accessed | tf_op | source)
XLA Modules:
  0.0 222.8 jit_solution(3095733743157479872)
XLA Ops:
  0.9 1.7 constant_dynamic-slice_fusion.1
  3.3 1.4 copy-done.14
  4.7 2.3 %pack_rows.1 = (bf16[16,2,128,128]{3,2,1,0:T(8,128)(2,1)S(1)}, bf16[16,128,128]{2,1,0:T(8,128)(2,1)}, bf16[16,384,128]{2,1,0:T(8,128)(2,1)S(1)}) custom-call(s32[3]{0:T(128)S(1)} %get-tuple-element.57.info, s32[48]{0:T(128)S(1)} %reshape_squeeze.11.mask, bf16[16,128,384]{2,1,0:T(8,128)(2,1)S(1)} %bitcast.88), custom_call_target="tpu_custom_call" | custom-call | bytes 8388608 | tf_op jit(solution)/shard_map/pack_rows/pallas_call | solution.py:43
  7.0 3.2 %collective-permute-start.2 = (bf16[16,2,128,128]{3,2,1,0:T(8,128)(2,1)S(1)}, bf16[16,2,128,128]{3,2,1,0:T(8,128)(2,1)S(1)}, u32[]{:S(2)}, u32[]{:S(2)}) collective-permute-start(bf16[16,2,128,128]{3,2,1,0:T(8,128)(2,1)S(1)} %get-tuple-element.24.refs_1_), channel_id=1, source_target_pairs={{0,8},{4,12},{8,16},{12,20},{16,24},{20,28},{1,9},{5,13},{9,17},{1... | collective-permute-start | bytes 3145736 | tf_op jit(solution)/shard_map/ppermute | solution.py:217
  10.2 2.1 collective-permute-start.3
  13.3 19.6 %collective-permute-done.2.refs_3_ = bf16[16,2,128,128]{3,2,1,0:T(8,128)(2,1)S(1)} collective-permute-done((bf16[16,2,128,128]{3,2,1,0:T(8,128)(2,1)S(1)}, bf16[16,2,128,128]{3,2,1,0:T(8,128)(2,1)S(1)}, u32[]{:S(2)}, u32[]{:S(2)}) %collective-permute-start.2) | collective-permute-done | bytes 1048608 | tf_op jit(solution)/shard_map/ppermute | solution.py:217
  32.9 3.2 %collective-permute-start.11 = (bf16[16,2,128,128]{3,2,1,0:T(8,128)(2,1)S(1)}, bf16[16,2,128,128]{3,2,1,0:T(8,128)(2,1)}, u32[]{:S(2)}, u32[]{:S(2)}) collective-permute-start(bf16[16,2,128,128]{3,2,1,0:T(8,128)(2,1)S(1)} %collective-permute-done.2.refs_3_), channel_id=1, source_target_pairs={{8,16},{12,20},{16,24},{20,28},{9,17},{13,21},{17,25},{21,29},{10,... | collective-permute-start | bytes 3145736 | tf_op jit(solution)/shard_map/ppermute | solution.py:217
  36.1 4.0 %collective-permute-start.12 = (bf16[16,2,128,128]{3,2,1,0:T(8,128)(2,1)S(1)}, bf16[16,2,128,128]{3,2,1,0:T(8,128)(2,1)}, u32[]{:S(2)}, u32[]{:S(2)}) collective-permute-start(bf16[16,2,128,128]{3,2,1,0:T(8,128)(2,1)S(1)} %collective-permute-done.3.refs_4_), channel_id=1, source_target_pairs={{8,0},{12,4},{16,8},{20,12},{9,1},{13,5},{17,9},{21,13},{10,2},{14... | collective-permute-start | bytes 3145736 | tf_op jit(solution)/shard_map/ppermute | solution.py:217
  40.2 1.9 collective-permute-start.6
  42.1 3.4 %collective-permute-start.7 = (bf16[16,128,128]{2,1,0:T(8,128)(2,1)}, bf16[16,128,128]{2,1,0:T(8,128)(2,1)}, u32[]{:S(2)}, u32[]{:S(2)}) collective-permute-start(bf16[16,128,128]{2,1,0:T(8,128)(2,1)} %get-tuple-element.25.refs_2_), channel_id=1, source_target_pairs={{9,1},{13,5},{17,9},{21,13},{25,17},{29,21},{10,2},{14,6},{18,10},... | collective-permute-start | bytes 1572872 | tf_op jit(solution)/shard_map/ppermute | solution.py:217
  45.5 12.6 %collective-permute-done.11.refs_3_ = bf16[16,2,128,128]{3,2,1,0:T(8,128)(2,1)} collective-permute-done((bf16[16,2,128,128]{3,2,1,0:T(8,128)(2,1)S(1)}, bf16[16,2,128,128]{3,2,1,0:T(8,128)(2,1)}, u32[]{:S(2)}, u32[]{:S(2)}) %collective-permute-start.11) | collective-permute-done | bytes 1048608 | tf_op jit(solution)/shard_map/ppermute | solution.py:217
  58.0 3.3 %collective-permute-start.21 = (bf16[16,2,128,128]{3,2,1,0:T(8,128)(2,1)}, bf16[16,2,128,128]{3,2,1,0:T(8,128)(2,1)S(1)}, u32[]{:S(2)}, u32[]{:S(2)}) collective-permute-start(bf16[16,2,128,128]{3,2,1,0:T(8,128)(2,1)} %collective-permute-done.11.refs_3_), channel_id=1, source_target_pairs={{16,24},{20,28},{17,25},{21,29},{18,26},{22,30},{19,27},{23,31}} | collective-permute-start | bytes 3145736 | tf_op jit(solution)/shard_map/ppermute | solution.py:217
  61.3 1.7 collective-permute-start.22
  66.1 1.6 copy-done
  69.0 2.1 stage_products.5
  71.9 6.5 %collective-permute-start = (bf16[1,3,128,128]{3,2,1,0:T(8,128)(2,1)S(1)}, bf16[1,3,128,128]{3,2,1,0:T(8,128)(2,1)S(1)}, u32[]{:S(2)}, u32[]{:S(2)}) collective-permute-start(bf16[1,3,128,128]{3,2,1,0:T(8,128)(2,1)S(1)} %get-tuple-element.27), channel_id=1, source_target_pairs={{0,1},{1,2},{2,3},{4,5},{5,6},{6,7},{8,9},{9,10},{10,11},{12,13},{... | collective-permute-start | bytes 294920 | tf_op jit(solution)/shard_map/ppermute | solution.py:295
  78.4 1.9 collective-permute-start.15
  80.3 6.1 %collective-permute-start.16 = (bf16[16,128,128]{2,1,0:T(8,128)(2,1)}, bf16[16,128,128]{2,1,0:T(8,128)(2,1)}, u32[]{:S(2)}, u32[]{:S(2)}) collective-permute-start(bf16[16,128,128]{2,1,0:T(8,128)(2,1)} %collective-permute-done.7.refs_7_), channel_id=1, source_target_pairs={{9,1},{13,5},{17,9},{21,13},{10,2},{14,6},{18,10},{22,14}} | collective-permute-start | bytes 1572872 | tf_op jit(solution)/shard_map/ppermute | solution.py:217
  87.0 2.6 %gather_fusion = bf16[8,2,128,128]{3,2,1,0:T(8,128)(2,1)} fusion(bf16[16,2,128,128]{3,2,1,0:T(8,128)(2,1)} %copy-done.12, s32[1024]{0:T(1024)S(1)} %pad_clamp_fusion.4), kind=kCustom, calls=%fused_computation | custom fusion | bytes 1048608 | tf_op jit(solution)/shard_map/gather | solution.py:244
  89.6 2.3 %gather_fusion.1 = bf16[8,128,128]{2,1,0:T(8,128)(2,1)} fusion(bf16[16,128,128]{2,1,0:T(8,128)(2,1)} %get-tuple-element.25.refs_2_, s32[1024]{0:T(1024)S(1)} %pad_clamp_fusion.4), kind=kCustom, calls=%fused_computation.1 | custom fusion | bytes 524320 | tf_op jit(solution)/shard_map/gather | solution.py:244
  92.0 1.2 pad_clamp_fusion.3
  93.2 1.2 pad_clamp_fusion.2
  95.1 1.9 collective-permute-start.1
  97.6 3.4 %collective-permute-done.1.refs_2_ = bf16[1,3,128,128]{3,2,1,0:T(8,128)(2,1)S(1)} collective-permute-done((bf16[1,3,128,128]{3,2,1,0:T(8,128)(2,1)S(1)}, bf16[1,3,128,128]{3,2,1,0:T(8,128)(2,1)S(1)}, u32[]{:S(2)}, u32[]{:S(2)}) %collective-permute-start.1) | collective-permute-done | bytes 98336 | tf_op jit(solution)/shard_map/ppermute | solution.py:296
  102.2 2.8 %collective-permute-start.8 = (bf16[8,128,128]{2,1,0:T(8,128)(2,1)}, bf16[8,128,128]{2,1,0:T(8,128)(2,1)S(1)}, u32[]{:S(2)}, u32[]{:S(2)}) collective-permute-start(bf16[8,128,128]{2,1,0:T(8,128)(2,1)} %gather_fusion.1), channel_id=1, source_target_pairs={{1,5},{5,1},{9,13},{13,9},{17,21},{21,17},{25,29},{29,25},{2,6},{6... | collective-permute-start | bytes 786440 | tf_op jit(solution)/shard_map/ppermute | solution.py:217
  105.0 2.1 collective-permute-start.24
  107.7 2.5 %gather_fusion.4 = bf16[8,128,128]{2,1,0:T(8,128)(2,1)} fusion(bf16[16,128,128]{2,1,0:T(8,128)(2,1)} %collective-permute-done.6.refs_6_, s32[1024]{0:T(1024)} %pad_clamp_fusion.3), kind=kCustom, calls=%fused_computation.4 | custom fusion | bytes 524320 | tf_op jit(solution)/shard_map/gather | solution.py:244
  110.2 2.4 %gather_fusion.5 = bf16[8,128,128]{2,1,0:T(8,128)(2,1)} fusion(bf16[16,128,128]{2,1,0:T(8,128)(2,1)} %collective-permute-done.7.refs_7_, s32[1024]{0:T(1024)} %pad_clamp_fusion.2), kind=kCustom, calls=%fused_computation.5 | custom fusion | bytes 524320 | tf_op jit(solution)/shard_map/gather | solution.py:244
  112.6 1.6 gather_fusion.2
  114.2 1.5 gather_fusion.3
  115.7 1.6 gather_fusion.8
  117.4 1.6 gather_fusion.9
  119.7 1.9 gather_fusion.6
  121.6 1.9 gather_fusion.7
  124.2 2.4 %collective-permute-start.17 = (bf16[8,128,128]{2,1,0:T(8,128)(2,1)}, bf16[8,128,128]{2,1,0:T(8,128)(2,1)S(1)}, u32[]{:S(2)}, u32[]{:S(2)}) collective-permute-start(bf16[8,128,128]{2,1,0:T(8,128)(2,1)} %gather_fusion.4), channel_id=1, source_target_pairs={{9,13},{13,9},{17,21},{21,17},{25,29},{29,25},{10,14},{14,10},{18,... | collective-permute-start | bytes 786440 | tf_op jit(solution)/shard_map/ppermute | solution.py:217
  126.7 2.8 %collective-permute-start.13 = (bf16[8,2,128,128]{3,2,1,0:T(8,128)(2,1)}, bf16[8,2,128,128]{3,2,1,0:T(8,128)(2,1)}, u32[]{:S(2)}, u32[]{:S(2)}) collective-permute-start(bf16[8,2,128,128]{3,2,1,0:T(8,128)(2,1)} %gather_fusion.2), channel_id=1, source_target_pairs={{8,12},{12,8},{16,20},{20,16},{24,28},{28,24},{9,13},{13,9},{17,21... | collective-permute-start | bytes 1572872 | tf_op jit(solution)/shard_map/ppermute | solution.py:217
  129.5 1.5 collective-permute-start.25
  131.9 1.4 gather_fusion.10
  133.3 2.7 %gather_fusion.11 = bf16[8,2,128,128]{3,2,1,0:T(8,128)(2,1)} fusion(bf16[16,2,128,128]{3,2,1,0:T(8,128)(2,1)} %collective-permute-done.22.refs_3_, s32[1024]{0:T(1024)S(1)} %pad_clamp_fusion), kind=kCustom, calls=%fused_computation.11 | custom fusion | bytes 1048608 | tf_op jit(solution)/shard_map/gather | solution.py:244
  135.9 2.6 %collective-permute-start.18 = (bf16[8,128,128]{2,1,0:T(8,128)(2,1)}, bf16[8,128,128]{2,1,0:T(8,128)(2,1)}, u32[]{:S(2)}, u32[]{:S(2)}) collective-permute-start(bf16[8,128,128]{2,1,0:T(8,128)(2,1)} %gather_fusion.5), channel_id=1, source_target_pairs={{1,5},{5,1},{9,13},{13,9},{17,21},{21,17},{2,6},{6,2},{10,14},{14,... | collective-permute-start | bytes 786440 | tf_op jit(solution)/shard_map/ppermute | solution.py:217
  138.5 2.8 %collective-permute-start.14 = (bf16[8,2,128,128]{3,2,1,0:T(8,128)(2,1)}, bf16[8,2,128,128]{3,2,1,0:T(8,128)(2,1)}, u32[]{:S(2)}, u32[]{:S(2)}) collective-permute-start(bf16[8,2,128,128]{3,2,1,0:T(8,128)(2,1)} %gather_fusion.3), channel_id=1, source_target_pairs={{0,4},{4,0},{8,12},{12,8},{16,20},{20,16},{1,5},{5,1},{9,13},{13,9... | collective-permute-start | bytes 1572872 | tf_op jit(solution)/shard_map/ppermute | solution.py:217
  142.0 1.9 broadcast_select_fusion
  143.9 1.5 collective-permute-start.29
  148.8 5.4 %stage_products.6 = (bf16[3,3,128,128]{3,2,1,0:T(8,128)(2,1)S(1)}, bf16[3,3,128,128]{3,2,1,0:T(8,128)(2,1)S(1)}, bf16[3,3,128,128]{3,2,1,0:T(8,128)(2,1)}) custom-call(s32[7]{0:T(128)S(1)} %stack.167.scalars, s32[64]{0:T(128)S(1)} %reshape_squeeze.9.slot_rows, s32[64]{0:T(128)S(1)} %reshape_squeeze.10.slot_cols, bf16[16,384,128]{2,1,0:T(8,128)(2,1)S(1)} %copy-done.3, ...), custom_call_target="tpu_custom_call" | custom-call | flops 754974720 | bytes 6291456 | tf_op jit(solution)/shard_map/stage_products/pallas_call | solution.py:132
  154.9 2.3 %gather_fusion.12 = bf16[8,128,128]{2,1,0:T(8,128)(2,1)} fusion(bf16[16,128,128]{2,1,0:T(8,128)(2,1)} %collective-permute-done.24.refs_5_, s32[1024]{0:T(1024)S(1)} %pad_clamp_fusion), kind=kCustom, calls=%fused_computation.12 | custom fusion | bytes 524320 | tf_op jit(solution)/shard_map/gather | solution.py:244
  157.2 2.3 %gather_fusion.13 = bf16[8,128,128]{2,1,0:T(8,128)(2,1)} fusion(bf16[16,128,128]{2,1,0:T(8,128)(2,1)} %collective-permute-done.25.refs_6_, s32[1024]{0:T(1024)S(1)} %pad_clamp_fusion), kind=kCustom, calls=%fused_computation.13 | custom fusion | bytes 524320 | tf_op jit(solution)/shard_map/gather | solution.py:244
  159.5 3.8 %collective-permute-start.9 = (bf16[3,3,128,128]{3,2,1,0:T(8,128)(2,1)}, bf16[3,3,128,128]{3,2,1,0:T(8,128)(2,1)}, u32[]{:S(2)}, u32[]{:S(2)}) collective-permute-start(bf16[3,3,128,128]{3,2,1,0:T(8,128)(2,1)} %copy-done.27), channel_id=1, source_target_pairs={{0,1},{1,2},{2,3},{4,5},{5,6},{6,7},{8,9},{9,10},{10,11},{12,13},{... | collective-permute-start | bytes 884744 | tf_op jit(solution)/shard_map/ppermute | solution.py:295
  163.4 3.3 %collective-permute-start.26 = (bf16[8,128,128]{2,1,0:T(8,128)(2,1)}, bf16[8,128,128]{2,1,0:T(8,128)(2,1)}, u32[]{:S(2)}, u32[]{:S(2)}) collective-permute-start(bf16[8,128,128]{2,1,0:T(8,128)(2,1)} %broadcast_select_fusion.3), channel_id=1, source_target_pairs={{1,5},{5,1},{9,13},{13,9},{17,21},{21,17},{25,29},{29,25},{2,6},{6... | collective-permute-start | bytes 786440 | tf_op jit(solution)/shard_map/ppermute | solution.py:217
  166.7 1.7 broadcast_select_fusion.2
  168.4 1.4 collective-permute-start.30
  172.1 1.4 copy-done.4
  174.5 7.7 %stage_products.7 = (bf16[3,3,128,128]{3,2,1,0:T(8,128)(2,1)S(1)}, bf16[3,3,128,128]{3,2,1,0:T(8,128)(2,1)}, bf16[3,3,128,128]{3,2,1,0:T(8,128)(2,1)}) custom-call(s32[8]{0:T(128)S(1)} %stack.172.scalars, s32[64]{0:T(128)S(1)} %reshape_squeeze.9.slot_rows, s32[64]{0:T(128)S(1)} %reshape_squeeze.10.slot_cols, bf16[16,384,128]{2,1,0:T(8,128)(2,1)S(1)} %copy-done.4, ...), custom_call_target="tpu_custom_call" | custom-call | flops 754974720 | bytes 7077888 | tf_op jit(solution)/shard_map/stage_products/pallas_call | solution.py:132
  182.9 1.9 collective-permute-start.10
  184.8 3.6 %collective-permute-start.19 = (bf16[3,3,128,128]{3,2,1,0:T(8,128)(2,1)}, bf16[3,3,128,128]{3,2,1,0:T(8,128)(2,1)}, u32[]{:S(2)}, u32[]{:S(2)}) collective-permute-start(bf16[3,3,128,128]{3,2,1,0:T(8,128)(2,1)} %get-tuple-element.33), channel_id=1, source_target_pairs={{0,1},{1,2},{2,3},{4,5},{5,6},{6,7},{8,9},{9,10},{10,11},{12,13},{... | collective-permute-start | bytes 884744 | tf_op jit(solution)/shard_map/ppermute | solution.py:295
  188.5 1.9 collective-permute-start.20
  192.9 1.4 copy-done.5
  194.3 5.0 %stage_products.8 = (bf16[2,3,128,128]{3,2,1,0:T(8,128)(2,1)S(1)}, bf16[2,3,128,128]{3,2,1,0:T(8,128)(2,1)}, bf16[2,3,128,128]{3,2,1,0:T(8,128)(2,1)}) custom-call(s32[6]{0:T(128)S(1)} %stack.176.scalars, s32[64]{0:T(128)S(1)} %reshape_squeeze.9.slot_rows, s32[64]{0:T(128)S(1)} %reshape_squeeze.10.slot_cols, bf16[16,384,128]{2,1,0:T(8,128)(2,1)S(1)} %copy-done.5, ...), custom_call_target="tpu_custom_call" | custom-call | flops 503316480 | bytes 6029312 | tf_op jit(solution)/shard_map/stage_products/pallas_call | solution.py:132
  199.3 3.6 %collective-permute-start.27 = (bf16[2,3,128,128]{3,2,1,0:T(8,128)(2,1)}, bf16[2,3,128,128]{3,2,1,0:T(8,128)(2,1)S(1)}, u32[]{:S(2)}, u32[]{:S(2)}) collective-permute-start(bf16[2,3,128,128]{3,2,1,0:T(8,128)(2,1)} %get-tuple-element.36), channel_id=1, source_target_pairs={{0,1},{1,2},{2,3},{4,5},{5,6},{6,7},{8,9},{9,10},{10,11},{12,13},{... | collective-permute-start | bytes 589832 | tf_op jit(solution)/shard_map/ppermute | solution.py:295
  203.0 1.9 collective-permute-start.28
  205.0 2.4 %stage_products.9 = (bf16[1,3,128,128]{3,2,1,0:T(8,128)(2,1)S(1)}, bf16[1,3,128,128]{3,2,1,0:T(8,128)(2,1)}, bf16[1,3,128,128]{3,2,1,0:T(8,128)(2,1)}) custom-call(s32[3]{0:T(128)S(1)} %pad_add_fusion.2.scalars, s32[64]{0:T(128)S(1)} %reshape_squeeze.9.slot_rows, s32[64]{0:T(128)S(1)} %reshape_squeeze.10.slot_cols, bf16[16,384,128]{2,1,0:T(8,128)(2,1)S(1)} %copy-done.5, ...), custom_call_target="tpu_custom_call" | custom-call | flops 251658240 | bytes 2621440 | tf_op jit(solution)/shard_map/stage_products/pallas_call | solution.py:132
  207.4 3.6 %collective-permute-start.31 = (bf16[1,3,128,128]{3,2,1,0:T(8,128)(2,1)}, bf16[1,3,128,128]{3,2,1,0:T(8,128)(2,1)S(1)}, u32[]{:S(2)}, u32[]{:S(2)}) collective-permute-start(bf16[1,3,128,128]{3,2,1,0:T(8,128)(2,1)} %get-tuple-element.39), channel_id=1, source_target_pairs={{0,1},{1,2},{2,3},{4,5},{5,6},{6,7},{8,9},{9,10},{10,11},{12,13},{... | collective-permute-start | bytes 294920 | tf_op jit(solution)/shard_map/ppermute | solution.py:295
  211.0 1.9 collective-permute-start.32
  213.1 4.1 %collective-permute-done.32.refs_14_ = bf16[1,3,128,128]{3,2,1,0:T(8,128)(2,1)S(1)} collective-permute-done((bf16[1,3,128,128]{3,2,1,0:T(8,128)(2,1)}, bf16[1,3,128,128]{3,2,1,0:T(8,128)(2,1)S(1)}, u32[]{:S(2)}, u32[]{:S(2)}) %collective-permute-start.32) | collective-permute-done | bytes 98336 | tf_op jit(solution)/shard_map/ppermute | solution.py:296
  218.1 4.7 %assemble_coarse.1 = f32[5120,128]{1,0:T(8,128)} custom-call(s32[20]{0:T(128)S(1)} %stack.157.info, bf16[1,3,128,128]{3,2,1,0:T(8,128)(2,1)S(1)} %get-tuple-element.26.refs_0_, bf16[1,3,128,128]{3,2,1,0:T(8,128)(2,1)S(1)} %copy-done.24, bf16[1,3,128,128]{3,2,1,0:T(8,128)(2,1)S(1)} %copy-done.26, bf16[3,3,128,128]{3,2,1,0:T(8,128)(2,1)S(1)} %get-tuple-element.29.refs_3_, ...), custom_call_target="tpu_custom_call" | custom-call | bytes 8388608 | tf_op jit(solution)/shard_map/assemble_coarse/pallas_call | solution.py:179
  (100 shorter events, 20.0 us)
Async XLA Ops:
  3.3 1.4 copy-start.14
  7.0 64.1 %copy-start.2 = (bf16[16,384,128]{2,1,0:T(8,128)(2,1)}, bf16[16,384,128]{2,1,0:T(8,128)(2,1)S(1)}, u32[]{:S(2)}) copy-start(bf16[16,384,128]{2,1,0:T(8,128)(2,1)S(1)} %get-tuple-element.23.turned) | copy-start | bytes 4718596
  7.0 25.9 %collective-permute-start.2 = (bf16[16,2,128,128]{3,2,1,0:T(8,128)(2,1)S(1)}, bf16[16,2,128,128]{3,2,1,0:T(8,128)(2,1)S(1)}, u32[]{:S(2)}, u32[]{:S(2)}) collective-permute-start(bf16[16,2,128,128]{3,2,1,0:T(8,128)(2,1)S(1)} %get-tuple-element.24.refs_1_), channel_id=1, source_target_pairs={{0,8},{4,12},{8,16},{12,20},{16,24},{20,28},{1,9},{5,13},{9,17},{1... | collective-permute-start | bytes 3145736 | tf_op jit(solution)/shard_map/ppermute | solution.py:217
  10.2 25.9 %collective-permute-start.3 = (bf16[16,2,128,128]{3,2,1,0:T(8,128)(2,1)S(1)}, bf16[16,2,128,128]{3,2,1,0:T(8,128)(2,1)S(1)}, u32[]{:S(2)}, u32[]{:S(2)}) collective-permute-start(bf16[16,2,128,128]{3,2,1,0:T(8,128)(2,1)S(1)} %get-tuple-element.24.refs_1_), channel_id=1, source_target_pairs={{8,0},{12,4},{16,8},{20,12},{24,16},{28,20},{9,1},{13,5},{17,9},{2... | collective-permute-start | bytes 3145736 | tf_op jit(solution)/shard_map/ppermute | solution.py:217
  12.3 1.0 copy-start.12
  32.9 12.5 %copy-start.6 = (bf16[16,2,128,128]{3,2,1,0:T(8,128)(2,1)}, bf16[16,2,128,128]{3,2,1,0:T(8,128)(2,1)S(1)}, u32[]{:S(2)}) copy-start(bf16[16,2,128,128]{3,2,1,0:T(8,128)(2,1)S(1)} %collective-permute-done.2.refs_3_) | copy-start | bytes 3145732
  32.9 25.1 %collective-permute-start.11 = (bf16[16,2,128,128]{3,2,1,0:T(8,128)(2,1)S(1)}, bf16[16,2,128,128]{3,2,1,0:T(8,128)(2,1)}, u32[]{:S(2)}, u32[]{:S(2)}) collective-permute-start(bf16[16,2,128,128]{3,2,1,0:T(8,128)(2,1)S(1)} %collective-permute-done.2.refs_3_), channel_id=1, source_target_pairs={{8,16},{12,20},{16,24},{20,28},{9,17},{13,21},{17,25},{21,29},{10,... | collective-permute-start | bytes 3145736 | tf_op jit(solution)/shard_map/ppermute | solution.py:217
  36.1 21.9 %copy-start.9 = (bf16[16,2,128,128]{3,2,1,0:T(8,128)(2,1)}, bf16[16,2,128,128]{3,2,1,0:T(8,128)(2,1)S(1)}, u32[]{:S(2)}) copy-start(bf16[16,2,128,128]{3,2,1,0:T(8,128)(2,1)S(1)} %collective-permute-done.3.refs_4_) | copy-start | bytes 3145732
  36.1 25.1 %collective-permute-start.12 = (bf16[16,2,128,128]{3,2,1,0:T(8,128)(2,1)S(1)}, bf16[16,2,128,128]{3,2,1,0:T(8,128)(2,1)}, u32[]{:S(2)}, u32[]{:S(2)}) collective-permute-start(bf16[16,2,128,128]{3,2,1,0:T(8,128)(2,1)S(1)} %collective-permute-done.3.refs_4_), channel_id=1, source_target_pairs={{8,0},{12,4},{16,8},{20,12},{9,1},{13,5},{17,9},{21,13},{10,2},{14... | collective-permute-start | bytes 3145736 | tf_op jit(solution)/shard_map/ppermute | solution.py:217
  40.2 38.2 %collective-permute-start.6 = (bf16[16,128,128]{2,1,0:T(8,128)(2,1)}, bf16[16,128,128]{2,1,0:T(8,128)(2,1)}, u32[]{:S(2)}, u32[]{:S(2)}) collective-permute-start(bf16[16,128,128]{2,1,0:T(8,128)(2,1)} %get-tuple-element.25.refs_2_), channel_id=1, source_target_pairs={{1,9},{5,13},{9,17},{13,21},{17,25},{21,29},{2,10},{6,14},{10,18},... | collective-permute-start | bytes 1572872 | tf_op jit(solution)/shard_map/ppermute | solution.py:217
  42.1 38.2 %collective-permute-start.7 = (bf16[16,128,128]{2,1,0:T(8,128)(2,1)}, bf16[16,128,128]{2,1,0:T(8,128)(2,1)}, u32[]{:S(2)}, u32[]{:S(2)}) collective-permute-start(bf16[16,128,128]{2,1,0:T(8,128)(2,1)} %get-tuple-element.25.refs_2_), channel_id=1, source_target_pairs={{9,1},{13,5},{17,9},{21,13},{25,17},{29,21},{10,2},{14,6},{18,10},... | collective-permute-start | bytes 1572872 | tf_op jit(solution)/shard_map/ppermute | solution.py:217
  58.0 68.6 %collective-permute-start.21 = (bf16[16,2,128,128]{3,2,1,0:T(8,128)(2,1)}, bf16[16,2,128,128]{3,2,1,0:T(8,128)(2,1)S(1)}, u32[]{:S(2)}, u32[]{:S(2)}) collective-permute-start(bf16[16,2,128,128]{3,2,1,0:T(8,128)(2,1)} %collective-permute-done.11.refs_3_), channel_id=1, source_target_pairs={{16,24},{20,28},{17,25},{21,29},{18,26},{22,30},{19,27},{23,31}} | collective-permute-start | bytes 3145736 | tf_op jit(solution)/shard_map/ppermute | solution.py:217
  61.3 68.2 %collective-permute-start.22 = (bf16[16,2,128,128]{3,2,1,0:T(8,128)(2,1)}, bf16[16,2,128,128]{3,2,1,0:T(8,128)(2,1)}, u32[]{:S(2)}, u32[]{:S(2)}) collective-permute-start(bf16[16,2,128,128]{3,2,1,0:T(8,128)(2,1)} %collective-permute-done.12.refs_4_), channel_id=1, source_target_pairs={{8,0},{12,4},{9,1},{13,5},{10,2},{14,6},{11,3},{15,7}} | collective-permute-start | bytes 3145736 | tf_op jit(solution)/shard_map/ppermute | solution.py:217
  63.0 8.9 %collective-permute-start.4 = (s32[8,8]{1,0:T(8,128)}, s32[8,8]{1,0:T(8,128)S(1)}, u32[]{:S(2)}, u32[]{:S(2)}) collective-permute-start(s32[8,8]{1,0:T(8,128)} %bitcast.89), channel_id=1, source_target_pairs={{4,0},{0,4},{12,8},{8,12},{20,16},{16,20},{28,24},{24,28},{5,1},{1... | collective-permute-start | bytes 776 | tf_op jit(solution)/shard_map/ppermute | solution.py:217
  66.1 1.6 copy-start
  67.7 1.2 copy-start.13
  71.1 41.6 %copy-start.7 = (bf16[16,2,128,128]{3,2,1,0:T(8,128)(2,1)S(1)}, bf16[16,2,128,128]{3,2,1,0:T(8,128)(2,1)}, u32[]{:S(2)}) copy-start(bf16[16,2,128,128]{3,2,1,0:T(8,128)(2,1)} %copy-done.6) | copy-start | bytes 3145732
  71.1 43.1 %copy-start.10 = (bf16[16,2,128,128]{3,2,1,0:T(8,128)(2,1)S(1)}, bf16[16,2,128,128]{3,2,1,0:T(8,128)(2,1)}, u32[]{:S(2)}) copy-start(bf16[16,2,128,128]{3,2,1,0:T(8,128)(2,1)} %copy-done.9) | copy-start | bytes 3145732
  71.9 22.5 %collective-permute-start = (bf16[1,3,128,128]{3,2,1,0:T(8,128)(2,1)S(1)}, bf16[1,3,128,128]{3,2,1,0:T(8,128)(2,1)S(1)}, u32[]{:S(2)}, u32[]{:S(2)}) collective-permute-start(bf16[1,3,128,128]{3,2,1,0:T(8,128)(2,1)S(1)} %get-tuple-element.27), channel_id=1, source_target_pairs={{0,1},{1,2},{2,3},{4,5},{5,6},{6,7},{8,9},{9,10},{10,11},{12,13},{... | collective-permute-start | bytes 294920 | tf_op jit(solution)/shard_map/ppermute | solution.py:295
  78.4 23.8 %collective-permute-start.15 = (bf16[16,128,128]{2,1,0:T(8,128)(2,1)}, bf16[16,128,128]{2,1,0:T(8,128)(2,1)}, u32[]{:S(2)}, u32[]{:S(2)}) collective-permute-start(bf16[16,128,128]{2,1,0:T(8,128)(2,1)} %collective-permute-done.6.refs_6_), channel_id=1, source_target_pairs={{9,17},{13,21},{17,25},{21,29},{10,18},{14,22},{18,26},{22,30}} | collective-permute-start | bytes 1572872 | tf_op jit(solution)/shard_map/ppermute | solution.py:217
  80.3 24.7 %collective-permute-start.16 = (bf16[16,128,128]{2,1,0:T(8,128)(2,1)}, bf16[16,128,128]{2,1,0:T(8,128)(2,1)}, u32[]{:S(2)}, u32[]{:S(2)}) collective-permute-start(bf16[16,128,128]{2,1,0:T(8,128)(2,1)} %collective-permute-done.7.refs_7_), channel_id=1, source_target_pairs={{9,1},{13,5},{17,9},{21,13},{10,2},{14,6},{18,10},{22,14}} | collective-permute-start | bytes 1572872 | tf_op jit(solution)/shard_map/ppermute | solution.py:217
  94.4 0.6 copy-start.23
  95.1 5.9 %collective-permute-start.1 = (bf16[1,3,128,128]{3,2,1,0:T(8,128)(2,1)S(1)}, bf16[1,3,128,128]{3,2,1,0:T(8,128)(2,1)S(1)}, u32[]{:S(2)}, u32[]{:S(2)}) collective-permute-start(bf16[1,3,128,128]{3,2,1,0:T(8,128)(2,1)S(1)} %get-tuple-element.28), channel_id=1, source_target_pairs={{1,0},{2,1},{3,2},{5,4},{6,5},{7,6},{9,8},{10,9},{11,10},{13,12},{... | collective-permute-start | bytes 294920 | tf_op jit(solution)/shard_map/ppermute | solution.py:296
  101.0 0.6 copy-start.25
  101.6 34.3 %collective-permute-start.5 = (bf16[8,2,128,128]{3,2,1,0:T(8,128)(2,1)}, bf16[8,2,128,128]{3,2,1,0:T(8,128)(2,1)}, u32[]{:S(2)}, u32[]{:S(2)}) collective-permute-start(bf16[8,2,128,128]{3,2,1,0:T(8,128)(2,1)} %gather_fusion), channel_id=1, source_target_pairs={{0,4},{4,0},{8,12},{12,8},{16,20},{20,16},{24,28},{28,24},{1,5},{5... | collective-permute-start | bytes 1572872 | tf_op jit(solution)/shard_map/ppermute | solution.py:217
  102.2 21.3 %collective-permute-start.8 = (bf16[8,128,128]{2,1,0:T(8,128)(2,1)}, bf16[8,128,128]{2,1,0:T(8,128)(2,1)S(1)}, u32[]{:S(2)}, u32[]{:S(2)}) collective-permute-start(bf16[8,128,128]{2,1,0:T(8,128)(2,1)} %gather_fusion.1), channel_id=1, source_target_pairs={{1,5},{5,1},{9,13},{13,9},{17,21},{21,17},{25,29},{29,25},{2,6},{6... | collective-permute-start | bytes 786440 | tf_op jit(solution)/shard_map/ppermute | solution.py:217
  105.0 36.4 %collective-permute-start.24 = (bf16[16,128,128]{2,1,0:T(8,128)(2,1)}, bf16[16,128,128]{2,1,0:T(8,128)(2,1)}, u32[]{:S(2)}, u32[]{:S(2)}) collective-permute-start(bf16[16,128,128]{2,1,0:T(8,128)(2,1)} %collective-permute-done.15.refs_7_), channel_id=1, source_target_pairs={{17,25},{21,29},{18,26},{22,30}} | collective-permute-start | bytes 1572872 | tf_op jit(solution)/shard_map/ppermute | solution.py:217
  123.5 0.7 copy-start.19
  124.2 14.3 %collective-permute-start.17 = (bf16[8,128,128]{2,1,0:T(8,128)(2,1)}, bf16[8,128,128]{2,1,0:T(8,128)(2,1)S(1)}, u32[]{:S(2)}, u32[]{:S(2)}) collective-permute-start(bf16[8,128,128]{2,1,0:T(8,128)(2,1)} %gather_fusion.4), channel_id=1, source_target_pairs={{9,13},{13,9},{17,21},{21,17},{25,29},{29,25},{10,14},{14,10},{18,... | collective-permute-start | bytes 786440 | tf_op jit(solution)/shard_map/ppermute | solution.py:217
  126.7 36.7 %collective-permute-start.13 = (bf16[8,2,128,128]{3,2,1,0:T(8,128)(2,1)}, bf16[8,2,128,128]{3,2,1,0:T(8,128)(2,1)}, u32[]{:S(2)}, u32[]{:S(2)}) collective-permute-start(bf16[8,2,128,128]{3,2,1,0:T(8,128)(2,1)} %gather_fusion.2), channel_id=1, source_target_pairs={{8,12},{12,8},{16,20},{20,16},{24,28},{28,24},{9,13},{13,9},{17,21... | collective-permute-start | bytes 1572872 | tf_op jit(solution)/shard_map/ppermute | solution.py:217
  129.5 14.4 %collective-permute-start.25 = (bf16[16,128,128]{2,1,0:T(8,128)(2,1)}, bf16[16,128,128]{2,1,0:T(8,128)(2,1)}, u32[]{:S(2)}, u32[]{:S(2)}) collective-permute-start(bf16[16,128,128]{2,1,0:T(8,128)(2,1)} %collective-permute-done.16.refs_8_), channel_id=1, source_target_pairs={{9,1},{13,5},{10,2},{14,6}} | collective-permute-start | bytes 1572872 | tf_op jit(solution)/shard_map/ppermute | solution.py:217
  131.9 13.5 %copy-start.1 = (bf16[1,1,8,8,128,128]{5,4,3,2,1,0:T(8,128)(2,1)S(1)}, bf16[1,1,8,8,128,128]{5,4,3,2,1,0:T(8,128)(2,1)}, u32[]{:S(2)}) copy-start(bf16[1,1,8,8,128,128]{5,4,3,2,1,0:T(8,128)(2,1)} %param.6) | copy-start | bytes 6291460
  135.9 9.5 %copy-start.3 = (bf16[16,384,128]{2,1,0:T(8,128)(2,1)S(1)}, bf16[16,384,128]{2,1,0:T(8,128)(2,1)}, u32[]{:S(2)}) copy-start(bf16[16,384,128]{2,1,0:T(8,128)(2,1)} %copy-done.2) | copy-start | bytes 4718596
  135.9 23.6 %collective-permute-start.18 = (bf16[8,128,128]{2,1,0:T(8,128)(2,1)}, bf16[8,128,128]{2,1,0:T(8,128)(2,1)}, u32[]{:S(2)}, u32[]{:S(2)}) collective-permute-start(bf16[8,128,128]{2,1,0:T(8,128)(2,1)} %gather_fusion.5), channel_id=1, source_target_pairs={{1,5},{5,1},{9,13},{13,9},{17,21},{21,17},{2,6},{6,2},{10,14},{14,... | collective-permute-start | bytes 786440 | tf_op jit(solution)/shard_map/ppermute | solution.py:217
  138.5 5.4 %copy-start.17 = (bf16[8,128,128]{2,1,0:T(8,128)(2,1)}, bf16[8,128,128]{2,1,0:T(8,128)(2,1)S(1)}, u32[]{:S(2)}) copy-start(bf16[8,128,128]{2,1,0:T(8,128)(2,1)S(1)} %collective-permute-done.17.refs_9_) | copy-start | bytes 786436
  138.5 29.8 %collective-permute-start.14 = (bf16[8,2,128,128]{3,2,1,0:T(8,128)(2,1)}, bf16[8,2,128,128]{3,2,1,0:T(8,128)(2,1)}, u32[]{:S(2)}, u32[]{:S(2)}) collective-permute-start(bf16[8,2,128,128]{3,2,1,0:T(8,128)(2,1)} %gather_fusion.3), channel_id=1, source_target_pairs={{0,4},{4,0},{8,12},{12,8},{16,20},{20,16},{1,5},{5,1},{9,13},{13,9... | collective-permute-start | bytes 1572872 | tf_op jit(solution)/shard_map/ppermute | solution.py:217
  141.4 47.1 %collective-permute-start.23 = (bf16[8,2,128,128]{3,2,1,0:T(8,128)(2,1)}, bf16[8,2,128,128]{3,2,1,0:T(8,128)(2,1)}, u32[]{:S(2)}, u32[]{:S(2)}) collective-permute-start(bf16[8,2,128,128]{3,2,1,0:T(8,128)(2,1)} %broadcast_select_fusion.1), channel_id=1, source_target_pairs={{0,4},{4,0},{8,12},{12,8},{16,20},{20,16},{24,28},{28,24},{1,5},{5... | collective-permute-start | bytes 1572872 | tf_op jit(solution)/shard_map/ppermute | solution.py:217
  143.9 59.1 %collective-permute-start.29 = (bf16[8,2,128,128]{3,2,1,0:T(8,128)(2,1)}, bf16[8,2,128,128]{3,2,1,0:T(8,128)(2,1)}, u32[]{:S(2)}, u32[]{:S(2)}) collective-permute-start(bf16[8,2,128,128]{3,2,1,0:T(8,128)(2,1)} %broadcast_select_fusion), channel_id=1, source_target_pairs={{0,4},{4,0},{24,28},{28,24},{1,5},{5,1},{25,29},{29,25},{2,6},{6,2... | collective-permute-start | bytes 1572872 | tf_op jit(solution)/shard_map/ppermute | solution.py:217
  145.4 1.2 copy-start.8
  146.6 1.2 copy-start.11
  147.8 0.9 copy-start.20
  154.2 0.7 copy-start.27
  159.5 25.3 %collective-permute-start.9 = (bf16[3,3,128,128]{3,2,1,0:T(8,128)(2,1)}, bf16[3,3,128,128]{3,2,1,0:T(8,128)(2,1)}, u32[]{:S(2)}, u32[]{:S(2)}) collective-permute-start(bf16[3,3,128,128]{3,2,1,0:T(8,128)(2,1)} %copy-done.27), channel_id=1, source_target_pairs={{0,1},{1,2},{2,3},{4,5},{5,6},{6,7},{8,9},{9,10},{10,11},{12,13},{... | collective-permute-start | bytes 884744 | tf_op jit(solution)/shard_map/ppermute | solution.py:295
  163.4 19.5 %collective-permute-start.26 = (bf16[8,128,128]{2,1,0:T(8,128)(2,1)}, bf16[8,128,128]{2,1,0:T(8,128)(2,1)}, u32[]{:S(2)}, u32[]{:S(2)}) collective-permute-start(bf16[8,128,128]{2,1,0:T(8,128)(2,1)} %broadcast_select_fusion.3), channel_id=1, source_target_pairs={{1,5},{5,1},{9,13},{13,9},{17,21},{21,17},{25,29},{29,25},{2,6},{6... | collective-permute-start | bytes 786440 | tf_op jit(solution)/shard_map/ppermute | solution.py:217
  168.4 30.9 %collective-permute-start.30 = (bf16[8,128,128]{2,1,0:T(8,128)(2,1)}, bf16[8,128,128]{2,1,0:T(8,128)(2,1)}, u32[]{:S(2)}, u32[]{:S(2)}) collective-permute-start(bf16[8,128,128]{2,1,0:T(8,128)(2,1)} %broadcast_select_fusion.2), channel_id=1, source_target_pairs={{1,5},{5,1},{25,29},{29,25},{2,6},{6,2},{26,30},{30,26}} | collective-permute-start | bytes 786440 | tf_op jit(solution)/shard_map/ppermute | solution.py:217
  172.1 1.4 copy-start.4
  173.5 0.9 copy-start.18
  182.2 0.7 copy-start.15
  182.9 24.5 %collective-permute-start.10 = (bf16[3,3,128,128]{3,2,1,0:T(8,128)(2,1)}, bf16[3,3,128,128]{3,2,1,0:T(8,128)(2,1)}, u32[]{:S(2)}, u32[]{:S(2)}) collective-permute-start(bf16[3,3,128,128]{3,2,1,0:T(8,128)(2,1)} %get-tuple-element.31), channel_id=1, source_target_pairs={{1,0},{2,1},{3,2},{5,4},{6,5},{7,6},{9,8},{10,9},{11,10},{13,12},{... | collective-permute-start | bytes 884744 | tf_op jit(solution)/shard_map/ppermute | solution.py:296
  184.8 26.2 %collective-permute-start.19 = (bf16[3,3,128,128]{3,2,1,0:T(8,128)(2,1)}, bf16[3,3,128,128]{3,2,1,0:T(8,128)(2,1)}, u32[]{:S(2)}, u32[]{:S(2)}) collective-permute-start(bf16[3,3,128,128]{3,2,1,0:T(8,128)(2,1)} %get-tuple-element.33), channel_id=1, source_target_pairs={{0,1},{1,2},{2,3},{4,5},{5,6},{6,7},{8,9},{9,10},{10,11},{12,13},{... | collective-permute-start | bytes 884744 | tf_op jit(solution)/shard_map/ppermute | solution.py:295
  188.5 24.6 %collective-permute-start.20 = (bf16[3,3,128,128]{3,2,1,0:T(8,128)(2,1)}, bf16[3,3,128,128]{3,2,1,0:T(8,128)(2,1)}, u32[]{:S(2)}, u32[]{:S(2)}) collective-permute-start(bf16[3,3,128,128]{3,2,1,0:T(8,128)(2,1)} %get-tuple-element.34), channel_id=1, source_target_pairs={{1,0},{2,1},{3,2},{5,4},{6,5},{7,6},{9,8},{10,9},{11,10},{13,12},{... | collective-permute-start | bytes 884744 | tf_op jit(solution)/shard_map/ppermute | solution.py:296
  192.9 1.4 copy-start.5
  199.3 8.1 %copy-start.21 = (bf16[2,3,128,128]{3,2,1,0:T(8,128)(2,1)}, bf16[2,3,128,128]{3,2,1,0:T(8,128)(2,1)S(1)}, u32[]{:S(2)}) copy-start(bf16[2,3,128,128]{3,2,1,0:T(8,128)(2,1)S(1)} %get-tuple-element.35.refs_9_) | copy-start | bytes 589828
  199.3 13.8 %collective-permute-start.27 = (bf16[2,3,128,128]{3,2,1,0:T(8,128)(2,1)}, bf16[2,3,128,128]{3,2,1,0:T(8,128)(2,1)S(1)}, u32[]{:S(2)}, u32[]{:S(2)}) collective-permute-start(bf16[2,3,128,128]{3,2,1,0:T(8,128)(2,1)} %get-tuple-element.36), channel_id=1, source_target_pairs={{0,1},{1,2},{2,3},{4,5},{5,6},{6,7},{8,9},{9,10},{10,11},{12,13},{... | collective-permute-start | bytes 589832 | tf_op jit(solution)/shard_map/ppermute | solution.py:295
  203.0 10.1 %collective-permute-start.28 = (bf16[2,3,128,128]{3,2,1,0:T(8,128)(2,1)}, bf16[2,3,128,128]{3,2,1,0:T(8,128)(2,1)S(1)}, u32[]{:S(2)}, u32[]{:S(2)}) collective-permute-start(bf16[2,3,128,128]{3,2,1,0:T(8,128)(2,1)} %get-tuple-element.37), channel_id=1, source_target_pairs={{1,0},{2,1},{3,2},{5,4},{6,5},{7,6},{9,8},{10,9},{11,10},{13,12},{... | collective-permute-start | bytes 589832 | tf_op jit(solution)/shard_map/ppermute | solution.py:296
  205.0 12.2 %copy-start.16 = (bf16[3,3,128,128]{3,2,1,0:T(8,128)(2,1)S(1)}, bf16[3,3,128,128]{3,2,1,0:T(8,128)(2,1)}, u32[]{:S(2)}) copy-start(bf16[3,3,128,128]{3,2,1,0:T(8,128)(2,1)} %copy-done.15) | copy-start | bytes 884740
  205.0 12.2 %copy-start.24 = (bf16[1,3,128,128]{3,2,1,0:T(8,128)(2,1)S(1)}, bf16[1,3,128,128]{3,2,1,0:T(8,128)(2,1)}, u32[]{:S(2)}) copy-start(bf16[1,3,128,128]{3,2,1,0:T(8,128)(2,1)} %copy-done.23) | copy-start | bytes 294916
  205.0 12.2 %copy-start.26 = (bf16[1,3,128,128]{3,2,1,0:T(8,128)(2,1)S(1)}, bf16[1,3,128,128]{3,2,1,0:T(8,128)(2,1)}, u32[]{:S(2)}) copy-start(bf16[1,3,128,128]{3,2,1,0:T(8,128)(2,1)} %copy-done.25) | copy-start | bytes 294916
  207.4 5.7 %collective-permute-start.31 = (bf16[1,3,128,128]{3,2,1,0:T(8,128)(2,1)}, bf16[1,3,128,128]{3,2,1,0:T(8,128)(2,1)S(1)}, u32[]{:S(2)}, u32[]{:S(2)}) collective-permute-start(bf16[1,3,128,128]{3,2,1,0:T(8,128)(2,1)} %get-tuple-element.39), channel_id=1, source_target_pairs={{0,1},{1,2},{2,3},{4,5},{5,6},{6,7},{8,9},{9,10},{10,11},{12,13},{... | collective-permute-start | bytes 294920 | tf_op jit(solution)/shard_map/ppermute | solution.py:295
  211.0 6.1 %collective-permute-start.32 = (bf16[1,3,128,128]{3,2,1,0:T(8,128)(2,1)}, bf16[1,3,128,128]{3,2,1,0:T(8,128)(2,1)S(1)}, u32[]{:S(2)}, u32[]{:S(2)}) collective-permute-start(bf16[1,3,128,128]{3,2,1,0:T(8,128)(2,1)} %get-tuple-element.40), channel_id=1, source_target_pairs={{1,0},{2,1},{3,2},{5,4},{6,5},{7,6},{9,8},{10,9},{11,10},{13,12},{... | collective-permute-start | bytes 294920 | tf_op jit(solution)/shard_map/ppermute | solution.py:296
  217.2 0.9 copy-start.22

commit v2 on v1

--- a/solution.py
+++ b/solution.py
@@ -63,27 +63,82 @@
     )(info, mask, prolong)
 
 
-def stage_kernel(layout, scalars, slot_rows, slot_cols, turned, *refs):
+def pick_kernel(plan, outputs, wanted, choice, *refs):
+    panels = len(refs) - 2 * outputs - 1
+    sources = max(max(options) for _, _, options in plan) + 1
+    heads, tails = refs[:sources], refs[sources:2 * sources]
+    out = refs[panels:panels + 2 * outputs]
+    done = refs[-1]
+    cap = wanted.shape[0] // len(plan)
+
+    def copies(request, option, entry):
+        target, base, options = plan[request]
+        row = wanted[request * cap + entry]
+        source = options[option]
+        return [
+            pltpu.make_async_copy(x.at[row], out[2 * target + part].at[base + entry], done.at[request, entry, part])
+            for part, x in enumerate((heads[source], tails[source]))]
+
+    for request, (_, _, options) in enumerate(plan):
+        for option in range(len(options)):
+            def begin(request=request, option=option):
+                for entry in range(cap):
+                    for copy in copies(request, option, entry):
+                        copy.start()
+            if len(options) == 1:
+                begin()
+            else:
+                pl.when(choice[request] == option)(begin)
+    for request in range(len(plan)):
+        for entry in range(cap):
+            for copy in copies(request, 0, entry):
+                copy.wait()
+
+
+def pick(plan, sizes, wanted, choice, pairs, after):
+    cap = wanted.shape[0] // len(plan)
+    heads, tails = [p[0] for p in pairs], [p[1] for p in pairs]
+    anywhere = pl.BlockSpec(memory_space=pl.ANY)
+    shapes = []
+    for size in sizes:
+        shapes += [jax.ShapeDtypeStruct((size, *x.shape[1:]), x.dtype) for x in pairs[0]]
+    moved = sum(2 * 2 * x.size for x in shapes)
+    result = pl.pallas_call(
+        functools.partial(pick_kernel, plan, len(sizes)),
+        grid_spec=pltpu.PrefetchScalarGridSpec(
+            num_scalar_prefetch=2,
+            grid=(1,),
+            in_specs=[anywhere] * (2 * len(pairs) + len(after)),
+            out_specs=[anywhere] * len(shapes),
+            scratch_shapes=[pltpu.SemaphoreType.DMA((len(plan), cap, 2))],
+        ),
+        out_shape=shapes,
+        compiler_params=pltpu.CompilerParams(vmem_limit_bytes=VMEM_LIMIT),
+        cost_estimate=pl.CostEstimate(flops=0, bytes_accessed=moved, transcendentals=0),
+        name="pick_rows",
+    )(wanted, choice, *heads, *tails, *after)
+    return [(result[2 * i], result[2 * i + 1]) for i in range(len(sizes))]
+
+
+def stage_kernel(layout, arrays, extra, scalars, slot_rows, slot_cols, turned, *refs):
     slots = len(layout)
-    sources = sum(len(s) for s in layout)
     matrix = refs[:slots]
-    heads = refs[slots:slots + sources]
-    tails = refs[slots + sources:slots + 2 * sources]
-    own, up, down, total = refs[slots + 2 * sources:]
+    heads = refs[slots:slots + arrays]
+    tails = refs[slots + arrays:slots + 2 * arrays]
+    own, up, down, total = refs[slots + 2 * arrays + extra:]
     cap = matrix[0].shape[1]
-    pores = matrix[0].shape[2]
     width = tails[0].shape[-1]
     turn = scalars[0]
     at = 0
-    for slot, kinds in enumerate(layout):
+    for slot, sources in enumerate(layout):
         panel = scalars[1 + slot]
         total[...] = jnp.zeros_like(total)
-        for whole in kinds:
+        for array, base, whole in sources:
             live = scalars[1 + slots + at]
-            head, tail = heads[at], tails[at]
-
-            def product(entry, whole=whole, head=head, tail=tail, slot=slot, panel=panel):
-                pick = slot_cols[panel * cap + entry] if whole else entry
+            head, tail = heads[array], tails[array]
+
+            def product(entry, whole=whole, base=base, head=head, tail=tail, slot=slot, panel=panel):
+                pick = slot_cols[panel * cap + entry] if whole else base + entry
                 right = jnp.concatenate([head[pick, 0], head[pick, 1], tail[pick]], axis=1)
                 return jnp.dot(matrix[slot][0, entry], right, preferred_element_type=jnp.float32)
 
@@ -115,11 +170,12 @@
             down[slot, f] = total[k, 0:width, :].astype(down.dtype)
 
 
-def stage(layout, scalars, slot_rows, slot_cols, turned, matrix, heads, tails):
+def stage(layout, scalars, slot_rows, slot_cols, turned, matrix, pairs, after):
     slots = len(layout)
     panels, cap, pores, _ = matrix.shape
     width3 = turned.shape[1]
     width = width3 // 3
+    heads, tails = [p[0] for p in pairs], [p[1] for p in pairs]
 
     def whole_spec(x):
         return pl.BlockSpec(x.shape, lambda i, *_, n=x.ndim: (0,) * n)
@@ -130,11 +186,12 @@
     flops = 2 * slots * 5 * (pores * pores * width3 + width3 * width3 * pores)
     size = sum(2 * x.size for x in (*heads, *tails)) + 2 * turned.size + 2 * slots * cap * pores * pores
     return pl.pallas_call(
-        functools.partial(stage_kernel, layout),
+        functools.partial(stage_kernel, layout, len(pairs), len(after)),
         grid_spec=pltpu.PrefetchScalarGridSpec(
             num_scalar_prefetch=3,
             grid=(1,),
-            in_specs=[whole_spec(turned), *matrix_specs, *map(whole_spec, heads), *map(whole_spec, tails)],
+            in_specs=[whole_spec(turned), *matrix_specs, *map(whole_spec, heads), *map(whole_spec, tails),
+                      *([pl.BlockSpec(memory_space=pl.ANY)] * len(after))],
             out_specs=[pl.BlockSpec(out.shape, lambda i, *_: (0, 0, 0, 0))] * 3,
             scratch_shapes=[pltpu.VMEM((3, width3, width), jnp.float32)],
         ),
@@ -142,7 +199,7 @@
         compiler_params=pltpu.CompilerParams(vmem_limit_bytes=VMEM_LIMIT),
         cost_estimate=pl.CostEstimate(flops=flops, bytes_accessed=size, transcendentals=0),
         name="stage_products",
-    )(scalars, slot_rows, slot_cols, turned, *([matrix] * slots), *heads, *tails)
+    )(scalars, slot_rows, slot_cols, turned, *([matrix] * slots), *heads, *tails, *after)
 
 
 def assemble_kernel(counts, panels, info, *refs):
@@ -198,6 +255,7 @@
     cols_list = block_cols[0, 0]
     count_list = block_counts[0, 0]
     prolong = prolong_blocks[0]
+    cap = cols_list.shape[1]
     panels = lax.axis_size("blk")
     groups = lax.axis_size("rows")
     lines, columns = grid_of(panels)
@@ -206,9 +264,10 @@
     z, y = place // columns, place % columns
     turn = (group == 0).astype(jnp.int32)
     flat_rows, flat_cols = rows_list.reshape(-1), cols_list.reshape(-1)
-
     every = range(groups)
     inner = range(1, groups - 1)
+    sides = range(1, columns)
+    relays = min(2, lines - 1)
 
     def move(x, pairs, members):
         perm = [(a * groups + g, b * groups + g) for g in members for a, b in pairs]
@@ -219,84 +278,103 @@
     def move_both(pair, pairs):
         return move(pair[0], pairs, every), move(pair[1], pairs, inner)
 
-    def line_pairs(s, sign):
+    def ways(s):
+        return [(1, -1)] if 2 * s >= lines else [(1,), (-1,)]
+
+    def far_pairs(s, signs, shift):
+        return [(h * columns + c, (h + sign * s) * columns + (c + shift) % columns)
+                for h in range(lines) for sign in signs if 0 <= h + sign * s < lines for c in range(columns)]
+
+    def relay_pairs(s, sign):
         return [(h * columns + c, (h + sign) * columns + c)
                 for h in range(lines) for c in range(columns)
                 if 0 <= h + sign < lines and 0 <= h + sign - sign * s < lines]
 
-    def across_pairs(shift, present):
-        return [(h * columns + c, h * columns + (c + shift) % columns)
-                for h in range(lines) if present(h) for c in range(columns)]
-
-    served = [move(cols_list, [(b, a) for a, b in across_pairs(shift, lambda h: True)], every)
-              for shift in range(1, columns)]
+    def back(pairs):
+        return [(b, a) for a, b in pairs]
+
+    def has(s, sign):
+        return (z + sign * s >= 0) & (z + sign * s < lines)
+
+    def panel_at(line, shift):
+        return jnp.clip(line, 0, lines - 1) * columns + (y - shift) % columns
+
+    def exchange(parts):
+        lower = lax.ppermute(parts[1], "rows", [(g, g + 1) for g in range(groups - 1)])
+        upper = lax.ppermute(parts[2], "rows", [(g + 1, g) for g in range(groups - 1)])
+        return parts[0], lower, upper
+
+    def run(work, pairs, after):
+        layout = tuple(tuple(source[:3] for source in sources) for _, _, sources in work)
+        lives = [jnp.where(ok, count_list[panel], 0) for panel, _, sources in work for *_, ok in sources]
+        scalars = jnp.stack([turn, *[panel for panel, _, _ in work], *lives]).astype(jnp.int32)
+        for panel, there, _ in work:
+            slot_panels.append(panel)
+            slot_present.append(there)
+        return stage(layout, scalars, flat_rows, flat_cols, turned, matrix, pairs, after)
+
+    slot_panels, slot_present, pieces = [], [], []
+    yes = jnp.bool_(True)
 
     info = jnp.stack([group, jnp.int32(groups), turn]).astype(jnp.int32)
     head, tail, turned = pack(info, prolong_mask[0].reshape(-1), prolong)
     own = (head, tail)
-
-    def has(s, sign):
-        source = z + sign * s
-        return (source >= 0) & (source < lines)
-
-    def picked(pair, line, shift):
-        wanted = lax.dynamic_index_in_dim(served[shift - 1], jnp.clip(line, 0, lines - 1) * columns + y, 0, False)
-        return tuple(x.at[wanted].get(mode="promise_in_bounds") for x in pair)
-
-    def entry(line, shift):
-        return jnp.clip(line, 0, lines - 1) * columns + (y - shift) % columns
-
-    merged = [2 * s > lines - 1 for s in range(lines)]
-    received = [[(z, jnp.bool_(True), [(own, jnp.bool_(True))])]]
-    below, above = own, own
-    crossing = []
-    pieces, slot_panels, slot_present = [], [], []
-    for s in range(lines + 1):
-        if 0 < s < lines:
-            below = move_both(below, line_pairs(s, 1))
-            above = move_both(above, line_pairs(s, -1))
-            has_below, has_above = has(s, -1), has(s, 1)
-            if merged[s]:
-                line = jnp.where(has_below, z - s, z + s)
-                received.append([(line, has_below | has_above, [(below, has_below), (above, has_above)])])
-            else:
-                received.append([(z - s, has_below, [(below, has_below)]), (z + s, has_above, [(above, has_above)])])
-        work = []
-        if s < lines:
-            work += [(entry(line, 0), there, [(p, ok, True) for p, ok in sources])
-                     for line, there, sources in received[s]]
-        if s > 0:
-            work += crossing
-        crossing = []
-        if s < lines:
-            for shift in range(1, columns):
-                for index, (line, there, sources) in enumerate(received[s]):
-                    pair = picked(sources[0][0], line, shift)
-                    if len(sources) == 2:
-                        other = picked(sources[1][0], line, shift)
-                        pair = tuple(jnp.where(sources[0][1], a, b) for a, b in zip(pair, other))
-                    if s == 0:
-                        present = lambda h: True
-                    elif merged[s]:
-                        present = lambda h: 0 <= h - s or h + s < lines
-                    else:
-                        present = (lambda h: 0 <= h - s) if index == 0 else (lambda h: h + s < lines)
-                    crossing.append((entry(line, shift), there,
-                                     [(move_both(pair, across_pairs(shift, present)), there, False)]))
-        if not work:
-            continue
-        layout = tuple(tuple(whole for _, _, whole in sources) for _, _, sources in work)
-        panel_of = [panel for panel, _, _ in work]
-        lives = [jnp.where(ok, count_list[panel], 0) for panel, _, sources in work for _, ok, _ in sources]
-        scalars = jnp.stack([turn, *panel_of, *lives]).astype(jnp.int32)
-        heads = [pair[0] for _, _, sources in work for pair, _, _ in sources]
-        tails = [pair[1] for _, _, sources in work for pair, _, _ in sources]
-        mine, up, down = stage(layout, scalars, flat_rows, flat_cols, turned, matrix, heads, tails)
-        lower = lax.ppermute(up, "rows", [(g, g + 1) for g in range(groups - 1)])
-        upper = lax.ppermute(down, "rows", [(g + 1, g) for g in range(groups - 1)])
-        pieces.append((mine, lower, upper))
-        slot_panels += panel_of
-        slot_present += [there.astype(jnp.int32) for _, there, _ in work]
+    near = [move_both(own, relay_pairs(1, 1)), move_both(own, relay_pairs(1, -1))]
+    beside = [move_both(own, far_pairs(0, (1,), shift)) for shift in sides]
+    side_lists = [move(cols_list, back(far_pairs(0, (1,), shift)), every) for shift in sides]
+    far = [(s, signs, shift) for s in range(relays + 1, lines) for signs in ways(s) for shift in range(columns)]
+    far_lists = [move(cols_list, back(far_pairs(*entry)), every) for entry in far]
+    parts = run([(place, yes, [(0, 0, True, yes)])], [own], [*side_lists, *far_lists])
+    pieces.append(exchange(parts))
+
+    next_up = move_both(near[0], relay_pairs(2, 1))
+    next_down = move_both(near[1], relay_pairs(2, -1))
+    plan, wanted = [], []
+    for index, shift in enumerate(sides):
+        for side, line in enumerate((z - 1, z + 1)):
+            plan.append((index, side * cap, (side,)))
+            wanted.append(lax.dynamic_index_in_dim(side_lists[index], panel_at(line, 0), 0, False))
+    picked = pick(tuple(plan), [2 * cap] * len(sides), jnp.concatenate(wanted), jnp.zeros((len(plan),), jnp.int32),
+                  near, pieces[-1][1:])
+    crossed = [move_both(pair, far_pairs(0, (1,), shift)) for pair, shift in zip(picked, sides)]
+    work = [(panel_at(z - 1, 0), has(1, -1), [(0, 0, True, has(1, -1))]),
+            (panel_at(z + 1, 0), has(1, 1), [(1, 0, True, has(1, 1))])]
+    work += [(panel_at(z, shift), yes, [(2 + i, 0, True, yes)]) for i, shift in enumerate(sides)]
+    parts = run(work, [*near, *beside], [])
+    pieces.append(exchange(parts))
+
+    from_below = has(2, -1)
+    second = jnp.where(from_below, z - 2, z + 2)
+    second_there = from_below | has(2, 1)
+    plan, wanted, choice = [], [], []
+    for index, shift in enumerate(sides):
+        plan.append((index, 0, (0, 1)))
+        wanted.append(lax.dynamic_index_in_dim(side_lists[index], panel_at(second, 0), 0, False))
+        choice.append(jnp.where(from_below, 0, 1))
+    for index in range(len(far)):
+        plan.append((len(sides) + index, 0, (2,)))
+        wanted.append(lax.dynamic_index_in_dim(far_lists[index], place, 0, False))
+        choice.append(0)
+    picked = pick(tuple(plan), [cap] * len(plan), jnp.concatenate(wanted), jnp.stack(choice).astype(jnp.int32),
+                  [next_up, next_down, own], pieces[-1][1:])
+    second_crossed = [move_both(pair, far_pairs(0, (1,), shift)) for pair, shift in zip(picked, sides)]
+    far_crossed = [move_both(pair, far_pairs(*entry)) for pair, entry in zip(picked[len(sides):], far)]
+    work = [(panel_at(second, 0), second_there, [(0, 0, True, from_below), (1, 0, True, has(2, 1))])]
+    for i, shift in enumerate(sides):
+        work += [(panel_at(z - 1, shift), has(1, -1), [(2 + i, 0, False, has(1, -1))]),
+                 (panel_at(z + 1, shift), has(1, 1), [(2 + i, cap, False, has(1, 1))])]
+    parts = run(work, [next_up, next_down, *crossed], [])
+    pieces.append(exchange(parts))
+
+    work = [(panel_at(second, shift), second_there, [(i, 0, False, second_there)]) for i, shift in enumerate(sides)]
+    for i, (s, signs, shift) in enumerate(far):
+        present = [has(s, -sign) for sign in signs]
+        line = jnp.where(present[0], z - signs[0] * s, z - signs[-1] * s)
+        there = functools.reduce(jnp.logical_or, present)
+        work.append((panel_at(line, shift), there, [(len(sides) + i, 0, False, there)]))
+    parts = run(work, [*second_crossed, *far_crossed], pieces[-1][1:])
+    pieces.append(exchange(parts))
+
     where = jnp.stack([*slot_panels, *slot_present]).astype(jnp.int32)
     return assemble(where, pieces, panels)[None, None]
 

time: 225 us -> 264 us (1.17)
  the two profiles are of different devices: /device:TPU:21 before, /device:TPU:1 now
where the time goes in v2:
time: 264 us; the launch traced here: 261 us
  Pallas kernels  109 us (41%)
  starting transfers between devices  75 us (28%)
  waiting for transfers between devices  40.1 us (15%)
  local copies, waits for them, and re-layouts  29.1 us (11%)
  between operations  6.36 us (2%)
    pallas_call x2, Pallas kernels, pick(): pl.pallas_call(functools.partial(pick_kernel, plan, len(sizes)), grid_spe...  83.5 us
    ppermute x21, starting transfers between devices, move(): return lax.ppermute(x, ('blk', 'rows'), perm)  53.1 us
    unnamed x63, local copies, waits for them, and re-layouts  24.2 us
    ppermute x21, waiting for transfers between devices, move(): return lax.ppermute(x, ('blk', 'rows'), perm)  21.6 us
    pallas_call x4, Pallas kernels, stage(): pl.pallas_call(functools.partial(stage_kernel, layout, len(pairs), len(af...  20.2 us
    ppermute x4, waiting for transfers between devices, exchange(): lax.ppermute(parts[2], 'rows', [(g + 1, g) for g in range(groups - 1)])  15.1 us
    ppermute x4, starting transfers between devices, exchange(): lax.ppermute(parts[1], 'rows', [(g, g + 1) for g in range(groups - 1)])  13.8 us
    ppermute x4, starting transfers between devices, exchange(): lax.ppermute(parts[2], 'rows', [(g + 1, g) for g in range(groups - 1)])  8.16 us
  transfers between devices with their start and end apart: 29, of which 8 were waited for; matrix products, arithmetic and copies ran while one was open for 2% of the time, Pallas kernels for 38%

profile of v2, /device:TPU:1, one launch (start us, length us, event | category | flops | bytes accessed | tf_op | source)
XLA Modules:
  0.0 261.4 jit_solution(15188410196083813698)
XLA Ops:
  0.0 0.8 copy.8
  0.9 1.4 copy-done.6
  2.3 2.5 pack_rows.1
  4.9 1.3 collective-permute-start.6
  6.1 5.6 %collective-permute-start.5 = (bf16[16,2,128,128]{3,2,1,0:T(8,128)(2,1)}, bf16[16,2,128,128]{3,2,1,0:T(8,128)(2,1)}, u32[]{:S(2)}, u32[]{:S(2)}) collective-permute-start(bf16[16,2,128,128]{3,2,1,0:T(8,128)(2,1)} %get-tuple-element.29.refs_1_.refs_2_), channel_id=1, source_target_pairs={{0,8},{4,12},{8,16},{12,20},{16,24},{20,28},{1,9},{5,13},{9,17},{1... | collective-permute-start | bytes 3145736 | tf_op jit(solution)/shard_map/ppermute | solution.py:276
  11.8 3.5 %collective-permute-start.2 = (s32[8,8]{1,0:T(8,128)}, s32[8,8]{1,0:T(8,128)S(1)}, u32[]{:S(2)}, u32[]{:S(2)}) collective-permute-start(s32[8,8]{1,0:T(8,128)} %bitcast.69), channel_id=1, source_target_pairs={{28,0},{24,4},{4,24},{0,28},{29,1},{25,5},{5,25},{1,29},{30,2},{26... | collective-permute-start | bytes 776 | tf_op jit(solution)/shard_map/ppermute | solution.py:276
  15.3 4.7 %collective-permute-start.1 = (s32[8,8]{1,0:T(8,128)}, s32[8,8]{1,0:T(8,128)S(1)}, u32[]{:S(2)}, u32[]{:S(2)}) collective-permute-start(s32[8,8]{1,0:T(8,128)} %bitcast.70), channel_id=1, source_target_pairs={{24,0},{28,4},{0,24},{4,28},{25,1},{29,5},{1,25},{5,29},{26,2},{30... | collective-permute-start | bytes 776 | tf_op jit(solution)/shard_map/ppermute | solution.py:276
  20.2 1.7 constant_dynamic-slice_fusion.3
  22.0 12.6 %collective-permute-done.2.refs_5_ = s32[8,8]{1,0:T(8,128)S(1)} collective-permute-done((s32[8,8]{1,0:T(8,128)}, s32[8,8]{1,0:T(8,128)S(1)}, u32[]{:S(2)}, u32[]{:S(2)}) %collective-permute-start.2) | collective-permute-done | bytes 288 | tf_op jit(solution)/shard_map/ppermute | solution.py:276
  34.6 2.1 collective-permute-start.10
  37.4 0.8 reshape_squeeze.10.slot_cols
  38.2 0.8 reshape_squeeze.9.slot_rows
  39.0 1.6 copy-done
  40.6 2.9 %stage_products.4 = (bf16[1,3,128,128]{3,2,1,0:T(8,128)(2,1)S(1)}, bf16[1,3,128,128]{3,2,1,0:T(8,128)(2,1)S(1)}, bf16[1,3,128,128]{3,2,1,0:T(8,128)(2,1)S(1)}) custom-call(s32[3]{0:T(128)S(1)} %pad_add_fusion.scalars, s32[64]{0:T(128)S(1)} %reshape_squeeze.9.slot_rows, s32[64]{0:T(128)S(1)} %reshape_squeeze.10.slot_cols, ...), custom_call_target="tpu_custom_call" | custom-call | flops 251658240 | bytes 3407872 | tf_op jit(solution)/shard_map/stage_products/pallas_call | solution.py:188
  43.5 1.1 copy-done.2
  44.6 4.8 %collective-permute-start.3 = (bf16[1,3,128,128]{3,2,1,0:T(8,128)(2,1)S(1)}, bf16[1,3,128,128]{3,2,1,0:T(8,128)(2,1)S(1)}, u32[]{:S(2)}, u32[]{:S(2)}) collective-permute-start(bf16[1,3,128,128]{3,2,1,0:T(8,128)(2,1)S(1)} %get-tuple-element.32), channel_id=1, source_target_pairs={{0,1},{1,2},{2,3},{4,5},{5,6},{6,7},{8,9},{9,10},{10,11},{12,13},{... | collective-permute-start | bytes 294920 | tf_op jit(solution)/shard_map/ppermute | solution.py:303
  49.5 1.7 collective-permute-start.7
  51.2 1.9 collective-permute-start.4
  53.1 4.8 %collective-permute-done.4.refs_5_.refs_2_ = bf16[1,3,128,128]{3,2,1,0:T(8,128)(2,1)S(1)} collective-permute-done((bf16[1,3,128,128]{3,2,1,0:T(8,128)(2,1)S(1)}, bf16[1,3,128,128]{3,2,1,0:T(8,128)(2,1)S(1)}, u32[]{:S(2)}, u32[]{:S(2)}) %collective-permute-start.4) | collective-permute-done | bytes 98336 | tf_op jit(solution)/shard_map/ppermute | solution.py:304
  58.0 1.3 collective-permute-start.9
  59.3 4.8 %collective-permute-start.8 = (bf16[16,128,128]{2,1,0:T(8,128)(2,1)}, bf16[16,128,128]{2,1,0:T(8,128)(2,1)}, u32[]{:S(2)}, u32[]{:S(2)}) collective-permute-start(bf16[16,128,128]{2,1,0:T(8,128)(2,1)} %get-tuple-element.30.refs_2_.refs_5_), channel_id=1, source_target_pairs={{1,9},{5,13},{9,17},{13,21},{17,25},{21,29},{2,10},{6,14},{10,18},... | collective-permute-start | bytes 1572872 | tf_op jit(solution)/shard_map/ppermute | solution.py:276
  64.1 8.9 %collective-permute-done.9.refs_7_.refs_3_ = bf16[16,128,128]{2,1,0:T(8,128)(2,1)} collective-permute-done((bf16[16,128,128]{2,1,0:T(8,128)(2,1)}, bf16[16,128,128]{2,1,0:T(8,128)(2,1)}, u32[]{:S(2)}, u32[]{:S(2)}) %collective-permute-start.9) | collective-permute-done | bytes 524320 | tf_op jit(solution)/shard_map/ppermute | solution.py:276
  73.0 1.3 collective-permute-start.17
  74.3 1.3 collective-permute-start.14
  75.6 1.7 collective-permute-start.13
  77.8 1.4 collective-permute-start.16
  79.3 17.8 %pick_rows.2 = (bf16[16,2,128,128]{3,2,1,0:T(8,128)(2,1)}, bf16[16,128,128]{2,1,0:T(8,128)(2,1)S(1)}) custom-call(s32[16]{0:T(128)S(1)} %pad_add_fusion.2.wanted, s32[2]{0:T(128)S(1)} %broadcast_1_choice.2.choice, bf16[16,2,128,128]{3,2,1,0:T(8,128)(2,1)} %collective-permute-done.5.refs_3_.refs_0_, ...), custom_call_target="tpu_custom_call" | custom-call | bytes 3145728 | tf_op jit(solution)/shard_map/pick_rows/pallas_call | solution.py:106
  97.2 1.0 copy-done.9
  98.3 1.8 collective-permute-start.15
  102.2 1.4 copy-done.3
  103.6 1.2 copy-done.10
  104.8 6.3 %stage_products.5 = (bf16[3,3,128,128]{3,2,1,0:T(8,128)(2,1)S(1)}, bf16[3,3,128,128]{3,2,1,0:T(8,128)(2,1)}, bf16[3,3,128,128]{3,2,1,0:T(8,128)(2,1)S(1)}) custom-call(s32[7]{0:T(128)S(1)} %stack.166.scalars, s32[64]{0:T(128)S(1)} %reshape_squeeze.9.slot_rows, s32[64]{0:T(128)S(1)} %reshape_squeeze.10.slot_cols, bf16[16,384,128]{2,1,0:T(8,128)(2,1)S(1)} %copy-done.3, ...), custom_call_target="tpu_custom_call" | custom-call | flops 754974720 | bytes 7077888 | tf_op jit(solution)/shard_map/stage_products/pallas_call | solution.py:188
  112.5 1.9 collective-permute-start.11
  114.5 2.4 collective-permute-start.12
  116.9 1.5 collective-permute-done.11.refs_6_.refs_4_
  118.4 1.9 collective-permute-start.18
  121.0 1.7 collective-permute-done.12.refs_7_.refs_5_
  122.7 65.6 %pick_rows.3 = (bf16[8,2,128,128]{3,2,1,0:T(8,128)(2,1)}, bf16[8,128,128]{2,1,0:T(8,128)(2,1)S(1)}, bf16[8,2,128,128]{3,2,1,0:T(8,128)(2,1)}, bf16[8,128,128]{2,...) custom-call(s32[24]{0:T(128)S(1)} %pad_add_fusion.3.wanted, s32[3]{0:T(128)S(1)} %stack.177.choice, ...), custom_call_target="tpu_custom_call" | custom-call | bytes 4718592 | tf_op jit(solution)/shard_map/pick_rows/pallas_call | solution.py:106
  188.4 1.9 collective-permute-start.24
  190.3 3.1 %collective-permute-start.25 = (bf16[8,128,128]{2,1,0:T(8,128)(2,1)}, bf16[8,128,128]{2,1,0:T(8,128)(2,1)S(1)}, u32[]{:S(2)}, u32[]{:S(2)}) collective-permute-start(bf16[8,128,128]{2,1,0:T(8,128)(2,1)} %get-tuple-element.46), channel_id=1, source_target_pairs={{1,25},{5,29},{25,1},{29,5},{2,26},{6,30},{26,2},{30,6}} | collective-permute-start | bytes 786440 | tf_op jit(solution)/shard_map/ppermute | solution.py:276
  193.5 5.1 %collective-permute-start.26 = (bf16[8,128,128]{2,1,0:T(8,128)(2,1)}, bf16[8,128,128]{2,1,0:T(8,128)(2,1)S(1)}, u32[]{:S(2)}, u32[]{:S(2)}) collective-permute-start(bf16[8,128,128]{2,1,0:T(8,128)(2,1)} %get-tuple-element.47), channel_id=1, source_target_pairs={{1,29},{5,25},{25,5},{29,1},{2,30},{6,26},{26,6},{30,2}} | collective-permute-start | bytes 786440 | tf_op jit(solution)/shard_map/ppermute | solution.py:276
  198.6 0.8 copy-done.11
  199.4 3.1 %collective-permute-start.22 = (bf16[8,2,128,128]{3,2,1,0:T(8,128)(2,1)}, bf16[8,2,128,128]{3,2,1,0:T(8,128)(2,1)}, u32[]{:S(2)}, u32[]{:S(2)}) collective-permute-start(bf16[8,2,128,128]{3,2,1,0:T(8,128)(2,1)} %get-tuple-element.43), channel_id=1, source_target_pairs={{0,24},{4,28},{24,0},{28,4},{1,25},{5,29},{25,1},{29,5},{2,26},{6,... | collective-permute-start | bytes 1572872 | tf_op jit(solution)/shard_map/ppermute | solution.py:276
  202.6 5.1 %collective-permute-start.23 = (bf16[8,2,128,128]{3,2,1,0:T(8,128)(2,1)}, bf16[8,2,128,128]{3,2,1,0:T(8,128)(2,1)}, u32[]{:S(2)}, u32[]{:S(2)}) collective-permute-start(bf16[8,2,128,128]{3,2,1,0:T(8,128)(2,1)} %get-tuple-element.44), channel_id=1, source_target_pairs={{0,28},{4,24},{24,4},{28,0},{1,29},{5,25},{25,5},{29,1},{2,30},{6,... | collective-permute-start | bytes 1572872 | tf_op jit(solution)/shard_map/ppermute | solution.py:276
  210.4 1.4 copy-done.4
  211.8 1.0 copy-done.12
  212.8 6.4 %stage_products.6 = (bf16[3,3,128,128]{3,2,1,0:T(8,128)(2,1)S(1)}, bf16[3,3,128,128]{3,2,1,0:T(8,128)(2,1)}, bf16[3,3,128,128]{3,2,1,0:T(8,128)(2,1)}) custom-call(s32[8]{0:T(128)S(1)} %stack.171.scalars, s32[64]{0:T(128)S(1)} %reshape_squeeze.9.slot_rows, s32[64]{0:T(128)S(1)} %reshape_squeeze.10.slot_cols, bf16[16,384,128]{2,1,0:T(8,128)(2,1)S(1)} %copy-done.4, ...), custom_call_target="tpu_custom_call" | custom-call | flops 754974720 | bytes 7077888 | tf_op jit(solution)/shard_map/stage_products/pallas_call | solution.py:188
  220.6 3.4 %collective-permute-start.19 = (bf16[3,3,128,128]{3,2,1,0:T(8,128)(2,1)}, bf16[3,3,128,128]{3,2,1,0:T(8,128)(2,1)S(1)}, u32[]{:S(2)}, u32[]{:S(2)}) collective-permute-start(bf16[3,3,128,128]{3,2,1,0:T(8,128)(2,1)} %get-tuple-element.40), channel_id=1, source_target_pairs={{0,1},{1,2},{2,3},{4,5},{5,6},{6,7},{8,9},{9,10},{10,11},{12,13},{... | collective-permute-start | bytes 884744 | tf_op jit(solution)/shard_map/ppermute | solution.py:303
  224.7 1.9 collective-permute-start.20
  228.7 4.3 %collective-permute-done.20.refs_10_.refs_8_ = bf16[3,3,128,128]{3,2,1,0:T(8,128)(2,1)S(1)} collective-permute-done((bf16[3,3,128,128]{3,2,1,0:T(8,128)(2,1)}, bf16[3,3,128,128]{3,2,1,0:T(8,128)(2,1)S(1)}, u32[]{:S(2)}, u32[]{:S(2)}) %collective-permute-start.20) | collective-permute-done | bytes 294944 | tf_op jit(solution)/shard_map/ppermute | solution.py:304
  233.0 1.4 copy-done.5
  234.4 0.9 copy-done.22
  235.3 0.9 copy-done.24
  236.3 0.9 copy-done.26
  237.2 4.7 %stage_products.7 = (bf16[3,3,128,128]{3,2,1,0:T(8,128)(2,1)S(1)}, bf16[3,3,128,128]{3,2,1,0:T(8,128)(2,1)}, bf16[3,3,128,128]{3,2,1,0:T(8,128)(2,1)}) custom-call(s32[7]{0:T(128)S(1)} %stack.175.scalars, s32[64]{0:T(128)S(1)} %reshape_squeeze.9.slot_rows, s32[64]{0:T(128)S(1)} %reshape_squeeze.10.slot_cols, bf16[16,384,128]{2,1,0:T(8,128)(2,1)S(1)} %copy-done.5, ...), custom_call_target="tpu_custom_call" | custom-call | flops 754974720 | bytes 4718592 | tf_op jit(solution)/shard_map/stage_products/pallas_call | solution.py:188
  242.6 3.6 %collective-permute-start.27 = (bf16[3,3,128,128]{3,2,1,0:T(8,128)(2,1)}, bf16[3,3,128,128]{3,2,1,0:T(8,128)(2,1)S(1)}, u32[]{:S(2)}, u32[]{:S(2)}) collective-permute-start(bf16[3,3,128,128]{3,2,1,0:T(8,128)(2,1)} %get-tuple-element.49), channel_id=1, source_target_pairs={{0,1},{1,2},{2,3},{4,5},{5,6},{6,7},{8,9},{9,10},{10,11},{12,13},{... | collective-permute-start | bytes 884744 | tf_op jit(solution)/shard_map/ppermute | solution.py:303
  246.3 1.9 collective-permute-start.28
  248.3 1.9 collective-permute-done.27.refs_10_
  250.2 4.3 %collective-permute-done.28.refs_11_ = bf16[3,3,128,128]{3,2,1,0:T(8,128)(2,1)S(1)} collective-permute-done((bf16[3,3,128,128]{3,2,1,0:T(8,128)(2,1)}, bf16[3,3,128,128]{3,2,1,0:T(8,128)(2,1)S(1)}, u32[]{:S(2)}, u32[]{:S(2)}) %collective-permute-start.28) | collective-permute-done | bytes 294944 | tf_op jit(solution)/shard_map/ppermute | solution.py:304
  254.5 1.0 copy-done.16
  255.5 1.0 copy-done.18
  256.4 1.0 copy-done.20
  257.4 0.9 copy-done.28
  258.3 3.1 %assemble_coarse.1 = f32[5120,128]{1,0:T(8,128)} custom-call(s32[20]{0:T(128)S(1)} %stack.156.info, bf16[1,3,128,128]{3,2,1,0:T(8,128)(2,1)S(1)} %copy-done.28, bf16[1,3,128,128]{3,2,1,0:T(8,128)(2,1)S(1)} %collective-permute-done.3.refs_4_.refs_1_, bf16[1,3,128,128]{3,2,1,0:T(8,128)(2,1)S(1)} %copy-done.14, bf16[3,3,128,128]{3,2,1,0:T(8,128)(2,1)S(1)} %copy-done.16, ...), custom_call_target="tpu_custom_call" | custom-call | bytes 8388608 | tf_op jit(solution)/shard_map/assemble_coarse/pallas_call | solution.py:236
  (82 shorter events, 7.8 us)
Async XLA Ops:
  0.9 1.4 copy-start.6
  4.9 69.4 %collective-permute-start.6 = (bf16[16,2,128,128]{3,2,1,0:T(8,128)(2,1)}, bf16[16,2,128,128]{3,2,1,0:T(8,128)(2,1)S(1)}, u32[]{:S(2)}, u32[]{:S(2)}) collective-permute-start(bf16[16,2,128,128]{3,2,1,0:T(8,128)(2,1)} %get-tuple-element.29.refs_1_.refs_2_), channel_id=1, source_target_pairs={{8,0},{12,4},{16,8},{20,12},{24,16},{28,20},{9,1},{13,5},{17,9},{2... | collective-permute-start | bytes 3145736 | tf_op jit(solution)/shard_map/ppermute | solution.py:276
  6.1 69.4 %collective-permute-start.5 = (bf16[16,2,128,128]{3,2,1,0:T(8,128)(2,1)}, bf16[16,2,128,128]{3,2,1,0:T(8,128)(2,1)}, u32[]{:S(2)}, u32[]{:S(2)}) collective-permute-start(bf16[16,2,128,128]{3,2,1,0:T(8,128)(2,1)} %get-tuple-element.29.refs_1_.refs_2_), channel_id=1, source_target_pairs={{0,8},{4,12},{8,16},{12,20},{16,24},{20,28},{1,9},{5,13},{9,17},{1... | collective-permute-start | bytes 3145736 | tf_op jit(solution)/shard_map/ppermute | solution.py:276
  11.8 22.8 %collective-permute-start.2 = (s32[8,8]{1,0:T(8,128)}, s32[8,8]{1,0:T(8,128)S(1)}, u32[]{:S(2)}, u32[]{:S(2)}) collective-permute-start(s32[8,8]{1,0:T(8,128)} %bitcast.69), channel_id=1, source_target_pairs={{28,0},{24,4},{4,24},{0,28},{29,1},{25,5},{5,25},{1,29},{30,2},{26... | collective-permute-start | bytes 776 | tf_op jit(solution)/shard_map/ppermute | solution.py:276
  15.3 23.7 %collective-permute-start.1 = (s32[8,8]{1,0:T(8,128)}, s32[8,8]{1,0:T(8,128)S(1)}, u32[]{:S(2)}, u32[]{:S(2)}) collective-permute-start(s32[8,8]{1,0:T(8,128)} %bitcast.70), channel_id=1, source_target_pairs={{24,0},{28,4},{0,24},{4,28},{25,1},{29,5},{1,25},{5,29},{26,2},{30... | collective-permute-start | bytes 776 | tf_op jit(solution)/shard_map/ppermute | solution.py:276
  20.0 19.0 %collective-permute-start = (s32[8,8]{1,0:T(8,128)}, s32[8,8]{1,0:T(8,128)S(1)}, u32[]{:S(2)}, u32[]{:S(2)}) collective-permute-start(s32[8,8]{1,0:T(8,128)} %bitcast.71), channel_id=1, source_target_pairs={{4,0},{0,4},{12,8},{8,12},{20,16},{16,20},{28,24},{24,28},{5,1},{1... | collective-permute-start | bytes 776 | tf_op jit(solution)/shard_map/ppermute | solution.py:276
  34.6 24.7 %collective-permute-start.10 = (bf16[16,128,128]{2,1,0:T(8,128)(2,1)}, bf16[16,128,128]{2,1,0:T(8,128)(2,1)}, u32[]{:S(2)}, u32[]{:S(2)}) collective-permute-start(bf16[16,128,128]{2,1,0:T(8,128)(2,1)} %get-tuple-element.30.refs_2_.refs_5_), channel_id=1, source_target_pairs={{1,5},{5,1},{9,13},{13,9},{17,21},{21,17},{25,29},{29,25},{2,6},{6... | collective-permute-start | bytes 1572872 | tf_op jit(solution)/shard_map/ppermute | solution.py:276
  39.0 1.6 copy-start
  43.5 1.1 copy-start.2
  44.6 53.6 %copy-start.27 = (bf16[1,3,128,128]{3,2,1,0:T(8,128)(2,1)}, bf16[1,3,128,128]{3,2,1,0:T(8,128)(2,1)S(1)}, u32[]{:S(2)}) copy-start(bf16[1,3,128,128]{3,2,1,0:T(8,128)(2,1)S(1)} %get-tuple-element.31.refs_0_) | copy-start | bytes 294916
  44.6 57.6 %copy-start.1 = (bf16[1,1,8,8,128,128]{5,4,3,2,1,0:T(8,128)(2,1)S(1)}, bf16[1,1,8,8,128,128]{5,4,3,2,1,0:T(8,128)(2,1)}, u32[]{:S(2)}) copy-start(bf16[1,1,8,8,128,128]{5,4,3,2,1,0:T(8,128)(2,1)} %param.6) | copy-start | bytes 6291460
  44.6 6.6 %collective-permute-start.3 = (bf16[1,3,128,128]{3,2,1,0:T(8,128)(2,1)S(1)}, bf16[1,3,128,128]{3,2,1,0:T(8,128)(2,1)S(1)}, u32[]{:S(2)}, u32[]{:S(2)}) collective-permute-start(bf16[1,3,128,128]{3,2,1,0:T(8,128)(2,1)S(1)} %get-tuple-element.32), channel_id=1, source_target_pairs={{0,1},{1,2},{2,3},{4,5},{5,6},{6,7},{8,9},{9,10},{10,11},{12,13},{... | collective-permute-start | bytes 294920 | tf_op jit(solution)/shard_map/ppermute | solution.py:303
  49.5 47.7 %collective-permute-start.7 = (bf16[16,2,128,128]{3,2,1,0:T(8,128)(2,1)}, bf16[16,2,128,128]{3,2,1,0:T(8,128)(2,1)S(1)}, u32[]{:S(2)}, u32[]{:S(2)}) collective-permute-start(bf16[16,2,128,128]{3,2,1,0:T(8,128)(2,1)} %get-tuple-element.29.refs_1_.refs_2_), channel_id=1, source_target_pairs={{0,4},{4,0},{8,12},{12,8},{16,20},{20,16},{24,28},{28,24},{1,5},{5... | collective-permute-start | bytes 3145736 | tf_op jit(solution)/shard_map/ppermute | solution.py:276
  51.2 6.8 %collective-permute-start.4 = (bf16[1,3,128,128]{3,2,1,0:T(8,128)(2,1)S(1)}, bf16[1,3,128,128]{3,2,1,0:T(8,128)(2,1)S(1)}, u32[]{:S(2)}, u32[]{:S(2)}) collective-permute-start(bf16[1,3,128,128]{3,2,1,0:T(8,128)(2,1)S(1)} %get-tuple-element.33), channel_id=1, source_target_pairs={{1,0},{2,1},{3,2},{5,4},{6,5},{7,6},{9,8},{10,9},{11,10},{13,12},{... | collective-permute-start | bytes 294920 | tf_op jit(solution)/shard_map/ppermute | solution.py:304
  58.0 39.2 %copy-start.13 = (bf16[1,3,128,128]{3,2,1,0:T(8,128)(2,1)}, bf16[1,3,128,128]{3,2,1,0:T(8,128)(2,1)S(1)}, u32[]{:S(2)}) copy-start(bf16[1,3,128,128]{3,2,1,0:T(8,128)(2,1)S(1)} %collective-permute-done.4.refs_5_.refs_2_) | copy-start | bytes 294916
  58.0 15.0 %collective-permute-start.9 = (bf16[16,128,128]{2,1,0:T(8,128)(2,1)}, bf16[16,128,128]{2,1,0:T(8,128)(2,1)}, u32[]{:S(2)}, u32[]{:S(2)}) collective-permute-start(bf16[16,128,128]{2,1,0:T(8,128)(2,1)} %get-tuple-element.30.refs_2_.refs_5_), channel_id=1, source_target_pairs={{9,1},{13,5},{17,9},{21,13},{25,17},{29,21},{10,2},{14,6},{18,10},... | collective-permute-start | bytes 1572872 | tf_op jit(solution)/shard_map/ppermute | solution.py:276
  59.3 18.5 %collective-permute-start.8 = (bf16[16,128,128]{2,1,0:T(8,128)(2,1)}, bf16[16,128,128]{2,1,0:T(8,128)(2,1)}, u32[]{:S(2)}, u32[]{:S(2)}) collective-permute-start(bf16[16,128,128]{2,1,0:T(8,128)(2,1)} %get-tuple-element.30.refs_2_.refs_5_), channel_id=1, source_target_pairs={{1,9},{5,13},{9,17},{13,21},{17,25},{21,29},{2,10},{6,14},{10,18},... | collective-permute-start | bytes 1572872 | tf_op jit(solution)/shard_map/ppermute | solution.py:276
  73.0 38.9 %collective-permute-start.17 = (bf16[16,128,128]{2,1,0:T(8,128)(2,1)}, bf16[16,128,128]{2,1,0:T(8,128)(2,1)}, u32[]{:S(2)}, u32[]{:S(2)}) collective-permute-start(bf16[16,128,128]{2,1,0:T(8,128)(2,1)} %collective-permute-done.9.refs_7_.refs_3_), channel_id=1, source_target_pairs={{9,1},{13,5},{17,9},{21,13},{10,2},{14,6},{18,10},{22,14}} | collective-permute-start | bytes 1572872 | tf_op jit(solution)/shard_map/ppermute | solution.py:276
  74.3 48.5 %collective-permute-start.14 = (bf16[16,2,128,128]{3,2,1,0:T(8,128)(2,1)S(1)}, bf16[16,2,128,128]{3,2,1,0:T(8,128)(2,1)}, u32[]{:S(2)}, u32[]{:S(2)}) collective-permute-start(bf16[16,2,128,128]{3,2,1,0:T(8,128)(2,1)S(1)} %collective-permute-done.6.refs_4_.refs_1_), channel_id=1, source_target_pairs={{8,0},{12,4},{16,8},{20,12},{9,1},{13,5},{17,9},{21,13},{10,2},{14... | collective-permute-start | bytes 3145736 | tf_op jit(solution)/shard_map/ppermute | solution.py:276
  75.6 47.2 %collective-permute-start.13 = (bf16[16,2,128,128]{3,2,1,0:T(8,128)(2,1)}, bf16[16,2,128,128]{3,2,1,0:T(8,128)(2,1)}, u32[]{:S(2)}, u32[]{:S(2)}) collective-permute-start(bf16[16,2,128,128]{3,2,1,0:T(8,128)(2,1)} %collective-permute-done.5.refs_3_.refs_0_), channel_id=1, source_target_pairs={{8,16},{12,20},{16,24},{20,28},{9,17},{13,21},{17,25},{21,29},{10,... | collective-permute-start | bytes 3145736 | tf_op jit(solution)/shard_map/ppermute | solution.py:276
  77.8 36.7 %collective-permute-start.16 = (bf16[16,128,128]{2,1,0:T(8,128)(2,1)}, bf16[16,128,128]{2,1,0:T(8,128)(2,1)}, u32[]{:S(2)}, u32[]{:S(2)}) collective-permute-start(bf16[16,128,128]{2,1,0:T(8,128)(2,1)} %collective-permute-done.8.refs_6_.refs_2_), channel_id=1, source_target_pairs={{9,17},{13,21},{17,25},{21,29},{10,18},{14,22},{18,26},{22,30}} | collective-permute-start | bytes 1572872 | tf_op jit(solution)/shard_map/ppermute | solution.py:276
  97.1 1.2 copy-start.29
  97.2 1.0 copy-start.9
  98.3 101.1 %collective-permute-start.15 = (bf16[16,2,128,128]{3,2,1,0:T(8,128)(2,1)}, bf16[16,2,128,128]{3,2,1,0:T(8,128)(2,1)}, u32[]{:S(2)}, u32[]{:S(2)}) collective-permute-start(bf16[16,2,128,128]{3,2,1,0:T(8,128)(2,1)} %get-tuple-element.37), channel_id=1, source_target_pairs={{0,4},{4,0},{8,12},{12,8},{16,20},{20,16},{24,28},{28,24},{1,5},{5... | collective-permute-start | bytes 3145736 | tf_op jit(solution)/shard_map/ppermute | solution.py:276
  102.2 1.4 copy-start.3
  103.6 1.2 copy-start.10
  111.1 0.7 copy-start.15
  111.8 0.7 copy-start.30
  112.5 5.9 %collective-permute-start.11 = (bf16[3,3,128,128]{3,2,1,0:T(8,128)(2,1)}, bf16[3,3,128,128]{3,2,1,0:T(8,128)(2,1)S(1)}, u32[]{:S(2)}, u32[]{:S(2)}) collective-permute-start(bf16[3,3,128,128]{3,2,1,0:T(8,128)(2,1)} %get-tuple-element.35), channel_id=1, source_target_pairs={{0,1},{1,2},{2,3},{4,5},{5,6},{6,7},{8,9},{9,10},{10,11},{12,13},{... | collective-permute-start | bytes 884744 | tf_op jit(solution)/shard_map/ppermute | solution.py:303
  114.5 8.3 %collective-permute-start.12 = (bf16[3,3,128,128]{3,2,1,0:T(8,128)(2,1)}, bf16[3,3,128,128]{3,2,1,0:T(8,128)(2,1)S(1)}, u32[]{:S(2)}, u32[]{:S(2)}) collective-permute-start(bf16[3,3,128,128]{3,2,1,0:T(8,128)(2,1)} %copy-done.30), channel_id=1, source_target_pairs={{1,0},{2,1},{3,2},{5,4},{6,5},{7,6},{9,8},{10,9},{11,10},{13,12},{... | collective-permute-start | bytes 884744 | tf_op jit(solution)/shard_map/ppermute | solution.py:304
  118.4 80.2 %collective-permute-start.18 = (bf16[16,128,128]{2,1,0:T(8,128)(2,1)}, bf16[16,128,128]{2,1,0:T(8,128)(2,1)S(1)}, u32[]{:S(2)}, u32[]{:S(2)}) collective-permute-start(bf16[16,128,128]{2,1,0:T(8,128)(2,1)} %copy-done.29), channel_id=1, source_target_pairs={{1,5},{5,1},{9,13},{13,9},{17,21},{21,17},{25,29},{29,25},{2,6},{6... | collective-permute-start | bytes 1572872 | tf_op jit(solution)/shard_map/ppermute | solution.py:276
  122.7 65.7 %copy-start.7 = (bf16[3,3,128,128]{3,2,1,0:T(8,128)(2,1)}, bf16[3,3,128,128]{3,2,1,0:T(8,128)(2,1)S(1)}, u32[]{:S(2)}) copy-start(bf16[3,3,128,128]{3,2,1,0:T(8,128)(2,1)S(1)} %collective-permute-done.12.refs_7_.refs_5_) | copy-start | bytes 884740
  188.4 14.2 %collective-permute-start.24 = (bf16[8,128,128]{2,1,0:T(8,128)(2,1)S(1)}, bf16[8,128,128]{2,1,0:T(8,128)(2,1)S(1)}, u32[]{:S(2)}, u32[]{:S(2)}) collective-permute-start(bf16[8,128,128]{2,1,0:T(8,128)(2,1)S(1)} %get-tuple-element.45), channel_id=1, source_target_pairs={{1,5},{5,1},{9,13},{13,9},{17,21},{21,17},{25,29},{29,25},{2,6},{6... | collective-permute-start | bytes 786440 | tf_op jit(solution)/shard_map/ppermute | solution.py:276
  190.3 29.6 %collective-permute-start.25 = (bf16[8,128,128]{2,1,0:T(8,128)(2,1)}, bf16[8,128,128]{2,1,0:T(8,128)(2,1)S(1)}, u32[]{:S(2)}, u32[]{:S(2)}) collective-permute-start(bf16[8,128,128]{2,1,0:T(8,128)(2,1)} %get-tuple-element.46), channel_id=1, source_target_pairs={{1,25},{5,29},{25,1},{29,5},{2,26},{6,30},{26,2},{30,6}} | collective-permute-start | bytes 786440 | tf_op jit(solution)/shard_map/ppermute | solution.py:276
  193.5 30.5 %collective-permute-start.26 = (bf16[8,128,128]{2,1,0:T(8,128)(2,1)}, bf16[8,128,128]{2,1,0:T(8,128)(2,1)S(1)}, u32[]{:S(2)}, u32[]{:S(2)}) collective-permute-start(bf16[8,128,128]{2,1,0:T(8,128)(2,1)} %get-tuple-element.47), channel_id=1, source_target_pairs={{1,29},{5,25},{25,5},{29,1},{2,30},{6,26},{26,6},{30,2}} | collective-permute-start | bytes 786440 | tf_op jit(solution)/shard_map/ppermute | solution.py:276
  198.6 0.8 copy-start.11
  199.4 33.5 %collective-permute-start.21 = (bf16[8,2,128,128]{3,2,1,0:T(8,128)(2,1)}, bf16[8,2,128,128]{3,2,1,0:T(8,128)(2,1)}, u32[]{:S(2)}, u32[]{:S(2)}) collective-permute-start(bf16[8,2,128,128]{3,2,1,0:T(8,128)(2,1)} %get-tuple-element.42), channel_id=1, source_target_pairs={{0,4},{4,0},{8,12},{12,8},{16,20},{20,16},{24,28},{28,24},{1,5},{5... | collective-permute-start | bytes 1572872 | tf_op jit(solution)/shard_map/ppermute | solution.py:276
  199.4 33.5 %collective-permute-start.22 = (bf16[8,2,128,128]{3,2,1,0:T(8,128)(2,1)}, bf16[8,2,128,128]{3,2,1,0:T(8,128)(2,1)}, u32[]{:S(2)}, u32[]{:S(2)}) collective-permute-start(bf16[8,2,128,128]{3,2,1,0:T(8,128)(2,1)} %get-tuple-element.43), channel_id=1, source_target_pairs={{0,24},{4,28},{24,0},{28,4},{1,25},{5,29},{25,1},{29,5},{2,26},{6,... | collective-permute-start | bytes 1572872 | tf_op jit(solution)/shard_map/ppermute | solution.py:276
  202.6 16.6 %copy-start.21 = (bf16[8,128,128]{2,1,0:T(8,128)(2,1)}, bf16[8,128,128]{2,1,0:T(8,128)(2,1)S(1)}, u32[]{:S(2)}) copy-start(bf16[8,128,128]{2,1,0:T(8,128)(2,1)S(1)} %collective-permute-done.24.refs_6_) | copy-start | bytes 786436
  202.6 30.4 %collective-permute-start.23 = (bf16[8,2,128,128]{3,2,1,0:T(8,128)(2,1)}, bf16[8,2,128,128]{3,2,1,0:T(8,128)(2,1)}, u32[]{:S(2)}, u32[]{:S(2)}) collective-permute-start(bf16[8,2,128,128]{3,2,1,0:T(8,128)(2,1)} %get-tuple-element.44), channel_id=1, source_target_pairs={{0,28},{4,24},{24,4},{28,0},{1,29},{5,25},{25,5},{29,1},{2,30},{6,... | collective-permute-start | bytes 1572872 | tf_op jit(solution)/shard_map/ppermute | solution.py:276
  210.4 1.4 copy-start.4
  211.8 1.0 copy-start.12
  219.2 0.7 copy-start.17
  219.9 0.7 copy-start.23
  220.6 8.1 %collective-permute-start.19 = (bf16[3,3,128,128]{3,2,1,0:T(8,128)(2,1)}, bf16[3,3,128,128]{3,2,1,0:T(8,128)(2,1)S(1)}, u32[]{:S(2)}, u32[]{:S(2)}) collective-permute-start(bf16[3,3,128,128]{3,2,1,0:T(8,128)(2,1)} %get-tuple-element.40), channel_id=1, source_target_pairs={{0,1},{1,2},{2,3},{4,5},{5,6},{6,7},{8,9},{9,10},{10,11},{12,13},{... | collective-permute-start | bytes 884744 | tf_op jit(solution)/shard_map/ppermute | solution.py:303
  224.0 0.7 copy-start.25
  224.7 8.2 %collective-permute-start.20 = (bf16[3,3,128,128]{3,2,1,0:T(8,128)(2,1)}, bf16[3,3,128,128]{3,2,1,0:T(8,128)(2,1)S(1)}, u32[]{:S(2)}, u32[]{:S(2)}) collective-permute-start(bf16[3,3,128,128]{3,2,1,0:T(8,128)(2,1)} %get-tuple-element.41), channel_id=1, source_target_pairs={{1,0},{2,1},{3,2},{5,4},{6,5},{7,6},{9,8},{10,9},{11,10},{13,12},{... | collective-permute-start | bytes 884744 | tf_op jit(solution)/shard_map/ppermute | solution.py:304
  233.0 1.4 copy-start.5
  234.4 0.9 copy-start.22
  235.3 0.9 copy-start.24
  236.3 0.9 copy-start.26
  237.2 17.3 %copy-start.8 = (bf16[3,3,128,128]{3,2,1,0:T(8,128)(2,1)S(1)}, bf16[3,3,128,128]{3,2,1,0:T(8,128)(2,1)}, u32[]{:S(2)}) copy-start(bf16[3,3,128,128]{3,2,1,0:T(8,128)(2,1)} %copy-done.7) | copy-start | bytes 884740
  237.2 17.3 %copy-start.14 = (bf16[1,3,128,128]{3,2,1,0:T(8,128)(2,1)S(1)}, bf16[1,3,128,128]{3,2,1,0:T(8,128)(2,1)}, u32[]{:S(2)}) copy-start(bf16[1,3,128,128]{3,2,1,0:T(8,128)(2,1)} %copy-done.13) | copy-start | bytes 294916
  241.9 0.7 copy-start.19
  242.6 7.6 %collective-permute-start.27 = (bf16[3,3,128,128]{3,2,1,0:T(8,128)(2,1)}, bf16[3,3,128,128]{3,2,1,0:T(8,128)(2,1)S(1)}, u32[]{:S(2)}, u32[]{:S(2)}) collective-permute-start(bf16[3,3,128,128]{3,2,1,0:T(8,128)(2,1)} %get-tuple-element.49), channel_id=1, source_target_pairs={{0,1},{1,2},{2,3},{4,5},{5,6},{6,7},{8,9},{9,10},{10,11},{12,13},{... | collective-permute-start | bytes 884744 | tf_op jit(solution)/shard_map/ppermute | solution.py:303
  246.3 8.3 %collective-permute-start.28 = (bf16[3,3,128,128]{3,2,1,0:T(8,128)(2,1)}, bf16[3,3,128,128]{3,2,1,0:T(8,128)(2,1)S(1)}, u32[]{:S(2)}, u32[]{:S(2)}) collective-permute-start(bf16[3,3,128,128]{3,2,1,0:T(8,128)(2,1)} %get-tuple-element.50), channel_id=1, source_target_pairs={{1,0},{2,1},{3,2},{5,4},{6,5},{7,6},{9,8},{10,9},{11,10},{13,12},{... | collective-permute-start | bytes 884744 | tf_op jit(solution)/shard_map/ppermute | solution.py:304
  254.5 1.0 copy-start.16
  255.5 1.0 copy-start.18
  256.4 1.0 copy-start.20
  257.4 0.9 copy-start.28

commit v3 on v2

--- a/solution.py
+++ b/solution.py
@@ -6,7 +6,7 @@
 from jax.experimental.pallas import tpu as pltpu
 from jax.sharding import PartitionSpec as P
 
-VMEM_LIMIT = 28 * 1024 * 1024
+VMEM_LIMIT = 56 * 1024 * 1024
 
 
 def grid_of(panels):
@@ -14,11 +14,12 @@
     return panels // columns, columns
 
 
-def pack_kernel(info, mask, prolong, head, tail, turned):
+def pack_kernel(info, mask, prolong, *refs):
+    head, tail, full, turned = refs[-4:]
     step = pl.program_id(0)
     group, groups, turn = info[0], info[1], info[2]
     rows = prolong.shape[0]
-    width = head.shape[-1]
+    width = tail.shape[-1]
     for i in range(rows):
         row = step * rows + i
         blocks = []
@@ -30,56 +31,62 @@
         packed = [jnp.where(turn == 1, blocks[(k + 1) % 3], blocks[k]) for k in range(3)]
         head[i, 0] = packed[0]
         head[i, 1] = packed[1]
-        tail[i] = packed[2]
+        tail[i, 0] = packed[2]
         for k in range(3):
+            full[i, k] = packed[k]
             turned[i, k * width:(k + 1) * width, :] = packed[k].T
 
 
-def pack(info, mask, prolong):
+def pack(info, mask, prolong, after):
     rows, pores, width3 = prolong.shape
     width = width3 // 3
     step = 4 if rows % 4 == 0 else rows
     kind = prolong.dtype
+
+    def part(blocks):
+        return (pl.BlockSpec((step, blocks, pores, width), lambda i, *_: (i, 0, 0, 0)),
+                jax.ShapeDtypeStruct((rows, blocks, pores, width), kind))
+
+    outs = [part(2), part(1), part(3), (pl.BlockSpec((step, width3, pores), lambda i, *_: (i, 0, 0)),
+                                        jax.ShapeDtypeStruct((rows, width3, pores), kind))]
     return pl.pallas_call(
         pack_kernel,
         grid_spec=pltpu.PrefetchScalarGridSpec(
             num_scalar_prefetch=2,
             grid=(rows // step,),
-            in_specs=[pl.BlockSpec((step, pores, width3), lambda i, *_: (i, 0, 0))],
-            out_specs=[
-                pl.BlockSpec((step, 2, pores, width), lambda i, *_: (i, 0, 0, 0)),
-                pl.BlockSpec((step, pores, width), lambda i, *_: (i, 0, 0)),
-                pl.BlockSpec((step, width3, pores), lambda i, *_: (i, 0, 0)),
-            ],
+            in_specs=[pl.BlockSpec((step, pores, width3), lambda i, *_: (i, 0, 0)),
+                      *([pl.BlockSpec(memory_space=pl.ANY)] * len(after))],
+            out_specs=[spec for spec, _ in outs],
         ),
-        out_shape=[
-            jax.ShapeDtypeStruct((rows, 2, pores, width), kind),
-            jax.ShapeDtypeStruct((rows, pores, width), kind),
-            jax.ShapeDtypeStruct((rows, width3, pores), kind),
-        ],
+        out_shape=[shape for _, shape in outs],
         compiler_params=pltpu.CompilerParams(vmem_limit_bytes=VMEM_LIMIT),
         cost_estimate=pl.CostEstimate(flops=0, bytes_accessed=8 * 2 ** 20, transcendentals=0),
         name="pack_rows",
-    )(info, mask, prolong)
-
-
-def pick_kernel(plan, outputs, wanted, choice, *refs):
-    panels = len(refs) - 2 * outputs - 1
-    sources = max(max(options) for _, _, options in plan) + 1
-    heads, tails = refs[:sources], refs[sources:2 * sources]
-    out = refs[panels:panels + 2 * outputs]
+    )(info, mask, prolong, *after)
+
+
+def pick_kernel(plan, sources, counts, wanted, choice, *refs):
     done = refs[-1]
     cap = wanted.shape[0] // len(plan)
+    arrays, at = [], 0
+    for count in counts:
+        arrays.append(refs[at:at + count])
+        at += count
+    outs = refs[-1 - sources:-1]
 
     def copies(request, option, entry):
-        target, base, options = plan[request]
+        options, target = plan[request]
         row = wanted[request * cap + entry]
-        source = options[option]
-        return [
-            pltpu.make_async_copy(x.at[row], out[2 * target + part].at[base + entry], done.at[request, entry, part])
-            for part, x in enumerate((heads[source], tails[source]))]
-
-    for request, (_, _, options) in enumerate(plan):
+        result, k = [], 0
+        for x in arrays[options[option]]:
+            for block in range(x.shape[1]):
+                output, base, place = target[k]
+                result.append(pltpu.make_async_copy(
+                    x.at[row, block], outs[output].at[base + entry, place], done.at[request, entry, k]))
+                k += 1
+        return result
+
+    for request, (options, _) in enumerate(plan):
         for option in range(len(options)):
             def begin(request=request, option=option):
                 for entry in range(cap):
@@ -95,39 +102,37 @@
                 copy.wait()
 
 
-def pick(plan, sizes, wanted, choice, pairs, after):
+def pick(plan, sizes, wanted, choice, sources, after):
     cap = wanted.shape[0] // len(plan)
-    heads, tails = [p[0] for p in pairs], [p[1] for p in pairs]
+    flat = [x for source in sources for x in source]
     anywhere = pl.BlockSpec(memory_space=pl.ANY)
-    shapes = []
-    for size in sizes:
-        shapes += [jax.ShapeDtypeStruct((size, *x.shape[1:]), x.dtype) for x in pairs[0]]
-    moved = sum(2 * 2 * x.size for x in shapes)
-    result = pl.pallas_call(
-        functools.partial(pick_kernel, plan, len(sizes)),
+    shapes = [jax.ShapeDtypeStruct((*size, *flat[0].shape[2:]), flat[0].dtype) for size in sizes]
+    return pl.pallas_call(
+        functools.partial(pick_kernel, plan, len(sizes), tuple(len(source) for source in sources)),
         grid_spec=pltpu.PrefetchScalarGridSpec(
             num_scalar_prefetch=2,
             grid=(1,),
-            in_specs=[anywhere] * (2 * len(pairs) + len(after)),
-            out_specs=[anywhere] * len(shapes),
-            scratch_shapes=[pltpu.SemaphoreType.DMA((len(plan), cap, 2))],
+            in_specs=[anywhere] * (len(flat) + len(after)),
+            out_specs=[pl.BlockSpec(x.shape, lambda i, *_: (0, 0, 0, 0)) for x in shapes],
+            scratch_shapes=[pltpu.SemaphoreType.DMA((len(plan), cap, 3))],
         ),
         out_shape=shapes,
         compiler_params=pltpu.CompilerParams(vmem_limit_bytes=VMEM_LIMIT),
-        cost_estimate=pl.CostEstimate(flops=0, bytes_accessed=moved, transcendentals=0),
+        cost_estimate=pl.CostEstimate(flops=0, bytes_accessed=sum(4 * x.size for x in shapes), transcendentals=0),
         name="pick_rows",
-    )(wanted, choice, *heads, *tails, *after)
-    return [(result[2 * i], result[2 * i + 1]) for i in range(len(sizes))]
-
-
-def stage_kernel(layout, arrays, extra, scalars, slot_rows, slot_cols, turned, *refs):
+    )(wanted, choice, *flat, *after)
+
+
+def stage_kernel(layout, counts, extra, scalars, slot_rows, slot_cols, turned, *refs):
     slots = len(layout)
     matrix = refs[:slots]
-    heads = refs[slots:slots + arrays]
-    tails = refs[slots + arrays:slots + 2 * arrays]
-    own, up, down, total = refs[slots + 2 * arrays + extra:]
+    arrays, at = [], slots
+    for count in counts:
+        arrays.append(refs[at:at + count])
+        at += count
+    own, up, down, total = refs[at + extra:]
     cap = matrix[0].shape[1]
-    width = tails[0].shape[-1]
+    width = own.shape[-1]
     turn = scalars[0]
     at = 0
     for slot, sources in enumerate(layout):
@@ -135,11 +140,11 @@
         total[...] = jnp.zeros_like(total)
         for array, base, whole in sources:
             live = scalars[1 + slots + at]
-            head, tail = heads[array], tails[array]
-
-            def product(entry, whole=whole, base=base, head=head, tail=tail, slot=slot, panel=panel):
+            parts = arrays[array]
+
+            def product(entry, whole=whole, base=base, parts=parts, slot=slot, panel=panel):
                 pick = slot_cols[panel * cap + entry] if whole else base + entry
-                right = jnp.concatenate([head[pick, 0], head[pick, 1], tail[pick]], axis=1)
+                right = jnp.concatenate([x[pick, block] for x in parts for block in range(x.shape[1])], axis=1)
                 return jnp.dot(matrix[slot][0, entry], right, preferred_element_type=jnp.float32)
 
             def add(left, value):
@@ -170,12 +175,12 @@
             down[slot, f] = total[k, 0:width, :].astype(down.dtype)
 
 
-def stage(layout, scalars, slot_rows, slot_cols, turned, matrix, pairs, after):
+def stage(layout, scalars, slot_rows, slot_cols, turned, matrix, sources, after):
     slots = len(layout)
     panels, cap, pores, _ = matrix.shape
     width3 = turned.shape[1]
     width = width3 // 3
-    heads, tails = [p[0] for p in pairs], [p[1] for p in pairs]
+    flat = [x for source in sources for x in source]
 
     def whole_spec(x):
         return pl.BlockSpec(x.shape, lambda i, *_, n=x.ndim: (0,) * n)
@@ -184,13 +189,13 @@
         pl.BlockSpec((1, cap, pores, pores), lambda i, s, *_, j=j: (s[1 + j], 0, 0, 0)) for j in range(slots)]
     out = jax.ShapeDtypeStruct((slots, 3, width, width), jnp.bfloat16)
     flops = 2 * slots * 5 * (pores * pores * width3 + width3 * width3 * pores)
-    size = sum(2 * x.size for x in (*heads, *tails)) + 2 * turned.size + 2 * slots * cap * pores * pores
+    size = sum(2 * x.size for x in flat) + 2 * turned.size + 2 * slots * cap * pores * pores
     return pl.pallas_call(
-        functools.partial(stage_kernel, layout, len(pairs), len(after)),
+        functools.partial(stage_kernel, layout, tuple(len(source) for source in sources), len(after)),
         grid_spec=pltpu.PrefetchScalarGridSpec(
             num_scalar_prefetch=3,
             grid=(1,),
-            in_specs=[whole_spec(turned), *matrix_specs, *map(whole_spec, heads), *map(whole_spec, tails),
+            in_specs=[whole_spec(turned), *matrix_specs, *map(whole_spec, flat),
                       *([pl.BlockSpec(memory_space=pl.ANY)] * len(after))],
             out_specs=[pl.BlockSpec(out.shape, lambda i, *_: (0, 0, 0, 0))] * 3,
             scratch_shapes=[pltpu.VMEM((3, width3, width), jnp.float32)],
@@ -199,7 +204,7 @@
         compiler_params=pltpu.CompilerParams(vmem_limit_bytes=VMEM_LIMIT),
         cost_estimate=pl.CostEstimate(flops=flops, bytes_accessed=size, transcendentals=0),
         name="stage_products",
-    )(scalars, slot_rows, slot_cols, turned, *([matrix] * slots), *heads, *tails, *after)
+    )(scalars, slot_rows, slot_cols, turned, *([matrix] * slots), *flat, *after)
 
 
 def assemble_kernel(counts, panels, info, *refs):
@@ -304,75 +309,82 @@
         upper = lax.ppermute(parts[2], "rows", [(g + 1, g) for g in range(groups - 1)])
         return parts[0], lower, upper
 
-    def run(work, pairs, after):
+    def run(work, arrays, after):
         layout = tuple(tuple(source[:3] for source in sources) for _, _, sources in work)
         lives = [jnp.where(ok, count_list[panel], 0) for panel, _, sources in work for *_, ok in sources]
         scalars = jnp.stack([turn, *[panel for panel, _, _ in work], *lives]).astype(jnp.int32)
         for panel, there, _ in work:
             slot_panels.append(panel)
             slot_present.append(there)
-        return stage(layout, scalars, flat_rows, flat_cols, turned, matrix, pairs, after)
+        return stage(layout, scalars, flat_rows, flat_cols, turned, matrix, arrays, after)
 
     slot_panels, slot_present, pieces = [], [], []
     yes = jnp.bool_(True)
 
-    info = jnp.stack([group, jnp.int32(groups), turn]).astype(jnp.int32)
-    head, tail, turned = pack(info, prolong_mask[0].reshape(-1), prolong)
-    own = (head, tail)
-    near = [move_both(own, relay_pairs(1, 1)), move_both(own, relay_pairs(1, -1))]
-    beside = [move_both(own, far_pairs(0, (1,), shift)) for shift in sides]
     side_lists = [move(cols_list, back(far_pairs(0, (1,), shift)), every) for shift in sides]
     far = [(s, signs, shift) for s in range(relays + 1, lines) for signs in ways(s) for shift in range(columns)]
     far_lists = [move(cols_list, back(far_pairs(*entry)), every) for entry in far]
-    parts = run([(place, yes, [(0, 0, True, yes)])], [own], [*side_lists, *far_lists])
-    pieces.append(exchange(parts))
+
+    info = jnp.stack([group, jnp.int32(groups), turn]).astype(jnp.int32)
+    head, tail, full, turned = pack(info, prolong_mask[0].reshape(-1), prolong, [*side_lists, *far_lists])
+    own = (head, tail)
+    near = [move_both(own, relay_pairs(1, 1)), move_both(own, relay_pairs(1, -1))]
+    beside = [move(full, far_pairs(0, (1,), shift), every) for shift in sides]
 
     next_up = move_both(near[0], relay_pairs(2, 1))
     next_down = move_both(near[1], relay_pairs(2, -1))
     plan, wanted = [], []
     for index, shift in enumerate(sides):
         for side, line in enumerate((z - 1, z + 1)):
-            plan.append((index, side * cap, (side,)))
+            plan.append(((side,), tuple((index, side * cap, k) for k in range(3))))
             wanted.append(lax.dynamic_index_in_dim(side_lists[index], panel_at(line, 0), 0, False))
-    picked = pick(tuple(plan), [2 * cap] * len(sides), jnp.concatenate(wanted), jnp.zeros((len(plan),), jnp.int32),
-                  near, pieces[-1][1:])
-    crossed = [move_both(pair, far_pairs(0, (1,), shift)) for pair, shift in zip(picked, sides)]
-    work = [(panel_at(z - 1, 0), has(1, -1), [(0, 0, True, has(1, -1))]),
+    picked = pick(tuple(plan), [(2 * cap, 3)] * len(sides), jnp.concatenate(wanted),
+                  jnp.zeros((len(plan),), jnp.int32), near, [])
+    crossed = [move(x, far_pairs(0, (1,), shift), every) for x, shift in zip(picked, sides)]
+    work = [(place, yes, [(2, 0, True, yes)]),
+            (panel_at(z - 1, 0), has(1, -1), [(0, 0, True, has(1, -1))]),
             (panel_at(z + 1, 0), has(1, 1), [(1, 0, True, has(1, 1))])]
-    work += [(panel_at(z, shift), yes, [(2 + i, 0, True, yes)]) for i, shift in enumerate(sides)]
-    parts = run(work, [*near, *beside], [])
+    work += [(panel_at(z, shift), yes, [(3 + i, 0, True, yes)]) for i, shift in enumerate(sides)]
+    parts = run(work, [*near, (full,), *[(x,) for x in beside]], [])
     pieces.append(exchange(parts))
 
     from_below = has(2, -1)
     second = jnp.where(from_below, z - 2, z + 2)
     second_there = from_below | has(2, 1)
-    plan, wanted, choice = [], [], []
+    plan, wanted, choice, sizes = [], [], [], []
     for index, shift in enumerate(sides):
-        plan.append((index, 0, (0, 1)))
+        plan.append(((0, 1), tuple((index, 0, k) for k in range(3))))
         wanted.append(lax.dynamic_index_in_dim(side_lists[index], panel_at(second, 0), 0, False))
         choice.append(jnp.where(from_below, 0, 1))
+        sizes.append((cap, 3))
     for index in range(len(far)):
-        plan.append((len(sides) + index, 0, (2,)))
+        at = len(sizes)
+        plan.append(((2,), ((at, 0, 0), (at, 0, 1), (at + 1, 0, 0))))
         wanted.append(lax.dynamic_index_in_dim(far_lists[index], place, 0, False))
         choice.append(0)
-    picked = pick(tuple(plan), [cap] * len(plan), jnp.concatenate(wanted), jnp.stack(choice).astype(jnp.int32),
-                  [next_up, next_down, own], pieces[-1][1:])
-    second_crossed = [move_both(pair, far_pairs(0, (1,), shift)) for pair, shift in zip(picked, sides)]
-    far_crossed = [move_both(pair, far_pairs(*entry)) for pair, entry in zip(picked[len(sides):], far)]
+        sizes += [(cap, 2), (cap, 1)]
+    picked = pick(tuple(plan), sizes, jnp.concatenate(wanted), jnp.stack(choice).astype(jnp.int32),
+                  [next_up, next_down, (full,)], pieces[-1][1:])
+    second_crossed = [move(x, far_pairs(0, (1,), shift), every) for x, shift in zip(picked, sides)]
+    picked = picked[len(sides):]
+    far_crossed = [move_both(picked[2 * i:2 * i + 2], far_pairs(*entry)) for i, entry in enumerate(far)]
     work = [(panel_at(second, 0), second_there, [(0, 0, True, from_below), (1, 0, True, has(2, 1))])]
     for i, shift in enumerate(sides):
         work += [(panel_at(z - 1, shift), has(1, -1), [(2 + i, 0, False, has(1, -1))]),
                  (panel_at(z + 1, shift), has(1, 1), [(2 + i, cap, False, has(1, 1))])]
-    parts = run(work, [next_up, next_down, *crossed], [])
+    parts = run(work, [next_up, next_down, *[(x,) for x in crossed]], [])
     pieces.append(exchange(parts))
-
     work = [(panel_at(second, shift), second_there, [(i, 0, False, second_there)]) for i, shift in enumerate(sides)]
+    parts = run(work, [(x,) for x in second_crossed], pieces[-1][1:])
+    pieces.append(exchange(parts))
+
+    work = []
     for i, (s, signs, shift) in enumerate(far):
         present = [has(s, -sign) for sign in signs]
         line = jnp.where(present[0], z - signs[0] * s, z - signs[-1] * s)
         there = functools.reduce(jnp.logical_or, present)
-        work.append((panel_at(line, shift), there, [(len(sides) + i, 0, False, there)]))
-    parts = run(work, [*second_crossed, *far_crossed], pieces[-1][1:])
+        work.append((panel_at(line, shift), there, [(i, 0, False, there)]))
+    parts = run(work, far_crossed, pieces[-1][1:])
     pieces.append(exchange(parts))
 
     where = jnp.stack([*slot_panels, *slot_present]).astype(jnp.int32)

time: 264 us -> 184 us (0.70)
  Pallas kernels: 109 us -> 43.8 us
  starting transfers between devices: 75 us -> 60.4 us
  local copies, waits for them, and re-layouts: 29.1 us -> 15.8 us
  waiting for transfers between devices: 40.1 us -> 52.6 us
    pallas_call x6, Pallas kernels: 104 us -> 33.9 us  [the longest x4 25.7 us: stage(): pl.pallas_call(functools.partial(stage_kernel, layout, tuple((len(source)...]
    ppermute x21 -> x18, waiting for transfers between devices: 21.6 us -> 41.2 us  [move(): return lax.ppermute(x, ('blk', 'rows'), perm)]
    unnamed x63 -> x55, local copies, waits for them, and re-layouts: 24.2 us -> 6.2 us
    ppermute x21 -> x18, starting transfers between devices: 53.1 us -> 38.9 us  [move(): return lax.ppermute(x, ('blk', 'rows'), perm)]
    ppermute x4, waiting for transfers between devices: 15.1 us -> 11.4 us  [exchange(): lax.ppermute(parts[2], 'rows', [(g + 1, g) for g in range(groups - 1)])]
    ppermute x4, waiting for transfers between devices: 3.43 us -> 0.01 us  [exchange(): lax.ppermute(parts[1], 'rows', [(g, g + 1) for g in range(groups - 1)])]
  transfers between devices with their start and end apart: 29 -> 26, of which waited for: 8 -> 8; matrix products, arithmetic and copies ran while one was open for 2% -> 7% of each run, Pallas kernels for 38% -> 16%
where the time goes in v3:
time: 184 us; the launch traced here: 182 us
  starting transfers between devices  60.4 us (33%)
  waiting for transfers between devices  52.6 us (29%)
  Pallas kernels  43.8 us (24%)
  local copies, waits for them, and re-layouts  15.8 us (9%)
  between operations  6.48 us (4%)
  other arithmetic  2.46 us (1%)
    ppermute x18, waiting for transfers between devices, move(): return lax.ppermute(x, ('blk', 'rows'), perm)  41.2 us
    ppermute x18, starting transfers between devices, move(): return lax.ppermute(x, ('blk', 'rows'), perm)  38.9 us
    pallas_call x4, Pallas kernels, stage(): pl.pallas_call(functools.partial(stage_kernel, layout, tuple((len(source)...  25.7 us
    ppermute x4, starting transfers between devices, exchange(): lax.ppermute(parts[1], 'rows', [(g, g + 1) for g in range(groups - 1)])  12.8 us
    ppermute x4, waiting for transfers between devices, exchange(): lax.ppermute(parts[2], 'rows', [(g + 1, g) for g in range(groups - 1)])  11.4 us
    ppermute x4, starting transfers between devices, exchange(): lax.ppermute(parts[2], 'rows', [(g + 1, g) for g in range(groups - 1)])  8.62 us
    pallas_call x2, Pallas kernels, pick(): pl.pallas_call(functools.partial(pick_kernel, plan, len(sizes), tuple((le...  8.2 us
    unnamed x55, local copies, waits for them, and re-layouts  6.2 us
  transfers between devices with their start and end apart: 26, of which 8 were waited for; matrix products, arithmetic and copies ran while one was open for 7% of the time, Pallas kernels for 16%

profile of v3, /device:TPU:1, one launch (start us, length us, event | category | flops | bytes accessed | tf_op | source)
XLA Modules:
  0.0 181.6 jit_solution(16785357436179401692)
XLA Ops:
  0.0 2.1 %collective-permute-start = (s32[8,8]{1,0:T(8,128)}, s32[8,8]{1,0:T(8,128)S(1)}, u32[]{:S(2)}, u32[]{:S(2)}) collective-permute-start(s32[8,8]{1,0:T(8,128)} %bitcast.69), channel_id=1, source_target_pairs={{4,0},{0,4},{12,8},{8,12},{20,16},{16,20},{28,24},{24,28},{5,1},{1... | collective-permute-start | bytes 776 | tf_op jit(solution)/shard_map/ppermute | solution.py:281
  2.1 5.2 %collective-permute-start.1 = (s32[8,8]{1,0:T(8,128)}, s32[8,8]{1,0:T(8,128)S(1)}, u32[]{:S(2)}, u32[]{:S(2)}) collective-permute-start(s32[8,8]{1,0:T(8,128)} %bitcast.70), channel_id=1, source_target_pairs={{24,0},{28,4},{0,24},{4,28},{25,1},{29,5},{1,25},{5,29},{26,2},{30... | collective-permute-start | bytes 776 | tf_op jit(solution)/shard_map/ppermute | solution.py:281
  7.3 1.9 %collective-permute-start.2 = (s32[8,8]{1,0:T(8,128)}, s32[8,8]{1,0:T(8,128)S(1)}, u32[]{:S(2)}, u32[]{:S(2)}) collective-permute-start(s32[8,8]{1,0:T(8,128)} %bitcast.71), channel_id=1, source_target_pairs={{28,0},{24,4},{4,24},{0,28},{29,1},{25,5},{5,25},{1,29},{30,2},{26... | collective-permute-start | bytes 776 | tf_op jit(solution)/shard_map/ppermute | solution.py:281
  9.2 0.6 pad_add_fusion.info
  9.9 0.8 copy.8
  10.6 0.6 reshape_squeeze.11.mask
  11.3 3.3 %collective-permute-done.2.refs_2_ = s32[8,8]{1,0:T(8,128)S(1)} collective-permute-done((s32[8,8]{1,0:T(8,128)}, s32[8,8]{1,0:T(8,128)S(1)}, u32[]{:S(2)}, u32[]{:S(2)}) %collective-permute-start.2) | collective-permute-done | bytes 288 | tf_op jit(solution)/shard_map/ppermute | solution.py:281
  14.6 0.6 copy-done.23
  15.1 4.9 %pack_rows.1 = (bf16[16,2,128,128]{3,2,1,0:T(8,128)(2,1)}, bf16[16,1,128,128]{3,2,1,0:T(8,128)(2,1)}, bf16[16,3,128,128]{3,2,1,0:T(8,128)(2,1)}, bf16[16,384,128]{2,1,0:T(8,128)(2,1)}) custom-call(s32[3]{0:T(128)} %pad_add_fusion.info, s32[48]{0:T(128)} %reshape_squeeze.11.mask, bf16[16,128,384]{2,1,0:T(8,128)(2,1)} %bitcast.68, s32[8,8]{1,0:T(8,128)} %copy-done.21, ...), custom_call_target="tpu_custom_call" | custom-call | bytes 8388608 | tf_op jit(solution)/shard_map/pack_rows/pallas_call | solution.py:52
  20.3 1.3 collective-permute-start.3
  21.6 1.3 collective-permute-start.5
  22.9 4.0 %collective-permute-start.4 = (bf16[16,1,128,128]{3,2,1,0:T(8,128)(2,1)}, bf16[16,1,128,128]{3,2,1,0:T(8,128)(2,1)S(1)}, u32[]{:S(2)}, u32[]{:S(2)}) collective-permute-start(bf16[16,1,128,128]{3,2,1,0:T(8,128)(2,1)} %get-tuple-element.28), channel_id=1, source_target_pairs={{1,9},{5,13},{9,17},{13,21},{17,25},{21,29},{2,10},{6,14},{10,18},... | collective-permute-start | bytes 1572872 | tf_op jit(solution)/shard_map/ppermute | solution.py:281
  26.9 1.3 collective-permute-start.6
  28.3 0.8 fusion.2
  29.1 0.6 pad_add_fusion.1.wanted
  29.7 20.7 %collective-permute-done.4.refs_5_.refs_1_ = bf16[16,1,128,128]{3,2,1,0:T(8,128)(2,1)S(1)} collective-permute-done((bf16[16,1,128,128]{3,2,1,0:T(8,128)(2,1)}, bf16[16,1,128,128]{3,2,1,0:T(8,128)(2,1)S(1)}, u32[]{:S(2)}, u32[]{:S(2)}) %collective-permute-start.4) | collective-permute-done | bytes 524320 | tf_op jit(solution)/shard_map/ppermute | solution.py:281
  50.4 4.2 %collective-permute-done.6.refs_7_.refs_3_ = bf16[16,1,128,128]{3,2,1,0:T(8,128)(2,1)S(1)} collective-permute-done((bf16[16,1,128,128]{3,2,1,0:T(8,128)(2,1)}, bf16[16,1,128,128]{3,2,1,0:T(8,128)(2,1)S(1)}, u32[]{:S(2)}, u32[]{:S(2)}) %collective-permute-start.6) | collective-permute-done | bytes 524320 | tf_op jit(solution)/shard_map/ppermute | solution.py:281
  54.6 0.6 broadcast_1_choice.2.choice
  56.2 3.8 %pick_rows.2 = bf16[16,3,128,128]{3,2,1,0:T(8,128)(2,1)} custom-call(s32[16]{0:T(128)} %pad_add_fusion.1.wanted, s32[2]{0:T(128)} %broadcast_1_choice.2.choice, bf16[16,2,128,128]{3,2,1,0:T(8,128)(2,1)} %copy-done, bf16[16,1,128,128]{3,2,1,0:T(8,128)(2,1)} %copy-done.5, bf16[16,2,128,128]{3,2,1,0:T(8,128)(2,1)} %copy-done.1, bf16[16,1,128,128]{3,2,1,0:T(8,128)(2,1)} %copy-done.4), custom_call_target="tpu_custom_call" | custom-call | bytes 3145728 | tf_op jit(solution)/shard_map/pick_rows/pallas_call | solution.py:110
  60.0 1.2 collective-permute-start.14
  61.2 0.7 collective-permute-start.10
  61.9 1.3 collective-permute-start.12
  63.2 0.7 collective-permute-start.11
  63.9 1.3 collective-permute-start.13
  65.3 0.7 reshape_squeeze.10.slot_cols
  66.0 0.6 reshape_squeeze.9.slot_rows
  66.6 0.7 constant_dynamic-slice_fusion
  68.7 1.9 %stack.163.scalars = s32[9]{0:T(128)} concatenate(s32[1]{0:T(128)} %bitcast.14, s32[1]{0:T(128)} %bitcast, s32[1]{0:T(128)} %bitcast.1, s32[1]{0:T(128)} %bitcast.2, s32[1]{0:T(128)} %bitcast.3, s32[1]{0:T(128)} %bitcast.15, s32[1]{0:T(128)} %bitcast.17, s32[1]{0:T(128)} %bitcast.19, s32[1]{0:T(128)} %bitcast.20), dimensions={0} | concatenate | bytes 72 | tf_op jit(solution)/shard_map/stack | solution.py:315
  70.6 8.6 %stage_products.4 = (bf16[4,3,128,128]{3,2,1,0:T(8,128)(2,1)}, bf16[4,3,128,128]{3,2,1,0:T(8,128)(2,1)}, bf16[4,3,128,128]{3,2,1,0:T(8,128)(2,1)}) custom-call(s32[9]{0:T(128)} %stack.163.scalars, s32[64]{0:T(128)} %reshape_squeeze.9.slot_rows, s32[64]{0:T(128)} %reshape_squeeze.10.slot_cols, bf16[16,384,128]{2,1,0:T(8,128)(2,1)} %get-tuple-element.26.turned, ...), custom_call_target="tpu_custom_call" | custom-call | flops 1006632960 | bytes 8912896 | tf_op jit(solution)/shard_map/stage_products/pallas_call | solution.py:193
  79.2 5.0 %collective-permute-start.8 = (bf16[4,3,128,128]{3,2,1,0:T(8,128)(2,1)}, bf16[4,3,128,128]{3,2,1,0:T(8,128)(2,1)S(1)}, u32[]{:S(2)}, u32[]{:S(2)}) collective-permute-start(bf16[4,3,128,128]{3,2,1,0:T(8,128)(2,1)} %get-tuple-element.31), channel_id=1, source_target_pairs={{0,1},{1,2},{2,3},{4,5},{5,6},{6,7},{8,9},{9,10},{10,11},{12,13},{... | collective-permute-start | bytes 1179656 | tf_op jit(solution)/shard_map/ppermute | solution.py:308
  84.2 9.6 %collective-permute-done.13.refs_6_.refs_3_ = bf16[16,1,128,128]{3,2,1,0:T(8,128)(2,1)S(1)} collective-permute-done((bf16[16,1,128,128]{3,2,1,0:T(8,128)(2,1)}, bf16[16,1,128,128]{3,2,1,0:T(8,128)(2,1)S(1)}, u32[]{:S(2)}, u32[]{:S(2)}) %collective-permute-start.13) | collective-permute-done | bytes 524320 | tf_op jit(solution)/shard_map/ppermute | solution.py:281
  93.8 1.9 %collective-permute-start.9 = (bf16[4,3,128,128]{3,2,1,0:T(8,128)(2,1)}, bf16[4,3,128,128]{3,2,1,0:T(8,128)(2,1)}, u32[]{:S(2)}, u32[]{:S(2)}) collective-permute-start(bf16[4,3,128,128]{3,2,1,0:T(8,128)(2,1)} %get-tuple-element.32), channel_id=1, source_target_pairs={{1,0},{2,1},{3,2},{5,4},{6,5},{7,6},{9,8},{10,9},{11,10},{13,12},{... | collective-permute-start | bytes 1179656 | tf_op jit(solution)/shard_map/ppermute | solution.py:309
  96.2 0.7 fusion.4
  96.9 0.7 fusion.3
  97.6 0.6 pad_add_fusion.3.wanted
  98.2 5.0 %collective-permute-done.9.refs_6_.refs_2_ = bf16[4,3,128,128]{3,2,1,0:T(8,128)(2,1)} collective-permute-done((bf16[4,3,128,128]{3,2,1,0:T(8,128)(2,1)}, bf16[4,3,128,128]{3,2,1,0:T(8,128)(2,1)}, u32[]{:S(2)}, u32[]{:S(2)}) %collective-permute-start.9) | collective-permute-done | bytes 393248 | tf_op jit(solution)/shard_map/ppermute | solution.py:309
  103.2 0.9 copy-done.2
  104.2 1.0 copy-done.3
  105.1 4.4 %pick_rows.3 = (bf16[8,3,128,128]{3,2,1,0:T(8,128)(2,1)}, bf16[8,2,128,128]{3,2,1,0:T(8,128)(2,1)}, bf16[8,1,128,128]{3,2,1,0:T(8,128)(2,1)}, bf16[8,2,128,128]{3,2,1,0:T(8,128)(2,1)}, bf16[8,1,128,128]{3,2,1,0:T(8,128)(2,1)}) custom-call(s32[24]{0:T(128)} %pad_add_fusion.3.wanted, s32[3]{0:T(128)} %stack.174.choice, bf16[16,2,128,128]{3,2,1,0:T(8,128)(2,1)} %copy-done.2, ...), custom_call_target="tpu_custom_call" | custom-call | bytes 4718592 | tf_op jit(solution)/shard_map/pick_rows/pallas_call | solution.py:110
  109.5 0.7 collective-permute-start.17
  112.8 0.6 stack.170.scalars
  113.4 7.7 %stage_products.5 = (bf16[3,3,128,128]{3,2,1,0:T(8,128)(2,1)}, bf16[3,3,128,128]{3,2,1,0:T(8,128)(2,1)}, bf16[3,3,128,128]{3,2,1,0:T(8,128)(2,1)}) custom-call(s32[8]{0:T(128)} %stack.170.scalars, s32[64]{0:T(128)} %reshape_squeeze.9.slot_rows, s32[64]{0:T(128)} %reshape_squeeze.10.slot_cols, bf16[16,384,128]{2,1,0:T(8,128)(2,1)} %get-tuple-element.26.turned, ...), custom_call_target="tpu_custom_call" | custom-call | flops 754974720 | bytes 7077888 | tf_op jit(solution)/shard_map/stage_products/pallas_call | solution.py:193
  121.1 1.9 %collective-permute-start.15 = (bf16[3,3,128,128]{3,2,1,0:T(8,128)(2,1)}, bf16[3,3,128,128]{3,2,1,0:T(8,128)(2,1)S(1)}, u32[]{:S(2)}, u32[]{:S(2)}) collective-permute-start(bf16[3,3,128,128]{3,2,1,0:T(8,128)(2,1)} %get-tuple-element.34), channel_id=1, source_target_pairs={{0,1},{1,2},{2,3},{4,5},{5,6},{6,7},{8,9},{9,10},{10,11},{12,13},{... | collective-permute-start | bytes 884744 | tf_op jit(solution)/shard_map/ppermute | solution.py:308
  123.0 2.6 %collective-permute-start.20 = (bf16[8,2,128,128]{3,2,1,0:T(8,128)(2,1)}, bf16[8,2,128,128]{3,2,1,0:T(8,128)(2,1)S(1)}, u32[]{:S(2)}, u32[]{:S(2)}) collective-permute-start(bf16[8,2,128,128]{3,2,1,0:T(8,128)(2,1)} %get-tuple-element.40), channel_id=1, source_target_pairs={{0,24},{4,28},{24,0},{28,4},{1,25},{5,29},{25,1},{29,5},{2,26},{6,... | collective-permute-start | bytes 1572872 | tf_op jit(solution)/shard_map/ppermute | solution.py:281
  125.6 4.2 %collective-permute-start.22 = (bf16[8,2,128,128]{3,2,1,0:T(8,128)(2,1)S(1)}, bf16[8,2,128,128]{3,2,1,0:T(8,128)(2,1)S(1)}, u32[]{:S(2)}, u32[]{:S(2)}) collective-permute-start(bf16[8,2,128,128]{3,2,1,0:T(8,128)(2,1)S(1)} %copy-done.26), channel_id=1, source_target_pairs={{0,28},{4,24},{24,4},{28,0},{1,29},{5,25},{25,5},{29,1},{2,30},{6,... | collective-permute-start | bytes 1572872 | tf_op jit(solution)/shard_map/ppermute | solution.py:281
  129.8 2.4 %collective-permute-start.16 = (bf16[3,3,128,128]{3,2,1,0:T(8,128)(2,1)}, bf16[3,3,128,128]{3,2,1,0:T(8,128)(2,1)S(1)}, u32[]{:S(2)}, u32[]{:S(2)}) collective-permute-start(bf16[3,3,128,128]{3,2,1,0:T(8,128)(2,1)} %get-tuple-element.35), channel_id=1, source_target_pairs={{1,0},{2,1},{3,2},{5,4},{6,5},{7,6},{9,8},{10,9},{11,10},{13,12},{... | collective-permute-start | bytes 884744 | tf_op jit(solution)/shard_map/ppermute | solution.py:309
  132.3 3.7 %collective-permute-start.21 = (bf16[8,1,128,128]{3,2,1,0:T(8,128)(2,1)}, bf16[8,1,128,128]{3,2,1,0:T(8,128)(2,1)S(1)}, u32[]{:S(2)}, u32[]{:S(2)}) collective-permute-start(bf16[8,1,128,128]{3,2,1,0:T(8,128)(2,1)} %get-tuple-element.41), channel_id=1, source_target_pairs={{1,25},{5,29},{25,1},{29,5},{2,26},{6,30},{26,2},{30,6}} | collective-permute-start | bytes 786440 | tf_op jit(solution)/shard_map/ppermute | solution.py:281
  136.0 5.1 %collective-permute-start.23 = (bf16[8,1,128,128]{3,2,1,0:T(8,128)(2,1)}, bf16[8,1,128,128]{3,2,1,0:T(8,128)(2,1)S(1)}, u32[]{:S(2)}, u32[]{:S(2)}) collective-permute-start(bf16[8,1,128,128]{3,2,1,0:T(8,128)(2,1)} %get-tuple-element.43), channel_id=1, source_target_pairs={{1,29},{5,25},{25,5},{29,1},{2,30},{6,26},{26,6},{30,2}} | collective-permute-start | bytes 786440 | tf_op jit(solution)/shard_map/ppermute | solution.py:281
  141.8 0.7 pad_add_fusion.2.scalars
  142.5 0.7 copy-done.10
  143.2 4.0 %stage_products.6 = (bf16[1,3,128,128]{3,2,1,0:T(8,128)(2,1)}, bf16[1,3,128,128]{3,2,1,0:T(8,128)(2,1)}, bf16[1,3,128,128]{3,2,1,0:T(8,128)(2,1)}) custom-call(s32[3]{0:T(128)} %pad_add_fusion.2.scalars, s32[64]{0:T(128)} %reshape_squeeze.9.slot_rows, s32[64]{0:T(128)} %reshape_squeeze.10.slot_cols, bf16[16,384,128]{2,1,0:T(8,128)(2,1)} %get-tuple-element.26.turned, ...), custom_call_target="tpu_custom_call" | custom-call | flops 251658240 | bytes 2621440 | tf_op jit(solution)/shard_map/stage_products/pallas_call | solution.py:193
  147.2 4.1 %collective-permute-start.18 = (bf16[1,3,128,128]{3,2,1,0:T(8,128)(2,1)}, bf16[1,3,128,128]{3,2,1,0:T(8,128)(2,1)S(1)}, u32[]{:S(2)}, u32[]{:S(2)}) collective-permute-start(bf16[1,3,128,128]{3,2,1,0:T(8,128)(2,1)} %get-tuple-element.38), channel_id=1, source_target_pairs={{0,1},{1,2},{2,3},{4,5},{5,6},{6,7},{8,9},{9,10},{10,11},{12,13},{... | collective-permute-start | bytes 294920 | tf_op jit(solution)/shard_map/ppermute | solution.py:308
  151.2 3.4 %collective-permute-done.21.refs_3_ = bf16[8,1,128,128]{3,2,1,0:T(8,128)(2,1)S(1)} collective-permute-done((bf16[8,1,128,128]{3,2,1,0:T(8,128)(2,1)}, bf16[8,1,128,128]{3,2,1,0:T(8,128)(2,1)S(1)}, u32[]{:S(2)}, u32[]{:S(2)}) %collective-permute-start.21) | collective-permute-done | bytes 262176 | tf_op jit(solution)/shard_map/ppermute | solution.py:281
  154.6 1.9 %collective-permute-start.19 = (bf16[1,3,128,128]{3,2,1,0:T(8,128)(2,1)}, bf16[1,3,128,128]{3,2,1,0:T(8,128)(2,1)S(1)}, u32[]{:S(2)}, u32[]{:S(2)}) collective-permute-start(bf16[1,3,128,128]{3,2,1,0:T(8,128)(2,1)} %get-tuple-element.39), channel_id=1, source_target_pairs={{1,0},{2,1},{3,2},{5,4},{6,5},{7,6},{9,8},{10,9},{11,10},{13,12},{... | collective-permute-start | bytes 294920 | tf_op jit(solution)/shard_map/ppermute | solution.py:309
  157.9 0.6 stack.177.scalars
  158.6 2.2 %collective-permute-done.19.refs_7_.refs_8_ = bf16[1,3,128,128]{3,2,1,0:T(8,128)(2,1)S(1)} collective-permute-done((bf16[1,3,128,128]{3,2,1,0:T(8,128)(2,1)}, bf16[1,3,128,128]{3,2,1,0:T(8,128)(2,1)S(1)}, u32[]{:S(2)}, u32[]{:S(2)}) %collective-permute-start.19) | collective-permute-done | bytes 98336 | tf_op jit(solution)/shard_map/ppermute | solution.py:309
  160.8 0.6 copy-done.15
  161.4 5.4 %stage_products.7 = (bf16[2,3,128,128]{3,2,1,0:T(8,128)(2,1)}, bf16[2,3,128,128]{3,2,1,0:T(8,128)(2,1)}, bf16[2,3,128,128]{3,2,1,0:T(8,128)(2,1)}) custom-call(s32[5]{0:T(128)} %stack.177.scalars, s32[64]{0:T(128)} %reshape_squeeze.9.slot_rows, s32[64]{0:T(128)} %reshape_squeeze.10.slot_cols, bf16[16,384,128]{2,1,0:T(8,128)(2,1)} %get-tuple-element.26.turned, ...), custom_call_target="tpu_custom_call" | custom-call | flops 503316480 | bytes 3670016 | tf_op jit(solution)/shard_map/stage_products/pallas_call | solution.py:193
  166.8 1.9 %collective-permute-start.24 = (bf16[2,3,128,128]{3,2,1,0:T(8,128)(2,1)}, bf16[2,3,128,128]{3,2,1,0:T(8,128)(2,1)S(1)}, u32[]{:S(2)}, u32[]{:S(2)}) collective-permute-start(bf16[2,3,128,128]{3,2,1,0:T(8,128)(2,1)} %get-tuple-element.45), channel_id=1, source_target_pairs={{0,1},{1,2},{2,3},{4,5},{5,6},{6,7},{8,9},{9,10},{10,11},{12,13},{... | collective-permute-start | bytes 589832 | tf_op jit(solution)/shard_map/ppermute | solution.py:308
  168.7 2.4 %collective-permute-start.25 = (bf16[2,3,128,128]{3,2,1,0:T(8,128)(2,1)}, bf16[2,3,128,128]{3,2,1,0:T(8,128)(2,1)S(1)}, u32[]{:S(2)}, u32[]{:S(2)}) collective-permute-start(bf16[2,3,128,128]{3,2,1,0:T(8,128)(2,1)} %get-tuple-element.46), channel_id=1, source_target_pairs={{1,0},{2,1},{3,2},{5,4},{6,5},{7,6},{9,8},{10,9},{11,10},{13,12},{... | collective-permute-start | bytes 589832 | tf_op jit(solution)/shard_map/ppermute | solution.py:309
  171.2 0.6 stack.156.info
  171.8 4.2 %collective-permute-done.25.refs_11_ = bf16[2,3,128,128]{3,2,1,0:T(8,128)(2,1)S(1)} collective-permute-done((bf16[2,3,128,128]{3,2,1,0:T(8,128)(2,1)}, bf16[2,3,128,128]{3,2,1,0:T(8,128)(2,1)S(1)}, u32[]{:S(2)}, u32[]{:S(2)}) %collective-permute-start.25) | collective-permute-done | bytes 196640 | tf_op jit(solution)/shard_map/ppermute | solution.py:309
  175.9 0.7 copy-done.19
  176.6 4.9 %assemble_coarse.1 = f32[5120,128]{1,0:T(8,128)} custom-call(s32[20]{0:T(128)} %stack.156.info, bf16[4,3,128,128]{3,2,1,0:T(8,128)(2,1)} %get-tuple-element.30.refs_0_, bf16[4,3,128,128]{3,2,1,0:T(8,128)(2,1)} %copy-done.8, bf16[4,3,128,128]{3,2,1,0:T(8,128)(2,1)} %collective-permute-done.9.refs_6_.refs_2_, ...), custom_call_target="tpu_custom_call" | custom-call | bytes 8388608 | tf_op jit(solution)/shard_map/assemble_coarse/pallas_call | solution.py:241
  (68 shorter events, 1.8 us)
Async XLA Ops:
  0.0 11.2 %collective-permute-start = (s32[8,8]{1,0:T(8,128)}, s32[8,8]{1,0:T(8,128)S(1)}, u32[]{:S(2)}, u32[]{:S(2)}) collective-permute-start(s32[8,8]{1,0:T(8,128)} %bitcast.69), channel_id=1, source_target_pairs={{4,0},{0,4},{12,8},{8,12},{20,16},{16,20},{28,24},{24,28},{5,1},{1... | collective-permute-start | bytes 776 | tf_op jit(solution)/shard_map/ppermute | solution.py:281
  2.1 9.2 %collective-permute-start.1 = (s32[8,8]{1,0:T(8,128)}, s32[8,8]{1,0:T(8,128)S(1)}, u32[]{:S(2)}, u32[]{:S(2)}) collective-permute-start(s32[8,8]{1,0:T(8,128)} %bitcast.70), channel_id=1, source_target_pairs={{24,0},{28,4},{0,24},{4,28},{25,1},{29,5},{1,25},{5,29},{26,2},{30... | collective-permute-start | bytes 776 | tf_op jit(solution)/shard_map/ppermute | solution.py:281
  7.3 7.3 %collective-permute-start.2 = (s32[8,8]{1,0:T(8,128)}, s32[8,8]{1,0:T(8,128)S(1)}, u32[]{:S(2)}, u32[]{:S(2)}) collective-permute-start(s32[8,8]{1,0:T(8,128)} %bitcast.71), channel_id=1, source_target_pairs={{28,0},{24,4},{4,24},{0,28},{29,1},{25,5},{5,25},{1,29},{30,2},{26... | collective-permute-start | bytes 776 | tf_op jit(solution)/shard_map/ppermute | solution.py:281
  11.2 3.3 %copy-start.21 = (s32[8,8]{1,0:T(8,128)}, s32[8,8]{1,0:T(8,128)S(1)}, u32[]{:S(2)}) copy-start(s32[8,8]{1,0:T(8,128)S(1)} %collective-permute-done.refs_0_) | copy-start | bytes 772
  11.3 3.3 %copy-start.22 = (s32[8,8]{1,0:T(8,128)}, s32[8,8]{1,0:T(8,128)S(1)}, u32[]{:S(2)}) copy-start(s32[8,8]{1,0:T(8,128)S(1)} %collective-permute-done.1.refs_1_) | copy-start | bytes 772
  14.6 0.6 copy-start.23
  20.0 43.9 %collective-permute-start.7 = (bf16[16,3,128,128]{3,2,1,0:T(8,128)(2,1)}, bf16[16,3,128,128]{3,2,1,0:T(8,128)(2,1)}, u32[]{:S(2)}, u32[]{:S(2)}) collective-permute-start(bf16[16,3,128,128]{3,2,1,0:T(8,128)(2,1)} %get-tuple-element.29.refs_8_.refs_4_), channel_id=1, source_target_pairs={{0,4},{4,0},{8,12},{12,8},{16,20},{20,16},{24,28},{28,24},{1,5},{5... | collective-permute-start | bytes 4718600 | tf_op jit(solution)/shard_map/ppermute | solution.py:281
  20.3 34.4 %collective-permute-start.3 = (bf16[16,2,128,128]{3,2,1,0:T(8,128)(2,1)}, bf16[16,2,128,128]{3,2,1,0:T(8,128)(2,1)S(1)}, u32[]{:S(2)}, u32[]{:S(2)}) collective-permute-start(bf16[16,2,128,128]{3,2,1,0:T(8,128)(2,1)} %get-tuple-element.27), channel_id=1, source_target_pairs={{0,8},{4,12},{8,16},{12,20},{16,24},{20,28},{1,9},{5,13},{9,17},{1... | collective-permute-start | bytes 3145736 | tf_op jit(solution)/shard_map/ppermute | solution.py:281
  21.6 33.0 %collective-permute-start.5 = (bf16[16,2,128,128]{3,2,1,0:T(8,128)(2,1)}, bf16[16,2,128,128]{3,2,1,0:T(8,128)(2,1)S(1)}, u32[]{:S(2)}, u32[]{:S(2)}) collective-permute-start(bf16[16,2,128,128]{3,2,1,0:T(8,128)(2,1)} %get-tuple-element.27), channel_id=1, source_target_pairs={{8,0},{12,4},{16,8},{20,12},{24,16},{28,20},{9,1},{13,5},{17,9},{2... | collective-permute-start | bytes 3145736 | tf_op jit(solution)/shard_map/ppermute | solution.py:281
  22.9 27.5 %collective-permute-start.4 = (bf16[16,1,128,128]{3,2,1,0:T(8,128)(2,1)}, bf16[16,1,128,128]{3,2,1,0:T(8,128)(2,1)S(1)}, u32[]{:S(2)}, u32[]{:S(2)}) collective-permute-start(bf16[16,1,128,128]{3,2,1,0:T(8,128)(2,1)} %get-tuple-element.28), channel_id=1, source_target_pairs={{1,9},{5,13},{9,17},{13,21},{17,25},{21,29},{2,10},{6,14},{10,18},... | collective-permute-start | bytes 1572872 | tf_op jit(solution)/shard_map/ppermute | solution.py:281
  26.9 27.7 %collective-permute-start.6 = (bf16[16,1,128,128]{3,2,1,0:T(8,128)(2,1)}, bf16[16,1,128,128]{3,2,1,0:T(8,128)(2,1)S(1)}, u32[]{:S(2)}, u32[]{:S(2)}) collective-permute-start(bf16[16,1,128,128]{3,2,1,0:T(8,128)(2,1)} %get-tuple-element.28), channel_id=1, source_target_pairs={{9,1},{13,5},{17,9},{21,13},{25,17},{29,21},{10,2},{14,6},{18,10},... | collective-permute-start | bytes 1572872 | tf_op jit(solution)/shard_map/ppermute | solution.py:281
  50.4 4.8 %copy-start.5 = (bf16[16,1,128,128]{3,2,1,0:T(8,128)(2,1)}, bf16[16,1,128,128]{3,2,1,0:T(8,128)(2,1)S(1)}, u32[]{:S(2)}) copy-start(bf16[16,1,128,128]{3,2,1,0:T(8,128)(2,1)S(1)} %collective-permute-done.4.refs_5_.refs_1_) | copy-start | bytes 1572868
  54.6 0.8 copy-start.4
  54.6 1.1 copy-start
  54.6 1.5 copy-start.1
  56.1 9.2 %copy-start.24 = (s32[1,1,8,8]{3,2,1,0:T(8,128)S(1)}, s32[1,1,8,8]{3,2,1,0:T(8,128)}, u32[]{:S(2)}) copy-start(s32[1,1,8,8]{3,2,1,0:T(8,128)} %param.8) | copy-start | bytes 772
  56.1 9.8 %copy-start.25 = (s32[1,1,8,8]{3,2,1,0:T(8,128)S(1)}, s32[1,1,8,8]{3,2,1,0:T(8,128)}, u32[]{:S(2)}) copy-start(s32[1,1,8,8]{3,2,1,0:T(8,128)} %param.7) | copy-start | bytes 772
  56.2 10.5 %copy-start.20 = (s32[1,1,8]{2,1,0:T(1,128)S(1)}, s32[1,1,8]{2,1,0:T(1,128)}, u32[]{:S(2)}) copy-start(s32[1,1,8]{2,1,0:T(1,128)} %param.9) | copy-start | bytes 100
  60.0 53.4 %collective-permute-start.14 = (bf16[16,3,128,128]{3,2,1,0:T(8,128)(2,1)}, bf16[16,3,128,128]{3,2,1,0:T(8,128)(2,1)}, u32[]{:S(2)}, u32[]{:S(2)}) collective-permute-start(bf16[16,3,128,128]{3,2,1,0:T(8,128)(2,1)} %pick_rows.2), channel_id=1, source_target_pairs={{0,4},{4,0},{8,12},{12,8},{16,20},{20,16},{24,28},{28,24},{1,5},{5... | collective-permute-start | bytes 4718600 | tf_op jit(solution)/shard_map/ppermute | solution.py:281
  61.2 42.0 %collective-permute-start.10 = (bf16[16,2,128,128]{3,2,1,0:T(8,128)(2,1)}, bf16[16,2,128,128]{3,2,1,0:T(8,128)(2,1)S(1)}, u32[]{:S(2)}, u32[]{:S(2)}) collective-permute-start(bf16[16,2,128,128]{3,2,1,0:T(8,128)(2,1)} %copy-done), channel_id=1, source_target_pairs={{8,16},{12,20},{16,24},{20,28},{9,17},{13,21},{17,25},{21,29},{10,... | collective-permute-start | bytes 3145736 | tf_op jit(solution)/shard_map/ppermute | solution.py:281
  61.9 41.3 %collective-permute-start.12 = (bf16[16,2,128,128]{3,2,1,0:T(8,128)(2,1)}, bf16[16,2,128,128]{3,2,1,0:T(8,128)(2,1)S(1)}, u32[]{:S(2)}, u32[]{:S(2)}) collective-permute-start(bf16[16,2,128,128]{3,2,1,0:T(8,128)(2,1)} %copy-done.1), channel_id=1, source_target_pairs={{8,0},{12,4},{16,8},{20,12},{9,1},{13,5},{17,9},{21,13},{10,2},{14... | collective-permute-start | bytes 3145736 | tf_op jit(solution)/shard_map/ppermute | solution.py:281
  63.2 16.0 %collective-permute-start.11 = (bf16[16,1,128,128]{3,2,1,0:T(8,128)(2,1)}, bf16[16,1,128,128]{3,2,1,0:T(8,128)(2,1)S(1)}, u32[]{:S(2)}, u32[]{:S(2)}) collective-permute-start(bf16[16,1,128,128]{3,2,1,0:T(8,128)(2,1)} %copy-done.5), channel_id=1, source_target_pairs={{9,17},{13,21},{17,25},{21,29},{10,18},{14,22},{18,26},{22,30}} | collective-permute-start | bytes 1572872 | tf_op jit(solution)/shard_map/ppermute | solution.py:281
  63.9 29.9 %collective-permute-start.13 = (bf16[16,1,128,128]{3,2,1,0:T(8,128)(2,1)}, bf16[16,1,128,128]{3,2,1,0:T(8,128)(2,1)S(1)}, u32[]{:S(2)}, u32[]{:S(2)}) collective-permute-start(bf16[16,1,128,128]{3,2,1,0:T(8,128)(2,1)} %copy-done.4), channel_id=1, source_target_pairs={{9,1},{13,5},{17,9},{21,13},{10,2},{14,6},{18,10},{22,14}} | collective-permute-start | bytes 1572872 | tf_op jit(solution)/shard_map/ppermute | solution.py:281
  79.2 24.0 %copy-start.6 = (bf16[16,1,128,128]{3,2,1,0:T(8,128)(2,1)}, bf16[16,1,128,128]{3,2,1,0:T(8,128)(2,1)S(1)}, u32[]{:S(2)}) copy-start(bf16[16,1,128,128]{3,2,1,0:T(8,128)(2,1)S(1)} %collective-permute-done.11.refs_4_.refs_1_) | copy-start | bytes 1572868
  79.2 19.0 %collective-permute-start.8 = (bf16[4,3,128,128]{3,2,1,0:T(8,128)(2,1)}, bf16[4,3,128,128]{3,2,1,0:T(8,128)(2,1)S(1)}, u32[]{:S(2)}, u32[]{:S(2)}) collective-permute-start(bf16[4,3,128,128]{3,2,1,0:T(8,128)(2,1)} %get-tuple-element.31), channel_id=1, source_target_pairs={{0,1},{1,2},{2,3},{4,5},{5,6},{6,7},{8,9},{9,10},{10,11},{12,13},{... | collective-permute-start | bytes 1179656 | tf_op jit(solution)/shard_map/ppermute | solution.py:308
  93.8 9.4 %copy-start.7 = (bf16[16,1,128,128]{3,2,1,0:T(8,128)(2,1)}, bf16[16,1,128,128]{3,2,1,0:T(8,128)(2,1)S(1)}, u32[]{:S(2)}) copy-start(bf16[16,1,128,128]{3,2,1,0:T(8,128)(2,1)S(1)} %collective-permute-done.13.refs_6_.refs_3_) | copy-start | bytes 1572868
  93.8 9.4 %collective-permute-start.9 = (bf16[4,3,128,128]{3,2,1,0:T(8,128)(2,1)}, bf16[4,3,128,128]{3,2,1,0:T(8,128)(2,1)}, u32[]{:S(2)}, u32[]{:S(2)}) collective-permute-start(bf16[4,3,128,128]{3,2,1,0:T(8,128)(2,1)} %get-tuple-element.32), channel_id=1, source_target_pairs={{1,0},{2,1},{3,2},{5,4},{6,5},{7,6},{9,8},{10,9},{11,10},{13,12},{... | collective-permute-start | bytes 1179656 | tf_op jit(solution)/shard_map/ppermute | solution.py:309
  98.2 5.1 %copy-start.8 = (bf16[4,3,128,128]{3,2,1,0:T(8,128)(2,1)}, bf16[4,3,128,128]{3,2,1,0:T(8,128)(2,1)S(1)}, u32[]{:S(2)}) copy-start(bf16[4,3,128,128]{3,2,1,0:T(8,128)(2,1)S(1)} %collective-permute-done.8.refs_5_.refs_1_) | copy-start | bytes 1179652
  103.2 1.0 copy-start.2
  104.2 1.0 copy-start.3
  109.5 22.7 %collective-permute-start.17 = (bf16[8,3,128,128]{3,2,1,0:T(8,128)(2,1)}, bf16[8,3,128,128]{3,2,1,0:T(8,128)(2,1)S(1)}, u32[]{:S(2)}, u32[]{:S(2)}) collective-permute-start(bf16[8,3,128,128]{3,2,1,0:T(8,128)(2,1)} %get-tuple-element.36), channel_id=1, source_target_pairs={{0,4},{4,0},{8,12},{12,8},{16,20},{20,16},{24,28},{28,24},{1,5},{5... | collective-permute-start | bytes 2359304 | tf_op jit(solution)/shard_map/ppermute | solution.py:281
  113.4 12.2 %copy-start.26 = (bf16[8,2,128,128]{3,2,1,0:T(8,128)(2,1)S(1)}, bf16[8,2,128,128]{3,2,1,0:T(8,128)(2,1)}, u32[]{:S(2)}) copy-start(bf16[8,2,128,128]{3,2,1,0:T(8,128)(2,1)} %get-tuple-element.42) | copy-start | bytes 1572868
  121.1 14.9 %collective-permute-start.15 = (bf16[3,3,128,128]{3,2,1,0:T(8,128)(2,1)}, bf16[3,3,128,128]{3,2,1,0:T(8,128)(2,1)S(1)}, u32[]{:S(2)}, u32[]{:S(2)}) collective-permute-start(bf16[3,3,128,128]{3,2,1,0:T(8,128)(2,1)} %get-tuple-element.34), channel_id=1, source_target_pairs={{0,1},{1,2},{2,3},{4,5},{5,6},{6,7},{8,9},{9,10},{10,11},{12,13},{... | collective-permute-start | bytes 884744 | tf_op jit(solution)/shard_map/ppermute | solution.py:308
  123.0 35.5 %collective-permute-start.20 = (bf16[8,2,128,128]{3,2,1,0:T(8,128)(2,1)}, bf16[8,2,128,128]{3,2,1,0:T(8,128)(2,1)S(1)}, u32[]{:S(2)}, u32[]{:S(2)}) collective-permute-start(bf16[8,2,128,128]{3,2,1,0:T(8,128)(2,1)} %get-tuple-element.40), channel_id=1, source_target_pairs={{0,24},{4,28},{24,0},{28,4},{1,25},{5,29},{25,1},{29,5},{2,26},{6,... | collective-permute-start | bytes 1572872 | tf_op jit(solution)/shard_map/ppermute | solution.py:281
  125.6 32.9 %collective-permute-start.22 = (bf16[8,2,128,128]{3,2,1,0:T(8,128)(2,1)S(1)}, bf16[8,2,128,128]{3,2,1,0:T(8,128)(2,1)S(1)}, u32[]{:S(2)}, u32[]{:S(2)}) collective-permute-start(bf16[8,2,128,128]{3,2,1,0:T(8,128)(2,1)S(1)} %copy-done.26), channel_id=1, source_target_pairs={{0,28},{4,24},{24,4},{28,0},{1,29},{5,25},{25,5},{29,1},{2,30},{6,... | collective-permute-start | bytes 1572872 | tf_op jit(solution)/shard_map/ppermute | solution.py:281
  129.8 12.6 %collective-permute-start.16 = (bf16[3,3,128,128]{3,2,1,0:T(8,128)(2,1)}, bf16[3,3,128,128]{3,2,1,0:T(8,128)(2,1)S(1)}, u32[]{:S(2)}, u32[]{:S(2)}) collective-permute-start(bf16[3,3,128,128]{3,2,1,0:T(8,128)(2,1)} %get-tuple-element.35), channel_id=1, source_target_pairs={{1,0},{2,1},{3,2},{5,4},{6,5},{7,6},{9,8},{10,9},{11,10},{13,12},{... | collective-permute-start | bytes 884744 | tf_op jit(solution)/shard_map/ppermute | solution.py:309
  132.2 10.2 %copy-start.11 = (bf16[8,3,128,128]{3,2,1,0:T(8,128)(2,1)}, bf16[8,3,128,128]{3,2,1,0:T(8,128)(2,1)S(1)}, u32[]{:S(2)}) copy-start(bf16[8,3,128,128]{3,2,1,0:T(8,128)(2,1)S(1)} %collective-permute-done.17.refs_1_) | copy-start | bytes 2359300
  132.3 22.4 %collective-permute-start.21 = (bf16[8,1,128,128]{3,2,1,0:T(8,128)(2,1)}, bf16[8,1,128,128]{3,2,1,0:T(8,128)(2,1)S(1)}, u32[]{:S(2)}, u32[]{:S(2)}) collective-permute-start(bf16[8,1,128,128]{3,2,1,0:T(8,128)(2,1)} %get-tuple-element.41), channel_id=1, source_target_pairs={{1,25},{5,29},{25,1},{29,5},{2,26},{6,30},{26,2},{30,6}} | collective-permute-start | bytes 786440 | tf_op jit(solution)/shard_map/ppermute | solution.py:281
  136.0 6.4 %copy-start.9 = (bf16[3,3,128,128]{3,2,1,0:T(8,128)(2,1)}, bf16[3,3,128,128]{3,2,1,0:T(8,128)(2,1)S(1)}, u32[]{:S(2)}) copy-start(bf16[3,3,128,128]{3,2,1,0:T(8,128)(2,1)S(1)} %collective-permute-done.15.refs_2_.refs_4_) | copy-start | bytes 884740
  136.0 22.5 %collective-permute-start.23 = (bf16[8,1,128,128]{3,2,1,0:T(8,128)(2,1)}, bf16[8,1,128,128]{3,2,1,0:T(8,128)(2,1)S(1)}, u32[]{:S(2)}, u32[]{:S(2)}) collective-permute-start(bf16[8,1,128,128]{3,2,1,0:T(8,128)(2,1)} %get-tuple-element.43), channel_id=1, source_target_pairs={{1,29},{5,25},{25,5},{29,1},{2,30},{6,26},{26,6},{30,2}} | collective-permute-start | bytes 786440 | tf_op jit(solution)/shard_map/ppermute | solution.py:281
  142.5 0.7 copy-start.10
  147.2 11.4 %collective-permute-start.18 = (bf16[1,3,128,128]{3,2,1,0:T(8,128)(2,1)}, bf16[1,3,128,128]{3,2,1,0:T(8,128)(2,1)S(1)}, u32[]{:S(2)}, u32[]{:S(2)}) collective-permute-start(bf16[1,3,128,128]{3,2,1,0:T(8,128)(2,1)} %get-tuple-element.38), channel_id=1, source_target_pairs={{0,1},{1,2},{2,3},{4,5},{5,6},{6,7},{8,9},{9,10},{10,11},{12,13},{... | collective-permute-start | bytes 294920 | tf_op jit(solution)/shard_map/ppermute | solution.py:308
  154.6 6.1 %copy-start.16 = (bf16[8,1,128,128]{3,2,1,0:T(8,128)(2,1)}, bf16[8,1,128,128]{3,2,1,0:T(8,128)(2,1)S(1)}, u32[]{:S(2)}) copy-start(bf16[8,1,128,128]{3,2,1,0:T(8,128)(2,1)S(1)} %collective-permute-done.21.refs_3_) | copy-start | bytes 786436
  154.6 6.1 %collective-permute-start.19 = (bf16[1,3,128,128]{3,2,1,0:T(8,128)(2,1)}, bf16[1,3,128,128]{3,2,1,0:T(8,128)(2,1)S(1)}, u32[]{:S(2)}, u32[]{:S(2)}) collective-permute-start(bf16[1,3,128,128]{3,2,1,0:T(8,128)(2,1)} %get-tuple-element.39), channel_id=1, source_target_pairs={{1,0},{2,1},{3,2},{5,4},{6,5},{7,6},{9,8},{10,9},{11,10},{13,12},{... | collective-permute-start | bytes 294920 | tf_op jit(solution)/shard_map/ppermute | solution.py:309
  158.5 2.3 %copy-start.17 = (bf16[8,1,128,128]{3,2,1,0:T(8,128)(2,1)}, bf16[8,1,128,128]{3,2,1,0:T(8,128)(2,1)S(1)}, u32[]{:S(2)}) copy-start(bf16[8,1,128,128]{3,2,1,0:T(8,128)(2,1)S(1)} %collective-permute-done.23.refs_5_) | copy-start | bytes 786436
  158.5 2.3 %copy-start.12 = (bf16[8,2,128,128]{3,2,1,0:T(8,128)(2,1)}, bf16[8,2,128,128]{3,2,1,0:T(8,128)(2,1)S(1)}, u32[]{:S(2)}) copy-start(bf16[8,2,128,128]{3,2,1,0:T(8,128)(2,1)S(1)} %collective-permute-done.20.refs_2_) | copy-start | bytes 1572868
  158.5 2.2 %copy-start.13 = (bf16[8,2,128,128]{3,2,1,0:T(8,128)(2,1)}, bf16[8,2,128,128]{3,2,1,0:T(8,128)(2,1)S(1)}, u32[]{:S(2)}) copy-start(bf16[8,2,128,128]{3,2,1,0:T(8,128)(2,1)S(1)} %collective-permute-done.22.refs_4_) | copy-start | bytes 1572868
  158.5 2.2 %copy-start.14 = (bf16[1,3,128,128]{3,2,1,0:T(8,128)(2,1)}, bf16[1,3,128,128]{3,2,1,0:T(8,128)(2,1)S(1)}, u32[]{:S(2)}) copy-start(bf16[1,3,128,128]{3,2,1,0:T(8,128)(2,1)S(1)} %collective-permute-done.18.refs_6_.refs_7_) | copy-start | bytes 294916
  160.8 0.6 copy-start.15
  166.8 4.9 %collective-permute-start.24 = (bf16[2,3,128,128]{3,2,1,0:T(8,128)(2,1)}, bf16[2,3,128,128]{3,2,1,0:T(8,128)(2,1)S(1)}, u32[]{:S(2)}, u32[]{:S(2)}) collective-permute-start(bf16[2,3,128,128]{3,2,1,0:T(8,128)(2,1)} %get-tuple-element.45), channel_id=1, source_target_pairs={{0,1},{1,2},{2,3},{4,5},{5,6},{6,7},{8,9},{9,10},{10,11},{12,13},{... | collective-permute-start | bytes 589832 | tf_op jit(solution)/shard_map/ppermute | solution.py:308
  168.7 7.2 %collective-permute-start.25 = (bf16[2,3,128,128]{3,2,1,0:T(8,128)(2,1)}, bf16[2,3,128,128]{3,2,1,0:T(8,128)(2,1)S(1)}, u32[]{:S(2)}, u32[]{:S(2)}) collective-permute-start(bf16[2,3,128,128]{3,2,1,0:T(8,128)(2,1)} %get-tuple-element.46), channel_id=1, source_target_pairs={{1,0},{2,1},{3,2},{5,4},{6,5},{7,6},{9,8},{10,9},{11,10},{13,12},{... | collective-permute-start | bytes 589832 | tf_op jit(solution)/shard_map/ppermute | solution.py:309
  171.8 4.2 %copy-start.18 = (bf16[2,3,128,128]{3,2,1,0:T(8,128)(2,1)}, bf16[2,3,128,128]{3,2,1,0:T(8,128)(2,1)S(1)}, u32[]{:S(2)}) copy-start(bf16[2,3,128,128]{3,2,1,0:T(8,128)(2,1)S(1)} %collective-permute-done.24.refs_10_) | copy-start | bytes 589828
  175.9 0.7 copy-start.19

commit v4 on v0

v4 whole, which is shorter than its diff:
```python
import functools
import jax
import jax.numpy as jnp
from jax import lax
from jax.experimental import pallas as pl
from jax.experimental.pallas import tpu as pltpu
from jax.sharding import PartitionSpec as P

VMEM_LIMIT = 24 * 1024 * 1024
PARAMS = pltpu.CompilerParams(vmem_limit_bytes=VMEM_LIMIT)
COST = pl.CostEstimate(flops=1024, bytes_accessed=1024, transcendentals=0)
PICK_COST = pl.CostEstimate(flops=2 * 10 ** 10, bytes_accessed=1024, transcendentals=0)
ANYWHERE = pl.BlockSpec(memory_space=pl.ANY)


def resident(x):
    return pl.BlockSpec(x.shape, lambda i, *_, n=len(x.shape): (0,) * n)


class Grid:
    def __init__(self, panels):
        self.columns = max(d for d in range(1, panels + 1) if panels % d == 0 and d * d <= panels)
        self.lines = panels // self.columns
        self.sides = range(1, self.columns)
        self.far = [(s, signs, shift) for s in range(3, self.lines)
                    for signs in ([(1, -1)] if 2 * s >= self.lines else [(1,), (-1,)])
                    for shift in range(self.columns)]

    def spot(self):
        place = lax.axis_index("blk")
        return place // self.columns, place % self.columns

    def has(self, z, s, sign):
        return (z + sign * s >= 0) & (z + sign * s < self.lines)

    def panel(self, line, y, shift):
        column = y - shift
        return jnp.clip(line, 0, self.lines - 1) * self.columns + jnp.where(column < 0, column + self.columns, column)

    def second(self, z):
        below = self.has(z, 2, -1)
        return jnp.where(below, z - 2, z + 2), below, self.has(z, 2, 1)

    def hops(self, s, sign):
        return [(h * self.columns + c, (h + sign) * self.columns + c)
                for h in range(self.lines) for c in range(self.columns)
                if 0 <= h + sign < self.lines and 0 <= h + sign - sign * s < self.lines]

    def jumps(self, s, signs, shift):
        return [(h * self.columns + c, (h + sign * s) * self.columns + (c + shift) % self.columns)
                for h in range(self.lines) for sign in signs if 0 <= h + sign * s < self.lines
                for c in range(self.columns)]


    def work_near(self, z, y, cap):
        below, above = self.has(z, 1, -1), self.has(z, 1, 1)
        work = [(self.panel(z, y, 0), True, [(2, 0, True, True)]),
                (self.panel(z - 1, y, 0), below, [(0, 0, True, below)]),
                (self.panel(z + 1, y, 0), above, [(1, 0, True, above)])]
        return work + [(self.panel(z, y, shift), True, [(3 + i, 0, False, True)]) for i, shift in enumerate(self.sides)]

    def work_second(self, z, y, cap):
        line, below, above = self.second(z)
        work = [(self.panel(line, y, 0), below | above, [(0, 0, True, below), (1, 0, True, above)])]
        below, above = self.has(z, 1, -1), self.has(z, 1, 1)
        for i, shift in enumerate(self.sides):
            work += [(self.panel(z - 1, y, shift), below, [(2 + i, 0, False, below)]),
                     (self.panel(z + 1, y, shift), above, [(2 + i, cap, False, above)])]
        return work

    def work_crossed(self, z, y, cap):
        line, below, above = self.second(z)
        return [(self.panel(line, y, shift), below | above, [(i, 0, False, below | above)])
                for i, shift in enumerate(self.sides)]

    def work_far(self, z, y, cap):
        work = []
        for i, (s, signs, shift) in enumerate(self.far):
            present = [self.has(z, s, -sign) for sign in signs]
            line = jnp.where(present[0], z - signs[0] * s, z - signs[-1] * s)
            there = functools.reduce(jnp.logical_or, present)
            work.append((self.panel(line, y, shift), there, [(i, 0, False, there)]))
        return work


def pack_kernel(grid, mask, *refs):
    sides = len(grid.sides)
    wanted, prolong = refs[:sides], refs[sides]
    head, tail, *listed = refs[len(refs) - 2 - sides:]
    group, groups = lax.axis_index("rows"), lax.axis_size("rows")
    width = tail.shape[-1]
    for i in range(prolong.shape[0]):
        blocks = []
        for e in range(3):
            candidate = group + e - 1
            keep = (mask[e, 0, i] == 1) & (candidate >= 0) & (candidate < groups)
            block = prolong[i, :, e * width:(e + 1) * width]
            blocks.append(block * jnp.where(keep, 1.0, 0.0).astype(block.dtype))
        head[i, 0] = jnp.where(group == 0, blocks[1], blocks[0])
        head[i, 1] = jnp.where(group == 0, blocks[2], blocks[1])
        tail[i, 0] = jnp.where(group == 0, blocks[0], blocks[2])
    z, y = grid.spot()
    for rows, out in zip(wanted, listed):
        for entry in range(rows.shape[1]):
            row = rows[grid.panel(z, y, 0), entry]
            out[entry, 0] = head[row, 0]
            out[entry, 1] = head[row, 1]
            out[entry, 2] = tail[row, 0]


def pack(grid, mask, prolong, side_lists, after):
    rows, pores, width3 = prolong.shape
    shapes = [(rows, 2), (rows, 1), *[(x.shape[1], 3) for x in side_lists]]
    outs = [jax.ShapeDtypeStruct((*shape, pores, width3 // 3), prolong.dtype) for shape in shapes]
    return pl.pallas_call(
        functools.partial(pack_kernel, grid),
        grid_spec=pltpu.PrefetchScalarGridSpec(
            num_scalar_prefetch=1 + len(side_lists),
            grid=(1,),
            in_specs=[resident(prolong), *([ANYWHERE] * len(after))],
            out_specs=[*map(resident, outs)],
        ),
        out_shape=outs,
        compiler_params=PARAMS,
        cost_estimate=COST,
        name="pack_rows",
    )(mask, *side_lists, prolong, *after)


def turn_kernel(head, tail, turned):
    width = head.shape[-1]
    for i in range(head.shape[0]):
        for k, block in enumerate((head[i, 0], head[i, 1], tail[i, 0])):
            turned[i, k * width:(k + 1) * width, :] = block.T


def turn(head, tail):
    rows, _, pores, width = head.shape
    out = jax.ShapeDtypeStruct((rows, 3 * width, pores), head.dtype)
    return pl.pallas_call(
        turn_kernel,
        grid=(1,),
        in_specs=[resident(head), resident(tail)],
        out_specs=resident(out),
        out_shape=out,
        compiler_params=PARAMS,
        cost_estimate=COST,
        name="turn_rows",
    )(head, tail)


def pick_kernel(grid, plan, lists, counts, outputs, *refs):
    wanted = refs[:lists]
    arrays, at = [], lists
    for count in counts:
        arrays.append(refs[at:at + count])
        at += count
    outs = refs[len(refs) - outputs:]
    cap = wanted[0].shape[1]
    for index, entry_row, options, target in plan(*grid.spot()):
        for present, source in options:
            def copy(index=index, entry_row=entry_row, source=source, target=target):
                for entry in range(cap):
                    row = wanted[index][entry_row, entry]
                    blocks = [(x, block) for x in arrays[source] for block in range(x.shape[1])]
                    for (x, block), (output, base, place) in zip(blocks, target):
                        outs[output][base + entry, place] = x[row, block]
            if present is True:
                copy()
            else:
                pl.when(present)(copy)


def pick(grid, plan, sizes, lists, sources, after):
    flat = [x for source in sources for x in source]
    shapes = [jax.ShapeDtypeStruct((*size, *flat[0].shape[2:]), flat[0].dtype) for size in sizes]
    return pl.pallas_call(
        functools.partial(
            pick_kernel, grid, plan, len(lists), tuple(len(source) for source in sources), len(sizes)),
        grid_spec=pltpu.PrefetchScalarGridSpec(
            num_scalar_prefetch=len(lists),
            grid=(1,),
            in_specs=[*map(resident, flat), *([ANYWHERE] * len(after))],
            out_specs=[*map(resident, shapes)],
        ),
        out_shape=shapes,
        compiler_params=PARAMS,
        cost_estimate=PICK_COST,
        name="pick_rows",
    )(*lists, *flat, *after)


def stage_kernel(grid, plan, counts, carried, slot_rows, slot_cols, slot_counts, turned, matrix, *refs):
    arrays, at = [], 0
    for count in counts:
        arrays.append(refs[at:at + count])
        at += count
    earlier = refs[at:at + 3] if carried else ()
    own, up, down, total = refs[-4:]
    cap = matrix.shape[1]
    width = own.shape[-1]
    first_group = lax.axis_index("rows") == 0
    for old, new in zip(earlier, (own, up, down)):
        for slot in range(carried):
            for f in range(3):
                new[slot, f] = old[slot, f]
    z, y = grid.spot()
    for slot, (panel, _, sources) in enumerate(plan(z, y, cap), start=carried):
        total[...] = jnp.zeros_like(total)
        for array, base, whole, present in sources:
            live = slot_counts[0, panel]
            if present is not True:
                live = jnp.where(present, live, 0)
            parts = arrays[array]

            def product(entry, whole=whole, base=base, parts=parts, panel=panel):
                pick = slot_cols[panel, entry] if whole else base + entry
                right = jnp.concatenate([x[pick, block] for x in parts for block in range(x.shape[1])], axis=1)
                return jnp.dot(matrix[panel, entry], right, preferred_element_type=jnp.float32)

            def add(left, value):
                result = jnp.dot(left, value, preferred_element_type=jnp.float32)
                for k in range(3):
                    total[k] += result[:, k * width:(k + 1) * width]

            def two(u, carry, product=product, panel=panel):
                first, second = 2 * u, 2 * u + 1
                left = jnp.concatenate(
                    [turned[slot_rows[panel, first]], turned[slot_rows[panel, second]]], axis=1)
                value = jnp.concatenate([product(first), product(second)], axis=0).astype(jnp.bfloat16)
                add(left, value)
                return carry

            lax.fori_loop(0, live // 2, two, 0)

            @pl.when(live % 2 == 1)
            def _(live=live, product=product, panel=panel):
                add(turned[slot_rows[panel, live - 1]], product(live - 1).astype(jnp.bfloat16))

        begin = jnp.where(first_group, 0, width)
        for f in range(3):
            k = jnp.where(first_group, (f + 2) % 3, f)
            own[slot, f] = total[k, pl.ds(pl.multiple_of(begin, width), width), :].astype(own.dtype)
            up[slot, f] = total[k, pl.ds(pl.multiple_of(begin + width, width), width), :].astype(up.dtype)
            down[slot, f] = total[k, 0:width, :].astype(down.dtype)


def stage(grid, plan, lists, turned, matrix, sources, earlier=(), after=()):
    cap = matrix.shape[1]
    width = turned.shape[1] // 3
    carried = earlier[0].shape[0] if earlier else 0
    slots = carried + len(plan(jnp.int32(0), jnp.int32(0), cap))
    flat = [x for source in sources for x in source]
    out = jax.ShapeDtypeStruct((slots, 3, width, width), jnp.bfloat16)
    return pl.pallas_call(
        functools.partial(stage_kernel, grid, plan, tuple(len(source) for source in sources), carried),
        grid_spec=pltpu.PrefetchScalarGridSpec(
            num_scalar_prefetch=3,
            grid=(1,),
            in_specs=[*map(resident, (turned, matrix, *flat, *earlier)), *([ANYWHERE] * len(after))],
            out_specs=[resident(out)] * 3,
            scratch_shapes=[pltpu.VMEM((3, 3 * width, width), jnp.float32)],
        ),
        out_shape=[out] * 3,
        compiler_params=PARAMS,
        cost_estimate=COST,
        name="stage_products",
    )(*lists, turned, matrix, *flat, *earlier, *after)


def assemble_kernel(grid, plans, cap, *refs):
    out = refs[-1]
    rows = refs[0].shape[2]
    panels = grid.lines * grid.columns
    z, y = grid.spot()
    for index, group in enumerate(plans):
        own, lower, upper = refs[3 * index:3 * index + 3]
        slots = [slot for plan in group for slot in plan(z, y, cap)]
        for slot, (panel, present, _) in enumerate(slots):
            def write(slot=slot, own=own, lower=lower, upper=upper, panel=panel):
                for d in range(5):
                    terms = []
                    if 0 <= d - 1 < 3:
                        terms.append(own[slot, d - 1].astype(jnp.float32))
                    if d < 3:
                        terms.append(lower[slot, d].astype(jnp.float32))
                    if 0 <= d - 2 < 3:
                        terms.append(upper[slot, d - 2].astype(jnp.float32))
                    out[pl.ds(d * panels + panel, rows, stride=5 * panels), :] = functools.reduce(jnp.add, terms)
            if present is True:
                write()
            else:
                pl.when(present)(write)


def assemble(grid, plans, cap, pieces):
    panels = grid.lines * grid.columns
    width = pieces[0][0].shape[-1]
    rows = width // 4
    flat = [x for piece in pieces for x in piece]
    result = pl.pallas_call(
        functools.partial(assemble_kernel, grid, plans, cap),
        grid=(width // rows,),
        in_specs=[pl.BlockSpec((x.shape[0], 3, rows, width), lambda i: (0, 0, i, 0)) for x in flat],
        out_specs=pl.BlockSpec((rows * 5 * panels, width), lambda i: (i, 0)),
        out_shape=jax.ShapeDtypeStruct((width * 5 * panels, width), jnp.float32),
        compiler_params=PARAMS,
        cost_estimate=COST,
        name="assemble_coarse",
    )(*flat)
    return result.reshape(width, 5, panels, width).transpose(0, 2, 1, 3)


def per_device(fine_blocks, block_rows, block_cols, block_counts, prolong_blocks, prolong_mask):
    matrix = fine_blocks[0, 0]
    cols_list = block_cols[0, 0]
    lists = (block_rows[0, 0], cols_list, block_counts[0])
    cap = cols_list.shape[1]
    panels = lax.axis_size("blk")
    groups = lax.axis_size("rows")
    grid = Grid(panels)
    sides, far = grid.sides, grid.far
    every, inner = range(groups), range(1, groups - 1)

    def move(x, pairs, members=every):
        perm = [(a * groups + g, b * groups + g) for g in members for a, b in pairs]
        return lax.ppermute(x, ("blk", "rows"), perm) if perm else jnp.zeros_like(x)

    def move_both(pair, pairs):
        return move(pair[0], pairs), move(pair[1], pairs, inner)

    def back(pairs):
        return [(b, a) for a, b in pairs]

    def exchange(parts):
        lower = lax.ppermute(parts[1], "rows", [(g, g + 1) for g in range(groups - 1)])
        upper = lax.ppermute(parts[2], "rows", [(g + 1, g) for g in range(groups - 1)])
        return parts[0], lower, upper

    side_lists = [move(cols_list, back(grid.jumps(0, (1,), shift))) for shift in sides]
    far_lists = [move(cols_list, back(grid.jumps(*entry))) for entry in far]

    head, tail, *picked = pack(grid, prolong_mask.transpose(2, 0, 1), prolong_blocks[0], side_lists, far_lists)
    own = (head, tail)
    near = [move_both(own, grid.hops(1, 1)), move_both(own, grid.hops(1, -1))]
    beside = [move(x, grid.jumps(0, (1,), shift)) for x, shift in zip(picked, sides)]
    turned = turn(head, tail)

    second = [move_both(near[0], grid.hops(2, 1)), move_both(near[1], grid.hops(2, -1))]

    def near_requests(z, y):
        return [(index, grid.panel(z + step, y, 0), [(True, side)], [(index, side * cap, k) for k in range(3)])
                for index in range(len(sides)) for side, step in enumerate((-1, 1))]

    picked = pick(grid, near_requests, [(2 * cap, 3)] * len(sides), side_lists, near, beside)
    crossed = [move(x, grid.jumps(0, (1,), shift)) for x, shift in zip(picked, sides)]
    parts = stage(grid, grid.work_near, lists, turned, matrix, [*near, own, *[(x,) for x in beside]])

    def second_requests(z, y):
        line, below, above = grid.second(z)
        requests = [(index, grid.panel(line, y, 0), [(below, 0), (above, 1)], [(index, 0, k) for k in range(3)])
                    for index in range(len(sides))]
        for index in range(len(sides), len(sides) + len(far)):
            requests.append((index, grid.panel(z, y, 0), [(True, 2)], [(index, 0, k) for k in range(3)]))
        return requests

    sizes = [(cap, 3)] * (len(sides) + len(far))
    picked = pick(grid, second_requests, sizes, [*side_lists, *far_lists], [*second, own], [parts[0]])
    second_crossed = [move(x, grid.jumps(0, (1,), shift)) for x, shift in zip(picked, sides)]
    far_crossed = [move(x, grid.jumps(*entry)) for x, entry in zip(picked[len(sides):], far)]
    parts = stage(grid, grid.work_second, lists, turned, matrix, [*second, *[(x,) for x in crossed]], parts)
    first = exchange(parts)
    parts = stage(grid, grid.work_crossed, lists, turned, matrix, [(x,) for x in second_crossed], (), [parts[0]])

    parts = stage(grid, grid.work_far, lists, turned, matrix, [(x,) for x in far_crossed], parts, first[1:])
    last = exchange(parts)
    plans = ((grid.work_near, grid.work_second), (grid.work_crossed, grid.work_far))
    return assemble(grid, plans, cap, [first, last])[None, None]


def solution(mesh):
    in_specs = (
        P("rows", "blk", None, None, None, None),
        P("rows", "blk", None, None),
        P("rows", "blk", None, None),
        P("rows", "blk", None),
        P("rows", "blk", None, None),
        P("rows", "blk", None),
    )
    out_specs = P("rows", "blk", None, None, None, None)
    return jax.shard_map(
        per_device, mesh=mesh, in_specs=in_specs, out_specs=out_specs, check_vma=False
    )
```

time: 324 us -> 140 us (0.43)
  waiting for transfers between devices: 189 us -> 64 us
  local copies, waits for them, and re-layouts: 52.7 us -> 2.11 us
  starting transfers between devices: 5.97 us -> 55.2 us
  matrix products: 38.6 us -> 0 us
  other arithmetic: 22 us -> 0 us
  Pallas kernels: 0 us -> 17.6 us
  between operations: 13.5 us -> 0.28 us
    all_gather x1 -> x0, waiting for transfers between devices: 178 us -> none  [per_device(): panel_rows = lax.all_gather(masked, 'blk', axis=0, tiled=True)]
    ppermute x2 -> x20, waiting for transfers between devices: 11.2 us -> 64 us  [the longest x16 57.7 us: move(): return lax.ppermute(x, ('blk', 'rows'), perm) if perm else jnp.zeros_like(x)]
    ppermute x2 -> x20, starting transfers between devices: 5.97 us -> 55.2 us  [the longest x16 32.6 us: move(): return lax.ppermute(x, ('blk', 'rows'), perm) if perm else jnp.zeros_like(x)]
    dot_general x17 -> x0, matrix products: 38.6 us -> none  [the longest x8 17.4 us: row_products(): jnp.einsum('pr,pwy->rwy', selector_mask, block_products, precision=lax.Pr...]
    dynamic_update_slice x16 -> x0, local copies, waits for them, and re-layouts: 19.6 us -> none  [store_slab(): return lax.dynamic_update_index_in_dim(current, slab, peer_index, 0)]
    dynamic_slice x16 -> x0, local copies, waits for them, and re-layouts: 18 us -> none  [the longest x8 12.7 us: one_shard(): lax.dynamic_slice_in_dim(panel_rows, shard_step * shard_rows, shard_rows, 0)]
    pallas_call x0 -> x9, Pallas kernels: none -> 17.6 us  [the longest x4 12 us: stage(): pl.pallas_call(functools.partial(stage_kernel, grid, plan, tuple((len(sou...]
    gather x8 -> x0, local copies, waits for them, and re-layouts: 5.73 us -> none  [row_products(): chosen_entries = jnp.take(panel_rows, cols_here, axis=0)]
  transfers between devices with their start and end apart: 3 -> 20, of which waited for: 3 -> 10; matrix products, arithmetic and copies ran while one was open for 1% -> 0% of each run, Pallas kernels for 0% -> 7%
where the time goes in v4:
time: 140 us; the launch traced here: 139 us
  waiting for transfers between devices  64 us (46%)
  starting transfers between devices  55.2 us (39%)
  Pallas kernels  17.6 us (13%)
  local copies, waits for them, and re-layouts  2.11 us (2%)
    ppermute x16, waiting for transfers between devices, move(): return lax.ppermute(x, ('blk', 'rows'), perm) if perm else jnp.zeros_like(x)  57.7 us
    ppermute x16, starting transfers between devices, move(): return lax.ppermute(x, ('blk', 'rows'), perm) if perm else jnp.zeros_like(x)  32.6 us
    ppermute x2, starting transfers between devices, exchange(): lax.ppermute(parts[1], 'rows', [(g, g + 1) for g in range(groups - 1)])  18.3 us
    pallas_call x4, Pallas kernels, stage(): pl.pallas_call(functools.partial(stage_kernel, grid, plan, tuple((len(sou...  12 us
    ppermute x2, waiting for transfers between devices, exchange(): lax.ppermute(parts[2], 'rows', [(g + 1, g) for g in range(groups - 1)])  5.08 us
    ppermute x2, starting transfers between devices, exchange(): lax.ppermute(parts[2], 'rows', [(g + 1, g) for g in range(groups - 1)])  4.34 us
  transfers between devices with their start and end apart: 20, of which 10 were waited for; matrix products, arithmetic and copies ran while one was open for 0% of the time, Pallas kernels for 7%

profile of v4, /device:TPU:1, one launch (start us, length us, event | category | flops | bytes accessed | tf_op | source)
XLA Modules:
  0.0 139.2 jit_solution(8036613017587988099)
XLA Ops:
  0.0 7.0 %collective-permute-start.2 = (s32[8,8]{1,0:T(8,128)}, s32[8,8]{1,0:T(8,128)S(1)}, u32[]{:S(2)}, u32[]{:S(2)}) collective-permute-start(s32[8,8]{1,0:T(8,128)} %bitcast.20), channel_id=1, source_target_pairs={{28,0},{24,4},{4,24},{0,28},{29,1},{25,5},{5,25},{1,29},{30,2},{26... | collective-permute-start | bytes 776 | tf_op jit(solution)/shard_map/ppermute | solution.py:327
  7.0 1.9 %collective-permute-start.1 = (s32[8,8]{1,0:T(8,128)}, s32[8,8]{1,0:T(8,128)S(1)}, u32[]{:S(2)}, u32[]{:S(2)}) collective-permute-start(s32[8,8]{1,0:T(8,128)} %bitcast.21), channel_id=1, source_target_pairs={{24,0},{28,4},{0,24},{4,28},{25,1},{29,5},{1,25},{5,29},{26,2},{30... | collective-permute-start | bytes 776 | tf_op jit(solution)/shard_map/ppermute | solution.py:327
  8.9 0.3 collective-permute-start
  9.3 0.0 collective-permute-done.2.refs_3_.refs_2_
  9.3 4.2 %collective-permute-done.1.refs_2_.refs_1_ = s32[8,8]{1,0:T(8,128)S(1)} collective-permute-done((s32[8,8]{1,0:T(8,128)}, s32[8,8]{1,0:T(8,128)S(1)}, u32[]{:S(2)}, u32[]{:S(2)}) %collective-permute-start.1) | collective-permute-done | bytes 288 | tf_op jit(solution)/shard_map/ppermute | solution.py:327
  13.5 0.0 collective-permute-done.refs_0_
  13.5 0.0 copy-start.1
  13.5 1.4 %copy-done.1 = bf16[1,16,128,384]{3,2,1,0:T(8,128)(2,1)S(1)} copy-done((bf16[1,16,128,384]{3,2,1,0:T(8,128)(2,1)S(1)}, bf16[1,16,128,384]{3,2,1,0:T(8,128)(2,1)}, u32[]{:S(2)}) %copy-start.1) | copy-done | bytes 1572888
  14.9 0.0 copy-start.5
  14.9 0.7 copy-done.5
  15.6 1.0 pack_rows.1
  16.6 1.3 collective-permute-start.7
  17.9 4.1 %collective-permute-start.3 = (bf16[16,2,128,128]{3,2,1,0:T(8,128)(2,1)S(1)}, bf16[16,2,128,128]{3,2,1,0:T(8,128)(2,1)S(1)}, u32[]{:S(2)}, u32[]{:S(2)}) collective-permute-start(bf16[16,2,128,128]{3,2,1,0:T(8,128)(2,1)S(1)} %get-tuple-element.23.head.refs_4_.refs_7_), channel_id=1, source_target_pairs={{0,8},{4,12},{8,16},{12,20},{16,24},{20,28},{1,9},{5,13},{9,17},{1... | collective-permute-start | bytes 3145736 | tf_op jit(solution)/shard_map/ppermute | solution.py:327
  21.9 0.2 collective-permute-start.11
  22.1 1.3 collective-permute-start.9
  23.4 4.0 %collective-permute-start.5 = (bf16[16,1,128,128]{3,2,1,0:T(8,128)(2,1)S(1)}, bf16[16,1,128,128]{3,2,1,0:T(8,128)(2,1)S(1)}, u32[]{:S(2)}, u32[]{:S(2)}) collective-permute-start(bf16[16,1,128,128]{3,2,1,0:T(8,128)(2,1)S(1)} %get-tuple-element.24.tail.refs_5_.refs_8_), channel_id=1, source_target_pairs={{1,9},{5,13},{9,17},{13,21},{17,25},{21,29},{2,10},{6,14},{10,18},... | collective-permute-start | bytes 1572872 | tf_op jit(solution)/shard_map/ppermute | solution.py:327
  27.4 0.5 turn_rows.1.turned
  27.9 0.0 copy-start
  27.9 0.0 copy-start.2
  27.9 0.0 copy-start.3
  27.9 0.0 copy-start.4
  27.9 21.0 %collective-permute-done.9.refs_4_.refs_3_ = bf16[16,1,128,128]{3,2,1,0:T(8,128)(2,1)S(1)} collective-permute-done((bf16[16,1,128,128]{3,2,1,0:T(8,128)(2,1)S(1)}, bf16[16,1,128,128]{3,2,1,0:T(8,128)(2,1)S(1)}, u32[]{:S(2)}, u32[]{:S(2)}) %collective-permute-start.9) | collective-permute-done | bytes 524320 | tf_op jit(solution)/shard_map/ppermute | solution.py:327
  49.0 1.3 collective-permute-start.10
  50.3 0.2 collective-permute-done.5.refs_2_.refs_1_
  50.4 0.7 collective-permute-start.6
  51.1 0.0 collective-permute-done.7.refs_3_.refs_2_
  51.1 1.3 collective-permute-start.8
  52.4 0.0 collective-permute-done.3.refs_1_.refs_0_
  52.5 0.7 collective-permute-start.4
  53.2 0.0 collective-permute-done.11.refs_5_.refs_6_
  53.2 0.7 pick_rows.2
  53.9 0.2 collective-permute-start.12
  54.1 0.0 copy-done
  54.1 0.0 copy-done.2
  54.1 0.0 copy-done.3
  54.1 0.0 copy-done.4
  54.1 2.3 %stage_products.4 = (bf16[4,3,128,128]{3,2,1,0:T(8,128)(2,1)S(1)}, bf16[4,3,128,128]{3,2,1,0:T(8,128)(2,1)S(1)}, bf16[4,3,128,128]{3,2,1,0:T(8,128)(2,1)S(1)}) custom-call(s32[8,8]{1,0:T(8,128)S(1)} %bitcast.16, s32[8,8]{1,0:T(8,128)S(1)} %bitcast.23, s32[1,8]{1,0:T(1,128)S(1)} %bitcast.27, bf16[16,384,128]{2,1,0:T(8,128)(2,1)S(1)} %turn_rows.1.turned, ...), custom_call_target="tpu_custom_call" | custom-call | flops 1024 | bytes 1024 | tf_op jit(solution)/shard_map/stage_products/pallas_call | solution.py:255
  56.5 8.4 %collective-permute-done.10.refs_3_.refs_6_ = bf16[16,1,128,128]{3,2,1,0:T(8,128)(2,1)S(1)} collective-permute-done((bf16[16,1,128,128]{3,2,1,0:T(8,128)(2,1)S(1)}, bf16[16,1,128,128]{3,2,1,0:T(8,128)(2,1)S(1)}, u32[]{:S(2)}, u32[]{:S(2)}) %collective-permute-start.10) | collective-permute-done | bytes 524320 | tf_op jit(solution)/shard_map/ppermute | solution.py:327
  64.9 0.0 collective-permute-done.6.refs_1_.refs_4_
  64.9 14.9 %collective-permute-done.8.refs_2_.refs_5_ = bf16[16,2,128,128]{3,2,1,0:T(8,128)(2,1)S(1)} collective-permute-done((bf16[16,2,128,128]{3,2,1,0:T(8,128)(2,1)S(1)}, bf16[16,2,128,128]{3,2,1,0:T(8,128)(2,1)S(1)}, u32[]{:S(2)}, u32[]{:S(2)}) %collective-permute-start.8) | collective-permute-done | bytes 1048608 | tf_op jit(solution)/shard_map/ppermute | solution.py:327
  79.8 0.0 collective-permute-done.4.refs_0_.refs_3_
  79.8 0.9 pick_rows.3
  80.7 0.3 collective-permute-start.17
  81.0 5.0 %collective-permute-start.15 = (bf16[8,3,128,128]{3,2,1,0:T(8,128)(2,1)S(1)}, bf16[8,3,128,128]{3,2,1,0:T(8,128)(2,1)S(1)}, u32[]{:S(2)}, u32[]{:S(2)}) collective-permute-start(bf16[8,3,128,128]{3,2,1,0:T(8,128)(2,1)S(1)} %get-tuple-element.32), channel_id=1, source_target_pairs={{0,24},{4,28},{24,0},{28,4},{1,25},{5,29},{25,1},{29,5},{2,26},{6,... | collective-permute-start | bytes 2359304 | tf_op jit(solution)/shard_map/ppermute | solution.py:327
  86.0 3.0 %collective-permute-start.16 = (bf16[8,3,128,128]{3,2,1,0:T(8,128)(2,1)S(1)}, bf16[8,3,128,128]{3,2,1,0:T(8,128)(2,1)S(1)}, u32[]{:S(2)}, u32[]{:S(2)}) collective-permute-start(bf16[8,3,128,128]{3,2,1,0:T(8,128)(2,1)S(1)} %get-tuple-element.33), channel_id=1, source_target_pairs={{0,28},{4,24},{24,4},{28,0},{1,29},{5,25},{25,5},{29,1},{2,30},{6,... | collective-permute-start | bytes 2359304 | tf_op jit(solution)/shard_map/ppermute | solution.py:327
  89.1 1.4 %collective-permute-done.12.refs_4_ = bf16[16,3,128,128]{3,2,1,0:T(8,128)(2,1)S(1)} collective-permute-done((bf16[16,3,128,128]{3,2,1,0:T(8,128)(2,1)S(1)}, bf16[16,3,128,128]{3,2,1,0:T(8,128)(2,1)S(1)}, u32[]{:S(2)}, u32[]{:S(2)}) %collective-permute-start.12) | collective-permute-done | bytes 1572896 | tf_op jit(solution)/shard_map/ppermute | solution.py:327
  90.5 3.6 %stage_products.5 = (bf16[7,3,128,128]{3,2,1,0:T(8,128)(2,1)S(1)}, bf16[7,3,128,128]{3,2,1,0:T(8,128)(2,1)S(1)}, bf16[7,3,128,128]{3,2,1,0:T(8,128)(2,1)S(1)}) custom-call(s32[8,8]{1,0:T(8,128)S(1)} %bitcast.17, s32[8,8]{1,0:T(8,128)S(1)} %bitcast.24, s32[1,8]{1,0:T(1,128)S(1)} %bitcast.28, bf16[16,384,128]{2,1,0:T(8,128)(2,1)S(1)} %turn_rows.1.turned, ...), custom_call_target="tpu_custom_call" | custom-call | flops 1024 | bytes 1024 | tf_op jit(solution)/shard_map/stage_products/pallas_call | solution.py:255
  94.1 16.4 %collective-permute-start.13 = (bf16[7,3,128,128]{3,2,1,0:T(8,128)(2,1)S(1)}, bf16[7,3,128,128]{3,2,1,0:T(8,128)(2,1)S(1)}, u32[]{:S(2)}, u32[]{:S(2)}) collective-permute-start(bf16[7,3,128,128]{3,2,1,0:T(8,128)(2,1)S(1)} %get-tuple-element.30), channel_id=1, source_target_pairs={{0,1},{1,2},{2,3},{4,5},{5,6},{6,7},{8,9},{9,10},{10,11},{12,13},{... | collective-permute-start | bytes 2064392 | tf_op jit(solution)/shard_map/ppermute | solution.py:336
  110.5 1.9 %collective-permute-start.14 = (bf16[7,3,128,128]{3,2,1,0:T(8,128)(2,1)S(1)}, bf16[7,3,128,128]{3,2,1,0:T(8,128)(2,1)S(1)}, u32[]{:S(2)}, u32[]{:S(2)}) collective-permute-start(bf16[7,3,128,128]{3,2,1,0:T(8,128)(2,1)S(1)} %get-tuple-element.31), channel_id=1, source_target_pairs={{1,0},{2,1},{3,2},{5,4},{6,5},{7,6},{9,8},{10,9},{11,10},{13,12},{... | collective-permute-start | bytes 2064392 | tf_op jit(solution)/shard_map/ppermute | solution.py:337
  112.4 7.5 %collective-permute-done.17.refs_0_ = bf16[8,3,128,128]{3,2,1,0:T(8,128)(2,1)S(1)} collective-permute-done((bf16[8,3,128,128]{3,2,1,0:T(8,128)(2,1)S(1)}, bf16[8,3,128,128]{3,2,1,0:T(8,128)(2,1)S(1)}, u32[]{:S(2)}, u32[]{:S(2)}) %collective-permute-start.17) | collective-permute-done | bytes 786464 | tf_op jit(solution)/shard_map/ppermute | solution.py:327
  119.9 2.1 %stage_products.6 = (bf16[1,3,128,128]{3,2,1,0:T(8,128)(2,1)S(1)}, bf16[1,3,128,128]{3,2,1,0:T(8,128)(2,1)S(1)}, bf16[1,3,128,128]{3,2,1,0:T(8,128)(2,1)S(1)}) custom-call(s32[8,8]{1,0:T(8,128)S(1)} %bitcast.18, s32[8,8]{1,0:T(8,128)S(1)} %bitcast.25, s32[1,8]{1,0:T(1,128)S(1)} %bitcast.29, bf16[16,384,128]{2,1,0:T(8,128)(2,1)S(1)} %turn_rows.1.turned, ...), custom_call_target="tpu_custom_call" | custom-call | flops 1024 | bytes 1024 | tf_op jit(solution)/shard_map/stage_products/pallas_call | solution.py:255
  122.0 0.0 collective-permute-done.15.refs_0_
  122.0 0.0 collective-permute-done.16.refs_1_
  122.0 0.0 collective-permute-done.13.refs_5_.refs_1_
  122.0 0.7 collective-permute-done.14.refs_6_.refs_2_
  122.7 3.9 %stage_products.7 = (bf16[3,3,128,128]{3,2,1,0:T(8,128)(2,1)S(1)}, bf16[3,3,128,128]{3,2,1,0:T(8,128)(2,1)S(1)}, bf16[3,3,128,128]{3,2,1,0:T(8,128)(2,1)S(1)}) custom-call(s32[8,8]{1,0:T(8,128)S(1)} %bitcast.19, s32[8,8]{1,0:T(8,128)S(1)} %bitcast.26, s32[1,8]{1,0:T(1,128)S(1)} %bitcast.30, bf16[16,384,128]{2,1,0:T(8,128)(2,1)S(1)} %turn_rows.1.turned, ...), custom_call_target="tpu_custom_call" | custom-call | flops 1024 | bytes 1024 | tf_op jit(solution)/shard_map/stage_products/pallas_call | solution.py:255
  126.7 1.9 %collective-permute-start.18 = (bf16[3,3,128,128]{3,2,1,0:T(8,128)(2,1)S(1)}, bf16[3,3,128,128]{3,2,1,0:T(8,128)(2,1)S(1)}, u32[]{:S(2)}, u32[]{:S(2)}) collective-permute-start(bf16[3,3,128,128]{3,2,1,0:T(8,128)(2,1)S(1)} %get-tuple-element.39), channel_id=1, source_target_pairs={{0,1},{1,2},{2,3},{4,5},{5,6},{6,7},{8,9},{9,10},{10,11},{12,13},{... | collective-permute-start | bytes 884744 | tf_op jit(solution)/shard_map/ppermute | solution.py:336
  128.6 2.4 %collective-permute-start.19 = (bf16[3,3,128,128]{3,2,1,0:T(8,128)(2,1)S(1)}, bf16[3,3,128,128]{3,2,1,0:T(8,128)(2,1)S(1)}, u32[]{:S(2)}, u32[]{:S(2)}) collective-permute-start(bf16[3,3,128,128]{3,2,1,0:T(8,128)(2,1)S(1)} %get-tuple-element.40), channel_id=1, source_target_pairs={{1,0},{2,1},{3,2},{5,4},{6,5},{7,6},{9,8},{10,9},{11,10},{13,12},{... | collective-permute-start | bytes 884744 | tf_op jit(solution)/shard_map/ppermute | solution.py:337
  131.0 1.2 collective-permute-done.18.refs_4_
  132.3 4.4 %collective-permute-done.19.refs_5_ = bf16[3,3,128,128]{3,2,1,0:T(8,128)(2,1)S(1)} collective-permute-done((bf16[3,3,128,128]{3,2,1,0:T(8,128)(2,1)S(1)}, bf16[3,3,128,128]{3,2,1,0:T(8,128)(2,1)S(1)}, u32[]{:S(2)}, u32[]{:S(2)}) %collective-permute-start.19) | collective-permute-done | bytes 294944 | tf_op jit(solution)/shard_map/ppermute | solution.py:337
  136.7 2.5 %assemble_coarse.1 = f32[5120,128]{1,0:T(8,128)} custom-call(bf16[7,3,128,128]{3,2,1,0:T(8,128)(2,1)S(1)} %get-tuple-element.29.refs_1_.refs_0_, bf16[7,3,128,128]{3,2,1,0:T(8,128)(2,1)S(1)} %collective-permute-done.13.refs_5_.refs_1_, bf16[7,3,128,128]{3,2,1,0:T(8,128)(2,1)S(1)} %collective-permute-done.14.refs_6_.refs_2_, ...), custom_call_target="tpu_custom_call" | custom-call | flops 1024 | bytes 1024 | tf_op jit(solution)/shard_map/assemble_coarse/pallas_call | solution.py:301
Async XLA Ops:
  0.0 9.3 %collective-permute-start.2 = (s32[8,8]{1,0:T(8,128)}, s32[8,8]{1,0:T(8,128)S(1)}, u32[]{:S(2)}, u32[]{:S(2)}) collective-permute-start(s32[8,8]{1,0:T(8,128)} %bitcast.20), channel_id=1, source_target_pairs={{28,0},{24,4},{4,24},{0,28},{29,1},{25,5},{5,25},{1,29},{30,2},{26... | collective-permute-start | bytes 776 | tf_op jit(solution)/shard_map/ppermute | solution.py:327
  7.0 6.5 %collective-permute-start.1 = (s32[8,8]{1,0:T(8,128)}, s32[8,8]{1,0:T(8,128)S(1)}, u32[]{:S(2)}, u32[]{:S(2)}) collective-permute-start(s32[8,8]{1,0:T(8,128)} %bitcast.21), channel_id=1, source_target_pairs={{24,0},{28,4},{0,24},{4,28},{25,1},{29,5},{1,25},{5,29},{26,2},{30... | collective-permute-start | bytes 776 | tf_op jit(solution)/shard_map/ppermute | solution.py:327
  8.9 4.5 %collective-permute-start = (s32[8,8]{1,0:T(8,128)}, s32[8,8]{1,0:T(8,128)S(1)}, u32[]{:S(2)}, u32[]{:S(2)}) collective-permute-start(s32[8,8]{1,0:T(8,128)} %bitcast.22), channel_id=1, source_target_pairs={{4,0},{0,4},{12,8},{8,12},{20,16},{16,20},{28,24},{24,28},{5,1},{1... | collective-permute-start | bytes 776 | tf_op jit(solution)/shard_map/ppermute | solution.py:327
  13.5 1.4 %copy-start.1 = (bf16[1,16,128,384]{3,2,1,0:T(8,128)(2,1)S(1)}, bf16[1,16,128,384]{3,2,1,0:T(8,128)(2,1)}, u32[]{:S(2)}) copy-start(bf16[1,16,128,384]{3,2,1,0:T(8,128)(2,1)} %param.10) | copy-start | bytes 4718596
  14.9 0.7 copy-start.5
  16.6 34.6 %collective-permute-start.7 = (bf16[16,2,128,128]{3,2,1,0:T(8,128)(2,1)S(1)}, bf16[16,2,128,128]{3,2,1,0:T(8,128)(2,1)S(1)}, u32[]{:S(2)}, u32[]{:S(2)}) collective-permute-start(bf16[16,2,128,128]{3,2,1,0:T(8,128)(2,1)S(1)} %get-tuple-element.23.head.refs_4_.refs_7_), channel_id=1, source_target_pairs={{8,0},{12,4},{16,8},{20,12},{24,16},{28,20},{9,1},{13,5},{17,9},{2... | collective-permute-start | bytes 3145736 | tf_op jit(solution)/shard_map/ppermute | solution.py:327
  17.9 34.6 %collective-permute-start.3 = (bf16[16,2,128,128]{3,2,1,0:T(8,128)(2,1)S(1)}, bf16[16,2,128,128]{3,2,1,0:T(8,128)(2,1)S(1)}, u32[]{:S(2)}, u32[]{:S(2)}) collective-permute-start(bf16[16,2,128,128]{3,2,1,0:T(8,128)(2,1)S(1)} %get-tuple-element.23.head.refs_4_.refs_7_), channel_id=1, source_target_pairs={{0,8},{4,12},{8,16},{12,20},{16,24},{20,28},{1,9},{5,13},{9,17},{1... | collective-permute-start | bytes 3145736 | tf_op jit(solution)/shard_map/ppermute | solution.py:327
  21.9 31.3 %collective-permute-start.11 = (bf16[8,3,128,128]{3,2,1,0:T(8,128)(2,1)S(1)}, bf16[8,3,128,128]{3,2,1,0:T(8,128)(2,1)S(1)}, u32[]{:S(2)}, u32[]{:S(2)}) collective-permute-start(bf16[8,3,128,128]{3,2,1,0:T(8,128)(2,1)S(1)} %get-tuple-element.25), channel_id=1, source_target_pairs={{0,4},{4,0},{8,12},{12,8},{16,20},{20,16},{24,28},{28,24},{1,5},{5... | collective-permute-start | bytes 2359304 | tf_op jit(solution)/shard_map/ppermute | solution.py:327
  22.1 26.8 %collective-permute-start.9 = (bf16[16,1,128,128]{3,2,1,0:T(8,128)(2,1)S(1)}, bf16[16,1,128,128]{3,2,1,0:T(8,128)(2,1)S(1)}, u32[]{:S(2)}, u32[]{:S(2)}) collective-permute-start(bf16[16,1,128,128]{3,2,1,0:T(8,128)(2,1)S(1)} %get-tuple-element.24.tail.refs_5_.refs_8_), channel_id=1, source_target_pairs={{9,1},{13,5},{17,9},{21,13},{25,17},{29,21},{10,2},{14,6},{18,10},... | collective-permute-start | bytes 1572872 | tf_op jit(solution)/shard_map/ppermute | solution.py:327
  23.4 27.0 %collective-permute-start.5 = (bf16[16,1,128,128]{3,2,1,0:T(8,128)(2,1)S(1)}, bf16[16,1,128,128]{3,2,1,0:T(8,128)(2,1)S(1)}, u32[]{:S(2)}, u32[]{:S(2)}) collective-permute-start(bf16[16,1,128,128]{3,2,1,0:T(8,128)(2,1)S(1)} %get-tuple-element.24.tail.refs_5_.refs_8_), channel_id=1, source_target_pairs={{1,9},{5,13},{9,17},{13,21},{17,25},{21,29},{2,10},{6,14},{10,18},... | collective-permute-start | bytes 1572872 | tf_op jit(solution)/shard_map/ppermute | solution.py:327
  27.9 26.2 %copy-start = (bf16[1,1,8,8,128,128]{5,4,3,2,1,0:T(8,128)(2,1)S(1)}, bf16[1,1,8,8,128,128]{5,4,3,2,1,0:T(8,128)(2,1)}, u32[]{:S(2)}) copy-start(bf16[1,1,8,8,128,128]{5,4,3,2,1,0:T(8,128)(2,1)} %param.6) | copy-start | bytes 6291460
  27.9 26.2 %copy-start.2 = (s32[1,1,8,8]{3,2,1,0:T(8,128)S(1)}, s32[1,1,8,8]{3,2,1,0:T(8,128)}, u32[]{:S(2)}) copy-start(s32[1,1,8,8]{3,2,1,0:T(8,128)} %param.7) | copy-start | bytes 772
  27.9 26.2 %copy-start.3 = (s32[1,1,8,8]{3,2,1,0:T(8,128)S(1)}, s32[1,1,8,8]{3,2,1,0:T(8,128)}, u32[]{:S(2)}) copy-start(s32[1,1,8,8]{3,2,1,0:T(8,128)} %param.8) | copy-start | bytes 772
  27.9 26.2 %copy-start.4 = (s32[1,1,8]{2,1,0:T(1,128)S(1)}, s32[1,1,8]{2,1,0:T(1,128)}, u32[]{:S(2)}) copy-start(s32[1,1,8]{2,1,0:T(1,128)} %param.9) | copy-start | bytes 100
  49.0 15.9 %collective-permute-start.10 = (bf16[16,1,128,128]{3,2,1,0:T(8,128)(2,1)S(1)}, bf16[16,1,128,128]{3,2,1,0:T(8,128)(2,1)S(1)}, u32[]{:S(2)}, u32[]{:S(2)}) collective-permute-start(bf16[16,1,128,128]{3,2,1,0:T(8,128)(2,1)S(1)} %collective-permute-done.9.refs_4_.refs_3_), channel_id=1, source_target_pairs={{9,1},{13,5},{17,9},{21,13},{10,2},{14,6},{18,10},{22,14}} | collective-permute-start | bytes 1572872 | tf_op jit(solution)/shard_map/ppermute | solution.py:327
  50.4 14.4 %collective-permute-start.6 = (bf16[16,1,128,128]{3,2,1,0:T(8,128)(2,1)S(1)}, bf16[16,1,128,128]{3,2,1,0:T(8,128)(2,1)S(1)}, u32[]{:S(2)}, u32[]{:S(2)}) collective-permute-start(bf16[16,1,128,128]{3,2,1,0:T(8,128)(2,1)S(1)} %collective-permute-done.5.refs_2_.refs_1_), channel_id=1, source_target_pairs={{9,17},{13,21},{17,25},{21,29},{10,18},{14,22},{18,26},{22,30}} | collective-permute-start | bytes 1572872 | tf_op jit(solution)/shard_map/ppermute | solution.py:327
  51.1 28.7 %collective-permute-start.8 = (bf16[16,2,128,128]{3,2,1,0:T(8,128)(2,1)S(1)}, bf16[16,2,128,128]{3,2,1,0:T(8,128)(2,1)S(1)}, u32[]{:S(2)}, u32[]{:S(2)}) collective-permute-start(bf16[16,2,128,128]{3,2,1,0:T(8,128)(2,1)S(1)} %collective-permute-done.7.refs_3_.refs_2_), channel_id=1, source_target_pairs={{8,0},{12,4},{16,8},{20,12},{9,1},{13,5},{17,9},{21,13},{10,2},{14... | collective-permute-start | bytes 3145736 | tf_op jit(solution)/shard_map/ppermute | solution.py:327
  52.5 27.4 %collective-permute-start.4 = (bf16[16,2,128,128]{3,2,1,0:T(8,128)(2,1)S(1)}, bf16[16,2,128,128]{3,2,1,0:T(8,128)(2,1)S(1)}, u32[]{:S(2)}, u32[]{:S(2)}) collective-permute-start(bf16[16,2,128,128]{3,2,1,0:T(8,128)(2,1)S(1)} %collective-permute-done.3.refs_1_.refs_0_), channel_id=1, source_target_pairs={{8,16},{12,20},{16,24},{20,28},{9,17},{13,21},{17,25},{21,29},{10,... | collective-permute-start | bytes 3145736 | tf_op jit(solution)/shard_map/ppermute | solution.py:327
  53.9 36.5 %collective-permute-start.12 = (bf16[16,3,128,128]{3,2,1,0:T(8,128)(2,1)S(1)}, bf16[16,3,128,128]{3,2,1,0:T(8,128)(2,1)S(1)}, u32[]{:S(2)}, u32[]{:S(2)}) collective-permute-start(bf16[16,3,128,128]{3,2,1,0:T(8,128)(2,1)S(1)} %pick_rows.2), channel_id=1, source_target_pairs={{0,4},{4,0},{8,12},{12,8},{16,20},{20,16},{24,28},{28,24},{1,5},{5... | collective-permute-start | bytes 4718600 | tf_op jit(solution)/shard_map/ppermute | solution.py:327
  80.7 39.2 %collective-permute-start.17 = (bf16[8,3,128,128]{3,2,1,0:T(8,128)(2,1)S(1)}, bf16[8,3,128,128]{3,2,1,0:T(8,128)(2,1)S(1)}, u32[]{:S(2)}, u32[]{:S(2)}) collective-permute-start(bf16[8,3,128,128]{3,2,1,0:T(8,128)(2,1)S(1)} %get-tuple-element.34), channel_id=1, source_target_pairs={{0,4},{4,0},{8,12},{12,8},{16,20},{20,16},{24,28},{28,24},{1,5},{5... | collective-permute-start | bytes 2359304 | tf_op jit(solution)/shard_map/ppermute | solution.py:327
  81.0 41.0 %collective-permute-start.15 = (bf16[8,3,128,128]{3,2,1,0:T(8,128)(2,1)S(1)}, bf16[8,3,128,128]{3,2,1,0:T(8,128)(2,1)S(1)}, u32[]{:S(2)}, u32[]{:S(2)}) collective-permute-start(bf16[8,3,128,128]{3,2,1,0:T(8,128)(2,1)S(1)} %get-tuple-element.32), channel_id=1, source_target_pairs={{0,24},{4,28},{24,0},{28,4},{1,25},{5,29},{25,1},{29,5},{2,26},{6,... | collective-permute-start | bytes 2359304 | tf_op jit(solution)/shard_map/ppermute | solution.py:327
  86.0 36.0 %collective-permute-start.16 = (bf16[8,3,128,128]{3,2,1,0:T(8,128)(2,1)S(1)}, bf16[8,3,128,128]{3,2,1,0:T(8,128)(2,1)S(1)}, u32[]{:S(2)}, u32[]{:S(2)}) collective-permute-start(bf16[8,3,128,128]{3,2,1,0:T(8,128)(2,1)S(1)} %get-tuple-element.33), channel_id=1, source_target_pairs={{0,28},{4,24},{24,4},{28,0},{1,29},{5,25},{25,5},{29,1},{2,30},{6,... | collective-permute-start | bytes 2359304 | tf_op jit(solution)/shard_map/ppermute | solution.py:327
  94.1 27.9 %collective-permute-start.13 = (bf16[7,3,128,128]{3,2,1,0:T(8,128)(2,1)S(1)}, bf16[7,3,128,128]{3,2,1,0:T(8,128)(2,1)S(1)}, u32[]{:S(2)}, u32[]{:S(2)}) collective-permute-start(bf16[7,3,128,128]{3,2,1,0:T(8,128)(2,1)S(1)} %get-tuple-element.30), channel_id=1, source_target_pairs={{0,1},{1,2},{2,3},{4,5},{5,6},{6,7},{8,9},{9,10},{10,11},{12,13},{... | collective-permute-start | bytes 2064392 | tf_op jit(solution)/shard_map/ppermute | solution.py:336
  110.5 12.3 %collective-permute-start.14 = (bf16[7,3,128,128]{3,2,1,0:T(8,128)(2,1)S(1)}, bf16[7,3,128,128]{3,2,1,0:T(8,128)(2,1)S(1)}, u32[]{:S(2)}, u32[]{:S(2)}) collective-permute-start(bf16[7,3,128,128]{3,2,1,0:T(8,128)(2,1)S(1)} %get-tuple-element.31), channel_id=1, source_target_pairs={{1,0},{2,1},{3,2},{5,4},{6,5},{7,6},{9,8},{10,9},{11,10},{13,12},{... | collective-permute-start | bytes 2064392 | tf_op jit(solution)/shard_map/ppermute | solution.py:337
  126.7 5.6 %collective-permute-start.18 = (bf16[3,3,128,128]{3,2,1,0:T(8,128)(2,1)S(1)}, bf16[3,3,128,128]{3,2,1,0:T(8,128)(2,1)S(1)}, u32[]{:S(2)}, u32[]{:S(2)}) collective-permute-start(bf16[3,3,128,128]{3,2,1,0:T(8,128)(2,1)S(1)} %get-tuple-element.39), channel_id=1, source_target_pairs={{0,1},{1,2},{2,3},{4,5},{5,6},{6,7},{8,9},{9,10},{10,11},{12,13},{... | collective-permute-start | bytes 884744 | tf_op jit(solution)/shard_map/ppermute | solution.py:336
  128.6 8.0 %collective-permute-start.19 = (bf16[3,3,128,128]{3,2,1,0:T(8,128)(2,1)S(1)}, bf16[3,3,128,128]{3,2,1,0:T(8,128)(2,1)S(1)}, u32[]{:S(2)}, u32[]{:S(2)}) collective-permute-start(bf16[3,3,128,128]{3,2,1,0:T(8,128)(2,1)S(1)} %get-tuple-element.40), channel_id=1, source_target_pairs={{1,0},{2,1},{3,2},{5,4},{6,5},{7,6},{9,8},{10,9},{11,10},{13,12},{... | collective-permute-start | bytes 884744 | tf_op jit(solution)/shard_map/ppermute | solution.py:337

commit v5 on v4

v5 whole, which is shorter than its diff:
```python
import functools
import jax
import jax.numpy as jnp
from jax import lax
from jax.experimental import pallas as pl
from jax.experimental.pallas import tpu as pltpu
from jax.sharding import PartitionSpec as P

VMEM_LIMIT = 24 * 1024 * 1024
PARAMS = pltpu.CompilerParams(vmem_limit_bytes=VMEM_LIMIT)
COST = pl.CostEstimate(flops=1024, bytes_accessed=1024, transcendentals=0)
NEAR_COST = pl.CostEstimate(flops=6 * 10 ** 9, bytes_accessed=1024, transcendentals=0)
PICK_COST = pl.CostEstimate(flops=2 * 10 ** 10, bytes_accessed=1024, transcendentals=0)
ANYWHERE = pl.BlockSpec(memory_space=pl.ANY)


def resident(x):
    return pl.BlockSpec(x.shape, lambda i, *_, n=len(x.shape): (0,) * n)


LINES = 4


class Grid:
    def __init__(self, panels, cap, pores):
        self.panels, self.cap, self.pores = panels, cap, pores
        self.columns = panels // LINES
        self.sides = range(1, self.columns)
        self.list_rows = -(-panels // 16) * 16

    def spot(self):
        place = lax.axis_index("blk")
        return place // self.columns, place % self.columns

    def has(self, z, s, sign):
        return (z + sign * s >= 0) & (z + sign * s < LINES)

    def panel(self, line, y, shift):
        column = y - shift
        return jnp.clip(line, 0, LINES - 1) * self.columns + jnp.where(column < 0, column + self.columns, column)

    def second(self, z):
        below = self.has(z, 2, -1)
        return jnp.where(below, z - 2, z + 2), below, self.has(z, 2, 1)

    def hops(self, s, sign):
        return [(h * self.columns + c, (h + sign) * self.columns + c)
                for h in range(LINES) for c in range(self.columns)
                if 0 <= h + sign < LINES and 0 <= h + sign - sign * s < LINES]

    def across(self, shift):
        return [(h * self.columns + c, h * self.columns + (c + shift) % self.columns)
                for h in range(LINES) for c in range(self.columns)]

    def ends(self, shift):
        return [(h * self.columns + c, end * self.columns + (c + shift) % self.columns)
                for h, end in ((1, 0), (LINES - 2, LINES - 1)) for c in range(self.columns)]

    def part(self, ref, blocks, row, block):
        start = (row * blocks + block) * self.pores
        if not isinstance(start, int):
            start = pl.multiple_of(start, self.pores)
        return ref.at[pl.ds(start, self.pores), :]

    def shape(self, rows, blocks, width, lists=0):
        return jax.ShapeDtypeStruct((rows * blocks * self.pores + lists * self.list_rows, width), jnp.bfloat16)


    def work_near(self, z, y):
        below, above = self.has(z, 1, -1), self.has(z, 1, 1)
        work = [(self.panel(z, y, 0), True, [(2, 0, True, True)]),
                (self.panel(z - 1, y, 0), below, [(0, 0, True, below)]),
                (self.panel(z + 1, y, 0), above, [(1, 0, True, above)])]
        return work + [(self.panel(z, y, shift), True, [(3 + i, 0, False, True)]) for i, shift in enumerate(self.sides)]

    def work_second(self, z, y):
        line, below, above = self.second(z)
        work = [(self.panel(line, y, 0), below | above, [(0, 0, True, below), (1, 0, True, above)])]
        below, above = self.has(z, 1, -1), self.has(z, 1, 1)
        for i, shift in enumerate(self.sides):
            work += [(self.panel(z - 1, y, shift), below, [(2 + i, 0, False, below)]),
                     (self.panel(z + 1, y, shift), above, [(2 + i, self.cap, False, above)])]
        return work

    def work_crossed(self, z, y):
        line, below, above = self.second(z)
        return [(self.panel(line, y, shift), below | above, [(i, 0, False, below | above)])
                for i, shift in enumerate(self.sides)]

    def work_far(self, z, y):
        there = (z == 0) | (z == LINES - 1)
        return [(self.panel(LINES - 1 - z, y, shift), there, [(shift, 0, False, there)])
                for shift in range(self.columns)]


def pack_kernel(grid, mask, cols, prolong, head, tail):
    group, groups = lax.axis_index("rows"), lax.axis_size("rows")
    width = tail.shape[-1]
    for i in range(prolong.shape[0]):
        blocks = []
        for e in range(3):
            candidate = group + e - 1
            keep = (mask[e, 0, i] == 1) & (candidate >= 0) & (candidate < groups)
            block = prolong[i, :, e * width:(e + 1) * width]
            blocks.append(block * jnp.where(keep, 1.0, 0.0).astype(block.dtype))
        grid.part(head, 2, i, 0)[...] = jnp.where(group == 0, blocks[1], blocks[0])
        grid.part(head, 2, i, 1)[...] = jnp.where(group == 0, blocks[2], blocks[1])
        grid.part(tail, 1, i, 0)[...] = jnp.where(group == 0, blocks[0], blocks[2])
    row = lax.broadcasted_iota(jnp.int32, (grid.list_rows, width), 0)
    column = lax.broadcasted_iota(jnp.int32, (grid.list_rows, width), 1)
    numbers = jnp.zeros((grid.list_rows, width), jnp.int32)
    for panel in range(grid.panels):
        for entry in range(grid.cap):
            numbers = jnp.where((row == panel) & (column == entry), cols[panel, entry], numbers)
    start = prolong.shape[0] * 2 * grid.pores
    head[start:start + grid.list_rows, :] = numbers.astype(jnp.float32).astype(head.dtype)


def pack(grid, mask, cols, prolong):
    rows, _, width3 = prolong.shape
    outs = [grid.shape(rows, 2, width3 // 3, 1), grid.shape(rows, 1, width3 // 3)]
    return pl.pallas_call(
        functools.partial(pack_kernel, grid),
        grid_spec=pltpu.PrefetchScalarGridSpec(
            num_scalar_prefetch=2,
            grid=(1,),
            in_specs=[resident(prolong)],
            out_specs=[*map(resident, outs)],
        ),
        out_shape=outs,
        compiler_params=PARAMS,
        cost_estimate=COST,
        name="pack_rows",
    )(mask, cols, prolong)


def turn_kernel(grid, head, tail, turned):
    width = head.shape[-1]
    for i in range(turned.shape[0]):
        parts = (grid.part(head, 2, i, 0), grid.part(head, 2, i, 1), grid.part(tail, 1, i, 0))
        for k, part in enumerate(parts):
            turned[i, k * width:(k + 1) * width, :] = part[...].T


def turn(grid, head, tail):
    rows, width = tail.shape[0] // grid.pores, tail.shape[1]
    out = jax.ShapeDtypeStruct((rows, 3 * width, grid.pores), head.dtype)
    return pl.pallas_call(
        functools.partial(turn_kernel, grid),
        grid=(1,),
        in_specs=[resident(head), resident(tail)],
        out_specs=resident(out),
        out_shape=out,
        compiler_params=PARAMS,
        cost_estimate=COST,
        name="turn_rows",
    )(head, tail)


def pick_kernel(grid, plan, layout, carry, tables, lists, outputs, *refs):
    wanted = list(refs[:lists])
    sources, at = [], lists
    for blocks in layout:
        sources.append([(refs[at + i], k) for i, k in enumerate(blocks)])
        at += len(blocks)
    scratch = 2 * len(tables) + 1 if tables else 0
    outs = refs[len(refs) - outputs - scratch:len(refs) - scratch]
    z, y = grid.spot()

    def list_at(ref, place):
        start = ref.shape[0] - (place + 1) * grid.list_rows
        return ref[start:start + grid.list_rows, :]

    if tables:
        numbers, plain, done = refs[-scratch:-1 - len(tables)], refs[-1 - len(tables):-1], refs[-1]
        for table, options in enumerate(tables):
            value = None
            for present, source, place in options:
                here = list_at(sources[source][0][0], place).astype(jnp.float32)
                value = here if value is None else jnp.where(present(z), here, value)
            numbers[table][...] = value.astype(jnp.int32)
            pltpu.make_async_copy(numbers[table], plain[table], done.at[table]).start()
        for table in range(len(tables)):
            pltpu.make_async_copy(numbers[table], plain[table], done.at[table]).wait()
        wanted += plain
    for index, list_row, options, output, base in plan(z, y):
        for present, source in options:
            def copy(index=index, list_row=list_row, source=source, output=output, base=base):
                for entry in range(grid.cap):
                    row = wanted[index][list_row, entry]
                    place = 0
                    for ref, blocks in sources[source]:
                        for block in range(blocks):
                            grid.part(outs[output], 3, base + entry, place)[...] = grid.part(ref, blocks, row, block)[...]
                            place += 1
            if present is True:
                copy()
            else:
                pl.when(present)(copy)
    for source, place in carry:
        for out in outs:
            start = out.shape[0] - (place + 1) * grid.list_rows
            out[start:start + grid.list_rows, :] = list_at(sources[source][0][0], 0)


def pick(grid, plan, sizes, lists, sources, carry=(), tables=(), after=(), cost=COST):
    flat = [x for source in sources for x, _ in source]
    width = flat[0].shape[-1]
    shapes = [grid.shape(size, 3, width, len(carry)) for size in sizes]
    layout = tuple(tuple(blocks for _, blocks in source) for source in sources)
    table = (grid.list_rows, width)
    scratch = [pltpu.VMEM(table, jnp.int32)] * len(tables) + [pltpu.SMEM(table, jnp.int32)] * len(tables)
    scratch += [pltpu.SemaphoreType.DMA((len(tables),))] if tables else []
    return pl.pallas_call(
        functools.partial(pick_kernel, grid, plan, layout, carry, tables, len(lists), len(sizes)),
        grid_spec=pltpu.PrefetchScalarGridSpec(
            num_scalar_prefetch=len(lists),
            grid=(1,),
            in_specs=[*map(resident, flat), *([ANYWHERE] * len(after))],
            out_specs=[*map(resident, shapes)],
            scratch_shapes=scratch,
        ),
        out_shape=shapes,
        compiler_params=PARAMS,
        cost_estimate=cost,
        name="pick_rows",
    )(*lists, *flat, *after)


def stage_kernel(grid, plan, layout, carried, slot_rows, slot_cols, slot_counts, turned, matrix, *refs):
    arrays, at = [], 0
    for blocks in layout:
        arrays.append([(refs[at + i], k) for i, k in enumerate(blocks)])
        at += len(blocks)
    earlier = refs[at:at + 3] if carried else ()
    own, up, down, total = refs[-4:]
    width = own.shape[-1]
    first_group = lax.axis_index("rows") == 0
    for old, new in zip(earlier, (own, up, down)):
        for slot in range(carried):
            for f in range(3):
                new[slot, f] = old[slot, f]
    z, y = grid.spot()
    for slot, (panel, _, sources) in enumerate(plan(z, y), start=carried):
        total[...] = jnp.zeros_like(total)
        for array, base, whole, present in sources:
            live = slot_counts[0, panel]
            if present is not True:
                live = jnp.where(present, live, 0)
            parts = arrays[array]

            def product(entry, whole=whole, base=base, parts=parts, panel=panel):
                pick = slot_cols[panel, entry] if whole else base + entry
                right = jnp.concatenate(
                    [grid.part(x, blocks, pick, block)[...] for x, blocks in parts for block in range(blocks)], axis=1)
                return jnp.dot(matrix[panel, entry], right, preferred_element_type=jnp.float32)

            def add(left, value):
                result = jnp.dot(left, value, preferred_element_type=jnp.float32)
                for k in range(3):
                    total[k] += result[:, k * width:(k + 1) * width]

            def two(u, carry, product=product, panel=panel):
                first, second = 2 * u, 2 * u + 1
                left = jnp.concatenate(
                    [turned[slot_rows[panel, first]], turned[slot_rows[panel, second]]], axis=1)
                value = jnp.concatenate([product(first), product(second)], axis=0).astype(jnp.bfloat16)
                add(left, value)
                return carry

            lax.fori_loop(0, live // 2, two, 0)

            @pl.when(live % 2 == 1)
            def _(live=live, product=product, panel=panel):
                add(turned[slot_rows[panel, live - 1]], product(live - 1).astype(jnp.bfloat16))

        begin = jnp.where(first_group, 0, width)
        for f in range(3):
            k = jnp.where(first_group, (f + 2) % 3, f)
            own[slot, f] = total[k, pl.ds(pl.multiple_of(begin, width), width), :].astype(own.dtype)
            up[slot, f] = total[k, pl.ds(pl.multiple_of(begin + width, width), width), :].astype(up.dtype)
            down[slot, f] = total[k, 0:width, :].astype(down.dtype)


def stage(grid, plan, lists, turned, matrix, sources, earlier=(), after=()):
    width = turned.shape[1] // 3
    carried = earlier[0].shape[0] if earlier else 0
    slots = carried + len(plan(jnp.int32(0), jnp.int32(0)))
    flat = [x for source in sources for x, _ in source]
    layout = tuple(tuple(blocks for _, blocks in source) for source in sources)
    out = jax.ShapeDtypeStruct((slots, 3, width, width), jnp.bfloat16)
    return pl.pallas_call(
        functools.partial(stage_kernel, grid, plan, layout, carried),
        grid_spec=pltpu.PrefetchScalarGridSpec(
            num_scalar_prefetch=3,
            grid=(1,),
            in_specs=[*map(resident, (turned, matrix, *flat, *earlier)), *([ANYWHERE] * len(after))],
            out_specs=[resident(out)] * 3,
            scratch_shapes=[pltpu.VMEM((3, 3 * width, width), jnp.float32)],
        ),
        out_shape=[out] * 3,
        compiler_params=PARAMS,
        cost_estimate=COST,
        name="stage_products",
    )(*lists, turned, matrix, *flat, *earlier, *after)


def assemble_kernel(grid, plans, *refs):
    out = refs[-1]
    rows = refs[0].shape[2]
    panels = grid.panels
    z, y = grid.spot()
    for index, group in enumerate(plans):
        own, lower, upper = refs[3 * index:3 * index + 3]
        slots = [slot for plan in group for slot in plan(z, y)]
        for slot, (panel, present, _) in enumerate(slots):
            def write(slot=slot, own=own, lower=lower, upper=upper, panel=panel):
                for d in range(5):
                    terms = []
                    if 0 <= d - 1 < 3:
                        terms.append(own[slot, d - 1].astype(jnp.float32))
                    if d < 3:
                        terms.append(lower[slot, d].astype(jnp.float32))
                    if 0 <= d - 2 < 3:
                        terms.append(upper[slot, d - 2].astype(jnp.float32))
                    out[pl.ds(d * panels + panel, rows, stride=5 * panels), :] = functools.reduce(jnp.add, terms)
            if present is True:
                write()
            else:
                pl.when(present)(write)


def assemble(grid, plans, pieces):
    panels = grid.panels
    width = pieces[0][0].shape[-1]
    rows = width // 4
    flat = [x for piece in pieces for x in piece]
    result = pl.pallas_call(
        functools.partial(assemble_kernel, grid, plans),
        grid=(width // rows,),
        in_specs=[pl.BlockSpec((x.shape[0], 3, rows, width), lambda i: (0, 0, i, 0)) for x in flat],
        out_specs=pl.BlockSpec((rows * 5 * panels, width), lambda i: (i, 0)),
        out_shape=jax.ShapeDtypeStruct((width * 5 * panels, width), jnp.float32),
        compiler_params=PARAMS,
        cost_estimate=COST,
        name="assemble_coarse",
    )(*flat)
    return result.reshape(width, 5, panels, width).transpose(0, 2, 1, 3)


def per_device(fine_blocks, block_rows, block_cols, block_counts, prolong_blocks, prolong_mask):
    matrix = fine_blocks[0, 0]
    cols_list = block_cols[0, 0]
    lists = (block_rows[0, 0], cols_list, block_counts[0])
    groups = lax.axis_size("rows")
    grid = Grid(lax.axis_size("blk"), cols_list.shape[1], matrix.shape[2])
    cap, sides, columns = grid.cap, grid.sides, grid.columns
    every, inner = range(groups), range(1, groups - 1)

    def move(x, pairs, members=every):
        perm = [(a * groups + g, b * groups + g) for g in members for a, b in pairs]
        return lax.ppermute(x, ("blk", "rows"), perm) if perm else jnp.zeros_like(x)

    def move_both(pair, pairs):
        return (move(pair[0][0], pairs), 2), (move(pair[1][0], pairs, inner), 1)

    def move_across(arrays):
        return [((move(x, grid.across(shift)), 3),) for x, shift in zip(arrays, sides)]

    def exchange(parts):
        lower = lax.ppermute(parts[1], "rows", [(g, g + 1) for g in range(groups - 1)])
        upper = lax.ppermute(parts[2], "rows", [(g + 1, g) for g in range(groups - 1)])
        return parts[0], lower, upper

    head, tail = pack(grid, prolong_mask.transpose(2, 0, 1), cols_list, prolong_blocks[0])
    own = ((head, 2), (tail, 1))
    near = [move_both(own, grid.hops(1, 1)), move_both(own, grid.hops(1, -1))]
    side_lists = [move(cols_list, [(b, a) for a, b in grid.across(shift)]) for shift in sides]

    def own_requests(z, y):
        return [(index, grid.panel(z, y, 0), [(True, 0)], index, 0) for index in range(len(sides))]

    beside = move_across(pick(grid, own_requests, [cap] * len(sides), side_lists, [own]))
    turned = turn(grid, head, tail)

    second = [move_both(near[0], grid.hops(2, 1)), move_both(near[1], grid.hops(2, -1))]

    def near_requests(z, y):
        return [(index, grid.panel(z + step, y, 0), [(True, side)], index, side * cap)
                for index in range(len(sides)) for side, step in enumerate((-1, 1))]

    picked = pick(grid, near_requests, [2 * cap] * len(sides), side_lists, near, ((0, 1), (1, 0)),
                  after=[x for ((x, _),) in beside], cost=NEAR_COST)
    crossed = move_across(picked)
    parts = stage(grid, grid.work_near, lists, turned, matrix, [*near, own, *beside])

    def second_requests(z, y):
        line, below, above = grid.second(z)
        return [(index, grid.panel(line, y, 0), [(below, 0), (above, 1)], index, 0) for index in range(columns)]

    def far_requests(z, y):
        line, below, above = grid.second(z)
        return [(index, grid.panel(line, y, 0), [(below, 0), (above, 1)], index, 0) for index in range(len(sides))]

    def low(z):
        return z == 1

    picked = pick(grid, second_requests, [cap] * columns, side_lists, [*second, *near],
                  tables=(((None, 3, 0), (low, 2, 0)),), after=[parts[0]], cost=PICK_COST)
    second_crossed = move_across(picked[:-1])
    far = [((move(picked[-1], grid.ends(0)), 3),)]
    tables = tuple(((None, 2 + columns - 1 - shift, 0), (low, 2 + columns - 1 - shift, 1)) for shift in sides)
    picked = pick(grid, far_requests, [cap] * len(sides), [], [*second, *crossed], tables=tables)
    far += [((move(x, grid.ends(shift)), 3),) for shift, x in zip(sides, picked)]
    parts = stage(grid, grid.work_second, lists, turned, matrix, [*second, *crossed], parts)
    first = exchange(parts)
    parts = stage(grid, grid.work_crossed, lists, turned, matrix, second_crossed, (), [parts[0]])

    parts = stage(grid, grid.work_far, lists, turned, matrix, far, parts, first[1:])
    last = exchange(parts)
    plans = ((grid.work_near, grid.work_second), (grid.work_crossed, grid.work_far))
    return assemble(grid, plans, [first, last])[None, None]


def solution(mesh):
    in_specs = (
        P("rows", "blk", None, None, None, None),
        P("rows", "blk", None, None),
        P("rows", "blk", None, None),
        P("rows", "blk", None),
        P("rows", "blk", None, None),
        P("rows", "blk", None),
    )
    out_specs = P("rows", "blk", None, None, None, None)
    return jax.shard_map(
        per_device, mesh=mesh, in_specs=in_specs, out_specs=out_specs, check_vma=False
    )
```

time: 140 us -> 129 us (0.921); the launches traced: 139 us -> 127 us
  starting transfers between devices: 55.2 us -> 42.7 us
  waiting for transfers between devices: 64 us -> 61.2 us
  Pallas kernels: 17.6 us -> 19.6 us
    ppermute x16 -> x14, starting transfers between devices: 32.6 us -> 23.8 us  [move(): return lax.ppermute(x, ('blk', 'rows'), perm) if perm else jnp.zeros_like(x)]
    ppermute x2, starting transfers between devices: 18.3 us -> 14.6 us  [exchange(): lax.ppermute(parts[1], 'rows', [(g, g + 1) for g in range(groups - 1)])]
    ppermute x16 -> x14, waiting for transfers between devices: 57.7 us -> 55.5 us  [move(): return lax.ppermute(x, ('blk', 'rows'), perm) if perm else jnp.zeros_like(x)]
    pallas_call x8 -> x10, Pallas kernels: 16.6 us -> 18.6 us  [the longest x4 12 us: stage(): pl.pallas_call(functools.partial(stage_kernel, grid, plan, layout, carrie...]
  transfers between devices with their start and end apart: 20 -> 18, of which waited for: 10 -> 9; matrix products, arithmetic and copies ran while one was open for 0% -> 0% of each run, Pallas kernels for 7% -> 9%
where the time goes in v5:
time: 129 us; the launch traced here: 127 us
  waiting for transfers between devices  61.2 us (47%)
  starting transfers between devices  42.7 us (33%)
  Pallas kernels  19.6 us (15%)
  local copies, waits for them, and re-layouts  2.8 us (2%)
    ppermute x14, waiting for transfers between devices, move(): return lax.ppermute(x, ('blk', 'rows'), perm) if perm else jnp.zeros_like(x)  55.5 us
    ppermute x14, starting transfers between devices, move(): return lax.ppermute(x, ('blk', 'rows'), perm) if perm else jnp.zeros_like(x)  23.8 us
    ppermute x2, starting transfers between devices, exchange(): lax.ppermute(parts[1], 'rows', [(g, g + 1) for g in range(groups - 1)])  14.6 us
    pallas_call x4, Pallas kernels, stage(): pl.pallas_call(functools.partial(stage_kernel, grid, plan, layout, carrie...  12 us
    ppermute x2, waiting for transfers between devices, exchange(): lax.ppermute(parts[2], 'rows', [(g + 1, g) for g in range(groups - 1)])  4.4 us
    ppermute x2, starting transfers between devices, exchange(): lax.ppermute(parts[2], 'rows', [(g + 1, g) for g in range(groups - 1)])  4.34 us
    pallas_call x4, Pallas kernels, pick(): pl.pallas_call(functools.partial(pick_kernel, grid, plan, layout, carry,...  3.57 us
    unnamed x14, local copies, waits for them, and re-layouts  2.8 us
  transfers between devices with their start and end apart: 18, of which 9 were waited for; matrix products, arithmetic and copies ran while one was open for 0% of the time, Pallas kernels for 9%

profile of v5, /device:TPU:1, one launch (start us, length us, event | category | flops | bytes accessed | tf_op | source)
XLA Modules:
  0.0 126.5 jit_solution(1996834462459359746)
XLA Ops:
  0.0 0.0 copy-start.1
  0.0 1.4 %copy-done.1 = bf16[1,16,128,384]{3,2,1,0:T(8,128)(2,1)S(1)} copy-done((bf16[1,16,128,384]{3,2,1,0:T(8,128)(2,1)S(1)}, bf16[1,16,128,384]{3,2,1,0:T(8,128)(2,1)}, u32[]{:S(2)}) %copy-start.1) | copy-done | bytes 1572888
  1.4 0.0 copy-start.2
  1.4 0.7 copy-done.2
  2.1 0.0 copy-start.6
  2.1 0.7 copy-done.6
  2.8 1.0 pack_rows.1
  3.8 1.3 %collective-permute-start.4 = (bf16[4112,128]{1,0:T(8,128)(2,1)S(1)}, bf16[4112,128]{1,0:T(8,128)(2,1)S(1)}, u32[]{:S(2)}, u32[]{:S(2)}) collective-permute-start(bf16[4112,128]{1,0:T(8,128)(2,1)S(1)} %get-tuple-element.21.head.refs_1_.refs_4_), channel_id=1, source_target_pairs={{8,0},{12,4},{16,8},{20,12},{24,16},{28,20},{9,1},{13,5},{17,9},{2... | collective-permute-start | bytes 3158024 | tf_op jit(solution)/shard_map/ppermute | solution.py:362
  5.1 4.7 %collective-permute-start = (bf16[4112,128]{1,0:T(8,128)(2,1)S(1)}, bf16[4112,128]{1,0:T(8,128)(2,1)S(1)}, u32[]{:S(2)}, u32[]{:S(2)}) collective-permute-start(bf16[4112,128]{1,0:T(8,128)(2,1)S(1)} %get-tuple-element.21.head.refs_1_.refs_4_), channel_id=1, source_target_pairs={{0,8},{4,12},{8,16},{12,20},{16,24},{20,28},{1,9},{5,13},{9,17},{1... | collective-permute-start | bytes 3158024 | tf_op jit(solution)/shard_map/ppermute | solution.py:362
  9.8 1.5 %collective-permute-start.8 = (s32[8,8]{1,0:T(8,128)S(1)}, s32[8,8]{1,0:T(8,128)S(1)}, u32[]{:S(2)}, u32[]{:S(2)}) collective-permute-start(s32[8,8]{1,0:T(8,128)S(1)} %bitcast.17), channel_id=1, source_target_pairs={{4,0},{0,4},{12,8},{8,12},{20,16},{16,20},{28,24},{24,28},{5,1},{1... | collective-permute-start | bytes 776 | tf_op jit(solution)/shard_map/ppermute | solution.py:362
  11.2 1.4 %collective-permute-done.8.refs_0_ = s32[8,8]{1,0:T(8,128)S(1)} collective-permute-done((s32[8,8]{1,0:T(8,128)S(1)}, s32[8,8]{1,0:T(8,128)S(1)}, u32[]{:S(2)}, u32[]{:S(2)}) %collective-permute-start.8) | collective-permute-done | bytes 288 | tf_op jit(solution)/shard_map/ppermute | solution.py:362
  12.6 0.7 pick_rows.4
  13.3 1.5 %collective-permute-start.9 = (bf16[3072,128]{1,0:T(8,128)(2,1)S(1)}, bf16[3072,128]{1,0:T(8,128)(2,1)S(1)}, u32[]{:S(2)}, u32[]{:S(2)}) collective-permute-start(bf16[3072,128]{1,0:T(8,128)(2,1)S(1)} %pick_rows.4), channel_id=1, source_target_pairs={{0,4},{4,0},{8,12},{12,8},{16,20},{20,16},{24,28},{28,24},{1,5},{5... | collective-permute-start | bytes 2359304 | tf_op jit(solution)/shard_map/ppermute | solution.py:362
  14.7 1.3 %collective-permute-start.6 = (bf16[2048,128]{1,0:T(8,128)(2,1)S(1)}, bf16[2048,128]{1,0:T(8,128)(2,1)S(1)}, u32[]{:S(2)}, u32[]{:S(2)}) collective-permute-start(bf16[2048,128]{1,0:T(8,128)(2,1)S(1)} %get-tuple-element.22.tail.refs_2_.refs_5_), channel_id=1, source_target_pairs={{9,1},{13,5},{17,9},{21,13},{25,17},{29,21},{10,2},{14,6},{18,10},... | collective-permute-start | bytes 1572872 | tf_op jit(solution)/shard_map/ppermute | solution.py:362
  16.0 4.0 %collective-permute-start.2 = (bf16[2048,128]{1,0:T(8,128)(2,1)S(1)}, bf16[2048,128]{1,0:T(8,128)(2,1)S(1)}, u32[]{:S(2)}, u32[]{:S(2)}) collective-permute-start(bf16[2048,128]{1,0:T(8,128)(2,1)S(1)} %get-tuple-element.22.tail.refs_2_.refs_5_), channel_id=1, source_target_pairs={{1,9},{5,13},{9,17},{13,21},{17,25},{21,29},{2,10},{6,14},{10,18},... | collective-permute-start | bytes 1572872 | tf_op jit(solution)/shard_map/ppermute | solution.py:362
  20.1 10.7 %collective-permute-done.4.refs_3_.refs_2_.refs_7_ = bf16[4112,128]{1,0:T(8,128)(2,1)S(1)} collective-permute-done((bf16[4112,128]{1,0:T(8,128)(2,1)S(1)}, bf16[4112,128]{1,0:T(8,128)(2,1)S(1)}, u32[]{:S(2)}, u32[]{:S(2)}) %collective-permute-start.4) | collective-permute-done | bytes 1052704 | tf_op jit(solution)/shard_map/ppermute | solution.py:362
  30.8 1.3 %collective-permute-start.5 = (bf16[4112,128]{1,0:T(8,128)(2,1)S(1)}, bf16[4112,128]{1,0:T(8,128)(2,1)S(1)}, u32[]{:S(2)}, u32[]{:S(2)}) collective-permute-start(bf16[4112,128]{1,0:T(8,128)(2,1)S(1)} %collective-permute-done.4.refs_3_.refs_2_.refs_7_), channel_id=1, source_target_pairs={{8,0},{12,4},{16,8},{20,12},{9,1},{13,5},{17,9},{21,13},{10,2},{14... | collective-permute-start | bytes 3158024 | tf_op jit(solution)/shard_map/ppermute | solution.py:362
  32.0 0.0 collective-permute-done.refs_1_.refs_0_.refs_5_
  32.0 0.7 collective-permute-start.1
  32.8 0.5 turn_rows.1.turned
  33.3 0.0 copy-start
  33.3 0.0 copy-start.4
  33.3 0.0 copy-start.5
  33.3 3.6 %collective-permute-done.6.refs_4_.refs_3_.refs_8_ = bf16[2048,128]{1,0:T(8,128)(2,1)S(1)} collective-permute-done((bf16[2048,128]{1,0:T(8,128)(2,1)S(1)}, bf16[2048,128]{1,0:T(8,128)(2,1)S(1)}, u32[]{:S(2)}, u32[]{:S(2)}) %collective-permute-start.6) | collective-permute-done | bytes 524320 | tf_op jit(solution)/shard_map/ppermute | solution.py:362
  36.9 1.3 %collective-permute-start.7 = (bf16[2048,128]{1,0:T(8,128)(2,1)S(1)}, bf16[2048,128]{1,0:T(8,128)(2,1)S(1)}, u32[]{:S(2)}, u32[]{:S(2)}) collective-permute-start(bf16[2048,128]{1,0:T(8,128)(2,1)S(1)} %collective-permute-done.6.refs_4_.refs_3_.refs_8_), channel_id=1, source_target_pairs={{9,1},{13,5},{17,9},{21,13},{10,2},{14,6},{18,10},{22,14}} | collective-permute-start | bytes 1572872 | tf_op jit(solution)/shard_map/ppermute | solution.py:362
  38.2 0.2 collective-permute-done.2.refs_2_.refs_1_.refs_6_
  38.4 0.7 collective-permute-start.3
  39.1 0.0 collective-permute-done.9.refs_5_.refs_6_
  39.1 0.7 pick_rows.5
  39.8 1.5 %collective-permute-start.10 = (bf16[6176,128]{1,0:T(8,128)(2,1)S(1)}, bf16[6176,128]{1,0:T(8,128)(2,1)S(1)}, u32[]{:S(2)}, u32[]{:S(2)}) collective-permute-start(bf16[6176,128]{1,0:T(8,128)(2,1)S(1)} %pick_rows.5), channel_id=1, source_target_pairs={{0,4},{4,0},{8,12},{12,8},{16,20},{20,16},{24,28},{28,24},{1,5},{5... | collective-permute-start | bytes 4743176 | tf_op jit(solution)/shard_map/ppermute | solution.py:362
  41.3 0.0 copy-done
  41.3 0.0 copy-done.4
  41.3 0.0 copy-done.5
  41.3 3.2 %stage_products.4 = (bf16[4,3,128,128]{3,2,1,0:T(8,128)(2,1)S(1)}, bf16[4,3,128,128]{3,2,1,0:T(8,128)(2,1)S(1)}, bf16[4,3,128,128]{3,2,1,0:T(8,128)(2,1)S(1)}) custom-call(s32[8,8]{1,0:T(8,128)S(1)} %bitcast.22, s32[8,8]{1,0:T(8,128)S(1)} %bitcast.18, s32[1,8]{1,0:T(1,128)S(1)} %bitcast.26, bf16[16,384,128]{2,1,0:T(8,128)(2,1)S(1)} %turn_rows.1.turned, ...), custom_call_target="tpu_custom_call" | custom-call | flops 1024 | bytes 1024 | tf_op jit(solution)/shard_map/stage_products/pallas_call | solution.py:292
  44.5 20.9 %collective-permute-done.7.refs_3_.refs_4_ = bf16[2048,128]{1,0:T(8,128)(2,1)S(1)} collective-permute-done((bf16[2048,128]{1,0:T(8,128)(2,1)S(1)}, bf16[2048,128]{1,0:T(8,128)(2,1)S(1)}, u32[]{:S(2)}, u32[]{:S(2)}) %collective-permute-start.7) | collective-permute-done | bytes 524320 | tf_op jit(solution)/shard_map/ppermute | solution.py:362
  65.4 0.0 collective-permute-done.3.refs_1_.refs_2_
  65.4 0.0 collective-permute-done.5.refs_2_.refs_3_
  65.4 0.0 collective-permute-done.1.refs_0_.refs_1_
  65.4 1.4 %pick_rows.6 = (bf16[3072,128]{1,0:T(8,128)(2,1)S(1)}, bf16[3072,128]{1,0:T(8,128)(2,1)S(1)}) custom-call(s32[8,8]{1,0:T(8,128)S(1)} %collective-permute-done.8.refs_0_, bf16[4112,128]{1,0:T(8,128)(2,1)S(1)} %collective-permute-done.1.refs_0_.refs_1_, bf16[2048,128]{1,0:T(8,128)(2,1)S(1)} %collective-permute-done.3.refs_1_.refs_2_, ...), custom_call_target="tpu_custom_call" | custom-call | flops 20000000000 | bytes 1024 | tf_op jit(solution)/shard_map/pick_rows/pallas_call | solution.py:214
  66.8 1.5 %collective-permute-start.15 = (bf16[3072,128]{1,0:T(8,128)(2,1)S(1)}, bf16[3072,128]{1,0:T(8,128)(2,1)S(1)}, u32[]{:S(2)}, u32[]{:S(2)}) collective-permute-start(bf16[3072,128]{1,0:T(8,128)(2,1)S(1)} %get-tuple-element.30), channel_id=1, source_target_pairs={{0,4},{4,0},{8,12},{12,8},{16,20},{20,16},{24,28},{28,24},{1,5},{5... | collective-permute-start | bytes 2359304 | tf_op jit(solution)/shard_map/ppermute | solution.py:362
  68.3 0.0 copy-start.3
  68.3 1.4 %collective-permute-start.13 = (bf16[3072,128]{1,0:T(8,128)(2,1)S(1)}, bf16[3072,128]{1,0:T(8,128)(2,1)S(1)}, u32[]{:S(2)}, u32[]{:S(2)}) collective-permute-start(bf16[3072,128]{1,0:T(8,128)(2,1)S(1)} %get-tuple-element.29), channel_id=1, source_target_pairs={{8,0},{12,4},{16,24},{20,28},{9,1},{13,5},{17,25},{21,29},{10,2},{... | collective-permute-start | bytes 2359304 | tf_op jit(solution)/shard_map/ppermute | solution.py:362
  69.7 6.8 %collective-permute-done.10.refs_4_ = bf16[6176,128]{1,0:T(8,128)(2,1)S(1)} collective-permute-done((bf16[6176,128]{1,0:T(8,128)(2,1)S(1)}, bf16[6176,128]{1,0:T(8,128)(2,1)S(1)}, u32[]{:S(2)}, u32[]{:S(2)}) %collective-permute-start.10) | collective-permute-done | bytes 1581088 | tf_op jit(solution)/shard_map/ppermute | solution.py:362
  76.5 0.7 pick_rows.7
  77.3 1.3 %collective-permute-start.14 = (bf16[3072,128]{1,0:T(8,128)(2,1)S(1)}, bf16[3072,128]{1,0:T(8,128)(2,1)S(1)}, u32[]{:S(2)}, u32[]{:S(2)}) collective-permute-start(bf16[3072,128]{1,0:T(8,128)(2,1)S(1)} %pick_rows.7), channel_id=1, source_target_pairs={{8,4},{12,0},{16,28},{20,24},{9,5},{13,1},{17,29},{21,25},{10,6},{... | collective-permute-start | bytes 2359304 | tf_op jit(solution)/shard_map/ppermute | solution.py:362
  78.6 0.0 copy-done.3
  78.6 3.2 %stage_products.5 = (bf16[7,3,128,128]{3,2,1,0:T(8,128)(2,1)S(1)}, bf16[7,3,128,128]{3,2,1,0:T(8,128)(2,1)S(1)}, bf16[7,3,128,128]{3,2,1,0:T(8,128)(2,1)S(1)}) custom-call(s32[8,8]{1,0:T(8,128)S(1)} %bitcast.23, s32[8,8]{1,0:T(8,128)S(1)} %bitcast.19, s32[1,8]{1,0:T(1,128)S(1)} %bitcast.27, bf16[16,384,128]{2,1,0:T(8,128)(2,1)S(1)} %turn_rows.1.turned, ...), custom_call_target="tpu_custom_call" | custom-call | flops 1024 | bytes 1024 | tf_op jit(solution)/shard_map/stage_products/pallas_call | solution.py:292
  81.8 12.6 %collective-permute-start.11 = (bf16[7,3,128,128]{3,2,1,0:T(8,128)(2,1)S(1)}, bf16[7,3,128,128]{3,2,1,0:T(8,128)(2,1)S(1)}, u32[]{:S(2)}, u32[]{:S(2)}) collective-permute-start(bf16[7,3,128,128]{3,2,1,0:T(8,128)(2,1)S(1)} %get-tuple-element.27), channel_id=1, source_target_pairs={{0,1},{1,2},{2,3},{4,5},{5,6},{6,7},{8,9},{9,10},{10,11},{12,13},{... | collective-permute-start | bytes 2064392 | tf_op jit(solution)/shard_map/ppermute | solution.py:371
  94.5 1.9 %collective-permute-start.12 = (bf16[7,3,128,128]{3,2,1,0:T(8,128)(2,1)S(1)}, bf16[7,3,128,128]{3,2,1,0:T(8,128)(2,1)S(1)}, u32[]{:S(2)}, u32[]{:S(2)}) collective-permute-start(bf16[7,3,128,128]{3,2,1,0:T(8,128)(2,1)S(1)} %get-tuple-element.28), channel_id=1, source_target_pairs={{1,0},{2,1},{3,2},{5,4},{6,5},{7,6},{9,8},{10,9},{11,10},{13,12},{... | collective-permute-start | bytes 2064392 | tf_op jit(solution)/shard_map/ppermute | solution.py:372
  96.4 12.0 %collective-permute-done.15.refs_0_ = bf16[3072,128]{1,0:T(8,128)(2,1)S(1)} collective-permute-done((bf16[3072,128]{1,0:T(8,128)(2,1)S(1)}, bf16[3072,128]{1,0:T(8,128)(2,1)S(1)}, u32[]{:S(2)}, u32[]{:S(2)}) %collective-permute-start.15) | collective-permute-done | bytes 786464 | tf_op jit(solution)/shard_map/ppermute | solution.py:362
  108.4 1.2 stage_products.6
  109.6 0.0 collective-permute-done.13.refs_0_
  109.6 0.0 collective-permute-done.11.refs_5_.refs_1_
  109.6 0.0 collective-permute-done.12.refs_6_.refs_2_
  109.6 0.0 collective-permute-done.14.refs_1_
  109.6 4.4 %stage_products.7 = (bf16[3,3,128,128]{3,2,1,0:T(8,128)(2,1)S(1)}, bf16[3,3,128,128]{3,2,1,0:T(8,128)(2,1)S(1)}, bf16[3,3,128,128]{3,2,1,0:T(8,128)(2,1)S(1)}) custom-call(s32[8,8]{1,0:T(8,128)S(1)} %bitcast.25, s32[8,8]{1,0:T(8,128)S(1)} %bitcast.21, s32[1,8]{1,0:T(1,128)S(1)} %bitcast.29, bf16[16,384,128]{2,1,0:T(8,128)(2,1)S(1)} %turn_rows.1.turned, ...), custom_call_target="tpu_custom_call" | custom-call | flops 1024 | bytes 1024 | tf_op jit(solution)/shard_map/stage_products/pallas_call | solution.py:292
  114.0 1.9 %collective-permute-start.16 = (bf16[3,3,128,128]{3,2,1,0:T(8,128)(2,1)S(1)}, bf16[3,3,128,128]{3,2,1,0:T(8,128)(2,1)S(1)}, u32[]{:S(2)}, u32[]{:S(2)}) collective-permute-start(bf16[3,3,128,128]{3,2,1,0:T(8,128)(2,1)S(1)} %get-tuple-element.35), channel_id=1, source_target_pairs={{0,1},{1,2},{2,3},{4,5},{5,6},{6,7},{8,9},{9,10},{10,11},{12,13},{... | collective-permute-start | bytes 884744 | tf_op jit(solution)/shard_map/ppermute | solution.py:371
  116.0 2.4 %collective-permute-start.17 = (bf16[3,3,128,128]{3,2,1,0:T(8,128)(2,1)S(1)}, bf16[3,3,128,128]{3,2,1,0:T(8,128)(2,1)S(1)}, u32[]{:S(2)}, u32[]{:S(2)}) collective-permute-start(bf16[3,3,128,128]{3,2,1,0:T(8,128)(2,1)S(1)} %get-tuple-element.36), channel_id=1, source_target_pairs={{1,0},{2,1},{3,2},{5,4},{6,5},{7,6},{9,8},{10,9},{11,10},{13,12},{... | collective-permute-start | bytes 884744 | tf_op jit(solution)/shard_map/ppermute | solution.py:372
  118.4 1.2 collective-permute-done.16.refs_4_
  119.6 4.4 %collective-permute-done.17.refs_5_ = bf16[3,3,128,128]{3,2,1,0:T(8,128)(2,1)S(1)} collective-permute-done((bf16[3,3,128,128]{3,2,1,0:T(8,128)(2,1)S(1)}, bf16[3,3,128,128]{3,2,1,0:T(8,128)(2,1)S(1)}, u32[]{:S(2)}, u32[]{:S(2)}) %collective-permute-start.17) | collective-permute-done | bytes 294944 | tf_op jit(solution)/shard_map/ppermute | solution.py:372
  124.0 2.5 %assemble_coarse.1 = f32[5120,128]{1,0:T(8,128)} custom-call(bf16[7,3,128,128]{3,2,1,0:T(8,128)(2,1)S(1)} %get-tuple-element.26.refs_1_.refs_0_, bf16[7,3,128,128]{3,2,1,0:T(8,128)(2,1)S(1)} %collective-permute-done.11.refs_5_.refs_1_, bf16[7,3,128,128]{3,2,1,0:T(8,128)(2,1)S(1)} %collective-permute-done.12.refs_6_.refs_2_, ...), custom_call_target="tpu_custom_call" | custom-call | flops 1024 | bytes 1024 | tf_op jit(solution)/shard_map/assemble_coarse/pallas_call | solution.py:338
Async XLA Ops:
  0.0 1.4 %copy-start.1 = (bf16[1,16,128,384]{3,2,1,0:T(8,128)(2,1)S(1)}, bf16[1,16,128,384]{3,2,1,0:T(8,128)(2,1)}, u32[]{:S(2)}) copy-start(bf16[1,16,128,384]{3,2,1,0:T(8,128)(2,1)} %param.10) | copy-start | bytes 4718596
  1.4 0.7 copy-start.2
  2.1 0.7 copy-start.6
  3.8 27.0 %collective-permute-start.4 = (bf16[4112,128]{1,0:T(8,128)(2,1)S(1)}, bf16[4112,128]{1,0:T(8,128)(2,1)S(1)}, u32[]{:S(2)}, u32[]{:S(2)}) collective-permute-start(bf16[4112,128]{1,0:T(8,128)(2,1)S(1)} %get-tuple-element.21.head.refs_1_.refs_4_), channel_id=1, source_target_pairs={{8,0},{12,4},{16,8},{20,12},{24,16},{28,20},{9,1},{13,5},{17,9},{2... | collective-permute-start | bytes 3158024 | tf_op jit(solution)/shard_map/ppermute | solution.py:362
  5.1 27.0 %collective-permute-start = (bf16[4112,128]{1,0:T(8,128)(2,1)S(1)}, bf16[4112,128]{1,0:T(8,128)(2,1)S(1)}, u32[]{:S(2)}, u32[]{:S(2)}) collective-permute-start(bf16[4112,128]{1,0:T(8,128)(2,1)S(1)} %get-tuple-element.21.head.refs_1_.refs_4_), channel_id=1, source_target_pairs={{0,8},{4,12},{8,16},{12,20},{16,24},{20,28},{1,9},{5,13},{9,17},{1... | collective-permute-start | bytes 3158024 | tf_op jit(solution)/shard_map/ppermute | solution.py:362
  9.8 2.8 %collective-permute-start.8 = (s32[8,8]{1,0:T(8,128)S(1)}, s32[8,8]{1,0:T(8,128)S(1)}, u32[]{:S(2)}, u32[]{:S(2)}) collective-permute-start(s32[8,8]{1,0:T(8,128)S(1)} %bitcast.17), channel_id=1, source_target_pairs={{4,0},{0,4},{12,8},{8,12},{20,16},{16,20},{28,24},{24,28},{5,1},{1... | collective-permute-start | bytes 776 | tf_op jit(solution)/shard_map/ppermute | solution.py:362
  13.3 25.8 %collective-permute-start.9 = (bf16[3072,128]{1,0:T(8,128)(2,1)S(1)}, bf16[3072,128]{1,0:T(8,128)(2,1)S(1)}, u32[]{:S(2)}, u32[]{:S(2)}) collective-permute-start(bf16[3072,128]{1,0:T(8,128)(2,1)S(1)} %pick_rows.4), channel_id=1, source_target_pairs={{0,4},{4,0},{8,12},{12,8},{16,20},{20,16},{24,28},{28,24},{1,5},{5... | collective-permute-start | bytes 2359304 | tf_op jit(solution)/shard_map/ppermute | solution.py:362
  14.7 22.2 %collective-permute-start.6 = (bf16[2048,128]{1,0:T(8,128)(2,1)S(1)}, bf16[2048,128]{1,0:T(8,128)(2,1)S(1)}, u32[]{:S(2)}, u32[]{:S(2)}) collective-permute-start(bf16[2048,128]{1,0:T(8,128)(2,1)S(1)} %get-tuple-element.22.tail.refs_2_.refs_5_), channel_id=1, source_target_pairs={{9,1},{13,5},{17,9},{21,13},{25,17},{29,21},{10,2},{14,6},{18,10},... | collective-permute-start | bytes 1572872 | tf_op jit(solution)/shard_map/ppermute | solution.py:362
  16.0 22.3 %collective-permute-start.2 = (bf16[2048,128]{1,0:T(8,128)(2,1)S(1)}, bf16[2048,128]{1,0:T(8,128)(2,1)S(1)}, u32[]{:S(2)}, u32[]{:S(2)}) collective-permute-start(bf16[2048,128]{1,0:T(8,128)(2,1)S(1)} %get-tuple-element.22.tail.refs_2_.refs_5_), channel_id=1, source_target_pairs={{1,9},{5,13},{9,17},{13,21},{17,25},{21,29},{2,10},{6,14},{10,18},... | collective-permute-start | bytes 1572872 | tf_op jit(solution)/shard_map/ppermute | solution.py:362
  30.8 34.6 %collective-permute-start.5 = (bf16[4112,128]{1,0:T(8,128)(2,1)S(1)}, bf16[4112,128]{1,0:T(8,128)(2,1)S(1)}, u32[]{:S(2)}, u32[]{:S(2)}) collective-permute-start(bf16[4112,128]{1,0:T(8,128)(2,1)S(1)} %collective-permute-done.4.refs_3_.refs_2_.refs_7_), channel_id=1, source_target_pairs={{8,0},{12,4},{16,8},{20,12},{9,1},{13,5},{17,9},{21,13},{10,2},{14... | collective-permute-start | bytes 3158024 | tf_op jit(solution)/shard_map/ppermute | solution.py:362
  32.0 33.3 %collective-permute-start.1 = (bf16[4112,128]{1,0:T(8,128)(2,1)S(1)}, bf16[4112,128]{1,0:T(8,128)(2,1)S(1)}, u32[]{:S(2)}, u32[]{:S(2)}) collective-permute-start(bf16[4112,128]{1,0:T(8,128)(2,1)S(1)} %collective-permute-done.refs_1_.refs_0_.refs_5_), channel_id=1, source_target_pairs={{8,16},{12,20},{16,24},{20,28},{9,17},{13,21},{17,25},{21,29},{10,... | collective-permute-start | bytes 3158024 | tf_op jit(solution)/shard_map/ppermute | solution.py:362
  33.3 8.0 %copy-start = (bf16[1,1,8,8,128,128]{5,4,3,2,1,0:T(8,128)(2,1)S(1)}, bf16[1,1,8,8,128,128]{5,4,3,2,1,0:T(8,128)(2,1)}, u32[]{:S(2)}) copy-start(bf16[1,1,8,8,128,128]{5,4,3,2,1,0:T(8,128)(2,1)} %param.6) | copy-start | bytes 6291460
  33.3 8.0 %copy-start.4 = (s32[1,1,8,8]{3,2,1,0:T(8,128)S(1)}, s32[1,1,8,8]{3,2,1,0:T(8,128)}, u32[]{:S(2)}) copy-start(s32[1,1,8,8]{3,2,1,0:T(8,128)} %param.7) | copy-start | bytes 772
  33.3 8.0 %copy-start.5 = (s32[1,1,8]{2,1,0:T(1,128)S(1)}, s32[1,1,8]{2,1,0:T(1,128)}, u32[]{:S(2)}) copy-start(s32[1,1,8]{2,1,0:T(1,128)} %param.9) | copy-start | bytes 100
  36.9 28.5 %collective-permute-start.7 = (bf16[2048,128]{1,0:T(8,128)(2,1)S(1)}, bf16[2048,128]{1,0:T(8,128)(2,1)S(1)}, u32[]{:S(2)}, u32[]{:S(2)}) collective-permute-start(bf16[2048,128]{1,0:T(8,128)(2,1)S(1)} %collective-permute-done.6.refs_4_.refs_3_.refs_8_), channel_id=1, source_target_pairs={{9,1},{13,5},{17,9},{21,13},{10,2},{14,6},{18,10},{22,14}} | collective-permute-start | bytes 1572872 | tf_op jit(solution)/shard_map/ppermute | solution.py:362
  38.4 27.0 %collective-permute-start.3 = (bf16[2048,128]{1,0:T(8,128)(2,1)S(1)}, bf16[2048,128]{1,0:T(8,128)(2,1)S(1)}, u32[]{:S(2)}, u32[]{:S(2)}) collective-permute-start(bf16[2048,128]{1,0:T(8,128)(2,1)S(1)} %collective-permute-done.2.refs_2_.refs_1_.refs_6_), channel_id=1, source_target_pairs={{9,17},{13,21},{17,25},{21,29},{10,18},{14,22},{18,26},{22,30}} | collective-permute-start | bytes 1572872 | tf_op jit(solution)/shard_map/ppermute | solution.py:362
  39.8 36.7 %collective-permute-start.10 = (bf16[6176,128]{1,0:T(8,128)(2,1)S(1)}, bf16[6176,128]{1,0:T(8,128)(2,1)S(1)}, u32[]{:S(2)}, u32[]{:S(2)}) collective-permute-start(bf16[6176,128]{1,0:T(8,128)(2,1)S(1)} %pick_rows.5), channel_id=1, source_target_pairs={{0,4},{4,0},{8,12},{12,8},{16,20},{20,16},{24,28},{28,24},{1,5},{5... | collective-permute-start | bytes 4743176 | tf_op jit(solution)/shard_map/ppermute | solution.py:362
  66.8 41.5 %collective-permute-start.15 = (bf16[3072,128]{1,0:T(8,128)(2,1)S(1)}, bf16[3072,128]{1,0:T(8,128)(2,1)S(1)}, u32[]{:S(2)}, u32[]{:S(2)}) collective-permute-start(bf16[3072,128]{1,0:T(8,128)(2,1)S(1)} %get-tuple-element.30), channel_id=1, source_target_pairs={{0,4},{4,0},{8,12},{12,8},{16,20},{20,16},{24,28},{28,24},{1,5},{5... | collective-permute-start | bytes 2359304 | tf_op jit(solution)/shard_map/ppermute | solution.py:362
  68.3 10.3 %copy-start.3 = (s32[1,1,8,8]{3,2,1,0:T(8,128)S(1)}, s32[1,1,8,8]{3,2,1,0:T(8,128)}, u32[]{:S(2)}) copy-start(s32[1,1,8,8]{3,2,1,0:T(8,128)} %param.8) | copy-start | bytes 772
  68.3 41.3 %collective-permute-start.13 = (bf16[3072,128]{1,0:T(8,128)(2,1)S(1)}, bf16[3072,128]{1,0:T(8,128)(2,1)S(1)}, u32[]{:S(2)}, u32[]{:S(2)}) collective-permute-start(bf16[3072,128]{1,0:T(8,128)(2,1)S(1)} %get-tuple-element.29), channel_id=1, source_target_pairs={{8,0},{12,4},{16,24},{20,28},{9,1},{13,5},{17,25},{21,29},{10,2},{... | collective-permute-start | bytes 2359304 | tf_op jit(solution)/shard_map/ppermute | solution.py:362
  77.3 32.3 %collective-permute-start.14 = (bf16[3072,128]{1,0:T(8,128)(2,1)S(1)}, bf16[3072,128]{1,0:T(8,128)(2,1)S(1)}, u32[]{:S(2)}, u32[]{:S(2)}) collective-permute-start(bf16[3072,128]{1,0:T(8,128)(2,1)S(1)} %pick_rows.7), channel_id=1, source_target_pairs={{8,4},{12,0},{16,28},{20,24},{9,5},{13,1},{17,29},{21,25},{10,6},{... | collective-permute-start | bytes 2359304 | tf_op jit(solution)/shard_map/ppermute | solution.py:362
  81.8 27.8 %collective-permute-start.11 = (bf16[7,3,128,128]{3,2,1,0:T(8,128)(2,1)S(1)}, bf16[7,3,128,128]{3,2,1,0:T(8,128)(2,1)S(1)}, u32[]{:S(2)}, u32[]{:S(2)}) collective-permute-start(bf16[7,3,128,128]{3,2,1,0:T(8,128)(2,1)S(1)} %get-tuple-element.27), channel_id=1, source_target_pairs={{0,1},{1,2},{2,3},{4,5},{5,6},{6,7},{8,9},{9,10},{10,11},{12,13},{... | collective-permute-start | bytes 2064392 | tf_op jit(solution)/shard_map/ppermute | solution.py:371
  94.5 15.1 %collective-permute-start.12 = (bf16[7,3,128,128]{3,2,1,0:T(8,128)(2,1)S(1)}, bf16[7,3,128,128]{3,2,1,0:T(8,128)(2,1)S(1)}, u32[]{:S(2)}, u32[]{:S(2)}) collective-permute-start(bf16[7,3,128,128]{3,2,1,0:T(8,128)(2,1)S(1)} %get-tuple-element.28), channel_id=1, source_target_pairs={{1,0},{2,1},{3,2},{5,4},{6,5},{7,6},{9,8},{10,9},{11,10},{13,12},{... | collective-permute-start | bytes 2064392 | tf_op jit(solution)/shard_map/ppermute | solution.py:372
  114.0 5.6 %collective-permute-start.16 = (bf16[3,3,128,128]{3,2,1,0:T(8,128)(2,1)S(1)}, bf16[3,3,128,128]{3,2,1,0:T(8,128)(2,1)S(1)}, u32[]{:S(2)}, u32[]{:S(2)}) collective-permute-start(bf16[3,3,128,128]{3,2,1,0:T(8,128)(2,1)S(1)} %get-tuple-element.35), channel_id=1, source_target_pairs={{0,1},{1,2},{2,3},{4,5},{5,6},{6,7},{8,9},{9,10},{10,11},{12,13},{... | collective-permute-start | bytes 884744 | tf_op jit(solution)/shard_map/ppermute | solution.py:371
  116.0 8.0 %collective-permute-start.17 = (bf16[3,3,128,128]{3,2,1,0:T(8,128)(2,1)S(1)}, bf16[3,3,128,128]{3,2,1,0:T(8,128)(2,1)S(1)}, u32[]{:S(2)}, u32[]{:S(2)}) collective-permute-start(bf16[3,3,128,128]{3,2,1,0:T(8,128)(2,1)S(1)} %get-tuple-element.36), channel_id=1, source_target_pairs={{1,0},{2,1},{3,2},{5,4},{6,5},{7,6},{9,8},{10,9},{11,10},{13,12},{... | collective-permute-start | bytes 884744 | tf_op jit(solution)/shard_map/ppermute | solution.py:372

commit v6 on v5

--- a/solution.py
+++ b/solution.py
@@ -48,9 +48,9 @@
                 for h in range(LINES) for c in range(self.columns)
                 if 0 <= h + sign < LINES and 0 <= h + sign - sign * s < LINES]
 
-    def across(self, shift):
+    def across(self, shift, lines=range(LINES)):
         return [(h * self.columns + c, h * self.columns + (c + shift) % self.columns)
-                for h in range(LINES) for c in range(self.columns)]
+                for h in lines for c in range(self.columns)]
 
     def ends(self, shift):
         return [(h * self.columns + c, end * self.columns + (c + shift) % self.columns)
@@ -73,13 +73,18 @@
                 (self.panel(z + 1, y, 0), above, [(1, 0, True, above)])]
         return work + [(self.panel(z, y, shift), True, [(3 + i, 0, False, True)]) for i, shift in enumerate(self.sides)]
 
+    def paired(self, z):
+        odd = z % 2 == 1
+        return jnp.where(odd, z - 1, z + 1), jnp.where(odd, z + 1, z - 1), odd
+
     def work_second(self, z, y):
         line, below, above = self.second(z)
         work = [(self.panel(line, y, 0), below | above, [(0, 0, True, below), (1, 0, True, above)])]
-        below, above = self.has(z, 1, -1), self.has(z, 1, 1)
+        first, other, _ = self.paired(z)
+        middle = (z == 1) | (z == LINES - 2)
         for i, shift in enumerate(self.sides):
-            work += [(self.panel(z - 1, y, shift), below, [(2 + i, 0, False, below)]),
-                     (self.panel(z + 1, y, shift), above, [(2 + i, self.cap, False, above)])]
+            work += [(self.panel(first, y, shift), True, [(2 + 2 * i, 0, False, True)]),
+                     (self.panel(other, y, shift), middle, [(3 + 2 * i, 0, False, middle)])]
         return work
 
     def work_crossed(self, z, y):
@@ -167,18 +172,18 @@
     outs = refs[len(refs) - outputs - scratch:len(refs) - scratch]
     z, y = grid.spot()
 
-    def list_at(ref, place):
-        start = ref.shape[0] - (place + 1) * grid.list_rows
-        return ref[start:start + grid.list_rows, :]
+    def list_at(options):
+        value = None
+        for present, source in options:
+            ref = sources[source][0][0]
+            here = ref[ref.shape[0] - grid.list_rows:, :].astype(jnp.float32)
+            value = here if value is None else jnp.where(present(z), here, value)
+        return value
 
     if tables:
         numbers, plain, done = refs[-scratch:-1 - len(tables)], refs[-1 - len(tables):-1], refs[-1]
         for table, options in enumerate(tables):
-            value = None
-            for present, source, place in options:
-                here = list_at(sources[source][0][0], place).astype(jnp.float32)
-                value = here if value is None else jnp.where(present(z), here, value)
-            numbers[table][...] = value.astype(jnp.int32)
+            numbers[table][...] = list_at(options).astype(jnp.int32)
             pltpu.make_async_copy(numbers[table], plain[table], done.at[table]).start()
         for table in range(len(tables)):
             pltpu.make_async_copy(numbers[table], plain[table], done.at[table]).wait()
@@ -197,16 +202,16 @@
                 copy()
             else:
                 pl.when(present)(copy)
-    for source, place in carry:
-        for out in outs:
-            start = out.shape[0] - (place + 1) * grid.list_rows
-            out[start:start + grid.list_rows, :] = list_at(sources[source][0][0], 0)
+    for out, options in zip(outs, carry):
+        if options:
+            out[out.shape[0] - grid.list_rows:, :] = list_at(options).astype(out.dtype)
 
 
 def pick(grid, plan, sizes, lists, sources, carry=(), tables=(), after=(), cost=COST):
     flat = [x for source in sources for x, _ in source]
     width = flat[0].shape[-1]
-    shapes = [grid.shape(size, 3, width, len(carry)) for size in sizes]
+    carry = carry or ((),) * len(sizes)
+    shapes = [grid.shape(size, 3, width, 1 if options else 0) for size, options in zip(sizes, carry)]
     layout = tuple(tuple(blocks for _, blocks in source) for source in sources)
     table = (grid.list_rows, width)
     scratch = [pltpu.VMEM(table, jnp.int32)] * len(tables) + [pltpu.SMEM(table, jnp.int32)] * len(tables)
@@ -364,8 +369,8 @@
     def move_both(pair, pairs):
         return (move(pair[0][0], pairs), 2), (move(pair[1][0], pairs, inner), 1)
 
-    def move_across(arrays):
-        return [((move(x, grid.across(shift)), 3),) for x, shift in zip(arrays, sides)]
+    def move_across(arrays, lines=range(LINES)):
+        return [((move(x, grid.across(shift, lines)), 3),) for x, shift in zip(arrays, sides)]
 
     def exchange(parts):
         lower = lax.ppermute(parts[1], "rows", [(g, g + 1) for g in range(groups - 1)])
@@ -386,33 +391,35 @@
     second = [move_both(near[0], grid.hops(2, 1)), move_both(near[1], grid.hops(2, -1))]
 
     def near_requests(z, y):
-        return [(index, grid.panel(z + step, y, 0), [(True, side)], index, side * cap)
-                for index in range(len(sides)) for side, step in enumerate((-1, 1))]
-
-    picked = pick(grid, near_requests, [2 * cap] * len(sides), side_lists, near, ((0, 1), (1, 0)),
+        first, other, odd = grid.paired(z)
+        requests = []
+        for index in range(len(sides)):
+            requests += [
+                (index, grid.panel(first, y, 0), [(odd, 0), (jnp.logical_not(odd), 1)], 2 * index, 0),
+                (index, grid.panel(other, y, 0), [(z == 1, 1), (z == LINES - 2, 0)], 2 * index + 1, 0)]
+        return requests
+
+    def is_odd(z):
+        return z % 2 == 1
+
+    paired = ((None, 1), (is_odd, 0))
+    picked = pick(grid, near_requests, [cap] * (2 * len(sides)), side_lists, near, (paired, ()) * len(sides),
                   after=[x for ((x, _),) in beside], cost=NEAR_COST)
-    crossed = move_across(picked)
+    crossed, middle = move_across(picked[::2]), move_across(picked[1::2], (1, LINES - 2))
     parts = stage(grid, grid.work_near, lists, turned, matrix, [*near, own, *beside])
 
     def second_requests(z, y):
         line, below, above = grid.second(z)
-        return [(index, grid.panel(line, y, 0), [(below, 0), (above, 1)], index, 0) for index in range(columns)]
-
-    def far_requests(z, y):
-        line, below, above = grid.second(z)
-        return [(index, grid.panel(line, y, 0), [(below, 0), (above, 1)], index, 0) for index in range(len(sides))]
-
-    def low(z):
-        return z == 1
-
-    picked = pick(grid, second_requests, [cap] * columns, side_lists, [*second, *near],
-                  tables=(((None, 3, 0), (low, 2, 0)),), after=[parts[0]], cost=PICK_COST)
-    second_crossed = move_across(picked[:-1])
-    far = [((move(picked[-1], grid.ends(0)), 3),)]
-    tables = tuple(((None, 2 + columns - 1 - shift, 0), (low, 2 + columns - 1 - shift, 1)) for shift in sides)
-    picked = pick(grid, far_requests, [cap] * len(sides), [], [*second, *crossed], tables=tables)
-    far += [((move(x, grid.ends(shift)), 3),) for shift, x in zip(sides, picked)]
-    parts = stage(grid, grid.work_second, lists, turned, matrix, [*second, *crossed], parts)
+        return [(index, grid.panel(line, y, 0), [(below, 0), (above, 1)], index, 0)
+                for index in range(len(sides) + columns)]
+
+    tables = [((None, 3), (is_odd, 2))] + [((None, 4 + columns - 1 - shift),) for shift in sides]
+    picked = pick(grid, second_requests, [cap] * (len(sides) + columns), side_lists, [*second, *near, *crossed],
+                  tables=tuple(tables), after=[parts[0]], cost=PICK_COST)
+    second_crossed = move_across(picked)
+    far = [((move(x, grid.ends(shift)), 3),) for shift, x in enumerate(picked[len(sides):])]
+    both = [x for pair in zip(crossed, middle) for x in pair]
+    parts = stage(grid, grid.work_second, lists, turned, matrix, [*second, *both], parts)
     first = exchange(parts)
     parts = stage(grid, grid.work_crossed, lists, turned, matrix, second_crossed, (), [parts[0]])
 

time: 129 us -> 121 us (0.938)
  the two profiles are of different devices: /device:TPU:1 before, /device:TPU:29 now
where the time goes in v6:
time: 121 us
  waiting for transfers between devices  68.9 us (57%)
  starting transfers between devices  29.4 us (24%)
  Pallas kernels  19.3 us (16%)
  local copies, waits for them, and re-layouts  2.8 us (2%)
    ppermute x15, waiting for transfers between devices, move(): return lax.ppermute(x, ('blk', 'rows'), perm) if perm else jnp.zeros_like(x)  56.1 us
    ppermute x15, starting transfers between devices, move(): return lax.ppermute(x, ('blk', 'rows'), perm) if perm else jnp.zeros_like(x)  17.6 us
    pallas_call x4, Pallas kernels, stage(): pl.pallas_call(functools.partial(stage_kernel, grid, plan, layout, carrie...  12.3 us
    ppermute x2, waiting for transfers between devices, exchange(): lax.ppermute(parts[2], 'rows', [(g + 1, g) for g in range(groups - 1)])  9.09 us
    ppermute x2, starting transfers between devices, exchange(): lax.ppermute(parts[1], 'rows', [(g, g + 1) for g in range(groups - 1)])  7.45 us
    ppermute x2, starting transfers between devices, exchange(): lax.ppermute(parts[2], 'rows', [(g + 1, g) for g in range(groups - 1)])  4.34 us
    ppermute x2, waiting for transfers between devices, exchange(): lax.ppermute(parts[1], 'rows', [(g, g + 1) for g in range(groups - 1)])  3.73 us
    pallas_call x3, Pallas kernels, pick(): pl.pallas_call(functools.partial(pick_kernel, grid, plan, layout, carry,...  3 us
  transfers between devices with their start and end apart: 19, of which 12 were waited for; matrix products, arithmetic and copies ran while one was open for 0% of the time, Pallas kernels for 10%

profile of v6, /device:TPU:29, one launch (start us, length us, event | category | flops | bytes accessed | tf_op | source)
XLA Modules:
  0.0 120.7 jit_solution(3512933627960147967)
XLA Ops:
  0.0 0.0 copy-start.1
  0.0 1.4 %copy-done.1 = bf16[1,16,128,384]{3,2,1,0:T(8,128)(2,1)S(1)} copy-done((bf16[1,16,128,384]{3,2,1,0:T(8,128)(2,1)S(1)}, bf16[1,16,128,384]{3,2,1,0:T(8,128)(2,1)}, u32[]{:S(2)}) %copy-start.1) | copy-done | bytes 1572888
  1.4 0.0 copy-start.2
  1.4 0.7 copy-done.2
  2.1 0.0 copy-start.6
  2.1 0.7 copy-done.6
  2.8 1.0 pack_rows.1
  3.8 2.1 %collective-permute-start.4 = (bf16[4112,128]{1,0:T(8,128)(2,1)S(1)}, bf16[4112,128]{1,0:T(8,128)(2,1)S(1)}, u32[]{:S(2)}, u32[]{:S(2)}) collective-permute-start(bf16[4112,128]{1,0:T(8,128)(2,1)S(1)} %get-tuple-element.24.head.refs_1_.refs_4_), channel_id=1, source_target_pairs={{8,0},{12,4},{16,8},{20,12},{24,16},{28,20},{9,1},{13,5},{17,9},{2... | collective-permute-start | bytes 3158024 | tf_op jit(solution)/shard_map/ppermute | solution.py:367
  5.9 1.3 %collective-permute-start = (bf16[4112,128]{1,0:T(8,128)(2,1)S(1)}, bf16[4112,128]{1,0:T(8,128)(2,1)S(1)}, u32[]{:S(2)}, u32[]{:S(2)}) collective-permute-start(bf16[4112,128]{1,0:T(8,128)(2,1)S(1)} %get-tuple-element.24.head.refs_1_.refs_4_), channel_id=1, source_target_pairs={{0,8},{4,12},{8,16},{12,20},{16,24},{20,28},{1,9},{5,13},{9,17},{1... | collective-permute-start | bytes 3158024 | tf_op jit(solution)/shard_map/ppermute | solution.py:367
  7.2 0.3 collective-permute-start.8
  7.5 2.2 %collective-permute-done.8.refs_0_ = s32[8,8]{1,0:T(8,128)S(1)} collective-permute-done((s32[8,8]{1,0:T(8,128)S(1)}, s32[8,8]{1,0:T(8,128)S(1)}, u32[]{:S(2)}, u32[]{:S(2)}) %collective-permute-start.8) | collective-permute-done | bytes 288 | tf_op jit(solution)/shard_map/ppermute | solution.py:367
  9.7 0.7 pick_rows.3
  10.4 0.3 collective-permute-start.9
  10.7 4.3 %collective-permute-start.6 = (bf16[2048,128]{1,0:T(8,128)(2,1)S(1)}, bf16[2048,128]{1,0:T(8,128)(2,1)S(1)}, u32[]{:S(2)}, u32[]{:S(2)}) collective-permute-start(bf16[2048,128]{1,0:T(8,128)(2,1)S(1)} %get-tuple-element.25.tail.refs_2_.refs_5_), channel_id=1, source_target_pairs={{9,1},{13,5},{17,9},{21,13},{25,17},{29,21},{10,2},{14,6},{18,10},... | collective-permute-start | bytes 1572872 | tf_op jit(solution)/shard_map/ppermute | solution.py:367
  15.0 1.3 %collective-permute-start.2 = (bf16[2048,128]{1,0:T(8,128)(2,1)S(1)}, bf16[2048,128]{1,0:T(8,128)(2,1)S(1)}, u32[]{:S(2)}, u32[]{:S(2)}) collective-permute-start(bf16[2048,128]{1,0:T(8,128)(2,1)S(1)} %get-tuple-element.25.tail.refs_2_.refs_5_), channel_id=1, source_target_pairs={{1,9},{5,13},{9,17},{13,21},{17,25},{21,29},{2,10},{6,14},{10,18},... | collective-permute-start | bytes 1572872 | tf_op jit(solution)/shard_map/ppermute | solution.py:367
  16.3 11.4 %collective-permute-done.4.refs_3_.refs_2_.refs_7_ = bf16[4112,128]{1,0:T(8,128)(2,1)S(1)} collective-permute-done((bf16[4112,128]{1,0:T(8,128)(2,1)S(1)}, bf16[4112,128]{1,0:T(8,128)(2,1)S(1)}, u32[]{:S(2)}, u32[]{:S(2)}) %collective-permute-start.4) | collective-permute-done | bytes 1052704 | tf_op jit(solution)/shard_map/ppermute | solution.py:367
  27.7 0.7 collective-permute-start.5
  28.5 3.1 %collective-permute-done.refs_1_.refs_0_.refs_5_ = bf16[4112,128]{1,0:T(8,128)(2,1)S(1)} collective-permute-done((bf16[4112,128]{1,0:T(8,128)(2,1)S(1)}, bf16[4112,128]{1,0:T(8,128)(2,1)S(1)}, u32[]{:S(2)}, u32[]{:S(2)}) %collective-permute-start) | collective-permute-done | bytes 1052704 | tf_op jit(solution)/shard_map/ppermute | solution.py:367
  31.6 1.3 %collective-permute-start.1 = (bf16[4112,128]{1,0:T(8,128)(2,1)S(1)}, bf16[4112,128]{1,0:T(8,128)(2,1)S(1)}, u32[]{:S(2)}, u32[]{:S(2)}) collective-permute-start(bf16[4112,128]{1,0:T(8,128)(2,1)S(1)} %collective-permute-done.refs_1_.refs_0_.refs_5_), channel_id=1, source_target_pairs={{8,16},{12,20},{16,24},{20,28},{9,17},{13,21},{17,25},{21,29},{10,... | collective-permute-start | bytes 3158024 | tf_op jit(solution)/shard_map/ppermute | solution.py:367
  32.9 1.6 %collective-permute-done.6.refs_4_.refs_3_.refs_8_ = bf16[2048,128]{1,0:T(8,128)(2,1)S(1)} collective-permute-done((bf16[2048,128]{1,0:T(8,128)(2,1)S(1)}, bf16[2048,128]{1,0:T(8,128)(2,1)S(1)}, u32[]{:S(2)}, u32[]{:S(2)}) %collective-permute-start.6) | collective-permute-done | bytes 524320 | tf_op jit(solution)/shard_map/ppermute | solution.py:367
  34.5 3.9 %collective-permute-done.2.refs_2_.refs_1_.refs_6_ = bf16[2048,128]{1,0:T(8,128)(2,1)S(1)} collective-permute-done((bf16[2048,128]{1,0:T(8,128)(2,1)S(1)}, bf16[2048,128]{1,0:T(8,128)(2,1)S(1)}, u32[]{:S(2)}, u32[]{:S(2)}) %collective-permute-start.2) | collective-permute-done | bytes 524320 | tf_op jit(solution)/shard_map/ppermute | solution.py:367
  38.4 0.0 collective-permute-done.9.refs_5_.refs_6_
  38.4 0.7 pick_rows.4
  39.1 0.0 copy-start
  39.1 0.0 copy-start.4
  39.1 0.0 copy-start.5
  39.1 0.3 collective-permute-start.10
  39.4 0.8 collective-permute-start.7
  40.2 1.3 %collective-permute-start.3 = (bf16[2048,128]{1,0:T(8,128)(2,1)S(1)}, bf16[2048,128]{1,0:T(8,128)(2,1)S(1)}, u32[]{:S(2)}, u32[]{:S(2)}) collective-permute-start(bf16[2048,128]{1,0:T(8,128)(2,1)S(1)} %collective-permute-done.2.refs_2_.refs_1_.refs_6_), channel_id=1, source_target_pairs={{9,17},{13,21},{17,25},{21,29},{10,18},{14,22},{18,26},{22,30}} | collective-permute-start | bytes 1572872 | tf_op jit(solution)/shard_map/ppermute | solution.py:367
  41.5 0.5 turn_rows.1.turned
  42.0 0.0 copy-done
  42.0 0.0 copy-done.4
  42.0 0.0 copy-done.5
  42.0 4.0 %stage_products.4 = (bf16[4,3,128,128]{3,2,1,0:T(8,128)(2,1)S(1)}, bf16[4,3,128,128]{3,2,1,0:T(8,128)(2,1)S(1)}, bf16[4,3,128,128]{3,2,1,0:T(8,128)(2,1)S(1)}) custom-call(s32[8,8]{1,0:T(8,128)S(1)} %bitcast.22, s32[8,8]{1,0:T(8,128)S(1)} %bitcast.18, s32[1,8]{1,0:T(1,128)S(1)} %bitcast.26, bf16[16,384,128]{2,1,0:T(8,128)(2,1)S(1)} %turn_rows.1.turned, ...), custom_call_target="tpu_custom_call" | custom-call | flops 1024 | bytes 1024 | tf_op jit(solution)/shard_map/stage_products/pallas_call | solution.py:297
  46.1 0.0 collective-permute-done.7.refs_3_.refs_4_
  46.1 0.7 collective-permute-start.11
  46.8 19.8 %collective-permute-done.3.refs_1_.refs_2_ = bf16[2048,128]{1,0:T(8,128)(2,1)S(1)} collective-permute-done((bf16[2048,128]{1,0:T(8,128)(2,1)S(1)}, bf16[2048,128]{1,0:T(8,128)(2,1)S(1)}, u32[]{:S(2)}, u32[]{:S(2)}) %collective-permute-start.3) | collective-permute-done | bytes 524320 | tf_op jit(solution)/shard_map/ppermute | solution.py:367
  66.6 0.0 collective-permute-done.10.refs_4_.refs_9_
  66.6 0.0 collective-permute-done.5.refs_2_.refs_3_
  66.6 0.0 collective-permute-done.1.refs_0_.refs_1_
  66.6 0.0 copy-start.3
  66.6 1.6 %pick_rows.5 = (bf16[3072,128]{1,0:T(8,128)(2,1)S(1)}, bf16[3072,128]{1,0:T(8,128)(2,1)S(1)}, bf16[3072,128]{1,0:T(8,128)(2,1)S(1)}) custom-call(s32[8,8]{1,0:T(8,128)S(1)} %collective-permute-done.8.refs_0_, bf16[4112,128]{1,0:T(8,128)(2,1)S(1)} %collective-permute-done.1.refs_0_.refs_1_, bf16[2048,128]{1,0:T(8,128)(2,1)S(1)} %collective-permute-done.3.refs_1_.refs_2_, ...), custom_call_target="tpu_custom_call" | custom-call | flops 20000000000 | bytes 1024 | tf_op jit(solution)/shard_map/pick_rows/pallas_call | solution.py:219
  68.2 0.3 collective-permute-start.16
  68.5 1.3 %collective-permute-start.14 = (bf16[3072,128]{1,0:T(8,128)(2,1)S(1)}, bf16[3072,128]{1,0:T(8,128)(2,1)S(1)}, u32[]{:S(2)}, u32[]{:S(2)}) collective-permute-start(bf16[3072,128]{1,0:T(8,128)(2,1)S(1)} %get-tuple-element.34), channel_id=1, source_target_pairs={{8,0},{12,4},{16,24},{20,28},{9,1},{13,5},{17,25},{21,29},{10,2},{... | collective-permute-start | bytes 2359304 | tf_op jit(solution)/shard_map/ppermute | solution.py:367
  69.8 1.3 %collective-permute-start.15 = (bf16[3072,128]{1,0:T(8,128)(2,1)S(1)}, bf16[3072,128]{1,0:T(8,128)(2,1)S(1)}, u32[]{:S(2)}, u32[]{:S(2)}) collective-permute-start(bf16[3072,128]{1,0:T(8,128)(2,1)S(1)} %get-tuple-element.35), channel_id=1, source_target_pairs={{8,4},{12,0},{16,28},{20,24},{9,5},{13,1},{17,29},{21,25},{10,6},{... | collective-permute-start | bytes 2359304 | tf_op jit(solution)/shard_map/ppermute | solution.py:367
  71.1 0.0 collective-permute-done.11.refs_5_
  71.1 0.0 copy-done.3
  71.1 3.6 %stage_products.5 = (bf16[7,3,128,128]{3,2,1,0:T(8,128)(2,1)S(1)}, bf16[7,3,128,128]{3,2,1,0:T(8,128)(2,1)S(1)}, bf16[7,3,128,128]{3,2,1,0:T(8,128)(2,1)S(1)}) custom-call(s32[8,8]{1,0:T(8,128)S(1)} %bitcast.23, s32[8,8]{1,0:T(8,128)S(1)} %bitcast.19, s32[1,8]{1,0:T(1,128)S(1)} %bitcast.27, bf16[16,384,128]{2,1,0:T(8,128)(2,1)S(1)} %turn_rows.1.turned, ...), custom_call_target="tpu_custom_call" | custom-call | flops 1024 | bytes 1024 | tf_op jit(solution)/shard_map/stage_products/pallas_call | solution.py:297
  74.7 5.5 %collective-permute-start.12 = (bf16[7,3,128,128]{3,2,1,0:T(8,128)(2,1)S(1)}, bf16[7,3,128,128]{3,2,1,0:T(8,128)(2,1)S(1)}, u32[]{:S(2)}, u32[]{:S(2)}) collective-permute-start(bf16[7,3,128,128]{3,2,1,0:T(8,128)(2,1)S(1)} %get-tuple-element.32), channel_id=1, source_target_pairs={{0,1},{1,2},{2,3},{4,5},{5,6},{6,7},{8,9},{9,10},{10,11},{12,13},{... | collective-permute-start | bytes 2064392 | tf_op jit(solution)/shard_map/ppermute | solution.py:376
  80.3 1.9 %collective-permute-start.13 = (bf16[7,3,128,128]{3,2,1,0:T(8,128)(2,1)S(1)}, bf16[7,3,128,128]{3,2,1,0:T(8,128)(2,1)S(1)}, u32[]{:S(2)}, u32[]{:S(2)}) collective-permute-start(bf16[7,3,128,128]{3,2,1,0:T(8,128)(2,1)S(1)} %get-tuple-element.33), channel_id=1, source_target_pairs={{1,0},{2,1},{3,2},{5,4},{6,5},{7,6},{9,8},{10,9},{11,10},{13,12},{... | collective-permute-start | bytes 2064392 | tf_op jit(solution)/shard_map/ppermute | solution.py:377
  82.2 2.2 %collective-permute-done.16.refs_0_ = bf16[3072,128]{1,0:T(8,128)(2,1)S(1)} collective-permute-done((bf16[3072,128]{1,0:T(8,128)(2,1)S(1)}, bf16[3072,128]{1,0:T(8,128)(2,1)S(1)}, u32[]{:S(2)}, u32[]{:S(2)}) %collective-permute-start.16) | collective-permute-done | bytes 786464 | tf_op jit(solution)/shard_map/ppermute | solution.py:367
  84.4 1.2 stage_products.6
  85.6 2.5 %collective-permute-done.12.refs_5_.refs_1_ = bf16[7,3,128,128]{3,2,1,0:T(8,128)(2,1)S(1)} collective-permute-done((bf16[7,3,128,128]{3,2,1,0:T(8,128)(2,1)S(1)}, bf16[7,3,128,128]{3,2,1,0:T(8,128)(2,1)S(1)}, u32[]{:S(2)}, u32[]{:S(2)}) %collective-permute-start.12) | collective-permute-done | bytes 688160 | tf_op jit(solution)/shard_map/ppermute | solution.py:376
  88.1 4.7 %collective-permute-done.13.refs_6_.refs_2_ = bf16[7,3,128,128]{3,2,1,0:T(8,128)(2,1)S(1)} collective-permute-done((bf16[7,3,128,128]{3,2,1,0:T(8,128)(2,1)S(1)}, bf16[7,3,128,128]{3,2,1,0:T(8,128)(2,1)S(1)}, u32[]{:S(2)}, u32[]{:S(2)}) %collective-permute-start.13) | collective-permute-done | bytes 688160 | tf_op jit(solution)/shard_map/ppermute | solution.py:377
  92.8 0.0 collective-permute-done.14.refs_0_
  92.8 11.8 %collective-permute-done.15.refs_1_ = bf16[3072,128]{1,0:T(8,128)(2,1)S(1)} collective-permute-done((bf16[3072,128]{1,0:T(8,128)(2,1)S(1)}, bf16[3072,128]{1,0:T(8,128)(2,1)S(1)}, u32[]{:S(2)}, u32[]{:S(2)}) %collective-permute-start.15) | collective-permute-done | bytes 786464 | tf_op jit(solution)/shard_map/ppermute | solution.py:367
  104.6 3.5 %stage_products.7 = (bf16[3,3,128,128]{3,2,1,0:T(8,128)(2,1)S(1)}, bf16[3,3,128,128]{3,2,1,0:T(8,128)(2,1)S(1)}, bf16[3,3,128,128]{3,2,1,0:T(8,128)(2,1)S(1)}) custom-call(s32[8,8]{1,0:T(8,128)S(1)} %bitcast.25, s32[8,8]{1,0:T(8,128)S(1)} %bitcast.21, s32[1,8]{1,0:T(1,128)S(1)} %bitcast.29, bf16[16,384,128]{2,1,0:T(8,128)(2,1)S(1)} %turn_rows.1.turned, ...), custom_call_target="tpu_custom_call" | custom-call | flops 1024 | bytes 1024 | tf_op jit(solution)/shard_map/stage_products/pallas_call | solution.py:297
  108.1 1.9 %collective-permute-start.17 = (bf16[3,3,128,128]{3,2,1,0:T(8,128)(2,1)S(1)}, bf16[3,3,128,128]{3,2,1,0:T(8,128)(2,1)S(1)}, u32[]{:S(2)}, u32[]{:S(2)}) collective-permute-start(bf16[3,3,128,128]{3,2,1,0:T(8,128)(2,1)S(1)} %get-tuple-element.41), channel_id=1, source_target_pairs={{0,1},{1,2},{2,3},{4,5},{5,6},{6,7},{8,9},{9,10},{10,11},{12,13},{... | collective-permute-start | bytes 884744 | tf_op jit(solution)/shard_map/ppermute | solution.py:376
  110.1 2.4 %collective-permute-start.18 = (bf16[3,3,128,128]{3,2,1,0:T(8,128)(2,1)S(1)}, bf16[3,3,128,128]{3,2,1,0:T(8,128)(2,1)S(1)}, u32[]{:S(2)}, u32[]{:S(2)}) collective-permute-start(bf16[3,3,128,128]{3,2,1,0:T(8,128)(2,1)S(1)} %get-tuple-element.42), channel_id=1, source_target_pairs={{1,0},{2,1},{3,2},{5,4},{6,5},{7,6},{9,8},{10,9},{11,10},{13,12},{... | collective-permute-start | bytes 884744 | tf_op jit(solution)/shard_map/ppermute | solution.py:377
  112.5 1.2 %collective-permute-done.17.refs_4_ = bf16[3,3,128,128]{3,2,1,0:T(8,128)(2,1)S(1)} collective-permute-done((bf16[3,3,128,128]{3,2,1,0:T(8,128)(2,1)S(1)}, bf16[3,3,128,128]{3,2,1,0:T(8,128)(2,1)S(1)}, u32[]{:S(2)}, u32[]{:S(2)}) %collective-permute-start.17) | collective-permute-done | bytes 294944 | tf_op jit(solution)/shard_map/ppermute | solution.py:376
  113.7 4.4 %collective-permute-done.18.refs_5_ = bf16[3,3,128,128]{3,2,1,0:T(8,128)(2,1)S(1)} collective-permute-done((bf16[3,3,128,128]{3,2,1,0:T(8,128)(2,1)S(1)}, bf16[3,3,128,128]{3,2,1,0:T(8,128)(2,1)S(1)}, u32[]{:S(2)}, u32[]{:S(2)}) %collective-permute-start.18) | collective-permute-done | bytes 294944 | tf_op jit(solution)/shard_map/ppermute | solution.py:377
  118.1 2.6 %assemble_coarse.1 = f32[5120,128]{1,0:T(8,128)} custom-call(bf16[7,3,128,128]{3,2,1,0:T(8,128)(2,1)S(1)} %get-tuple-element.31.refs_1_.refs_0_, bf16[7,3,128,128]{3,2,1,0:T(8,128)(2,1)S(1)} %collective-permute-done.12.refs_5_.refs_1_, bf16[7,3,128,128]{3,2,1,0:T(8,128)(2,1)S(1)} %collective-permute-done.13.refs_6_.refs_2_, ...), custom_call_target="tpu_custom_call" | custom-call | flops 1024 | bytes 1024 | tf_op jit(solution)/shard_map/assemble_coarse/pallas_call | solution.py:343
Async XLA Ops:
  0.0 1.4 %copy-start.1 = (bf16[1,16,128,384]{3,2,1,0:T(8,128)(2,1)S(1)}, bf16[1,16,128,384]{3,2,1,0:T(8,128)(2,1)}, u32[]{:S(2)}) copy-start(bf16[1,16,128,384]{3,2,1,0:T(8,128)(2,1)} %param.10) | copy-start | bytes 4718596
  1.4 0.7 copy-start.2
  2.1 0.7 copy-start.6
  3.8 24.0 %collective-permute-start.4 = (bf16[4112,128]{1,0:T(8,128)(2,1)S(1)}, bf16[4112,128]{1,0:T(8,128)(2,1)S(1)}, u32[]{:S(2)}, u32[]{:S(2)}) collective-permute-start(bf16[4112,128]{1,0:T(8,128)(2,1)S(1)} %get-tuple-element.24.head.refs_1_.refs_4_), channel_id=1, source_target_pairs={{8,0},{12,4},{16,8},{20,12},{24,16},{28,20},{9,1},{13,5},{17,9},{2... | collective-permute-start | bytes 3158024 | tf_op jit(solution)/shard_map/ppermute | solution.py:367
  5.9 25.7 %collective-permute-start = (bf16[4112,128]{1,0:T(8,128)(2,1)S(1)}, bf16[4112,128]{1,0:T(8,128)(2,1)S(1)}, u32[]{:S(2)}, u32[]{:S(2)}) collective-permute-start(bf16[4112,128]{1,0:T(8,128)(2,1)S(1)} %get-tuple-element.24.head.refs_1_.refs_4_), channel_id=1, source_target_pairs={{0,8},{4,12},{8,16},{12,20},{16,24},{20,28},{1,9},{5,13},{9,17},{1... | collective-permute-start | bytes 3158024 | tf_op jit(solution)/shard_map/ppermute | solution.py:367
  7.2 2.5 %collective-permute-start.8 = (s32[8,8]{1,0:T(8,128)S(1)}, s32[8,8]{1,0:T(8,128)S(1)}, u32[]{:S(2)}, u32[]{:S(2)}) collective-permute-start(s32[8,8]{1,0:T(8,128)S(1)} %bitcast.17), channel_id=1, source_target_pairs={{4,0},{0,4},{12,8},{8,12},{20,16},{16,20},{28,24},{24,28},{5,1},{1... | collective-permute-start | bytes 776 | tf_op jit(solution)/shard_map/ppermute | solution.py:367
  10.4 28.0 %collective-permute-start.9 = (bf16[3072,128]{1,0:T(8,128)(2,1)S(1)}, bf16[3072,128]{1,0:T(8,128)(2,1)S(1)}, u32[]{:S(2)}, u32[]{:S(2)}) collective-permute-start(bf16[3072,128]{1,0:T(8,128)(2,1)S(1)} %pick_rows.3), channel_id=1, source_target_pairs={{0,4},{4,0},{8,12},{12,8},{16,20},{20,16},{24,28},{28,24},{1,5},{5... | collective-permute-start | bytes 2359304 | tf_op jit(solution)/shard_map/ppermute | solution.py:367
  10.7 23.8 %collective-permute-start.6 = (bf16[2048,128]{1,0:T(8,128)(2,1)S(1)}, bf16[2048,128]{1,0:T(8,128)(2,1)S(1)}, u32[]{:S(2)}, u32[]{:S(2)}) collective-permute-start(bf16[2048,128]{1,0:T(8,128)(2,1)S(1)} %get-tuple-element.25.tail.refs_2_.refs_5_), channel_id=1, source_target_pairs={{9,1},{13,5},{17,9},{21,13},{25,17},{29,21},{10,2},{14,6},{18,10},... | collective-permute-start | bytes 1572872 | tf_op jit(solution)/shard_map/ppermute | solution.py:367
  15.0 23.4 %collective-permute-start.2 = (bf16[2048,128]{1,0:T(8,128)(2,1)S(1)}, bf16[2048,128]{1,0:T(8,128)(2,1)S(1)}, u32[]{:S(2)}, u32[]{:S(2)}) collective-permute-start(bf16[2048,128]{1,0:T(8,128)(2,1)S(1)} %get-tuple-element.25.tail.refs_2_.refs_5_), channel_id=1, source_target_pairs={{1,9},{5,13},{9,17},{13,21},{17,25},{21,29},{2,10},{6,14},{10,18},... | collective-permute-start | bytes 1572872 | tf_op jit(solution)/shard_map/ppermute | solution.py:367
  27.7 38.8 %collective-permute-start.5 = (bf16[4112,128]{1,0:T(8,128)(2,1)S(1)}, bf16[4112,128]{1,0:T(8,128)(2,1)S(1)}, u32[]{:S(2)}, u32[]{:S(2)}) collective-permute-start(bf16[4112,128]{1,0:T(8,128)(2,1)S(1)} %collective-permute-done.4.refs_3_.refs_2_.refs_7_), channel_id=1, source_target_pairs={{8,0},{12,4},{16,8},{20,12},{9,1},{13,5},{17,9},{21,13},{10,2},{14... | collective-permute-start | bytes 3158024 | tf_op jit(solution)/shard_map/ppermute | solution.py:367
  31.6 35.0 %collective-permute-start.1 = (bf16[4112,128]{1,0:T(8,128)(2,1)S(1)}, bf16[4112,128]{1,0:T(8,128)(2,1)S(1)}, u32[]{:S(2)}, u32[]{:S(2)}) collective-permute-start(bf16[4112,128]{1,0:T(8,128)(2,1)S(1)} %collective-permute-done.refs_1_.refs_0_.refs_5_), channel_id=1, source_target_pairs={{8,16},{12,20},{16,24},{20,28},{9,17},{13,21},{17,25},{21,29},{10,... | collective-permute-start | bytes 3158024 | tf_op jit(solution)/shard_map/ppermute | solution.py:367
  39.1 2.9 %copy-start = (bf16[1,1,8,8,128,128]{5,4,3,2,1,0:T(8,128)(2,1)S(1)}, bf16[1,1,8,8,128,128]{5,4,3,2,1,0:T(8,128)(2,1)}, u32[]{:S(2)}) copy-start(bf16[1,1,8,8,128,128]{5,4,3,2,1,0:T(8,128)(2,1)} %param.6) | copy-start | bytes 6291460
  39.1 2.9 %copy-start.4 = (s32[1,1,8,8]{3,2,1,0:T(8,128)S(1)}, s32[1,1,8,8]{3,2,1,0:T(8,128)}, u32[]{:S(2)}) copy-start(s32[1,1,8,8]{3,2,1,0:T(8,128)} %param.7) | copy-start | bytes 772
  39.1 2.9 %copy-start.5 = (s32[1,1,8]{2,1,0:T(1,128)S(1)}, s32[1,1,8]{2,1,0:T(1,128)}, u32[]{:S(2)}) copy-start(s32[1,1,8]{2,1,0:T(1,128)} %param.9) | copy-start | bytes 100
  39.1 27.4 %collective-permute-start.10 = (bf16[3088,128]{1,0:T(8,128)(2,1)S(1)}, bf16[3088,128]{1,0:T(8,128)(2,1)S(1)}, u32[]{:S(2)}, u32[]{:S(2)}) collective-permute-start(bf16[3088,128]{1,0:T(8,128)(2,1)S(1)} %get-tuple-element.26), channel_id=1, source_target_pairs={{0,4},{4,0},{8,12},{12,8},{16,20},{20,16},{24,28},{28,24},{1,5},{5... | collective-permute-start | bytes 2371592 | tf_op jit(solution)/shard_map/ppermute | solution.py:367
  39.4 6.7 %collective-permute-start.7 = (bf16[2048,128]{1,0:T(8,128)(2,1)S(1)}, bf16[2048,128]{1,0:T(8,128)(2,1)S(1)}, u32[]{:S(2)}, u32[]{:S(2)}) collective-permute-start(bf16[2048,128]{1,0:T(8,128)(2,1)S(1)} %collective-permute-done.6.refs_4_.refs_3_.refs_8_), channel_id=1, source_target_pairs={{9,1},{13,5},{17,9},{21,13},{10,2},{14,6},{18,10},{22,14}} | collective-permute-start | bytes 1572872 | tf_op jit(solution)/shard_map/ppermute | solution.py:367
  40.2 26.3 %collective-permute-start.3 = (bf16[2048,128]{1,0:T(8,128)(2,1)S(1)}, bf16[2048,128]{1,0:T(8,128)(2,1)S(1)}, u32[]{:S(2)}, u32[]{:S(2)}) collective-permute-start(bf16[2048,128]{1,0:T(8,128)(2,1)S(1)} %collective-permute-done.2.refs_2_.refs_1_.refs_6_), channel_id=1, source_target_pairs={{9,17},{13,21},{17,25},{21,29},{10,18},{14,22},{18,26},{22,30}} | collective-permute-start | bytes 1572872 | tf_op jit(solution)/shard_map/ppermute | solution.py:367
  46.1 25.0 %collective-permute-start.11 = (bf16[3072,128]{1,0:T(8,128)(2,1)S(1)}, bf16[3072,128]{1,0:T(8,128)(2,1)S(1)}, u32[]{:S(2)}, u32[]{:S(2)}) collective-permute-start(bf16[3072,128]{1,0:T(8,128)(2,1)S(1)} %get-tuple-element.27), channel_id=1, source_target_pairs={{8,12},{12,8},{16,20},{20,16},{9,13},{13,9},{17,21},{21,17},{10,14... | collective-permute-start | bytes 2359304 | tf_op jit(solution)/shard_map/ppermute | solution.py:367
  66.6 4.5 %copy-start.3 = (s32[1,1,8,8]{3,2,1,0:T(8,128)S(1)}, s32[1,1,8,8]{3,2,1,0:T(8,128)}, u32[]{:S(2)}) copy-start(s32[1,1,8,8]{3,2,1,0:T(8,128)} %param.8) | copy-start | bytes 772
  68.2 16.2 %collective-permute-start.16 = (bf16[3072,128]{1,0:T(8,128)(2,1)S(1)}, bf16[3072,128]{1,0:T(8,128)(2,1)S(1)}, u32[]{:S(2)}, u32[]{:S(2)}) collective-permute-start(bf16[3072,128]{1,0:T(8,128)(2,1)S(1)} %get-tuple-element.36), channel_id=1, source_target_pairs={{0,4},{4,0},{8,12},{12,8},{16,20},{20,16},{24,28},{28,24},{1,5},{5... | collective-permute-start | bytes 2359304 | tf_op jit(solution)/shard_map/ppermute | solution.py:367
  68.5 24.3 %collective-permute-start.14 = (bf16[3072,128]{1,0:T(8,128)(2,1)S(1)}, bf16[3072,128]{1,0:T(8,128)(2,1)S(1)}, u32[]{:S(2)}, u32[]{:S(2)}) collective-permute-start(bf16[3072,128]{1,0:T(8,128)(2,1)S(1)} %get-tuple-element.34), channel_id=1, source_target_pairs={{8,0},{12,4},{16,24},{20,28},{9,1},{13,5},{17,25},{21,29},{10,2},{... | collective-permute-start | bytes 2359304 | tf_op jit(solution)/shard_map/ppermute | solution.py:367
  69.8 34.8 %collective-permute-start.15 = (bf16[3072,128]{1,0:T(8,128)(2,1)S(1)}, bf16[3072,128]{1,0:T(8,128)(2,1)S(1)}, u32[]{:S(2)}, u32[]{:S(2)}) collective-permute-start(bf16[3072,128]{1,0:T(8,128)(2,1)S(1)} %get-tuple-element.35), channel_id=1, source_target_pairs={{8,4},{12,0},{16,28},{20,24},{9,5},{13,1},{17,29},{21,25},{10,6},{... | collective-permute-start | bytes 2359304 | tf_op jit(solution)/shard_map/ppermute | solution.py:367
  74.7 13.4 %collective-permute-start.12 = (bf16[7,3,128,128]{3,2,1,0:T(8,128)(2,1)S(1)}, bf16[7,3,128,128]{3,2,1,0:T(8,128)(2,1)S(1)}, u32[]{:S(2)}, u32[]{:S(2)}) collective-permute-start(bf16[7,3,128,128]{3,2,1,0:T(8,128)(2,1)S(1)} %get-tuple-element.32), channel_id=1, source_target_pairs={{0,1},{1,2},{2,3},{4,5},{5,6},{6,7},{8,9},{9,10},{10,11},{12,13},{... | collective-permute-start | bytes 2064392 | tf_op jit(solution)/shard_map/ppermute | solution.py:376
  80.3 12.6 %collective-permute-start.13 = (bf16[7,3,128,128]{3,2,1,0:T(8,128)(2,1)S(1)}, bf16[7,3,128,128]{3,2,1,0:T(8,128)(2,1)S(1)}, u32[]{:S(2)}, u32[]{:S(2)}) collective-permute-start(bf16[7,3,128,128]{3,2,1,0:T(8,128)(2,1)S(1)} %get-tuple-element.33), channel_id=1, source_target_pairs={{1,0},{2,1},{3,2},{5,4},{6,5},{7,6},{9,8},{10,9},{11,10},{13,12},{... | collective-permute-start | bytes 2064392 | tf_op jit(solution)/shard_map/ppermute | solution.py:377
  108.1 5.6 %collective-permute-start.17 = (bf16[3,3,128,128]{3,2,1,0:T(8,128)(2,1)S(1)}, bf16[3,3,128,128]{3,2,1,0:T(8,128)(2,1)S(1)}, u32[]{:S(2)}, u32[]{:S(2)}) collective-permute-start(bf16[3,3,128,128]{3,2,1,0:T(8,128)(2,1)S(1)} %get-tuple-element.41), channel_id=1, source_target_pairs={{0,1},{1,2},{2,3},{4,5},{5,6},{6,7},{8,9},{9,10},{10,11},{12,13},{... | collective-permute-start | bytes 884744 | tf_op jit(solution)/shard_map/ppermute | solution.py:376
  110.1 8.0 %collective-permute-start.18 = (bf16[3,3,128,128]{3,2,1,0:T(8,128)(2,1)S(1)}, bf16[3,3,128,128]{3,2,1,0:T(8,128)(2,1)S(1)}, u32[]{:S(2)}, u32[]{:S(2)}) collective-permute-start(bf16[3,3,128,128]{3,2,1,0:T(8,128)(2,1)S(1)} %get-tuple-element.42), channel_id=1, source_target_pairs={{1,0},{2,1},{3,2},{5,4},{6,5},{7,6},{9,8},{10,9},{11,10},{13,12},{... | collective-permute-start | bytes 884744 | tf_op jit(solution)/shard_map/ppermute | solution.py:377

commit v7 on v6

--- a/solution.py
+++ b/solution.py
@@ -9,6 +9,7 @@
 VMEM_LIMIT = 24 * 1024 * 1024
 PARAMS = pltpu.CompilerParams(vmem_limit_bytes=VMEM_LIMIT)
 COST = pl.CostEstimate(flops=1024, bytes_accessed=1024, transcendentals=0)
+EARLY_COST = pl.CostEstimate(flops=1024, bytes_accessed=1024, transcendentals=0)
 NEAR_COST = pl.CostEstimate(flops=6 * 10 ** 9, bytes_accessed=1024, transcendentals=0)
 PICK_COST = pl.CostEstimate(flops=2 * 10 ** 10, bytes_accessed=1024, transcendentals=0)
 ANYWHERE = pl.BlockSpec(memory_space=pl.ANY)
@@ -162,14 +163,14 @@
     )(head, tail)
 
 
-def pick_kernel(grid, plan, layout, carry, tables, lists, outputs, *refs):
+def pick_kernel(grid, plan, layout, carry, tables, lists, filled, *refs):
     wanted = list(refs[:lists])
     sources, at = [], lists
     for blocks in layout:
         sources.append([(refs[at + i], k) for i, k in enumerate(blocks)])
         at += len(blocks)
     scratch = 2 * len(tables) + 1 if tables else 0
-    outs = refs[len(refs) - outputs - scratch:len(refs) - scratch]
+    outs = refs[len(refs) - len(filled) - scratch:len(refs) - scratch]
     z, y = grid.spot()
 
     def list_at(options):
@@ -188,15 +189,16 @@
         for table in range(len(tables)):
             pltpu.make_async_copy(numbers[table], plain[table], done.at[table]).wait()
         wanted += plain
-    for index, list_row, options, output, base in plan(z, y):
+    for index, list_row, options, output in plan(z, y):
         for present, source in options:
-            def copy(index=index, list_row=list_row, source=source, output=output, base=base):
+            def copy(index=index, list_row=list_row, source=source, output=output):
                 for entry in range(grid.cap):
                     row = wanted[index][list_row, entry]
                     place = 0
                     for ref, blocks in sources[source]:
                         for block in range(blocks):
-                            grid.part(outs[output], 3, base + entry, place)[...] = grid.part(ref, blocks, row, block)[...]
+                            target = grid.part(outs[output], filled[output], entry, place)
+                            target[...] = grid.part(ref, blocks, row, block)[...]
                             place += 1
             if present is True:
                 copy()
@@ -207,17 +209,17 @@
             out[out.shape[0] - grid.list_rows:, :] = list_at(options).astype(out.dtype)
 
 
-def pick(grid, plan, sizes, lists, sources, carry=(), tables=(), after=(), cost=COST):
+def pick(grid, plan, filled, lists, sources, carry=(), tables=(), after=(), cost=COST):
     flat = [x for source in sources for x, _ in source]
     width = flat[0].shape[-1]
-    carry = carry or ((),) * len(sizes)
-    shapes = [grid.shape(size, 3, width, 1 if options else 0) for size, options in zip(sizes, carry)]
+    carry = carry or ((),) * len(filled)
+    shapes = [grid.shape(grid.cap, blocks, width, 1 if options else 0) for blocks, options in zip(filled, carry)]
     layout = tuple(tuple(blocks for _, blocks in source) for source in sources)
     table = (grid.list_rows, width)
     scratch = [pltpu.VMEM(table, jnp.int32)] * len(tables) + [pltpu.SMEM(table, jnp.int32)] * len(tables)
     scratch += [pltpu.SemaphoreType.DMA((len(tables),))] if tables else []
     return pl.pallas_call(
-        functools.partial(pick_kernel, grid, plan, layout, carry, tables, len(lists), len(sizes)),
+        functools.partial(pick_kernel, grid, plan, layout, carry, tables, len(lists), tuple(filled)),
         grid_spec=pltpu.PrefetchScalarGridSpec(
             num_scalar_prefetch=len(lists),
             grid=(1,),
@@ -383,9 +385,9 @@
     side_lists = [move(cols_list, [(b, a) for a, b in grid.across(shift)]) for shift in sides]
 
     def own_requests(z, y):
-        return [(index, grid.panel(z, y, 0), [(True, 0)], index, 0) for index in range(len(sides))]
-
-    beside = move_across(pick(grid, own_requests, [cap] * len(sides), side_lists, [own]))
+        return [(index, grid.panel(z, y, 0), [(True, 0)], index) for index in range(len(sides))]
+
+    beside = move_across(pick(grid, own_requests, [3] * len(sides), side_lists, [own]))
     turned = turn(grid, head, tail)
 
     second = [move_both(near[0], grid.hops(2, 1)), move_both(near[1], grid.hops(2, -1))]
@@ -395,31 +397,42 @@
         requests = []
         for index in range(len(sides)):
             requests += [
-                (index, grid.panel(first, y, 0), [(odd, 0), (jnp.logical_not(odd), 1)], 2 * index, 0),
-                (index, grid.panel(other, y, 0), [(z == 1, 1), (z == LINES - 2, 0)], 2 * index + 1, 0)]
+                (index, grid.panel(first, y, 0), [(odd, 0), (jnp.logical_not(odd), 1)], 2 * index),
+                (index, grid.panel(other, y, 0), [(z == 1, 1), (z == LINES - 2, 0)], 2 * index + 1)]
         return requests
 
     def is_odd(z):
         return z % 2 == 1
 
     paired = ((None, 1), (is_odd, 0))
-    picked = pick(grid, near_requests, [cap] * (2 * len(sides)), side_lists, near, (paired, ()) * len(sides),
+    picked = pick(grid, near_requests, [3] * (2 * len(sides)), side_lists, near, (paired, ()) * len(sides),
                   after=[x for ((x, _),) in beside], cost=NEAR_COST)
     crossed, middle = move_across(picked[::2]), move_across(picked[1::2], (1, LINES - 2))
     parts = stage(grid, grid.work_near, lists, turned, matrix, [*near, own, *beside])
 
-    def second_requests(z, y):
+    def early_requests(z, y):
         line, below, above = grid.second(z)
-        return [(index, grid.panel(line, y, 0), [(below, 0), (above, 1)], index, 0)
-                for index in range(len(sides) + columns)]
-
-    tables = [((None, 3), (is_odd, 2))] + [((None, 4 + columns - 1 - shift),) for shift in sides]
-    picked = pick(grid, second_requests, [cap] * (len(sides) + columns), side_lists, [*second, *near, *crossed],
-                  tables=tuple(tables), after=[parts[0]], cost=PICK_COST)
+        return [(0, grid.panel(line, y, 0), [(below, 0), (above, 1)], 0)]
+
+    def late_requests(z, y):
+        line, below, above = grid.second(z)
+        row = grid.panel(line, y, 0)
+        return ([(index, row, [(below, 0), (above, 1)], index) for index in range(2 * len(sides))] +
+                [(2 * len(sides), row, [(below, 2), (above, 3)], 2 * len(sides))])
+
+    heads, tails = [(pair[0],) for pair in second], [(pair[1],) for pair in second]
+    near_heads = [(pair[0],) for pair in near]
+    end_list = ((None, 3), (is_odd, 2))
+    early = pick(grid, early_requests, [2], [], [*heads, *near_heads], tables=(end_list,), cost=EARLY_COST)
+    far_head = move(early[0], grid.ends(0))
+    tables = [((None, 6 + columns - 1 - shift),) for shift in sides] + [((None, 5), (is_odd, 4))]
+    picked = pick(grid, late_requests, [3] * (2 * len(sides)) + [1], side_lists,
+                  [*second, *tails, *near_heads, *crossed], tables=tuple(tables), after=[parts[0]], cost=PICK_COST)
     second_crossed = move_across(picked)
-    far = [((move(x, grid.ends(shift)), 3),) for shift, x in enumerate(picked[len(sides):])]
+    far = [((far_head, 2), (move(picked[-1], grid.ends(0), inner), 1))]
+    far += [((move(x, grid.ends(shift)), 3),) for shift, x in zip(sides, picked[len(sides):])]
     both = [x for pair in zip(crossed, middle) for x in pair]
-    parts = stage(grid, grid.work_second, lists, turned, matrix, [*second, *both], parts)
+    parts = stage(grid, grid.work_second, lists, turned, matrix, [*second, *both], parts, [far_head])
     first = exchange(parts)
     parts = stage(grid, grid.work_crossed, lists, turned, matrix, second_crossed, (), [parts[0]])
 

time: 121 us -> 121 us (level)
  the two profiles are of different devices: /device:TPU:29 before, /device:TPU:1 now
where the time goes in v7:
time: 121 us; the launch traced here: 119 us
  waiting for transfers between devices  56 us (46%)
  starting transfers between devices  39.9 us (33%)
  Pallas kernels  20 us (17%)
  local copies, waits for them, and re-layouts  2.8 us (2%)
    ppermute x16, waiting for transfers between devices, move(): return lax.ppermute(x, ('blk', 'rows'), perm) if perm else jnp.zeros_like(x)  50.4 us
    ppermute x16, starting transfers between devices, move(): return lax.ppermute(x, ('blk', 'rows'), perm) if perm else jnp.zeros_like(x)  25.7 us
    pallas_call x4, Pallas kernels, stage(): pl.pallas_call(functools.partial(stage_kernel, grid, plan, layout, carrie...  12.3 us
    ppermute x2, starting transfers between devices, exchange(): lax.ppermute(parts[1], 'rows', [(g, g + 1) for g in range(groups - 1)])  9.9 us
    ppermute x2, waiting for transfers between devices, exchange(): lax.ppermute(parts[2], 'rows', [(g + 1, g) for g in range(groups - 1)])  4.4 us
    ppermute x2, starting transfers between devices, exchange(): lax.ppermute(parts[2], 'rows', [(g + 1, g) for g in range(groups - 1)])  4.34 us
    pallas_call x4, Pallas kernels, pick(): pl.pallas_call(functools.partial(pick_kernel, grid, plan, layout, carry,...  3.69 us
    unnamed x14, local copies, waits for them, and re-layouts  2.8 us
  transfers between devices with their start and end apart: 20, of which 10 were waited for; matrix products, arithmetic and copies ran while one was open for 0% of the time, Pallas kernels for 12%

profile of v7, /device:TPU:1, one launch (start us, length us, event | category | flops | bytes accessed | tf_op | source)
XLA Modules:
  0.0 119.1 jit_solution(17773044201778883193)
XLA Ops:
  0.0 0.0 copy-start.1
  0.0 1.4 %copy-done.1 = bf16[1,16,128,384]{3,2,1,0:T(8,128)(2,1)S(1)} copy-done((bf16[1,16,128,384]{3,2,1,0:T(8,128)(2,1)S(1)}, bf16[1,16,128,384]{3,2,1,0:T(8,128)(2,1)}, u32[]{:S(2)}) %copy-start.1) | copy-done | bytes 1572888
  1.4 0.0 copy-start.2
  1.4 0.7 copy-done.2
  2.1 0.7 copy-done.6
  2.8 1.0 pack_rows.1
  3.8 1.3 %collective-permute-start.4 = (bf16[4112,128]{1,0:T(8,128)(2,1)S(1)}, bf16[4112,128]{1,0:T(8,128)(2,1)S(1)}, u32[]{:S(2)}, u32[]{:S(2)}) collective-permute-start(bf16[4112,128]{1,0:T(8,128)(2,1)S(1)} %get-tuple-element.24.head.refs_1_.refs_4_), channel_id=1, source_target_pairs={{8,0},{12,4},{16,8},{20,12},{24,16},{28,20},{9,1},{13,5},{17,9},{2... | collective-permute-start | bytes 3158024 | tf_op jit(solution)/shard_map/ppermute | solution.py:369
  5.1 4.7 %collective-permute-start = (bf16[4112,128]{1,0:T(8,128)(2,1)S(1)}, bf16[4112,128]{1,0:T(8,128)(2,1)S(1)}, u32[]{:S(2)}, u32[]{:S(2)}) collective-permute-start(bf16[4112,128]{1,0:T(8,128)(2,1)S(1)} %get-tuple-element.24.head.refs_1_.refs_4_), channel_id=1, source_target_pairs={{0,8},{4,12},{8,16},{12,20},{16,24},{20,28},{1,9},{5,13},{9,17},{1... | collective-permute-start | bytes 3158024 | tf_op jit(solution)/shard_map/ppermute | solution.py:369
  9.8 1.5 %collective-permute-start.8 = (s32[8,8]{1,0:T(8,128)S(1)}, s32[8,8]{1,0:T(8,128)S(1)}, u32[]{:S(2)}, u32[]{:S(2)}) collective-permute-start(s32[8,8]{1,0:T(8,128)S(1)} %bitcast.17), channel_id=1, source_target_pairs={{4,0},{0,4},{12,8},{8,12},{20,16},{16,20},{28,24},{24,28},{5,1},{1... | collective-permute-start | bytes 776 | tf_op jit(solution)/shard_map/ppermute | solution.py:369
  11.2 1.4 %collective-permute-done.8.refs_0_ = s32[8,8]{1,0:T(8,128)S(1)} collective-permute-done((s32[8,8]{1,0:T(8,128)S(1)}, s32[8,8]{1,0:T(8,128)S(1)}, u32[]{:S(2)}, u32[]{:S(2)}) %collective-permute-start.8) | collective-permute-done | bytes 288 | tf_op jit(solution)/shard_map/ppermute | solution.py:369
  12.6 0.7 pick_rows.4
  13.3 1.5 %collective-permute-start.9 = (bf16[3072,128]{1,0:T(8,128)(2,1)S(1)}, bf16[3072,128]{1,0:T(8,128)(2,1)S(1)}, u32[]{:S(2)}, u32[]{:S(2)}) collective-permute-start(bf16[3072,128]{1,0:T(8,128)(2,1)S(1)} %pick_rows.4), channel_id=1, source_target_pairs={{0,4},{4,0},{8,12},{12,8},{16,20},{20,16},{24,28},{28,24},{1,5},{5... | collective-permute-start | bytes 2359304 | tf_op jit(solution)/shard_map/ppermute | solution.py:369
  14.7 1.3 %collective-permute-start.6 = (bf16[2048,128]{1,0:T(8,128)(2,1)S(1)}, bf16[2048,128]{1,0:T(8,128)(2,1)S(1)}, u32[]{:S(2)}, u32[]{:S(2)}) collective-permute-start(bf16[2048,128]{1,0:T(8,128)(2,1)S(1)} %get-tuple-element.25.tail.refs_2_.refs_5_), channel_id=1, source_target_pairs={{9,1},{13,5},{17,9},{21,13},{25,17},{29,21},{10,2},{14,6},{18,10},... | collective-permute-start | bytes 1572872 | tf_op jit(solution)/shard_map/ppermute | solution.py:369
  16.0 4.0 %collective-permute-start.2 = (bf16[2048,128]{1,0:T(8,128)(2,1)S(1)}, bf16[2048,128]{1,0:T(8,128)(2,1)S(1)}, u32[]{:S(2)}, u32[]{:S(2)}) collective-permute-start(bf16[2048,128]{1,0:T(8,128)(2,1)S(1)} %get-tuple-element.25.tail.refs_2_.refs_5_), channel_id=1, source_target_pairs={{1,9},{5,13},{9,17},{13,21},{17,25},{21,29},{2,10},{6,14},{10,18},... | collective-permute-start | bytes 1572872 | tf_op jit(solution)/shard_map/ppermute | solution.py:369
  20.1 10.7 %collective-permute-done.4.refs_3_.refs_2_.refs_8_ = bf16[4112,128]{1,0:T(8,128)(2,1)S(1)} collective-permute-done((bf16[4112,128]{1,0:T(8,128)(2,1)S(1)}, bf16[4112,128]{1,0:T(8,128)(2,1)S(1)}, u32[]{:S(2)}, u32[]{:S(2)}) %collective-permute-start.4) | collective-permute-done | bytes 1052704 | tf_op jit(solution)/shard_map/ppermute | solution.py:369
  30.8 1.3 %collective-permute-start.5 = (bf16[4112,128]{1,0:T(8,128)(2,1)S(1)}, bf16[4112,128]{1,0:T(8,128)(2,1)S(1)}, u32[]{:S(2)}, u32[]{:S(2)}) collective-permute-start(bf16[4112,128]{1,0:T(8,128)(2,1)S(1)} %collective-permute-done.4.refs_3_.refs_2_.refs_8_), channel_id=1, source_target_pairs={{8,0},{12,4},{16,8},{20,12},{9,1},{13,5},{17,9},{21,13},{10,2},{14... | collective-permute-start | bytes 3158024 | tf_op jit(solution)/shard_map/ppermute | solution.py:369
  32.0 0.0 collective-permute-done.refs_1_.refs_0_.refs_2_.refs_7_
  32.0 0.7 collective-permute-start.1
  32.8 4.1 %collective-permute-done.6.refs_4_.refs_3_ = bf16[2048,128]{1,0:T(8,128)(2,1)S(1)} collective-permute-done((bf16[2048,128]{1,0:T(8,128)(2,1)S(1)}, bf16[2048,128]{1,0:T(8,128)(2,1)S(1)}, u32[]{:S(2)}, u32[]{:S(2)}) %collective-permute-start.6) | collective-permute-done | bytes 524320 | tf_op jit(solution)/shard_map/ppermute | solution.py:369
  36.9 1.5 %collective-permute-done.2.refs_2_.refs_1_ = bf16[2048,128]{1,0:T(8,128)(2,1)S(1)} collective-permute-done((bf16[2048,128]{1,0:T(8,128)(2,1)S(1)}, bf16[2048,128]{1,0:T(8,128)(2,1)S(1)}, u32[]{:S(2)}, u32[]{:S(2)}) %collective-permute-start.2) | collective-permute-done | bytes 524320 | tf_op jit(solution)/shard_map/ppermute | solution.py:369
  38.4 0.0 collective-permute-done.9.refs_5_.refs_6_
  38.4 0.7 pick_rows.5
  39.1 0.0 copy-start
  39.1 0.0 copy-start.3
  39.1 0.0 copy-start.4
  39.1 0.0 copy-start.5
  39.1 1.5 %collective-permute-start.10 = (bf16[3088,128]{1,0:T(8,128)(2,1)S(1)}, bf16[3088,128]{1,0:T(8,128)(2,1)S(1)}, u32[]{:S(2)}, u32[]{:S(2)}) collective-permute-start(bf16[3088,128]{1,0:T(8,128)(2,1)S(1)} %get-tuple-element.26), channel_id=1, source_target_pairs={{0,4},{4,0},{8,12},{12,8},{16,20},{20,16},{24,28},{28,24},{1,5},{5... | collective-permute-start | bytes 2371592 | tf_op jit(solution)/shard_map/ppermute | solution.py:369
  40.6 1.3 %collective-permute-start.7 = (bf16[2048,128]{1,0:T(8,128)(2,1)S(1)}, bf16[2048,128]{1,0:T(8,128)(2,1)S(1)}, u32[]{:S(2)}, u32[]{:S(2)}) collective-permute-start(bf16[2048,128]{1,0:T(8,128)(2,1)S(1)} %collective-permute-done.6.refs_4_.refs_3_), channel_id=1, source_target_pairs={{9,1},{13,5},{17,9},{21,13},{10,2},{14,6},{18,10},{22,14}} | collective-permute-start | bytes 1572872 | tf_op jit(solution)/shard_map/ppermute | solution.py:369
  41.9 0.7 collective-permute-start.3
  42.6 0.5 turn_rows.1.turned
  43.1 0.0 copy-done
  43.1 0.0 copy-done.3
  43.1 0.0 copy-done.4
  43.1 0.0 copy-done.5
  43.1 3.2 %stage_products.4 = (bf16[4,3,128,128]{3,2,1,0:T(8,128)(2,1)S(1)}, bf16[4,3,128,128]{3,2,1,0:T(8,128)(2,1)S(1)}, bf16[4,3,128,128]{3,2,1,0:T(8,128)(2,1)S(1)}) custom-call(s32[8,8]{1,0:T(8,128)S(1)} %bitcast.22, s32[8,8]{1,0:T(8,128)S(1)} %bitcast.18, s32[1,8]{1,0:T(1,128)S(1)} %bitcast.26, bf16[16,384,128]{2,1,0:T(8,128)(2,1)S(1)} %turn_rows.1.turned, ...), custom_call_target="tpu_custom_call" | custom-call | flops 1024 | bytes 1024 | tf_op jit(solution)/shard_map/stage_products/pallas_call | solution.py:299
  46.3 12.7 %collective-permute-done.5.refs_1_.refs_2_.refs_3_ = bf16[4112,128]{1,0:T(8,128)(2,1)S(1)} collective-permute-done((bf16[4112,128]{1,0:T(8,128)(2,1)S(1)}, bf16[4112,128]{1,0:T(8,128)(2,1)S(1)}, u32[]{:S(2)}, u32[]{:S(2)}) %collective-permute-start.5) | collective-permute-done | bytes 1052704 | tf_op jit(solution)/shard_map/ppermute | solution.py:369
  59.0 0.7 collective-permute-start.11
  59.7 0.0 collective-permute-done.1.refs_0_.refs_1_
  59.7 0.7 pick_rows.6
  60.5 1.3 %collective-permute-start.12 = (bf16[2048,128]{1,0:T(8,128)(2,1)S(1)}, bf16[2048,128]{1,0:T(8,128)(2,1)S(1)}, u32[]{:S(2)}, u32[]{:S(2)}) collective-permute-start(bf16[2048,128]{1,0:T(8,128)(2,1)S(1)} %pick_rows.6), channel_id=1, source_target_pairs={{8,0},{12,4},{16,24},{20,28},{9,1},{13,5},{17,25},{21,29},{10,2},{... | collective-permute-start | bytes 1572872 | tf_op jit(solution)/shard_map/ppermute | solution.py:369
  61.8 3.3 %collective-permute-done.7.refs_3_.refs_4_.refs_6_ = bf16[2048,128]{1,0:T(8,128)(2,1)S(1)} collective-permute-done((bf16[2048,128]{1,0:T(8,128)(2,1)S(1)}, bf16[2048,128]{1,0:T(8,128)(2,1)S(1)}, u32[]{:S(2)}, u32[]{:S(2)}) %collective-permute-start.7) | collective-permute-done | bytes 524320 | tf_op jit(solution)/shard_map/ppermute | solution.py:369
  65.1 0.0 collective-permute-done.3.refs_1_.refs_2_.refs_5_
  65.1 0.0 collective-permute-done.10.refs_4_.refs_9_
  65.1 1.6 %pick_rows.7 = (bf16[3072,128]{1,0:T(8,128)(2,1)S(1)}, bf16[3072,128]{1,0:T(8,128)(2,1)S(1)}, bf16[1024,128]{1,0:T(8,128)(2,1)S(1)}) custom-call(s32[8,8]{1,0:T(8,128)S(1)} %collective-permute-done.8.refs_0_, bf16[4112,128]{1,0:T(8,128)(2,1)S(1)} %collective-permute-done.1.refs_0_.refs_1_, ...), custom_call_target="tpu_custom_call" | custom-call | flops 20000000000 | bytes 1024 | tf_op jit(solution)/shard_map/pick_rows/pallas_call | solution.py:221
  66.7 1.5 %collective-permute-start.17 = (bf16[3072,128]{1,0:T(8,128)(2,1)S(1)}, bf16[3072,128]{1,0:T(8,128)(2,1)S(1)}, u32[]{:S(2)}, u32[]{:S(2)}) collective-permute-start(bf16[3072,128]{1,0:T(8,128)(2,1)S(1)} %get-tuple-element.36), channel_id=1, source_target_pairs={{0,4},{4,0},{8,12},{12,8},{16,20},{20,16},{24,28},{28,24},{1,5},{5... | collective-permute-start | bytes 2359304 | tf_op jit(solution)/shard_map/ppermute | solution.py:369
  68.1 1.3 %collective-permute-start.16 = (bf16[3072,128]{1,0:T(8,128)(2,1)S(1)}, bf16[3072,128]{1,0:T(8,128)(2,1)S(1)}, u32[]{:S(2)}, u32[]{:S(2)}) collective-permute-start(bf16[3072,128]{1,0:T(8,128)(2,1)S(1)} %get-tuple-element.35), channel_id=1, source_target_pairs={{8,4},{12,0},{16,28},{20,24},{9,5},{13,1},{17,29},{21,25},{10,6},{... | collective-permute-start | bytes 2359304 | tf_op jit(solution)/shard_map/ppermute | solution.py:369
  69.4 0.0 collective-permute-done.11.refs_5_
  69.4 5.4 %collective-permute-done.12.refs_9_.refs_0_ = bf16[2048,128]{1,0:T(8,128)(2,1)S(1)} collective-permute-done((bf16[2048,128]{1,0:T(8,128)(2,1)S(1)}, bf16[2048,128]{1,0:T(8,128)(2,1)S(1)}, u32[]{:S(2)}, u32[]{:S(2)}) %collective-permute-start.12) | collective-permute-done | bytes 524320 | tf_op jit(solution)/shard_map/ppermute | solution.py:369
  74.8 4.5 %stage_products.5 = (bf16[7,3,128,128]{3,2,1,0:T(8,128)(2,1)S(1)}, bf16[7,3,128,128]{3,2,1,0:T(8,128)(2,1)S(1)}, bf16[7,3,128,128]{3,2,1,0:T(8,128)(2,1)S(1)}) custom-call(s32[8,8]{1,0:T(8,128)S(1)} %bitcast.23, s32[8,8]{1,0:T(8,128)S(1)} %bitcast.19, s32[1,8]{1,0:T(1,128)S(1)} %bitcast.27, bf16[16,384,128]{2,1,0:T(8,128)(2,1)S(1)} %turn_rows.1.turned, ...), custom_call_target="tpu_custom_call" | custom-call | flops 1024 | bytes 1024 | tf_op jit(solution)/shard_map/stage_products/pallas_call | solution.py:299
  79.4 8.0 %collective-permute-start.13 = (bf16[7,3,128,128]{3,2,1,0:T(8,128)(2,1)S(1)}, bf16[7,3,128,128]{3,2,1,0:T(8,128)(2,1)S(1)}, u32[]{:S(2)}, u32[]{:S(2)}) collective-permute-start(bf16[7,3,128,128]{3,2,1,0:T(8,128)(2,1)S(1)} %get-tuple-element.32), channel_id=1, source_target_pairs={{0,1},{1,2},{2,3},{4,5},{5,6},{6,7},{8,9},{9,10},{10,11},{12,13},{... | collective-permute-start | bytes 2064392 | tf_op jit(solution)/shard_map/ppermute | solution.py:378
  87.4 1.9 %collective-permute-start.14 = (bf16[7,3,128,128]{3,2,1,0:T(8,128)(2,1)S(1)}, bf16[7,3,128,128]{3,2,1,0:T(8,128)(2,1)S(1)}, u32[]{:S(2)}, u32[]{:S(2)}) collective-permute-start(bf16[7,3,128,128]{3,2,1,0:T(8,128)(2,1)S(1)} %get-tuple-element.33), channel_id=1, source_target_pairs={{1,0},{2,1},{3,2},{5,4},{6,5},{7,6},{9,8},{10,9},{11,10},{13,12},{... | collective-permute-start | bytes 2064392 | tf_op jit(solution)/shard_map/ppermute | solution.py:379
  89.3 1.3 %collective-permute-start.15 = (bf16[1024,128]{1,0:T(8,128)(2,1)S(1)}, bf16[1024,128]{1,0:T(8,128)(2,1)S(1)}, u32[]{:S(2)}, u32[]{:S(2)}) collective-permute-start(bf16[1024,128]{1,0:T(8,128)(2,1)S(1)} %get-tuple-element.34), channel_id=1, source_target_pairs={{9,1},{13,5},{17,25},{21,29},{10,2},{14,6},{18,26},{22,30}} | collective-permute-start | bytes 786440 | tf_op jit(solution)/shard_map/ppermute | solution.py:369
  90.6 11.4 %collective-permute-done.17.refs_0_ = bf16[3072,128]{1,0:T(8,128)(2,1)S(1)} collective-permute-done((bf16[3072,128]{1,0:T(8,128)(2,1)S(1)}, bf16[3072,128]{1,0:T(8,128)(2,1)S(1)}, u32[]{:S(2)}, u32[]{:S(2)}) %collective-permute-start.17) | collective-permute-done | bytes 786464 | tf_op jit(solution)/shard_map/ppermute | solution.py:369
  101.9 2.5 %stage_products.6 = (bf16[1,3,128,128]{3,2,1,0:T(8,128)(2,1)S(1)}, bf16[1,3,128,128]{3,2,1,0:T(8,128)(2,1)S(1)}, bf16[1,3,128,128]{3,2,1,0:T(8,128)(2,1)S(1)}) custom-call(s32[8,8]{1,0:T(8,128)S(1)} %bitcast.24, s32[8,8]{1,0:T(8,128)S(1)} %bitcast.20, s32[1,8]{1,0:T(1,128)S(1)} %bitcast.28, bf16[16,384,128]{2,1,0:T(8,128)(2,1)S(1)} %turn_rows.1.turned, ...), custom_call_target="tpu_custom_call" | custom-call | flops 1024 | bytes 1024 | tf_op jit(solution)/shard_map/stage_products/pallas_call | solution.py:299
  104.4 0.0 collective-permute-done.15.refs_1_
  104.4 0.0 collective-permute-done.16.refs_2_
  104.4 0.0 collective-permute-done.13.refs_6_.refs_1_
  104.4 0.0 collective-permute-done.14.refs_7_.refs_2_
  104.4 2.1 %stage_products.7 = (bf16[3,3,128,128]{3,2,1,0:T(8,128)(2,1)S(1)}, bf16[3,3,128,128]{3,2,1,0:T(8,128)(2,1)S(1)}, bf16[3,3,128,128]{3,2,1,0:T(8,128)(2,1)S(1)}) custom-call(s32[8,8]{1,0:T(8,128)S(1)} %bitcast.25, s32[8,8]{1,0:T(8,128)S(1)} %bitcast.21, s32[1,8]{1,0:T(1,128)S(1)} %bitcast.29, bf16[16,384,128]{2,1,0:T(8,128)(2,1)S(1)} %turn_rows.1.turned, ...), custom_call_target="tpu_custom_call" | custom-call | flops 1024 | bytes 1024 | tf_op jit(solution)/shard_map/stage_products/pallas_call | solution.py:299
  106.6 1.9 %collective-permute-start.18 = (bf16[3,3,128,128]{3,2,1,0:T(8,128)(2,1)S(1)}, bf16[3,3,128,128]{3,2,1,0:T(8,128)(2,1)S(1)}, u32[]{:S(2)}, u32[]{:S(2)}) collective-permute-start(bf16[3,3,128,128]{3,2,1,0:T(8,128)(2,1)S(1)} %get-tuple-element.41), channel_id=1, source_target_pairs={{0,1},{1,2},{2,3},{4,5},{5,6},{6,7},{8,9},{9,10},{10,11},{12,13},{... | collective-permute-start | bytes 884744 | tf_op jit(solution)/shard_map/ppermute | solution.py:378
  108.5 2.4 %collective-permute-start.19 = (bf16[3,3,128,128]{3,2,1,0:T(8,128)(2,1)S(1)}, bf16[3,3,128,128]{3,2,1,0:T(8,128)(2,1)S(1)}, u32[]{:S(2)}, u32[]{:S(2)}) collective-permute-start(bf16[3,3,128,128]{3,2,1,0:T(8,128)(2,1)S(1)} %get-tuple-element.42), channel_id=1, source_target_pairs={{1,0},{2,1},{3,2},{5,4},{6,5},{7,6},{9,8},{10,9},{11,10},{13,12},{... | collective-permute-start | bytes 884744 | tf_op jit(solution)/shard_map/ppermute | solution.py:379
  110.9 1.2 %collective-permute-done.18.refs_4_ = bf16[3,3,128,128]{3,2,1,0:T(8,128)(2,1)S(1)} collective-permute-done((bf16[3,3,128,128]{3,2,1,0:T(8,128)(2,1)S(1)}, bf16[3,3,128,128]{3,2,1,0:T(8,128)(2,1)S(1)}, u32[]{:S(2)}, u32[]{:S(2)}) %collective-permute-start.18) | collective-permute-done | bytes 294944 | tf_op jit(solution)/shard_map/ppermute | solution.py:378
  112.2 4.4 %collective-permute-done.19.refs_5_ = bf16[3,3,128,128]{3,2,1,0:T(8,128)(2,1)S(1)} collective-permute-done((bf16[3,3,128,128]{3,2,1,0:T(8,128)(2,1)S(1)}, bf16[3,3,128,128]{3,2,1,0:T(8,128)(2,1)S(1)}, u32[]{:S(2)}, u32[]{:S(2)}) %collective-permute-start.19) | collective-permute-done | bytes 294944 | tf_op jit(solution)/shard_map/ppermute | solution.py:379
  116.6 2.6 %assemble_coarse.1 = f32[5120,128]{1,0:T(8,128)} custom-call(bf16[7,3,128,128]{3,2,1,0:T(8,128)(2,1)S(1)} %get-tuple-element.31.refs_1_.refs_0_, bf16[7,3,128,128]{3,2,1,0:T(8,128)(2,1)S(1)} %collective-permute-done.13.refs_6_.refs_1_, bf16[7,3,128,128]{3,2,1,0:T(8,128)(2,1)S(1)} %collective-permute-done.14.refs_7_.refs_2_, ...), custom_call_target="tpu_custom_call" | custom-call | flops 1024 | bytes 1024 | tf_op jit(solution)/shard_map/assemble_coarse/pallas_call | solution.py:345
  (1 shorter events, 0.0 us)
Async XLA Ops:
  0.0 1.4 %copy-start.1 = (bf16[1,16,128,384]{3,2,1,0:T(8,128)(2,1)S(1)}, bf16[1,16,128,384]{3,2,1,0:T(8,128)(2,1)}, u32[]{:S(2)}) copy-start(bf16[1,16,128,384]{3,2,1,0:T(8,128)(2,1)} %param.10) | copy-start | bytes 4718596
  1.4 0.7 copy-start.2
  2.1 0.7 copy-start.6
  3.8 27.0 %collective-permute-start.4 = (bf16[4112,128]{1,0:T(8,128)(2,1)S(1)}, bf16[4112,128]{1,0:T(8,128)(2,1)S(1)}, u32[]{:S(2)}, u32[]{:S(2)}) collective-permute-start(bf16[4112,128]{1,0:T(8,128)(2,1)S(1)} %get-tuple-element.24.head.refs_1_.refs_4_), channel_id=1, source_target_pairs={{8,0},{12,4},{16,8},{20,12},{24,16},{28,20},{9,1},{13,5},{17,9},{2... | collective-permute-start | bytes 3158024 | tf_op jit(solution)/shard_map/ppermute | solution.py:369
  5.1 27.0 %collective-permute-start = (bf16[4112,128]{1,0:T(8,128)(2,1)S(1)}, bf16[4112,128]{1,0:T(8,128)(2,1)S(1)}, u32[]{:S(2)}, u32[]{:S(2)}) collective-permute-start(bf16[4112,128]{1,0:T(8,128)(2,1)S(1)} %get-tuple-element.24.head.refs_1_.refs_4_), channel_id=1, source_target_pairs={{0,8},{4,12},{8,16},{12,20},{16,24},{20,28},{1,9},{5,13},{9,17},{1... | collective-permute-start | bytes 3158024 | tf_op jit(solution)/shard_map/ppermute | solution.py:369
  9.8 2.8 %collective-permute-start.8 = (s32[8,8]{1,0:T(8,128)S(1)}, s32[8,8]{1,0:T(8,128)S(1)}, u32[]{:S(2)}, u32[]{:S(2)}) collective-permute-start(s32[8,8]{1,0:T(8,128)S(1)} %bitcast.17), channel_id=1, source_target_pairs={{4,0},{0,4},{12,8},{8,12},{20,16},{16,20},{28,24},{24,28},{5,1},{1... | collective-permute-start | bytes 776 | tf_op jit(solution)/shard_map/ppermute | solution.py:369
  13.3 25.1 %collective-permute-start.9 = (bf16[3072,128]{1,0:T(8,128)(2,1)S(1)}, bf16[3072,128]{1,0:T(8,128)(2,1)S(1)}, u32[]{:S(2)}, u32[]{:S(2)}) collective-permute-start(bf16[3072,128]{1,0:T(8,128)(2,1)S(1)} %pick_rows.4), channel_id=1, source_target_pairs={{0,4},{4,0},{8,12},{12,8},{16,20},{20,16},{24,28},{28,24},{1,5},{5... | collective-permute-start | bytes 2359304 | tf_op jit(solution)/shard_map/ppermute | solution.py:369
  14.7 22.2 %collective-permute-start.6 = (bf16[2048,128]{1,0:T(8,128)(2,1)S(1)}, bf16[2048,128]{1,0:T(8,128)(2,1)S(1)}, u32[]{:S(2)}, u32[]{:S(2)}) collective-permute-start(bf16[2048,128]{1,0:T(8,128)(2,1)S(1)} %get-tuple-element.25.tail.refs_2_.refs_5_), channel_id=1, source_target_pairs={{9,1},{13,5},{17,9},{21,13},{25,17},{29,21},{10,2},{14,6},{18,10},... | collective-permute-start | bytes 1572872 | tf_op jit(solution)/shard_map/ppermute | solution.py:369
  16.0 22.3 %collective-permute-start.2 = (bf16[2048,128]{1,0:T(8,128)(2,1)S(1)}, bf16[2048,128]{1,0:T(8,128)(2,1)S(1)}, u32[]{:S(2)}, u32[]{:S(2)}) collective-permute-start(bf16[2048,128]{1,0:T(8,128)(2,1)S(1)} %get-tuple-element.25.tail.refs_2_.refs_5_), channel_id=1, source_target_pairs={{1,9},{5,13},{9,17},{13,21},{17,25},{21,29},{2,10},{6,14},{10,18},... | collective-permute-start | bytes 1572872 | tf_op jit(solution)/shard_map/ppermute | solution.py:369
  30.8 28.2 %collective-permute-start.5 = (bf16[4112,128]{1,0:T(8,128)(2,1)S(1)}, bf16[4112,128]{1,0:T(8,128)(2,1)S(1)}, u32[]{:S(2)}, u32[]{:S(2)}) collective-permute-start(bf16[4112,128]{1,0:T(8,128)(2,1)S(1)} %collective-permute-done.4.refs_3_.refs_2_.refs_8_), channel_id=1, source_target_pairs={{8,0},{12,4},{16,8},{20,12},{9,1},{13,5},{17,9},{21,13},{10,2},{14... | collective-permute-start | bytes 3158024 | tf_op jit(solution)/shard_map/ppermute | solution.py:369
  32.0 27.7 %collective-permute-start.1 = (bf16[4112,128]{1,0:T(8,128)(2,1)S(1)}, bf16[4112,128]{1,0:T(8,128)(2,1)S(1)}, u32[]{:S(2)}, u32[]{:S(2)}) collective-permute-start(bf16[4112,128]{1,0:T(8,128)(2,1)S(1)} %collective-permute-done.refs_1_.refs_0_.refs_2_.refs_7_), channel_id=1, source_target_pairs={{8,16},{12,20},{16,24},{20,28},{9,17},{13,21},{17,25},{21,29},{10,... | collective-permute-start | bytes 3158024 | tf_op jit(solution)/shard_map/ppermute | solution.py:369
  39.1 4.0 %copy-start = (bf16[1,1,8,8,128,128]{5,4,3,2,1,0:T(8,128)(2,1)S(1)}, bf16[1,1,8,8,128,128]{5,4,3,2,1,0:T(8,128)(2,1)}, u32[]{:S(2)}) copy-start(bf16[1,1,8,8,128,128]{5,4,3,2,1,0:T(8,128)(2,1)} %param.6) | copy-start | bytes 6291460
  39.1 4.0 %copy-start.3 = (s32[1,1,8,8]{3,2,1,0:T(8,128)S(1)}, s32[1,1,8,8]{3,2,1,0:T(8,128)}, u32[]{:S(2)}) copy-start(s32[1,1,8,8]{3,2,1,0:T(8,128)} %param.8) | copy-start | bytes 772
  39.1 4.0 %copy-start.4 = (s32[1,1,8,8]{3,2,1,0:T(8,128)S(1)}, s32[1,1,8,8]{3,2,1,0:T(8,128)}, u32[]{:S(2)}) copy-start(s32[1,1,8,8]{3,2,1,0:T(8,128)} %param.7) | copy-start | bytes 772
  39.1 4.0 %copy-start.5 = (s32[1,1,8]{2,1,0:T(1,128)S(1)}, s32[1,1,8]{2,1,0:T(1,128)}, u32[]{:S(2)}) copy-start(s32[1,1,8]{2,1,0:T(1,128)} %param.9) | copy-start | bytes 100
  39.1 25.9 %collective-permute-start.10 = (bf16[3088,128]{1,0:T(8,128)(2,1)S(1)}, bf16[3088,128]{1,0:T(8,128)(2,1)S(1)}, u32[]{:S(2)}, u32[]{:S(2)}) collective-permute-start(bf16[3088,128]{1,0:T(8,128)(2,1)S(1)} %get-tuple-element.26), channel_id=1, source_target_pairs={{0,4},{4,0},{8,12},{12,8},{16,20},{20,16},{24,28},{28,24},{1,5},{5... | collective-permute-start | bytes 2371592 | tf_op jit(solution)/shard_map/ppermute | solution.py:369
  40.6 24.5 %collective-permute-start.7 = (bf16[2048,128]{1,0:T(8,128)(2,1)S(1)}, bf16[2048,128]{1,0:T(8,128)(2,1)S(1)}, u32[]{:S(2)}, u32[]{:S(2)}) collective-permute-start(bf16[2048,128]{1,0:T(8,128)(2,1)S(1)} %collective-permute-done.6.refs_4_.refs_3_), channel_id=1, source_target_pairs={{9,1},{13,5},{17,9},{21,13},{10,2},{14,6},{18,10},{22,14}} | collective-permute-start | bytes 1572872 | tf_op jit(solution)/shard_map/ppermute | solution.py:369
  41.9 23.2 %collective-permute-start.3 = (bf16[2048,128]{1,0:T(8,128)(2,1)S(1)}, bf16[2048,128]{1,0:T(8,128)(2,1)S(1)}, u32[]{:S(2)}, u32[]{:S(2)}) collective-permute-start(bf16[2048,128]{1,0:T(8,128)(2,1)S(1)} %collective-permute-done.2.refs_2_.refs_1_), channel_id=1, source_target_pairs={{9,17},{13,21},{17,25},{21,29},{10,18},{14,22},{18,26},{22,30}} | collective-permute-start | bytes 1572872 | tf_op jit(solution)/shard_map/ppermute | solution.py:369
  59.0 10.4 %collective-permute-start.11 = (bf16[3072,128]{1,0:T(8,128)(2,1)S(1)}, bf16[3072,128]{1,0:T(8,128)(2,1)S(1)}, u32[]{:S(2)}, u32[]{:S(2)}) collective-permute-start(bf16[3072,128]{1,0:T(8,128)(2,1)S(1)} %get-tuple-element.27), channel_id=1, source_target_pairs={{8,12},{12,8},{16,20},{20,16},{9,13},{13,9},{17,21},{21,17},{10,14... | collective-permute-start | bytes 2359304 | tf_op jit(solution)/shard_map/ppermute | solution.py:369
  60.5 14.4 %collective-permute-start.12 = (bf16[2048,128]{1,0:T(8,128)(2,1)S(1)}, bf16[2048,128]{1,0:T(8,128)(2,1)S(1)}, u32[]{:S(2)}, u32[]{:S(2)}) collective-permute-start(bf16[2048,128]{1,0:T(8,128)(2,1)S(1)} %pick_rows.6), channel_id=1, source_target_pairs={{8,0},{12,4},{16,24},{20,28},{9,1},{13,5},{17,25},{21,29},{10,2},{... | collective-permute-start | bytes 1572872 | tf_op jit(solution)/shard_map/ppermute | solution.py:369
  66.7 35.3 %collective-permute-start.17 = (bf16[3072,128]{1,0:T(8,128)(2,1)S(1)}, bf16[3072,128]{1,0:T(8,128)(2,1)S(1)}, u32[]{:S(2)}, u32[]{:S(2)}) collective-permute-start(bf16[3072,128]{1,0:T(8,128)(2,1)S(1)} %get-tuple-element.36), channel_id=1, source_target_pairs={{0,4},{4,0},{8,12},{12,8},{16,20},{20,16},{24,28},{28,24},{1,5},{5... | collective-permute-start | bytes 2359304 | tf_op jit(solution)/shard_map/ppermute | solution.py:369
  68.1 36.3 %collective-permute-start.16 = (bf16[3072,128]{1,0:T(8,128)(2,1)S(1)}, bf16[3072,128]{1,0:T(8,128)(2,1)S(1)}, u32[]{:S(2)}, u32[]{:S(2)}) collective-permute-start(bf16[3072,128]{1,0:T(8,128)(2,1)S(1)} %get-tuple-element.35), channel_id=1, source_target_pairs={{8,4},{12,0},{16,28},{20,24},{9,5},{13,1},{17,29},{21,25},{10,6},{... | collective-permute-start | bytes 2359304 | tf_op jit(solution)/shard_map/ppermute | solution.py:369
  79.4 25.1 %collective-permute-start.13 = (bf16[7,3,128,128]{3,2,1,0:T(8,128)(2,1)S(1)}, bf16[7,3,128,128]{3,2,1,0:T(8,128)(2,1)S(1)}, u32[]{:S(2)}, u32[]{:S(2)}) collective-permute-start(bf16[7,3,128,128]{3,2,1,0:T(8,128)(2,1)S(1)} %get-tuple-element.32), channel_id=1, source_target_pairs={{0,1},{1,2},{2,3},{4,5},{5,6},{6,7},{8,9},{9,10},{10,11},{12,13},{... | collective-permute-start | bytes 2064392 | tf_op jit(solution)/shard_map/ppermute | solution.py:378
  87.4 17.1 %collective-permute-start.14 = (bf16[7,3,128,128]{3,2,1,0:T(8,128)(2,1)S(1)}, bf16[7,3,128,128]{3,2,1,0:T(8,128)(2,1)S(1)}, u32[]{:S(2)}, u32[]{:S(2)}) collective-permute-start(bf16[7,3,128,128]{3,2,1,0:T(8,128)(2,1)S(1)} %get-tuple-element.33), channel_id=1, source_target_pairs={{1,0},{2,1},{3,2},{5,4},{6,5},{7,6},{9,8},{10,9},{11,10},{13,12},{... | collective-permute-start | bytes 2064392 | tf_op jit(solution)/shard_map/ppermute | solution.py:379
  89.3 15.1 %collective-permute-start.15 = (bf16[1024,128]{1,0:T(8,128)(2,1)S(1)}, bf16[1024,128]{1,0:T(8,128)(2,1)S(1)}, u32[]{:S(2)}, u32[]{:S(2)}) collective-permute-start(bf16[1024,128]{1,0:T(8,128)(2,1)S(1)} %get-tuple-element.34), channel_id=1, source_target_pairs={{9,1},{13,5},{17,25},{21,29},{10,2},{14,6},{18,26},{22,30}} | collective-permute-start | bytes 786440 | tf_op jit(solution)/shard_map/ppermute | solution.py:369
  106.6 5.6 %collective-permute-start.18 = (bf16[3,3,128,128]{3,2,1,0:T(8,128)(2,1)S(1)}, bf16[3,3,128,128]{3,2,1,0:T(8,128)(2,1)S(1)}, u32[]{:S(2)}, u32[]{:S(2)}) collective-permute-start(bf16[3,3,128,128]{3,2,1,0:T(8,128)(2,1)S(1)} %get-tuple-element.41), channel_id=1, source_target_pairs={{0,1},{1,2},{2,3},{4,5},{5,6},{6,7},{8,9},{9,10},{10,11},{12,13},{... | collective-permute-start | bytes 884744 | tf_op jit(solution)/shard_map/ppermute | solution.py:378
  108.5 8.0 %collective-permute-start.19 = (bf16[3,3,128,128]{3,2,1,0:T(8,128)(2,1)S(1)}, bf16[3,3,128,128]{3,2,1,0:T(8,128)(2,1)S(1)}, u32[]{:S(2)}, u32[]{:S(2)}) collective-permute-start(bf16[3,3,128,128]{3,2,1,0:T(8,128)(2,1)S(1)} %get-tuple-element.42), channel_id=1, source_target_pairs={{1,0},{2,1},{3,2},{5,4},{6,5},{7,6},{9,8},{10,9},{11,10},{13,12},{... | collective-permute-start | bytes 884744 | tf_op jit(solution)/shard_map/ppermute | solution.py:379

commit v8 on v7

--- a/solution.py
+++ b/solution.py
@@ -7,6 +7,7 @@
 from jax.sharding import PartitionSpec as P
 
 VMEM_LIMIT = 24 * 1024 * 1024
+PACK_VMEM_LIMIT = 60 * 1024 * 1024
 PARAMS = pltpu.CompilerParams(vmem_limit_bytes=VMEM_LIMIT)
 COST = pl.CostEstimate(flops=1024, bytes_accessed=1024, transcendentals=0)
 EARLY_COST = pl.CostEstimate(flops=1024, bytes_accessed=1024, transcendentals=0)
@@ -99,10 +100,22 @@
                 for shift in range(self.columns)]
 
 
-def pack_kernel(grid, mask, cols, prolong, head, tail):
+def pack_kernel(grid, mask_from, cols_from, prolong_from, head, tail, mask, cols, prolong, done):
     group, groups = lax.axis_index("rows"), lax.axis_size("rows")
     width = tail.shape[-1]
-    for i in range(prolong.shape[0]):
+    rows = prolong.shape[0]
+    step = rows // 4 if rows % 4 == 0 else rows
+    copies = [pltpu.make_async_copy(mask_from, mask, done.at[0]), pltpu.make_async_copy(cols_from, cols, done.at[1])]
+    for index in range(rows // step):
+        some = pl.ds(index * step, step)
+        copies.append(pltpu.make_async_copy(prolong_from.at[some], prolong.at[some], done.at[2 + index]))
+    for copy in copies:
+        copy.start()
+    copies[0].wait()
+    copies[1].wait()
+    for i in range(rows):
+        if i % step == 0:
+            copies[2 + i // step].wait()
         blocks = []
         for e in range(3):
             candidate = group + e - 1
@@ -112,13 +125,13 @@
         grid.part(head, 2, i, 0)[...] = jnp.where(group == 0, blocks[1], blocks[0])
         grid.part(head, 2, i, 1)[...] = jnp.where(group == 0, blocks[2], blocks[1])
         grid.part(tail, 1, i, 0)[...] = jnp.where(group == 0, blocks[0], blocks[2])
-    row = lax.broadcasted_iota(jnp.int32, (grid.list_rows, width), 0)
+    line = lax.broadcasted_iota(jnp.int32, (grid.list_rows, width), 0)
     column = lax.broadcasted_iota(jnp.int32, (grid.list_rows, width), 1)
     numbers = jnp.zeros((grid.list_rows, width), jnp.int32)
     for panel in range(grid.panels):
         for entry in range(grid.cap):
-            numbers = jnp.where((row == panel) & (column == entry), cols[panel, entry], numbers)
-    start = prolong.shape[0] * 2 * grid.pores
+            numbers = jnp.where((line == panel) & (column == entry), cols[panel, entry], numbers)
+    start = rows * 2 * grid.pores
     head[start:start + grid.list_rows, :] = numbers.astype(jnp.float32).astype(head.dtype)
 
 
@@ -127,14 +140,17 @@
     outs = [grid.shape(rows, 2, width3 // 3, 1), grid.shape(rows, 1, width3 // 3)]
     return pl.pallas_call(
         functools.partial(pack_kernel, grid),
-        grid_spec=pltpu.PrefetchScalarGridSpec(
-            num_scalar_prefetch=2,
-            grid=(1,),
-            in_specs=[resident(prolong)],
-            out_specs=[*map(resident, outs)],
-        ),
+        grid=(1,),
+        in_specs=[pl.BlockSpec(memory_space=pl.ANY)] * 3,
+        out_specs=[*map(resident, outs)],
+        scratch_shapes=[
+            pltpu.SMEM(mask.shape, mask.dtype),
+            pltpu.SMEM(cols.shape, cols.dtype),
+            pltpu.VMEM(prolong.shape, prolong.dtype),
+            pltpu.SemaphoreType.DMA((6,)),
+        ],
         out_shape=outs,
-        compiler_params=PARAMS,
+        compiler_params=pltpu.CompilerParams(vmem_limit_bytes=PACK_VMEM_LIMIT),
         cost_estimate=COST,
         name="pack_rows",
     )(mask, cols, prolong)
@@ -412,27 +428,32 @@
 
     def early_requests(z, y):
         line, below, above = grid.second(z)
-        return [(0, grid.panel(line, y, 0), [(below, 0), (above, 1)], 0)]
+        return [(index, grid.panel(line, y, 0), [(below, 0), (above, 1)], index) for index in range(len(sides) + 1)]
 
     def late_requests(z, y):
         line, below, above = grid.second(z)
         row = grid.panel(line, y, 0)
-        return ([(index, row, [(below, 0), (above, 1)], index) for index in range(2 * len(sides))] +
-                [(2 * len(sides), row, [(below, 2), (above, 3)], 2 * len(sides))])
+        last, whole = [(below, 2), (above, 3)], [(below, 0), (above, 1)]
+        return ([(index, row, last, index) for index in range(len(sides))] +
+                [(index, row, whole, index) for index in range(len(sides), 2 * len(sides))] +
+                [(2 * len(sides), row, last, 2 * len(sides))])
 
     heads, tails = [(pair[0],) for pair in second], [(pair[1],) for pair in second]
     near_heads = [(pair[0],) for pair in near]
     end_list = ((None, 3), (is_odd, 2))
-    early = pick(grid, early_requests, [2], [], [*heads, *near_heads], tables=(end_list,), cost=EARLY_COST)
-    far_head = move(early[0], grid.ends(0))
+    early = pick(grid, early_requests, [2] * (len(sides) + 1), side_lists, [*heads, *near_heads], tables=(end_list,),
+                 cost=EARLY_COST)
+    far_head = move(early[-1], grid.ends(0))
+    second_heads = [move(x, grid.across(shift)) for x, shift in zip(early, sides)]
     tables = [((None, 6 + columns - 1 - shift),) for shift in sides] + [((None, 5), (is_odd, 4))]
-    picked = pick(grid, late_requests, [3] * (2 * len(sides)) + [1], side_lists,
+    picked = pick(grid, late_requests, [1] * len(sides) + [3] * len(sides) + [1], side_lists,
                   [*second, *tails, *near_heads, *crossed], tables=tuple(tables), after=[parts[0]], cost=PICK_COST)
-    second_crossed = move_across(picked)
+    second_crossed = [((x, 2), (move(last, grid.across(shift), inner), 1))
+                      for x, last, shift in zip(second_heads, picked, sides)]
     far = [((far_head, 2), (move(picked[-1], grid.ends(0), inner), 1))]
     far += [((move(x, grid.ends(shift)), 3),) for shift, x in zip(sides, picked[len(sides):])]
     both = [x for pair in zip(crossed, middle) for x in pair]
-    parts = stage(grid, grid.work_second, lists, turned, matrix, [*second, *both], parts, [far_head])
+    parts = stage(grid, grid.work_second, lists, turned, matrix, [*second, *both], parts, [far_head, *second_heads])
     first = exchange(parts)
     parts = stage(grid, grid.work_crossed, lists, turned, matrix, second_crossed, (), [parts[0]])
 

time: 121 us -> 130 us (1.074)
  the two profiles are of different devices: /device:TPU:1 before, /device:TPU:25 now
where the time goes in v8:
time: 130 us
  waiting for transfers between devices  66.1 us (51%)
  starting transfers between devices  39.2 us (30%)
  Pallas kernels  22 us (17%)
  local copies, waits for them, and re-layouts  2.3 us (2%)
    ppermute x17, waiting for transfers between devices, move(): return lax.ppermute(x, ('blk', 'rows'), perm) if perm else jnp.zeros_like(x)  60 us
    ppermute x17, starting transfers between devices, move(): return lax.ppermute(x, ('blk', 'rows'), perm) if perm else jnp.zeros_like(x)  28.4 us
    pallas_call x4, Pallas kernels, stage(): pl.pallas_call(functools.partial(stage_kernel, grid, plan, layout, carrie...  12 us
    ppermute x2, starting transfers between devices, exchange(): lax.ppermute(parts[1], 'rows', [(g, g + 1) for g in range(groups - 1)])  6.3 us
    ppermute x2, starting transfers between devices, exchange(): lax.ppermute(parts[2], 'rows', [(g + 1, g) for g in range(groups - 1)])  4.52 us
    ppermute x2, waiting for transfers between devices, exchange(): lax.ppermute(parts[2], 'rows', [(g + 1, g) for g in range(groups - 1)])  4.4 us
    pallas_call x4, Pallas kernels, pick(): pl.pallas_call(functools.partial(pick_kernel, grid, plan, layout, carry,...  4.31 us
    pallas_call x1, Pallas kernels, pack(): pl.pallas_call(functools.partial(pack_kernel, grid), grid=(1,), in_specs=...  2.64 us
  transfers between devices with their start and end apart: 21, of which 12 were waited for; matrix products, arithmetic and copies ran while one was open for 0% of the time, Pallas kernels for 11%

profile of v8, /device:TPU:25, one launch (start us, length us, event | category | flops | bytes accessed | tf_op | source)
XLA Modules:
  0.0 129.9 jit_solution(12173190778024839365)
XLA Ops:
  0.0 2.6 %pack_rows.1 = (bf16[4112,128]{1,0:T(8,128)(2,1)}, bf16[2048,128]{1,0:T(8,128)(2,1)}) custom-call(s32[3,1,16]{2,1,0:T(1,128)} %bitcast.30, s32[8,8]{1,0:T(8,128)} %bitcast.15, bf16[16,128,384]{2,1,0:T(8,128)(2,1)} %bitcast.29), custom_call_target="tpu_custom_call" | custom-call | flops 1024 | bytes 1024 | tf_op jit(solution)/shard_map/pack_rows/pallas_call | solution.py:141
  2.6 1.3 collective-permute-start
  3.9 4.1 %collective-permute-start.4 = (bf16[4112,128]{1,0:T(8,128)(2,1)}, bf16[4112,128]{1,0:T(8,128)(2,1)S(1)}, u32[]{:S(2)}, u32[]{:S(2)}) collective-permute-start(bf16[4112,128]{1,0:T(8,128)(2,1)} %get-tuple-element.26.head.refs_1_.refs_4_), channel_id=1, source_target_pairs={{8,0},{12,4},{16,8},{20,12},{24,16},{28,20},{9,1},{13,5},{17,9},{2... | collective-permute-start | bytes 3158024 | tf_op jit(solution)/shard_map/ppermute | solution.py:385
  8.0 0.0 copy-done.5
  8.0 1.3 %collective-permute-start.8 = (s32[8,8]{1,0:T(8,128)S(1)}, s32[8,8]{1,0:T(8,128)S(1)}, u32[]{:S(2)}, u32[]{:S(2)}) collective-permute-start(s32[8,8]{1,0:T(8,128)S(1)} %bitcast.16), channel_id=1, source_target_pairs={{4,0},{0,4},{12,8},{8,12},{20,16},{16,20},{28,24},{24,28},{5,1},{1... | collective-permute-start | bytes 776 | tf_op jit(solution)/shard_map/ppermute | solution.py:385
  9.3 1.5 %collective-permute-done.8.refs_0_ = s32[8,8]{1,0:T(8,128)S(1)} collective-permute-done((s32[8,8]{1,0:T(8,128)S(1)}, s32[8,8]{1,0:T(8,128)S(1)}, u32[]{:S(2)}, u32[]{:S(2)}) %collective-permute-start.8) | collective-permute-done | bytes 288 | tf_op jit(solution)/shard_map/ppermute | solution.py:385
  10.8 1.2 copy-done.1
  12.1 1.0 copy-done.3
  13.1 0.7 pick_rows.4
  13.8 0.0 copy-start.2
  13.8 0.0 copy-start.4
  13.8 1.3 %collective-permute-start.9 = (bf16[3072,128]{1,0:T(8,128)(2,1)S(1)}, bf16[3072,128]{1,0:T(8,128)(2,1)S(1)}, u32[]{:S(2)}, u32[]{:S(2)}) collective-permute-start(bf16[3072,128]{1,0:T(8,128)(2,1)S(1)} %pick_rows.4), channel_id=1, source_target_pairs={{0,4},{4,0},{8,12},{12,8},{16,20},{20,16},{24,28},{28,24},{1,5},{5... | collective-permute-start | bytes 2359304 | tf_op jit(solution)/shard_map/ppermute | solution.py:385
  15.1 1.3 collective-permute-start.2
  16.4 4.0 %collective-permute-start.6 = (bf16[2048,128]{1,0:T(8,128)(2,1)S(1)}, bf16[2048,128]{1,0:T(8,128)(2,1)S(1)}, u32[]{:S(2)}, u32[]{:S(2)}) collective-permute-start(bf16[2048,128]{1,0:T(8,128)(2,1)S(1)} %copy-done.3), channel_id=1, source_target_pairs={{9,1},{13,5},{17,9},{21,13},{25,17},{29,21},{10,2},{14,6},{18,10},... | collective-permute-start | bytes 1572872 | tf_op jit(solution)/shard_map/ppermute | solution.py:385
  20.4 8.4 %collective-permute-done.refs_1_.refs_0_.refs_3_.refs_7_ = bf16[4112,128]{1,0:T(8,128)(2,1)S(1)} collective-permute-done((bf16[4112,128]{1,0:T(8,128)(2,1)}, bf16[4112,128]{1,0:T(8,128)(2,1)S(1)}, u32[]{:S(2)}, u32[]{:S(2)}) %collective-permute-start) | collective-permute-done | bytes 1052704 | tf_op jit(solution)/shard_map/ppermute | solution.py:385
  28.9 1.3 collective-permute-start.1
  30.2 0.0 collective-permute-done.4.refs_3_.refs_2_.refs_4_.refs_8_
  30.2 0.7 collective-permute-start.5
  30.9 4.4 %collective-permute-done.2.refs_2_.refs_1_ = bf16[2048,128]{1,0:T(8,128)(2,1)S(1)} collective-permute-done((bf16[2048,128]{1,0:T(8,128)(2,1)S(1)}, bf16[2048,128]{1,0:T(8,128)(2,1)S(1)}, u32[]{:S(2)}, u32[]{:S(2)}) %collective-permute-start.2) | collective-permute-done | bytes 524320 | tf_op jit(solution)/shard_map/ppermute | solution.py:385
  35.3 1.5 %collective-permute-done.6.refs_4_.refs_3_ = bf16[2048,128]{1,0:T(8,128)(2,1)S(1)} collective-permute-done((bf16[2048,128]{1,0:T(8,128)(2,1)S(1)}, bf16[2048,128]{1,0:T(8,128)(2,1)S(1)}, u32[]{:S(2)}, u32[]{:S(2)}) %collective-permute-start.6) | collective-permute-done | bytes 524320 | tf_op jit(solution)/shard_map/ppermute | solution.py:385
  36.8 0.0 collective-permute-done.9.refs_5_.refs_6_
  36.8 0.7 pick_rows.5
  37.5 0.0 copy-start
  37.5 0.0 copy-start.6
  37.6 0.0 copy-start.7
  37.6 1.3 %collective-permute-start.10 = (bf16[3088,128]{1,0:T(8,128)(2,1)S(1)}, bf16[3088,128]{1,0:T(8,128)(2,1)S(1)}, u32[]{:S(2)}, u32[]{:S(2)}) collective-permute-start(bf16[3088,128]{1,0:T(8,128)(2,1)S(1)} %get-tuple-element.28), channel_id=1, source_target_pairs={{0,4},{4,0},{8,12},{12,8},{16,20},{20,16},{24,28},{28,24},{1,5},{5... | collective-permute-start | bytes 2371592 | tf_op jit(solution)/shard_map/ppermute | solution.py:385
  38.9 1.3 collective-permute-start.3
  40.2 0.7 collective-permute-start.7
  40.9 0.0 copy-done.2
  40.9 0.0 copy-done.4
  40.9 0.5 turn_rows.1.turned
  41.3 0.0 copy-done
  41.4 5.9 %stage_products.4 = (bf16[4,3,128,128]{3,2,1,0:T(8,128)(2,1)S(1)}, bf16[4,3,128,128]{3,2,1,0:T(8,128)(2,1)S(1)}, bf16[4,3,128,128]{3,2,1,0:T(8,128)(2,1)S(1)}) custom-call(s32[8,8]{1,0:T(8,128)S(1)} %bitcast.21, s32[8,8]{1,0:T(8,128)S(1)} %bitcast.17, s32[1,8]{1,0:T(1,128)S(1)} %bitcast.25, bf16[16,384,128]{2,1,0:T(8,128)(2,1)S(1)} %turn_rows.1.turned, ...), custom_call_target="tpu_custom_call" | custom-call | flops 1024 | bytes 1024 | tf_op jit(solution)/shard_map/stage_products/pallas_call | solution.py:315
  47.2 9.9 %collective-permute-done.1.refs_1_.refs_0_ = bf16[4112,128]{1,0:T(8,128)(2,1)S(1)} collective-permute-done((bf16[4112,128]{1,0:T(8,128)(2,1)S(1)}, bf16[4112,128]{1,0:T(8,128)(2,1)S(1)}, u32[]{:S(2)}, u32[]{:S(2)}) %collective-permute-start.1) | collective-permute-done | bytes 1052704 | tf_op jit(solution)/shard_map/ppermute | solution.py:385
  57.2 0.7 collective-permute-start.11
  57.9 0.0 collective-permute-done.5.refs_2_.refs_3_
  57.9 1.4 %pick_rows.6 = (bf16[2048,128]{1,0:T(8,128)(2,1)S(1)}, bf16[2048,128]{1,0:T(8,128)(2,1)S(1)}) custom-call(s32[8,8]{1,0:T(8,128)S(1)} %collective-permute-done.8.refs_0_, bf16[4112,128]{1,0:T(8,128)(2,1)S(1)} %collective-permute-done.1.refs_1_.refs_0_, bf16[4112,128]{1,0:T(8,128)(2,1)S(1)} %collective-permute-done.5.refs_2_.refs_3_, ...), custom_call_target="tpu_custom_call" | custom-call | flops 1024 | bytes 1024 | tf_op jit(solution)/shard_map/pick_rows/pallas_call | solution.py:237
  59.3 1.3 collective-permute-start.12
  60.6 2.9 %collective-permute-done.3.refs_1_.refs_2_.refs_5_ = bf16[2048,128]{1,0:T(8,128)(2,1)S(1)} collective-permute-done((bf16[2048,128]{1,0:T(8,128)(2,1)S(1)}, bf16[2048,128]{1,0:T(8,128)(2,1)S(1)}, u32[]{:S(2)}, u32[]{:S(2)}) %collective-permute-start.3) | collective-permute-done | bytes 524320 | tf_op jit(solution)/shard_map/ppermute | solution.py:385
  63.5 1.2 collective-permute-start.13
  64.8 0.0 collective-permute-done.7.refs_3_.refs_4_.refs_6_
  64.8 0.0 collective-permute-done.10.refs_4_.refs_9_
  64.8 1.5 %pick_rows.7 = (bf16[1024,128]{1,0:T(8,128)(2,1)S(1)}, bf16[3072,128]{1,0:T(8,128)(2,1)S(1)}, bf16[1024,128]{1,0:T(8,128)(2,1)S(1)}) custom-call(s32[8,8]{1,0:T(8,128)S(1)} %collective-permute-done.8.refs_0_, bf16[4112,128]{1,0:T(8,128)(2,1)S(1)} %collective-permute-done.1.refs_1_.refs_0_, ...), custom_call_target="tpu_custom_call" | custom-call | flops 20000000000 | bytes 1024 | tf_op jit(solution)/shard_map/pick_rows/pallas_call | solution.py:237
  66.3 1.3 collective-permute-start.17
  67.6 0.0 collective-permute-done.11.refs_5_
  67.6 5.0 %collective-permute-done.12.refs_9_.refs_0_ = bf16[2048,128]{1,0:T(8,128)(2,1)S(1)} collective-permute-done((bf16[2048,128]{1,0:T(8,128)(2,1)S(1)}, bf16[2048,128]{1,0:T(8,128)(2,1)S(1)}, u32[]{:S(2)}, u32[]{:S(2)}) %collective-permute-start.12) | collective-permute-done | bytes 524320 | tf_op jit(solution)/shard_map/ppermute | solution.py:385
  72.6 21.6 %collective-permute-done.13.refs_10_.refs_0_ = bf16[2048,128]{1,0:T(8,128)(2,1)S(1)} collective-permute-done((bf16[2048,128]{1,0:T(8,128)(2,1)S(1)}, bf16[2048,128]{1,0:T(8,128)(2,1)S(1)}, u32[]{:S(2)}, u32[]{:S(2)}) %collective-permute-start.13) | collective-permute-done | bytes 524320 | tf_op jit(solution)/shard_map/ppermute | solution.py:385
  94.2 2.8 %stage_products.5 = (bf16[7,3,128,128]{3,2,1,0:T(8,128)(2,1)S(1)}, bf16[7,3,128,128]{3,2,1,0:T(8,128)(2,1)S(1)}, bf16[7,3,128,128]{3,2,1,0:T(8,128)(2,1)S(1)}) custom-call(s32[8,8]{1,0:T(8,128)S(1)} %bitcast.22, s32[8,8]{1,0:T(8,128)S(1)} %bitcast.18, s32[1,8]{1,0:T(1,128)S(1)} %bitcast.26, bf16[16,384,128]{2,1,0:T(8,128)(2,1)S(1)} %turn_rows.1.turned, ...), custom_call_target="tpu_custom_call" | custom-call | flops 1024 | bytes 1024 | tf_op jit(solution)/shard_map/stage_products/pallas_call | solution.py:315
  97.1 1.9 %collective-permute-start.14 = (bf16[7,3,128,128]{3,2,1,0:T(8,128)(2,1)S(1)}, bf16[7,3,128,128]{3,2,1,0:T(8,128)(2,1)S(1)}, u32[]{:S(2)}, u32[]{:S(2)}) collective-permute-start(bf16[7,3,128,128]{3,2,1,0:T(8,128)(2,1)S(1)} %get-tuple-element.36), channel_id=1, source_target_pairs={{0,1},{1,2},{2,3},{4,5},{5,6},{6,7},{8,9},{9,10},{10,11},{12,13},{... | collective-permute-start | bytes 2064392 | tf_op jit(solution)/shard_map/ppermute | solution.py:394
  99.0 2.6 %collective-permute-start.15 = (bf16[7,3,128,128]{3,2,1,0:T(8,128)(2,1)S(1)}, bf16[7,3,128,128]{3,2,1,0:T(8,128)(2,1)S(1)}, u32[]{:S(2)}, u32[]{:S(2)}) collective-permute-start(bf16[7,3,128,128]{3,2,1,0:T(8,128)(2,1)S(1)} %get-tuple-element.37), channel_id=1, source_target_pairs={{1,0},{2,1},{3,2},{5,4},{6,5},{7,6},{9,8},{10,9},{11,10},{13,12},{... | collective-permute-start | bytes 2064392 | tf_op jit(solution)/shard_map/ppermute | solution.py:395
  101.6 4.0 %collective-permute-start.18 = (bf16[1024,128]{1,0:T(8,128)(2,1)S(1)}, bf16[1024,128]{1,0:T(8,128)(2,1)S(1)}, u32[]{:S(2)}, u32[]{:S(2)}) collective-permute-start(bf16[1024,128]{1,0:T(8,128)(2,1)S(1)} %get-tuple-element.40), channel_id=1, source_target_pairs={{1,5},{5,1},{9,13},{13,9},{17,21},{21,17},{25,29},{29,25},{2,6},{6... | collective-permute-start | bytes 786440 | tf_op jit(solution)/shard_map/ppermute | solution.py:385
  105.7 1.3 collective-permute-start.16
  107.0 2.4 %collective-permute-done.18.refs_1_ = bf16[1024,128]{1,0:T(8,128)(2,1)S(1)} collective-permute-done((bf16[1024,128]{1,0:T(8,128)(2,1)S(1)}, bf16[1024,128]{1,0:T(8,128)(2,1)S(1)}, u32[]{:S(2)}, u32[]{:S(2)}) %collective-permute-start.18) | collective-permute-done | bytes 262176 | tf_op jit(solution)/shard_map/ppermute | solution.py:385
  109.4 1.2 stage_products.6
  110.6 2.2 %collective-permute-done.16.refs_1_ = bf16[1024,128]{1,0:T(8,128)(2,1)S(1)} collective-permute-done((bf16[1024,128]{1,0:T(8,128)(2,1)S(1)}, bf16[1024,128]{1,0:T(8,128)(2,1)S(1)}, u32[]{:S(2)}, u32[]{:S(2)}) %collective-permute-start.16) | collective-permute-done | bytes 262176 | tf_op jit(solution)/shard_map/ppermute | solution.py:385
  112.8 0.0 collective-permute-done.17.refs_2_
  112.8 0.0 collective-permute-done.14.refs_6_.refs_1_
  112.8 0.0 collective-permute-done.15.refs_7_.refs_2_
  112.8 2.1 %stage_products.7 = (bf16[3,3,128,128]{3,2,1,0:T(8,128)(2,1)S(1)}, bf16[3,3,128,128]{3,2,1,0:T(8,128)(2,1)S(1)}, bf16[3,3,128,128]{3,2,1,0:T(8,128)(2,1)S(1)}) custom-call(s32[8,8]{1,0:T(8,128)S(1)} %bitcast.24, s32[8,8]{1,0:T(8,128)S(1)} %bitcast.20, s32[1,8]{1,0:T(1,128)S(1)} %bitcast.28, bf16[16,384,128]{2,1,0:T(8,128)(2,1)S(1)} %turn_rows.1.turned, ...), custom_call_target="tpu_custom_call" | custom-call | flops 1024 | bytes 1024 | tf_op jit(solution)/shard_map/stage_products/pallas_call | solution.py:315
  114.9 4.4 %collective-permute-start.19 = (bf16[3,3,128,128]{3,2,1,0:T(8,128)(2,1)S(1)}, bf16[3,3,128,128]{3,2,1,0:T(8,128)(2,1)S(1)}, u32[]{:S(2)}, u32[]{:S(2)}) collective-permute-start(bf16[3,3,128,128]{3,2,1,0:T(8,128)(2,1)S(1)} %get-tuple-element.45), channel_id=1, source_target_pairs={{0,1},{1,2},{2,3},{4,5},{5,6},{6,7},{8,9},{9,10},{10,11},{12,13},{... | collective-permute-start | bytes 884744 | tf_op jit(solution)/shard_map/ppermute | solution.py:394
  119.3 1.9 %collective-permute-start.20 = (bf16[3,3,128,128]{3,2,1,0:T(8,128)(2,1)S(1)}, bf16[3,3,128,128]{3,2,1,0:T(8,128)(2,1)S(1)}, u32[]{:S(2)}, u32[]{:S(2)}) collective-permute-start(bf16[3,3,128,128]{3,2,1,0:T(8,128)(2,1)S(1)} %get-tuple-element.46), channel_id=1, source_target_pairs={{1,0},{2,1},{3,2},{5,4},{6,5},{7,6},{9,8},{10,9},{11,10},{13,12},{... | collective-permute-start | bytes 884744 | tf_op jit(solution)/shard_map/ppermute | solution.py:395
  121.2 1.7 %collective-permute-done.19.refs_4_ = bf16[3,3,128,128]{3,2,1,0:T(8,128)(2,1)S(1)} collective-permute-done((bf16[3,3,128,128]{3,2,1,0:T(8,128)(2,1)S(1)}, bf16[3,3,128,128]{3,2,1,0:T(8,128)(2,1)S(1)}, u32[]{:S(2)}, u32[]{:S(2)}) %collective-permute-start.19) | collective-permute-done | bytes 294944 | tf_op jit(solution)/shard_map/ppermute | solution.py:394
  123.0 4.4 %collective-permute-done.20.refs_5_ = bf16[3,3,128,128]{3,2,1,0:T(8,128)(2,1)S(1)} collective-permute-done((bf16[3,3,128,128]{3,2,1,0:T(8,128)(2,1)S(1)}, bf16[3,3,128,128]{3,2,1,0:T(8,128)(2,1)S(1)}, u32[]{:S(2)}, u32[]{:S(2)}) %collective-permute-start.20) | collective-permute-done | bytes 294944 | tf_op jit(solution)/shard_map/ppermute | solution.py:395
  127.4 2.6 %assemble_coarse.1 = f32[5120,128]{1,0:T(8,128)} custom-call(bf16[7,3,128,128]{3,2,1,0:T(8,128)(2,1)S(1)} %get-tuple-element.35.refs_2_.refs_0_, bf16[7,3,128,128]{3,2,1,0:T(8,128)(2,1)S(1)} %collective-permute-done.14.refs_6_.refs_1_, bf16[7,3,128,128]{3,2,1,0:T(8,128)(2,1)S(1)} %collective-permute-done.15.refs_7_.refs_2_, ...), custom_call_target="tpu_custom_call" | custom-call | flops 1024 | bytes 1024 | tf_op jit(solution)/shard_map/assemble_coarse/pallas_call | solution.py:361
  (5 shorter events, 0.0 us)
Async XLA Ops:
  0.0 8.0 %copy-start.5 = (s32[1,1,8,8]{3,2,1,0:T(8,128)S(1)}, s32[1,1,8,8]{3,2,1,0:T(8,128)}, u32[]{:S(2)}) copy-start(s32[1,1,8,8]{3,2,1,0:T(8,128)} %param.8) | copy-start | bytes 772
  2.6 26.2 %collective-permute-start = (bf16[4112,128]{1,0:T(8,128)(2,1)}, bf16[4112,128]{1,0:T(8,128)(2,1)S(1)}, u32[]{:S(2)}, u32[]{:S(2)}) collective-permute-start(bf16[4112,128]{1,0:T(8,128)(2,1)} %get-tuple-element.26.head.refs_1_.refs_4_), channel_id=1, source_target_pairs={{0,8},{4,12},{8,16},{12,20},{16,24},{20,28},{1,9},{5,13},{9,17},{1... | collective-permute-start | bytes 3158024 | tf_op jit(solution)/shard_map/ppermute | solution.py:385
  3.9 26.2 %collective-permute-start.4 = (bf16[4112,128]{1,0:T(8,128)(2,1)}, bf16[4112,128]{1,0:T(8,128)(2,1)S(1)}, u32[]{:S(2)}, u32[]{:S(2)}) collective-permute-start(bf16[4112,128]{1,0:T(8,128)(2,1)} %get-tuple-element.26.head.refs_1_.refs_4_), channel_id=1, source_target_pairs={{8,0},{12,4},{16,8},{20,12},{24,16},{28,20},{9,1},{13,5},{17,9},{2... | collective-permute-start | bytes 3158024 | tf_op jit(solution)/shard_map/ppermute | solution.py:385
  8.0 2.8 %collective-permute-start.8 = (s32[8,8]{1,0:T(8,128)S(1)}, s32[8,8]{1,0:T(8,128)S(1)}, u32[]{:S(2)}, u32[]{:S(2)}) collective-permute-start(s32[8,8]{1,0:T(8,128)S(1)} %bitcast.16), channel_id=1, source_target_pairs={{4,0},{0,4},{12,8},{8,12},{20,16},{16,20},{28,24},{24,28},{5,1},{1... | collective-permute-start | bytes 776 | tf_op jit(solution)/shard_map/ppermute | solution.py:385
  10.8 1.2 copy-start.1
  12.1 1.0 copy-start.3
  13.8 27.1 %copy-start.2 = (bf16[4112,128]{1,0:T(8,128)(2,1)S(1)}, bf16[4112,128]{1,0:T(8,128)(2,1)}, u32[]{:S(2)}) copy-start(bf16[4112,128]{1,0:T(8,128)(2,1)} %get-tuple-element.26.head.refs_1_.refs_4_) | copy-start | bytes 3158020
  13.8 27.1 %copy-start.4 = (bf16[2048,128]{1,0:T(8,128)(2,1)S(1)}, bf16[2048,128]{1,0:T(8,128)(2,1)}, u32[]{:S(2)}) copy-start(bf16[2048,128]{1,0:T(8,128)(2,1)} %get-tuple-element.27.tail.refs_2_.refs_5_) | copy-start | bytes 1572868
  13.8 23.0 %collective-permute-start.9 = (bf16[3072,128]{1,0:T(8,128)(2,1)S(1)}, bf16[3072,128]{1,0:T(8,128)(2,1)S(1)}, u32[]{:S(2)}, u32[]{:S(2)}) collective-permute-start(bf16[3072,128]{1,0:T(8,128)(2,1)S(1)} %pick_rows.4), channel_id=1, source_target_pairs={{0,4},{4,0},{8,12},{12,8},{16,20},{20,16},{24,28},{28,24},{1,5},{5... | collective-permute-start | bytes 2359304 | tf_op jit(solution)/shard_map/ppermute | solution.py:385
  15.1 20.2 %collective-permute-start.2 = (bf16[2048,128]{1,0:T(8,128)(2,1)S(1)}, bf16[2048,128]{1,0:T(8,128)(2,1)S(1)}, u32[]{:S(2)}, u32[]{:S(2)}) collective-permute-start(bf16[2048,128]{1,0:T(8,128)(2,1)S(1)} %copy-done.3), channel_id=1, source_target_pairs={{1,9},{5,13},{9,17},{13,21},{17,25},{21,29},{2,10},{6,14},{10,18},... | collective-permute-start | bytes 1572872 | tf_op jit(solution)/shard_map/ppermute | solution.py:385
  16.4 20.4 %collective-permute-start.6 = (bf16[2048,128]{1,0:T(8,128)(2,1)S(1)}, bf16[2048,128]{1,0:T(8,128)(2,1)S(1)}, u32[]{:S(2)}, u32[]{:S(2)}) collective-permute-start(bf16[2048,128]{1,0:T(8,128)(2,1)S(1)} %copy-done.3), channel_id=1, source_target_pairs={{9,1},{13,5},{17,9},{21,13},{25,17},{29,21},{10,2},{14,6},{18,10},... | collective-permute-start | bytes 1572872 | tf_op jit(solution)/shard_map/ppermute | solution.py:385
  28.9 28.3 %collective-permute-start.1 = (bf16[4112,128]{1,0:T(8,128)(2,1)S(1)}, bf16[4112,128]{1,0:T(8,128)(2,1)S(1)}, u32[]{:S(2)}, u32[]{:S(2)}) collective-permute-start(bf16[4112,128]{1,0:T(8,128)(2,1)S(1)} %collective-permute-done.refs_1_.refs_0_.refs_3_.refs_7_), channel_id=1, source_target_pairs={{8,16},{12,20},{16,24},{20,28},{9,17},{13,21},{17,25},{21,29},{10,... | collective-permute-start | bytes 3158024 | tf_op jit(solution)/shard_map/ppermute | solution.py:385
  30.2 27.7 %collective-permute-start.5 = (bf16[4112,128]{1,0:T(8,128)(2,1)S(1)}, bf16[4112,128]{1,0:T(8,128)(2,1)S(1)}, u32[]{:S(2)}, u32[]{:S(2)}) collective-permute-start(bf16[4112,128]{1,0:T(8,128)(2,1)S(1)} %collective-permute-done.4.refs_3_.refs_2_.refs_4_.refs_8_), channel_id=1, source_target_pairs={{8,0},{12,4},{16,8},{20,12},{9,1},{13,5},{17,9},{21,13},{10,2},{14... | collective-permute-start | bytes 3158024 | tf_op jit(solution)/shard_map/ppermute | solution.py:385
  37.5 3.8 %copy-start = (bf16[1,1,8,8,128,128]{5,4,3,2,1,0:T(8,128)(2,1)S(1)}, bf16[1,1,8,8,128,128]{5,4,3,2,1,0:T(8,128)(2,1)}, u32[]{:S(2)}) copy-start(bf16[1,1,8,8,128,128]{5,4,3,2,1,0:T(8,128)(2,1)} %param.6) | copy-start | bytes 6291460
  37.5 3.8 %copy-start.6 = (s32[1,1,8,8]{3,2,1,0:T(8,128)S(1)}, s32[1,1,8,8]{3,2,1,0:T(8,128)}, u32[]{:S(2)}) copy-start(s32[1,1,8,8]{3,2,1,0:T(8,128)} %param.7) | copy-start | bytes 772
  37.6 3.8 %copy-start.7 = (s32[1,1,8]{2,1,0:T(1,128)S(1)}, s32[1,1,8]{2,1,0:T(1,128)}, u32[]{:S(2)}) copy-start(s32[1,1,8]{2,1,0:T(1,128)} %param.9) | copy-start | bytes 100
  37.6 27.2 %collective-permute-start.10 = (bf16[3088,128]{1,0:T(8,128)(2,1)S(1)}, bf16[3088,128]{1,0:T(8,128)(2,1)S(1)}, u32[]{:S(2)}, u32[]{:S(2)}) collective-permute-start(bf16[3088,128]{1,0:T(8,128)(2,1)S(1)} %get-tuple-element.28), channel_id=1, source_target_pairs={{0,4},{4,0},{8,12},{12,8},{16,20},{20,16},{24,28},{28,24},{1,5},{5... | collective-permute-start | bytes 2371592 | tf_op jit(solution)/shard_map/ppermute | solution.py:385
  38.9 24.6 %collective-permute-start.3 = (bf16[2048,128]{1,0:T(8,128)(2,1)S(1)}, bf16[2048,128]{1,0:T(8,128)(2,1)S(1)}, u32[]{:S(2)}, u32[]{:S(2)}) collective-permute-start(bf16[2048,128]{1,0:T(8,128)(2,1)S(1)} %collective-permute-done.2.refs_2_.refs_1_), channel_id=1, source_target_pairs={{9,17},{13,21},{17,25},{21,29},{10,18},{14,22},{18,26},{22,30}} | collective-permute-start | bytes 1572872 | tf_op jit(solution)/shard_map/ppermute | solution.py:385
  40.2 24.6 %collective-permute-start.7 = (bf16[2048,128]{1,0:T(8,128)(2,1)S(1)}, bf16[2048,128]{1,0:T(8,128)(2,1)S(1)}, u32[]{:S(2)}, u32[]{:S(2)}) collective-permute-start(bf16[2048,128]{1,0:T(8,128)(2,1)S(1)} %collective-permute-done.6.refs_4_.refs_3_), channel_id=1, source_target_pairs={{9,1},{13,5},{17,9},{21,13},{10,2},{14,6},{18,10},{22,14}} | collective-permute-start | bytes 1572872 | tf_op jit(solution)/shard_map/ppermute | solution.py:385
  57.2 10.5 %collective-permute-start.11 = (bf16[3072,128]{1,0:T(8,128)(2,1)S(1)}, bf16[3072,128]{1,0:T(8,128)(2,1)S(1)}, u32[]{:S(2)}, u32[]{:S(2)}) collective-permute-start(bf16[3072,128]{1,0:T(8,128)(2,1)S(1)} %get-tuple-element.29), channel_id=1, source_target_pairs={{8,12},{12,8},{16,20},{20,16},{9,13},{13,9},{17,21},{21,17},{10,14... | collective-permute-start | bytes 2359304 | tf_op jit(solution)/shard_map/ppermute | solution.py:385
  59.3 13.4 %collective-permute-start.12 = (bf16[2048,128]{1,0:T(8,128)(2,1)S(1)}, bf16[2048,128]{1,0:T(8,128)(2,1)S(1)}, u32[]{:S(2)}, u32[]{:S(2)}) collective-permute-start(bf16[2048,128]{1,0:T(8,128)(2,1)S(1)} %get-tuple-element.33), channel_id=1, source_target_pairs={{8,0},{12,4},{16,24},{20,28},{9,1},{13,5},{17,25},{21,29},{10,2},{... | collective-permute-start | bytes 1572872 | tf_op jit(solution)/shard_map/ppermute | solution.py:385
  63.5 30.7 %collective-permute-start.13 = (bf16[2048,128]{1,0:T(8,128)(2,1)S(1)}, bf16[2048,128]{1,0:T(8,128)(2,1)S(1)}, u32[]{:S(2)}, u32[]{:S(2)}) collective-permute-start(bf16[2048,128]{1,0:T(8,128)(2,1)S(1)} %get-tuple-element.34), channel_id=1, source_target_pairs={{0,4},{4,0},{8,12},{12,8},{16,20},{20,16},{24,28},{28,24},{1,5},{5... | collective-permute-start | bytes 1572872 | tf_op jit(solution)/shard_map/ppermute | solution.py:385
  66.3 46.5 %collective-permute-start.17 = (bf16[3072,128]{1,0:T(8,128)(2,1)S(1)}, bf16[3072,128]{1,0:T(8,128)(2,1)S(1)}, u32[]{:S(2)}, u32[]{:S(2)}) collective-permute-start(bf16[3072,128]{1,0:T(8,128)(2,1)S(1)} %get-tuple-element.39), channel_id=1, source_target_pairs={{8,4},{12,0},{16,28},{20,24},{9,5},{13,1},{17,29},{21,25},{10,6},{... | collective-permute-start | bytes 2359304 | tf_op jit(solution)/shard_map/ppermute | solution.py:385
  97.1 15.7 %collective-permute-start.14 = (bf16[7,3,128,128]{3,2,1,0:T(8,128)(2,1)S(1)}, bf16[7,3,128,128]{3,2,1,0:T(8,128)(2,1)S(1)}, u32[]{:S(2)}, u32[]{:S(2)}) collective-permute-start(bf16[7,3,128,128]{3,2,1,0:T(8,128)(2,1)S(1)} %get-tuple-element.36), channel_id=1, source_target_pairs={{0,1},{1,2},{2,3},{4,5},{5,6},{6,7},{8,9},{9,10},{10,11},{12,13},{... | collective-permute-start | bytes 2064392 | tf_op jit(solution)/shard_map/ppermute | solution.py:394
  99.0 13.8 %collective-permute-start.15 = (bf16[7,3,128,128]{3,2,1,0:T(8,128)(2,1)S(1)}, bf16[7,3,128,128]{3,2,1,0:T(8,128)(2,1)S(1)}, u32[]{:S(2)}, u32[]{:S(2)}) collective-permute-start(bf16[7,3,128,128]{3,2,1,0:T(8,128)(2,1)S(1)} %get-tuple-element.37), channel_id=1, source_target_pairs={{1,0},{2,1},{3,2},{5,4},{6,5},{7,6},{9,8},{10,9},{11,10},{13,12},{... | collective-permute-start | bytes 2064392 | tf_op jit(solution)/shard_map/ppermute | solution.py:395
  101.6 7.8 %collective-permute-start.18 = (bf16[1024,128]{1,0:T(8,128)(2,1)S(1)}, bf16[1024,128]{1,0:T(8,128)(2,1)S(1)}, u32[]{:S(2)}, u32[]{:S(2)}) collective-permute-start(bf16[1024,128]{1,0:T(8,128)(2,1)S(1)} %get-tuple-element.40), channel_id=1, source_target_pairs={{1,5},{5,1},{9,13},{13,9},{17,21},{21,17},{25,29},{29,25},{2,6},{6... | collective-permute-start | bytes 786440 | tf_op jit(solution)/shard_map/ppermute | solution.py:385
  105.7 7.1 %collective-permute-start.16 = (bf16[1024,128]{1,0:T(8,128)(2,1)S(1)}, bf16[1024,128]{1,0:T(8,128)(2,1)S(1)}, u32[]{:S(2)}, u32[]{:S(2)}) collective-permute-start(bf16[1024,128]{1,0:T(8,128)(2,1)S(1)} %get-tuple-element.38), channel_id=1, source_target_pairs={{9,1},{13,5},{17,25},{21,29},{10,2},{14,6},{18,26},{22,30}} | collective-permute-start | bytes 786440 | tf_op jit(solution)/shard_map/ppermute | solution.py:385
  114.9 8.0 %collective-permute-start.19 = (bf16[3,3,128,128]{3,2,1,0:T(8,128)(2,1)S(1)}, bf16[3,3,128,128]{3,2,1,0:T(8,128)(2,1)S(1)}, u32[]{:S(2)}, u32[]{:S(2)}) collective-permute-start(bf16[3,3,128,128]{3,2,1,0:T(8,128)(2,1)S(1)} %get-tuple-element.45), channel_id=1, source_target_pairs={{0,1},{1,2},{2,3},{4,5},{5,6},{6,7},{8,9},{9,10},{10,11},{12,13},{... | collective-permute-start | bytes 884744 | tf_op jit(solution)/shard_map/ppermute | solution.py:394
  119.3 8.0 %collective-permute-start.20 = (bf16[3,3,128,128]{3,2,1,0:T(8,128)(2,1)S(1)}, bf16[3,3,128,128]{3,2,1,0:T(8,128)(2,1)S(1)}, u32[]{:S(2)}, u32[]{:S(2)}) collective-permute-start(bf16[3,3,128,128]{3,2,1,0:T(8,128)(2,1)S(1)} %get-tuple-element.46), channel_id=1, source_target_pairs={{1,0},{2,1},{3,2},{5,4},{6,5},{7,6},{9,8},{10,9},{11,10},{13,12},{... | collective-permute-start | bytes 884744 | tf_op jit(solution)/shard_map/ppermute | solution.py:395

commit v9 on v8

v9 whole, which is shorter than its diff:
```python
import functools
import jax
import jax.numpy as jnp
from jax import lax
from jax.experimental import pallas as pl
from jax.experimental.pallas import tpu as pltpu
from jax.sharding import PartitionSpec as P

VMEM_LIMIT = 24 * 1024 * 1024
PACK_VMEM_LIMIT = 60 * 1024 * 1024
PARAMS = pltpu.CompilerParams(vmem_limit_bytes=VMEM_LIMIT)
COST = pl.CostEstimate(flops=1024, bytes_accessed=1024, transcendentals=0)
EARLY_COST = pl.CostEstimate(flops=1024, bytes_accessed=1024, transcendentals=0)
FAR_COST = pl.CostEstimate(flops=1024, bytes_accessed=1024, transcendentals=0)
NEAR_COST = pl.CostEstimate(flops=6 * 10 ** 9, bytes_accessed=1024, transcendentals=0)
PICK_COST = pl.CostEstimate(flops=2 * 10 ** 10, bytes_accessed=1024, transcendentals=0)
ANYWHERE = pl.BlockSpec(memory_space=pl.ANY)


def resident(x):
    return pl.BlockSpec(x.shape, lambda i, *_, n=len(x.shape): (0,) * n)


LINES = 4


class Grid:
    def __init__(self, panels, cap, pores):
        self.panels, self.cap, self.pores = panels, cap, pores
        self.columns = panels // LINES
        self.sides = range(1, self.columns)
        self.list_rows = -(-panels // 16) * 16

    def spot(self):
        place = lax.axis_index("blk")
        return place // self.columns, place % self.columns

    def lines(self, z):
        upper = z >= 2
        return jnp.where(z % 2 == 1, z - 1, z + 1), jnp.where(upper, 1, 2), jnp.where(upper, 0, 3)

    def middle(self, z):
        return (z == 1) | (z == 2)

    def panel(self, line, y, shift):
        column = y - shift
        return line * self.columns + jnp.where(column < 0, column + self.columns, column)

    def swaps(self, lines):
        return [(h * self.columns + c, k * self.columns + c)
                for h, k in (*lines, *[(k, h) for h, k in lines]) for c in range(self.columns)]

    def across(self, shift, lines=range(LINES)):
        return [(h * self.columns + c, h * self.columns + (c + shift) % self.columns)
                for h in lines for c in range(self.columns)]

    def ends(self, shift):
        return [(h * self.columns + c, end * self.columns + (c + shift) % self.columns)
                for h, end in ((1, 0), (2, 3)) for c in range(self.columns)]

    def part(self, ref, blocks, row, block):
        start = (row * blocks + block) * self.pores
        if not isinstance(start, int):
            start = pl.multiple_of(start, self.pores)
        return ref.at[pl.ds(start, self.pores), :]

    def shape(self, rows, blocks, width, lists=0):
        return jax.ShapeDtypeStruct((rows * blocks * self.pores + lists * self.list_rows, width), jnp.bfloat16)


    def work_near(self, z, y):
        half, _, _ = self.lines(z)
        return ([(self.panel(z, y, 0), [(0, True, True)]), (self.panel(half, y, 0), [(1, True, True)])] +
                [(self.panel(z, y, shift), [(1 + shift, False, True)]) for shift in self.sides])

    def work_middle(self, z, y):
        _, other, _ = self.lines(z)
        middle = self.middle(z)
        end = jnp.logical_not(middle)
        return ([(self.panel(other, y, 0), [(0, True, middle), (1, False, end)])] +
                [(self.panel(other, y, shift), [(2 * shift, False, middle), (2 * shift + 1, False, end)])
                 for shift in self.sides])

    def work_far(self, z, y):
        half, _, far = self.lines(z)
        middle = self.middle(z)
        end = jnp.logical_not(middle)
        work = [(self.panel(far, y, 0), [(0, True, middle), (1, False, end)])]
        for i, shift in enumerate(self.sides):
            work += [(self.panel(half, y, shift), [(2 + 3 * i, False, True)]),
                     (self.panel(far, y, shift), [(3 + 3 * i, False, middle), (4 + 3 * i, False, end)])]
        return work


def pack_kernel(grid, mask_from, cols_from, prolong_from, head, tail, mask, cols, prolong, done):
    group, groups = lax.axis_index("rows"), lax.axis_size("rows")
    width = tail.shape[-1]
    rows = prolong.shape[0]
    step = rows // 4 if rows % 4 == 0 else rows
    copies = [pltpu.make_async_copy(mask_from, mask, done.at[0]), pltpu.make_async_copy(cols_from, cols, done.at[1])]
    for index in range(rows // step):
        some = pl.ds(index * step, step)
        copies.append(pltpu.make_async_copy(prolong_from.at[some], prolong.at[some], done.at[2 + index]))
    for copy in copies:
        copy.start()
    copies[0].wait()
    copies[1].wait()
    for i in range(rows):
        if i % step == 0:
            copies[2 + i // step].wait()
        blocks = []
        for e in range(3):
            candidate = group + e - 1
            keep = (mask[e, 0, i] == 1) & (candidate >= 0) & (candidate < groups)
            block = prolong[i, :, e * width:(e + 1) * width]
            blocks.append(block * jnp.where(keep, 1.0, 0.0).astype(block.dtype))
        grid.part(head, 2, i, 0)[...] = jnp.where(group == 0, blocks[1], blocks[0])
        grid.part(head, 2, i, 1)[...] = jnp.where(group == 0, blocks[2], blocks[1])
        grid.part(tail, 1, i, 0)[...] = jnp.where(group == 0, blocks[0], blocks[2])
    line = lax.broadcasted_iota(jnp.int32, (grid.list_rows, width), 0)
    column = lax.broadcasted_iota(jnp.int32, (grid.list_rows, width), 1)
    numbers = jnp.zeros((grid.list_rows, width), jnp.int32)
    for panel in range(grid.panels):
        for entry in range(grid.cap):
            numbers = jnp.where((line == panel) & (column == entry), cols[panel, entry], numbers)
    start = rows * 2 * grid.pores
    head[start:start + grid.list_rows, :] = numbers.astype(jnp.float32).astype(head.dtype)


def pack(grid, mask, cols, prolong):
    rows, _, width3 = prolong.shape
    outs = [grid.shape(rows, 2, width3 // 3, 1), grid.shape(rows, 1, width3 // 3)]
    return pl.pallas_call(
        functools.partial(pack_kernel, grid),
        grid=(1,),
        in_specs=[pl.BlockSpec(memory_space=pl.ANY)] * 3,
        out_specs=[*map(resident, outs)],
        scratch_shapes=[
            pltpu.SMEM(mask.shape, mask.dtype),
            pltpu.SMEM(cols.shape, cols.dtype),
            pltpu.VMEM(prolong.shape, prolong.dtype),
            pltpu.SemaphoreType.DMA((6,)),
        ],
        out_shape=outs,
        compiler_params=pltpu.CompilerParams(vmem_limit_bytes=PACK_VMEM_LIMIT),
        cost_estimate=COST,
        name="pack_rows",
    )(mask, cols, prolong)


def turn_kernel(grid, head, tail, turned):
    width = head.shape[-1]
    for i in range(turned.shape[0]):
        parts = (grid.part(head, 2, i, 0), grid.part(head, 2, i, 1), grid.part(tail, 1, i, 0))
        for k, part in enumerate(parts):
            turned[i, k * width:(k + 1) * width, :] = part[...].T


def turn(grid, head, tail):
    rows, width = tail.shape[0] // grid.pores, tail.shape[1]
    out = jax.ShapeDtypeStruct((rows, 3 * width, grid.pores), head.dtype)
    return pl.pallas_call(
        functools.partial(turn_kernel, grid),
        grid=(1,),
        in_specs=[resident(head), resident(tail)],
        out_specs=resident(out),
        out_shape=out,
        compiler_params=PARAMS,
        cost_estimate=COST,
        name="turn_rows",
    )(head, tail)


def pick_kernel(grid, plan, layout, carry, tables, lists, filled, passed, *refs):
    wanted = list(refs[:lists])
    sources, at = [], lists
    for blocks in layout:
        sources.append([(refs[at + i], k) for i, k in enumerate(blocks)])
        at += len(blocks)
    scratch = 2 * len(tables) + 1 if tables else 0
    outs = refs[len(refs) - len(filled) - scratch:len(refs) - scratch]
    z, y = grid.spot()

    def list_at(source):
        ref = sources[source][0][0]
        return ref[ref.shape[0] - grid.list_rows:, :]

    if tables:
        numbers, plain, done = refs[-scratch:-1 - len(tables)], refs[-1 - len(tables):-1], refs[-1]
        for table, source in enumerate(tables):
            numbers[table][...] = list_at(source).astype(jnp.float32).astype(jnp.int32)
            pltpu.make_async_copy(numbers[table], plain[table], done.at[table]).start()
        for table in range(len(tables)):
            pltpu.make_async_copy(numbers[table], plain[table], done.at[table]).wait()
        wanted += plain
    for index, list_row, source, output, base in plan(z, y):
        for entry in range(grid.cap):
            row = wanted[index][list_row, entry]
            place = 0
            for ref, blocks in sources[source]:
                for block in range(blocks):
                    target = grid.part(outs[output], filled[output][0], base + entry, place)
                    target[...] = grid.part(ref, blocks, row, block)[...]
                    place += 1
    if passed is not None:
        outs[-1][...] = sources[passed][0][0][...]
    for out, source in zip(outs, carry):
        if source is not None:
            out[out.shape[0] - grid.list_rows:, :] = list_at(source)


def pick(grid, plan, filled, lists, sources, carry=(), tables=(), passed=None, after=(), cost=COST):
    flat = [x for source in sources for x, _ in source]
    width = flat[0].shape[-1]
    carry = carry or (None,) * len(filled)
    shapes = [grid.shape(rows, blocks, width, 0 if source is None else 1)
              for (blocks, rows), source in zip(filled, carry)]
    if passed is not None:
        filled = [*filled, (0, 0)]
        shapes.append(jax.ShapeDtypeStruct(sources[passed][0][0].shape, flat[0].dtype))
    layout = tuple(tuple(blocks for _, blocks in source) for source in sources)
    table = (grid.list_rows, width)
    scratch = [pltpu.VMEM(table, jnp.int32)] * len(tables) + [pltpu.SMEM(table, jnp.int32)] * len(tables)
    scratch += [pltpu.SemaphoreType.DMA((len(tables),))] if tables else []
    return pl.pallas_call(
        functools.partial(pick_kernel, grid, plan, layout, carry, tables, len(lists), tuple(filled), passed),
        grid_spec=pltpu.PrefetchScalarGridSpec(
            num_scalar_prefetch=len(lists),
            grid=(1,),
            in_specs=[*map(resident, flat), *([ANYWHERE] * len(after))],
            out_specs=[*map(resident, shapes)],
            scratch_shapes=scratch,
        ),
        out_shape=shapes,
        compiler_params=PARAMS,
        cost_estimate=cost,
        name="pick_rows",
    )(*lists, *flat, *after)


def stage_kernel(grid, plan, layout, carried, slot_rows, slot_cols, slot_counts, turned, matrix, *refs):
    arrays, at = [], 0
    for blocks in layout:
        arrays.append([(refs[at + i], k, base) for i, (k, base) in enumerate(blocks)])
        at += len(blocks)
    earlier = refs[at:at + 3] if carried else ()
    own, up, down, total = refs[-4:]
    width = own.shape[-1]
    first_group = lax.axis_index("rows") == 0
    for old, new in zip(earlier, (own, up, down)):
        for slot in range(carried):
            for f in range(3):
                new[slot, f] = old[slot, f]
    z, y = grid.spot()
    for slot, (panel, sources) in enumerate(plan(z, y), start=carried):
        total[...] = jnp.zeros_like(total)
        for array, whole, present in sources:
            live = slot_counts[0, panel]
            if present is not True:
                live = jnp.where(present, live, 0)
            parts = arrays[array]

            def product(entry, whole=whole, parts=parts, panel=panel):
                pick = slot_cols[panel, entry] if whole else entry
                right = jnp.concatenate(
                    [grid.part(x, blocks, base + pick, block)[...] for x, blocks, base in parts for block in range(blocks)],
                    axis=1)
                return jnp.dot(matrix[panel, entry], right, preferred_element_type=jnp.float32)

            def add(left, value):
                result = jnp.dot(left, value, preferred_element_type=jnp.float32)
                for k in range(3):
                    total[k] += result[:, k * width:(k + 1) * width]

            def two(u, carry, product=product, panel=panel):
                first, second = 2 * u, 2 * u + 1
                left = jnp.concatenate(
                    [turned[slot_rows[panel, first]], turned[slot_rows[panel, second]]], axis=1)
                value = jnp.concatenate([product(first), product(second)], axis=0).astype(jnp.bfloat16)
                add(left, value)
                return carry

            lax.fori_loop(0, live // 2, two, 0)

            @pl.when(live % 2 == 1)
            def _(live=live, product=product, panel=panel):
                add(turned[slot_rows[panel, live - 1]], product(live - 1).astype(jnp.bfloat16))

        begin = jnp.where(first_group, 0, width)
        for f in range(3):
            k = jnp.where(first_group, (f + 2) % 3, f)
            own[slot, f] = total[k, pl.ds(pl.multiple_of(begin, width), width), :].astype(own.dtype)
            up[slot, f] = total[k, pl.ds(pl.multiple_of(begin + width, width), width), :].astype(up.dtype)
            down[slot, f] = total[k, 0:width, :].astype(down.dtype)


def stage(grid, plan, lists, turned, matrix, sources, earlier=(), after=()):
    width = turned.shape[1] // 3
    carried = earlier[0].shape[0] if earlier else 0
    slots = carried + len(plan(jnp.int32(0), jnp.int32(0)))
    flat = [x for source in sources for x, *_ in source]
    layout = tuple(tuple((blocks, base[0] if base else 0) for _, blocks, *base in source) for source in sources)
    out = jax.ShapeDtypeStruct((slots, 3, width, width), jnp.bfloat16)
    return pl.pallas_call(
        functools.partial(stage_kernel, grid, plan, layout, carried),
        grid_spec=pltpu.PrefetchScalarGridSpec(
            num_scalar_prefetch=3,
            grid=(1,),
            in_specs=[*map(resident, (turned, matrix, *flat, *earlier)), *([ANYWHERE] * len(after))],
            out_specs=[resident(out)] * 3,
            scratch_shapes=[pltpu.VMEM((3, 3 * width, width), jnp.float32)],
        ),
        out_shape=[out] * 3,
        compiler_params=PARAMS,
        cost_estimate=COST,
        name="stage_products",
    )(*lists, turned, matrix, *flat, *earlier, *after)


def assemble_kernel(grid, plans, *refs):
    out = refs[-1]
    rows = refs[0].shape[2]
    panels = grid.panels
    z, y = grid.spot()
    for index, group in enumerate(plans):
        own, lower, upper = refs[3 * index:3 * index + 3]
        slots = [slot for plan in group for slot in plan(z, y)]
        for slot, (panel, _) in enumerate(slots):
            for d in range(5):
                terms = []
                if 0 <= d - 1 < 3:
                    terms.append(own[slot, d - 1].astype(jnp.float32))
                if d < 3:
                    terms.append(lower[slot, d].astype(jnp.float32))
                if 0 <= d - 2 < 3:
                    terms.append(upper[slot, d - 2].astype(jnp.float32))
                out[pl.ds(d * panels + panel, rows, stride=5 * panels), :] = functools.reduce(jnp.add, terms)


def assemble(grid, plans, pieces):
    panels = grid.panels
    width = pieces[0][0].shape[-1]
    rows = width // 4
    flat = [x for piece in pieces for x in piece]
    result = pl.pallas_call(
        functools.partial(assemble_kernel, grid, plans),
        grid=(width // rows,),
        in_specs=[pl.BlockSpec((x.shape[0], 3, rows, width), lambda i: (0, 0, i, 0)) for x in flat],
        out_specs=pl.BlockSpec((rows * 5 * panels, width), lambda i: (i, 0)),
        out_shape=jax.ShapeDtypeStruct((width * 5 * panels, width), jnp.float32),
        compiler_params=PARAMS,
        cost_estimate=COST,
        name="assemble_coarse",
    )(*flat)
    return result.reshape(width, 5, panels, width).transpose(0, 2, 1, 3)


def per_device(fine_blocks, block_rows, block_cols, block_counts, prolong_blocks, prolong_mask):
    matrix = fine_blocks[0, 0]
    cols_list = block_cols[0, 0]
    lists = (block_rows[0, 0], cols_list, block_counts[0])
    groups = lax.axis_size("rows")
    grid = Grid(lax.axis_size("blk"), cols_list.shape[1], matrix.shape[2])
    cap, sides, columns = grid.cap, grid.sides, grid.columns
    every, inner = range(groups), range(1, groups - 1)

    def move(x, pairs, members=every):
        perm = [(a * groups + g, b * groups + g) for g in members for a, b in pairs]
        return lax.ppermute(x, ("blk", "rows"), perm) if perm else jnp.zeros_like(x)

    def move_both(pair, pairs):
        return (move(pair[0][0], pairs), 2), (move(pair[1][0], pairs, inner), 1)

    def move_across(arrays, lines=range(LINES)):
        return [((move(x, grid.across(shift, lines)), 3),) for x, shift in zip(arrays, sides)]

    def exchange(parts):
        lower = lax.ppermute(parts[1], "rows", [(g, g + 1) for g in range(groups - 1)])
        upper = lax.ppermute(parts[2], "rows", [(g + 1, g) for g in range(groups - 1)])
        return parts[0], lower, upper

    count = len(sides)
    mids = (1, 2)

    head, tail = pack(grid, prolong_mask.transpose(2, 0, 1), cols_list, prolong_blocks[0])
    own = ((head, 2), (tail, 1))
    half = move_both(own, grid.swaps([(0, 1), (2, 3)]))
    other = move_both(own, grid.swaps([(1, 2)]))
    side_lists = [move(cols_list, [(b, a) for a, b in grid.across(shift)]) for shift in sides]

    def own_requests(z, y):
        return [(index, grid.panel(z, y, 0), 0, index, 0) for index in range(count)]

    beside = move_across(pick(grid, own_requests, [(3, cap)] * count, side_lists, [own]))
    turned = turn(grid, head, tail)

    far_head = move(half[0][0], grid.swaps([(1, 2)]))

    def early_requests(z, y):
        return [(0, grid.panel(grid.lines(z)[1], y, 0), 0, 0, 0)]

    early, end_list = pick(grid, early_requests, [(2, cap), (0, 0)], [], [other[:1], half[:1]], (None, 1), (1,),
                           cost=EARLY_COST)
    end_lists = [move(end_list, [(b, a) for a, b in grid.across(shift, mids)]) for shift in sides]
    tables = [(half[0],), *[((x, 0),) for x in end_lists]]
    end_heads = [move(early, grid.ends(0))]

    def near_requests(z, y):
        line_half, line_other, _ = grid.lines(z)
        requests = []
        for index in range(count):
            requests += [(index, grid.panel(line_half, y, 0), 0, index, 0),
                         (index, grid.panel(line_other, y, 0), 1, count + index, 0),
                         (count + 1 + index, grid.panel(line_other, y, 0), 2, 2 * count + index, 0)]
        return requests

    picked = pick(grid, near_requests, [(3, cap)] * (2 * count) + [(2, cap)] * count, side_lists,
                  [half, other, other[:1], *tables], tables=tuple(range(3, 4 + count)),
                  after=[x for ((x, _),) in beside], cost=NEAR_COST)
    half_crossed = move_across(picked)
    other_crossed = move_across(picked[count:], mids)
    end_heads += [move(x, grid.ends(shift)) for x, shift in zip(picked[2 * count:], sides)]
    far_tail = move(half[1][0], grid.swaps([(1, 2)]), inner)
    far = ((far_head, 2), (far_tail, 1))
    parts = stage(grid, grid.work_near, lists, turned, matrix, [own, half, *beside])

    def far_requests(z, y):
        return [(index, grid.panel(grid.lines(z)[2], y, 0), 0, index, 0) for index in range(columns)]

    picked = pick(grid, far_requests, [(2, cap)] * columns, [], [far[:1], *tables], tables=tuple(range(1, 2 + count)),
                  cost=FAR_COST)
    far_heads = [move(x, grid.ends(shift)) for shift, x in enumerate(picked)]

    def last_requests(z, y):
        _, line_other, line_far = grid.lines(z)
        requests = [(index, grid.panel(line_far, y, 0), 0, index, 0) for index in range(count)]
        for index in range(columns):
            requests += [(count + index, grid.panel(line_other, y, 0), 1, count + index, 0),
                         (count + index, grid.panel(line_far, y, 0), 2, count + index, cap)]
        return requests

    picked = pick(grid, last_requests, [(3, cap)] * count + [(1, 2 * cap)] * columns, side_lists,
                  [far, other[1:], far[1:], *tables], tables=tuple(range(3, 4 + count)), after=[parts[0]],
                  cost=PICK_COST)
    far_crossed = move_across(picked, mids)
    end_tails = [move(x, grid.ends(shift), inner) for shift, x in enumerate(picked[count:])]
    end = [((x, 2), (last, 1, 0)) for x, last in zip(end_heads, end_tails)]
    far_end = [((x, 2), (last, 1, cap)) for x, last in zip(far_heads, end_tails)]
    sources = [other, end[0]]
    for i in range(count):
        sources += [other_crossed[i], end[1 + i]]
    parts = stage(grid, grid.work_middle, lists, turned, matrix, sources, parts)
    first = exchange(parts)

    sources = [far, far_end[0]]
    for i in range(count):
        sources += [half_crossed[i], far_crossed[i], far_end[1 + i]]
    last = exchange(stage(grid, grid.work_far, lists, turned, matrix, sources, (), first[1:]))
    return assemble(grid, ((grid.work_near, grid.work_middle), (grid.work_far,)), [first, last])[None, None]


def solution(mesh):
    in_specs = (
        P("rows", "blk", None, None, None, None),
        P("rows", "blk", None, None),
        P("rows", "blk", None, None),
        P("rows", "blk", None),
        P("rows", "blk", None, None),
        P("rows", "blk", None),
    )
    out_specs = P("rows", "blk", None, None, None, None)
    return jax.shard_map(
        per_device, mesh=mesh, in_specs=in_specs, out_specs=out_specs, check_vma=False
    )
```

time: 130 us -> 127 us (0.977)
  the two profiles are of different devices: /device:TPU:25 before, /device:TPU:1 now
where the time goes in v9:
time: 127 us; the launch traced here: 126 us
  waiting for transfers between devices  68.7 us (54%)
  starting transfers between devices  32.1 us (25%)
  Pallas kernels  22.5 us (18%)
  local copies, waits for them, and re-layouts  2.3 us (2%)
    ppermute x18, waiting for transfers between devices, move(): return lax.ppermute(x, ('blk', 'rows'), perm) if perm else jnp.zeros_like(x)  59.1 us
    ppermute x18, starting transfers between devices, move(): return lax.ppermute(x, ('blk', 'rows'), perm) if perm else jnp.zeros_like(x)  23.3 us
    pallas_call x3, Pallas kernels, stage(): pl.pallas_call(functools.partial(stage_kernel, grid, plan, layout, carrie...  11.6 us
    ppermute x2, waiting for transfers between devices, exchange(): lax.ppermute(parts[2], 'rows', [(g + 1, g) for g in range(groups - 1)])  7.92 us
    pallas_call x5, Pallas kernels, pick(): pl.pallas_call(functools.partial(pick_kernel, grid, plan, layout, carry,...  5.41 us
    ppermute x2, starting transfers between devices, exchange(): lax.ppermute(parts[1], 'rows', [(g, g + 1) for g in range(groups - 1)])  4.43 us
    ppermute x2, starting transfers between devices, exchange(): lax.ppermute(parts[2], 'rows', [(g + 1, g) for g in range(groups - 1)])  4.35 us
    pallas_call x1, Pallas kernels, pack(): pl.pallas_call(functools.partial(pack_kernel, grid), grid=(1,), in_specs=...  2.64 us
  transfers between devices with their start and end apart: 22, of which 11 were waited for; matrix products, arithmetic and copies ran while one was open for 0% of the time, Pallas kernels for 11%

profile of v9, /device:TPU:1, one launch (start us, length us, event | category | flops | bytes accessed | tf_op | source)
XLA Modules:
  0.0 126.1 jit_solution(17340473226521332266)
XLA Ops:
  0.0 2.6 %pack_rows.1 = (bf16[4112,128]{1,0:T(8,128)(2,1)}, bf16[2048,128]{1,0:T(8,128)(2,1)}) custom-call(s32[3,1,16]{2,1,0:T(1,128)} %bitcast.26, s32[8,8]{1,0:T(8,128)} %bitcast.14, bf16[16,128,384]{2,1,0:T(8,128)(2,1)} %bitcast.25), custom_call_target="tpu_custom_call" | custom-call | flops 1024 | bytes 1024 | tf_op jit(solution)/shard_map/pack_rows/pallas_call | solution.py:133
  2.6 2.2 %collective-permute-start.2 = (bf16[4112,128]{1,0:T(8,128)(2,1)}, bf16[4112,128]{1,0:T(8,128)(2,1)S(1)}, u32[]{:S(2)}, u32[]{:S(2)}) collective-permute-start(bf16[4112,128]{1,0:T(8,128)(2,1)} %get-tuple-element.26.head.refs_1_.refs_0_), channel_id=1, source_target_pairs={{0,8},{4,12},{16,24},{20,28},{8,0},{12,4},{24,16},{28,20},{1,9},{5... | collective-permute-start | bytes 3158024 | tf_op jit(solution)/shard_map/ppermute | solution.py:369
  4.8 0.7 collective-permute-start
  5.6 0.0 copy-done.4
  5.6 1.3 %collective-permute-start.4 = (s32[8,8]{1,0:T(8,128)S(1)}, s32[8,8]{1,0:T(8,128)S(1)}, u32[]{:S(2)}, u32[]{:S(2)}) collective-permute-start(s32[8,8]{1,0:T(8,128)S(1)} %bitcast.15), channel_id=1, source_target_pairs={{4,0},{0,4},{12,8},{8,12},{20,16},{16,20},{28,24},{24,28},{5,1},{1... | collective-permute-start | bytes 776 | tf_op jit(solution)/shard_map/ppermute | solution.py:369
  6.9 1.5 %collective-permute-done.4.refs_0_ = s32[8,8]{1,0:T(8,128)S(1)} collective-permute-done((s32[8,8]{1,0:T(8,128)S(1)}, s32[8,8]{1,0:T(8,128)S(1)}, u32[]{:S(2)}, u32[]{:S(2)}) %collective-permute-start.4) | collective-permute-done | bytes 288 | tf_op jit(solution)/shard_map/ppermute | solution.py:369
  8.4 1.2 copy-done.1
  9.6 1.0 copy-done.3
  10.7 0.7 pick_rows.6
  11.3 0.0 copy-start.2
  11.4 1.3 %collective-permute-start.9 = (bf16[3072,128]{1,0:T(8,128)(2,1)S(1)}, bf16[3072,128]{1,0:T(8,128)(2,1)S(1)}, u32[]{:S(2)}, u32[]{:S(2)}) collective-permute-start(bf16[3072,128]{1,0:T(8,128)(2,1)S(1)} %pick_rows.6), channel_id=1, source_target_pairs={{0,4},{4,0},{8,12},{12,8},{16,20},{20,16},{24,28},{28,24},{1,5},{5... | collective-permute-start | bytes 2359304 | tf_op jit(solution)/shard_map/ppermute | solution.py:369
  12.7 5.7 %collective-permute-start.6 = (bf16[2048,128]{1,0:T(8,128)(2,1)S(1)}, bf16[2048,128]{1,0:T(8,128)(2,1)S(1)}, u32[]{:S(2)}, u32[]{:S(2)}) collective-permute-start(bf16[2048,128]{1,0:T(8,128)(2,1)S(1)} %copy-done.3), channel_id=1, source_target_pairs={{1,9},{5,13},{17,25},{21,29},{9,1},{13,5},{25,17},{29,21},{2,10},{... | collective-permute-start | bytes 1572872 | tf_op jit(solution)/shard_map/ppermute | solution.py:369
  18.3 0.7 collective-permute-start.1
  19.0 9.0 %collective-permute-done.2.refs_1_.refs_2_.refs_5_.refs_6_ = bf16[4112,128]{1,0:T(8,128)(2,1)S(1)} collective-permute-done((bf16[4112,128]{1,0:T(8,128)(2,1)}, bf16[4112,128]{1,0:T(8,128)(2,1)S(1)}, u32[]{:S(2)}, u32[]{:S(2)}) %collective-permute-start.2) | collective-permute-done | bytes 1052704 | tf_op jit(solution)/shard_map/ppermute | solution.py:369
  28.0 0.7 collective-permute-start.5
  28.7 0.0 collective-permute-done.refs_0_.refs_3_.refs_5_
  28.8 0.7 pick_rows.5
  29.5 0.0 copy-start
  29.5 0.0 copy-start.5
  29.5 0.0 copy-start.6
  29.5 0.8 collective-permute-start.8
  30.3 0.0 copy-done.2
  30.3 0.5 turn_rows.1.turned
  30.8 3.4 %collective-permute-done.6.refs_3_.refs_2_ = bf16[2048,128]{1,0:T(8,128)(2,1)S(1)} collective-permute-done((bf16[2048,128]{1,0:T(8,128)(2,1)S(1)}, bf16[2048,128]{1,0:T(8,128)(2,1)S(1)}, u32[]{:S(2)}, u32[]{:S(2)}) %collective-permute-start.6) | collective-permute-done | bytes 524320 | tf_op jit(solution)/shard_map/ppermute | solution.py:369
  34.2 0.7 collective-permute-start.7
  34.9 0.0 collective-permute-done.9.refs_4_.refs_8_
  34.9 1.3 %collective-permute-start.3 = (bf16[2048,128]{1,0:T(8,128)(2,1)S(1)}, bf16[2048,128]{1,0:T(8,128)(2,1)S(1)}, u32[]{:S(2)}, u32[]{:S(2)}) collective-permute-start(bf16[2048,128]{1,0:T(8,128)(2,1)S(1)} %get-tuple-element.28), channel_id=1, source_target_pairs={{8,0},{12,4},{16,24},{20,28},{9,1},{13,5},{17,25},{21,29},{10,2},{... | collective-permute-start | bytes 1572872 | tf_op jit(solution)/shard_map/ppermute | solution.py:369
  36.2 0.0 copy-done
  36.2 4.4 %stage_products.3 = (bf16[3,3,128,128]{3,2,1,0:T(8,128)(2,1)S(1)}, bf16[3,3,128,128]{3,2,1,0:T(8,128)(2,1)S(1)}, bf16[3,3,128,128]{3,2,1,0:T(8,128)(2,1)S(1)}) custom-call(s32[8,8]{1,0:T(8,128)S(1)} %bitcast.19, s32[8,8]{1,0:T(8,128)S(1)} %bitcast.16, s32[1,8]{1,0:T(1,128)S(1)} %bitcast.22, bf16[16,384,128]{2,1,0:T(8,128)(2,1)S(1)} %turn_rows.1.turned, ...), custom_call_target="tpu_custom_call" | custom-call | flops 1024 | bytes 1024 | tf_op jit(solution)/shard_map/stage_products/pallas_call | solution.py:304
  40.6 0.0 collective-permute-done.1.refs_3_.refs_4_.refs_1_
  40.6 0.0 collective-permute-done.8.refs_6_.refs_7_.refs_2_
  40.6 1.6 %pick_rows.8 = (bf16[3072,128]{1,0:T(8,128)(2,1)S(1)}, bf16[3072,128]{1,0:T(8,128)(2,1)S(1)}, bf16[2048,128]{1,0:T(8,128)(2,1)S(1)}) custom-call(s32[8,8]{1,0:T(8,128)S(1)} %collective-permute-done.4.refs_0_, bf16[4112,128]{1,0:T(8,128)(2,1)S(1)} %collective-permute-done.2.refs_1_.refs_2_.refs_5_.refs_6_, ...), custom_call_target="tpu_custom_call" | custom-call | flops 6000000000 | bytes 1024 | tf_op jit(solution)/shard_map/pick_rows/pallas_call | solution.py:225
  42.2 1.3 %collective-permute-start.12 = (bf16[2048,128]{1,0:T(8,128)(2,1)S(1)}, bf16[2048,128]{1,0:T(8,128)(2,1)S(1)}, u32[]{:S(2)}, u32[]{:S(2)}) collective-permute-start(bf16[2048,128]{1,0:T(8,128)(2,1)S(1)} %get-tuple-element.33), channel_id=1, source_target_pairs={{8,4},{12,0},{16,28},{20,24},{9,5},{13,1},{17,29},{21,25},{10,6},{... | collective-permute-start | bytes 1572872 | tf_op jit(solution)/shard_map/ppermute | solution.py:369
  43.5 0.7 collective-permute-start.11
  44.2 0.0 collective-permute-done.7.refs_2_.refs_4_.refs_1_
  44.2 0.1 collective-permute-start.17
  44.4 0.0 collective-permute-done.5.refs_1_.refs_0_
  44.4 1.5 %pick_rows.7 = (bf16[3072,128]{1,0:T(8,128)(2,1)S(1)}, bf16[2048,128]{1,0:T(8,128)(2,1)S(1)}, bf16[2048,128]{1,0:T(8,128)(2,1)S(1)}) custom-call(s32[8,8]{1,0:T(8,128)S(1)} %collective-permute-done.4.refs_0_, bf16[4112,128]{1,0:T(8,128)(2,1)S(1)} %collective-permute-done.5.refs_1_.refs_0_, ...), custom_call_target="tpu_custom_call" | custom-call | flops 20000000000 | bytes 1024 | tf_op jit(solution)/shard_map/pick_rows/pallas_call | solution.py:225
  45.9 1.3 %collective-permute-start.10 = (bf16[2048,128]{1,0:T(8,128)(2,1)S(1)}, bf16[2048,128]{1,0:T(8,128)(2,1)S(1)}, u32[]{:S(2)}, u32[]{:S(2)}) collective-permute-start(bf16[2048,128]{1,0:T(8,128)(2,1)S(1)} %get-tuple-element.31), channel_id=1, source_target_pairs={{9,1},{13,5},{17,25},{21,29},{10,2},{14,6},{18,26},{22,30}} | collective-permute-start | bytes 1572872 | tf_op jit(solution)/shard_map/ppermute | solution.py:369
  47.2 5.0 %collective-permute-done.3.refs_2_ = bf16[2048,128]{1,0:T(8,128)(2,1)S(1)} collective-permute-done((bf16[2048,128]{1,0:T(8,128)(2,1)S(1)}, bf16[2048,128]{1,0:T(8,128)(2,1)S(1)}, u32[]{:S(2)}, u32[]{:S(2)}) %collective-permute-start.3) | collective-permute-done | bytes 524320 | tf_op jit(solution)/shard_map/ppermute | solution.py:369
  52.2 1.3 %collective-permute-start.13 = (bf16[2048,128]{1,0:T(8,128)(2,1)S(1)}, bf16[2048,128]{1,0:T(8,128)(2,1)S(1)}, u32[]{:S(2)}, u32[]{:S(2)}) collective-permute-start(bf16[2048,128]{1,0:T(8,128)(2,1)S(1)} %get-tuple-element.34), channel_id=1, source_target_pairs={{9,5},{13,1},{17,29},{21,25},{10,6},{14,2},{18,30},{22,26}} | collective-permute-start | bytes 1572872 | tf_op jit(solution)/shard_map/ppermute | solution.py:369
  53.5 10.1 %collective-permute-done.12.refs_5_ = bf16[2048,128]{1,0:T(8,128)(2,1)S(1)} collective-permute-done((bf16[2048,128]{1,0:T(8,128)(2,1)S(1)}, bf16[2048,128]{1,0:T(8,128)(2,1)S(1)}, u32[]{:S(2)}, u32[]{:S(2)}) %collective-permute-start.12) | collective-permute-done | bytes 524320 | tf_op jit(solution)/shard_map/ppermute | solution.py:369
  63.6 0.7 collective-permute-start.18
  64.3 0.9 pick_rows.9
  65.2 0.0 collective-permute-done.11.refs_4_
  65.2 1.3 %collective-permute-start.16 = (bf16[2048,128]{1,0:T(8,128)(2,1)S(1)}, bf16[2048,128]{1,0:T(8,128)(2,1)S(1)}, u32[]{:S(2)}, u32[]{:S(2)}) collective-permute-start(bf16[2048,128]{1,0:T(8,128)(2,1)S(1)} %get-tuple-element.40), channel_id=1, source_target_pairs={{8,0},{12,4},{16,24},{20,28},{9,1},{13,5},{17,25},{21,29},{10,2},{... | collective-permute-start | bytes 1572872 | tf_op jit(solution)/shard_map/ppermute | solution.py:369
  66.5 17.0 %collective-permute-done.10.refs_3_ = bf16[2048,128]{1,0:T(8,128)(2,1)S(1)} collective-permute-done((bf16[2048,128]{1,0:T(8,128)(2,1)S(1)}, bf16[2048,128]{1,0:T(8,128)(2,1)S(1)}, u32[]{:S(2)}, u32[]{:S(2)}) %collective-permute-start.10) | collective-permute-done | bytes 524320 | tf_op jit(solution)/shard_map/ppermute | solution.py:369
  83.5 1.3 %collective-permute-start.19 = (bf16[2048,128]{1,0:T(8,128)(2,1)S(1)}, bf16[2048,128]{1,0:T(8,128)(2,1)S(1)}, u32[]{:S(2)}, u32[]{:S(2)}) collective-permute-start(bf16[2048,128]{1,0:T(8,128)(2,1)S(1)} %get-tuple-element.43), channel_id=1, source_target_pairs={{8,4},{12,0},{16,28},{20,24},{9,5},{13,1},{17,29},{21,25},{10,6},{... | collective-permute-start | bytes 1572872 | tf_op jit(solution)/shard_map/ppermute | solution.py:369
  84.8 9.0 %collective-permute-done.13.refs_6_.refs_7_ = bf16[2048,128]{1,0:T(8,128)(2,1)S(1)} collective-permute-done((bf16[2048,128]{1,0:T(8,128)(2,1)S(1)}, bf16[2048,128]{1,0:T(8,128)(2,1)S(1)}, u32[]{:S(2)}, u32[]{:S(2)}) %collective-permute-start.13) | collective-permute-done | bytes 524320 | tf_op jit(solution)/shard_map/ppermute | solution.py:369
  93.8 3.5 %stage_products.4 = (bf16[5,3,128,128]{3,2,1,0:T(8,128)(2,1)S(1)}, bf16[5,3,128,128]{3,2,1,0:T(8,128)(2,1)S(1)}, bf16[5,3,128,128]{3,2,1,0:T(8,128)(2,1)S(1)}) custom-call(s32[8,8]{1,0:T(8,128)S(1)} %bitcast.20, s32[8,8]{1,0:T(8,128)S(1)} %bitcast.17, s32[1,8]{1,0:T(1,128)S(1)} %bitcast.23, bf16[16,384,128]{2,1,0:T(8,128)(2,1)S(1)} %turn_rows.1.turned, ...), custom_call_target="tpu_custom_call" | custom-call | flops 1024 | bytes 1024 | tf_op jit(solution)/shard_map/stage_products/pallas_call | solution.py:304
  97.2 1.9 %collective-permute-start.14 = (bf16[5,3,128,128]{3,2,1,0:T(8,128)(2,1)S(1)}, bf16[5,3,128,128]{3,2,1,0:T(8,128)(2,1)S(1)}, u32[]{:S(2)}, u32[]{:S(2)}) collective-permute-start(bf16[5,3,128,128]{3,2,1,0:T(8,128)(2,1)S(1)} %get-tuple-element.38), channel_id=1, source_target_pairs={{0,1},{1,2},{2,3},{4,5},{5,6},{6,7},{8,9},{9,10},{10,11},{12,13},{... | collective-permute-start | bytes 1474568 | tf_op jit(solution)/shard_map/ppermute | solution.py:378
  99.2 0.0 collective-permute-done.17.refs_4_
  99.2 2.4 %collective-permute-start.15 = (bf16[5,3,128,128]{3,2,1,0:T(8,128)(2,1)S(1)}, bf16[5,3,128,128]{3,2,1,0:T(8,128)(2,1)S(1)}, u32[]{:S(2)}, u32[]{:S(2)}) collective-permute-start(bf16[5,3,128,128]{3,2,1,0:T(8,128)(2,1)S(1)} %get-tuple-element.39), channel_id=1, source_target_pairs={{1,0},{2,1},{3,2},{5,4},{6,5},{7,6},{9,8},{10,9},{11,10},{13,12},{... | collective-permute-start | bytes 1474568 | tf_op jit(solution)/shard_map/ppermute | solution.py:379
  101.6 0.0 collective-permute-done.16.refs_2_
  101.6 4.2 %collective-permute-done.19.refs_6_ = bf16[2048,128]{1,0:T(8,128)(2,1)S(1)} collective-permute-done((bf16[2048,128]{1,0:T(8,128)(2,1)S(1)}, bf16[2048,128]{1,0:T(8,128)(2,1)S(1)}, u32[]{:S(2)}, u32[]{:S(2)}) %collective-permute-start.19) | collective-permute-done | bytes 524320 | tf_op jit(solution)/shard_map/ppermute | solution.py:369
  105.8 0.0 collective-permute-done.18.refs_5_
  105.8 0.0 collective-permute-done.14.refs_8_.refs_1_
  105.8 3.5 %collective-permute-done.15.refs_9_.refs_2_ = bf16[5,3,128,128]{3,2,1,0:T(8,128)(2,1)S(1)} collective-permute-done((bf16[5,3,128,128]{3,2,1,0:T(8,128)(2,1)S(1)}, bf16[5,3,128,128]{3,2,1,0:T(8,128)(2,1)S(1)}, u32[]{:S(2)}, u32[]{:S(2)}) %collective-permute-start.15) | collective-permute-done | bytes 491552 | tf_op jit(solution)/shard_map/ppermute | solution.py:379
  109.3 3.7 %stage_products.5 = (bf16[3,3,128,128]{3,2,1,0:T(8,128)(2,1)S(1)}, bf16[3,3,128,128]{3,2,1,0:T(8,128)(2,1)S(1)}, bf16[3,3,128,128]{3,2,1,0:T(8,128)(2,1)S(1)}) custom-call(s32[8,8]{1,0:T(8,128)S(1)} %bitcast.21, s32[8,8]{1,0:T(8,128)S(1)} %bitcast.18, s32[1,8]{1,0:T(1,128)S(1)} %bitcast.24, bf16[16,384,128]{2,1,0:T(8,128)(2,1)S(1)} %turn_rows.1.turned, ...), custom_call_target="tpu_custom_call" | custom-call | flops 1024 | bytes 1024 | tf_op jit(solution)/shard_map/stage_products/pallas_call | solution.py:304
  113.0 2.5 %collective-permute-start.20 = (bf16[3,3,128,128]{3,2,1,0:T(8,128)(2,1)S(1)}, bf16[3,3,128,128]{3,2,1,0:T(8,128)(2,1)S(1)}, u32[]{:S(2)}, u32[]{:S(2)}) collective-permute-start(bf16[3,3,128,128]{3,2,1,0:T(8,128)(2,1)S(1)} %get-tuple-element.45), channel_id=1, source_target_pairs={{0,1},{1,2},{2,3},{4,5},{5,6},{6,7},{8,9},{9,10},{10,11},{12,13},{... | collective-permute-start | bytes 884744 | tf_op jit(solution)/shard_map/ppermute | solution.py:378
  115.5 1.9 %collective-permute-start.21 = (bf16[3,3,128,128]{3,2,1,0:T(8,128)(2,1)S(1)}, bf16[3,3,128,128]{3,2,1,0:T(8,128)(2,1)S(1)}, u32[]{:S(2)}, u32[]{:S(2)}) collective-permute-start(bf16[3,3,128,128]{3,2,1,0:T(8,128)(2,1)S(1)} %get-tuple-element.46), channel_id=1, source_target_pairs={{1,0},{2,1},{3,2},{5,4},{6,5},{7,6},{9,8},{10,9},{11,10},{13,12},{... | collective-permute-start | bytes 884744 | tf_op jit(solution)/shard_map/ppermute | solution.py:379
  117.5 1.7 %collective-permute-done.20.refs_4_ = bf16[3,3,128,128]{3,2,1,0:T(8,128)(2,1)S(1)} collective-permute-done((bf16[3,3,128,128]{3,2,1,0:T(8,128)(2,1)S(1)}, bf16[3,3,128,128]{3,2,1,0:T(8,128)(2,1)S(1)}, u32[]{:S(2)}, u32[]{:S(2)}) %collective-permute-start.20) | collective-permute-done | bytes 294944 | tf_op jit(solution)/shard_map/ppermute | solution.py:378
  119.2 4.4 %collective-permute-done.21.refs_5_ = bf16[3,3,128,128]{3,2,1,0:T(8,128)(2,1)S(1)} collective-permute-done((bf16[3,3,128,128]{3,2,1,0:T(8,128)(2,1)S(1)}, bf16[3,3,128,128]{3,2,1,0:T(8,128)(2,1)S(1)}, u32[]{:S(2)}, u32[]{:S(2)}) %collective-permute-start.21) | collective-permute-done | bytes 294944 | tf_op jit(solution)/shard_map/ppermute | solution.py:379
  123.6 2.5 %assemble_coarse.1 = f32[5120,128]{1,0:T(8,128)} custom-call(bf16[5,3,128,128]{3,2,1,0:T(8,128)(2,1)S(1)} %get-tuple-element.37.refs_0_, bf16[5,3,128,128]{3,2,1,0:T(8,128)(2,1)S(1)} %collective-permute-done.14.refs_8_.refs_1_, bf16[5,3,128,128]{3,2,1,0:T(8,128)(2,1)S(1)} %collective-permute-done.15.refs_9_.refs_2_, ...), custom_call_target="tpu_custom_call" | custom-call | flops 1024 | bytes 1024 | tf_op jit(solution)/shard_map/assemble_coarse/pallas_call | solution.py:345
  (5 shorter events, 0.0 us)
Async XLA Ops:
  0.0 5.6 %copy-start.4 = (s32[1,1,8,8]{3,2,1,0:T(8,128)S(1)}, s32[1,1,8,8]{3,2,1,0:T(8,128)}, u32[]{:S(2)}) copy-start(s32[1,1,8,8]{3,2,1,0:T(8,128)} %param.8) | copy-start | bytes 772
  2.6 25.4 %collective-permute-start.2 = (bf16[4112,128]{1,0:T(8,128)(2,1)}, bf16[4112,128]{1,0:T(8,128)(2,1)S(1)}, u32[]{:S(2)}, u32[]{:S(2)}) collective-permute-start(bf16[4112,128]{1,0:T(8,128)(2,1)} %get-tuple-element.26.head.refs_1_.refs_0_), channel_id=1, source_target_pairs={{0,8},{4,12},{16,24},{20,28},{8,0},{12,4},{24,16},{28,20},{1,9},{5... | collective-permute-start | bytes 3158024 | tf_op jit(solution)/shard_map/ppermute | solution.py:369
  4.8 23.9 %collective-permute-start = (bf16[4112,128]{1,0:T(8,128)(2,1)}, bf16[4112,128]{1,0:T(8,128)(2,1)S(1)}, u32[]{:S(2)}, u32[]{:S(2)}) collective-permute-start(bf16[4112,128]{1,0:T(8,128)(2,1)} %get-tuple-element.26.head.refs_1_.refs_0_), channel_id=1, source_target_pairs={{8,16},{12,20},{16,8},{20,12},{9,17},{13,21},{17,9},{21,13},{10,18... | collective-permute-start | bytes 3158024 | tf_op jit(solution)/shard_map/ppermute | solution.py:369
  5.6 2.8 %collective-permute-start.4 = (s32[8,8]{1,0:T(8,128)S(1)}, s32[8,8]{1,0:T(8,128)S(1)}, u32[]{:S(2)}, u32[]{:S(2)}) collective-permute-start(s32[8,8]{1,0:T(8,128)S(1)} %bitcast.15), channel_id=1, source_target_pairs={{4,0},{0,4},{12,8},{8,12},{20,16},{16,20},{28,24},{24,28},{5,1},{1... | collective-permute-start | bytes 776 | tf_op jit(solution)/shard_map/ppermute | solution.py:369
  8.4 1.2 copy-start.1
  9.6 1.0 copy-start.3
  11.3 19.0 %copy-start.2 = (bf16[4112,128]{1,0:T(8,128)(2,1)S(1)}, bf16[4112,128]{1,0:T(8,128)(2,1)}, u32[]{:S(2)}) copy-start(bf16[4112,128]{1,0:T(8,128)(2,1)} %get-tuple-element.26.head.refs_1_.refs_0_) | copy-start | bytes 3158020
  11.4 23.5 %collective-permute-start.9 = (bf16[3072,128]{1,0:T(8,128)(2,1)S(1)}, bf16[3072,128]{1,0:T(8,128)(2,1)S(1)}, u32[]{:S(2)}, u32[]{:S(2)}) collective-permute-start(bf16[3072,128]{1,0:T(8,128)(2,1)S(1)} %pick_rows.6), channel_id=1, source_target_pairs={{0,4},{4,0},{8,12},{12,8},{16,20},{20,16},{24,28},{28,24},{1,5},{5... | collective-permute-start | bytes 2359304 | tf_op jit(solution)/shard_map/ppermute | solution.py:369
  12.7 21.5 %collective-permute-start.6 = (bf16[2048,128]{1,0:T(8,128)(2,1)S(1)}, bf16[2048,128]{1,0:T(8,128)(2,1)S(1)}, u32[]{:S(2)}, u32[]{:S(2)}) collective-permute-start(bf16[2048,128]{1,0:T(8,128)(2,1)S(1)} %copy-done.3), channel_id=1, source_target_pairs={{1,9},{5,13},{17,25},{21,29},{9,1},{13,5},{25,17},{29,21},{2,10},{... | collective-permute-start | bytes 1572872 | tf_op jit(solution)/shard_map/ppermute | solution.py:369
  18.3 22.3 %collective-permute-start.1 = (bf16[2048,128]{1,0:T(8,128)(2,1)S(1)}, bf16[2048,128]{1,0:T(8,128)(2,1)S(1)}, u32[]{:S(2)}, u32[]{:S(2)}) collective-permute-start(bf16[2048,128]{1,0:T(8,128)(2,1)S(1)} %copy-done.3), channel_id=1, source_target_pairs={{9,17},{13,21},{17,9},{21,13},{10,18},{14,22},{18,10},{22,14}} | collective-permute-start | bytes 1572872 | tf_op jit(solution)/shard_map/ppermute | solution.py:369
  28.0 16.3 %collective-permute-start.5 = (bf16[4112,128]{1,0:T(8,128)(2,1)S(1)}, bf16[4112,128]{1,0:T(8,128)(2,1)S(1)}, u32[]{:S(2)}, u32[]{:S(2)}) collective-permute-start(bf16[4112,128]{1,0:T(8,128)(2,1)S(1)} %collective-permute-done.2.refs_1_.refs_2_.refs_5_.refs_6_), channel_id=1, source_target_pairs={{8,16},{12,20},{16,8},{20,12},{9,17},{13,21},{17,9},{21,13},{10,18... | collective-permute-start | bytes 3158024 | tf_op jit(solution)/shard_map/ppermute | solution.py:369
  29.5 6.7 %copy-start = (bf16[1,1,8,8,128,128]{5,4,3,2,1,0:T(8,128)(2,1)S(1)}, bf16[1,1,8,8,128,128]{5,4,3,2,1,0:T(8,128)(2,1)}, u32[]{:S(2)}) copy-start(bf16[1,1,8,8,128,128]{5,4,3,2,1,0:T(8,128)(2,1)} %param.6) | copy-start | bytes 6291460
  29.5 6.7 %copy-start.5 = (s32[1,1,8,8]{3,2,1,0:T(8,128)S(1)}, s32[1,1,8,8]{3,2,1,0:T(8,128)}, u32[]{:S(2)}) copy-start(s32[1,1,8,8]{3,2,1,0:T(8,128)} %param.7) | copy-start | bytes 772
  29.5 6.7 %copy-start.6 = (s32[1,1,8]{2,1,0:T(1,128)S(1)}, s32[1,1,8]{2,1,0:T(1,128)}, u32[]{:S(2)}) copy-start(s32[1,1,8]{2,1,0:T(1,128)} %param.9) | copy-start | bytes 100
  29.5 11.1 %collective-permute-start.8 = (bf16[16,128]{1,0:T(8,128)(2,1)S(1)}, bf16[16,128]{1,0:T(8,128)(2,1)S(1)}, u32[]{:S(2)}, u32[]{:S(2)}) collective-permute-start(bf16[16,128]{1,0:T(8,128)(2,1)S(1)} %get-tuple-element.29), channel_id=1, source_target_pairs={{12,8},{8,12},{20,16},{16,20},{13,9},{9,13},{21,17},{17,21},{14,10... | collective-permute-start | bytes 12296 | tf_op jit(solution)/shard_map/ppermute | solution.py:369
  34.2 10.1 %collective-permute-start.7 = (bf16[2048,128]{1,0:T(8,128)(2,1)S(1)}, bf16[2048,128]{1,0:T(8,128)(2,1)S(1)}, u32[]{:S(2)}, u32[]{:S(2)}) collective-permute-start(bf16[2048,128]{1,0:T(8,128)(2,1)S(1)} %collective-permute-done.6.refs_3_.refs_2_), channel_id=1, source_target_pairs={{9,17},{13,21},{17,9},{21,13},{10,18},{14,22},{18,10},{22,14}} | collective-permute-start | bytes 1572872 | tf_op jit(solution)/shard_map/ppermute | solution.py:369
  34.9 17.3 %collective-permute-start.3 = (bf16[2048,128]{1,0:T(8,128)(2,1)S(1)}, bf16[2048,128]{1,0:T(8,128)(2,1)S(1)}, u32[]{:S(2)}, u32[]{:S(2)}) collective-permute-start(bf16[2048,128]{1,0:T(8,128)(2,1)S(1)} %get-tuple-element.28), channel_id=1, source_target_pairs={{8,0},{12,4},{16,24},{20,28},{9,1},{13,5},{17,25},{21,29},{10,2},{... | collective-permute-start | bytes 1572872 | tf_op jit(solution)/shard_map/ppermute | solution.py:369
  42.2 21.4 %collective-permute-start.12 = (bf16[2048,128]{1,0:T(8,128)(2,1)S(1)}, bf16[2048,128]{1,0:T(8,128)(2,1)S(1)}, u32[]{:S(2)}, u32[]{:S(2)}) collective-permute-start(bf16[2048,128]{1,0:T(8,128)(2,1)S(1)} %get-tuple-element.33), channel_id=1, source_target_pairs={{8,4},{12,0},{16,28},{20,24},{9,5},{13,1},{17,29},{21,25},{10,6},{... | collective-permute-start | bytes 1572872 | tf_op jit(solution)/shard_map/ppermute | solution.py:369
  43.5 21.7 %collective-permute-start.11 = (bf16[3072,128]{1,0:T(8,128)(2,1)S(1)}, bf16[3072,128]{1,0:T(8,128)(2,1)S(1)}, u32[]{:S(2)}, u32[]{:S(2)}) collective-permute-start(bf16[3072,128]{1,0:T(8,128)(2,1)S(1)} %get-tuple-element.32), channel_id=1, source_target_pairs={{8,12},{12,8},{16,20},{20,16},{9,13},{13,9},{17,21},{21,17},{10,14... | collective-permute-start | bytes 2359304 | tf_op jit(solution)/shard_map/ppermute | solution.py:369
  44.2 54.9 %collective-permute-start.17 = (bf16[3072,128]{1,0:T(8,128)(2,1)S(1)}, bf16[3072,128]{1,0:T(8,128)(2,1)S(1)}, u32[]{:S(2)}, u32[]{:S(2)}) collective-permute-start(bf16[3072,128]{1,0:T(8,128)(2,1)S(1)} %get-tuple-element.41), channel_id=1, source_target_pairs={{0,4},{4,0},{8,12},{12,8},{16,20},{20,16},{24,28},{28,24},{1,5},{5... | collective-permute-start | bytes 2359304 | tf_op jit(solution)/shard_map/ppermute | solution.py:369
  45.9 37.6 %collective-permute-start.10 = (bf16[2048,128]{1,0:T(8,128)(2,1)S(1)}, bf16[2048,128]{1,0:T(8,128)(2,1)S(1)}, u32[]{:S(2)}, u32[]{:S(2)}) collective-permute-start(bf16[2048,128]{1,0:T(8,128)(2,1)S(1)} %get-tuple-element.31), channel_id=1, source_target_pairs={{9,1},{13,5},{17,25},{21,29},{10,2},{14,6},{18,26},{22,30}} | collective-permute-start | bytes 1572872 | tf_op jit(solution)/shard_map/ppermute | solution.py:369
  52.2 41.5 %collective-permute-start.13 = (bf16[2048,128]{1,0:T(8,128)(2,1)S(1)}, bf16[2048,128]{1,0:T(8,128)(2,1)S(1)}, u32[]{:S(2)}, u32[]{:S(2)}) collective-permute-start(bf16[2048,128]{1,0:T(8,128)(2,1)S(1)} %get-tuple-element.34), channel_id=1, source_target_pairs={{9,5},{13,1},{17,29},{21,25},{10,6},{14,2},{18,30},{22,26}} | collective-permute-start | bytes 1572872 | tf_op jit(solution)/shard_map/ppermute | solution.py:369
  63.6 42.2 %collective-permute-start.18 = (bf16[3072,128]{1,0:T(8,128)(2,1)S(1)}, bf16[3072,128]{1,0:T(8,128)(2,1)S(1)}, u32[]{:S(2)}, u32[]{:S(2)}) collective-permute-start(bf16[3072,128]{1,0:T(8,128)(2,1)S(1)} %get-tuple-element.42), channel_id=1, source_target_pairs={{8,12},{12,8},{16,20},{20,16},{9,13},{13,9},{17,21},{21,17},{10,14... | collective-permute-start | bytes 2359304 | tf_op jit(solution)/shard_map/ppermute | solution.py:369
  65.2 36.4 %collective-permute-start.16 = (bf16[2048,128]{1,0:T(8,128)(2,1)S(1)}, bf16[2048,128]{1,0:T(8,128)(2,1)S(1)}, u32[]{:S(2)}, u32[]{:S(2)}) collective-permute-start(bf16[2048,128]{1,0:T(8,128)(2,1)S(1)} %get-tuple-element.40), channel_id=1, source_target_pairs={{8,0},{12,4},{16,24},{20,28},{9,1},{13,5},{17,25},{21,29},{10,2},{... | collective-permute-start | bytes 1572872 | tf_op jit(solution)/shard_map/ppermute | solution.py:369
  83.5 22.3 %collective-permute-start.19 = (bf16[2048,128]{1,0:T(8,128)(2,1)S(1)}, bf16[2048,128]{1,0:T(8,128)(2,1)S(1)}, u32[]{:S(2)}, u32[]{:S(2)}) collective-permute-start(bf16[2048,128]{1,0:T(8,128)(2,1)S(1)} %get-tuple-element.43), channel_id=1, source_target_pairs={{8,4},{12,0},{16,28},{20,24},{9,5},{13,1},{17,29},{21,25},{10,6},{... | collective-permute-start | bytes 1572872 | tf_op jit(solution)/shard_map/ppermute | solution.py:369
  97.2 8.6 %collective-permute-start.14 = (bf16[5,3,128,128]{3,2,1,0:T(8,128)(2,1)S(1)}, bf16[5,3,128,128]{3,2,1,0:T(8,128)(2,1)S(1)}, u32[]{:S(2)}, u32[]{:S(2)}) collective-permute-start(bf16[5,3,128,128]{3,2,1,0:T(8,128)(2,1)S(1)} %get-tuple-element.38), channel_id=1, source_target_pairs={{0,1},{1,2},{2,3},{4,5},{5,6},{6,7},{8,9},{9,10},{10,11},{12,13},{... | collective-permute-start | bytes 1474568 | tf_op jit(solution)/shard_map/ppermute | solution.py:378
  99.2 10.1 %collective-permute-start.15 = (bf16[5,3,128,128]{3,2,1,0:T(8,128)(2,1)S(1)}, bf16[5,3,128,128]{3,2,1,0:T(8,128)(2,1)S(1)}, u32[]{:S(2)}, u32[]{:S(2)}) collective-permute-start(bf16[5,3,128,128]{3,2,1,0:T(8,128)(2,1)S(1)} %get-tuple-element.39), channel_id=1, source_target_pairs={{1,0},{2,1},{3,2},{5,4},{6,5},{7,6},{9,8},{10,9},{11,10},{13,12},{... | collective-permute-start | bytes 1474568 | tf_op jit(solution)/shard_map/ppermute | solution.py:379
  113.0 6.2 %collective-permute-start.20 = (bf16[3,3,128,128]{3,2,1,0:T(8,128)(2,1)S(1)}, bf16[3,3,128,128]{3,2,1,0:T(8,128)(2,1)S(1)}, u32[]{:S(2)}, u32[]{:S(2)}) collective-permute-start(bf16[3,3,128,128]{3,2,1,0:T(8,128)(2,1)S(1)} %get-tuple-element.45), channel_id=1, source_target_pairs={{0,1},{1,2},{2,3},{4,5},{5,6},{6,7},{8,9},{9,10},{10,11},{12,13},{... | collective-permute-start | bytes 884744 | tf_op jit(solution)/shard_map/ppermute | solution.py:378
  115.5 8.0 %collective-permute-start.21 = (bf16[3,3,128,128]{3,2,1,0:T(8,128)(2,1)S(1)}, bf16[3,3,128,128]{3,2,1,0:T(8,128)(2,1)S(1)}, u32[]{:S(2)}, u32[]{:S(2)}) collective-permute-start(bf16[3,3,128,128]{3,2,1,0:T(8,128)(2,1)S(1)} %get-tuple-element.46), channel_id=1, source_target_pairs={{1,0},{2,1},{3,2},{5,4},{6,5},{7,6},{9,8},{10,9},{11,10},{13,12},{... | collective-permute-start | bytes 884744 | tf_op jit(solution)/shard_map/ppermute | solution.py:379

commit v10 on v9

--- a/solution.py
+++ b/solution.py
@@ -10,10 +10,6 @@
 PACK_VMEM_LIMIT = 60 * 1024 * 1024
 PARAMS = pltpu.CompilerParams(vmem_limit_bytes=VMEM_LIMIT)
 COST = pl.CostEstimate(flops=1024, bytes_accessed=1024, transcendentals=0)
-EARLY_COST = pl.CostEstimate(flops=1024, bytes_accessed=1024, transcendentals=0)
-FAR_COST = pl.CostEstimate(flops=1024, bytes_accessed=1024, transcendentals=0)
-NEAR_COST = pl.CostEstimate(flops=6 * 10 ** 9, bytes_accessed=1024, transcendentals=0)
-PICK_COST = pl.CostEstimate(flops=2 * 10 ** 10, bytes_accessed=1024, transcendentals=0)
 ANYWHERE = pl.BlockSpec(memory_space=pl.ANY)
 
 
@@ -92,9 +88,22 @@
         return work
 
 
-def pack_kernel(grid, mask_from, cols_from, prolong_from, head, tail, mask, cols, prolong, done):
+def keep(grid, mask, block, row, k):
     group, groups = lax.axis_index("rows"), lax.axis_size("rows")
-    width = tail.shape[-1]
+    first, other = k, (k + 1) % 3
+
+    def masked(e):
+        candidate = group + e - 1
+        present = (mask[e, 0, row] == 1) & (candidate >= 0) & (candidate < groups)
+        value = block(e)
+        return value * jnp.where(present, 1.0, 0.0).astype(value.dtype)
+
+    return jnp.where(group == 0, masked(other), masked(first))
+
+
+def pack_kernel(grid, blocks, passed, mask_from, cols_from, prolong_from, *refs):
+    out, mask, cols, prolong, done = refs[-5:]
+    width = out.shape[-1]
     rows = prolong.shape[0]
     step = rows // 4 if rows % 4 == 0 else rows
     copies = [pltpu.make_async_copy(mask_from, mask, done.at[0]), pltpu.make_async_copy(cols_from, cols, done.at[1])]
@@ -108,44 +117,40 @@
     for i in range(rows):
         if i % step == 0:
             copies[2 + i // step].wait()
-        blocks = []
-        for e in range(3):
-            candidate = group + e - 1
-            keep = (mask[e, 0, i] == 1) & (candidate >= 0) & (candidate < groups)
-            block = prolong[i, :, e * width:(e + 1) * width]
-            blocks.append(block * jnp.where(keep, 1.0, 0.0).astype(block.dtype))
-        grid.part(head, 2, i, 0)[...] = jnp.where(group == 0, blocks[1], blocks[0])
-        grid.part(head, 2, i, 1)[...] = jnp.where(group == 0, blocks[2], blocks[1])
-        grid.part(tail, 1, i, 0)[...] = jnp.where(group == 0, blocks[0], blocks[2])
-    line = lax.broadcasted_iota(jnp.int32, (grid.list_rows, width), 0)
-    column = lax.broadcasted_iota(jnp.int32, (grid.list_rows, width), 1)
-    numbers = jnp.zeros((grid.list_rows, width), jnp.int32)
-    for panel in range(grid.panels):
-        for entry in range(grid.cap):
-            numbers = jnp.where((line == panel) & (column == entry), cols[panel, entry], numbers)
-    start = rows * 2 * grid.pores
-    head[start:start + grid.list_rows, :] = numbers.astype(jnp.float32).astype(head.dtype)
-
-
-def pack(grid, mask, cols, prolong):
+        for place, k in enumerate(blocks):
+            grid.part(out, len(blocks), i, place)[...] = keep(
+                grid, mask, lambda e, i=i: prolong[i, :, e * width:(e + 1) * width], i, k)
+    if passed:
+        refs[-6][...] = refs[0][...]
+        line = lax.broadcasted_iota(jnp.int32, (grid.list_rows, width), 0)
+        column = lax.broadcasted_iota(jnp.int32, (grid.list_rows, width), 1)
+        numbers = jnp.zeros((grid.list_rows, width), jnp.int32)
+        for panel in range(grid.panels):
+            for entry in range(grid.cap):
+                numbers = jnp.where((line == panel) & (column == entry), cols[panel, entry], numbers)
+        out[out.shape[0] - grid.list_rows:, :] = numbers.astype(jnp.float32).astype(out.dtype)
+
+
+def pack(grid, blocks, mask, cols, prolong, passed=None, after=()):
     rows, _, width3 = prolong.shape
-    outs = [grid.shape(rows, 2, width3 // 3, 1), grid.shape(rows, 1, width3 // 3)]
+    out = grid.shape(rows, len(blocks), width3 // 3, 0 if passed is None else 1)
+    extra = [] if passed is None else [passed]
     return pl.pallas_call(
-        functools.partial(pack_kernel, grid),
+        functools.partial(pack_kernel, grid, blocks, bool(extra)),
         grid=(1,),
-        in_specs=[pl.BlockSpec(memory_space=pl.ANY)] * 3,
-        out_specs=[*map(resident, outs)],
+        in_specs=[ANYWHERE] * 3 + [*map(resident, extra)] + [ANYWHERE] * len(after),
+        out_specs=[*map(resident, extra), resident(out)],
         scratch_shapes=[
             pltpu.SMEM(mask.shape, mask.dtype),
             pltpu.SMEM(cols.shape, cols.dtype),
             pltpu.VMEM(prolong.shape, prolong.dtype),
             pltpu.SemaphoreType.DMA((6,)),
         ],
-        out_shape=outs,
+        out_shape=[*[jax.ShapeDtypeStruct(x.shape, x.dtype) for x in extra], out],
         compiler_params=pltpu.CompilerParams(vmem_limit_bytes=PACK_VMEM_LIMIT),
         cost_estimate=COST,
         name="pack_rows",
-    )(mask, cols, prolong)
+    )(mask, cols, prolong, *extra, *after)
 
 
 def turn_kernel(grid, head, tail, turned):
@@ -209,7 +214,7 @@
             out[out.shape[0] - grid.list_rows:, :] = list_at(source)
 
 
-def pick(grid, plan, filled, lists, sources, carry=(), tables=(), passed=None, after=(), cost=COST):
+def pick(grid, plan, filled, lists, sources, carry=(), tables=(), passed=None, after=()):
     flat = [x for source in sources for x, _ in source]
     width = flat[0].shape[-1]
     carry = carry or (None,) * len(filled)
@@ -233,7 +238,7 @@
         ),
         out_shape=shapes,
         compiler_params=PARAMS,
-        cost_estimate=cost,
+        cost_estimate=COST,
         name="pick_rows",
     )(*lists, *flat, *after)
 
@@ -382,10 +387,15 @@
     count = len(sides)
     mids = (1, 2)
 
-    head, tail = pack(grid, prolong_mask.transpose(2, 0, 1), cols_list, prolong_blocks[0])
+    inputs = (prolong_mask.transpose(2, 0, 1), cols_list, prolong_blocks[0])
+    within, across = grid.swaps([(0, 1), (2, 3)]), grid.swaps([(1, 2)])
+    (tail,) = pack(grid, (2,), *inputs)
+    half_tail, other_tail = move(tail, within, inner), move(tail, across, inner)
+    passed_tail, head = pack(grid, (0, 1), *inputs, half_tail, [other_tail])
     own = ((head, 2), (tail, 1))
-    half = move_both(own, grid.swaps([(0, 1), (2, 3)]))
-    other = move_both(own, grid.swaps([(1, 2)]))
+    half = ((move(head, within), 2), (half_tail, 1))
+    other = ((move(head, across), 2), (other_tail, 1))
+    far_tail = move(passed_tail, across, inner)
     side_lists = [move(cols_list, [(b, a) for a, b in grid.across(shift)]) for shift in sides]
 
     def own_requests(z, y):
@@ -394,13 +404,13 @@
     beside = move_across(pick(grid, own_requests, [(3, cap)] * count, side_lists, [own]))
     turned = turn(grid, head, tail)
 
-    far_head = move(half[0][0], grid.swaps([(1, 2)]))
-
     def early_requests(z, y):
         return [(0, grid.panel(grid.lines(z)[1], y, 0), 0, 0, 0)]
 
-    early, end_list = pick(grid, early_requests, [(2, cap), (0, 0)], [], [other[:1], half[:1]], (None, 1), (1,),
-                           cost=EARLY_COST)
+    early, end_list, head = pick(grid, early_requests, [(2, cap), (0, 0)], [], [other[:1], half[:1]], (None, 1), (1,), 1,
+                                 [x for ((x, _),) in beside])
+    far_head = move(head, across)
+    far = ((far_head, 2), (far_tail, 1))
     end_lists = [move(end_list, [(b, a) for a, b in grid.across(shift, mids)]) for shift in sides]
     tables = [(half[0],), *[((x, 0),) for x in end_lists]]
     end_heads = [move(early, grid.ends(0))]
@@ -415,35 +425,33 @@
         return requests
 
     picked = pick(grid, near_requests, [(3, cap)] * (2 * count) + [(2, cap)] * count, side_lists,
-                  [half, other, other[:1], *tables], tables=tuple(range(3, 4 + count)),
-                  after=[x for ((x, _),) in beside], cost=NEAR_COST)
+                  [half, other, other[:1], *tables], tables=tuple(range(3, 4 + count)))
     half_crossed = move_across(picked)
     other_crossed = move_across(picked[count:], mids)
     end_heads += [move(x, grid.ends(shift)) for x, shift in zip(picked[2 * count:], sides)]
-    far_tail = move(half[1][0], grid.swaps([(1, 2)]), inner)
-    far = ((far_head, 2), (far_tail, 1))
-    parts = stage(grid, grid.work_near, lists, turned, matrix, [own, half, *beside])
-
-    def far_requests(z, y):
-        return [(index, grid.panel(grid.lines(z)[2], y, 0), 0, index, 0) for index in range(columns)]
-
-    picked = pick(grid, far_requests, [(2, cap)] * columns, [], [far[:1], *tables], tables=tuple(range(1, 2 + count)),
-                  cost=FAR_COST)
-    far_heads = [move(x, grid.ends(shift)) for shift, x in enumerate(picked)]
 
     def last_requests(z, y):
         _, line_other, line_far = grid.lines(z)
-        requests = [(index, grid.panel(line_far, y, 0), 0, index, 0) for index in range(count)]
+        requests = []
         for index in range(columns):
-            requests += [(count + index, grid.panel(line_other, y, 0), 1, count + index, 0),
-                         (count + index, grid.panel(line_far, y, 0), 2, count + index, cap)]
+            requests += [(index, grid.panel(line_other, y, 0), 0, index, 0),
+                         (index, grid.panel(line_far, y, 0), 1, index, cap)]
         return requests
 
-    picked = pick(grid, last_requests, [(3, cap)] * count + [(1, 2 * cap)] * columns, side_lists,
-                  [far, other[1:], far[1:], *tables], tables=tuple(range(3, 4 + count)), after=[parts[0]],
-                  cost=PICK_COST)
+    picked = pick(grid, last_requests, [(1, 2 * cap)] * columns, [], [other[1:], far[1:], *tables],
+                  tables=tuple(range(2, 3 + count)), after=picked[:1])
+    end_tails = [move(x, grid.ends(shift), inner) for shift, x in enumerate(picked)]
+    parts = stage(grid, grid.work_near, lists, turned, matrix, [own, half, *beside], (), picked[:1])
+
+    def far_requests(z, y):
+        row = grid.panel(grid.lines(z)[2], y, 0)
+        return ([(index, row, 0, index, 0) for index in range(count)] +
+                [(count + index, row, 1, count + index, 0) for index in range(columns)])
+
+    picked = pick(grid, far_requests, [(3, cap)] * count + [(2, cap)] * columns, side_lists, [far, far[:1], *tables],
+                  tables=tuple(range(2, 3 + count)), after=[parts[0]])
     far_crossed = move_across(picked, mids)
-    end_tails = [move(x, grid.ends(shift), inner) for shift, x in enumerate(picked[count:])]
+    far_heads = [move(x, grid.ends(shift)) for shift, x in enumerate(picked[count:])]
     end = [((x, 2), (last, 1, 0)) for x, last in zip(end_heads, end_tails)]
     far_end = [((x, 2), (last, 1, cap)) for x, last in zip(far_heads, end_tails)]
     sources = [other, end[0]]

time: 127 us -> 140 us (1.10); the launches traced: 126 us -> 137 us
  starting transfers between devices: 32.1 us -> 43.9 us
  waiting for transfers between devices: 68.7 us -> 65.1 us
  Pallas kernels: 22.5 us -> 25.8 us
    ppermute x2, starting transfers between devices: 4.43 us -> 15.4 us  [exchange(): lax.ppermute(parts[1], 'rows', [(g, g + 1) for g in range(groups - 1)])]
    ppermute x18, waiting for transfers between devices: 59.1 us -> 50.7 us  [move(): return lax.ppermute(x, ('blk', 'rows'), perm) if perm else jnp.zeros_like(x)]
    ppermute x2, waiting for transfers between devices: 1.72 us -> 5.53 us  [exchange(): lax.ppermute(parts[1], 'rows', [(g, g + 1) for g in range(groups - 1)])]
    pallas_call x1 -> x2, Pallas kernels: 2.64 us -> 5.9 us  [pack(): pl.pallas_call(functools.partial(pack_kernel, grid, blocks, bool(extra)),...]
  transfers between devices with their start and end apart: 22 -> 22, of which waited for: 11 -> 10; matrix products, arithmetic and copies ran while one was open for 0% -> 0% of each run, Pallas kernels for 11% -> 10%
where the time goes in v10:
time: 140 us; the launch traced here: 137 us
  waiting for transfers between devices  65.1 us (46%)
  starting transfers between devices  43.9 us (31%)
  Pallas kernels  25.8 us (18%)
  local copies, waits for them, and re-layouts  2.06 us (1%)
    ppermute x18, waiting for transfers between devices, move(): return lax.ppermute(x, ('blk', 'rows'), perm) if perm else jnp.zeros_like(x)  50.7 us
    ppermute x18, starting transfers between devices, move(): return lax.ppermute(x, ('blk', 'rows'), perm) if perm else jnp.zeros_like(x)  24.6 us
    ppermute x2, starting transfers between devices, exchange(): lax.ppermute(parts[1], 'rows', [(g, g + 1) for g in range(groups - 1)])  15.4 us
    pallas_call x3, Pallas kernels, stage(): pl.pallas_call(functools.partial(stage_kernel, grid, plan, layout, carrie...  11.5 us
    ppermute x2, waiting for transfers between devices, exchange(): lax.ppermute(parts[2], 'rows', [(g + 1, g) for g in range(groups - 1)])  8.8 us
    pallas_call x2, Pallas kernels, pack(): pl.pallas_call(functools.partial(pack_kernel, grid, blocks, bool(extra)),...  5.9 us
    ppermute x2, waiting for transfers between devices, exchange(): lax.ppermute(parts[1], 'rows', [(g, g + 1) for g in range(groups - 1)])  5.53 us
    pallas_call x5, Pallas kernels, pick(): pl.pallas_call(functools.partial(pick_kernel, grid, plan, layout, carry,...  5.47 us
  transfers between devices with their start and end apart: 22, of which 10 were waited for; matrix products, arithmetic and copies ran while one was open for 0% of the time, Pallas kernels for 10%

profile of v10, /device:TPU:1, one launch (start us, length us, event | category | flops | bytes accessed | tf_op | source)
XLA Modules:
  0.0 137.2 jit_solution(3419634378899769972)
XLA Ops:
  0.0 2.2 %pack_rows.2.tail.refs_2_.refs_1_ = bf16[2048,128]{1,0:T(8,128)(2,1)} custom-call(s32[3,1,16]{2,1,0:T(1,128)} %bitcast.28, s32[8,8]{1,0:T(8,128)} %bitcast.14, bf16[16,128,384]{2,1,0:T(8,128)(2,1)} %bitcast.26), custom_call_target="tpu_custom_call" | custom-call | flops 1024 | bytes 1024 | tf_op jit(solution)/shard_map/pack_rows/pallas_call | solution.py:138
  2.2 0.0 copy-start.8
  2.3 0.8 collective-permute-start.1
  3.1 6.5 %collective-permute-start = (bf16[2048,128]{1,0:T(8,128)(2,1)}, bf16[2048,128]{1,0:T(8,128)(2,1)S(1)}, u32[]{:S(2)}, u32[]{:S(2)}) collective-permute-start(bf16[2048,128]{1,0:T(8,128)(2,1)} %pack_rows.2.tail.refs_2_.refs_1_), channel_id=1, source_target_pairs={{1,9},{5,13},{17,25},{21,29},{9,1},{13,5},{25,17},{29,21},{2,10},{... | collective-permute-start | bytes 1572872 | tf_op jit(solution)/shard_map/ppermute | solution.py:374
  9.6 0.0 collective-permute-done.1.refs_1_.refs_4_.refs_0_
  9.7 0.0 copy-start.3
  9.7 10.1 %collective-permute-done.refs_0_.refs_2_.refs_3_ = bf16[2048,128]{1,0:T(8,128)(2,1)S(1)} collective-permute-done((bf16[2048,128]{1,0:T(8,128)(2,1)}, bf16[2048,128]{1,0:T(8,128)(2,1)S(1)}, u32[]{:S(2)}, u32[]{:S(2)}) %collective-permute-start) | collective-permute-done | bytes 524320 | tf_op jit(solution)/shard_map/ppermute | solution.py:374
  19.8 0.8 copy-done.6
  20.5 3.7 %pack_rows.3 = (bf16[2048,128]{1,0:T(8,128)(2,1)}, bf16[4112,128]{1,0:T(8,128)(2,1)}) custom-call(s32[3,1,16]{2,1,0:T(1,128)} %bitcast.29, s32[8,8]{1,0:T(8,128)} %bitcast.15, bf16[16,128,384]{2,1,0:T(8,128)(2,1)} %bitcast.27, bf16[2048,128]{1,0:T(8,128)(2,1)} %copy-done.6, bf16[2048,128]{1,0:T(8,128)(2,1)} %copy-done.3), custom_call_target="tpu_custom_call" | custom-call | flops 1024 | bytes 1024 | tf_op jit(solution)/shard_map/pack_rows/pallas_call | solution.py:138
  24.2 1.2 collective-permute-start.3
  25.4 0.7 collective-permute-start.2
  26.2 1.3 collective-permute-start.4
  27.5 1.6 %collective-permute-done.4.refs_0_ = s32[8,8]{1,0:T(8,128)S(1)} collective-permute-done((s32[8,8]{1,0:T(8,128)S(1)}, s32[8,8]{1,0:T(8,128)S(1)}, u32[]{:S(2)}, u32[]{:S(2)}) %collective-permute-start.4) | collective-permute-done | bytes 288 | tf_op jit(solution)/shard_map/ppermute | solution.py:374
  29.1 1.2 copy-done.1
  30.3 0.7 pick_rows.5
  31.0 1.3 collective-permute-start.5
  32.3 10.3 %collective-permute-done.5.refs_2_.refs_4_ = bf16[3072,128]{1,0:T(8,128)(2,1)S(1)} collective-permute-done((bf16[3072,128]{1,0:T(8,128)(2,1)S(1)}, bf16[3072,128]{1,0:T(8,128)(2,1)S(1)}, u32[]{:S(2)}, u32[]{:S(2)}) %collective-permute-start.5) | collective-permute-done | bytes 786464 | tf_op jit(solution)/shard_map/ppermute | solution.py:374
  42.6 0.0 collective-permute-done.3.refs_1_.refs_6_.refs_2_.refs_4_
  42.6 0.0 collective-permute-done.2.refs_0_.refs_3_.refs_5_
  42.6 0.8 pick_rows.6
  43.4 0.7 collective-permute-start.15
  44.2 0.7 collective-permute-start.7
  44.9 1.3 collective-permute-start.6
  46.2 0.7 collective-permute-start.8
  46.9 0.0 collective-permute-done.8.refs_7_.refs_3_.refs_5_
  46.9 1.6 %pick_rows.7 = (bf16[3072,128]{1,0:T(8,128)(2,1)S(1)}, bf16[3072,128]{1,0:T(8,128)(2,1)S(1)}, bf16[2048,128]{1,0:T(8,128)(2,1)S(1)}) custom-call(s32[8,8]{1,0:T(8,128)S(1)} %collective-permute-done.4.refs_0_, bf16[4112,128]{1,0:T(8,128)(2,1)S(1)} %collective-permute-done.3.refs_1_.refs_6_.refs_2_.refs_4_, bf16[2048,128]{1,0:T(8,128)(2,1)S(1)} %copy-done.7, ...), custom_call_target="tpu_custom_call" | custom-call | flops 1024 | bytes 1024 | tf_op jit(solution)/shard_map/pick_rows/pallas_call | solution.py:230
  48.5 1.3 collective-permute-start.11
  49.8 0.7 collective-permute-start.10
  50.5 0.0 collective-permute-done.7.refs_1_.refs_2_
  50.5 0.0 copy-start.2
  50.5 1.3 collective-permute-start.17
  51.8 0.9 pick_rows.8
  52.7 7.6 %collective-permute-done.6.refs_2_ = bf16[2048,128]{1,0:T(8,128)(2,1)S(1)} collective-permute-done((bf16[2048,128]{1,0:T(8,128)(2,1)S(1)}, bf16[2048,128]{1,0:T(8,128)(2,1)S(1)}, u32[]{:S(2)}, u32[]{:S(2)}) %collective-permute-start.6) | collective-permute-done | bytes 524320 | tf_op jit(solution)/shard_map/ppermute | solution.py:374
  60.3 1.3 collective-permute-start.12
  61.6 0.0 collective-permute-done.15.refs_1_.refs_3_.refs_0_
  61.6 0.0 copy-start
  61.6 0.0 copy-start.9
  61.6 0.0 copy-start.10
  61.6 1.4 %collective-permute-start.9 = (bf16[2048,128]{1,0:T(8,128)(2,1)S(1)}, bf16[2048,128]{1,0:T(8,128)(2,1)S(1)}, u32[]{:S(2)}, u32[]{:S(2)}) collective-permute-start(bf16[2048,128]{1,0:T(8,128)(2,1)S(1)} %get-tuple-element.32.refs_5_), channel_id=1, source_target_pairs={{9,1},{13,5},{17,25},{21,29},{10,2},{14,6},{18,26},{22,30}} | collective-permute-start | bytes 1572872 | tf_op jit(solution)/shard_map/ppermute | solution.py:374
  63.0 0.5 turn_rows.1.turned
  63.5 5.3 %stage_products.3 = (bf16[3,3,128,128]{3,2,1,0:T(8,128)(2,1)S(1)}, bf16[3,3,128,128]{3,2,1,0:T(8,128)(2,1)S(1)}, bf16[3,3,128,128]{3,2,1,0:T(8,128)(2,1)S(1)}) custom-call(s32[8,8]{1,0:T(8,128)S(1)} %bitcast.20, s32[8,8]{1,0:T(8,128)S(1)} %bitcast.17, s32[1,8]{1,0:T(1,128)S(1)} %bitcast.23, bf16[16,384,128]{2,1,0:T(8,128)(2,1)S(1)} %turn_rows.1.turned, ...), custom_call_target="tpu_custom_call" | custom-call | flops 1024 | bytes 1024 | tf_op jit(solution)/shard_map/stage_products/pallas_call | solution.py:309
  68.8 1.6 %pick_rows.9 = (bf16[3072,128]{1,0:T(8,128)(2,1)S(1)}, bf16[2048,128]{1,0:T(8,128)(2,1)S(1)}, bf16[2048,128]{1,0:T(8,128)(2,1)S(1)}) custom-call(s32[8,8]{1,0:T(8,128)S(1)} %collective-permute-done.4.refs_0_, bf16[4112,128]{1,0:T(8,128)(2,1)S(1)} %collective-permute-done.15.refs_1_.refs_3_.refs_0_, ...), custom_call_target="tpu_custom_call" | custom-call | flops 1024 | bytes 1024 | tf_op jit(solution)/shard_map/pick_rows/pallas_call | solution.py:230
  70.4 0.0 collective-permute-done.11.refs_5_
  70.4 0.7 collective-permute-start.18
  71.1 14.8 %collective-permute-done.12.refs_6_.refs_7_ = bf16[2048,128]{1,0:T(8,128)(2,1)S(1)} collective-permute-done((bf16[2048,128]{1,0:T(8,128)(2,1)S(1)}, bf16[2048,128]{1,0:T(8,128)(2,1)S(1)}, u32[]{:S(2)}, u32[]{:S(2)}) %collective-permute-start.12) | collective-permute-done | bytes 524320 | tf_op jit(solution)/shard_map/ppermute | solution.py:374
  85.9 1.3 collective-permute-start.16
  87.2 6.3 %collective-permute-done.9.refs_3_ = bf16[2048,128]{1,0:T(8,128)(2,1)S(1)} collective-permute-done((bf16[2048,128]{1,0:T(8,128)(2,1)S(1)}, bf16[2048,128]{1,0:T(8,128)(2,1)S(1)}, u32[]{:S(2)}, u32[]{:S(2)}) %collective-permute-start.9) | collective-permute-done | bytes 524320 | tf_op jit(solution)/shard_map/ppermute | solution.py:374
  93.5 1.3 collective-permute-start.19
  94.8 0.0 collective-permute-done.10.refs_4_
  94.8 3.5 %stage_products.4 = (bf16[5,3,128,128]{3,2,1,0:T(8,128)(2,1)S(1)}, bf16[5,3,128,128]{3,2,1,0:T(8,128)(2,1)S(1)}, bf16[5,3,128,128]{3,2,1,0:T(8,128)(2,1)S(1)}) custom-call(s32[8,8]{1,0:T(8,128)S(1)} %bitcast.21, s32[8,8]{1,0:T(8,128)S(1)} %bitcast.18, s32[1,8]{1,0:T(1,128)S(1)} %bitcast.24, bf16[16,384,128]{2,1,0:T(8,128)(2,1)S(1)} %turn_rows.1.turned, ...), custom_call_target="tpu_custom_call" | custom-call | flops 1024 | bytes 1024 | tf_op jit(solution)/shard_map/stage_products/pallas_call | solution.py:309
  98.4 12.4 %collective-permute-start.13 = (bf16[5,3,128,128]{3,2,1,0:T(8,128)(2,1)S(1)}, bf16[5,3,128,128]{3,2,1,0:T(8,128)(2,1)S(1)}, u32[]{:S(2)}, u32[]{:S(2)}) collective-permute-start(bf16[5,3,128,128]{3,2,1,0:T(8,128)(2,1)S(1)} %get-tuple-element.40), channel_id=1, source_target_pairs={{0,1},{1,2},{2,3},{4,5},{5,6},{6,7},{8,9},{9,10},{10,11},{12,13},{... | collective-permute-start | bytes 1474568 | tf_op jit(solution)/shard_map/ppermute | solution.py:383
  110.8 0.0 collective-permute-done.17.refs_4_
  110.8 1.9 %collective-permute-start.14 = (bf16[5,3,128,128]{3,2,1,0:T(8,128)(2,1)S(1)}, bf16[5,3,128,128]{3,2,1,0:T(8,128)(2,1)S(1)}, u32[]{:S(2)}, u32[]{:S(2)}) collective-permute-start(bf16[5,3,128,128]{3,2,1,0:T(8,128)(2,1)S(1)} %get-tuple-element.41), channel_id=1, source_target_pairs={{1,0},{2,1},{3,2},{5,4},{6,5},{7,6},{9,8},{10,9},{11,10},{13,12},{... | collective-permute-start | bytes 1474568 | tf_op jit(solution)/shard_map/ppermute | solution.py:384
  112.8 3.8 %collective-permute-done.13.refs_8_.refs_1_ = bf16[5,3,128,128]{3,2,1,0:T(8,128)(2,1)S(1)} collective-permute-done((bf16[5,3,128,128]{3,2,1,0:T(8,128)(2,1)S(1)}, bf16[5,3,128,128]{3,2,1,0:T(8,128)(2,1)S(1)}, u32[]{:S(2)}, u32[]{:S(2)}) %collective-permute-start.13) | collective-permute-done | bytes 491552 | tf_op jit(solution)/shard_map/ppermute | solution.py:383
  116.6 4.4 %collective-permute-done.14.refs_9_.refs_2_ = bf16[5,3,128,128]{3,2,1,0:T(8,128)(2,1)S(1)} collective-permute-done((bf16[5,3,128,128]{3,2,1,0:T(8,128)(2,1)S(1)}, bf16[5,3,128,128]{3,2,1,0:T(8,128)(2,1)S(1)}, u32[]{:S(2)}, u32[]{:S(2)}) %collective-permute-start.14) | collective-permute-done | bytes 491552 | tf_op jit(solution)/shard_map/ppermute | solution.py:384
  121.0 0.0 collective-permute-done.16.refs_2_
  121.0 0.0 collective-permute-done.19.refs_6_
  121.0 0.0 collective-permute-done.18.refs_5_
  121.0 2.7 %stage_products.5 = (bf16[3,3,128,128]{3,2,1,0:T(8,128)(2,1)S(1)}, bf16[3,3,128,128]{3,2,1,0:T(8,128)(2,1)S(1)}, bf16[3,3,128,128]{3,2,1,0:T(8,128)(2,1)S(1)}) custom-call(s32[8,8]{1,0:T(8,128)S(1)} %bitcast.22, s32[8,8]{1,0:T(8,128)S(1)} %bitcast.19, s32[1,8]{1,0:T(1,128)S(1)} %bitcast.25, bf16[16,384,128]{2,1,0:T(8,128)(2,1)S(1)} %turn_rows.1.turned, ...), custom_call_target="tpu_custom_call" | custom-call | flops 1024 | bytes 1024 | tf_op jit(solution)/shard_map/stage_products/pallas_call | solution.py:309
  123.7 3.0 %collective-permute-start.20 = (bf16[3,3,128,128]{3,2,1,0:T(8,128)(2,1)S(1)}, bf16[3,3,128,128]{3,2,1,0:T(8,128)(2,1)S(1)}, u32[]{:S(2)}, u32[]{:S(2)}) collective-permute-start(bf16[3,3,128,128]{3,2,1,0:T(8,128)(2,1)S(1)} %get-tuple-element.47), channel_id=1, source_target_pairs={{0,1},{1,2},{2,3},{4,5},{5,6},{6,7},{8,9},{9,10},{10,11},{12,13},{... | collective-permute-start | bytes 884744 | tf_op jit(solution)/shard_map/ppermute | solution.py:383
  126.7 1.9 %collective-permute-start.21 = (bf16[3,3,128,128]{3,2,1,0:T(8,128)(2,1)S(1)}, bf16[3,3,128,128]{3,2,1,0:T(8,128)(2,1)S(1)}, u32[]{:S(2)}, u32[]{:S(2)}) collective-permute-start(bf16[3,3,128,128]{3,2,1,0:T(8,128)(2,1)S(1)} %get-tuple-element.48), channel_id=1, source_target_pairs={{1,0},{2,1},{3,2},{5,4},{6,5},{7,6},{9,8},{10,9},{11,10},{13,12},{... | collective-permute-start | bytes 884744 | tf_op jit(solution)/shard_map/ppermute | solution.py:384
  128.6 1.7 %collective-permute-done.20.refs_4_ = bf16[3,3,128,128]{3,2,1,0:T(8,128)(2,1)S(1)} collective-permute-done((bf16[3,3,128,128]{3,2,1,0:T(8,128)(2,1)S(1)}, bf16[3,3,128,128]{3,2,1,0:T(8,128)(2,1)S(1)}, u32[]{:S(2)}, u32[]{:S(2)}) %collective-permute-start.20) | collective-permute-done | bytes 294944 | tf_op jit(solution)/shard_map/ppermute | solution.py:383
  130.4 4.4 %collective-permute-done.21.refs_5_ = bf16[3,3,128,128]{3,2,1,0:T(8,128)(2,1)S(1)} collective-permute-done((bf16[3,3,128,128]{3,2,1,0:T(8,128)(2,1)S(1)}, bf16[3,3,128,128]{3,2,1,0:T(8,128)(2,1)S(1)}, u32[]{:S(2)}, u32[]{:S(2)}) %collective-permute-start.21) | collective-permute-done | bytes 294944 | tf_op jit(solution)/shard_map/ppermute | solution.py:384
  134.8 2.5 %assemble_coarse.1 = f32[5120,128]{1,0:T(8,128)} custom-call(bf16[5,3,128,128]{3,2,1,0:T(8,128)(2,1)S(1)} %get-tuple-element.39.refs_0_, bf16[5,3,128,128]{3,2,1,0:T(8,128)(2,1)S(1)} %collective-permute-done.13.refs_8_.refs_1_, bf16[5,3,128,128]{3,2,1,0:T(8,128)(2,1)S(1)} %collective-permute-done.14.refs_9_.refs_2_, ...), custom_call_target="tpu_custom_call" | custom-call | flops 1024 | bytes 1024 | tf_op jit(solution)/shard_map/assemble_coarse/pallas_call | solution.py:350
  (16 shorter events, 0.0 us)
Async XLA Ops:
  2.2 23.9 %copy-start.8 = (s32[1,1,8,8]{3,2,1,0:T(8,128)S(1)}, s32[1,1,8,8]{3,2,1,0:T(8,128)}, u32[]{:S(2)}) copy-start(s32[1,1,8,8]{3,2,1,0:T(8,128)} %param.8) | copy-start | bytes 772
  2.3 26.9 %copy-start.5 = (bf16[2048,128]{1,0:T(8,128)(2,1)S(1)}, bf16[2048,128]{1,0:T(8,128)(2,1)}, u32[]{:S(2)}) copy-start(bf16[2048,128]{1,0:T(8,128)(2,1)} %pack_rows.2.tail.refs_2_.refs_1_) | copy-start | bytes 1572868
  2.3 7.4 %collective-permute-start.1 = (bf16[2048,128]{1,0:T(8,128)(2,1)}, bf16[2048,128]{1,0:T(8,128)(2,1)S(1)}, u32[]{:S(2)}, u32[]{:S(2)}) collective-permute-start(bf16[2048,128]{1,0:T(8,128)(2,1)} %pack_rows.2.tail.refs_2_.refs_1_), channel_id=1, source_target_pairs={{9,17},{13,21},{17,9},{21,13},{10,18},{14,22},{18,10},{22,14}} | collective-permute-start | bytes 1572872 | tf_op jit(solution)/shard_map/ppermute | solution.py:374
  3.1 16.7 %collective-permute-start = (bf16[2048,128]{1,0:T(8,128)(2,1)}, bf16[2048,128]{1,0:T(8,128)(2,1)S(1)}, u32[]{:S(2)}, u32[]{:S(2)}) collective-permute-start(bf16[2048,128]{1,0:T(8,128)(2,1)} %pack_rows.2.tail.refs_2_.refs_1_), channel_id=1, source_target_pairs={{1,9},{5,13},{17,25},{21,29},{9,1},{13,5},{25,17},{29,21},{2,10},{... | collective-permute-start | bytes 1572872 | tf_op jit(solution)/shard_map/ppermute | solution.py:374
  9.7 10.1 %copy-start.3 = (bf16[2048,128]{1,0:T(8,128)(2,1)}, bf16[2048,128]{1,0:T(8,128)(2,1)S(1)}, u32[]{:S(2)}) copy-start(bf16[2048,128]{1,0:T(8,128)(2,1)S(1)} %collective-permute-done.1.refs_1_.refs_4_.refs_0_) | copy-start | bytes 1572868
  19.8 0.8 copy-start.6
  24.2 18.4 %collective-permute-start.3 = (bf16[4112,128]{1,0:T(8,128)(2,1)}, bf16[4112,128]{1,0:T(8,128)(2,1)S(1)}, u32[]{:S(2)}, u32[]{:S(2)}) collective-permute-start(bf16[4112,128]{1,0:T(8,128)(2,1)} %get-tuple-element.27.head.refs_1_.refs_0_), channel_id=1, source_target_pairs={{0,8},{4,12},{16,24},{20,28},{8,0},{12,4},{24,16},{28,20},{1,9},{5... | collective-permute-start | bytes 3158024 | tf_op jit(solution)/shard_map/ppermute | solution.py:374
  25.4 17.2 %collective-permute-start.2 = (bf16[4112,128]{1,0:T(8,128)(2,1)}, bf16[4112,128]{1,0:T(8,128)(2,1)S(1)}, u32[]{:S(2)}, u32[]{:S(2)}) collective-permute-start(bf16[4112,128]{1,0:T(8,128)(2,1)} %get-tuple-element.27.head.refs_1_.refs_0_), channel_id=1, source_target_pairs={{8,16},{12,20},{16,8},{20,12},{9,17},{13,21},{17,9},{21,13},{10,18... | collective-permute-start | bytes 3158024 | tf_op jit(solution)/shard_map/ppermute | solution.py:374
  26.2 2.9 %collective-permute-start.4 = (s32[8,8]{1,0:T(8,128)S(1)}, s32[8,8]{1,0:T(8,128)S(1)}, u32[]{:S(2)}, u32[]{:S(2)}) collective-permute-start(s32[8,8]{1,0:T(8,128)S(1)} %bitcast.16), channel_id=1, source_target_pairs={{4,0},{0,4},{12,8},{8,12},{20,16},{16,20},{28,24},{24,28},{5,1},{1... | collective-permute-start | bytes 776 | tf_op jit(solution)/shard_map/ppermute | solution.py:374
  29.1 1.2 copy-start.1
  31.0 13.2 %copy-start.11 = (bf16[2048,128]{1,0:T(8,128)(2,1)S(1)}, bf16[2048,128]{1,0:T(8,128)(2,1)}, u32[]{:S(2)}) copy-start(bf16[2048,128]{1,0:T(8,128)(2,1)} %get-tuple-element.29) | copy-start | bytes 1572868
  31.0 15.8 %copy-start.4 = (bf16[2048,128]{1,0:T(8,128)(2,1)S(1)}, bf16[2048,128]{1,0:T(8,128)(2,1)}, u32[]{:S(2)}) copy-start(bf16[2048,128]{1,0:T(8,128)(2,1)} %copy-done.3) | copy-start | bytes 1572868
  31.0 15.8 %copy-start.7 = (bf16[2048,128]{1,0:T(8,128)(2,1)S(1)}, bf16[2048,128]{1,0:T(8,128)(2,1)}, u32[]{:S(2)}) copy-start(bf16[2048,128]{1,0:T(8,128)(2,1)} %copy-done.6) | copy-start | bytes 1572868
  31.0 11.6 %collective-permute-start.5 = (bf16[3072,128]{1,0:T(8,128)(2,1)S(1)}, bf16[3072,128]{1,0:T(8,128)(2,1)S(1)}, u32[]{:S(2)}, u32[]{:S(2)}) collective-permute-start(bf16[3072,128]{1,0:T(8,128)(2,1)S(1)} %pick_rows.5), channel_id=1, source_target_pairs={{0,4},{4,0},{8,12},{12,8},{16,20},{20,16},{24,28},{28,24},{1,5},{5... | collective-permute-start | bytes 2359304 | tf_op jit(solution)/shard_map/ppermute | solution.py:374
  43.4 18.1 %collective-permute-start.15 = (bf16[4112,128]{1,0:T(8,128)(2,1)S(1)}, bf16[4112,128]{1,0:T(8,128)(2,1)S(1)}, u32[]{:S(2)}, u32[]{:S(2)}) collective-permute-start(bf16[4112,128]{1,0:T(8,128)(2,1)S(1)} %get-tuple-element.42), channel_id=1, source_target_pairs={{8,16},{12,20},{16,8},{20,12},{9,17},{13,21},{17,9},{21,13},{10,18... | collective-permute-start | bytes 3158024 | tf_op jit(solution)/shard_map/ppermute | solution.py:374
  44.2 6.3 %collective-permute-start.7 = (bf16[2048,128]{1,0:T(8,128)(2,1)S(1)}, bf16[2048,128]{1,0:T(8,128)(2,1)S(1)}, u32[]{:S(2)}, u32[]{:S(2)}) collective-permute-start(bf16[2048,128]{1,0:T(8,128)(2,1)S(1)} %copy-done.11), channel_id=1, source_target_pairs={{9,17},{13,21},{17,9},{21,13},{10,18},{14,22},{18,10},{22,14}} | collective-permute-start | bytes 1572872 | tf_op jit(solution)/shard_map/ppermute | solution.py:374
  44.9 15.4 %collective-permute-start.6 = (bf16[2048,128]{1,0:T(8,128)(2,1)S(1)}, bf16[2048,128]{1,0:T(8,128)(2,1)S(1)}, u32[]{:S(2)}, u32[]{:S(2)}) collective-permute-start(bf16[2048,128]{1,0:T(8,128)(2,1)S(1)} %get-tuple-element.28), channel_id=1, source_target_pairs={{8,0},{12,4},{16,24},{20,28},{9,1},{13,5},{17,25},{21,29},{10,2},{... | collective-permute-start | bytes 1572872 | tf_op jit(solution)/shard_map/ppermute | solution.py:374
  46.2 0.7 collective-permute-start.8
  48.5 21.9 %collective-permute-start.11 = (bf16[2048,128]{1,0:T(8,128)(2,1)S(1)}, bf16[2048,128]{1,0:T(8,128)(2,1)S(1)}, u32[]{:S(2)}, u32[]{:S(2)}) collective-permute-start(bf16[2048,128]{1,0:T(8,128)(2,1)S(1)} %get-tuple-element.34), channel_id=1, source_target_pairs={{8,4},{12,0},{16,28},{20,24},{9,5},{13,1},{17,29},{21,25},{10,6},{... | collective-permute-start | bytes 1572872 | tf_op jit(solution)/shard_map/ppermute | solution.py:374
  49.8 45.1 %collective-permute-start.10 = (bf16[3072,128]{1,0:T(8,128)(2,1)S(1)}, bf16[3072,128]{1,0:T(8,128)(2,1)S(1)}, u32[]{:S(2)}, u32[]{:S(2)}) collective-permute-start(bf16[3072,128]{1,0:T(8,128)(2,1)S(1)} %get-tuple-element.33), channel_id=1, source_target_pairs={{8,12},{12,8},{16,20},{20,16},{9,13},{13,9},{17,21},{21,17},{10,14... | collective-permute-start | bytes 2359304 | tf_op jit(solution)/shard_map/ppermute | solution.py:374
  50.5 12.5 %copy-start.2 = (bf16[4112,128]{1,0:T(8,128)(2,1)S(1)}, bf16[4112,128]{1,0:T(8,128)(2,1)}, u32[]{:S(2)}) copy-start(bf16[4112,128]{1,0:T(8,128)(2,1)} %get-tuple-element.27.head.refs_1_.refs_0_) | copy-start | bytes 3158020
  50.5 60.3 %collective-permute-start.17 = (bf16[3072,128]{1,0:T(8,128)(2,1)S(1)}, bf16[3072,128]{1,0:T(8,128)(2,1)S(1)}, u32[]{:S(2)}, u32[]{:S(2)}) collective-permute-start(bf16[3072,128]{1,0:T(8,128)(2,1)S(1)} %get-tuple-element.31.refs_4_), channel_id=1, source_target_pairs={{0,4},{4,0},{8,12},{12,8},{16,20},{20,16},{24,28},{28,24},{1,5},{5... | collective-permute-start | bytes 2359304 | tf_op jit(solution)/shard_map/ppermute | solution.py:374
  60.3 25.7 %collective-permute-start.12 = (bf16[2048,128]{1,0:T(8,128)(2,1)S(1)}, bf16[2048,128]{1,0:T(8,128)(2,1)S(1)}, u32[]{:S(2)}, u32[]{:S(2)}) collective-permute-start(bf16[2048,128]{1,0:T(8,128)(2,1)S(1)} %get-tuple-element.35), channel_id=1, source_target_pairs={{9,5},{13,1},{17,29},{21,25},{10,6},{14,2},{18,30},{22,26}} | collective-permute-start | bytes 1572872 | tf_op jit(solution)/shard_map/ppermute | solution.py:374
  61.6 1.9 %copy-start = (bf16[1,1,8,8,128,128]{5,4,3,2,1,0:T(8,128)(2,1)S(1)}, bf16[1,1,8,8,128,128]{5,4,3,2,1,0:T(8,128)(2,1)}, u32[]{:S(2)}) copy-start(bf16[1,1,8,8,128,128]{5,4,3,2,1,0:T(8,128)(2,1)} %param.6) | copy-start | bytes 6291460
  61.6 1.9 %copy-start.9 = (s32[1,1,8,8]{3,2,1,0:T(8,128)S(1)}, s32[1,1,8,8]{3,2,1,0:T(8,128)}, u32[]{:S(2)}) copy-start(s32[1,1,8,8]{3,2,1,0:T(8,128)} %param.7) | copy-start | bytes 772
  61.6 1.9 %copy-start.10 = (s32[1,1,8]{2,1,0:T(1,128)S(1)}, s32[1,1,8]{2,1,0:T(1,128)}, u32[]{:S(2)}) copy-start(s32[1,1,8]{2,1,0:T(1,128)} %param.9) | copy-start | bytes 100
  61.6 31.9 %collective-permute-start.9 = (bf16[2048,128]{1,0:T(8,128)(2,1)S(1)}, bf16[2048,128]{1,0:T(8,128)(2,1)S(1)}, u32[]{:S(2)}, u32[]{:S(2)}) collective-permute-start(bf16[2048,128]{1,0:T(8,128)(2,1)S(1)} %get-tuple-element.32.refs_5_), channel_id=1, source_target_pairs={{9,1},{13,5},{17,25},{21,29},{10,2},{14,6},{18,26},{22,30}} | collective-permute-start | bytes 1572872 | tf_op jit(solution)/shard_map/ppermute | solution.py:374
  70.4 50.6 %collective-permute-start.18 = (bf16[3072,128]{1,0:T(8,128)(2,1)S(1)}, bf16[3072,128]{1,0:T(8,128)(2,1)S(1)}, u32[]{:S(2)}, u32[]{:S(2)}) collective-permute-start(bf16[3072,128]{1,0:T(8,128)(2,1)S(1)} %get-tuple-element.44), channel_id=1, source_target_pairs={{8,12},{12,8},{16,20},{20,16},{9,13},{13,9},{17,21},{21,17},{10,14... | collective-permute-start | bytes 2359304 | tf_op jit(solution)/shard_map/ppermute | solution.py:374
  85.9 35.1 %collective-permute-start.16 = (bf16[2048,128]{1,0:T(8,128)(2,1)S(1)}, bf16[2048,128]{1,0:T(8,128)(2,1)S(1)}, u32[]{:S(2)}, u32[]{:S(2)}) collective-permute-start(bf16[2048,128]{1,0:T(8,128)(2,1)S(1)} %get-tuple-element.43), channel_id=1, source_target_pairs={{8,0},{12,4},{16,24},{20,28},{9,1},{13,5},{17,25},{21,29},{10,2},{... | collective-permute-start | bytes 1572872 | tf_op jit(solution)/shard_map/ppermute | solution.py:374
  93.5 27.4 %collective-permute-start.19 = (bf16[2048,128]{1,0:T(8,128)(2,1)S(1)}, bf16[2048,128]{1,0:T(8,128)(2,1)S(1)}, u32[]{:S(2)}, u32[]{:S(2)}) collective-permute-start(bf16[2048,128]{1,0:T(8,128)(2,1)S(1)} %get-tuple-element.45), channel_id=1, source_target_pairs={{8,4},{12,0},{16,28},{20,24},{9,5},{13,1},{17,29},{21,25},{10,6},{... | collective-permute-start | bytes 1572872 | tf_op jit(solution)/shard_map/ppermute | solution.py:374
  98.4 18.2 %collective-permute-start.13 = (bf16[5,3,128,128]{3,2,1,0:T(8,128)(2,1)S(1)}, bf16[5,3,128,128]{3,2,1,0:T(8,128)(2,1)S(1)}, u32[]{:S(2)}, u32[]{:S(2)}) collective-permute-start(bf16[5,3,128,128]{3,2,1,0:T(8,128)(2,1)S(1)} %get-tuple-element.40), channel_id=1, source_target_pairs={{0,1},{1,2},{2,3},{4,5},{5,6},{6,7},{8,9},{9,10},{10,11},{12,13},{... | collective-permute-start | bytes 1474568 | tf_op jit(solution)/shard_map/ppermute | solution.py:383
  110.8 10.1 %collective-permute-start.14 = (bf16[5,3,128,128]{3,2,1,0:T(8,128)(2,1)S(1)}, bf16[5,3,128,128]{3,2,1,0:T(8,128)(2,1)S(1)}, u32[]{:S(2)}, u32[]{:S(2)}) collective-permute-start(bf16[5,3,128,128]{3,2,1,0:T(8,128)(2,1)S(1)} %get-tuple-element.41), channel_id=1, source_target_pairs={{1,0},{2,1},{3,2},{5,4},{6,5},{7,6},{9,8},{10,9},{11,10},{13,12},{... | collective-permute-start | bytes 1474568 | tf_op jit(solution)/shard_map/ppermute | solution.py:384
  123.7 6.7 %collective-permute-start.20 = (bf16[3,3,128,128]{3,2,1,0:T(8,128)(2,1)S(1)}, bf16[3,3,128,128]{3,2,1,0:T(8,128)(2,1)S(1)}, u32[]{:S(2)}, u32[]{:S(2)}) collective-permute-start(bf16[3,3,128,128]{3,2,1,0:T(8,128)(2,1)S(1)} %get-tuple-element.47), channel_id=1, source_target_pairs={{0,1},{1,2},{2,3},{4,5},{5,6},{6,7},{8,9},{9,10},{10,11},{12,13},{... | collective-permute-start | bytes 884744 | tf_op jit(solution)/shard_map/ppermute | solution.py:383
  126.7 8.0 %collective-permute-start.21 = (bf16[3,3,128,128]{3,2,1,0:T(8,128)(2,1)S(1)}, bf16[3,3,128,128]{3,2,1,0:T(8,128)(2,1)S(1)}, u32[]{:S(2)}, u32[]{:S(2)}) collective-permute-start(bf16[3,3,128,128]{3,2,1,0:T(8,128)(2,1)S(1)} %get-tuple-element.48), channel_id=1, source_target_pairs={{1,0},{2,1},{3,2},{5,4},{6,5},{7,6},{9,8},{10,9},{11,10},{13,12},{... | collective-permute-start | bytes 884744 | tf_op jit(solution)/shard_map/ppermute | solution.py:384

commit v11 on v9

--- a/solution.py
+++ b/solution.py
@@ -10,10 +10,7 @@
 PACK_VMEM_LIMIT = 60 * 1024 * 1024
 PARAMS = pltpu.CompilerParams(vmem_limit_bytes=VMEM_LIMIT)
 COST = pl.CostEstimate(flops=1024, bytes_accessed=1024, transcendentals=0)
-EARLY_COST = pl.CostEstimate(flops=1024, bytes_accessed=1024, transcendentals=0)
-FAR_COST = pl.CostEstimate(flops=1024, bytes_accessed=1024, transcendentals=0)
-NEAR_COST = pl.CostEstimate(flops=6 * 10 ** 9, bytes_accessed=1024, transcendentals=0)
-PICK_COST = pl.CostEstimate(flops=2 * 10 ** 10, bytes_accessed=1024, transcendentals=0)
+PICK_COST = pl.CostEstimate(flops=20000000000, bytes_accessed=1024, transcendentals=0)
 ANYWHERE = pl.BlockSpec(memory_space=pl.ANY)
 
 
@@ -74,22 +71,23 @@
                 [(self.panel(z, y, shift), [(1 + shift, False, True)]) for shift in self.sides])
 
     def work_middle(self, z, y):
-        _, other, _ = self.lines(z)
+        half, other, _ = self.lines(z)
         middle = self.middle(z)
         end = jnp.logical_not(middle)
-        return ([(self.panel(other, y, 0), [(0, True, middle), (1, False, end)])] +
-                [(self.panel(other, y, shift), [(2 * shift, False, middle), (2 * shift + 1, False, end)])
-                 for shift in self.sides])
+        work = []
+        for i, shift in enumerate(self.sides):
+            work += [(self.panel(half, y, shift), [(3 * i, False, True)]),
+                     (self.panel(other, y, shift), [(3 * i + 1, False, middle), (3 * i + 2, False, end)])]
+        return work
 
     def work_far(self, z, y):
-        half, _, far = self.lines(z)
+        _, other, far = self.lines(z)
         middle = self.middle(z)
         end = jnp.logical_not(middle)
-        work = [(self.panel(far, y, 0), [(0, True, middle), (1, False, end)])]
-        for i, shift in enumerate(self.sides):
-            work += [(self.panel(half, y, shift), [(2 + 3 * i, False, True)]),
-                     (self.panel(far, y, shift), [(3 + 3 * i, False, middle), (4 + 3 * i, False, end)])]
-        return work
+        return ([(self.panel(other, y, 0), [(0, True, middle), (1, False, end)]),
+                 (self.panel(far, y, 0), [(2, True, middle), (3, False, end)])] +
+                [(self.panel(far, y, shift), [(2 + 2 * shift, False, middle), (3 + 2 * shift, False, end)])
+                 for shift in self.sides])
 
 
 def pack_kernel(grid, mask_from, cols_from, prolong_from, head, tail, mask, cols, prolong, done):
@@ -400,26 +398,29 @@
         return [(0, grid.panel(grid.lines(z)[1], y, 0), 0, 0, 0)]
 
     early, end_list = pick(grid, early_requests, [(2, cap), (0, 0)], [], [other[:1], half[:1]], (None, 1), (1,),
-                           cost=EARLY_COST)
+                           cost=COST)
     end_lists = [move(end_list, [(b, a) for a, b in grid.across(shift, mids)]) for shift in sides]
     tables = [(half[0],), *[((x, 0),) for x in end_lists]]
     end_heads = [move(early, grid.ends(0))]
 
     def near_requests(z, y):
-        line_half, line_other, _ = grid.lines(z)
+        _, line_other, _ = grid.lines(z)
         requests = []
         for index in range(count):
-            requests += [(index, grid.panel(line_half, y, 0), 0, index, 0),
-                         (index, grid.panel(line_other, y, 0), 1, count + index, 0),
-                         (count + 1 + index, grid.panel(line_other, y, 0), 2, 2 * count + index, 0)]
+            requests += [(index, grid.panel(line_other, y, 0), 0, index, 0),
+                         (count + 1 + index, grid.panel(line_other, y, 0), 0, count + index, 0)]
         return requests
 
-    picked = pick(grid, near_requests, [(3, cap)] * (2 * count) + [(2, cap)] * count, side_lists,
-                  [half, other, other[:1], *tables], tables=tuple(range(3, 4 + count)),
-                  after=[x for ((x, _),) in beside], cost=NEAR_COST)
+    picked = pick(grid, near_requests, [(3, cap)] * (2 * count), side_lists, [other, *tables],
+                  tables=tuple(range(1, 2 + count)), after=[x for ((x, _),) in beside], cost=COST)
+    other_crossed = move_across(picked, mids)
+    end_crossed = [((move(x, grid.ends(shift)), 3),) for x, shift in zip(picked[count:], sides)]
+
+    def half_requests(z, y):
+        return [(index, grid.panel(grid.lines(z)[0], y, 0), 0, index, 0) for index in range(count)]
+
+    picked = pick(grid, half_requests, [(3, cap)] * count, side_lists, [half], after=[x for ((x, _),) in other_crossed], cost=COST)
     half_crossed = move_across(picked)
-    other_crossed = move_across(picked[count:], mids)
-    end_heads += [move(x, grid.ends(shift)) for x, shift in zip(picked[2 * count:], sides)]
     far_tail = move(half[1][0], grid.swaps([(1, 2)]), inner)
     far = ((far_head, 2), (far_tail, 1))
     parts = stage(grid, grid.work_near, lists, turned, matrix, [own, half, *beside])
@@ -427,34 +428,32 @@
     def far_requests(z, y):
         return [(index, grid.panel(grid.lines(z)[2], y, 0), 0, index, 0) for index in range(columns)]
 
-    picked = pick(grid, far_requests, [(2, cap)] * columns, [], [far[:1], *tables], tables=tuple(range(1, 2 + count)),
-                  cost=FAR_COST)
-    far_heads = [move(x, grid.ends(shift)) for shift, x in enumerate(picked)]
+    far_picked = pick(grid, far_requests, [(2, cap)] * columns, [], [far[:1], *tables], tables=tuple(range(1, 2 + count)),
+                      after=[parts[0]], cost=COST)
+    far_heads = [move(x, grid.ends(shift)) for shift, x in enumerate(far_picked)]
 
     def last_requests(z, y):
         _, line_other, line_far = grid.lines(z)
-        requests = [(index, grid.panel(line_far, y, 0), 0, index, 0) for index in range(count)]
-        for index in range(columns):
-            requests += [(count + index, grid.panel(line_other, y, 0), 1, count + index, 0),
-                         (count + index, grid.panel(line_far, y, 0), 2, count + index, cap)]
-        return requests
-
-    picked = pick(grid, last_requests, [(3, cap)] * count + [(1, 2 * cap)] * columns, side_lists,
-                  [far, other[1:], far[1:], *tables], tables=tuple(range(3, 4 + count)), after=[parts[0]],
+        row = grid.panel(line_far, y, 0)
+        return ([(index, row, 0, index, 0) for index in range(count)] +
+                [(count, grid.panel(line_other, y, 0), 1, count, 0), (count, row, 2, count, cap)] +
+                [(count + 1 + index, row, 2, count + 1 + index, 0) for index in range(count)])
+
+    picked = pick(grid, last_requests, [(3, cap)] * count + [(1, 2 * cap)] + [(1, cap)] * count, side_lists,
+                  [far, other[1:], far[1:], *tables], tables=tuple(range(3, 4 + count)), after=[*far_picked, end_heads[0], *[x for ((x, _),) in end_crossed], *[x for ((x, _),) in other_crossed]],
                   cost=PICK_COST)
     far_crossed = move_across(picked, mids)
-    end_tails = [move(x, grid.ends(shift), inner) for shift, x in enumerate(picked[count:])]
-    end = [((x, 2), (last, 1, 0)) for x, last in zip(end_heads, end_tails)]
-    far_end = [((x, 2), (last, 1, cap)) for x, last in zip(far_heads, end_tails)]
-    sources = [other, end[0]]
+    end_tail = move(picked[count], grid.ends(0), inner)
+    far_tails = [move(x, grid.ends(shift), inner) for x, shift in zip(picked[count + 1:], sides)]
+    sources = []
     for i in range(count):
-        sources += [other_crossed[i], end[1 + i]]
-    parts = stage(grid, grid.work_middle, lists, turned, matrix, sources, parts)
+        sources += [half_crossed[i], other_crossed[i], end_crossed[i]]
+    parts = stage(grid, grid.work_middle, lists, turned, matrix, sources, parts, far_heads[:1])
     first = exchange(parts)
 
-    sources = [far, far_end[0]]
+    sources = [other, ((end_heads[0], 2), (end_tail, 1, 0)), far, ((far_heads[0], 2), (end_tail, 1, cap))]
     for i in range(count):
-        sources += [half_crossed[i], far_crossed[i], far_end[1 + i]]
+        sources += [far_crossed[i], ((far_heads[1 + i], 2), (far_tails[i], 1))]
     last = exchange(stage(grid, grid.work_far, lists, turned, matrix, sources, (), first[1:]))
     return assemble(grid, ((grid.work_near, grid.work_middle), (grid.work_far,)), [first, last])[None, None]
 

time: 127 us -> 125 us (0.984)
  waiting for transfers between devices: 68.7 us -> 63.5 us
  starting transfers between devices: 32.1 us -> 34.2 us
    ppermute x2, waiting for transfers between devices: 7.92 us -> 4.4 us  [exchange(): lax.ppermute(parts[2], 'rows', [(g + 1, g) for g in range(groups - 1)])]
    ppermute x18, starting transfers between devices: 23.3 us -> 25.5 us  [move(): return lax.ppermute(x, ('blk', 'rows'), perm) if perm else jnp.zeros_like(x)]
    ppermute x18, waiting for transfers between devices: 59.1 us -> 57.6 us  [move(): return lax.ppermute(x, ('blk', 'rows'), perm) if perm else jnp.zeros_like(x)]
    pallas_call x5 -> x6, Pallas kernels: 5.41 us -> 6.03 us  [pick(): pl.pallas_call(functools.partial(pick_kernel, grid, plan, layout, carry,...]
  transfers between devices with their start and end apart: 22 -> 22, of which waited for: 11 -> 9; matrix products, arithmetic and copies ran while one was open for 0% -> 0% of each run, Pallas kernels for 11% -> 12%
where the time goes in v11:
time: 125 us; the launch traced here: 124 us
  waiting for transfers between devices  63.5 us (51%)
  starting transfers between devices  34.2 us (27%)
  Pallas kernels  23.1 us (18%)
  local copies, waits for them, and re-layouts  2.3 us (2%)
    ppermute x18, waiting for transfers between devices, move(): return lax.ppermute(x, ('blk', 'rows'), perm) if perm else jnp.zeros_like(x)  57.6 us
    ppermute x18, starting transfers between devices, move(): return lax.ppermute(x, ('blk', 'rows'), perm) if perm else jnp.zeros_like(x)  25.5 us
    pallas_call x3, Pallas kernels, stage(): pl.pallas_call(functools.partial(stage_kernel, grid, plan, layout, carrie...  11.5 us
    pallas_call x6, Pallas kernels, pick(): pl.pallas_call(functools.partial(pick_kernel, grid, plan, layout, carry,...  6.03 us
    ppermute x2, starting transfers between devices, exchange(): lax.ppermute(parts[2], 'rows', [(g + 1, g) for g in range(groups - 1)])  4.5 us
    ppermute x2, waiting for transfers between devices, exchange(): lax.ppermute(parts[2], 'rows', [(g + 1, g) for g in range(groups - 1)])  4.4 us
    ppermute x2, starting transfers between devices, exchange(): lax.ppermute(parts[1], 'rows', [(g, g + 1) for g in range(groups - 1)])  4.19 us
    pallas_call x1, Pallas kernels, pack(): pl.pallas_call(functools.partial(pack_kernel, grid), grid=(1,), in_specs=...  2.64 us
  transfers between devices with their start and end apart: 22, of which 9 were waited for; matrix products, arithmetic and copies ran while one was open for 0% of the time, Pallas kernels for 12%

profile of v11, /device:TPU:1, one launch (start us, length us, event | category | flops | bytes accessed | tf_op | source)
XLA Modules:
  0.0 123.5 jit_solution(16550432387760289071)
XLA Ops:
  0.0 2.6 %pack_rows.1 = (bf16[4112,128]{1,0:T(8,128)(2,1)}, bf16[2048,128]{1,0:T(8,128)(2,1)}) custom-call(s32[3,1,16]{2,1,0:T(1,128)} %bitcast.26, s32[8,8]{1,0:T(8,128)} %bitcast.14, bf16[16,128,384]{2,1,0:T(8,128)(2,1)} %bitcast.25), custom_call_target="tpu_custom_call" | custom-call | flops 1024 | bytes 1024 | tf_op jit(solution)/shard_map/pack_rows/pallas_call | solution.py:131
  2.6 2.2 %collective-permute-start.1 = (bf16[4112,128]{1,0:T(8,128)(2,1)}, bf16[4112,128]{1,0:T(8,128)(2,1)S(1)}, u32[]{:S(2)}, u32[]{:S(2)}) collective-permute-start(bf16[4112,128]{1,0:T(8,128)(2,1)} %get-tuple-element.25.head.refs_1_.refs_0_), channel_id=1, source_target_pairs={{0,8},{4,12},{16,24},{20,28},{8,0},{12,4},{24,16},{28,20},{1,9},{5... | collective-permute-start | bytes 3158024 | tf_op jit(solution)/shard_map/ppermute | solution.py:367
  4.8 0.7 collective-permute-start.3
  5.6 0.0 copy-done.4
  5.6 1.3 %collective-permute-start = (s32[8,8]{1,0:T(8,128)S(1)}, s32[8,8]{1,0:T(8,128)S(1)}, u32[]{:S(2)}, u32[]{:S(2)}) collective-permute-start(s32[8,8]{1,0:T(8,128)S(1)} %bitcast.15), channel_id=1, source_target_pairs={{4,0},{0,4},{12,8},{8,12},{20,16},{16,20},{28,24},{24,28},{5,1},{1... | collective-permute-start | bytes 776 | tf_op jit(solution)/shard_map/ppermute | solution.py:367
  6.9 1.5 %collective-permute-done.refs_0_ = s32[8,8]{1,0:T(8,128)S(1)} collective-permute-done((s32[8,8]{1,0:T(8,128)S(1)}, s32[8,8]{1,0:T(8,128)S(1)}, u32[]{:S(2)}, u32[]{:S(2)}) %collective-permute-start) | collective-permute-done | bytes 288 | tf_op jit(solution)/shard_map/ppermute | solution.py:367
  8.4 1.2 copy-done.1
  9.6 1.0 copy-done.3
  10.7 0.7 pick_rows.7
  11.3 1.3 %collective-permute-start.6 = (bf16[3072,128]{1,0:T(8,128)(2,1)S(1)}, bf16[3072,128]{1,0:T(8,128)(2,1)S(1)}, u32[]{:S(2)}, u32[]{:S(2)}) collective-permute-start(bf16[3072,128]{1,0:T(8,128)(2,1)S(1)} %pick_rows.7), channel_id=1, source_target_pairs={{0,4},{4,0},{8,12},{12,8},{16,20},{20,16},{24,28},{28,24},{1,5},{5... | collective-permute-start | bytes 2359304 | tf_op jit(solution)/shard_map/ppermute | solution.py:367
  12.6 0.7 collective-permute-start.4
  13.3 14.7 %collective-permute-done.1.refs_1_.refs_3_.refs_2_.refs_5_ = bf16[4112,128]{1,0:T(8,128)(2,1)S(1)} collective-permute-done((bf16[4112,128]{1,0:T(8,128)(2,1)}, bf16[4112,128]{1,0:T(8,128)(2,1)S(1)}, u32[]{:S(2)}, u32[]{:S(2)}) %collective-permute-start.1) | collective-permute-done | bytes 1052704 | tf_op jit(solution)/shard_map/ppermute | solution.py:367
  28.0 0.7 collective-permute-start.10
  28.7 5.5 %collective-permute-start.2 = (bf16[2048,128]{1,0:T(8,128)(2,1)S(1)}, bf16[2048,128]{1,0:T(8,128)(2,1)S(1)}, u32[]{:S(2)}, u32[]{:S(2)}) collective-permute-start(bf16[2048,128]{1,0:T(8,128)(2,1)S(1)} %copy-done.3), channel_id=1, source_target_pairs={{1,9},{5,13},{17,25},{21,29},{9,1},{13,5},{25,17},{29,21},{2,10},{... | collective-permute-start | bytes 1572872 | tf_op jit(solution)/shard_map/ppermute | solution.py:367
  34.3 0.0 collective-permute-done.3.refs_0_.refs_1_
  34.3 0.7 pick_rows.6
  35.0 0.7 collective-permute-start.5
  35.7 0.0 collective-permute-done.4.refs_2_.refs_3_.refs_1_
  35.7 0.0 collective-permute-done.6.refs_5_.refs_4_
  35.7 0.0 collective-permute-done.5.refs_4_.refs_2_.refs_6_
  35.7 1.5 %pick_rows.8 = (bf16[3072,128]{1,0:T(8,128)(2,1)S(1)}, bf16[3072,128]{1,0:T(8,128)(2,1)S(1)}) custom-call(s32[8,8]{1,0:T(8,128)S(1)} %collective-permute-done.refs_0_, bf16[4112,128]{1,0:T(8,128)(2,1)S(1)} %collective-permute-done.3.refs_0_.refs_1_, bf16[2048,128]{1,0:T(8,128)(2,1)S(1)} %collective-permute-done.4.refs_2_.refs_3_.refs_1_, ...), custom_call_target="tpu_custom_call" | custom-call | flops 1024 | bytes 1024 | tf_op jit(solution)/shard_map/pick_rows/pallas_call | solution.py:223
  37.3 0.7 collective-permute-start.7
  38.0 1.3 %collective-permute-start.9 = (bf16[3072,128]{1,0:T(8,128)(2,1)S(1)}, bf16[3072,128]{1,0:T(8,128)(2,1)S(1)}, u32[]{:S(2)}, u32[]{:S(2)}) collective-permute-start(bf16[3072,128]{1,0:T(8,128)(2,1)S(1)} %get-tuple-element.29), channel_id=1, source_target_pairs={{8,4},{12,0},{16,28},{20,24},{9,5},{13,1},{17,29},{21,25},{10,6},{... | collective-permute-start | bytes 2359304 | tf_op jit(solution)/shard_map/ppermute | solution.py:367
  39.3 1.6 %collective-permute-done.2.refs_2_.refs_3_ = bf16[2048,128]{1,0:T(8,128)(2,1)S(1)} collective-permute-done((bf16[2048,128]{1,0:T(8,128)(2,1)S(1)}, bf16[2048,128]{1,0:T(8,128)(2,1)S(1)}, u32[]{:S(2)}, u32[]{:S(2)}) %collective-permute-start.2) | collective-permute-done | bytes 524320 | tf_op jit(solution)/shard_map/ppermute | solution.py:367
  40.8 0.7 collective-permute-start.15
  41.5 0.0 copy-start
  41.5 0.0 copy-start.2
  41.6 0.0 copy-start.5
  41.6 0.0 copy-start.6
  41.6 1.6 %collective-permute-start.14 = (bf16[2048,128]{1,0:T(8,128)(2,1)S(1)}, bf16[2048,128]{1,0:T(8,128)(2,1)S(1)}, u32[]{:S(2)}, u32[]{:S(2)}) collective-permute-start(bf16[2048,128]{1,0:T(8,128)(2,1)S(1)} %get-tuple-element.37), channel_id=1, source_target_pairs={{8,0},{12,4},{16,24},{20,28},{9,1},{13,5},{17,25},{21,29},{10,2},{... | collective-permute-start | bytes 1572872 | tf_op jit(solution)/shard_map/ppermute | solution.py:367
  43.1 0.5 turn_rows.1.turned
  43.6 0.0 copy-done
  43.6 3.9 %stage_products.3 = (bf16[3,3,128,128]{3,2,1,0:T(8,128)(2,1)S(1)}, bf16[3,3,128,128]{3,2,1,0:T(8,128)(2,1)S(1)}, bf16[3,3,128,128]{3,2,1,0:T(8,128)(2,1)S(1)}) custom-call(s32[8,8]{1,0:T(8,128)S(1)} %bitcast.19, s32[8,8]{1,0:T(8,128)S(1)} %bitcast.16, s32[1,8]{1,0:T(1,128)S(1)} %bitcast.22, bf16[16,384,128]{2,1,0:T(8,128)(2,1)S(1)} %turn_rows.1.turned, ...), custom_call_target="tpu_custom_call" | custom-call | flops 1024 | bytes 1024 | tf_op jit(solution)/shard_map/stage_products/pallas_call | solution.py:302
  47.6 0.0 collective-permute-done.7.refs_3_.refs_1_.refs_11_
  47.6 0.7 pick_rows.9
  48.3 2.2 %collective-permute-start.8 = (bf16[3072,128]{1,0:T(8,128)(2,1)S(1)}, bf16[3072,128]{1,0:T(8,128)(2,1)S(1)}, u32[]{:S(2)}, u32[]{:S(2)}) collective-permute-start(bf16[3072,128]{1,0:T(8,128)(2,1)S(1)} %pick_rows.9), channel_id=1, source_target_pairs={{0,4},{4,0},{8,12},{12,8},{16,20},{20,16},{24,28},{28,24},{1,5},{5... | collective-permute-start | bytes 2359304 | tf_op jit(solution)/shard_map/ppermute | solution.py:367
  50.5 0.0 collective-permute-done.10.refs_0_.refs_1_.refs_4_
  50.5 0.9 pick_rows.10
  51.4 1.3 %collective-permute-start.11 = (bf16[2048,128]{1,0:T(8,128)(2,1)S(1)}, bf16[2048,128]{1,0:T(8,128)(2,1)S(1)}, u32[]{:S(2)}, u32[]{:S(2)}) collective-permute-start(bf16[2048,128]{1,0:T(8,128)(2,1)S(1)} %get-tuple-element.33.refs_7_), channel_id=1, source_target_pairs={{8,0},{12,4},{16,24},{20,28},{9,1},{13,5},{17,25},{21,29},{10,2},{... | collective-permute-start | bytes 1572872 | tf_op jit(solution)/shard_map/ppermute | solution.py:367
  52.7 0.0 collective-permute-done.15.refs_2_.refs_4_.refs_5_
  52.8 24.6 %collective-permute-done.14.refs_9_.refs_2_ = bf16[2048,128]{1,0:T(8,128)(2,1)S(1)} collective-permute-done((bf16[2048,128]{1,0:T(8,128)(2,1)S(1)}, bf16[2048,128]{1,0:T(8,128)(2,1)S(1)}, u32[]{:S(2)}, u32[]{:S(2)}) %collective-permute-start.14) | collective-permute-done | bytes 524320 | tf_op jit(solution)/shard_map/ppermute | solution.py:367
  77.4 0.0 collective-permute-done.9.refs_2_.refs_10_
  77.4 1.5 %pick_rows.11 = (bf16[3072,128]{1,0:T(8,128)(2,1)S(1)}, bf16[2048,128]{1,0:T(8,128)(2,1)S(1)}, bf16[1024,128]{1,0:T(8,128)(2,1)S(1)}) custom-call(s32[8,8]{1,0:T(8,128)S(1)} %collective-permute-done.refs_0_, bf16[4112,128]{1,0:T(8,128)(2,1)S(1)} %collective-permute-done.10.refs_0_.refs_1_.refs_4_, ...), custom_call_target="tpu_custom_call" | custom-call | flops 20000000000 | bytes 1024 | tf_op jit(solution)/shard_map/pick_rows/pallas_call | solution.py:223
  78.9 0.7 collective-permute-start.17
  79.6 1.3 %collective-permute-start.19 = (bf16[1024,128]{1,0:T(8,128)(2,1)S(1)}, bf16[1024,128]{1,0:T(8,128)(2,1)S(1)}, u32[]{:S(2)}, u32[]{:S(2)}) collective-permute-start(bf16[1024,128]{1,0:T(8,128)(2,1)S(1)} %get-tuple-element.41), channel_id=1, source_target_pairs={{9,5},{13,1},{17,29},{21,25},{10,6},{14,2},{18,30},{22,26}} | collective-permute-start | bytes 786440 | tf_op jit(solution)/shard_map/ppermute | solution.py:367
  80.9 1.3 %collective-permute-start.16 = (bf16[2048,128]{1,0:T(8,128)(2,1)S(1)}, bf16[2048,128]{1,0:T(8,128)(2,1)S(1)}, u32[]{:S(2)}, u32[]{:S(2)}) collective-permute-start(bf16[2048,128]{1,0:T(8,128)(2,1)S(1)} %get-tuple-element.39), channel_id=1, source_target_pairs={{9,1},{13,5},{17,25},{21,29},{10,2},{14,6},{18,26},{22,30}} | collective-permute-start | bytes 1572872 | tf_op jit(solution)/shard_map/ppermute | solution.py:367
  82.2 0.0 collective-permute-done.8.refs_0_
  82.2 1.3 %collective-permute-start.18 = (bf16[2048,128]{1,0:T(8,128)(2,1)S(1)}, bf16[2048,128]{1,0:T(8,128)(2,1)S(1)}, u32[]{:S(2)}, u32[]{:S(2)}) collective-permute-start(bf16[2048,128]{1,0:T(8,128)(2,1)S(1)} %get-tuple-element.38.refs_8_), channel_id=1, source_target_pairs={{8,4},{12,0},{16,28},{20,24},{9,5},{13,1},{17,29},{21,25},{10,6},{... | collective-permute-start | bytes 1572872 | tf_op jit(solution)/shard_map/ppermute | solution.py:367
  83.5 4.4 %collective-permute-done.11.refs_6_ = bf16[2048,128]{1,0:T(8,128)(2,1)S(1)} collective-permute-done((bf16[2048,128]{1,0:T(8,128)(2,1)S(1)}, bf16[2048,128]{1,0:T(8,128)(2,1)S(1)}, u32[]{:S(2)}, u32[]{:S(2)}) %collective-permute-start.11) | collective-permute-done | bytes 524320 | tf_op jit(solution)/shard_map/ppermute | solution.py:367
  87.9 4.4 %stage_products.4 = (bf16[5,3,128,128]{3,2,1,0:T(8,128)(2,1)S(1)}, bf16[5,3,128,128]{3,2,1,0:T(8,128)(2,1)S(1)}, bf16[5,3,128,128]{3,2,1,0:T(8,128)(2,1)S(1)}) custom-call(s32[8,8]{1,0:T(8,128)S(1)} %bitcast.20, s32[8,8]{1,0:T(8,128)S(1)} %bitcast.17, s32[1,8]{1,0:T(1,128)S(1)} %bitcast.23, bf16[16,384,128]{2,1,0:T(8,128)(2,1)S(1)} %turn_rows.1.turned, ...), custom_call_target="tpu_custom_call" | custom-call | flops 1024 | bytes 1024 | tf_op jit(solution)/shard_map/stage_products/pallas_call | solution.py:302
  92.3 1.9 %collective-permute-start.12 = (bf16[5,3,128,128]{3,2,1,0:T(8,128)(2,1)S(1)}, bf16[5,3,128,128]{3,2,1,0:T(8,128)(2,1)S(1)}, u32[]{:S(2)}, u32[]{:S(2)}) collective-permute-start(bf16[5,3,128,128]{3,2,1,0:T(8,128)(2,1)S(1)} %get-tuple-element.35), channel_id=1, source_target_pairs={{0,1},{1,2},{2,3},{4,5},{5,6},{6,7},{8,9},{9,10},{10,11},{12,13},{... | collective-permute-start | bytes 1474568 | tf_op jit(solution)/shard_map/ppermute | solution.py:376
  94.2 0.0 collective-permute-done.19.refs_10_
  94.2 2.4 %collective-permute-start.13 = (bf16[5,3,128,128]{3,2,1,0:T(8,128)(2,1)S(1)}, bf16[5,3,128,128]{3,2,1,0:T(8,128)(2,1)S(1)}, u32[]{:S(2)}, u32[]{:S(2)}) collective-permute-start(bf16[5,3,128,128]{3,2,1,0:T(8,128)(2,1)S(1)} %get-tuple-element.36), channel_id=1, source_target_pairs={{1,0},{2,1},{3,2},{5,4},{6,5},{7,6},{9,8},{10,9},{11,10},{13,12},{... | collective-permute-start | bytes 1474568 | tf_op jit(solution)/shard_map/ppermute | solution.py:377
  96.7 5.3 %collective-permute-done.16.refs_3_.refs_7_ = bf16[2048,128]{1,0:T(8,128)(2,1)S(1)} collective-permute-done((bf16[2048,128]{1,0:T(8,128)(2,1)S(1)}, bf16[2048,128]{1,0:T(8,128)(2,1)S(1)}, u32[]{:S(2)}, u32[]{:S(2)}) %collective-permute-start.16) | collective-permute-done | bytes 524320 | tf_op jit(solution)/shard_map/ppermute | solution.py:367
  101.9 5.6 %collective-permute-done.18.refs_9_ = bf16[2048,128]{1,0:T(8,128)(2,1)S(1)} collective-permute-done((bf16[2048,128]{1,0:T(8,128)(2,1)S(1)}, bf16[2048,128]{1,0:T(8,128)(2,1)S(1)}, u32[]{:S(2)}, u32[]{:S(2)}) %collective-permute-start.18) | collective-permute-done | bytes 524320 | tf_op jit(solution)/shard_map/ppermute | solution.py:367
  107.5 0.0 collective-permute-done.17.refs_8_
  107.5 0.0 collective-permute-done.12.refs_11_.refs_1_
  107.5 0.0 collective-permute-done.13.refs_12_.refs_2_
  107.5 3.2 %stage_products.5 = (bf16[3,3,128,128]{3,2,1,0:T(8,128)(2,1)S(1)}, bf16[3,3,128,128]{3,2,1,0:T(8,128)(2,1)S(1)}, bf16[3,3,128,128]{3,2,1,0:T(8,128)(2,1)S(1)}) custom-call(s32[8,8]{1,0:T(8,128)S(1)} %bitcast.21, s32[8,8]{1,0:T(8,128)S(1)} %bitcast.18, s32[1,8]{1,0:T(1,128)S(1)} %bitcast.24, bf16[16,384,128]{2,1,0:T(8,128)(2,1)S(1)} %turn_rows.1.turned, ...), custom_call_target="tpu_custom_call" | custom-call | flops 1024 | bytes 1024 | tf_op jit(solution)/shard_map/stage_products/pallas_call | solution.py:302
  110.7 2.3 %collective-permute-start.20 = (bf16[3,3,128,128]{3,2,1,0:T(8,128)(2,1)S(1)}, bf16[3,3,128,128]{3,2,1,0:T(8,128)(2,1)S(1)}, u32[]{:S(2)}, u32[]{:S(2)}) collective-permute-start(bf16[3,3,128,128]{3,2,1,0:T(8,128)(2,1)S(1)} %get-tuple-element.43), channel_id=1, source_target_pairs={{0,1},{1,2},{2,3},{4,5},{5,6},{6,7},{8,9},{9,10},{10,11},{12,13},{... | collective-permute-start | bytes 884744 | tf_op jit(solution)/shard_map/ppermute | solution.py:376
  113.0 2.1 %collective-permute-start.21 = (bf16[3,3,128,128]{3,2,1,0:T(8,128)(2,1)S(1)}, bf16[3,3,128,128]{3,2,1,0:T(8,128)(2,1)S(1)}, u32[]{:S(2)}, u32[]{:S(2)}) collective-permute-start(bf16[3,3,128,128]{3,2,1,0:T(8,128)(2,1)S(1)} %get-tuple-element.44), channel_id=1, source_target_pairs={{1,0},{2,1},{3,2},{5,4},{6,5},{7,6},{9,8},{10,9},{11,10},{13,12},{... | collective-permute-start | bytes 884744 | tf_op jit(solution)/shard_map/ppermute | solution.py:377
  115.1 1.6 %collective-permute-done.20.refs_4_ = bf16[3,3,128,128]{3,2,1,0:T(8,128)(2,1)S(1)} collective-permute-done((bf16[3,3,128,128]{3,2,1,0:T(8,128)(2,1)S(1)}, bf16[3,3,128,128]{3,2,1,0:T(8,128)(2,1)S(1)}, u32[]{:S(2)}, u32[]{:S(2)}) %collective-permute-start.20) | collective-permute-done | bytes 294944 | tf_op jit(solution)/shard_map/ppermute | solution.py:376
  116.6 4.4 %collective-permute-done.21.refs_5_ = bf16[3,3,128,128]{3,2,1,0:T(8,128)(2,1)S(1)} collective-permute-done((bf16[3,3,128,128]{3,2,1,0:T(8,128)(2,1)S(1)}, bf16[3,3,128,128]{3,2,1,0:T(8,128)(2,1)S(1)}, u32[]{:S(2)}, u32[]{:S(2)}) %collective-permute-start.21) | collective-permute-done | bytes 294944 | tf_op jit(solution)/shard_map/ppermute | solution.py:377
  121.0 2.5 %assemble_coarse.1 = f32[5120,128]{1,0:T(8,128)} custom-call(bf16[5,3,128,128]{3,2,1,0:T(8,128)(2,1)S(1)} %get-tuple-element.34.refs_0_, bf16[5,3,128,128]{3,2,1,0:T(8,128)(2,1)S(1)} %collective-permute-done.12.refs_11_.refs_1_, bf16[5,3,128,128]{3,2,1,0:T(8,128)(2,1)S(1)} %collective-permute-done.13.refs_12_.refs_2_, ...), custom_call_target="tpu_custom_call" | custom-call | flops 1024 | bytes 1024 | tf_op jit(solution)/shard_map/assemble_coarse/pallas_call | solution.py:343
  (6 shorter events, 0.0 us)
Async XLA Ops:
  0.0 5.6 %copy-start.4 = (s32[1,1,8,8]{3,2,1,0:T(8,128)S(1)}, s32[1,1,8,8]{3,2,1,0:T(8,128)}, u32[]{:S(2)}) copy-start(s32[1,1,8,8]{3,2,1,0:T(8,128)} %param.8) | copy-start | bytes 772
  2.6 25.4 %collective-permute-start.1 = (bf16[4112,128]{1,0:T(8,128)(2,1)}, bf16[4112,128]{1,0:T(8,128)(2,1)S(1)}, u32[]{:S(2)}, u32[]{:S(2)}) collective-permute-start(bf16[4112,128]{1,0:T(8,128)(2,1)} %get-tuple-element.25.head.refs_1_.refs_0_), channel_id=1, source_target_pairs={{0,8},{4,12},{16,24},{20,28},{8,0},{12,4},{24,16},{28,20},{1,9},{5... | collective-permute-start | bytes 3158024 | tf_op jit(solution)/shard_map/ppermute | solution.py:367
  4.8 29.4 %collective-permute-start.3 = (bf16[4112,128]{1,0:T(8,128)(2,1)}, bf16[4112,128]{1,0:T(8,128)(2,1)S(1)}, u32[]{:S(2)}, u32[]{:S(2)}) collective-permute-start(bf16[4112,128]{1,0:T(8,128)(2,1)} %get-tuple-element.25.head.refs_1_.refs_0_), channel_id=1, source_target_pairs={{8,16},{12,20},{16,8},{20,12},{9,17},{13,21},{17,9},{21,13},{10,18... | collective-permute-start | bytes 3158024 | tf_op jit(solution)/shard_map/ppermute | solution.py:367
  5.6 2.8 %collective-permute-start = (s32[8,8]{1,0:T(8,128)S(1)}, s32[8,8]{1,0:T(8,128)S(1)}, u32[]{:S(2)}, u32[]{:S(2)}) collective-permute-start(s32[8,8]{1,0:T(8,128)S(1)} %bitcast.15), channel_id=1, source_target_pairs={{4,0},{0,4},{12,8},{8,12},{20,16},{16,20},{28,24},{24,28},{5,1},{1... | collective-permute-start | bytes 776 | tf_op jit(solution)/shard_map/ppermute | solution.py:367
  8.4 1.2 copy-start.1
  9.6 1.0 copy-start.3
  11.3 24.4 %collective-permute-start.6 = (bf16[3072,128]{1,0:T(8,128)(2,1)S(1)}, bf16[3072,128]{1,0:T(8,128)(2,1)S(1)}, u32[]{:S(2)}, u32[]{:S(2)}) collective-permute-start(bf16[3072,128]{1,0:T(8,128)(2,1)S(1)} %pick_rows.7), channel_id=1, source_target_pairs={{0,4},{4,0},{8,12},{12,8},{16,20},{20,16},{24,28},{28,24},{1,5},{5... | collective-permute-start | bytes 2359304 | tf_op jit(solution)/shard_map/ppermute | solution.py:367
  12.6 23.1 %collective-permute-start.4 = (bf16[2048,128]{1,0:T(8,128)(2,1)S(1)}, bf16[2048,128]{1,0:T(8,128)(2,1)S(1)}, u32[]{:S(2)}, u32[]{:S(2)}) collective-permute-start(bf16[2048,128]{1,0:T(8,128)(2,1)S(1)} %copy-done.3), channel_id=1, source_target_pairs={{9,17},{13,21},{17,9},{21,13},{10,18},{14,22},{18,10},{22,14}} | collective-permute-start | bytes 1572872 | tf_op jit(solution)/shard_map/ppermute | solution.py:367
  28.0 22.5 %collective-permute-start.10 = (bf16[4112,128]{1,0:T(8,128)(2,1)S(1)}, bf16[4112,128]{1,0:T(8,128)(2,1)S(1)}, u32[]{:S(2)}, u32[]{:S(2)}) collective-permute-start(bf16[4112,128]{1,0:T(8,128)(2,1)S(1)} %collective-permute-done.1.refs_1_.refs_3_.refs_2_.refs_5_), channel_id=1, source_target_pairs={{8,16},{12,20},{16,8},{20,12},{9,17},{13,21},{17,9},{21,13},{10,18... | collective-permute-start | bytes 3158024 | tf_op jit(solution)/shard_map/ppermute | solution.py:367
  28.7 12.1 %collective-permute-start.2 = (bf16[2048,128]{1,0:T(8,128)(2,1)S(1)}, bf16[2048,128]{1,0:T(8,128)(2,1)S(1)}, u32[]{:S(2)}, u32[]{:S(2)}) collective-permute-start(bf16[2048,128]{1,0:T(8,128)(2,1)S(1)} %copy-done.3), channel_id=1, source_target_pairs={{1,9},{5,13},{17,25},{21,29},{9,1},{13,5},{25,17},{29,21},{2,10},{... | collective-permute-start | bytes 1572872 | tf_op jit(solution)/shard_map/ppermute | solution.py:367
  35.0 0.7 collective-permute-start.5
  37.3 10.3 %collective-permute-start.7 = (bf16[3072,128]{1,0:T(8,128)(2,1)S(1)}, bf16[3072,128]{1,0:T(8,128)(2,1)S(1)}, u32[]{:S(2)}, u32[]{:S(2)}) collective-permute-start(bf16[3072,128]{1,0:T(8,128)(2,1)S(1)} %get-tuple-element.28), channel_id=1, source_target_pairs={{8,12},{12,8},{16,20},{20,16},{9,13},{13,9},{17,21},{21,17},{10,14... | collective-permute-start | bytes 2359304 | tf_op jit(solution)/shard_map/ppermute | solution.py:367
  38.0 39.4 %collective-permute-start.9 = (bf16[3072,128]{1,0:T(8,128)(2,1)S(1)}, bf16[3072,128]{1,0:T(8,128)(2,1)S(1)}, u32[]{:S(2)}, u32[]{:S(2)}) collective-permute-start(bf16[3072,128]{1,0:T(8,128)(2,1)S(1)} %get-tuple-element.29), channel_id=1, source_target_pairs={{8,4},{12,0},{16,28},{20,24},{9,5},{13,1},{17,29},{21,25},{10,6},{... | collective-permute-start | bytes 2359304 | tf_op jit(solution)/shard_map/ppermute | solution.py:367
  40.8 11.9 %collective-permute-start.15 = (bf16[2048,128]{1,0:T(8,128)(2,1)S(1)}, bf16[2048,128]{1,0:T(8,128)(2,1)S(1)}, u32[]{:S(2)}, u32[]{:S(2)}) collective-permute-start(bf16[2048,128]{1,0:T(8,128)(2,1)S(1)} %collective-permute-done.2.refs_2_.refs_3_), channel_id=1, source_target_pairs={{9,17},{13,21},{17,9},{21,13},{10,18},{14,22},{18,10},{22,14}} | collective-permute-start | bytes 1572872 | tf_op jit(solution)/shard_map/ppermute | solution.py:367
  41.5 2.1 %copy-start = (bf16[1,1,8,8,128,128]{5,4,3,2,1,0:T(8,128)(2,1)S(1)}, bf16[1,1,8,8,128,128]{5,4,3,2,1,0:T(8,128)(2,1)}, u32[]{:S(2)}) copy-start(bf16[1,1,8,8,128,128]{5,4,3,2,1,0:T(8,128)(2,1)} %param.6) | copy-start | bytes 6291460
  41.5 2.1 %copy-start.2 = (bf16[4112,128]{1,0:T(8,128)(2,1)S(1)}, bf16[4112,128]{1,0:T(8,128)(2,1)}, u32[]{:S(2)}) copy-start(bf16[4112,128]{1,0:T(8,128)(2,1)} %get-tuple-element.25.head.refs_1_.refs_0_) | copy-start | bytes 3158020
  41.6 2.1 %copy-start.5 = (s32[1,1,8,8]{3,2,1,0:T(8,128)S(1)}, s32[1,1,8,8]{3,2,1,0:T(8,128)}, u32[]{:S(2)}) copy-start(s32[1,1,8,8]{3,2,1,0:T(8,128)} %param.7) | copy-start | bytes 772
  41.6 2.1 %copy-start.6 = (s32[1,1,8]{2,1,0:T(1,128)S(1)}, s32[1,1,8]{2,1,0:T(1,128)}, u32[]{:S(2)}) copy-start(s32[1,1,8]{2,1,0:T(1,128)} %param.9) | copy-start | bytes 100
  41.6 35.8 %collective-permute-start.14 = (bf16[2048,128]{1,0:T(8,128)(2,1)S(1)}, bf16[2048,128]{1,0:T(8,128)(2,1)S(1)}, u32[]{:S(2)}, u32[]{:S(2)}) collective-permute-start(bf16[2048,128]{1,0:T(8,128)(2,1)S(1)} %get-tuple-element.37), channel_id=1, source_target_pairs={{8,0},{12,4},{16,24},{20,28},{9,1},{13,5},{17,25},{21,29},{10,2},{... | collective-permute-start | bytes 1572872 | tf_op jit(solution)/shard_map/ppermute | solution.py:367
  48.3 33.9 %collective-permute-start.8 = (bf16[3072,128]{1,0:T(8,128)(2,1)S(1)}, bf16[3072,128]{1,0:T(8,128)(2,1)S(1)}, u32[]{:S(2)}, u32[]{:S(2)}) collective-permute-start(bf16[3072,128]{1,0:T(8,128)(2,1)S(1)} %pick_rows.9), channel_id=1, source_target_pairs={{0,4},{4,0},{8,12},{12,8},{16,20},{20,16},{24,28},{28,24},{1,5},{5... | collective-permute-start | bytes 2359304 | tf_op jit(solution)/shard_map/ppermute | solution.py:367
  51.4 36.4 %collective-permute-start.11 = (bf16[2048,128]{1,0:T(8,128)(2,1)S(1)}, bf16[2048,128]{1,0:T(8,128)(2,1)S(1)}, u32[]{:S(2)}, u32[]{:S(2)}) collective-permute-start(bf16[2048,128]{1,0:T(8,128)(2,1)S(1)} %get-tuple-element.33.refs_7_), channel_id=1, source_target_pairs={{8,0},{12,4},{16,24},{20,28},{9,1},{13,5},{17,25},{21,29},{10,2},{... | collective-permute-start | bytes 1572872 | tf_op jit(solution)/shard_map/ppermute | solution.py:367
  78.9 28.6 %collective-permute-start.17 = (bf16[3072,128]{1,0:T(8,128)(2,1)S(1)}, bf16[3072,128]{1,0:T(8,128)(2,1)S(1)}, u32[]{:S(2)}, u32[]{:S(2)}) collective-permute-start(bf16[3072,128]{1,0:T(8,128)(2,1)S(1)} %get-tuple-element.40), channel_id=1, source_target_pairs={{8,12},{12,8},{16,20},{20,16},{9,13},{13,9},{17,21},{21,17},{10,14... | collective-permute-start | bytes 2359304 | tf_op jit(solution)/shard_map/ppermute | solution.py:367
  79.6 14.6 %collective-permute-start.19 = (bf16[1024,128]{1,0:T(8,128)(2,1)S(1)}, bf16[1024,128]{1,0:T(8,128)(2,1)S(1)}, u32[]{:S(2)}, u32[]{:S(2)}) collective-permute-start(bf16[1024,128]{1,0:T(8,128)(2,1)S(1)} %get-tuple-element.41), channel_id=1, source_target_pairs={{9,5},{13,1},{17,29},{21,25},{10,6},{14,2},{18,30},{22,26}} | collective-permute-start | bytes 786440 | tf_op jit(solution)/shard_map/ppermute | solution.py:367
  80.9 21.0 %collective-permute-start.16 = (bf16[2048,128]{1,0:T(8,128)(2,1)S(1)}, bf16[2048,128]{1,0:T(8,128)(2,1)S(1)}, u32[]{:S(2)}, u32[]{:S(2)}) collective-permute-start(bf16[2048,128]{1,0:T(8,128)(2,1)S(1)} %get-tuple-element.39), channel_id=1, source_target_pairs={{9,1},{13,5},{17,25},{21,29},{10,2},{14,6},{18,26},{22,30}} | collective-permute-start | bytes 1572872 | tf_op jit(solution)/shard_map/ppermute | solution.py:367
  82.2 25.3 %collective-permute-start.18 = (bf16[2048,128]{1,0:T(8,128)(2,1)S(1)}, bf16[2048,128]{1,0:T(8,128)(2,1)S(1)}, u32[]{:S(2)}, u32[]{:S(2)}) collective-permute-start(bf16[2048,128]{1,0:T(8,128)(2,1)S(1)} %get-tuple-element.38.refs_8_), channel_id=1, source_target_pairs={{8,4},{12,0},{16,28},{20,24},{9,5},{13,1},{17,29},{21,25},{10,6},{... | collective-permute-start | bytes 1572872 | tf_op jit(solution)/shard_map/ppermute | solution.py:367
  92.3 15.2 %collective-permute-start.12 = (bf16[5,3,128,128]{3,2,1,0:T(8,128)(2,1)S(1)}, bf16[5,3,128,128]{3,2,1,0:T(8,128)(2,1)S(1)}, u32[]{:S(2)}, u32[]{:S(2)}) collective-permute-start(bf16[5,3,128,128]{3,2,1,0:T(8,128)(2,1)S(1)} %get-tuple-element.35), channel_id=1, source_target_pairs={{0,1},{1,2},{2,3},{4,5},{5,6},{6,7},{8,9},{9,10},{10,11},{12,13},{... | collective-permute-start | bytes 1474568 | tf_op jit(solution)/shard_map/ppermute | solution.py:376
  94.2 13.3 %collective-permute-start.13 = (bf16[5,3,128,128]{3,2,1,0:T(8,128)(2,1)S(1)}, bf16[5,3,128,128]{3,2,1,0:T(8,128)(2,1)S(1)}, u32[]{:S(2)}, u32[]{:S(2)}) collective-permute-start(bf16[5,3,128,128]{3,2,1,0:T(8,128)(2,1)S(1)} %get-tuple-element.36), channel_id=1, source_target_pairs={{1,0},{2,1},{3,2},{5,4},{6,5},{7,6},{9,8},{10,9},{11,10},{13,12},{... | collective-permute-start | bytes 1474568 | tf_op jit(solution)/shard_map/ppermute | solution.py:377
  110.7 5.9 %collective-permute-start.20 = (bf16[3,3,128,128]{3,2,1,0:T(8,128)(2,1)S(1)}, bf16[3,3,128,128]{3,2,1,0:T(8,128)(2,1)S(1)}, u32[]{:S(2)}, u32[]{:S(2)}) collective-permute-start(bf16[3,3,128,128]{3,2,1,0:T(8,128)(2,1)S(1)} %get-tuple-element.43), channel_id=1, source_target_pairs={{0,1},{1,2},{2,3},{4,5},{5,6},{6,7},{8,9},{9,10},{10,11},{12,13},{... | collective-permute-start | bytes 884744 | tf_op jit(solution)/shard_map/ppermute | solution.py:376
  113.0 8.0 %collective-permute-start.21 = (bf16[3,3,128,128]{3,2,1,0:T(8,128)(2,1)S(1)}, bf16[3,3,128,128]{3,2,1,0:T(8,128)(2,1)S(1)}, u32[]{:S(2)}, u32[]{:S(2)}) collective-permute-start(bf16[3,3,128,128]{3,2,1,0:T(8,128)(2,1)S(1)} %get-tuple-element.44), channel_id=1, source_target_pairs={{1,0},{2,1},{3,2},{5,4},{6,5},{7,6},{9,8},{10,9},{11,10},{13,12},{... | collective-permute-start | bytes 884744 | tf_op jit(solution)/shard_map/ppermute | solution.py:377

commit v12 on v11

--- a/solution.py
+++ b/solution.py
@@ -403,18 +403,14 @@
     tables = [(half[0],), *[((x, 0),) for x in end_lists]]
     end_heads = [move(early, grid.ends(0))]
 
-    def near_requests(z, y):
-        _, line_other, _ = grid.lines(z)
-        requests = []
-        for index in range(count):
-            requests += [(index, grid.panel(line_other, y, 0), 0, index, 0),
-                         (count + 1 + index, grid.panel(line_other, y, 0), 0, count + index, 0)]
-        return requests
-
-    picked = pick(grid, near_requests, [(3, cap)] * (2 * count), side_lists, [other, *tables],
-                  tables=tuple(range(1, 2 + count)), after=[x for ((x, _),) in beside], cost=COST)
+    def other_requests(z, y):
+        return [(index, grid.panel(grid.lines(z)[1], y, 0), 0, index, 0) for index in range(count)]
+
+    picked = pick(grid, other_requests, [(3, cap)] * count, side_lists, [other], after=[x for ((x, _),) in beside], cost=COST)
     other_crossed = move_across(picked, mids)
-    end_crossed = [((move(x, grid.ends(shift)), 3),) for x, shift in zip(picked[count:], sides)]
+    end_picked = pick(grid, other_requests, [(3, cap)] * count, [], [other, *tables[1:]],
+                      tables=tuple(range(1, 1 + count)), after=[*picked, end_heads[0]], cost=COST)
+    end_crossed = [((move(x, grid.ends(shift)), 3),) for x, shift in zip(end_picked, sides)]
 
     def half_requests(z, y):
         return [(index, grid.panel(grid.lines(z)[0], y, 0), 0, index, 0) for index in range(count)]
@@ -448,7 +444,7 @@
     sources = []
     for i in range(count):
         sources += [half_crossed[i], other_crossed[i], end_crossed[i]]
-    parts = stage(grid, grid.work_middle, lists, turned, matrix, sources, parts, far_heads[:1])
+    parts = stage(grid, grid.work_middle, lists, turned, matrix, sources, parts, ())
     first = exchange(parts)
 
     sources = [other, ((end_heads[0], 2), (end_tail, 1, 0)), far, ((far_heads[0], 2), (end_tail, 1, cap))]

time: 125 us -> 137 us (1.096)
  waiting for transfers between devices: 63.5 us -> 74.4 us
  starting transfers between devices: 34.2 us -> 36.1 us
    ppermute x2, waiting for transfers between devices: 4.4 us -> 8.8 us  [exchange(): lax.ppermute(parts[2], 'rows', [(g + 1, g) for g in range(groups - 1)])]
    ppermute x2, waiting for transfers between devices: 1.57 us -> 5.51 us  [exchange(): lax.ppermute(parts[1], 'rows', [(g, g + 1) for g in range(groups - 1)])]
    ppermute x18, waiting for transfers between devices: 57.6 us -> 60.1 us  [move(): return lax.ppermute(x, ('blk', 'rows'), perm) if perm else jnp.zeros_like(x)]
    ppermute x2, starting transfers between devices: 4.19 us -> 6.09 us  [exchange(): lax.ppermute(parts[1], 'rows', [(g, g + 1) for g in range(groups - 1)])]
    pallas_call x6 -> x7, Pallas kernels: 6.03 us -> 5.92 us  [pick(): pl.pallas_call(functools.partial(pick_kernel, grid, plan, layout, carry,...]
  transfers between devices with their start and end apart: 22 -> 22, of which waited for: 9 -> 10; matrix products, arithmetic and copies ran while one was open for 0% -> 0% of each run, Pallas kernels for 12% -> 11%
where the time goes in v12:
time: 137 us; the launch traced here: 136 us
  waiting for transfers between devices  74.4 us (54%)
  starting transfers between devices  36.1 us (26%)
  Pallas kernels  22.7 us (17%)
  local copies, waits for them, and re-layouts  2.3 us (2%)
    ppermute x18, waiting for transfers between devices, move(): return lax.ppermute(x, ('blk', 'rows'), perm) if perm else jnp.zeros_like(x)  60.1 us
    ppermute x18, starting transfers between devices, move(): return lax.ppermute(x, ('blk', 'rows'), perm) if perm else jnp.zeros_like(x)  26.2 us
    pallas_call x3, Pallas kernels, stage(): pl.pallas_call(functools.partial(stage_kernel, grid, plan, layout, carrie...  11.2 us
    ppermute x2, waiting for transfers between devices, exchange(): lax.ppermute(parts[2], 'rows', [(g + 1, g) for g in range(groups - 1)])  8.8 us
    ppermute x2, starting transfers between devices, exchange(): lax.ppermute(parts[1], 'rows', [(g, g + 1) for g in range(groups - 1)])  6.09 us
    pallas_call x7, Pallas kernels, pick(): pl.pallas_call(functools.partial(pick_kernel, grid, plan, layout, carry,...  5.92 us
    ppermute x2, waiting for transfers between devices, exchange(): lax.ppermute(parts[1], 'rows', [(g, g + 1) for g in range(groups - 1)])  5.51 us
    ppermute x2, starting transfers between devices, exchange(): lax.ppermute(parts[2], 'rows', [(g + 1, g) for g in range(groups - 1)])  3.84 us
  transfers between devices with their start and end apart: 22, of which 10 were waited for; matrix products, arithmetic and copies ran while one was open for 0% of the time, Pallas kernels for 11%

profile of v12, /device:TPU:1, one launch (start us, length us, event | category | flops | bytes accessed | tf_op | source)
XLA Modules:
  0.0 135.9 jit_solution(5743048484858556517)
XLA Ops:
  0.0 2.6 %pack_rows.1 = (bf16[4112,128]{1,0:T(8,128)(2,1)}, bf16[2048,128]{1,0:T(8,128)(2,1)}) custom-call(s32[3,1,16]{2,1,0:T(1,128)} %bitcast.26, s32[8,8]{1,0:T(8,128)} %bitcast.14, bf16[16,128,384]{2,1,0:T(8,128)(2,1)} %bitcast.25), custom_call_target="tpu_custom_call" | custom-call | flops 1024 | bytes 1024 | tf_op jit(solution)/shard_map/pack_rows/pallas_call | solution.py:131
  2.6 2.2 %collective-permute-start.1 = (bf16[4112,128]{1,0:T(8,128)(2,1)}, bf16[4112,128]{1,0:T(8,128)(2,1)S(1)}, u32[]{:S(2)}, u32[]{:S(2)}) collective-permute-start(bf16[4112,128]{1,0:T(8,128)(2,1)} %get-tuple-element.23.head.refs_1_.refs_0_), channel_id=1, source_target_pairs={{0,8},{4,12},{16,24},{20,28},{8,0},{12,4},{24,16},{28,20},{1,9},{5... | collective-permute-start | bytes 3158024 | tf_op jit(solution)/shard_map/ppermute | solution.py:367
  4.8 0.7 collective-permute-start.3
  5.6 0.0 copy-done.4
  5.6 1.3 collective-permute-start
  6.9 1.5 %collective-permute-done.refs_0_ = s32[8,8]{1,0:T(8,128)S(1)} collective-permute-done((s32[8,8]{1,0:T(8,128)S(1)}, s32[8,8]{1,0:T(8,128)S(1)}, u32[]{:S(2)}, u32[]{:S(2)}) %collective-permute-start) | collective-permute-done | bytes 288 | tf_op jit(solution)/shard_map/ppermute | solution.py:367
  8.4 1.2 copy-done.1
  9.6 1.0 copy-done.3
  10.7 0.7 pick_rows.7
  11.3 1.3 collective-permute-start.5
  12.6 0.7 collective-permute-start.4
  13.3 14.7 %collective-permute-done.1.refs_1_.refs_2_.refs_5_ = bf16[4112,128]{1,0:T(8,128)(2,1)S(1)} collective-permute-done((bf16[4112,128]{1,0:T(8,128)(2,1)}, bf16[4112,128]{1,0:T(8,128)(2,1)S(1)}, u32[]{:S(2)}, u32[]{:S(2)}) %collective-permute-start.1) | collective-permute-done | bytes 1052704 | tf_op jit(solution)/shard_map/ppermute | solution.py:367
  28.0 0.0 collective-permute-done.3.refs_1_.refs_0_
  28.0 0.7 pick_rows.10
  28.8 1.3 collective-permute-start.9
  30.1 0.7 collective-permute-start.13
  30.8 8.4 %collective-permute-start.2 = (bf16[2048,128]{1,0:T(8,128)(2,1)S(1)}, bf16[2048,128]{1,0:T(8,128)(2,1)S(1)}, u32[]{:S(2)}, u32[]{:S(2)}) collective-permute-start(bf16[2048,128]{1,0:T(8,128)(2,1)S(1)} %copy-done.3), channel_id=1, source_target_pairs={{1,9},{5,13},{17,25},{21,29},{9,1},{13,5},{25,17},{29,21},{2,10},{... | collective-permute-start | bytes 1572872 | tf_op jit(solution)/shard_map/ppermute | solution.py:367
  39.2 0.0 collective-permute-done.4.refs_2_.refs_1_.refs_3_
  39.2 0.7 collective-permute-start.8
  39.9 0.0 collective-permute-done.5.refs_3_.refs_4_
  39.9 0.7 pick_rows.8.refs_3_
  40.6 0.0 copy-start.2
  40.6 0.8 collective-permute-start.6
  41.5 0.0 collective-permute-done.8.refs_2_.refs_6_
  41.5 2.3 %collective-permute-done.9.refs_4_.refs_9_.refs_2_ = bf16[2048,128]{1,0:T(8,128)(2,1)S(1)} collective-permute-done((bf16[2048,128]{1,0:T(8,128)(2,1)S(1)}, bf16[2048,128]{1,0:T(8,128)(2,1)S(1)}, u32[]{:S(2)}, u32[]{:S(2)}) %collective-permute-start.9) | collective-permute-done | bytes 524320 | tf_op jit(solution)/shard_map/ppermute | solution.py:367
  43.7 0.7 pick_rows.11
  44.5 0.0 copy-start
  44.5 0.0 copy-start.5
  44.5 0.0 copy-start.6
  44.5 1.4 %collective-permute-start.10 = (bf16[3072,128]{1,0:T(8,128)(2,1)S(1)}, bf16[3072,128]{1,0:T(8,128)(2,1)S(1)}, u32[]{:S(2)}, u32[]{:S(2)}) collective-permute-start(bf16[3072,128]{1,0:T(8,128)(2,1)S(1)} %pick_rows.11), channel_id=1, source_target_pairs={{8,4},{12,0},{16,28},{20,24},{9,5},{13,1},{17,29},{21,25},{10,6},{... | collective-permute-start | bytes 2359304 | tf_op jit(solution)/shard_map/ppermute | solution.py:367
  45.9 6.0 %collective-permute-done.2.refs_2_.refs_3_ = bf16[2048,128]{1,0:T(8,128)(2,1)S(1)} collective-permute-done((bf16[2048,128]{1,0:T(8,128)(2,1)S(1)}, bf16[2048,128]{1,0:T(8,128)(2,1)S(1)}, u32[]{:S(2)}, u32[]{:S(2)}) %collective-permute-start.2) | collective-permute-done | bytes 524320 | tf_op jit(solution)/shard_map/ppermute | solution.py:367
  52.0 0.7 collective-permute-start.14
  52.7 0.5 turn_rows.1.turned
  53.2 4.4 %stage_products.3 = (bf16[3,3,128,128]{3,2,1,0:T(8,128)(2,1)S(1)}, bf16[3,3,128,128]{3,2,1,0:T(8,128)(2,1)S(1)}, bf16[3,3,128,128]{3,2,1,0:T(8,128)(2,1)S(1)}) custom-call(s32[8,8]{1,0:T(8,128)S(1)} %bitcast.19, s32[8,8]{1,0:T(8,128)S(1)} %bitcast.16, s32[1,8]{1,0:T(1,128)S(1)} %bitcast.22, bf16[16,384,128]{2,1,0:T(8,128)(2,1)S(1)} %turn_rows.1.turned, ...), custom_call_target="tpu_custom_call" | custom-call | flops 1024 | bytes 1024 | tf_op jit(solution)/shard_map/stage_products/pallas_call | solution.py:302
  57.6 0.0 collective-permute-done.6.refs_3_.refs_1_.refs_11_
  57.6 0.7 pick_rows.9
  58.3 0.1 collective-permute-start.7
  58.4 0.0 collective-permute-done.13.refs_0_.refs_1_.refs_4_
  58.4 0.9 pick_rows.12
  59.3 1.3 collective-permute-start.16
  60.6 0.0 collective-permute-done.14.refs_2_.refs_4_.refs_5_
  60.6 5.9 %collective-permute-done.10.refs_2_.refs_10_ = bf16[3072,128]{1,0:T(8,128)(2,1)S(1)} collective-permute-done((bf16[3072,128]{1,0:T(8,128)(2,1)S(1)}, bf16[3072,128]{1,0:T(8,128)(2,1)S(1)}, u32[]{:S(2)}, u32[]{:S(2)}) %collective-permute-start.10) | collective-permute-done | bytes 786464 | tf_op jit(solution)/shard_map/ppermute | solution.py:367
  66.4 1.5 %pick_rows.13 = (bf16[3072,128]{1,0:T(8,128)(2,1)S(1)}, bf16[2048,128]{1,0:T(8,128)(2,1)S(1)}, bf16[1024,128]{1,0:T(8,128)(2,1)S(1)}) custom-call(s32[8,8]{1,0:T(8,128)S(1)} %collective-permute-done.refs_0_, bf16[4112,128]{1,0:T(8,128)(2,1)S(1)} %collective-permute-done.13.refs_0_.refs_1_.refs_4_, ...), custom_call_target="tpu_custom_call" | custom-call | flops 20000000000 | bytes 1024 | tf_op jit(solution)/shard_map/pick_rows/pallas_call | solution.py:223
  68.0 0.7 collective-permute-start.17
  68.7 1.3 collective-permute-start.19
  70.0 1.3 collective-permute-start.18
  71.3 29.7 %collective-permute-done.7.refs_0_ = bf16[3072,128]{1,0:T(8,128)(2,1)S(1)} collective-permute-done((bf16[3072,128]{1,0:T(8,128)(2,1)S(1)}, bf16[3072,128]{1,0:T(8,128)(2,1)S(1)}, u32[]{:S(2)}, u32[]{:S(2)}) %collective-permute-start.7) | collective-permute-done | bytes 786464 | tf_op jit(solution)/shard_map/ppermute | solution.py:367
  101.0 1.3 collective-permute-start.15
  102.3 4.0 %stage_products.4 = (bf16[5,3,128,128]{3,2,1,0:T(8,128)(2,1)S(1)}, bf16[5,3,128,128]{3,2,1,0:T(8,128)(2,1)S(1)}, bf16[5,3,128,128]{3,2,1,0:T(8,128)(2,1)S(1)}) custom-call(s32[8,8]{1,0:T(8,128)S(1)} %bitcast.20, s32[8,8]{1,0:T(8,128)S(1)} %bitcast.17, s32[1,8]{1,0:T(1,128)S(1)} %bitcast.23, bf16[16,384,128]{2,1,0:T(8,128)(2,1)S(1)} %turn_rows.1.turned, ...), custom_call_target="tpu_custom_call" | custom-call | flops 1024 | bytes 1024 | tf_op jit(solution)/shard_map/stage_products/pallas_call | solution.py:302
  106.3 0.0 collective-permute-done.19.refs_10_
  106.3 3.0 %collective-permute-start.11 = (bf16[5,3,128,128]{3,2,1,0:T(8,128)(2,1)S(1)}, bf16[5,3,128,128]{3,2,1,0:T(8,128)(2,1)S(1)}, u32[]{:S(2)}, u32[]{:S(2)}) collective-permute-start(bf16[5,3,128,128]{3,2,1,0:T(8,128)(2,1)S(1)} %get-tuple-element.31), channel_id=1, source_target_pairs={{0,1},{1,2},{2,3},{4,5},{5,6},{6,7},{8,9},{9,10},{10,11},{12,13},{... | collective-permute-start | bytes 1474568 | tf_op jit(solution)/shard_map/ppermute | solution.py:376
  109.4 0.0 collective-permute-done.16.refs_6_
  109.4 1.9 %collective-permute-start.12 = (bf16[5,3,128,128]{3,2,1,0:T(8,128)(2,1)S(1)}, bf16[5,3,128,128]{3,2,1,0:T(8,128)(2,1)S(1)}, u32[]{:S(2)}, u32[]{:S(2)}) collective-permute-start(bf16[5,3,128,128]{3,2,1,0:T(8,128)(2,1)S(1)} %get-tuple-element.32), channel_id=1, source_target_pairs={{1,0},{2,1},{3,2},{5,4},{6,5},{7,6},{9,8},{10,9},{11,10},{13,12},{... | collective-permute-start | bytes 1474568 | tf_op jit(solution)/shard_map/ppermute | solution.py:377
  111.3 0.0 collective-permute-done.18.refs_9_
  111.3 0.0 collective-permute-done.15.refs_3_.refs_7_
  111.3 3.8 %collective-permute-done.11.refs_11_.refs_1_ = bf16[5,3,128,128]{3,2,1,0:T(8,128)(2,1)S(1)} collective-permute-done((bf16[5,3,128,128]{3,2,1,0:T(8,128)(2,1)S(1)}, bf16[5,3,128,128]{3,2,1,0:T(8,128)(2,1)S(1)}, u32[]{:S(2)}, u32[]{:S(2)}) %collective-permute-start.11) | collective-permute-done | bytes 491552 | tf_op jit(solution)/shard_map/ppermute | solution.py:376
  115.1 4.4 %collective-permute-done.12.refs_12_.refs_2_ = bf16[5,3,128,128]{3,2,1,0:T(8,128)(2,1)S(1)} collective-permute-done((bf16[5,3,128,128]{3,2,1,0:T(8,128)(2,1)S(1)}, bf16[5,3,128,128]{3,2,1,0:T(8,128)(2,1)S(1)}, u32[]{:S(2)}, u32[]{:S(2)}) %collective-permute-start.12) | collective-permute-done | bytes 491552 | tf_op jit(solution)/shard_map/ppermute | solution.py:377
  119.5 0.0 collective-permute-done.17.refs_8_
  119.5 2.8 %stage_products.5 = (bf16[3,3,128,128]{3,2,1,0:T(8,128)(2,1)S(1)}, bf16[3,3,128,128]{3,2,1,0:T(8,128)(2,1)S(1)}, bf16[3,3,128,128]{3,2,1,0:T(8,128)(2,1)S(1)}) custom-call(s32[8,8]{1,0:T(8,128)S(1)} %bitcast.21, s32[8,8]{1,0:T(8,128)S(1)} %bitcast.18, s32[1,8]{1,0:T(1,128)S(1)} %bitcast.24, bf16[16,384,128]{2,1,0:T(8,128)(2,1)S(1)} %turn_rows.1.turned, ...), custom_call_target="tpu_custom_call" | custom-call | flops 1024 | bytes 1024 | tf_op jit(solution)/shard_map/stage_products/pallas_call | solution.py:302
  122.3 3.0 %collective-permute-start.20 = (bf16[3,3,128,128]{3,2,1,0:T(8,128)(2,1)S(1)}, bf16[3,3,128,128]{3,2,1,0:T(8,128)(2,1)S(1)}, u32[]{:S(2)}, u32[]{:S(2)}) collective-permute-start(bf16[3,3,128,128]{3,2,1,0:T(8,128)(2,1)S(1)} %get-tuple-element.39), channel_id=1, source_target_pairs={{0,1},{1,2},{2,3},{4,5},{5,6},{6,7},{8,9},{9,10},{10,11},{12,13},{... | collective-permute-start | bytes 884744 | tf_op jit(solution)/shard_map/ppermute | solution.py:376
  125.4 1.9 %collective-permute-start.21 = (bf16[3,3,128,128]{3,2,1,0:T(8,128)(2,1)S(1)}, bf16[3,3,128,128]{3,2,1,0:T(8,128)(2,1)S(1)}, u32[]{:S(2)}, u32[]{:S(2)}) collective-permute-start(bf16[3,3,128,128]{3,2,1,0:T(8,128)(2,1)S(1)} %get-tuple-element.40), channel_id=1, source_target_pairs={{1,0},{2,1},{3,2},{5,4},{6,5},{7,6},{9,8},{10,9},{11,10},{13,12},{... | collective-permute-start | bytes 884744 | tf_op jit(solution)/shard_map/ppermute | solution.py:377
  127.3 1.7 %collective-permute-done.20.refs_4_ = bf16[3,3,128,128]{3,2,1,0:T(8,128)(2,1)S(1)} collective-permute-done((bf16[3,3,128,128]{3,2,1,0:T(8,128)(2,1)S(1)}, bf16[3,3,128,128]{3,2,1,0:T(8,128)(2,1)S(1)}, u32[]{:S(2)}, u32[]{:S(2)}) %collective-permute-start.20) | collective-permute-done | bytes 294944 | tf_op jit(solution)/shard_map/ppermute | solution.py:376
  129.0 4.4 %collective-permute-done.21.refs_5_ = bf16[3,3,128,128]{3,2,1,0:T(8,128)(2,1)S(1)} collective-permute-done((bf16[3,3,128,128]{3,2,1,0:T(8,128)(2,1)S(1)}, bf16[3,3,128,128]{3,2,1,0:T(8,128)(2,1)S(1)}, u32[]{:S(2)}, u32[]{:S(2)}) %collective-permute-start.21) | collective-permute-done | bytes 294944 | tf_op jit(solution)/shard_map/ppermute | solution.py:377
  133.4 2.5 %assemble_coarse.1 = f32[5120,128]{1,0:T(8,128)} custom-call(bf16[5,3,128,128]{3,2,1,0:T(8,128)(2,1)S(1)} %get-tuple-element.30.refs_0_, bf16[5,3,128,128]{3,2,1,0:T(8,128)(2,1)S(1)} %collective-permute-done.11.refs_11_.refs_1_, bf16[5,3,128,128]{3,2,1,0:T(8,128)(2,1)S(1)} %collective-permute-done.12.refs_12_.refs_2_, ...), custom_call_target="tpu_custom_call" | custom-call | flops 1024 | bytes 1024 | tf_op jit(solution)/shard_map/assemble_coarse/pallas_call | solution.py:343
  (7 shorter events, 0.0 us)
Async XLA Ops:
  0.0 5.6 %copy-start.4 = (s32[1,1,8,8]{3,2,1,0:T(8,128)S(1)}, s32[1,1,8,8]{3,2,1,0:T(8,128)}, u32[]{:S(2)}) copy-start(s32[1,1,8,8]{3,2,1,0:T(8,128)} %param.8) | copy-start | bytes 772
  2.6 25.4 %collective-permute-start.1 = (bf16[4112,128]{1,0:T(8,128)(2,1)}, bf16[4112,128]{1,0:T(8,128)(2,1)S(1)}, u32[]{:S(2)}, u32[]{:S(2)}) collective-permute-start(bf16[4112,128]{1,0:T(8,128)(2,1)} %get-tuple-element.23.head.refs_1_.refs_0_), channel_id=1, source_target_pairs={{0,8},{4,12},{16,24},{20,28},{8,0},{12,4},{24,16},{28,20},{1,9},{5... | collective-permute-start | bytes 3158024 | tf_op jit(solution)/shard_map/ppermute | solution.py:367
  4.8 23.2 %collective-permute-start.3 = (bf16[4112,128]{1,0:T(8,128)(2,1)}, bf16[4112,128]{1,0:T(8,128)(2,1)S(1)}, u32[]{:S(2)}, u32[]{:S(2)}) collective-permute-start(bf16[4112,128]{1,0:T(8,128)(2,1)} %get-tuple-element.23.head.refs_1_.refs_0_), channel_id=1, source_target_pairs={{8,16},{12,20},{16,8},{20,12},{9,17},{13,21},{17,9},{21,13},{10,18... | collective-permute-start | bytes 3158024 | tf_op jit(solution)/shard_map/ppermute | solution.py:367
  5.6 2.8 %collective-permute-start = (s32[8,8]{1,0:T(8,128)S(1)}, s32[8,8]{1,0:T(8,128)S(1)}, u32[]{:S(2)}, u32[]{:S(2)}) collective-permute-start(s32[8,8]{1,0:T(8,128)S(1)} %bitcast.15), channel_id=1, source_target_pairs={{4,0},{0,4},{12,8},{8,12},{20,16},{16,20},{28,24},{24,28},{5,1},{1... | collective-permute-start | bytes 776 | tf_op jit(solution)/shard_map/ppermute | solution.py:367
  8.4 1.2 copy-start.1
  9.6 1.0 copy-start.3
  11.3 28.6 %collective-permute-start.5 = (bf16[3072,128]{1,0:T(8,128)(2,1)S(1)}, bf16[3072,128]{1,0:T(8,128)(2,1)S(1)}, u32[]{:S(2)}, u32[]{:S(2)}) collective-permute-start(bf16[3072,128]{1,0:T(8,128)(2,1)S(1)} %pick_rows.7), channel_id=1, source_target_pairs={{0,4},{4,0},{8,12},{12,8},{16,20},{20,16},{24,28},{28,24},{1,5},{5... | collective-permute-start | bytes 2359304 | tf_op jit(solution)/shard_map/ppermute | solution.py:367
  12.6 26.6 %collective-permute-start.4 = (bf16[2048,128]{1,0:T(8,128)(2,1)S(1)}, bf16[2048,128]{1,0:T(8,128)(2,1)S(1)}, u32[]{:S(2)}, u32[]{:S(2)}) collective-permute-start(bf16[2048,128]{1,0:T(8,128)(2,1)S(1)} %copy-done.3), channel_id=1, source_target_pairs={{9,17},{13,21},{17,9},{21,13},{10,18},{14,22},{18,10},{22,14}} | collective-permute-start | bytes 1572872 | tf_op jit(solution)/shard_map/ppermute | solution.py:367
  28.8 15.0 %collective-permute-start.9 = (bf16[2048,128]{1,0:T(8,128)(2,1)S(1)}, bf16[2048,128]{1,0:T(8,128)(2,1)S(1)}, u32[]{:S(2)}, u32[]{:S(2)}) collective-permute-start(bf16[2048,128]{1,0:T(8,128)(2,1)S(1)} %get-tuple-element.26), channel_id=1, source_target_pairs={{8,0},{12,4},{16,24},{20,28},{9,1},{13,5},{17,25},{21,29},{10,2},{... | collective-permute-start | bytes 1572872 | tf_op jit(solution)/shard_map/ppermute | solution.py:367
  30.1 28.3 %collective-permute-start.13 = (bf16[4112,128]{1,0:T(8,128)(2,1)S(1)}, bf16[4112,128]{1,0:T(8,128)(2,1)S(1)}, u32[]{:S(2)}, u32[]{:S(2)}) collective-permute-start(bf16[4112,128]{1,0:T(8,128)(2,1)S(1)} %collective-permute-done.1.refs_1_.refs_2_.refs_5_), channel_id=1, source_target_pairs={{8,16},{12,20},{16,8},{20,12},{9,17},{13,21},{17,9},{21,13},{10,18... | collective-permute-start | bytes 3158024 | tf_op jit(solution)/shard_map/ppermute | solution.py:367
  30.8 21.2 %collective-permute-start.2 = (bf16[2048,128]{1,0:T(8,128)(2,1)S(1)}, bf16[2048,128]{1,0:T(8,128)(2,1)S(1)}, u32[]{:S(2)}, u32[]{:S(2)}) collective-permute-start(bf16[2048,128]{1,0:T(8,128)(2,1)S(1)} %copy-done.3), channel_id=1, source_target_pairs={{1,9},{5,13},{17,25},{21,29},{9,1},{13,5},{25,17},{29,21},{2,10},{... | collective-permute-start | bytes 1572872 | tf_op jit(solution)/shard_map/ppermute | solution.py:367
  39.2 2.2 %collective-permute-start.8 = (bf16[16,128]{1,0:T(8,128)(2,1)S(1)}, bf16[16,128]{1,0:T(8,128)(2,1)S(1)}, u32[]{:S(2)}, u32[]{:S(2)}) collective-permute-start(bf16[16,128]{1,0:T(8,128)(2,1)S(1)} %get-tuple-element.25), channel_id=1, source_target_pairs={{12,8},{8,12},{20,16},{16,20},{13,9},{9,13},{21,17},{17,21},{14,10... | collective-permute-start | bytes 12296 | tf_op jit(solution)/shard_map/ppermute | solution.py:367
  40.6 12.1 %copy-start.2 = (bf16[4112,128]{1,0:T(8,128)(2,1)S(1)}, bf16[4112,128]{1,0:T(8,128)(2,1)}, u32[]{:S(2)}) copy-start(bf16[4112,128]{1,0:T(8,128)(2,1)} %get-tuple-element.23.head.refs_1_.refs_0_) | copy-start | bytes 3158020
  40.6 17.0 %collective-permute-start.6 = (bf16[3072,128]{1,0:T(8,128)(2,1)S(1)}, bf16[3072,128]{1,0:T(8,128)(2,1)S(1)}, u32[]{:S(2)}, u32[]{:S(2)}) collective-permute-start(bf16[3072,128]{1,0:T(8,128)(2,1)S(1)} %pick_rows.8.refs_3_), channel_id=1, source_target_pairs={{8,12},{12,8},{16,20},{20,16},{9,13},{13,9},{17,21},{21,17},{10,14... | collective-permute-start | bytes 2359304 | tf_op jit(solution)/shard_map/ppermute | solution.py:367
  44.5 8.7 %copy-start = (bf16[1,1,8,8,128,128]{5,4,3,2,1,0:T(8,128)(2,1)S(1)}, bf16[1,1,8,8,128,128]{5,4,3,2,1,0:T(8,128)(2,1)}, u32[]{:S(2)}) copy-start(bf16[1,1,8,8,128,128]{5,4,3,2,1,0:T(8,128)(2,1)} %param.6) | copy-start | bytes 6291460
  44.5 8.7 %copy-start.5 = (s32[1,1,8,8]{3,2,1,0:T(8,128)S(1)}, s32[1,1,8,8]{3,2,1,0:T(8,128)}, u32[]{:S(2)}) copy-start(s32[1,1,8,8]{3,2,1,0:T(8,128)} %param.7) | copy-start | bytes 772
  44.5 8.7 %copy-start.6 = (s32[1,1,8]{2,1,0:T(1,128)S(1)}, s32[1,1,8]{2,1,0:T(1,128)}, u32[]{:S(2)}) copy-start(s32[1,1,8]{2,1,0:T(1,128)} %param.9) | copy-start | bytes 100
  44.5 21.9 %collective-permute-start.10 = (bf16[3072,128]{1,0:T(8,128)(2,1)S(1)}, bf16[3072,128]{1,0:T(8,128)(2,1)S(1)}, u32[]{:S(2)}, u32[]{:S(2)}) collective-permute-start(bf16[3072,128]{1,0:T(8,128)(2,1)S(1)} %pick_rows.11), channel_id=1, source_target_pairs={{8,4},{12,0},{16,28},{20,24},{9,5},{13,1},{17,29},{21,25},{10,6},{... | collective-permute-start | bytes 2359304 | tf_op jit(solution)/shard_map/ppermute | solution.py:367
  52.0 8.6 %collective-permute-start.14 = (bf16[2048,128]{1,0:T(8,128)(2,1)S(1)}, bf16[2048,128]{1,0:T(8,128)(2,1)S(1)}, u32[]{:S(2)}, u32[]{:S(2)}) collective-permute-start(bf16[2048,128]{1,0:T(8,128)(2,1)S(1)} %collective-permute-done.2.refs_2_.refs_3_), channel_id=1, source_target_pairs={{9,17},{13,21},{17,9},{21,13},{10,18},{14,22},{18,10},{22,14}} | collective-permute-start | bytes 1572872 | tf_op jit(solution)/shard_map/ppermute | solution.py:367
  58.3 42.7 %collective-permute-start.7 = (bf16[3072,128]{1,0:T(8,128)(2,1)S(1)}, bf16[3072,128]{1,0:T(8,128)(2,1)S(1)}, u32[]{:S(2)}, u32[]{:S(2)}) collective-permute-start(bf16[3072,128]{1,0:T(8,128)(2,1)S(1)} %pick_rows.9), channel_id=1, source_target_pairs={{0,4},{4,0},{8,12},{12,8},{16,20},{20,16},{24,28},{28,24},{1,5},{5... | collective-permute-start | bytes 2359304 | tf_op jit(solution)/shard_map/ppermute | solution.py:367
  59.3 50.1 %collective-permute-start.16 = (bf16[2048,128]{1,0:T(8,128)(2,1)S(1)}, bf16[2048,128]{1,0:T(8,128)(2,1)S(1)}, u32[]{:S(2)}, u32[]{:S(2)}) collective-permute-start(bf16[2048,128]{1,0:T(8,128)(2,1)S(1)} %get-tuple-element.33.refs_7_), channel_id=1, source_target_pairs={{8,0},{12,4},{16,24},{20,28},{9,1},{13,5},{17,25},{21,29},{10,2},{... | collective-permute-start | bytes 1572872 | tf_op jit(solution)/shard_map/ppermute | solution.py:367
  68.0 51.6 %collective-permute-start.17 = (bf16[3072,128]{1,0:T(8,128)(2,1)S(1)}, bf16[3072,128]{1,0:T(8,128)(2,1)S(1)}, u32[]{:S(2)}, u32[]{:S(2)}) collective-permute-start(bf16[3072,128]{1,0:T(8,128)(2,1)S(1)} %get-tuple-element.36), channel_id=1, source_target_pairs={{8,12},{12,8},{16,20},{20,16},{9,13},{13,9},{17,21},{21,17},{10,14... | collective-permute-start | bytes 2359304 | tf_op jit(solution)/shard_map/ppermute | solution.py:367
  68.7 37.6 %collective-permute-start.19 = (bf16[1024,128]{1,0:T(8,128)(2,1)S(1)}, bf16[1024,128]{1,0:T(8,128)(2,1)S(1)}, u32[]{:S(2)}, u32[]{:S(2)}) collective-permute-start(bf16[1024,128]{1,0:T(8,128)(2,1)S(1)} %get-tuple-element.37), channel_id=1, source_target_pairs={{9,5},{13,1},{17,29},{21,25},{10,6},{14,2},{18,30},{22,26}} | collective-permute-start | bytes 786440 | tf_op jit(solution)/shard_map/ppermute | solution.py:367
  70.0 41.3 %collective-permute-start.18 = (bf16[2048,128]{1,0:T(8,128)(2,1)S(1)}, bf16[2048,128]{1,0:T(8,128)(2,1)S(1)}, u32[]{:S(2)}, u32[]{:S(2)}) collective-permute-start(bf16[2048,128]{1,0:T(8,128)(2,1)S(1)} %get-tuple-element.34.refs_8_), channel_id=1, source_target_pairs={{8,4},{12,0},{16,28},{20,24},{9,5},{13,1},{17,29},{21,25},{10,6},{... | collective-permute-start | bytes 1572872 | tf_op jit(solution)/shard_map/ppermute | solution.py:367
  101.0 10.3 %collective-permute-start.15 = (bf16[2048,128]{1,0:T(8,128)(2,1)S(1)}, bf16[2048,128]{1,0:T(8,128)(2,1)S(1)}, u32[]{:S(2)}, u32[]{:S(2)}) collective-permute-start(bf16[2048,128]{1,0:T(8,128)(2,1)S(1)} %get-tuple-element.35), channel_id=1, source_target_pairs={{9,1},{13,5},{17,25},{21,29},{10,2},{14,6},{18,26},{22,30}} | collective-permute-start | bytes 1572872 | tf_op jit(solution)/shard_map/ppermute | solution.py:367
  106.3 8.8 %collective-permute-start.11 = (bf16[5,3,128,128]{3,2,1,0:T(8,128)(2,1)S(1)}, bf16[5,3,128,128]{3,2,1,0:T(8,128)(2,1)S(1)}, u32[]{:S(2)}, u32[]{:S(2)}) collective-permute-start(bf16[5,3,128,128]{3,2,1,0:T(8,128)(2,1)S(1)} %get-tuple-element.31), channel_id=1, source_target_pairs={{0,1},{1,2},{2,3},{4,5},{5,6},{6,7},{8,9},{9,10},{10,11},{12,13},{... | collective-permute-start | bytes 1474568 | tf_op jit(solution)/shard_map/ppermute | solution.py:376
  109.4 10.1 %collective-permute-start.12 = (bf16[5,3,128,128]{3,2,1,0:T(8,128)(2,1)S(1)}, bf16[5,3,128,128]{3,2,1,0:T(8,128)(2,1)S(1)}, u32[]{:S(2)}, u32[]{:S(2)}) collective-permute-start(bf16[5,3,128,128]{3,2,1,0:T(8,128)(2,1)S(1)} %get-tuple-element.32), channel_id=1, source_target_pairs={{1,0},{2,1},{3,2},{5,4},{6,5},{7,6},{9,8},{10,9},{11,10},{13,12},{... | collective-permute-start | bytes 1474568 | tf_op jit(solution)/shard_map/ppermute | solution.py:377
  122.3 6.7 %collective-permute-start.20 = (bf16[3,3,128,128]{3,2,1,0:T(8,128)(2,1)S(1)}, bf16[3,3,128,128]{3,2,1,0:T(8,128)(2,1)S(1)}, u32[]{:S(2)}, u32[]{:S(2)}) collective-permute-start(bf16[3,3,128,128]{3,2,1,0:T(8,128)(2,1)S(1)} %get-tuple-element.39), channel_id=1, source_target_pairs={{0,1},{1,2},{2,3},{4,5},{5,6},{6,7},{8,9},{9,10},{10,11},{12,13},{... | collective-permute-start | bytes 884744 | tf_op jit(solution)/shard_map/ppermute | solution.py:376
  125.4 8.0 %collective-permute-start.21 = (bf16[3,3,128,128]{3,2,1,0:T(8,128)(2,1)S(1)}, bf16[3,3,128,128]{3,2,1,0:T(8,128)(2,1)S(1)}, u32[]{:S(2)}, u32[]{:S(2)}) collective-permute-start(bf16[3,3,128,128]{3,2,1,0:T(8,128)(2,1)S(1)} %get-tuple-element.40), channel_id=1, source_target_pairs={{1,0},{2,1},{3,2},{5,4},{6,5},{7,6},{9,8},{10,9},{11,10},{13,12},{... | collective-permute-start | bytes 884744 | tf_op jit(solution)/shard_map/ppermute | solution.py:377

commit v13 on v12

--- a/solution.py
+++ b/solution.py
@@ -403,20 +403,21 @@
     tables = [(half[0],), *[((x, 0),) for x in end_lists]]
     end_heads = [move(early, grid.ends(0))]
 
+    def half_requests(z, y):
+        return [(index, grid.panel(grid.lines(z)[0], y, 0), 0, index, 0) for index in range(count)]
+
+    half_picked = pick(grid, half_requests, [(3, cap)] * count, side_lists, [half], after=[x for ((x, _),) in beside], cost=COST)
+    half_crossed = move_across(half_picked)
+
     def other_requests(z, y):
         return [(index, grid.panel(grid.lines(z)[1], y, 0), 0, index, 0) for index in range(count)]
 
-    picked = pick(grid, other_requests, [(3, cap)] * count, side_lists, [other], after=[x for ((x, _),) in beside], cost=COST)
+    end_picked = pick(grid, other_requests, [(3, cap)] * count, [], [other, *tables[1:]],
+                      tables=tuple(range(1, 1 + count)), after=[*half_picked, end_heads[0]], cost=COST)
+    end_crossed = [((move(x, grid.ends(shift)), 3),) for x, shift in zip(end_picked, sides)]
+    picked = pick(grid, other_requests, [(3, cap)] * count, side_lists, [other],
+                  after=[x for ((x, _),) in half_crossed], cost=COST)
     other_crossed = move_across(picked, mids)
-    end_picked = pick(grid, other_requests, [(3, cap)] * count, [], [other, *tables[1:]],
-                      tables=tuple(range(1, 1 + count)), after=[*picked, end_heads[0]], cost=COST)
-    end_crossed = [((move(x, grid.ends(shift)), 3),) for x, shift in zip(end_picked, sides)]
-
-    def half_requests(z, y):
-        return [(index, grid.panel(grid.lines(z)[0], y, 0), 0, index, 0) for index in range(count)]
-
-    picked = pick(grid, half_requests, [(3, cap)] * count, side_lists, [half], after=[x for ((x, _),) in other_crossed], cost=COST)
-    half_crossed = move_across(picked)
     far_tail = move(half[1][0], grid.swaps([(1, 2)]), inner)
     far = ((far_head, 2), (far_tail, 1))
     parts = stage(grid, grid.work_near, lists, turned, matrix, [own, half, *beside])
@@ -436,7 +437,7 @@
                 [(count + 1 + index, row, 2, count + 1 + index, 0) for index in range(count)])
 
     picked = pick(grid, last_requests, [(3, cap)] * count + [(1, 2 * cap)] + [(1, cap)] * count, side_lists,
-                  [far, other[1:], far[1:], *tables], tables=tuple(range(3, 4 + count)), after=[*far_picked, end_heads[0], *[x for ((x, _),) in end_crossed], *[x for ((x, _),) in other_crossed]],
+                  [far, other[1:], far[1:], *tables], tables=tuple(range(3, 4 + count)), after=[*far_picked, end_heads[0], *[x for ((x, _),) in end_crossed], *[x for ((x, _),) in half_crossed]],
                   cost=PICK_COST)
     far_crossed = move_across(picked, mids)
     end_tail = move(picked[count], grid.ends(0), inner)

time: 137 us -> 126 us (0.920)
  waiting for transfers between devices: 74.4 us -> 63.4 us
  Pallas kernels: 22.7 us -> 25.8 us
  starting transfers between devices: 36.1 us -> 33.6 us
    ppermute x2, waiting for transfers between devices: 8.8 us -> 4.4 us  [exchange(): lax.ppermute(parts[2], 'rows', [(g + 1, g) for g in range(groups - 1)])]
    ppermute x2, waiting for transfers between devices: 5.51 us -> 1.72 us  [exchange(): lax.ppermute(parts[1], 'rows', [(g, g + 1) for g in range(groups - 1)])]
    ppermute x18, waiting for transfers between devices: 60.1 us -> 57.2 us  [move(): return lax.ppermute(x, ('blk', 'rows'), perm) if perm else jnp.zeros_like(x)]
    ppermute x2, starting transfers between devices: 6.09 us -> 4.56 us  [exchange(): lax.ppermute(parts[1], 'rows', [(g, g + 1) for g in range(groups - 1)])]
    ppermute x18, starting transfers between devices: 26.2 us -> 24.7 us  [move(): return lax.ppermute(x, ('blk', 'rows'), perm) if perm else jnp.zeros_like(x)]
  transfers between devices with their start and end apart: 22 -> 22, of which waited for: 10 -> 10; matrix products, arithmetic and copies ran while one was open for 0% -> 0% of each run, Pallas kernels for 11% -> 14%
where the time goes in v13:
time: 126 us; the launch traced here: 124 us
  waiting for transfers between devices  63.4 us (50%)
  starting transfers between devices  33.6 us (27%)
  Pallas kernels  25.8 us (20%)
  local copies, waits for them, and re-layouts  1.26 us (1%)
    ppermute x18, waiting for transfers between devices, move(): return lax.ppermute(x, ('blk', 'rows'), perm) if perm else jnp.zeros_like(x)  57.2 us
    ppermute x18, starting transfers between devices, move(): return lax.ppermute(x, ('blk', 'rows'), perm) if perm else jnp.zeros_like(x)  24.7 us
    pallas_call x3, Pallas kernels, stage(): pl.pallas_call(functools.partial(stage_kernel, grid, plan, layout, carrie...  12.2 us
    pallas_call x7, Pallas kernels, pick(): pl.pallas_call(functools.partial(pick_kernel, grid, plan, layout, carry,...  6.95 us
    ppermute x2, starting transfers between devices, exchange(): lax.ppermute(parts[1], 'rows', [(g, g + 1) for g in range(groups - 1)])  4.56 us
    ppermute x2, waiting for transfers between devices, exchange(): lax.ppermute(parts[2], 'rows', [(g + 1, g) for g in range(groups - 1)])  4.4 us
    ppermute x2, starting transfers between devices, exchange(): lax.ppermute(parts[2], 'rows', [(g + 1, g) for g in range(groups - 1)])  4.35 us
    pallas_call x1, Pallas kernels, pack(): pl.pallas_call(functools.partial(pack_kernel, grid), grid=(1,), in_specs=...  2.64 us
  transfers between devices with their start and end apart: 22, of which 10 were waited for; matrix products, arithmetic and copies ran while one was open for 0% of the time, Pallas kernels for 14%

profile of v13, /device:TPU:1, one launch (start us, length us, event | category | flops | bytes accessed | tf_op | source)
XLA Modules:
  0.0 124.4 jit_solution(13710466825147457901)
XLA Ops:
  0.0 2.6 %pack_rows.1 = (bf16[4112,128]{1,0:T(8,128)(2,1)}, bf16[2048,128]{1,0:T(8,128)(2,1)}) custom-call(s32[3,1,16]{2,1,0:T(1,128)} %bitcast.26, s32[8,8]{1,0:T(8,128)} %bitcast.14, bf16[16,128,384]{2,1,0:T(8,128)(2,1)} %bitcast.25), custom_call_target="tpu_custom_call" | custom-call | flops 1024 | bytes 1024 | tf_op jit(solution)/shard_map/pack_rows/pallas_call | solution.py:131
  2.6 2.2 %collective-permute-start.1 = (bf16[4112,128]{1,0:T(8,128)(2,1)}, bf16[4112,128]{1,0:T(8,128)(2,1)S(1)}, u32[]{:S(2)}, u32[]{:S(2)}) collective-permute-start(bf16[4112,128]{1,0:T(8,128)(2,1)} %get-tuple-element.23.head.refs_1_.refs_0_), channel_id=1, source_target_pairs={{0,8},{4,12},{16,24},{20,28},{8,0},{12,4},{24,16},{28,20},{1,9},{5... | collective-permute-start | bytes 3158024 | tf_op jit(solution)/shard_map/ppermute | solution.py:367
  4.8 0.7 collective-permute-start.5
  5.6 0.0 copy-done.3
  5.6 1.3 %collective-permute-start = (s32[8,8]{1,0:T(8,128)S(1)}, s32[8,8]{1,0:T(8,128)S(1)}, u32[]{:S(2)}, u32[]{:S(2)}) collective-permute-start(s32[8,8]{1,0:T(8,128)S(1)} %bitcast.15), channel_id=1, source_target_pairs={{4,0},{0,4},{12,8},{8,12},{20,16},{16,20},{28,24},{24,28},{5,1},{1... | collective-permute-start | bytes 776 | tf_op jit(solution)/shard_map/ppermute | solution.py:367
  6.9 1.5 %collective-permute-done.refs_0_ = s32[8,8]{1,0:T(8,128)S(1)} collective-permute-done((s32[8,8]{1,0:T(8,128)S(1)}, s32[8,8]{1,0:T(8,128)S(1)}, u32[]{:S(2)}, u32[]{:S(2)}) %collective-permute-start) | collective-permute-done | bytes 288 | tf_op jit(solution)/shard_map/ppermute | solution.py:367
  8.4 1.2 copy-done.1
  9.6 1.7 %pick_rows.7 = bf16[3072,128]{1,0:T(8,128)(2,1)S(1)} custom-call(s32[8,8]{1,0:T(8,128)S(1)} %collective-permute-done.refs_0_, bf16[4112,128]{1,0:T(8,128)(2,1)S(1)} %copy-done.1, bf16[2048,128]{1,0:T(8,128)(2,1)} %get-tuple-element.24.tail.refs_2_.refs_1_), custom_call_target="tpu_custom_call" | custom-call | flops 1024 | bytes 1024 | tf_op jit(solution)/shard_map/pick_rows/pallas_call | solution.py:223
  11.3 1.3 %collective-permute-start.3 = (bf16[3072,128]{1,0:T(8,128)(2,1)S(1)}, bf16[3072,128]{1,0:T(8,128)(2,1)S(1)}, u32[]{:S(2)}, u32[]{:S(2)}) collective-permute-start(bf16[3072,128]{1,0:T(8,128)(2,1)S(1)} %pick_rows.7), channel_id=1, source_target_pairs={{0,4},{4,0},{8,12},{12,8},{16,20},{20,16},{24,28},{28,24},{1,5},{5... | collective-permute-start | bytes 2359304 | tf_op jit(solution)/shard_map/ppermute | solution.py:367
  12.6 5.7 %collective-permute-start.2 = (bf16[2048,128]{1,0:T(8,128)(2,1)}, bf16[2048,128]{1,0:T(8,128)(2,1)S(1)}, u32[]{:S(2)}, u32[]{:S(2)}) collective-permute-start(bf16[2048,128]{1,0:T(8,128)(2,1)} %get-tuple-element.24.tail.refs_2_.refs_1_), channel_id=1, source_target_pairs={{1,9},{5,13},{17,25},{21,29},{9,1},{13,5},{25,17},{29,21},{2,10},{... | collective-permute-start | bytes 1572872 | tf_op jit(solution)/shard_map/ppermute | solution.py:367
  18.3 0.7 collective-permute-start.6
  19.0 9.0 %collective-permute-done.1.refs_1_.refs_2_.refs_5_ = bf16[4112,128]{1,0:T(8,128)(2,1)S(1)} collective-permute-done((bf16[4112,128]{1,0:T(8,128)(2,1)}, bf16[4112,128]{1,0:T(8,128)(2,1)S(1)}, u32[]{:S(2)}, u32[]{:S(2)}) %collective-permute-start.1) | collective-permute-done | bytes 1052704 | tf_op jit(solution)/shard_map/ppermute | solution.py:367
  28.0 0.0 collective-permute-done.5.refs_1_.refs_0_
  28.0 0.7 pick_rows.10
  28.8 1.3 %collective-permute-start.9 = (bf16[2048,128]{1,0:T(8,128)(2,1)S(1)}, bf16[2048,128]{1,0:T(8,128)(2,1)S(1)}, u32[]{:S(2)}, u32[]{:S(2)}) collective-permute-start(bf16[2048,128]{1,0:T(8,128)(2,1)S(1)} %get-tuple-element.26), channel_id=1, source_target_pairs={{8,0},{12,4},{16,24},{20,28},{9,1},{13,5},{17,25},{21,29},{10,2},{... | collective-permute-start | bytes 1572872 | tf_op jit(solution)/shard_map/ppermute | solution.py:367
  30.1 0.7 collective-permute-start.13
  30.8 3.4 %collective-permute-done.2.refs_2_.refs_3_ = bf16[2048,128]{1,0:T(8,128)(2,1)S(1)} collective-permute-done((bf16[2048,128]{1,0:T(8,128)(2,1)}, bf16[2048,128]{1,0:T(8,128)(2,1)S(1)}, u32[]{:S(2)}, u32[]{:S(2)}) %collective-permute-start.2) | collective-permute-done | bytes 524320 | tf_op jit(solution)/shard_map/ppermute | solution.py:367
  34.2 0.7 collective-permute-start.8
  34.8 0.0 collective-permute-done.3.refs_3_.refs_4_
  34.8 0.7 pick_rows.8.refs_3_
  35.5 0.0 copy-start.2
  35.5 1.5 %collective-permute-start.4 = (bf16[3072,128]{1,0:T(8,128)(2,1)S(1)}, bf16[3072,128]{1,0:T(8,128)(2,1)S(1)}, u32[]{:S(2)}, u32[]{:S(2)}) collective-permute-start(bf16[3072,128]{1,0:T(8,128)(2,1)S(1)} %pick_rows.8.refs_3_), channel_id=1, source_target_pairs={{0,4},{4,0},{8,12},{12,8},{16,20},{20,16},{24,28},{28,24},{1,5},{5... | collective-permute-start | bytes 2359304 | tf_op jit(solution)/shard_map/ppermute | solution.py:367
  37.0 0.0 collective-permute-done.6.refs_2_.refs_1_.refs_3_
  37.0 0.0 collective-permute-done.8.refs_2_.refs_6_
  37.0 6.7 %collective-permute-done.9.refs_4_.refs_9_.refs_2_ = bf16[2048,128]{1,0:T(8,128)(2,1)S(1)} collective-permute-done((bf16[2048,128]{1,0:T(8,128)(2,1)S(1)}, bf16[2048,128]{1,0:T(8,128)(2,1)S(1)}, u32[]{:S(2)}, u32[]{:S(2)}) %collective-permute-start.9) | collective-permute-done | bytes 524320 | tf_op jit(solution)/shard_map/ppermute | solution.py:367
  43.7 0.7 pick_rows.11
  44.5 0.0 copy-start
  44.5 0.0 copy-start.4
  44.5 0.0 copy-start.5
  44.5 1.4 %collective-permute-start.10 = (bf16[3072,128]{1,0:T(8,128)(2,1)S(1)}, bf16[3072,128]{1,0:T(8,128)(2,1)S(1)}, u32[]{:S(2)}, u32[]{:S(2)}) collective-permute-start(bf16[3072,128]{1,0:T(8,128)(2,1)S(1)} %pick_rows.11), channel_id=1, source_target_pairs={{8,4},{12,0},{16,28},{20,24},{9,5},{13,1},{17,29},{21,25},{10,6},{... | collective-permute-start | bytes 2359304 | tf_op jit(solution)/shard_map/ppermute | solution.py:367
  46.0 0.7 collective-permute-start.14
  46.7 0.0 copy-done.2
  46.7 1.5 %turn_rows.1.turned = bf16[16,384,128]{2,1,0:T(8,128)(2,1)S(1)} custom-call(bf16[4112,128]{1,0:T(8,128)(2,1)S(1)} %copy-done.2, bf16[2048,128]{1,0:T(8,128)(2,1)} %get-tuple-element.24.tail.refs_2_.refs_1_), custom_call_target="tpu_custom_call" | custom-call | flops 1024 | bytes 1024 | tf_op jit(solution)/shard_map/turn_rows/pallas_call | solution.py:160
  48.2 5.9 %stage_products.3 = (bf16[3,3,128,128]{3,2,1,0:T(8,128)(2,1)S(1)}, bf16[3,3,128,128]{3,2,1,0:T(8,128)(2,1)S(1)}, bf16[3,3,128,128]{3,2,1,0:T(8,128)(2,1)S(1)}) custom-call(s32[8,8]{1,0:T(8,128)S(1)} %bitcast.19, s32[8,8]{1,0:T(8,128)S(1)} %bitcast.16, s32[1,8]{1,0:T(1,128)S(1)} %bitcast.22, bf16[16,384,128]{2,1,0:T(8,128)(2,1)S(1)} %turn_rows.1.turned, ...), custom_call_target="tpu_custom_call" | custom-call | flops 1024 | bytes 1024 | tf_op jit(solution)/shard_map/stage_products/pallas_call | solution.py:302
  54.1 16.7 %collective-permute-done.4.refs_3_.refs_0_.refs_11_ = bf16[3072,128]{1,0:T(8,128)(2,1)S(1)} collective-permute-done((bf16[3072,128]{1,0:T(8,128)(2,1)S(1)}, bf16[3072,128]{1,0:T(8,128)(2,1)S(1)}, u32[]{:S(2)}, u32[]{:S(2)}) %collective-permute-start.4) | collective-permute-done | bytes 786464 | tf_op jit(solution)/shard_map/ppermute | solution.py:367
  70.9 0.7 pick_rows.9
  71.6 0.7 collective-permute-start.7
  72.3 0.0 collective-permute-done.13.refs_0_.refs_1_.refs_4_
  72.3 0.9 pick_rows.12
  73.2 1.3 %collective-permute-start.16 = (bf16[2048,128]{1,0:T(8,128)(2,1)S(1)}, bf16[2048,128]{1,0:T(8,128)(2,1)S(1)}, u32[]{:S(2)}, u32[]{:S(2)}) collective-permute-start(bf16[2048,128]{1,0:T(8,128)(2,1)S(1)} %get-tuple-element.33.refs_7_), channel_id=1, source_target_pairs={{8,0},{12,4},{16,24},{20,28},{9,1},{13,5},{17,25},{21,29},{10,2},{... | collective-permute-start | bytes 1572872 | tf_op jit(solution)/shard_map/ppermute | solution.py:367
  74.5 0.0 collective-permute-done.14.refs_2_.refs_4_.refs_5_
  74.5 0.0 collective-permute-done.10.refs_2_.refs_10_
  74.5 1.5 %pick_rows.13 = (bf16[3072,128]{1,0:T(8,128)(2,1)S(1)}, bf16[2048,128]{1,0:T(8,128)(2,1)S(1)}, bf16[1024,128]{1,0:T(8,128)(2,1)S(1)}) custom-call(s32[8,8]{1,0:T(8,128)S(1)} %collective-permute-done.refs_0_, bf16[4112,128]{1,0:T(8,128)(2,1)S(1)} %collective-permute-done.13.refs_0_.refs_1_.refs_4_, ...), custom_call_target="tpu_custom_call" | custom-call | flops 20000000000 | bytes 1024 | tf_op jit(solution)/shard_map/pick_rows/pallas_call | solution.py:223
  76.1 0.7 collective-permute-start.17
  76.8 1.3 %collective-permute-start.19 = (bf16[1024,128]{1,0:T(8,128)(2,1)S(1)}, bf16[1024,128]{1,0:T(8,128)(2,1)S(1)}, u32[]{:S(2)}, u32[]{:S(2)}) collective-permute-start(bf16[1024,128]{1,0:T(8,128)(2,1)S(1)} %get-tuple-element.37), channel_id=1, source_target_pairs={{9,5},{13,1},{17,29},{21,25},{10,6},{14,2},{18,30},{22,26}} | collective-permute-start | bytes 786440 | tf_op jit(solution)/shard_map/ppermute | solution.py:367
  78.1 1.3 %collective-permute-start.18 = (bf16[2048,128]{1,0:T(8,128)(2,1)S(1)}, bf16[2048,128]{1,0:T(8,128)(2,1)S(1)}, u32[]{:S(2)}, u32[]{:S(2)}) collective-permute-start(bf16[2048,128]{1,0:T(8,128)(2,1)S(1)} %get-tuple-element.34.refs_8_), channel_id=1, source_target_pairs={{8,4},{12,0},{16,28},{20,24},{9,5},{13,1},{17,29},{21,25},{10,6},{... | collective-permute-start | bytes 1572872 | tf_op jit(solution)/shard_map/ppermute | solution.py:367
  79.4 0.0 collective-permute-done.7.refs_1_
  79.4 1.3 %collective-permute-start.15 = (bf16[2048,128]{1,0:T(8,128)(2,1)S(1)}, bf16[2048,128]{1,0:T(8,128)(2,1)S(1)}, u32[]{:S(2)}, u32[]{:S(2)}) collective-permute-start(bf16[2048,128]{1,0:T(8,128)(2,1)S(1)} %get-tuple-element.35), channel_id=1, source_target_pairs={{9,1},{13,5},{17,25},{21,29},{10,2},{14,6},{18,26},{22,30}} | collective-permute-start | bytes 1572872 | tf_op jit(solution)/shard_map/ppermute | solution.py:367
  80.7 3.5 %stage_products.4 = (bf16[5,3,128,128]{3,2,1,0:T(8,128)(2,1)S(1)}, bf16[5,3,128,128]{3,2,1,0:T(8,128)(2,1)S(1)}, bf16[5,3,128,128]{3,2,1,0:T(8,128)(2,1)S(1)}) custom-call(s32[8,8]{1,0:T(8,128)S(1)} %bitcast.20, s32[8,8]{1,0:T(8,128)S(1)} %bitcast.17, s32[1,8]{1,0:T(1,128)S(1)} %bitcast.23, bf16[16,384,128]{2,1,0:T(8,128)(2,1)S(1)} %turn_rows.1.turned, ...), custom_call_target="tpu_custom_call" | custom-call | flops 1024 | bytes 1024 | tf_op jit(solution)/shard_map/stage_products/pallas_call | solution.py:302
  84.2 11.2 %collective-permute-done.19.refs_10_ = bf16[1024,128]{1,0:T(8,128)(2,1)S(1)} collective-permute-done((bf16[1024,128]{1,0:T(8,128)(2,1)S(1)}, bf16[1024,128]{1,0:T(8,128)(2,1)S(1)}, u32[]{:S(2)}, u32[]{:S(2)}) %collective-permute-start.19) | collective-permute-done | bytes 262176 | tf_op jit(solution)/shard_map/ppermute | solution.py:367
  95.5 1.9 %collective-permute-start.11 = (bf16[5,3,128,128]{3,2,1,0:T(8,128)(2,1)S(1)}, bf16[5,3,128,128]{3,2,1,0:T(8,128)(2,1)S(1)}, u32[]{:S(2)}, u32[]{:S(2)}) collective-permute-start(bf16[5,3,128,128]{3,2,1,0:T(8,128)(2,1)S(1)} %get-tuple-element.31), channel_id=1, source_target_pairs={{0,1},{1,2},{2,3},{4,5},{5,6},{6,7},{8,9},{9,10},{10,11},{12,13},{... | collective-permute-start | bytes 1474568 | tf_op jit(solution)/shard_map/ppermute | solution.py:376
  97.4 0.0 collective-permute-done.16.refs_6_
  97.4 2.4 %collective-permute-start.12 = (bf16[5,3,128,128]{3,2,1,0:T(8,128)(2,1)S(1)}, bf16[5,3,128,128]{3,2,1,0:T(8,128)(2,1)S(1)}, u32[]{:S(2)}, u32[]{:S(2)}) collective-permute-start(bf16[5,3,128,128]{3,2,1,0:T(8,128)(2,1)S(1)} %get-tuple-element.32), channel_id=1, source_target_pairs={{1,0},{2,1},{3,2},{5,4},{6,5},{7,6},{9,8},{10,9},{11,10},{13,12},{... | collective-permute-start | bytes 1474568 | tf_op jit(solution)/shard_map/ppermute | solution.py:377
  99.8 4.4 %collective-permute-done.18.refs_9_ = bf16[2048,128]{1,0:T(8,128)(2,1)S(1)} collective-permute-done((bf16[2048,128]{1,0:T(8,128)(2,1)S(1)}, bf16[2048,128]{1,0:T(8,128)(2,1)S(1)}, u32[]{:S(2)}, u32[]{:S(2)}) %collective-permute-start.18) | collective-permute-done | bytes 524320 | tf_op jit(solution)/shard_map/ppermute | solution.py:367
  104.2 4.2 %collective-permute-done.15.refs_3_.refs_7_ = bf16[2048,128]{1,0:T(8,128)(2,1)S(1)} collective-permute-done((bf16[2048,128]{1,0:T(8,128)(2,1)S(1)}, bf16[2048,128]{1,0:T(8,128)(2,1)S(1)}, u32[]{:S(2)}, u32[]{:S(2)}) %collective-permute-start.15) | collective-permute-done | bytes 524320 | tf_op jit(solution)/shard_map/ppermute | solution.py:367
  108.4 0.0 collective-permute-done.11.refs_11_.refs_1_
  108.4 0.0 collective-permute-done.12.refs_12_.refs_2_
  108.4 0.0 collective-permute-done.17.refs_8_
  108.4 2.8 %stage_products.5 = (bf16[3,3,128,128]{3,2,1,0:T(8,128)(2,1)S(1)}, bf16[3,3,128,128]{3,2,1,0:T(8,128)(2,1)S(1)}, bf16[3,3,128,128]{3,2,1,0:T(8,128)(2,1)S(1)}) custom-call(s32[8,8]{1,0:T(8,128)S(1)} %bitcast.21, s32[8,8]{1,0:T(8,128)S(1)} %bitcast.18, s32[1,8]{1,0:T(1,128)S(1)} %bitcast.24, bf16[16,384,128]{2,1,0:T(8,128)(2,1)S(1)} %turn_rows.1.turned, ...), custom_call_target="tpu_custom_call" | custom-call | flops 1024 | bytes 1024 | tf_op jit(solution)/shard_map/stage_products/pallas_call | solution.py:302
  111.2 2.7 %collective-permute-start.20 = (bf16[3,3,128,128]{3,2,1,0:T(8,128)(2,1)S(1)}, bf16[3,3,128,128]{3,2,1,0:T(8,128)(2,1)S(1)}, u32[]{:S(2)}, u32[]{:S(2)}) collective-permute-start(bf16[3,3,128,128]{3,2,1,0:T(8,128)(2,1)S(1)} %get-tuple-element.39), channel_id=1, source_target_pairs={{0,1},{1,2},{2,3},{4,5},{5,6},{6,7},{8,9},{9,10},{10,11},{12,13},{... | collective-permute-start | bytes 884744 | tf_op jit(solution)/shard_map/ppermute | solution.py:376
  113.9 1.9 %collective-permute-start.21 = (bf16[3,3,128,128]{3,2,1,0:T(8,128)(2,1)S(1)}, bf16[3,3,128,128]{3,2,1,0:T(8,128)(2,1)S(1)}, u32[]{:S(2)}, u32[]{:S(2)}) collective-permute-start(bf16[3,3,128,128]{3,2,1,0:T(8,128)(2,1)S(1)} %get-tuple-element.40), channel_id=1, source_target_pairs={{1,0},{2,1},{3,2},{5,4},{6,5},{7,6},{9,8},{10,9},{11,10},{13,12},{... | collective-permute-start | bytes 884744 | tf_op jit(solution)/shard_map/ppermute | solution.py:377
  115.8 1.7 %collective-permute-done.20.refs_4_ = bf16[3,3,128,128]{3,2,1,0:T(8,128)(2,1)S(1)} collective-permute-done((bf16[3,3,128,128]{3,2,1,0:T(8,128)(2,1)S(1)}, bf16[3,3,128,128]{3,2,1,0:T(8,128)(2,1)S(1)}, u32[]{:S(2)}, u32[]{:S(2)}) %collective-permute-start.20) | collective-permute-done | bytes 294944 | tf_op jit(solution)/shard_map/ppermute | solution.py:376
  117.5 4.4 %collective-permute-done.21.refs_5_ = bf16[3,3,128,128]{3,2,1,0:T(8,128)(2,1)S(1)} collective-permute-done((bf16[3,3,128,128]{3,2,1,0:T(8,128)(2,1)S(1)}, bf16[3,3,128,128]{3,2,1,0:T(8,128)(2,1)S(1)}, u32[]{:S(2)}, u32[]{:S(2)}) %collective-permute-start.21) | collective-permute-done | bytes 294944 | tf_op jit(solution)/shard_map/ppermute | solution.py:377
  121.9 2.5 %assemble_coarse.1 = f32[5120,128]{1,0:T(8,128)} custom-call(bf16[5,3,128,128]{3,2,1,0:T(8,128)(2,1)S(1)} %get-tuple-element.30.refs_0_, bf16[5,3,128,128]{3,2,1,0:T(8,128)(2,1)S(1)} %collective-permute-done.11.refs_11_.refs_1_, bf16[5,3,128,128]{3,2,1,0:T(8,128)(2,1)S(1)} %collective-permute-done.12.refs_12_.refs_2_, ...), custom_call_target="tpu_custom_call" | custom-call | flops 1024 | bytes 1024 | tf_op jit(solution)/shard_map/assemble_coarse/pallas_call | solution.py:343
  (5 shorter events, 0.0 us)
Async XLA Ops:
  0.0 5.6 %copy-start.3 = (s32[1,1,8,8]{3,2,1,0:T(8,128)S(1)}, s32[1,1,8,8]{3,2,1,0:T(8,128)}, u32[]{:S(2)}) copy-start(s32[1,1,8,8]{3,2,1,0:T(8,128)} %param.8) | copy-start | bytes 772
  2.6 25.4 %collective-permute-start.1 = (bf16[4112,128]{1,0:T(8,128)(2,1)}, bf16[4112,128]{1,0:T(8,128)(2,1)S(1)}, u32[]{:S(2)}, u32[]{:S(2)}) collective-permute-start(bf16[4112,128]{1,0:T(8,128)(2,1)} %get-tuple-element.23.head.refs_1_.refs_0_), channel_id=1, source_target_pairs={{0,8},{4,12},{16,24},{20,28},{8,0},{12,4},{24,16},{28,20},{1,9},{5... | collective-permute-start | bytes 3158024 | tf_op jit(solution)/shard_map/ppermute | solution.py:367
  4.8 23.2 %collective-permute-start.5 = (bf16[4112,128]{1,0:T(8,128)(2,1)}, bf16[4112,128]{1,0:T(8,128)(2,1)S(1)}, u32[]{:S(2)}, u32[]{:S(2)}) collective-permute-start(bf16[4112,128]{1,0:T(8,128)(2,1)} %get-tuple-element.23.head.refs_1_.refs_0_), channel_id=1, source_target_pairs={{8,16},{12,20},{16,8},{20,12},{9,17},{13,21},{17,9},{21,13},{10,18... | collective-permute-start | bytes 3158024 | tf_op jit(solution)/shard_map/ppermute | solution.py:367
  5.6 2.8 %collective-permute-start = (s32[8,8]{1,0:T(8,128)S(1)}, s32[8,8]{1,0:T(8,128)S(1)}, u32[]{:S(2)}, u32[]{:S(2)}) collective-permute-start(s32[8,8]{1,0:T(8,128)S(1)} %bitcast.15), channel_id=1, source_target_pairs={{4,0},{0,4},{12,8},{8,12},{20,16},{16,20},{28,24},{24,28},{5,1},{1... | collective-permute-start | bytes 776 | tf_op jit(solution)/shard_map/ppermute | solution.py:367
  8.4 1.2 copy-start.1
  11.3 23.5 %collective-permute-start.3 = (bf16[3072,128]{1,0:T(8,128)(2,1)S(1)}, bf16[3072,128]{1,0:T(8,128)(2,1)S(1)}, u32[]{:S(2)}, u32[]{:S(2)}) collective-permute-start(bf16[3072,128]{1,0:T(8,128)(2,1)S(1)} %pick_rows.7), channel_id=1, source_target_pairs={{0,4},{4,0},{8,12},{12,8},{16,20},{20,16},{24,28},{28,24},{1,5},{5... | collective-permute-start | bytes 2359304 | tf_op jit(solution)/shard_map/ppermute | solution.py:367
  12.6 21.6 %collective-permute-start.2 = (bf16[2048,128]{1,0:T(8,128)(2,1)}, bf16[2048,128]{1,0:T(8,128)(2,1)S(1)}, u32[]{:S(2)}, u32[]{:S(2)}) collective-permute-start(bf16[2048,128]{1,0:T(8,128)(2,1)} %get-tuple-element.24.tail.refs_2_.refs_1_), channel_id=1, source_target_pairs={{1,9},{5,13},{17,25},{21,29},{9,1},{13,5},{25,17},{29,21},{2,10},{... | collective-permute-start | bytes 1572872 | tf_op jit(solution)/shard_map/ppermute | solution.py:367
  18.3 18.7 %collective-permute-start.6 = (bf16[2048,128]{1,0:T(8,128)(2,1)}, bf16[2048,128]{1,0:T(8,128)(2,1)S(1)}, u32[]{:S(2)}, u32[]{:S(2)}) collective-permute-start(bf16[2048,128]{1,0:T(8,128)(2,1)} %get-tuple-element.24.tail.refs_2_.refs_1_), channel_id=1, source_target_pairs={{9,17},{13,21},{17,9},{21,13},{10,18},{14,22},{18,10},{22,14}} | collective-permute-start | bytes 1572872 | tf_op jit(solution)/shard_map/ppermute | solution.py:367
  28.8 15.0 %collective-permute-start.9 = (bf16[2048,128]{1,0:T(8,128)(2,1)S(1)}, bf16[2048,128]{1,0:T(8,128)(2,1)S(1)}, u32[]{:S(2)}, u32[]{:S(2)}) collective-permute-start(bf16[2048,128]{1,0:T(8,128)(2,1)S(1)} %get-tuple-element.26), channel_id=1, source_target_pairs={{8,0},{12,4},{16,24},{20,28},{9,1},{13,5},{17,25},{21,29},{10,2},{... | collective-permute-start | bytes 1572872 | tf_op jit(solution)/shard_map/ppermute | solution.py:367
  30.1 42.2 %collective-permute-start.13 = (bf16[4112,128]{1,0:T(8,128)(2,1)S(1)}, bf16[4112,128]{1,0:T(8,128)(2,1)S(1)}, u32[]{:S(2)}, u32[]{:S(2)}) collective-permute-start(bf16[4112,128]{1,0:T(8,128)(2,1)S(1)} %collective-permute-done.1.refs_1_.refs_2_.refs_5_), channel_id=1, source_target_pairs={{8,16},{12,20},{16,8},{20,12},{9,17},{13,21},{17,9},{21,13},{10,18... | collective-permute-start | bytes 3158024 | tf_op jit(solution)/shard_map/ppermute | solution.py:367
  34.2 2.8 %collective-permute-start.8 = (bf16[16,128]{1,0:T(8,128)(2,1)S(1)}, bf16[16,128]{1,0:T(8,128)(2,1)S(1)}, u32[]{:S(2)}, u32[]{:S(2)}) collective-permute-start(bf16[16,128]{1,0:T(8,128)(2,1)S(1)} %get-tuple-element.25), channel_id=1, source_target_pairs={{12,8},{8,12},{20,16},{16,20},{13,9},{9,13},{21,17},{17,21},{14,10... | collective-permute-start | bytes 12296 | tf_op jit(solution)/shard_map/ppermute | solution.py:367
  35.5 11.1 %copy-start.2 = (bf16[4112,128]{1,0:T(8,128)(2,1)S(1)}, bf16[4112,128]{1,0:T(8,128)(2,1)}, u32[]{:S(2)}) copy-start(bf16[4112,128]{1,0:T(8,128)(2,1)} %get-tuple-element.23.head.refs_1_.refs_0_) | copy-start | bytes 3158020
  35.5 35.3 %collective-permute-start.4 = (bf16[3072,128]{1,0:T(8,128)(2,1)S(1)}, bf16[3072,128]{1,0:T(8,128)(2,1)S(1)}, u32[]{:S(2)}, u32[]{:S(2)}) collective-permute-start(bf16[3072,128]{1,0:T(8,128)(2,1)S(1)} %pick_rows.8.refs_3_), channel_id=1, source_target_pairs={{0,4},{4,0},{8,12},{12,8},{16,20},{20,16},{24,28},{28,24},{1,5},{5... | collective-permute-start | bytes 2359304 | tf_op jit(solution)/shard_map/ppermute | solution.py:367
  44.5 3.7 %copy-start = (bf16[1,1,8,8,128,128]{5,4,3,2,1,0:T(8,128)(2,1)S(1)}, bf16[1,1,8,8,128,128]{5,4,3,2,1,0:T(8,128)(2,1)}, u32[]{:S(2)}) copy-start(bf16[1,1,8,8,128,128]{5,4,3,2,1,0:T(8,128)(2,1)} %param.6) | copy-start | bytes 6291460
  44.5 3.7 %copy-start.4 = (s32[1,1,8,8]{3,2,1,0:T(8,128)S(1)}, s32[1,1,8,8]{3,2,1,0:T(8,128)}, u32[]{:S(2)}) copy-start(s32[1,1,8,8]{3,2,1,0:T(8,128)} %param.7) | copy-start | bytes 772
  44.5 3.7 %copy-start.5 = (s32[1,1,8]{2,1,0:T(1,128)S(1)}, s32[1,1,8]{2,1,0:T(1,128)}, u32[]{:S(2)}) copy-start(s32[1,1,8]{2,1,0:T(1,128)} %param.9) | copy-start | bytes 100
  44.5 30.0 %collective-permute-start.10 = (bf16[3072,128]{1,0:T(8,128)(2,1)S(1)}, bf16[3072,128]{1,0:T(8,128)(2,1)S(1)}, u32[]{:S(2)}, u32[]{:S(2)}) collective-permute-start(bf16[3072,128]{1,0:T(8,128)(2,1)S(1)} %pick_rows.11), channel_id=1, source_target_pairs={{8,4},{12,0},{16,28},{20,24},{9,5},{13,1},{17,29},{21,25},{10,6},{... | collective-permute-start | bytes 2359304 | tf_op jit(solution)/shard_map/ppermute | solution.py:367
  46.0 28.6 %collective-permute-start.14 = (bf16[2048,128]{1,0:T(8,128)(2,1)S(1)}, bf16[2048,128]{1,0:T(8,128)(2,1)S(1)}, u32[]{:S(2)}, u32[]{:S(2)}) collective-permute-start(bf16[2048,128]{1,0:T(8,128)(2,1)S(1)} %collective-permute-done.2.refs_2_.refs_3_), channel_id=1, source_target_pairs={{9,17},{13,21},{17,9},{21,13},{10,18},{14,22},{18,10},{22,14}} | collective-permute-start | bytes 1572872 | tf_op jit(solution)/shard_map/ppermute | solution.py:367
  71.6 7.8 %collective-permute-start.7 = (bf16[3072,128]{1,0:T(8,128)(2,1)S(1)}, bf16[3072,128]{1,0:T(8,128)(2,1)S(1)}, u32[]{:S(2)}, u32[]{:S(2)}) collective-permute-start(bf16[3072,128]{1,0:T(8,128)(2,1)S(1)} %pick_rows.9), channel_id=1, source_target_pairs={{8,12},{12,8},{16,20},{20,16},{9,13},{13,9},{17,21},{21,17},{10,14... | collective-permute-start | bytes 2359304 | tf_op jit(solution)/shard_map/ppermute | solution.py:367
  73.2 24.2 %collective-permute-start.16 = (bf16[2048,128]{1,0:T(8,128)(2,1)S(1)}, bf16[2048,128]{1,0:T(8,128)(2,1)S(1)}, u32[]{:S(2)}, u32[]{:S(2)}) collective-permute-start(bf16[2048,128]{1,0:T(8,128)(2,1)S(1)} %get-tuple-element.33.refs_7_), channel_id=1, source_target_pairs={{8,0},{12,4},{16,24},{20,28},{9,1},{13,5},{17,25},{21,29},{10,2},{... | collective-permute-start | bytes 1572872 | tf_op jit(solution)/shard_map/ppermute | solution.py:367
  76.1 32.4 %collective-permute-start.17 = (bf16[3072,128]{1,0:T(8,128)(2,1)S(1)}, bf16[3072,128]{1,0:T(8,128)(2,1)S(1)}, u32[]{:S(2)}, u32[]{:S(2)}) collective-permute-start(bf16[3072,128]{1,0:T(8,128)(2,1)S(1)} %get-tuple-element.36), channel_id=1, source_target_pairs={{8,12},{12,8},{16,20},{20,16},{9,13},{13,9},{17,21},{21,17},{10,14... | collective-permute-start | bytes 2359304 | tf_op jit(solution)/shard_map/ppermute | solution.py:367
  76.8 18.7 %collective-permute-start.19 = (bf16[1024,128]{1,0:T(8,128)(2,1)S(1)}, bf16[1024,128]{1,0:T(8,128)(2,1)S(1)}, u32[]{:S(2)}, u32[]{:S(2)}) collective-permute-start(bf16[1024,128]{1,0:T(8,128)(2,1)S(1)} %get-tuple-element.37), channel_id=1, source_target_pairs={{9,5},{13,1},{17,29},{21,25},{10,6},{14,2},{18,30},{22,26}} | collective-permute-start | bytes 786440 | tf_op jit(solution)/shard_map/ppermute | solution.py:367
  78.1 26.1 %collective-permute-start.18 = (bf16[2048,128]{1,0:T(8,128)(2,1)S(1)}, bf16[2048,128]{1,0:T(8,128)(2,1)S(1)}, u32[]{:S(2)}, u32[]{:S(2)}) collective-permute-start(bf16[2048,128]{1,0:T(8,128)(2,1)S(1)} %get-tuple-element.34.refs_8_), channel_id=1, source_target_pairs={{8,4},{12,0},{16,28},{20,24},{9,5},{13,1},{17,29},{21,25},{10,6},{... | collective-permute-start | bytes 1572872 | tf_op jit(solution)/shard_map/ppermute | solution.py:367
  79.4 29.0 %collective-permute-start.15 = (bf16[2048,128]{1,0:T(8,128)(2,1)S(1)}, bf16[2048,128]{1,0:T(8,128)(2,1)S(1)}, u32[]{:S(2)}, u32[]{:S(2)}) collective-permute-start(bf16[2048,128]{1,0:T(8,128)(2,1)S(1)} %get-tuple-element.35), channel_id=1, source_target_pairs={{9,1},{13,5},{17,25},{21,29},{10,2},{14,6},{18,26},{22,30}} | collective-permute-start | bytes 1572872 | tf_op jit(solution)/shard_map/ppermute | solution.py:367
  95.5 13.0 %collective-permute-start.11 = (bf16[5,3,128,128]{3,2,1,0:T(8,128)(2,1)S(1)}, bf16[5,3,128,128]{3,2,1,0:T(8,128)(2,1)S(1)}, u32[]{:S(2)}, u32[]{:S(2)}) collective-permute-start(bf16[5,3,128,128]{3,2,1,0:T(8,128)(2,1)S(1)} %get-tuple-element.31), channel_id=1, source_target_pairs={{0,1},{1,2},{2,3},{4,5},{5,6},{6,7},{8,9},{9,10},{10,11},{12,13},{... | collective-permute-start | bytes 1474568 | tf_op jit(solution)/shard_map/ppermute | solution.py:376
  97.4 11.0 %collective-permute-start.12 = (bf16[5,3,128,128]{3,2,1,0:T(8,128)(2,1)S(1)}, bf16[5,3,128,128]{3,2,1,0:T(8,128)(2,1)S(1)}, u32[]{:S(2)}, u32[]{:S(2)}) collective-permute-start(bf16[5,3,128,128]{3,2,1,0:T(8,128)(2,1)S(1)} %get-tuple-element.32), channel_id=1, source_target_pairs={{1,0},{2,1},{3,2},{5,4},{6,5},{7,6},{9,8},{10,9},{11,10},{13,12},{... | collective-permute-start | bytes 1474568 | tf_op jit(solution)/shard_map/ppermute | solution.py:377
  111.2 6.3 %collective-permute-start.20 = (bf16[3,3,128,128]{3,2,1,0:T(8,128)(2,1)S(1)}, bf16[3,3,128,128]{3,2,1,0:T(8,128)(2,1)S(1)}, u32[]{:S(2)}, u32[]{:S(2)}) collective-permute-start(bf16[3,3,128,128]{3,2,1,0:T(8,128)(2,1)S(1)} %get-tuple-element.39), channel_id=1, source_target_pairs={{0,1},{1,2},{2,3},{4,5},{5,6},{6,7},{8,9},{9,10},{10,11},{12,13},{... | collective-permute-start | bytes 884744 | tf_op jit(solution)/shard_map/ppermute | solution.py:376
  113.9 8.0 %collective-permute-start.21 = (bf16[3,3,128,128]{3,2,1,0:T(8,128)(2,1)S(1)}, bf16[3,3,128,128]{3,2,1,0:T(8,128)(2,1)S(1)}, u32[]{:S(2)}, u32[]{:S(2)}) collective-permute-start(bf16[3,3,128,128]{3,2,1,0:T(8,128)(2,1)S(1)} %get-tuple-element.40), channel_id=1, source_target_pairs={{1,0},{2,1},{3,2},{5,4},{6,5},{7,6},{9,8},{10,9},{11,10},{13,12},{... | collective-permute-start | bytes 884744 | tf_op jit(solution)/shard_map/ppermute | solution.py:377

commit v14 on v13

--- a/solution.py
+++ b/solution.py
@@ -10,7 +10,6 @@
 PACK_VMEM_LIMIT = 60 * 1024 * 1024
 PARAMS = pltpu.CompilerParams(vmem_limit_bytes=VMEM_LIMIT)
 COST = pl.CostEstimate(flops=1024, bytes_accessed=1024, transcendentals=0)
-PICK_COST = pl.CostEstimate(flops=20000000000, bytes_accessed=1024, transcendentals=0)
 ANYWHERE = pl.BlockSpec(memory_space=pl.ANY)
 
 
@@ -416,7 +415,7 @@
                       tables=tuple(range(1, 1 + count)), after=[*half_picked, end_heads[0]], cost=COST)
     end_crossed = [((move(x, grid.ends(shift)), 3),) for x, shift in zip(end_picked, sides)]
     picked = pick(grid, other_requests, [(3, cap)] * count, side_lists, [other],
-                  after=[x for ((x, _),) in half_crossed], cost=COST)
+                  after=[*end_picked], cost=COST)
     other_crossed = move_across(picked, mids)
     far_tail = move(half[1][0], grid.swaps([(1, 2)]), inner)
     far = ((far_head, 2), (far_tail, 1))
@@ -438,7 +437,7 @@
 
     picked = pick(grid, last_requests, [(3, cap)] * count + [(1, 2 * cap)] + [(1, cap)] * count, side_lists,
                   [far, other[1:], far[1:], *tables], tables=tuple(range(3, 4 + count)), after=[*far_picked, end_heads[0], *[x for ((x, _),) in end_crossed], *[x for ((x, _),) in half_crossed]],
-                  cost=PICK_COST)
+                  cost=COST)
     far_crossed = move_across(picked, mids)
     end_tail = move(picked[count], grid.ends(0), inner)
     far_tails = [move(x, grid.ends(shift), inner) for x, shift in zip(picked[count + 1:], sides)]

time: 126 us -> 119 us (0.944)
  waiting for transfers between devices: 63.4 us -> 52.1 us
  starting transfers between devices: 33.6 us -> 38.5 us
    ppermute x18, waiting for transfers between devices: 57.2 us -> 38.3 us  [move(): return lax.ppermute(x, ('blk', 'rows'), perm) if perm else jnp.zeros_like(x)]
    ppermute x2, starting transfers between devices: 4.56 us -> 9.26 us  [exchange(): lax.ppermute(parts[1], 'rows', [(g, g + 1) for g in range(groups - 1)])]
    ppermute x2, waiting for transfers between devices: 4.4 us -> 8.8 us  [exchange(): lax.ppermute(parts[2], 'rows', [(g + 1, g) for g in range(groups - 1)])]
    ppermute x2, waiting for transfers between devices: 1.72 us -> 5.02 us  [exchange(): lax.ppermute(parts[1], 'rows', [(g, g + 1) for g in range(groups - 1)])]
where the time goes in v14:
time: 119 us; the launch traced here: 118 us
  waiting for transfers between devices  52.1 us (44%)
  starting transfers between devices  38.5 us (32%)
  Pallas kernels  25.8 us (22%)
  local copies, waits for them, and re-layouts  1.26 us (1%)
    ppermute x18, waiting for transfers between devices, move(): return lax.ppermute(x, ('blk', 'rows'), perm) if perm else jnp.zeros_like(x)  38.3 us
    ppermute x18, starting transfers between devices, move(): return lax.ppermute(x, ('blk', 'rows'), perm) if perm else jnp.zeros_like(x)  24.9 us
    pallas_call x3, Pallas kernels, stage(): pl.pallas_call(functools.partial(stage_kernel, grid, plan, layout, carrie...  12.2 us
    ppermute x2, starting transfers between devices, exchange(): lax.ppermute(parts[1], 'rows', [(g, g + 1) for g in range(groups - 1)])  9.26 us
    ppermute x2, waiting for transfers between devices, exchange(): lax.ppermute(parts[2], 'rows', [(g + 1, g) for g in range(groups - 1)])  8.8 us
    pallas_call x7, Pallas kernels, pick(): pl.pallas_call(functools.partial(pick_kernel, grid, plan, layout, carry,...  6.93 us
    ppermute x2, waiting for transfers between devices, exchange(): lax.ppermute(parts[1], 'rows', [(g, g + 1) for g in range(groups - 1)])  5.02 us
    ppermute x2, starting transfers between devices, exchange(): lax.ppermute(parts[2], 'rows', [(g + 1, g) for g in range(groups - 1)])  4.34 us
  transfers between devices with their start and end apart: 22, of which 10 were waited for; matrix products, arithmetic and copies ran while one was open for 0% of the time, Pallas kernels for 14%

profile of v14, /device:TPU:1, one launch (start us, length us, event | category | flops | bytes accessed | tf_op | source)
XLA Modules:
  0.0 117.9 jit_solution(18103095678549523427)
XLA Ops:
  0.0 2.6 %pack_rows.1 = (bf16[4112,128]{1,0:T(8,128)(2,1)}, bf16[2048,128]{1,0:T(8,128)(2,1)}) custom-call(s32[3,1,16]{2,1,0:T(1,128)} %bitcast.26, s32[8,8]{1,0:T(8,128)} %bitcast.14, bf16[16,128,384]{2,1,0:T(8,128)(2,1)} %bitcast.25), custom_call_target="tpu_custom_call" | custom-call | flops 1024 | bytes 1024 | tf_op jit(solution)/shard_map/pack_rows/pallas_call | solution.py:130
  2.6 2.2 %collective-permute-start.1 = (bf16[4112,128]{1,0:T(8,128)(2,1)}, bf16[4112,128]{1,0:T(8,128)(2,1)S(1)}, u32[]{:S(2)}, u32[]{:S(2)}) collective-permute-start(bf16[4112,128]{1,0:T(8,128)(2,1)} %get-tuple-element.23.head.refs_1_.refs_0_), channel_id=1, source_target_pairs={{0,8},{4,12},{16,24},{20,28},{8,0},{12,4},{24,16},{28,20},{1,9},{5... | collective-permute-start | bytes 3158024 | tf_op jit(solution)/shard_map/ppermute | solution.py:366
  4.8 0.7 collective-permute-start.5
  5.6 0.0 copy-done.3
  5.6 1.3 %collective-permute-start = (s32[8,8]{1,0:T(8,128)S(1)}, s32[8,8]{1,0:T(8,128)S(1)}, u32[]{:S(2)}, u32[]{:S(2)}) collective-permute-start(s32[8,8]{1,0:T(8,128)S(1)} %bitcast.15), channel_id=1, source_target_pairs={{4,0},{0,4},{12,8},{8,12},{20,16},{16,20},{28,24},{24,28},{5,1},{1... | collective-permute-start | bytes 776 | tf_op jit(solution)/shard_map/ppermute | solution.py:366
  6.9 1.5 %collective-permute-done.refs_0_ = s32[8,8]{1,0:T(8,128)S(1)} collective-permute-done((s32[8,8]{1,0:T(8,128)S(1)}, s32[8,8]{1,0:T(8,128)S(1)}, u32[]{:S(2)}, u32[]{:S(2)}) %collective-permute-start) | collective-permute-done | bytes 288 | tf_op jit(solution)/shard_map/ppermute | solution.py:366
  8.4 1.2 %copy-done.1 = bf16[4112,128]{1,0:T(8,128)(2,1)S(1)} copy-done((bf16[4112,128]{1,0:T(8,128)(2,1)S(1)}, bf16[4112,128]{1,0:T(8,128)(2,1)}, u32[]{:S(2)}) %copy-start.1) | copy-done | bytes 1052696
  9.6 1.7 %pick_rows.7 = bf16[3072,128]{1,0:T(8,128)(2,1)S(1)} custom-call(s32[8,8]{1,0:T(8,128)S(1)} %collective-permute-done.refs_0_, bf16[4112,128]{1,0:T(8,128)(2,1)S(1)} %copy-done.1, bf16[2048,128]{1,0:T(8,128)(2,1)} %get-tuple-element.24.tail.refs_2_.refs_1_), custom_call_target="tpu_custom_call" | custom-call | flops 1024 | bytes 1024 | tf_op jit(solution)/shard_map/pick_rows/pallas_call | solution.py:222
  11.3 1.3 %collective-permute-start.3 = (bf16[3072,128]{1,0:T(8,128)(2,1)S(1)}, bf16[3072,128]{1,0:T(8,128)(2,1)S(1)}, u32[]{:S(2)}, u32[]{:S(2)}) collective-permute-start(bf16[3072,128]{1,0:T(8,128)(2,1)S(1)} %pick_rows.7), channel_id=1, source_target_pairs={{0,4},{4,0},{8,12},{12,8},{16,20},{20,16},{24,28},{28,24},{1,5},{5... | collective-permute-start | bytes 2359304 | tf_op jit(solution)/shard_map/ppermute | solution.py:366
  12.6 5.7 %collective-permute-start.2 = (bf16[2048,128]{1,0:T(8,128)(2,1)}, bf16[2048,128]{1,0:T(8,128)(2,1)S(1)}, u32[]{:S(2)}, u32[]{:S(2)}) collective-permute-start(bf16[2048,128]{1,0:T(8,128)(2,1)} %get-tuple-element.24.tail.refs_2_.refs_1_), channel_id=1, source_target_pairs={{1,9},{5,13},{17,25},{21,29},{9,1},{13,5},{25,17},{29,21},{2,10},{... | collective-permute-start | bytes 1572872 | tf_op jit(solution)/shard_map/ppermute | solution.py:366
  18.3 0.7 collective-permute-start.6
  19.0 9.0 %collective-permute-done.1.refs_1_.refs_2_.refs_5_ = bf16[4112,128]{1,0:T(8,128)(2,1)S(1)} collective-permute-done((bf16[4112,128]{1,0:T(8,128)(2,1)}, bf16[4112,128]{1,0:T(8,128)(2,1)S(1)}, u32[]{:S(2)}, u32[]{:S(2)}) %collective-permute-start.1) | collective-permute-done | bytes 1052704 | tf_op jit(solution)/shard_map/ppermute | solution.py:366
  28.0 0.0 collective-permute-done.5.refs_0_.refs_1_
  28.0 0.7 pick_rows.9
  28.8 1.3 %collective-permute-start.8 = (bf16[2048,128]{1,0:T(8,128)(2,1)S(1)}, bf16[2048,128]{1,0:T(8,128)(2,1)S(1)}, u32[]{:S(2)}, u32[]{:S(2)}) collective-permute-start(bf16[2048,128]{1,0:T(8,128)(2,1)S(1)} %get-tuple-element.26), channel_id=1, source_target_pairs={{8,0},{12,4},{16,24},{20,28},{9,1},{13,5},{17,25},{21,29},{10,2},{... | collective-permute-start | bytes 1572872 | tf_op jit(solution)/shard_map/ppermute | solution.py:366
  30.1 0.7 collective-permute-start.13
  30.8 3.4 %collective-permute-done.2.refs_2_.refs_3_ = bf16[2048,128]{1,0:T(8,128)(2,1)S(1)} collective-permute-done((bf16[2048,128]{1,0:T(8,128)(2,1)}, bf16[2048,128]{1,0:T(8,128)(2,1)S(1)}, u32[]{:S(2)}, u32[]{:S(2)}) %collective-permute-start.2) | collective-permute-done | bytes 524320 | tf_op jit(solution)/shard_map/ppermute | solution.py:366
  34.2 0.7 collective-permute-start.7
  34.8 0.0 collective-permute-done.3.refs_3_.refs_4_
  34.8 0.7 pick_rows.8.refs_3_
  35.5 1.5 %collective-permute-start.4 = (bf16[3072,128]{1,0:T(8,128)(2,1)S(1)}, bf16[3072,128]{1,0:T(8,128)(2,1)S(1)}, u32[]{:S(2)}, u32[]{:S(2)}) collective-permute-start(bf16[3072,128]{1,0:T(8,128)(2,1)S(1)} %pick_rows.8.refs_3_), channel_id=1, source_target_pairs={{0,4},{4,0},{8,12},{12,8},{16,20},{20,16},{24,28},{28,24},{1,5},{5... | collective-permute-start | bytes 2359304 | tf_op jit(solution)/shard_map/ppermute | solution.py:366
  37.0 0.0 collective-permute-done.6.refs_1_.refs_2_.refs_3_
  37.0 0.0 collective-permute-done.7.refs_2_.refs_6_
  37.0 6.7 %collective-permute-done.8.refs_4_.refs_9_.refs_2_ = bf16[2048,128]{1,0:T(8,128)(2,1)S(1)} collective-permute-done((bf16[2048,128]{1,0:T(8,128)(2,1)S(1)}, bf16[2048,128]{1,0:T(8,128)(2,1)S(1)}, u32[]{:S(2)}, u32[]{:S(2)}) %collective-permute-start.8) | collective-permute-done | bytes 524320 | tf_op jit(solution)/shard_map/ppermute | solution.py:366
  43.7 0.7 pick_rows.10.refs_3_
  44.5 0.0 copy-start.2
  44.5 1.4 %collective-permute-start.10 = (bf16[3072,128]{1,0:T(8,128)(2,1)S(1)}, bf16[3072,128]{1,0:T(8,128)(2,1)S(1)}, u32[]{:S(2)}, u32[]{:S(2)}) collective-permute-start(bf16[3072,128]{1,0:T(8,128)(2,1)S(1)} %pick_rows.10.refs_3_), channel_id=1, source_target_pairs={{8,4},{12,0},{16,28},{20,24},{9,5},{13,1},{17,29},{21,25},{10,6},{... | collective-permute-start | bytes 2359304 | tf_op jit(solution)/shard_map/ppermute | solution.py:366
  45.9 0.7 collective-permute-start.14
  46.6 0.7 pick_rows.11
  47.3 0.0 copy-start
  47.3 0.0 copy-start.4
  47.3 0.0 copy-start.5
  47.3 0.8 collective-permute-start.9
  48.2 0.0 copy-done.2
  48.2 1.5 %turn_rows.1.turned = bf16[16,384,128]{2,1,0:T(8,128)(2,1)S(1)} custom-call(bf16[4112,128]{1,0:T(8,128)(2,1)S(1)} %copy-done.2, bf16[2048,128]{1,0:T(8,128)(2,1)} %get-tuple-element.24.tail.refs_2_.refs_1_), custom_call_target="tpu_custom_call" | custom-call | flops 1024 | bytes 1024 | tf_op jit(solution)/shard_map/turn_rows/pallas_call | solution.py:159
  49.7 5.1 %stage_products.3 = (bf16[3,3,128,128]{3,2,1,0:T(8,128)(2,1)S(1)}, bf16[3,3,128,128]{3,2,1,0:T(8,128)(2,1)S(1)}, bf16[3,3,128,128]{3,2,1,0:T(8,128)(2,1)S(1)}) custom-call(s32[8,8]{1,0:T(8,128)S(1)} %bitcast.19, s32[8,8]{1,0:T(8,128)S(1)} %bitcast.16, s32[1,8]{1,0:T(1,128)S(1)} %bitcast.22, bf16[16,384,128]{2,1,0:T(8,128)(2,1)S(1)} %turn_rows.1.turned, ...), custom_call_target="tpu_custom_call" | custom-call | flops 1024 | bytes 1024 | tf_op jit(solution)/shard_map/stage_products/pallas_call | solution.py:301
  54.8 0.0 collective-permute-done.13.refs_0_.refs_1_.refs_4_
  54.8 0.9 pick_rows.12
  55.7 1.3 %collective-permute-start.16 = (bf16[2048,128]{1,0:T(8,128)(2,1)S(1)}, bf16[2048,128]{1,0:T(8,128)(2,1)S(1)}, u32[]{:S(2)}, u32[]{:S(2)}) collective-permute-start(bf16[2048,128]{1,0:T(8,128)(2,1)S(1)} %get-tuple-element.33.refs_7_), channel_id=1, source_target_pairs={{8,0},{12,4},{16,24},{20,28},{9,1},{13,5},{17,25},{21,29},{10,2},{... | collective-permute-start | bytes 1572872 | tf_op jit(solution)/shard_map/ppermute | solution.py:366
  57.0 0.0 collective-permute-done.14.refs_2_.refs_4_.refs_5_
  57.1 14.1 %collective-permute-done.4.refs_0_.refs_11_ = bf16[3072,128]{1,0:T(8,128)(2,1)S(1)} collective-permute-done((bf16[3072,128]{1,0:T(8,128)(2,1)S(1)}, bf16[3072,128]{1,0:T(8,128)(2,1)S(1)}, u32[]{:S(2)}, u32[]{:S(2)}) %collective-permute-start.4) | collective-permute-done | bytes 786464 | tf_op jit(solution)/shard_map/ppermute | solution.py:366
  71.2 0.0 collective-permute-done.10.refs_2_.refs_10_
  71.2 1.5 %pick_rows.13 = (bf16[3072,128]{1,0:T(8,128)(2,1)S(1)}, bf16[2048,128]{1,0:T(8,128)(2,1)S(1)}, bf16[1024,128]{1,0:T(8,128)(2,1)S(1)}) custom-call(s32[8,8]{1,0:T(8,128)S(1)} %collective-permute-done.refs_0_, bf16[4112,128]{1,0:T(8,128)(2,1)S(1)} %collective-permute-done.13.refs_0_.refs_1_.refs_4_, ...), custom_call_target="tpu_custom_call" | custom-call | flops 1024 | bytes 1024 | tf_op jit(solution)/shard_map/pick_rows/pallas_call | solution.py:222
  72.7 0.7 collective-permute-start.17
  73.4 1.3 %collective-permute-start.19 = (bf16[1024,128]{1,0:T(8,128)(2,1)S(1)}, bf16[1024,128]{1,0:T(8,128)(2,1)S(1)}, u32[]{:S(2)}, u32[]{:S(2)}) collective-permute-start(bf16[1024,128]{1,0:T(8,128)(2,1)S(1)} %get-tuple-element.37), channel_id=1, source_target_pairs={{9,5},{13,1},{17,29},{21,25},{10,6},{14,2},{18,30},{22,26}} | collective-permute-start | bytes 786440 | tf_op jit(solution)/shard_map/ppermute | solution.py:366
  74.7 1.3 %collective-permute-start.18 = (bf16[2048,128]{1,0:T(8,128)(2,1)S(1)}, bf16[2048,128]{1,0:T(8,128)(2,1)S(1)}, u32[]{:S(2)}, u32[]{:S(2)}) collective-permute-start(bf16[2048,128]{1,0:T(8,128)(2,1)S(1)} %get-tuple-element.34.refs_8_), channel_id=1, source_target_pairs={{8,4},{12,0},{16,28},{20,24},{9,5},{13,1},{17,29},{21,25},{10,6},{... | collective-permute-start | bytes 1572872 | tf_op jit(solution)/shard_map/ppermute | solution.py:366
  76.0 0.0 collective-permute-done.9.refs_1_
  76.0 1.3 %collective-permute-start.15 = (bf16[2048,128]{1,0:T(8,128)(2,1)S(1)}, bf16[2048,128]{1,0:T(8,128)(2,1)S(1)}, u32[]{:S(2)}, u32[]{:S(2)}) collective-permute-start(bf16[2048,128]{1,0:T(8,128)(2,1)S(1)} %get-tuple-element.35), channel_id=1, source_target_pairs={{9,1},{13,5},{17,25},{21,29},{10,2},{14,6},{18,26},{22,30}} | collective-permute-start | bytes 1572872 | tf_op jit(solution)/shard_map/ppermute | solution.py:366
  77.3 3.1 %stage_products.4 = (bf16[5,3,128,128]{3,2,1,0:T(8,128)(2,1)S(1)}, bf16[5,3,128,128]{3,2,1,0:T(8,128)(2,1)S(1)}, bf16[5,3,128,128]{3,2,1,0:T(8,128)(2,1)S(1)}) custom-call(s32[8,8]{1,0:T(8,128)S(1)} %bitcast.20, s32[8,8]{1,0:T(8,128)S(1)} %bitcast.17, s32[1,8]{1,0:T(1,128)S(1)} %bitcast.23, bf16[16,384,128]{2,1,0:T(8,128)(2,1)S(1)} %turn_rows.1.turned, ...), custom_call_target="tpu_custom_call" | custom-call | flops 1024 | bytes 1024 | tf_op jit(solution)/shard_map/stage_products/pallas_call | solution.py:301
  80.4 3.5 %collective-permute-done.19.refs_10_ = bf16[1024,128]{1,0:T(8,128)(2,1)S(1)} collective-permute-done((bf16[1024,128]{1,0:T(8,128)(2,1)S(1)}, bf16[1024,128]{1,0:T(8,128)(2,1)S(1)}, u32[]{:S(2)}, u32[]{:S(2)}) %collective-permute-start.19) | collective-permute-done | bytes 262176 | tf_op jit(solution)/shard_map/ppermute | solution.py:366
  83.9 7.3 %collective-permute-start.11 = (bf16[5,3,128,128]{3,2,1,0:T(8,128)(2,1)S(1)}, bf16[5,3,128,128]{3,2,1,0:T(8,128)(2,1)S(1)}, u32[]{:S(2)}, u32[]{:S(2)}) collective-permute-start(bf16[5,3,128,128]{3,2,1,0:T(8,128)(2,1)S(1)} %get-tuple-element.31), channel_id=1, source_target_pairs={{0,1},{1,2},{2,3},{4,5},{5,6},{6,7},{8,9},{9,10},{10,11},{12,13},{... | collective-permute-start | bytes 1474568 | tf_op jit(solution)/shard_map/ppermute | solution.py:375
  91.2 0.0 collective-permute-done.16.refs_6_
  91.2 1.9 %collective-permute-start.12 = (bf16[5,3,128,128]{3,2,1,0:T(8,128)(2,1)S(1)}, bf16[5,3,128,128]{3,2,1,0:T(8,128)(2,1)S(1)}, u32[]{:S(2)}, u32[]{:S(2)}) collective-permute-start(bf16[5,3,128,128]{3,2,1,0:T(8,128)(2,1)S(1)} %get-tuple-element.32), channel_id=1, source_target_pairs={{1,0},{2,1},{3,2},{5,4},{6,5},{7,6},{9,8},{10,9},{11,10},{13,12},{... | collective-permute-start | bytes 1474568 | tf_op jit(solution)/shard_map/ppermute | solution.py:376
  93.2 0.0 collective-permute-done.18.refs_9_
  93.2 3.8 %collective-permute-done.11.refs_11_.refs_1_ = bf16[5,3,128,128]{3,2,1,0:T(8,128)(2,1)S(1)} collective-permute-done((bf16[5,3,128,128]{3,2,1,0:T(8,128)(2,1)S(1)}, bf16[5,3,128,128]{3,2,1,0:T(8,128)(2,1)S(1)}, u32[]{:S(2)}, u32[]{:S(2)}) %collective-permute-start.11) | collective-permute-done | bytes 491552 | tf_op jit(solution)/shard_map/ppermute | solution.py:375
  97.0 4.4 %collective-permute-done.12.refs_12_.refs_2_ = bf16[5,3,128,128]{3,2,1,0:T(8,128)(2,1)S(1)} collective-permute-done((bf16[5,3,128,128]{3,2,1,0:T(8,128)(2,1)S(1)}, bf16[5,3,128,128]{3,2,1,0:T(8,128)(2,1)S(1)}, u32[]{:S(2)}, u32[]{:S(2)}) %collective-permute-start.12) | collective-permute-done | bytes 491552 | tf_op jit(solution)/shard_map/ppermute | solution.py:376
  101.4 0.0 collective-permute-done.15.refs_3_.refs_7_
  101.4 0.0 collective-permute-done.17.refs_8_
  101.4 4.1 %stage_products.5 = (bf16[3,3,128,128]{3,2,1,0:T(8,128)(2,1)S(1)}, bf16[3,3,128,128]{3,2,1,0:T(8,128)(2,1)S(1)}, bf16[3,3,128,128]{3,2,1,0:T(8,128)(2,1)S(1)}) custom-call(s32[8,8]{1,0:T(8,128)S(1)} %bitcast.21, s32[8,8]{1,0:T(8,128)S(1)} %bitcast.18, s32[1,8]{1,0:T(1,128)S(1)} %bitcast.24, bf16[16,384,128]{2,1,0:T(8,128)(2,1)S(1)} %turn_rows.1.turned, ...), custom_call_target="tpu_custom_call" | custom-call | flops 1024 | bytes 1024 | tf_op jit(solution)/shard_map/stage_products/pallas_call | solution.py:301
  105.5 1.9 %collective-permute-start.20 = (bf16[3,3,128,128]{3,2,1,0:T(8,128)(2,1)S(1)}, bf16[3,3,128,128]{3,2,1,0:T(8,128)(2,1)S(1)}, u32[]{:S(2)}, u32[]{:S(2)}) collective-permute-start(bf16[3,3,128,128]{3,2,1,0:T(8,128)(2,1)S(1)} %get-tuple-element.39), channel_id=1, source_target_pairs={{0,1},{1,2},{2,3},{4,5},{5,6},{6,7},{8,9},{9,10},{10,11},{12,13},{... | collective-permute-start | bytes 884744 | tf_op jit(solution)/shard_map/ppermute | solution.py:375
  107.4 2.4 %collective-permute-start.21 = (bf16[3,3,128,128]{3,2,1,0:T(8,128)(2,1)S(1)}, bf16[3,3,128,128]{3,2,1,0:T(8,128)(2,1)S(1)}, u32[]{:S(2)}, u32[]{:S(2)}) collective-permute-start(bf16[3,3,128,128]{3,2,1,0:T(8,128)(2,1)S(1)} %get-tuple-element.40), channel_id=1, source_target_pairs={{1,0},{2,1},{3,2},{5,4},{6,5},{7,6},{9,8},{10,9},{11,10},{13,12},{... | collective-permute-start | bytes 884744 | tf_op jit(solution)/shard_map/ppermute | solution.py:376
  109.8 1.2 %collective-permute-done.20.refs_4_ = bf16[3,3,128,128]{3,2,1,0:T(8,128)(2,1)S(1)} collective-permute-done((bf16[3,3,128,128]{3,2,1,0:T(8,128)(2,1)S(1)}, bf16[3,3,128,128]{3,2,1,0:T(8,128)(2,1)S(1)}, u32[]{:S(2)}, u32[]{:S(2)}) %collective-permute-start.20) | collective-permute-done | bytes 294944 | tf_op jit(solution)/shard_map/ppermute | solution.py:375
  111.0 4.4 %collective-permute-done.21.refs_5_ = bf16[3,3,128,128]{3,2,1,0:T(8,128)(2,1)S(1)} collective-permute-done((bf16[3,3,128,128]{3,2,1,0:T(8,128)(2,1)S(1)}, bf16[3,3,128,128]{3,2,1,0:T(8,128)(2,1)S(1)}, u32[]{:S(2)}, u32[]{:S(2)}) %collective-permute-start.21) | collective-permute-done | bytes 294944 | tf_op jit(solution)/shard_map/ppermute | solution.py:376
  115.4 2.5 %assemble_coarse.1 = f32[5120,128]{1,0:T(8,128)} custom-call(bf16[5,3,128,128]{3,2,1,0:T(8,128)(2,1)S(1)} %get-tuple-element.30.refs_0_, bf16[5,3,128,128]{3,2,1,0:T(8,128)(2,1)S(1)} %collective-permute-done.11.refs_11_.refs_1_, bf16[5,3,128,128]{3,2,1,0:T(8,128)(2,1)S(1)} %collective-permute-done.12.refs_12_.refs_2_, ...), custom_call_target="tpu_custom_call" | custom-call | flops 1024 | bytes 1024 | tf_op jit(solution)/shard_map/assemble_coarse/pallas_call | solution.py:342
  (5 shorter events, 0.0 us)
Async XLA Ops:
  0.0 5.6 %copy-start.3 = (s32[1,1,8,8]{3,2,1,0:T(8,128)S(1)}, s32[1,1,8,8]{3,2,1,0:T(8,128)}, u32[]{:S(2)}) copy-start(s32[1,1,8,8]{3,2,1,0:T(8,128)} %param.8) | copy-start | bytes 772
  2.6 25.4 %collective-permute-start.1 = (bf16[4112,128]{1,0:T(8,128)(2,1)}, bf16[4112,128]{1,0:T(8,128)(2,1)S(1)}, u32[]{:S(2)}, u32[]{:S(2)}) collective-permute-start(bf16[4112,128]{1,0:T(8,128)(2,1)} %get-tuple-element.23.head.refs_1_.refs_0_), channel_id=1, source_target_pairs={{0,8},{4,12},{16,24},{20,28},{8,0},{12,4},{24,16},{28,20},{1,9},{5... | collective-permute-start | bytes 3158024 | tf_op jit(solution)/shard_map/ppermute | solution.py:366
  4.8 23.2 %collective-permute-start.5 = (bf16[4112,128]{1,0:T(8,128)(2,1)}, bf16[4112,128]{1,0:T(8,128)(2,1)S(1)}, u32[]{:S(2)}, u32[]{:S(2)}) collective-permute-start(bf16[4112,128]{1,0:T(8,128)(2,1)} %get-tuple-element.23.head.refs_1_.refs_0_), channel_id=1, source_target_pairs={{8,16},{12,20},{16,8},{20,12},{9,17},{13,21},{17,9},{21,13},{10,18... | collective-permute-start | bytes 3158024 | tf_op jit(solution)/shard_map/ppermute | solution.py:366
  5.6 2.8 %collective-permute-start = (s32[8,8]{1,0:T(8,128)S(1)}, s32[8,8]{1,0:T(8,128)S(1)}, u32[]{:S(2)}, u32[]{:S(2)}) collective-permute-start(s32[8,8]{1,0:T(8,128)S(1)} %bitcast.15), channel_id=1, source_target_pairs={{4,0},{0,4},{12,8},{8,12},{20,16},{16,20},{28,24},{24,28},{5,1},{1... | collective-permute-start | bytes 776 | tf_op jit(solution)/shard_map/ppermute | solution.py:366
  8.4 1.2 %copy-start.1 = (bf16[4112,128]{1,0:T(8,128)(2,1)S(1)}, bf16[4112,128]{1,0:T(8,128)(2,1)}, u32[]{:S(2)}) copy-start(bf16[4112,128]{1,0:T(8,128)(2,1)} %get-tuple-element.23.head.refs_1_.refs_0_) | copy-start | bytes 3158020
  11.3 23.5 %collective-permute-start.3 = (bf16[3072,128]{1,0:T(8,128)(2,1)S(1)}, bf16[3072,128]{1,0:T(8,128)(2,1)S(1)}, u32[]{:S(2)}, u32[]{:S(2)}) collective-permute-start(bf16[3072,128]{1,0:T(8,128)(2,1)S(1)} %pick_rows.7), channel_id=1, source_target_pairs={{0,4},{4,0},{8,12},{12,8},{16,20},{20,16},{24,28},{28,24},{1,5},{5... | collective-permute-start | bytes 2359304 | tf_op jit(solution)/shard_map/ppermute | solution.py:366
  12.6 21.6 %collective-permute-start.2 = (bf16[2048,128]{1,0:T(8,128)(2,1)}, bf16[2048,128]{1,0:T(8,128)(2,1)S(1)}, u32[]{:S(2)}, u32[]{:S(2)}) collective-permute-start(bf16[2048,128]{1,0:T(8,128)(2,1)} %get-tuple-element.24.tail.refs_2_.refs_1_), channel_id=1, source_target_pairs={{1,9},{5,13},{17,25},{21,29},{9,1},{13,5},{25,17},{29,21},{2,10},{... | collective-permute-start | bytes 1572872 | tf_op jit(solution)/shard_map/ppermute | solution.py:366
  18.3 18.7 %collective-permute-start.6 = (bf16[2048,128]{1,0:T(8,128)(2,1)}, bf16[2048,128]{1,0:T(8,128)(2,1)S(1)}, u32[]{:S(2)}, u32[]{:S(2)}) collective-permute-start(bf16[2048,128]{1,0:T(8,128)(2,1)} %get-tuple-element.24.tail.refs_2_.refs_1_), channel_id=1, source_target_pairs={{9,17},{13,21},{17,9},{21,13},{10,18},{14,22},{18,10},{22,14}} | collective-permute-start | bytes 1572872 | tf_op jit(solution)/shard_map/ppermute | solution.py:366
  28.8 15.0 %collective-permute-start.8 = (bf16[2048,128]{1,0:T(8,128)(2,1)S(1)}, bf16[2048,128]{1,0:T(8,128)(2,1)S(1)}, u32[]{:S(2)}, u32[]{:S(2)}) collective-permute-start(bf16[2048,128]{1,0:T(8,128)(2,1)S(1)} %get-tuple-element.26), channel_id=1, source_target_pairs={{8,0},{12,4},{16,24},{20,28},{9,1},{13,5},{17,25},{21,29},{10,2},{... | collective-permute-start | bytes 1572872 | tf_op jit(solution)/shard_map/ppermute | solution.py:366
  30.1 24.8 %collective-permute-start.13 = (bf16[4112,128]{1,0:T(8,128)(2,1)S(1)}, bf16[4112,128]{1,0:T(8,128)(2,1)S(1)}, u32[]{:S(2)}, u32[]{:S(2)}) collective-permute-start(bf16[4112,128]{1,0:T(8,128)(2,1)S(1)} %collective-permute-done.1.refs_1_.refs_2_.refs_5_), channel_id=1, source_target_pairs={{8,16},{12,20},{16,8},{20,12},{9,17},{13,21},{17,9},{21,13},{10,18... | collective-permute-start | bytes 3158024 | tf_op jit(solution)/shard_map/ppermute | solution.py:366
  34.2 2.8 %collective-permute-start.7 = (bf16[16,128]{1,0:T(8,128)(2,1)S(1)}, bf16[16,128]{1,0:T(8,128)(2,1)S(1)}, u32[]{:S(2)}, u32[]{:S(2)}) collective-permute-start(bf16[16,128]{1,0:T(8,128)(2,1)S(1)} %get-tuple-element.25), channel_id=1, source_target_pairs={{12,8},{8,12},{20,16},{16,20},{13,9},{9,13},{21,17},{17,21},{14,10... | collective-permute-start | bytes 12296 | tf_op jit(solution)/shard_map/ppermute | solution.py:366
  35.5 35.6 %collective-permute-start.4 = (bf16[3072,128]{1,0:T(8,128)(2,1)S(1)}, bf16[3072,128]{1,0:T(8,128)(2,1)S(1)}, u32[]{:S(2)}, u32[]{:S(2)}) collective-permute-start(bf16[3072,128]{1,0:T(8,128)(2,1)S(1)} %pick_rows.8.refs_3_), channel_id=1, source_target_pairs={{0,4},{4,0},{8,12},{12,8},{16,20},{20,16},{24,28},{28,24},{1,5},{5... | collective-permute-start | bytes 2359304 | tf_op jit(solution)/shard_map/ppermute | solution.py:366
  44.5 3.7 %copy-start.2 = (bf16[4112,128]{1,0:T(8,128)(2,1)S(1)}, bf16[4112,128]{1,0:T(8,128)(2,1)}, u32[]{:S(2)}) copy-start(bf16[4112,128]{1,0:T(8,128)(2,1)} %get-tuple-element.23.head.refs_1_.refs_0_) | copy-start | bytes 3158020
  44.5 26.7 %collective-permute-start.10 = (bf16[3072,128]{1,0:T(8,128)(2,1)S(1)}, bf16[3072,128]{1,0:T(8,128)(2,1)S(1)}, u32[]{:S(2)}, u32[]{:S(2)}) collective-permute-start(bf16[3072,128]{1,0:T(8,128)(2,1)S(1)} %pick_rows.10.refs_3_), channel_id=1, source_target_pairs={{8,4},{12,0},{16,28},{20,24},{9,5},{13,1},{17,29},{21,25},{10,6},{... | collective-permute-start | bytes 2359304 | tf_op jit(solution)/shard_map/ppermute | solution.py:366
  45.9 11.1 %collective-permute-start.14 = (bf16[2048,128]{1,0:T(8,128)(2,1)S(1)}, bf16[2048,128]{1,0:T(8,128)(2,1)S(1)}, u32[]{:S(2)}, u32[]{:S(2)}) collective-permute-start(bf16[2048,128]{1,0:T(8,128)(2,1)S(1)} %collective-permute-done.2.refs_2_.refs_3_), channel_id=1, source_target_pairs={{9,17},{13,21},{17,9},{21,13},{10,18},{14,22},{18,10},{22,14}} | collective-permute-start | bytes 1572872 | tf_op jit(solution)/shard_map/ppermute | solution.py:366
  47.3 2.4 %copy-start = (bf16[1,1,8,8,128,128]{5,4,3,2,1,0:T(8,128)(2,1)S(1)}, bf16[1,1,8,8,128,128]{5,4,3,2,1,0:T(8,128)(2,1)}, u32[]{:S(2)}) copy-start(bf16[1,1,8,8,128,128]{5,4,3,2,1,0:T(8,128)(2,1)} %param.6) | copy-start | bytes 6291460
  47.3 2.4 %copy-start.4 = (s32[1,1,8,8]{3,2,1,0:T(8,128)S(1)}, s32[1,1,8,8]{3,2,1,0:T(8,128)}, u32[]{:S(2)}) copy-start(s32[1,1,8,8]{3,2,1,0:T(8,128)} %param.7) | copy-start | bytes 772
  47.3 2.4 %copy-start.5 = (s32[1,1,8]{2,1,0:T(1,128)S(1)}, s32[1,1,8]{2,1,0:T(1,128)}, u32[]{:S(2)}) copy-start(s32[1,1,8]{2,1,0:T(1,128)} %param.9) | copy-start | bytes 100
  47.3 28.7 %collective-permute-start.9 = (bf16[3072,128]{1,0:T(8,128)(2,1)S(1)}, bf16[3072,128]{1,0:T(8,128)(2,1)S(1)}, u32[]{:S(2)}, u32[]{:S(2)}) collective-permute-start(bf16[3072,128]{1,0:T(8,128)(2,1)S(1)} %pick_rows.11), channel_id=1, source_target_pairs={{8,12},{12,8},{16,20},{20,16},{9,13},{13,9},{17,21},{21,17},{10,14... | collective-permute-start | bytes 2359304 | tf_op jit(solution)/shard_map/ppermute | solution.py:366
  55.7 35.5 %collective-permute-start.16 = (bf16[2048,128]{1,0:T(8,128)(2,1)S(1)}, bf16[2048,128]{1,0:T(8,128)(2,1)S(1)}, u32[]{:S(2)}, u32[]{:S(2)}) collective-permute-start(bf16[2048,128]{1,0:T(8,128)(2,1)S(1)} %get-tuple-element.33.refs_7_), channel_id=1, source_target_pairs={{8,0},{12,4},{16,24},{20,28},{9,1},{13,5},{17,25},{21,29},{10,2},{... | collective-permute-start | bytes 1572872 | tf_op jit(solution)/shard_map/ppermute | solution.py:366
  72.7 28.7 %collective-permute-start.17 = (bf16[3072,128]{1,0:T(8,128)(2,1)S(1)}, bf16[3072,128]{1,0:T(8,128)(2,1)S(1)}, u32[]{:S(2)}, u32[]{:S(2)}) collective-permute-start(bf16[3072,128]{1,0:T(8,128)(2,1)S(1)} %get-tuple-element.36), channel_id=1, source_target_pairs={{8,12},{12,8},{16,20},{20,16},{9,13},{13,9},{17,21},{21,17},{10,14... | collective-permute-start | bytes 2359304 | tf_op jit(solution)/shard_map/ppermute | solution.py:366
  73.4 10.4 %collective-permute-start.19 = (bf16[1024,128]{1,0:T(8,128)(2,1)S(1)}, bf16[1024,128]{1,0:T(8,128)(2,1)S(1)}, u32[]{:S(2)}, u32[]{:S(2)}) collective-permute-start(bf16[1024,128]{1,0:T(8,128)(2,1)S(1)} %get-tuple-element.37), channel_id=1, source_target_pairs={{9,5},{13,1},{17,29},{21,25},{10,6},{14,2},{18,30},{22,26}} | collective-permute-start | bytes 786440 | tf_op jit(solution)/shard_map/ppermute | solution.py:366
  74.7 18.4 %collective-permute-start.18 = (bf16[2048,128]{1,0:T(8,128)(2,1)S(1)}, bf16[2048,128]{1,0:T(8,128)(2,1)S(1)}, u32[]{:S(2)}, u32[]{:S(2)}) collective-permute-start(bf16[2048,128]{1,0:T(8,128)(2,1)S(1)} %get-tuple-element.34.refs_8_), channel_id=1, source_target_pairs={{8,4},{12,0},{16,28},{20,24},{9,5},{13,1},{17,29},{21,25},{10,6},{... | collective-permute-start | bytes 1572872 | tf_op jit(solution)/shard_map/ppermute | solution.py:366
  76.0 25.3 %collective-permute-start.15 = (bf16[2048,128]{1,0:T(8,128)(2,1)S(1)}, bf16[2048,128]{1,0:T(8,128)(2,1)S(1)}, u32[]{:S(2)}, u32[]{:S(2)}) collective-permute-start(bf16[2048,128]{1,0:T(8,128)(2,1)S(1)} %get-tuple-element.35), channel_id=1, source_target_pairs={{9,1},{13,5},{17,25},{21,29},{10,2},{14,6},{18,26},{22,30}} | collective-permute-start | bytes 1572872 | tf_op jit(solution)/shard_map/ppermute | solution.py:366
  83.9 13.1 %collective-permute-start.11 = (bf16[5,3,128,128]{3,2,1,0:T(8,128)(2,1)S(1)}, bf16[5,3,128,128]{3,2,1,0:T(8,128)(2,1)S(1)}, u32[]{:S(2)}, u32[]{:S(2)}) collective-permute-start(bf16[5,3,128,128]{3,2,1,0:T(8,128)(2,1)S(1)} %get-tuple-element.31), channel_id=1, source_target_pairs={{0,1},{1,2},{2,3},{4,5},{5,6},{6,7},{8,9},{9,10},{10,11},{12,13},{... | collective-permute-start | bytes 1474568 | tf_op jit(solution)/shard_map/ppermute | solution.py:375
  91.2 10.1 %collective-permute-start.12 = (bf16[5,3,128,128]{3,2,1,0:T(8,128)(2,1)S(1)}, bf16[5,3,128,128]{3,2,1,0:T(8,128)(2,1)S(1)}, u32[]{:S(2)}, u32[]{:S(2)}) collective-permute-start(bf16[5,3,128,128]{3,2,1,0:T(8,128)(2,1)S(1)} %get-tuple-element.32), channel_id=1, source_target_pairs={{1,0},{2,1},{3,2},{5,4},{6,5},{7,6},{9,8},{10,9},{11,10},{13,12},{... | collective-permute-start | bytes 1474568 | tf_op jit(solution)/shard_map/ppermute | solution.py:376
  105.5 5.6 %collective-permute-start.20 = (bf16[3,3,128,128]{3,2,1,0:T(8,128)(2,1)S(1)}, bf16[3,3,128,128]{3,2,1,0:T(8,128)(2,1)S(1)}, u32[]{:S(2)}, u32[]{:S(2)}) collective-permute-start(bf16[3,3,128,128]{3,2,1,0:T(8,128)(2,1)S(1)} %get-tuple-element.39), channel_id=1, source_target_pairs={{0,1},{1,2},{2,3},{4,5},{5,6},{6,7},{8,9},{9,10},{10,11},{12,13},{... | collective-permute-start | bytes 884744 | tf_op jit(solution)/shard_map/ppermute | solution.py:375
  107.4 8.0 %collective-permute-start.21 = (bf16[3,3,128,128]{3,2,1,0:T(8,128)(2,1)S(1)}, bf16[3,3,128,128]{3,2,1,0:T(8,128)(2,1)S(1)}, u32[]{:S(2)}, u32[]{:S(2)}) collective-permute-start(bf16[3,3,128,128]{3,2,1,0:T(8,128)(2,1)S(1)} %get-tuple-element.40), channel_id=1, source_target_pairs={{1,0},{2,1},{3,2},{5,4},{6,5},{7,6},{9,8},{10,9},{11,10},{13,12},{... | collective-permute-start | bytes 884744 | tf_op jit(solution)/shard_map/ppermute | solution.py:376

commit v15 on v14

--- a/solution.py
+++ b/solution.py
@@ -444,13 +444,13 @@
     sources = []
     for i in range(count):
         sources += [half_crossed[i], other_crossed[i], end_crossed[i]]
-    parts = stage(grid, grid.work_middle, lists, turned, matrix, sources, parts, ())
+    parts = stage(grid, grid.work_middle, lists, turned, matrix, sources, parts, far_heads[:1])
     first = exchange(parts)
 
     sources = [other, ((end_heads[0], 2), (end_tail, 1, 0)), far, ((far_heads[0], 2), (end_tail, 1, cap))]
     for i in range(count):
         sources += [far_crossed[i], ((far_heads[1 + i], 2), (far_tails[i], 1))]
-    last = exchange(stage(grid, grid.work_far, lists, turned, matrix, sources, (), first[1:]))
+    last = exchange(stage(grid, grid.work_far, lists, turned, matrix, sources, (), first[1:2]))
     return assemble(grid, ((grid.work_near, grid.work_middle), (grid.work_far,)), [first, last])[None, None]
 
 

time: 119 us -> 123 us (1.034)
  waiting for transfers between devices: 52.1 us -> 56.9 us
    ppermute x18, waiting for transfers between devices: 38.3 us -> 50.8 us  [move(): return lax.ppermute(x, ('blk', 'rows'), perm) if perm else jnp.zeros_like(x)]
    ppermute x2, waiting for transfers between devices: 8.8 us -> 4.4 us  [exchange(): lax.ppermute(parts[2], 'rows', [(g + 1, g) for g in range(groups - 1)])]
    ppermute x2, waiting for transfers between devices: 5.02 us -> 1.71 us  [exchange(): lax.ppermute(parts[1], 'rows', [(g, g + 1) for g in range(groups - 1)])]
    ppermute x18, starting transfers between devices: 24.9 us -> 23.4 us  [move(): return lax.ppermute(x, ('blk', 'rows'), perm) if perm else jnp.zeros_like(x)]
  transfers between devices with their start and end apart: 22 -> 22, of which waited for: 10 -> 8; matrix products, arithmetic and copies ran while one was open for 0% -> 0% of each run, Pallas kernels for 14% -> 17%
where the time goes in v15:
time: 123 us; the launch traced here: 122 us
  waiting for transfers between devices  56.9 us (46%)
  starting transfers between devices  37.3 us (30%)
  Pallas kernels  25.8 us (21%)
  local copies, waits for them, and re-layouts  1.26 us (1%)
    ppermute x18, waiting for transfers between devices, move(): return lax.ppermute(x, ('blk', 'rows'), perm) if perm else jnp.zeros_like(x)  50.8 us
    ppermute x18, starting transfers between devices, move(): return lax.ppermute(x, ('blk', 'rows'), perm) if perm else jnp.zeros_like(x)  23.4 us
    pallas_call x3, Pallas kernels, stage(): pl.pallas_call(functools.partial(stage_kernel, grid, plan, layout, carrie...  12.2 us
    ppermute x2, starting transfers between devices, exchange(): lax.ppermute(parts[1], 'rows', [(g, g + 1) for g in range(groups - 1)])  10.1 us
    pallas_call x7, Pallas kernels, pick(): pl.pallas_call(functools.partial(pick_kernel, grid, plan, layout, carry,...  6.94 us
    ppermute x2, waiting for transfers between devices, exchange(): lax.ppermute(parts[2], 'rows', [(g + 1, g) for g in range(groups - 1)])  4.4 us
    ppermute x2, starting transfers between devices, exchange(): lax.ppermute(parts[2], 'rows', [(g + 1, g) for g in range(groups - 1)])  3.83 us
    pallas_call x1, Pallas kernels, pack(): pl.pallas_call(functools.partial(pack_kernel, grid), grid=(1,), in_specs=...  2.64 us
  transfers between devices with their start and end apart: 22, of which 8 were waited for; matrix products, arithmetic and copies ran while one was open for 0% of the time, Pallas kernels for 17%

profile of v15, /device:TPU:1, one launch (start us, length us, event | category | flops | bytes accessed | tf_op | source)
XLA Modules:
  0.0 121.7 jit_solution(17621526310352773574)
XLA Ops:
  0.0 2.6 %pack_rows.1 = (bf16[4112,128]{1,0:T(8,128)(2,1)}, bf16[2048,128]{1,0:T(8,128)(2,1)}) custom-call(s32[3,1,16]{2,1,0:T(1,128)} %bitcast.26, s32[8,8]{1,0:T(8,128)} %bitcast.14, bf16[16,128,384]{2,1,0:T(8,128)(2,1)} %bitcast.25), custom_call_target="tpu_custom_call" | custom-call | flops 1024 | bytes 1024 | tf_op jit(solution)/shard_map/pack_rows/pallas_call | solution.py:130
  2.6 0.7 collective-permute-start.5
  3.4 4.7 %collective-permute-start.1 = (bf16[4112,128]{1,0:T(8,128)(2,1)}, bf16[4112,128]{1,0:T(8,128)(2,1)S(1)}, u32[]{:S(2)}, u32[]{:S(2)}) collective-permute-start(bf16[4112,128]{1,0:T(8,128)(2,1)} %get-tuple-element.23.head.refs_1_.refs_0_), channel_id=1, source_target_pairs={{0,8},{4,12},{16,24},{20,28},{8,0},{12,4},{24,16},{28,20},{1,9},{5... | collective-permute-start | bytes 3158024 | tf_op jit(solution)/shard_map/ppermute | solution.py:366
  8.1 1.2 %collective-permute-start = (s32[8,8]{1,0:T(8,128)S(1)}, s32[8,8]{1,0:T(8,128)S(1)}, u32[]{:S(2)}, u32[]{:S(2)}) collective-permute-start(s32[8,8]{1,0:T(8,128)S(1)} %bitcast.15), channel_id=1, source_target_pairs={{4,0},{0,4},{12,8},{8,12},{20,16},{16,20},{28,24},{24,28},{5,1},{1... | collective-permute-start | bytes 776 | tf_op jit(solution)/shard_map/ppermute | solution.py:366
  9.3 1.5 %collective-permute-done.refs_0_ = s32[8,8]{1,0:T(8,128)S(1)} collective-permute-done((s32[8,8]{1,0:T(8,128)S(1)}, s32[8,8]{1,0:T(8,128)S(1)}, u32[]{:S(2)}, u32[]{:S(2)}) %collective-permute-start) | collective-permute-done | bytes 288 | tf_op jit(solution)/shard_map/ppermute | solution.py:366
  10.8 1.2 %copy-done.1 = bf16[4112,128]{1,0:T(8,128)(2,1)S(1)} copy-done((bf16[4112,128]{1,0:T(8,128)(2,1)S(1)}, bf16[4112,128]{1,0:T(8,128)(2,1)}, u32[]{:S(2)}) %copy-start.1) | copy-done | bytes 1052696
  12.0 1.7 %pick_rows.7 = bf16[3072,128]{1,0:T(8,128)(2,1)S(1)} custom-call(s32[8,8]{1,0:T(8,128)S(1)} %collective-permute-done.refs_0_, bf16[4112,128]{1,0:T(8,128)(2,1)S(1)} %copy-done.1, bf16[2048,128]{1,0:T(8,128)(2,1)} %get-tuple-element.24.tail.refs_2_.refs_1_), custom_call_target="tpu_custom_call" | custom-call | flops 1024 | bytes 1024 | tf_op jit(solution)/shard_map/pick_rows/pallas_call | solution.py:222
  13.7 1.3 %collective-permute-start.3 = (bf16[3072,128]{1,0:T(8,128)(2,1)S(1)}, bf16[3072,128]{1,0:T(8,128)(2,1)S(1)}, u32[]{:S(2)}, u32[]{:S(2)}) collective-permute-start(bf16[3072,128]{1,0:T(8,128)(2,1)S(1)} %pick_rows.7), channel_id=1, source_target_pairs={{0,4},{4,0},{8,12},{12,8},{16,20},{20,16},{24,28},{28,24},{1,5},{5... | collective-permute-start | bytes 2359304 | tf_op jit(solution)/shard_map/ppermute | solution.py:366
  15.0 2.0 %collective-permute-start.2 = (bf16[2048,128]{1,0:T(8,128)(2,1)}, bf16[2048,128]{1,0:T(8,128)(2,1)S(1)}, u32[]{:S(2)}, u32[]{:S(2)}) collective-permute-start(bf16[2048,128]{1,0:T(8,128)(2,1)} %get-tuple-element.24.tail.refs_2_.refs_1_), channel_id=1, source_target_pairs={{1,9},{5,13},{17,25},{21,29},{9,1},{13,5},{25,17},{29,21},{2,10},{... | collective-permute-start | bytes 1572872 | tf_op jit(solution)/shard_map/ppermute | solution.py:366
  17.0 0.7 collective-permute-start.6
  17.7 0.0 collective-permute-done.5.refs_0_.refs_1_
  17.7 13.2 %collective-permute-done.1.refs_1_.refs_2_.refs_5_ = bf16[4112,128]{1,0:T(8,128)(2,1)S(1)} collective-permute-done((bf16[4112,128]{1,0:T(8,128)(2,1)}, bf16[4112,128]{1,0:T(8,128)(2,1)S(1)}, u32[]{:S(2)}, u32[]{:S(2)}) %collective-permute-start.1) | collective-permute-done | bytes 1052704 | tf_op jit(solution)/shard_map/ppermute | solution.py:366
  30.9 0.7 pick_rows.9
  31.6 1.3 %collective-permute-start.8 = (bf16[2048,128]{1,0:T(8,128)(2,1)S(1)}, bf16[2048,128]{1,0:T(8,128)(2,1)S(1)}, u32[]{:S(2)}, u32[]{:S(2)}) collective-permute-start(bf16[2048,128]{1,0:T(8,128)(2,1)S(1)} %get-tuple-element.26), channel_id=1, source_target_pairs={{8,0},{12,4},{16,24},{20,28},{9,1},{13,5},{17,25},{21,29},{10,2},{... | collective-permute-start | bytes 1572872 | tf_op jit(solution)/shard_map/ppermute | solution.py:366
  32.9 0.7 collective-permute-start.11
  33.7 3.7 %collective-permute-done.2.refs_2_.refs_3_ = bf16[2048,128]{1,0:T(8,128)(2,1)S(1)} collective-permute-done((bf16[2048,128]{1,0:T(8,128)(2,1)}, bf16[2048,128]{1,0:T(8,128)(2,1)S(1)}, u32[]{:S(2)}, u32[]{:S(2)}) %collective-permute-start.2) | collective-permute-done | bytes 524320 | tf_op jit(solution)/shard_map/ppermute | solution.py:366
  37.4 0.7 collective-permute-start.7
  38.0 0.0 collective-permute-done.3.refs_3_.refs_4_
  38.1 0.7 pick_rows.8.refs_3_
  38.7 1.3 %collective-permute-start.4 = (bf16[3072,128]{1,0:T(8,128)(2,1)S(1)}, bf16[3072,128]{1,0:T(8,128)(2,1)S(1)}, u32[]{:S(2)}, u32[]{:S(2)}) collective-permute-start(bf16[3072,128]{1,0:T(8,128)(2,1)S(1)} %pick_rows.8.refs_3_), channel_id=1, source_target_pairs={{0,4},{4,0},{8,12},{12,8},{16,20},{20,16},{24,28},{28,24},{1,5},{5... | collective-permute-start | bytes 2359304 | tf_op jit(solution)/shard_map/ppermute | solution.py:366
  40.1 0.0 collective-permute-done.6.refs_1_.refs_2_.refs_3_
  40.1 0.0 collective-permute-done.7.refs_2_.refs_6_
  40.1 7.1 %collective-permute-done.8.refs_4_.refs_9_.refs_2_ = bf16[2048,128]{1,0:T(8,128)(2,1)S(1)} collective-permute-done((bf16[2048,128]{1,0:T(8,128)(2,1)S(1)}, bf16[2048,128]{1,0:T(8,128)(2,1)S(1)}, u32[]{:S(2)}, u32[]{:S(2)}) %collective-permute-start.8) | collective-permute-done | bytes 524320 | tf_op jit(solution)/shard_map/ppermute | solution.py:366
  47.1 0.7 pick_rows.10.refs_3_
  47.9 0.0 copy-start.2
  47.9 1.4 %collective-permute-start.10 = (bf16[3072,128]{1,0:T(8,128)(2,1)S(1)}, bf16[3072,128]{1,0:T(8,128)(2,1)S(1)}, u32[]{:S(2)}, u32[]{:S(2)}) collective-permute-start(bf16[3072,128]{1,0:T(8,128)(2,1)S(1)} %pick_rows.10.refs_3_), channel_id=1, source_target_pairs={{8,4},{12,0},{16,28},{20,24},{9,5},{13,1},{17,29},{21,25},{10,6},{... | collective-permute-start | bytes 2359304 | tf_op jit(solution)/shard_map/ppermute | solution.py:366
  49.3 0.7 collective-permute-start.15
  50.0 0.7 pick_rows.11
  50.7 0.0 copy-start
  50.7 0.0 copy-start.4
  50.7 0.0 copy-start.5
  50.8 0.8 collective-permute-start.9
  51.6 1.5 %turn_rows.1.turned = bf16[16,384,128]{2,1,0:T(8,128)(2,1)S(1)} custom-call(bf16[4112,128]{1,0:T(8,128)(2,1)S(1)} %copy-done.2, bf16[2048,128]{1,0:T(8,128)(2,1)} %get-tuple-element.24.tail.refs_2_.refs_1_), custom_call_target="tpu_custom_call" | custom-call | flops 1024 | bytes 1024 | tf_op jit(solution)/shard_map/turn_rows/pallas_call | solution.py:159
  53.1 0.0 copy-done
  53.1 0.0 copy-done.4
  53.2 4.1 %stage_products.3 = (bf16[3,3,128,128]{3,2,1,0:T(8,128)(2,1)S(1)}, bf16[3,3,128,128]{3,2,1,0:T(8,128)(2,1)S(1)}, bf16[3,3,128,128]{3,2,1,0:T(8,128)(2,1)S(1)}) custom-call(s32[8,8]{1,0:T(8,128)S(1)} %bitcast.19, s32[8,8]{1,0:T(8,128)S(1)} %bitcast.16, s32[1,8]{1,0:T(1,128)S(1)} %bitcast.22, bf16[16,384,128]{2,1,0:T(8,128)(2,1)S(1)} %turn_rows.1.turned, ...), custom_call_target="tpu_custom_call" | custom-call | flops 1024 | bytes 1024 | tf_op jit(solution)/shard_map/stage_products/pallas_call | solution.py:301
  57.3 0.0 collective-permute-done.11.refs_0_.refs_1_.refs_4_
  57.3 0.9 pick_rows.12
  58.2 1.3 %collective-permute-start.12 = (bf16[2048,128]{1,0:T(8,128)(2,1)S(1)}, bf16[2048,128]{1,0:T(8,128)(2,1)S(1)}, u32[]{:S(2)}, u32[]{:S(2)}) collective-permute-start(bf16[2048,128]{1,0:T(8,128)(2,1)S(1)} %get-tuple-element.30.refs_7_), channel_id=1, source_target_pairs={{8,0},{12,4},{16,24},{20,28},{9,1},{13,5},{17,25},{21,29},{10,2},{... | collective-permute-start | bytes 1572872 | tf_op jit(solution)/shard_map/ppermute | solution.py:366
  59.5 0.0 collective-permute-done.15.refs_2_.refs_4_.refs_5_
  59.5 15.2 %collective-permute-done.4.refs_0_.refs_11_ = bf16[3072,128]{1,0:T(8,128)(2,1)S(1)} collective-permute-done((bf16[3072,128]{1,0:T(8,128)(2,1)S(1)}, bf16[3072,128]{1,0:T(8,128)(2,1)S(1)}, u32[]{:S(2)}, u32[]{:S(2)}) %collective-permute-start.4) | collective-permute-done | bytes 786464 | tf_op jit(solution)/shard_map/ppermute | solution.py:366
  74.7 0.0 collective-permute-done.10.refs_2_.refs_10_
  74.7 1.5 %pick_rows.13 = (bf16[3072,128]{1,0:T(8,128)(2,1)S(1)}, bf16[2048,128]{1,0:T(8,128)(2,1)S(1)}, bf16[1024,128]{1,0:T(8,128)(2,1)S(1)}) custom-call(s32[8,8]{1,0:T(8,128)S(1)} %collective-permute-done.refs_0_, bf16[4112,128]{1,0:T(8,128)(2,1)S(1)} %collective-permute-done.11.refs_0_.refs_1_.refs_4_, ...), custom_call_target="tpu_custom_call" | custom-call | flops 1024 | bytes 1024 | tf_op jit(solution)/shard_map/pick_rows/pallas_call | solution.py:222
  76.2 0.7 collective-permute-start.17
  77.0 1.3 %collective-permute-start.18 = (bf16[2048,128]{1,0:T(8,128)(2,1)S(1)}, bf16[2048,128]{1,0:T(8,128)(2,1)S(1)}, u32[]{:S(2)}, u32[]{:S(2)}) collective-permute-start(bf16[2048,128]{1,0:T(8,128)(2,1)S(1)} %get-tuple-element.34.refs_8_), channel_id=1, source_target_pairs={{8,4},{12,0},{16,28},{20,24},{9,5},{13,1},{17,29},{21,25},{10,6},{... | collective-permute-start | bytes 1572872 | tf_op jit(solution)/shard_map/ppermute | solution.py:366
  78.3 1.3 %collective-permute-start.16 = (bf16[2048,128]{1,0:T(8,128)(2,1)S(1)}, bf16[2048,128]{1,0:T(8,128)(2,1)S(1)}, u32[]{:S(2)}, u32[]{:S(2)}) collective-permute-start(bf16[2048,128]{1,0:T(8,128)(2,1)S(1)} %get-tuple-element.35), channel_id=1, source_target_pairs={{9,1},{13,5},{17,25},{21,29},{10,2},{14,6},{18,26},{22,30}} | collective-permute-start | bytes 1572872 | tf_op jit(solution)/shard_map/ppermute | solution.py:366
  79.6 0.0 collective-permute-done.9.refs_1_
  79.6 0.0 collective-permute-done.12.refs_6_
  79.6 4.0 %stage_products.4 = (bf16[5,3,128,128]{3,2,1,0:T(8,128)(2,1)S(1)}, bf16[5,3,128,128]{3,2,1,0:T(8,128)(2,1)S(1)}, bf16[5,3,128,128]{3,2,1,0:T(8,128)(2,1)S(1)}) custom-call(s32[8,8]{1,0:T(8,128)S(1)} %bitcast.20, s32[8,8]{1,0:T(8,128)S(1)} %bitcast.17, s32[1,8]{1,0:T(1,128)S(1)} %bitcast.23, bf16[16,384,128]{2,1,0:T(8,128)(2,1)S(1)} %turn_rows.1.turned, ...), custom_call_target="tpu_custom_call" | custom-call | flops 1024 | bytes 1024 | tf_op jit(solution)/shard_map/stage_products/pallas_call | solution.py:301
  83.6 6.8 %collective-permute-start.13 = (bf16[5,3,128,128]{3,2,1,0:T(8,128)(2,1)S(1)}, bf16[5,3,128,128]{3,2,1,0:T(8,128)(2,1)S(1)}, u32[]{:S(2)}, u32[]{:S(2)}) collective-permute-start(bf16[5,3,128,128]{3,2,1,0:T(8,128)(2,1)S(1)} %get-tuple-element.32), channel_id=1, source_target_pairs={{0,1},{1,2},{2,3},{4,5},{5,6},{6,7},{8,9},{9,10},{10,11},{12,13},{... | collective-permute-start | bytes 1474568 | tf_op jit(solution)/shard_map/ppermute | solution.py:375
  90.4 1.3 %collective-permute-start.19 = (bf16[1024,128]{1,0:T(8,128)(2,1)S(1)}, bf16[1024,128]{1,0:T(8,128)(2,1)S(1)}, u32[]{:S(2)}, u32[]{:S(2)}) collective-permute-start(bf16[1024,128]{1,0:T(8,128)(2,1)S(1)} %get-tuple-element.37), channel_id=1, source_target_pairs={{9,5},{13,1},{17,29},{21,25},{10,6},{14,2},{18,30},{22,26}} | collective-permute-start | bytes 786440 | tf_op jit(solution)/shard_map/ppermute | solution.py:366
  91.7 10.1 %collective-permute-done.19.refs_10_ = bf16[1024,128]{1,0:T(8,128)(2,1)S(1)} collective-permute-done((bf16[1024,128]{1,0:T(8,128)(2,1)S(1)}, bf16[1024,128]{1,0:T(8,128)(2,1)S(1)}, u32[]{:S(2)}, u32[]{:S(2)}) %collective-permute-start.19) | collective-permute-done | bytes 262176 | tf_op jit(solution)/shard_map/ppermute | solution.py:366
  101.8 1.9 %collective-permute-start.14 = (bf16[5,3,128,128]{3,2,1,0:T(8,128)(2,1)S(1)}, bf16[5,3,128,128]{3,2,1,0:T(8,128)(2,1)S(1)}, u32[]{:S(2)}, u32[]{:S(2)}) collective-permute-start(bf16[5,3,128,128]{3,2,1,0:T(8,128)(2,1)S(1)} %get-tuple-element.33), channel_id=1, source_target_pairs={{1,0},{2,1},{3,2},{5,4},{6,5},{7,6},{9,8},{10,9},{11,10},{13,12},{... | collective-permute-start | bytes 1474568 | tf_op jit(solution)/shard_map/ppermute | solution.py:376
  103.7 0.0 collective-permute-done.18.refs_9_
  103.8 0.0 collective-permute-done.16.refs_3_.refs_7_
  103.8 0.0 collective-permute-done.13.refs_11_.refs_1_
  103.8 0.0 collective-permute-done.17.refs_8_
  103.8 4.1 %stage_products.5 = (bf16[3,3,128,128]{3,2,1,0:T(8,128)(2,1)S(1)}, bf16[3,3,128,128]{3,2,1,0:T(8,128)(2,1)S(1)}, bf16[3,3,128,128]{3,2,1,0:T(8,128)(2,1)S(1)}) custom-call(s32[8,8]{1,0:T(8,128)S(1)} %bitcast.21, s32[8,8]{1,0:T(8,128)S(1)} %bitcast.18, s32[1,8]{1,0:T(1,128)S(1)} %bitcast.24, bf16[16,384,128]{2,1,0:T(8,128)(2,1)S(1)} %turn_rows.1.turned, ...), custom_call_target="tpu_custom_call" | custom-call | flops 1024 | bytes 1024 | tf_op jit(solution)/shard_map/stage_products/pallas_call | solution.py:301
  107.9 3.3 %collective-permute-start.20 = (bf16[3,3,128,128]{3,2,1,0:T(8,128)(2,1)S(1)}, bf16[3,3,128,128]{3,2,1,0:T(8,128)(2,1)S(1)}, u32[]{:S(2)}, u32[]{:S(2)}) collective-permute-start(bf16[3,3,128,128]{3,2,1,0:T(8,128)(2,1)S(1)} %get-tuple-element.39), channel_id=1, source_target_pairs={{0,1},{1,2},{2,3},{4,5},{5,6},{6,7},{8,9},{9,10},{10,11},{12,13},{... | collective-permute-start | bytes 884744 | tf_op jit(solution)/shard_map/ppermute | solution.py:375
  111.1 1.9 %collective-permute-start.21 = (bf16[3,3,128,128]{3,2,1,0:T(8,128)(2,1)S(1)}, bf16[3,3,128,128]{3,2,1,0:T(8,128)(2,1)S(1)}, u32[]{:S(2)}, u32[]{:S(2)}) collective-permute-start(bf16[3,3,128,128]{3,2,1,0:T(8,128)(2,1)S(1)} %get-tuple-element.40), channel_id=1, source_target_pairs={{1,0},{2,1},{3,2},{5,4},{6,5},{7,6},{9,8},{10,9},{11,10},{13,12},{... | collective-permute-start | bytes 884744 | tf_op jit(solution)/shard_map/ppermute | solution.py:376
  113.1 0.0 collective-permute-done.14.refs_2_
  113.1 1.7 %collective-permute-done.20.refs_4_ = bf16[3,3,128,128]{3,2,1,0:T(8,128)(2,1)S(1)} collective-permute-done((bf16[3,3,128,128]{3,2,1,0:T(8,128)(2,1)S(1)}, bf16[3,3,128,128]{3,2,1,0:T(8,128)(2,1)S(1)}, u32[]{:S(2)}, u32[]{:S(2)}) %collective-permute-start.20) | collective-permute-done | bytes 294944 | tf_op jit(solution)/shard_map/ppermute | solution.py:375
  114.8 4.4 %collective-permute-done.21.refs_5_ = bf16[3,3,128,128]{3,2,1,0:T(8,128)(2,1)S(1)} collective-permute-done((bf16[3,3,128,128]{3,2,1,0:T(8,128)(2,1)S(1)}, bf16[3,3,128,128]{3,2,1,0:T(8,128)(2,1)S(1)}, u32[]{:S(2)}, u32[]{:S(2)}) %collective-permute-start.21) | collective-permute-done | bytes 294944 | tf_op jit(solution)/shard_map/ppermute | solution.py:376
  119.2 2.5 %assemble_coarse.1 = f32[5120,128]{1,0:T(8,128)} custom-call(bf16[5,3,128,128]{3,2,1,0:T(8,128)(2,1)S(1)} %get-tuple-element.31.refs_0_, bf16[5,3,128,128]{3,2,1,0:T(8,128)(2,1)S(1)} %collective-permute-done.13.refs_11_.refs_1_, bf16[5,3,128,128]{3,2,1,0:T(8,128)(2,1)S(1)} %collective-permute-done.14.refs_2_, ...), custom_call_target="tpu_custom_call" | custom-call | flops 1024 | bytes 1024 | tf_op jit(solution)/shard_map/assemble_coarse/pallas_call | solution.py:342
  (5 shorter events, 0.0 us)
Async XLA Ops:
  0.0 8.1 %copy-start.3 = (s32[1,1,8,8]{3,2,1,0:T(8,128)S(1)}, s32[1,1,8,8]{3,2,1,0:T(8,128)}, u32[]{:S(2)}) copy-start(s32[1,1,8,8]{3,2,1,0:T(8,128)} %param.8) | copy-start | bytes 772
  2.6 15.1 %collective-permute-start.5 = (bf16[4112,128]{1,0:T(8,128)(2,1)}, bf16[4112,128]{1,0:T(8,128)(2,1)S(1)}, u32[]{:S(2)}, u32[]{:S(2)}) collective-permute-start(bf16[4112,128]{1,0:T(8,128)(2,1)} %get-tuple-element.23.head.refs_1_.refs_0_), channel_id=1, source_target_pairs={{8,16},{12,20},{16,8},{20,12},{9,17},{13,21},{17,9},{21,13},{10,18... | collective-permute-start | bytes 3158024 | tf_op jit(solution)/shard_map/ppermute | solution.py:366
  3.4 27.5 %collective-permute-start.1 = (bf16[4112,128]{1,0:T(8,128)(2,1)}, bf16[4112,128]{1,0:T(8,128)(2,1)S(1)}, u32[]{:S(2)}, u32[]{:S(2)}) collective-permute-start(bf16[4112,128]{1,0:T(8,128)(2,1)} %get-tuple-element.23.head.refs_1_.refs_0_), channel_id=1, source_target_pairs={{0,8},{4,12},{16,24},{20,28},{8,0},{12,4},{24,16},{28,20},{1,9},{5... | collective-permute-start | bytes 3158024 | tf_op jit(solution)/shard_map/ppermute | solution.py:366
  8.1 2.8 %collective-permute-start = (s32[8,8]{1,0:T(8,128)S(1)}, s32[8,8]{1,0:T(8,128)S(1)}, u32[]{:S(2)}, u32[]{:S(2)}) collective-permute-start(s32[8,8]{1,0:T(8,128)S(1)} %bitcast.15), channel_id=1, source_target_pairs={{4,0},{0,4},{12,8},{8,12},{20,16},{16,20},{28,24},{24,28},{5,1},{1... | collective-permute-start | bytes 776 | tf_op jit(solution)/shard_map/ppermute | solution.py:366
  10.8 1.2 %copy-start.1 = (bf16[4112,128]{1,0:T(8,128)(2,1)S(1)}, bf16[4112,128]{1,0:T(8,128)(2,1)}, u32[]{:S(2)}) copy-start(bf16[4112,128]{1,0:T(8,128)(2,1)} %get-tuple-element.23.head.refs_1_.refs_0_) | copy-start | bytes 3158020
  13.7 24.3 %collective-permute-start.3 = (bf16[3072,128]{1,0:T(8,128)(2,1)S(1)}, bf16[3072,128]{1,0:T(8,128)(2,1)S(1)}, u32[]{:S(2)}, u32[]{:S(2)}) collective-permute-start(bf16[3072,128]{1,0:T(8,128)(2,1)S(1)} %pick_rows.7), channel_id=1, source_target_pairs={{0,4},{4,0},{8,12},{12,8},{16,20},{20,16},{24,28},{28,24},{1,5},{5... | collective-permute-start | bytes 2359304 | tf_op jit(solution)/shard_map/ppermute | solution.py:366
  15.0 22.4 %collective-permute-start.2 = (bf16[2048,128]{1,0:T(8,128)(2,1)}, bf16[2048,128]{1,0:T(8,128)(2,1)S(1)}, u32[]{:S(2)}, u32[]{:S(2)}) collective-permute-start(bf16[2048,128]{1,0:T(8,128)(2,1)} %get-tuple-element.24.tail.refs_2_.refs_1_), channel_id=1, source_target_pairs={{1,9},{5,13},{17,25},{21,29},{9,1},{13,5},{25,17},{29,21},{2,10},{... | collective-permute-start | bytes 1572872 | tf_op jit(solution)/shard_map/ppermute | solution.py:366
  17.0 23.0 %collective-permute-start.6 = (bf16[2048,128]{1,0:T(8,128)(2,1)}, bf16[2048,128]{1,0:T(8,128)(2,1)S(1)}, u32[]{:S(2)}, u32[]{:S(2)}) collective-permute-start(bf16[2048,128]{1,0:T(8,128)(2,1)} %get-tuple-element.24.tail.refs_2_.refs_1_), channel_id=1, source_target_pairs={{9,17},{13,21},{17,9},{21,13},{10,18},{14,22},{18,10},{22,14}} | collective-permute-start | bytes 1572872 | tf_op jit(solution)/shard_map/ppermute | solution.py:366
  31.6 15.5 %collective-permute-start.8 = (bf16[2048,128]{1,0:T(8,128)(2,1)S(1)}, bf16[2048,128]{1,0:T(8,128)(2,1)S(1)}, u32[]{:S(2)}, u32[]{:S(2)}) collective-permute-start(bf16[2048,128]{1,0:T(8,128)(2,1)S(1)} %get-tuple-element.26), channel_id=1, source_target_pairs={{8,0},{12,4},{16,24},{20,28},{9,1},{13,5},{17,25},{21,29},{10,2},{... | collective-permute-start | bytes 1572872 | tf_op jit(solution)/shard_map/ppermute | solution.py:366
  32.9 24.4 %collective-permute-start.11 = (bf16[4112,128]{1,0:T(8,128)(2,1)S(1)}, bf16[4112,128]{1,0:T(8,128)(2,1)S(1)}, u32[]{:S(2)}, u32[]{:S(2)}) collective-permute-start(bf16[4112,128]{1,0:T(8,128)(2,1)S(1)} %collective-permute-done.1.refs_1_.refs_2_.refs_5_), channel_id=1, source_target_pairs={{8,16},{12,20},{16,8},{20,12},{9,17},{13,21},{17,9},{21,13},{10,18... | collective-permute-start | bytes 3158024 | tf_op jit(solution)/shard_map/ppermute | solution.py:366
  37.4 2.7 %collective-permute-start.7 = (bf16[16,128]{1,0:T(8,128)(2,1)S(1)}, bf16[16,128]{1,0:T(8,128)(2,1)S(1)}, u32[]{:S(2)}, u32[]{:S(2)}) collective-permute-start(bf16[16,128]{1,0:T(8,128)(2,1)S(1)} %get-tuple-element.25), channel_id=1, source_target_pairs={{12,8},{8,12},{20,16},{16,20},{13,9},{9,13},{21,17},{17,21},{14,10... | collective-permute-start | bytes 12296 | tf_op jit(solution)/shard_map/ppermute | solution.py:366
  38.7 35.9 %collective-permute-start.4 = (bf16[3072,128]{1,0:T(8,128)(2,1)S(1)}, bf16[3072,128]{1,0:T(8,128)(2,1)S(1)}, u32[]{:S(2)}, u32[]{:S(2)}) collective-permute-start(bf16[3072,128]{1,0:T(8,128)(2,1)S(1)} %pick_rows.8.refs_3_), channel_id=1, source_target_pairs={{0,4},{4,0},{8,12},{12,8},{16,20},{20,16},{24,28},{28,24},{1,5},{5... | collective-permute-start | bytes 2359304 | tf_op jit(solution)/shard_map/ppermute | solution.py:366
  47.9 3.7 %copy-start.2 = (bf16[4112,128]{1,0:T(8,128)(2,1)S(1)}, bf16[4112,128]{1,0:T(8,128)(2,1)}, u32[]{:S(2)}) copy-start(bf16[4112,128]{1,0:T(8,128)(2,1)} %get-tuple-element.23.head.refs_1_.refs_0_) | copy-start | bytes 3158020
  47.9 26.8 %collective-permute-start.10 = (bf16[3072,128]{1,0:T(8,128)(2,1)S(1)}, bf16[3072,128]{1,0:T(8,128)(2,1)S(1)}, u32[]{:S(2)}, u32[]{:S(2)}) collective-permute-start(bf16[3072,128]{1,0:T(8,128)(2,1)S(1)} %pick_rows.10.refs_3_), channel_id=1, source_target_pairs={{8,4},{12,0},{16,28},{20,24},{9,5},{13,1},{17,29},{21,25},{10,6},{... | collective-permute-start | bytes 2359304 | tf_op jit(solution)/shard_map/ppermute | solution.py:366
  49.3 10.2 %collective-permute-start.15 = (bf16[2048,128]{1,0:T(8,128)(2,1)S(1)}, bf16[2048,128]{1,0:T(8,128)(2,1)S(1)}, u32[]{:S(2)}, u32[]{:S(2)}) collective-permute-start(bf16[2048,128]{1,0:T(8,128)(2,1)S(1)} %collective-permute-done.2.refs_2_.refs_3_), channel_id=1, source_target_pairs={{9,17},{13,21},{17,9},{21,13},{10,18},{14,22},{18,10},{22,14}} | collective-permute-start | bytes 1572872 | tf_op jit(solution)/shard_map/ppermute | solution.py:366
  50.7 2.4 %copy-start = (bf16[1,1,8,8,128,128]{5,4,3,2,1,0:T(8,128)(2,1)S(1)}, bf16[1,1,8,8,128,128]{5,4,3,2,1,0:T(8,128)(2,1)}, u32[]{:S(2)}) copy-start(bf16[1,1,8,8,128,128]{5,4,3,2,1,0:T(8,128)(2,1)} %param.6) | copy-start | bytes 6291460
  50.7 2.4 %copy-start.4 = (s32[1,1,8,8]{3,2,1,0:T(8,128)S(1)}, s32[1,1,8,8]{3,2,1,0:T(8,128)}, u32[]{:S(2)}) copy-start(s32[1,1,8,8]{3,2,1,0:T(8,128)} %param.7) | copy-start | bytes 772
  50.7 2.4 %copy-start.5 = (s32[1,1,8]{2,1,0:T(1,128)S(1)}, s32[1,1,8]{2,1,0:T(1,128)}, u32[]{:S(2)}) copy-start(s32[1,1,8]{2,1,0:T(1,128)} %param.9) | copy-start | bytes 100
  50.8 28.8 %collective-permute-start.9 = (bf16[3072,128]{1,0:T(8,128)(2,1)S(1)}, bf16[3072,128]{1,0:T(8,128)(2,1)S(1)}, u32[]{:S(2)}, u32[]{:S(2)}) collective-permute-start(bf16[3072,128]{1,0:T(8,128)(2,1)S(1)} %pick_rows.11), channel_id=1, source_target_pairs={{8,12},{12,8},{16,20},{20,16},{9,13},{13,9},{17,21},{21,17},{10,14... | collective-permute-start | bytes 2359304 | tf_op jit(solution)/shard_map/ppermute | solution.py:366
  58.2 21.4 %collective-permute-start.12 = (bf16[2048,128]{1,0:T(8,128)(2,1)S(1)}, bf16[2048,128]{1,0:T(8,128)(2,1)S(1)}, u32[]{:S(2)}, u32[]{:S(2)}) collective-permute-start(bf16[2048,128]{1,0:T(8,128)(2,1)S(1)} %get-tuple-element.30.refs_7_), channel_id=1, source_target_pairs={{8,0},{12,4},{16,24},{20,28},{9,1},{13,5},{17,25},{21,29},{10,2},{... | collective-permute-start | bytes 1572872 | tf_op jit(solution)/shard_map/ppermute | solution.py:366
  76.2 27.5 %collective-permute-start.17 = (bf16[3072,128]{1,0:T(8,128)(2,1)S(1)}, bf16[3072,128]{1,0:T(8,128)(2,1)S(1)}, u32[]{:S(2)}, u32[]{:S(2)}) collective-permute-start(bf16[3072,128]{1,0:T(8,128)(2,1)S(1)} %get-tuple-element.36), channel_id=1, source_target_pairs={{8,12},{12,8},{16,20},{20,16},{9,13},{13,9},{17,21},{21,17},{10,14... | collective-permute-start | bytes 2359304 | tf_op jit(solution)/shard_map/ppermute | solution.py:366
  77.0 26.8 %collective-permute-start.18 = (bf16[2048,128]{1,0:T(8,128)(2,1)S(1)}, bf16[2048,128]{1,0:T(8,128)(2,1)S(1)}, u32[]{:S(2)}, u32[]{:S(2)}) collective-permute-start(bf16[2048,128]{1,0:T(8,128)(2,1)S(1)} %get-tuple-element.34.refs_8_), channel_id=1, source_target_pairs={{8,4},{12,0},{16,28},{20,24},{9,5},{13,1},{17,29},{21,25},{10,6},{... | collective-permute-start | bytes 1572872 | tf_op jit(solution)/shard_map/ppermute | solution.py:366
  78.3 25.5 %collective-permute-start.16 = (bf16[2048,128]{1,0:T(8,128)(2,1)S(1)}, bf16[2048,128]{1,0:T(8,128)(2,1)S(1)}, u32[]{:S(2)}, u32[]{:S(2)}) collective-permute-start(bf16[2048,128]{1,0:T(8,128)(2,1)S(1)} %get-tuple-element.35), channel_id=1, source_target_pairs={{9,1},{13,5},{17,25},{21,29},{10,2},{14,6},{18,26},{22,30}} | collective-permute-start | bytes 1572872 | tf_op jit(solution)/shard_map/ppermute | solution.py:366
  83.6 20.1 %collective-permute-start.13 = (bf16[5,3,128,128]{3,2,1,0:T(8,128)(2,1)S(1)}, bf16[5,3,128,128]{3,2,1,0:T(8,128)(2,1)S(1)}, u32[]{:S(2)}, u32[]{:S(2)}) collective-permute-start(bf16[5,3,128,128]{3,2,1,0:T(8,128)(2,1)S(1)} %get-tuple-element.32), channel_id=1, source_target_pairs={{0,1},{1,2},{2,3},{4,5},{5,6},{6,7},{8,9},{9,10},{10,11},{12,13},{... | collective-permute-start | bytes 1474568 | tf_op jit(solution)/shard_map/ppermute | solution.py:375
  90.4 11.4 %collective-permute-start.19 = (bf16[1024,128]{1,0:T(8,128)(2,1)S(1)}, bf16[1024,128]{1,0:T(8,128)(2,1)S(1)}, u32[]{:S(2)}, u32[]{:S(2)}) collective-permute-start(bf16[1024,128]{1,0:T(8,128)(2,1)S(1)} %get-tuple-element.37), channel_id=1, source_target_pairs={{9,5},{13,1},{17,29},{21,25},{10,6},{14,2},{18,30},{22,26}} | collective-permute-start | bytes 786440 | tf_op jit(solution)/shard_map/ppermute | solution.py:366
  101.8 11.2 %collective-permute-start.14 = (bf16[5,3,128,128]{3,2,1,0:T(8,128)(2,1)S(1)}, bf16[5,3,128,128]{3,2,1,0:T(8,128)(2,1)S(1)}, u32[]{:S(2)}, u32[]{:S(2)}) collective-permute-start(bf16[5,3,128,128]{3,2,1,0:T(8,128)(2,1)S(1)} %get-tuple-element.33), channel_id=1, source_target_pairs={{1,0},{2,1},{3,2},{5,4},{6,5},{7,6},{9,8},{10,9},{11,10},{13,12},{... | collective-permute-start | bytes 1474568 | tf_op jit(solution)/shard_map/ppermute | solution.py:376
  107.9 6.9 %collective-permute-start.20 = (bf16[3,3,128,128]{3,2,1,0:T(8,128)(2,1)S(1)}, bf16[3,3,128,128]{3,2,1,0:T(8,128)(2,1)S(1)}, u32[]{:S(2)}, u32[]{:S(2)}) collective-permute-start(bf16[3,3,128,128]{3,2,1,0:T(8,128)(2,1)S(1)} %get-tuple-element.39), channel_id=1, source_target_pairs={{0,1},{1,2},{2,3},{4,5},{5,6},{6,7},{8,9},{9,10},{10,11},{12,13},{... | collective-permute-start | bytes 884744 | tf_op jit(solution)/shard_map/ppermute | solution.py:375
  111.1 8.0 %collective-permute-start.21 = (bf16[3,3,128,128]{3,2,1,0:T(8,128)(2,1)S(1)}, bf16[3,3,128,128]{3,2,1,0:T(8,128)(2,1)S(1)}, u32[]{:S(2)}, u32[]{:S(2)}) collective-permute-start(bf16[3,3,128,128]{3,2,1,0:T(8,128)(2,1)S(1)} %get-tuple-element.40), channel_id=1, source_target_pairs={{1,0},{2,1},{3,2},{5,4},{6,5},{7,6},{9,8},{10,9},{11,10},{13,12},{... | collective-permute-start | bytes 884744 | tf_op jit(solution)/shard_map/ppermute | solution.py:376

commit v16 on v14

--- a/solution.py
+++ b/solution.py
@@ -10,6 +10,7 @@
 PACK_VMEM_LIMIT = 60 * 1024 * 1024
 PARAMS = pltpu.CompilerParams(vmem_limit_bytes=VMEM_LIMIT)
 COST = pl.CostEstimate(flops=1024, bytes_accessed=1024, transcendentals=0)
+PICK_COST = pl.CostEstimate(flops=20000000000, bytes_accessed=1024, transcendentals=0)
 ANYWHERE = pl.BlockSpec(memory_space=pl.ANY)
 
 
@@ -397,7 +398,7 @@
         return [(0, grid.panel(grid.lines(z)[1], y, 0), 0, 0, 0)]
 
     early, end_list = pick(grid, early_requests, [(2, cap), (0, 0)], [], [other[:1], half[:1]], (None, 1), (1,),
-                           cost=COST)
+                           cost=PICK_COST)
     end_lists = [move(end_list, [(b, a) for a, b in grid.across(shift, mids)]) for shift in sides]
     tables = [(half[0],), *[((x, 0),) for x in end_lists]]
     end_heads = [move(early, grid.ends(0))]
@@ -436,7 +437,7 @@
                 [(count + 1 + index, row, 2, count + 1 + index, 0) for index in range(count)])
 
     picked = pick(grid, last_requests, [(3, cap)] * count + [(1, 2 * cap)] + [(1, cap)] * count, side_lists,
-                  [far, other[1:], far[1:], *tables], tables=tuple(range(3, 4 + count)), after=[*far_picked, end_heads[0], *[x for ((x, _),) in end_crossed], *[x for ((x, _),) in half_crossed]],
+                  [far, other[1:], far[1:], *tables], tables=tuple(range(3, 4 + count)), after=[*far_picked, far_heads[0], end_heads[0], *[x for ((x, _),) in end_crossed], *[x for ((x, _),) in half_crossed]],
                   cost=COST)
     far_crossed = move_across(picked, mids)
     end_tail = move(picked[count], grid.ends(0), inner)
@@ -445,13 +446,12 @@
     for i in range(count):
         sources += [half_crossed[i], other_crossed[i], end_crossed[i]]
     parts = stage(grid, grid.work_middle, lists, turned, matrix, sources, parts, ())
-    first = exchange(parts)
 
     sources = [other, ((end_heads[0], 2), (end_tail, 1, 0)), far, ((far_heads[0], 2), (end_tail, 1, cap))]
     for i in range(count):
         sources += [far_crossed[i], ((far_heads[1 + i], 2), (far_tails[i], 1))]
-    last = exchange(stage(grid, grid.work_far, lists, turned, matrix, sources, (), first[1:]))
-    return assemble(grid, ((grid.work_near, grid.work_middle), (grid.work_far,)), [first, last])[None, None]
+    parts = stage(grid, grid.work_far, lists, turned, matrix, sources, parts)
+    return assemble(grid, ((grid.work_near, grid.work_middle, grid.work_far),), [exchange(parts)])[None, None]
 
 
 def solution(mesh):

time: 119 us -> 129 us (1.084)
  waiting for transfers between devices: 52.1 us -> 70.4 us
  starting transfers between devices: 38.5 us -> 32.8 us
  Pallas kernels: 25.8 us -> 22.7 us
    ppermute x18, waiting for transfers between devices: 38.3 us -> 59 us  [move(): return lax.ppermute(x, ('blk', 'rows'), perm) if perm else jnp.zeros_like(x)]
    ppermute x2 -> x1, waiting for transfers between devices: 8.8 us -> 4.4 us  [exchange(): lax.ppermute(parts[2], 'rows', [(g + 1, g) for g in range(groups - 1)])]
    ppermute x2 -> x1, starting transfers between devices: 4.34 us -> 1.92 us  [exchange(): lax.ppermute(parts[2], 'rows', [(g + 1, g) for g in range(groups - 1)])]
    ppermute x2 -> x1, starting transfers between devices: 9.26 us -> 7.03 us  [exchange(): lax.ppermute(parts[1], 'rows', [(g, g + 1) for g in range(groups - 1)])]
    ppermute x2 -> x1, waiting for transfers between devices: 5.02 us -> 6.98 us  [exchange(): lax.ppermute(parts[1], 'rows', [(g, g + 1) for g in range(groups - 1)])]
  transfers between devices with their start and end apart: 22 -> 20, of which waited for: 10 -> 9; matrix products, arithmetic and copies ran while one was open for 0% -> 0% of each run, Pallas kernels for 14% -> 12%
where the time goes in v16:
time: 129 us
  waiting for transfers between devices  70.4 us (55%)
  starting transfers between devices  32.8 us (25%)
  Pallas kernels  22.7 us (18%)
  local copies, waits for them, and re-layouts  2.3 us (2%)
    ppermute x18, waiting for transfers between devices, move(): return lax.ppermute(x, ('blk', 'rows'), perm) if perm else jnp.zeros_like(x)  59 us
    ppermute x18, starting transfers between devices, move(): return lax.ppermute(x, ('blk', 'rows'), perm) if perm else jnp.zeros_like(x)  23.8 us
    pallas_call x3, Pallas kernels, stage(): pl.pallas_call(functools.partial(stage_kernel, grid, plan, layout, carrie...  11.3 us
    ppermute x1, starting transfers between devices, exchange(): lax.ppermute(parts[1], 'rows', [(g, g + 1) for g in range(groups - 1)])  7.03 us
    ppermute x1, waiting for transfers between devices, exchange(): lax.ppermute(parts[1], 'rows', [(g, g + 1) for g in range(groups - 1)])  6.98 us
    pallas_call x7, Pallas kernels, pick(): pl.pallas_call(functools.partial(pick_kernel, grid, plan, layout, carry,...  5.93 us
    ppermute x1, waiting for transfers between devices, exchange(): lax.ppermute(parts[2], 'rows', [(g + 1, g) for g in range(groups - 1)])  4.4 us
    pallas_call x1, Pallas kernels, pack(): pl.pallas_call(functools.partial(pack_kernel, grid), grid=(1,), in_specs=...  2.64 us
  transfers between devices with their start and end apart: 20, of which 9 were waited for; matrix products, arithmetic and copies ran while one was open for 0% of the time, Pallas kernels for 12%

profile of v16, /device:TPU:1, one launch (start us, length us, event | category | flops | bytes accessed | tf_op | source)
XLA Modules:
  0.0 128.6 jit_solution(8358102307909296775)
XLA Ops:
  0.0 2.6 %pack_rows.1 = (bf16[4112,128]{1,0:T(8,128)(2,1)}, bf16[2048,128]{1,0:T(8,128)(2,1)}) custom-call(s32[3,1,16]{2,1,0:T(1,128)} %bitcast.26, s32[8,8]{1,0:T(8,128)} %bitcast.14, bf16[16,128,384]{2,1,0:T(8,128)(2,1)} %bitcast.25), custom_call_target="tpu_custom_call" | custom-call | flops 1024 | bytes 1024 | tf_op jit(solution)/shard_map/pack_rows/pallas_call | solution.py:131
  2.6 2.2 %collective-permute-start.2 = (bf16[4112,128]{1,0:T(8,128)(2,1)}, bf16[4112,128]{1,0:T(8,128)(2,1)S(1)}, u32[]{:S(2)}, u32[]{:S(2)}) collective-permute-start(bf16[4112,128]{1,0:T(8,128)(2,1)} %get-tuple-element.23.head.refs_1_.refs_0_), channel_id=1, source_target_pairs={{0,8},{4,12},{16,24},{20,28},{8,0},{12,4},{24,16},{28,20},{1,9},{5... | collective-permute-start | bytes 3158024 | tf_op jit(solution)/shard_map/ppermute | solution.py:367
  4.8 0.7 collective-permute-start
  5.6 0.0 copy-done.5
  5.6 1.3 %collective-permute-start.4 = (s32[8,8]{1,0:T(8,128)S(1)}, s32[8,8]{1,0:T(8,128)S(1)}, u32[]{:S(2)}, u32[]{:S(2)}) collective-permute-start(s32[8,8]{1,0:T(8,128)S(1)} %bitcast.15), channel_id=1, source_target_pairs={{4,0},{0,4},{12,8},{8,12},{20,16},{16,20},{28,24},{24,28},{5,1},{1... | collective-permute-start | bytes 776 | tf_op jit(solution)/shard_map/ppermute | solution.py:367
  6.9 5.7 %collective-permute-start.6 = (bf16[2048,128]{1,0:T(8,128)(2,1)}, bf16[2048,128]{1,0:T(8,128)(2,1)S(1)}, u32[]{:S(2)}, u32[]{:S(2)}) collective-permute-start(bf16[2048,128]{1,0:T(8,128)(2,1)} %get-tuple-element.24.tail.refs_2_.refs_1_), channel_id=1, source_target_pairs={{1,9},{5,13},{17,25},{21,29},{9,1},{13,5},{25,17},{29,21},{2,10},{... | collective-permute-start | bytes 1572872 | tf_op jit(solution)/shard_map/ppermute | solution.py:367
  12.6 0.7 collective-permute-start.1
  13.3 0.0 collective-permute-done.4.refs_0_
  13.3 0.0 copy-start.1
  13.3 1.2 copy-done.1
  14.5 1.0 copy-done.3
  15.5 0.7 pick_rows.8
  16.2 0.3 collective-permute-start.9
  16.5 11.5 %collective-permute-done.2.refs_1_.refs_2_.refs_5_ = bf16[4112,128]{1,0:T(8,128)(2,1)S(1)} collective-permute-done((bf16[4112,128]{1,0:T(8,128)(2,1)}, bf16[4112,128]{1,0:T(8,128)(2,1)S(1)}, u32[]{:S(2)}, u32[]{:S(2)}) %collective-permute-start.2) | collective-permute-done | bytes 1052704 | tf_op jit(solution)/shard_map/ppermute | solution.py:367
  28.0 0.7 collective-permute-start.5
  28.7 0.0 collective-permute-done.refs_0_.refs_1_
  28.8 0.7 pick_rows.7
  29.5 1.3 %collective-permute-start.3 = (bf16[2048,128]{1,0:T(8,128)(2,1)S(1)}, bf16[2048,128]{1,0:T(8,128)(2,1)S(1)}, u32[]{:S(2)}, u32[]{:S(2)}) collective-permute-start(bf16[2048,128]{1,0:T(8,128)(2,1)S(1)} %get-tuple-element.25), channel_id=1, source_target_pairs={{8,0},{12,4},{16,24},{20,28},{9,1},{13,5},{17,25},{21,29},{10,2},{... | collective-permute-start | bytes 1572872 | tf_op jit(solution)/shard_map/ppermute | solution.py:367
  30.8 3.4 %collective-permute-done.6.refs_3_.refs_2_ = bf16[2048,128]{1,0:T(8,128)(2,1)S(1)} collective-permute-done((bf16[2048,128]{1,0:T(8,128)(2,1)}, bf16[2048,128]{1,0:T(8,128)(2,1)S(1)}, u32[]{:S(2)}, u32[]{:S(2)}) %collective-permute-start.6) | collective-permute-done | bytes 524320 | tf_op jit(solution)/shard_map/ppermute | solution.py:367
  34.2 0.7 collective-permute-start.8
  34.8 0.0 collective-permute-done.9.refs_4_.refs_3_
  34.8 0.7 pick_rows.10.refs_3_
  35.5 0.0 copy-start.4
  35.5 1.5 %collective-permute-start.12 = (bf16[3072,128]{1,0:T(8,128)(2,1)S(1)}, bf16[3072,128]{1,0:T(8,128)(2,1)S(1)}, u32[]{:S(2)}, u32[]{:S(2)}) collective-permute-start(bf16[3072,128]{1,0:T(8,128)(2,1)S(1)} %pick_rows.10.refs_3_), channel_id=1, source_target_pairs={{0,4},{4,0},{8,12},{12,8},{16,20},{20,16},{24,28},{28,24},{1,5},{5... | collective-permute-start | bytes 2359304 | tf_op jit(solution)/shard_map/ppermute | solution.py:367
  37.0 0.0 collective-permute-done.1.refs_1_.refs_3_.refs_2_
  37.0 0.0 collective-permute-done.8.refs_2_.refs_6_
  37.0 6.6 %collective-permute-done.3.refs_4_.refs_10_.refs_2_ = bf16[2048,128]{1,0:T(8,128)(2,1)S(1)} collective-permute-done((bf16[2048,128]{1,0:T(8,128)(2,1)S(1)}, bf16[2048,128]{1,0:T(8,128)(2,1)S(1)}, u32[]{:S(2)}, u32[]{:S(2)}) %collective-permute-start.3) | collective-permute-done | bytes 524320 | tf_op jit(solution)/shard_map/ppermute | solution.py:367
  43.6 0.7 pick_rows.11.refs_3_
  44.4 0.0 copy-start
  44.4 0.0 copy-start.2
  44.4 0.0 copy-start.6
  44.4 0.0 copy-start.7
  44.4 1.6 %collective-permute-start.11 = (bf16[3072,128]{1,0:T(8,128)(2,1)S(1)}, bf16[3072,128]{1,0:T(8,128)(2,1)S(1)}, u32[]{:S(2)}, u32[]{:S(2)}) collective-permute-start(bf16[3072,128]{1,0:T(8,128)(2,1)S(1)} %pick_rows.11.refs_3_), channel_id=1, source_target_pairs={{8,4},{12,0},{16,28},{20,24},{9,5},{13,1},{17,29},{21,25},{10,6},{... | collective-permute-start | bytes 2359304 | tf_op jit(solution)/shard_map/ppermute | solution.py:367
  46.0 0.0 copy-done.4
  46.0 0.5 turn_rows.1.turned
  46.5 0.7 collective-permute-start.7
  47.2 0.0 copy-done
  47.2 5.0 %stage_products.3 = (bf16[3,3,128,128]{3,2,1,0:T(8,128)(2,1)S(1)}, bf16[3,3,128,128]{3,2,1,0:T(8,128)(2,1)S(1)}, bf16[3,3,128,128]{3,2,1,0:T(8,128)(2,1)S(1)}) custom-call(s32[8,8]{1,0:T(8,128)S(1)} %bitcast.19, s32[8,8]{1,0:T(8,128)S(1)} %bitcast.16, s32[1,8]{1,0:T(1,128)S(1)} %bitcast.22, bf16[16,384,128]{2,1,0:T(8,128)(2,1)S(1)} %turn_rows.1.turned, ...), custom_call_target="tpu_custom_call" | custom-call | flops 1024 | bytes 1024 | tf_op jit(solution)/shard_map/stage_products/pallas_call | solution.py:302
  52.2 0.0 collective-permute-done.5.refs_0_.refs_1_.refs_4_
  52.2 0.9 pick_rows.9
  53.1 1.3 %collective-permute-start.10 = (bf16[2048,128]{1,0:T(8,128)(2,1)S(1)}, bf16[2048,128]{1,0:T(8,128)(2,1)S(1)}, u32[]{:S(2)}, u32[]{:S(2)}) collective-permute-start(bf16[2048,128]{1,0:T(8,128)(2,1)S(1)} %get-tuple-element.28.refs_7_), channel_id=1, source_target_pairs={{8,0},{12,4},{16,24},{20,28},{9,1},{13,5},{17,25},{21,29},{10,2},{... | collective-permute-start | bytes 1572872 | tf_op jit(solution)/shard_map/ppermute | solution.py:367
  54.4 0.7 pick_rows.13
  55.1 0.7 collective-permute-start.17
  55.8 0.0 collective-permute-done.7.refs_2_.refs_4_.refs_5_
  55.8 15.4 %collective-permute-done.12.refs_12_.refs_0_ = bf16[3072,128]{1,0:T(8,128)(2,1)S(1)} collective-permute-done((bf16[3072,128]{1,0:T(8,128)(2,1)S(1)}, bf16[3072,128]{1,0:T(8,128)(2,1)S(1)}, u32[]{:S(2)}, u32[]{:S(2)}) %collective-permute-start.12) | collective-permute-done | bytes 786464 | tf_op jit(solution)/shard_map/ppermute | solution.py:367
  71.2 0.0 collective-permute-done.11.refs_11_.refs_2_
  71.2 4.8 %collective-permute-done.10.refs_9_.refs_6_ = bf16[2048,128]{1,0:T(8,128)(2,1)S(1)} collective-permute-done((bf16[2048,128]{1,0:T(8,128)(2,1)S(1)}, bf16[2048,128]{1,0:T(8,128)(2,1)S(1)}, u32[]{:S(2)}, u32[]{:S(2)}) %collective-permute-start.10) | collective-permute-done | bytes 524320 | tf_op jit(solution)/shard_map/ppermute | solution.py:367
  75.9 1.5 %pick_rows.12 = (bf16[3072,128]{1,0:T(8,128)(2,1)S(1)}, bf16[2048,128]{1,0:T(8,128)(2,1)S(1)}, bf16[1024,128]{1,0:T(8,128)(2,1)S(1)}) custom-call(s32[8,8]{1,0:T(8,128)S(1)} %collective-permute-done.4.refs_0_, bf16[4112,128]{1,0:T(8,128)(2,1)S(1)} %collective-permute-done.5.refs_0_.refs_1_.refs_4_, ...), custom_call_target="tpu_custom_call" | custom-call | flops 1024 | bytes 1024 | tf_op jit(solution)/shard_map/pick_rows/pallas_call | solution.py:223
  77.5 0.7 collective-permute-start.14
  78.2 1.3 %collective-permute-start.15 = (bf16[2048,128]{1,0:T(8,128)(2,1)S(1)}, bf16[2048,128]{1,0:T(8,128)(2,1)S(1)}, u32[]{:S(2)}, u32[]{:S(2)}) collective-permute-start(bf16[2048,128]{1,0:T(8,128)(2,1)S(1)} %get-tuple-element.29.refs_8_), channel_id=1, source_target_pairs={{8,4},{12,0},{16,28},{20,24},{9,5},{13,1},{17,29},{21,25},{10,6},{... | collective-permute-start | bytes 1572872 | tf_op jit(solution)/shard_map/ppermute | solution.py:367
  79.5 1.3 %collective-permute-start.13 = (bf16[2048,128]{1,0:T(8,128)(2,1)S(1)}, bf16[2048,128]{1,0:T(8,128)(2,1)S(1)}, u32[]{:S(2)}, u32[]{:S(2)}) collective-permute-start(bf16[2048,128]{1,0:T(8,128)(2,1)S(1)} %get-tuple-element.30), channel_id=1, source_target_pairs={{9,1},{13,5},{17,25},{21,29},{10,2},{14,6},{18,26},{22,30}} | collective-permute-start | bytes 1572872 | tf_op jit(solution)/shard_map/ppermute | solution.py:367
  80.8 1.3 %collective-permute-start.16 = (bf16[1024,128]{1,0:T(8,128)(2,1)S(1)}, bf16[1024,128]{1,0:T(8,128)(2,1)S(1)}, u32[]{:S(2)}, u32[]{:S(2)}) collective-permute-start(bf16[1024,128]{1,0:T(8,128)(2,1)S(1)} %get-tuple-element.32), channel_id=1, source_target_pairs={{9,5},{13,1},{17,29},{21,25},{10,6},{14,2},{18,30},{22,26}} | collective-permute-start | bytes 786440 | tf_op jit(solution)/shard_map/ppermute | solution.py:367
  82.1 0.0 collective-permute-done.17.refs_1_
  82.1 3.6 %stage_products.4 = (bf16[5,3,128,128]{3,2,1,0:T(8,128)(2,1)S(1)}, bf16[5,3,128,128]{3,2,1,0:T(8,128)(2,1)S(1)}, bf16[5,3,128,128]{3,2,1,0:T(8,128)(2,1)S(1)}) custom-call(s32[8,8]{1,0:T(8,128)S(1)} %bitcast.20, s32[8,8]{1,0:T(8,128)S(1)} %bitcast.17, s32[1,8]{1,0:T(1,128)S(1)} %bitcast.23, bf16[16,384,128]{2,1,0:T(8,128)(2,1)S(1)} %turn_rows.1.turned, ...), custom_call_target="tpu_custom_call" | custom-call | flops 1024 | bytes 1024 | tf_op jit(solution)/shard_map/stage_products/pallas_call | solution.py:302
  85.7 5.8 %collective-permute-done.15.refs_9_ = bf16[2048,128]{1,0:T(8,128)(2,1)S(1)} collective-permute-done((bf16[2048,128]{1,0:T(8,128)(2,1)S(1)}, bf16[2048,128]{1,0:T(8,128)(2,1)S(1)}, u32[]{:S(2)}, u32[]{:S(2)}) %collective-permute-start.15) | collective-permute-done | bytes 524320 | tf_op jit(solution)/shard_map/ppermute | solution.py:367
  91.5 11.5 %collective-permute-done.16.refs_10_ = bf16[1024,128]{1,0:T(8,128)(2,1)S(1)} collective-permute-done((bf16[1024,128]{1,0:T(8,128)(2,1)S(1)}, bf16[1024,128]{1,0:T(8,128)(2,1)S(1)}, u32[]{:S(2)}, u32[]{:S(2)}) %collective-permute-start.16) | collective-permute-done | bytes 262176 | tf_op jit(solution)/shard_map/ppermute | solution.py:367
  103.1 0.0 collective-permute-done.13.refs_3_.refs_7_
  103.1 0.0 collective-permute-done.14.refs_8_
  103.1 2.8 %stage_products.5 = (bf16[8,3,128,128]{3,2,1,0:T(8,128)(2,1)S(1)}, bf16[8,3,128,128]{3,2,1,0:T(8,128)(2,1)S(1)}, bf16[8,3,128,128]{3,2,1,0:T(8,128)(2,1)S(1)}) custom-call(s32[8,8]{1,0:T(8,128)S(1)} %bitcast.21, s32[8,8]{1,0:T(8,128)S(1)} %bitcast.18, s32[1,8]{1,0:T(1,128)S(1)} %bitcast.24, bf16[16,384,128]{2,1,0:T(8,128)(2,1)S(1)} %turn_rows.1.turned, ...), custom_call_target="tpu_custom_call" | custom-call | flops 1024 | bytes 1024 | tf_op jit(solution)/shard_map/stage_products/pallas_call | solution.py:302
  105.8 7.0 %collective-permute-start.18 = (bf16[8,3,128,128]{3,2,1,0:T(8,128)(2,1)S(1)}, bf16[8,3,128,128]{3,2,1,0:T(8,128)(2,1)S(1)}, u32[]{:S(2)}, u32[]{:S(2)}) collective-permute-start(bf16[8,3,128,128]{3,2,1,0:T(8,128)(2,1)S(1)} %get-tuple-element.39), channel_id=1, source_target_pairs={{0,1},{1,2},{2,3},{4,5},{5,6},{6,7},{8,9},{9,10},{10,11},{12,13},{... | collective-permute-start | bytes 2359304 | tf_op jit(solution)/shard_map/ppermute | solution.py:376
  112.9 1.9 %collective-permute-start.19 = (bf16[8,3,128,128]{3,2,1,0:T(8,128)(2,1)S(1)}, bf16[8,3,128,128]{3,2,1,0:T(8,128)(2,1)S(1)}, u32[]{:S(2)}, u32[]{:S(2)}) collective-permute-start(bf16[8,3,128,128]{3,2,1,0:T(8,128)(2,1)S(1)} %get-tuple-element.40), channel_id=1, source_target_pairs={{1,0},{2,1},{3,2},{5,4},{6,5},{7,6},{9,8},{10,9},{11,10},{13,12},{... | collective-permute-start | bytes 2359304 | tf_op jit(solution)/shard_map/ppermute | solution.py:377
  114.8 7.0 %collective-permute-done.18.refs_1_ = bf16[8,3,128,128]{3,2,1,0:T(8,128)(2,1)S(1)} collective-permute-done((bf16[8,3,128,128]{3,2,1,0:T(8,128)(2,1)S(1)}, bf16[8,3,128,128]{3,2,1,0:T(8,128)(2,1)S(1)}, u32[]{:S(2)}, u32[]{:S(2)}) %collective-permute-start.18) | collective-permute-done | bytes 786464 | tf_op jit(solution)/shard_map/ppermute | solution.py:376
  121.8 4.4 %collective-permute-done.19.refs_2_ = bf16[8,3,128,128]{3,2,1,0:T(8,128)(2,1)S(1)} collective-permute-done((bf16[8,3,128,128]{3,2,1,0:T(8,128)(2,1)S(1)}, bf16[8,3,128,128]{3,2,1,0:T(8,128)(2,1)S(1)}, u32[]{:S(2)}, u32[]{:S(2)}) %collective-permute-start.19) | collective-permute-done | bytes 786464 | tf_op jit(solution)/shard_map/ppermute | solution.py:377
  126.2 2.4 %assemble_coarse.1 = f32[5120,128]{1,0:T(8,128)} custom-call(bf16[8,3,128,128]{3,2,1,0:T(8,128)(2,1)S(1)} %get-tuple-element.38.refs_0_, bf16[8,3,128,128]{3,2,1,0:T(8,128)(2,1)S(1)} %collective-permute-done.18.refs_1_, bf16[8,3,128,128]{3,2,1,0:T(8,128)(2,1)S(1)} %collective-permute-done.19.refs_2_), custom_call_target="tpu_custom_call" | custom-call | flops 1024 | bytes 1024 | tf_op jit(solution)/shard_map/assemble_coarse/pallas_call | solution.py:343
  (5 shorter events, 0.0 us)
Async XLA Ops:
  0.0 5.6 %copy-start.5 = (s32[1,1,8,8]{3,2,1,0:T(8,128)S(1)}, s32[1,1,8,8]{3,2,1,0:T(8,128)}, u32[]{:S(2)}) copy-start(s32[1,1,8,8]{3,2,1,0:T(8,128)} %param.8) | copy-start | bytes 772
  2.6 25.4 %collective-permute-start.2 = (bf16[4112,128]{1,0:T(8,128)(2,1)}, bf16[4112,128]{1,0:T(8,128)(2,1)S(1)}, u32[]{:S(2)}, u32[]{:S(2)}) collective-permute-start(bf16[4112,128]{1,0:T(8,128)(2,1)} %get-tuple-element.23.head.refs_1_.refs_0_), channel_id=1, source_target_pairs={{0,8},{4,12},{16,24},{20,28},{8,0},{12,4},{24,16},{28,20},{1,9},{5... | collective-permute-start | bytes 3158024 | tf_op jit(solution)/shard_map/ppermute | solution.py:367
  4.8 23.9 %collective-permute-start = (bf16[4112,128]{1,0:T(8,128)(2,1)}, bf16[4112,128]{1,0:T(8,128)(2,1)S(1)}, u32[]{:S(2)}, u32[]{:S(2)}) collective-permute-start(bf16[4112,128]{1,0:T(8,128)(2,1)} %get-tuple-element.23.head.refs_1_.refs_0_), channel_id=1, source_target_pairs={{8,16},{12,20},{16,8},{20,12},{9,17},{13,21},{17,9},{21,13},{10,18... | collective-permute-start | bytes 3158024 | tf_op jit(solution)/shard_map/ppermute | solution.py:367
  5.6 7.7 %collective-permute-start.4 = (s32[8,8]{1,0:T(8,128)S(1)}, s32[8,8]{1,0:T(8,128)S(1)}, u32[]{:S(2)}, u32[]{:S(2)}) collective-permute-start(s32[8,8]{1,0:T(8,128)S(1)} %bitcast.15), channel_id=1, source_target_pairs={{4,0},{0,4},{12,8},{8,12},{20,16},{16,20},{28,24},{24,28},{5,1},{1... | collective-permute-start | bytes 776 | tf_op jit(solution)/shard_map/ppermute | solution.py:367
  6.9 27.3 %collective-permute-start.6 = (bf16[2048,128]{1,0:T(8,128)(2,1)}, bf16[2048,128]{1,0:T(8,128)(2,1)S(1)}, u32[]{:S(2)}, u32[]{:S(2)}) collective-permute-start(bf16[2048,128]{1,0:T(8,128)(2,1)} %get-tuple-element.24.tail.refs_2_.refs_1_), channel_id=1, source_target_pairs={{1,9},{5,13},{17,25},{21,29},{9,1},{13,5},{25,17},{29,21},{2,10},{... | collective-permute-start | bytes 1572872 | tf_op jit(solution)/shard_map/ppermute | solution.py:367
  12.6 24.5 %collective-permute-start.1 = (bf16[2048,128]{1,0:T(8,128)(2,1)}, bf16[2048,128]{1,0:T(8,128)(2,1)S(1)}, u32[]{:S(2)}, u32[]{:S(2)}) collective-permute-start(bf16[2048,128]{1,0:T(8,128)(2,1)} %get-tuple-element.24.tail.refs_2_.refs_1_), channel_id=1, source_target_pairs={{9,17},{13,21},{17,9},{21,13},{10,18},{14,22},{18,10},{22,14}} | collective-permute-start | bytes 1572872 | tf_op jit(solution)/shard_map/ppermute | solution.py:367
  13.3 1.2 copy-start.1
  14.5 1.0 copy-start.3
  16.2 18.6 %collective-permute-start.9 = (bf16[3072,128]{1,0:T(8,128)(2,1)S(1)}, bf16[3072,128]{1,0:T(8,128)(2,1)S(1)}, u32[]{:S(2)}, u32[]{:S(2)}) collective-permute-start(bf16[3072,128]{1,0:T(8,128)(2,1)S(1)} %pick_rows.8), channel_id=1, source_target_pairs={{0,4},{4,0},{8,12},{12,8},{16,20},{20,16},{24,28},{28,24},{1,5},{5... | collective-permute-start | bytes 2359304 | tf_op jit(solution)/shard_map/ppermute | solution.py:367
  28.0 24.2 %collective-permute-start.5 = (bf16[4112,128]{1,0:T(8,128)(2,1)S(1)}, bf16[4112,128]{1,0:T(8,128)(2,1)S(1)}, u32[]{:S(2)}, u32[]{:S(2)}) collective-permute-start(bf16[4112,128]{1,0:T(8,128)(2,1)S(1)} %collective-permute-done.2.refs_1_.refs_2_.refs_5_), channel_id=1, source_target_pairs={{8,16},{12,20},{16,8},{20,12},{9,17},{13,21},{17,9},{21,13},{10,18... | collective-permute-start | bytes 3158024 | tf_op jit(solution)/shard_map/ppermute | solution.py:367
  29.5 14.2 %collective-permute-start.3 = (bf16[2048,128]{1,0:T(8,128)(2,1)S(1)}, bf16[2048,128]{1,0:T(8,128)(2,1)S(1)}, u32[]{:S(2)}, u32[]{:S(2)}) collective-permute-start(bf16[2048,128]{1,0:T(8,128)(2,1)S(1)} %get-tuple-element.25), channel_id=1, source_target_pairs={{8,0},{12,4},{16,24},{20,28},{9,1},{13,5},{17,25},{21,29},{10,2},{... | collective-permute-start | bytes 1572872 | tf_op jit(solution)/shard_map/ppermute | solution.py:367
  34.2 2.8 %collective-permute-start.8 = (bf16[16,128]{1,0:T(8,128)(2,1)S(1)}, bf16[16,128]{1,0:T(8,128)(2,1)S(1)}, u32[]{:S(2)}, u32[]{:S(2)}) collective-permute-start(bf16[16,128]{1,0:T(8,128)(2,1)S(1)} %get-tuple-element.26), channel_id=1, source_target_pairs={{12,8},{8,12},{20,16},{16,20},{13,9},{9,13},{21,17},{17,21},{14,10... | collective-permute-start | bytes 12296 | tf_op jit(solution)/shard_map/ppermute | solution.py:367
  35.5 10.5 %copy-start.4 = (bf16[2048,128]{1,0:T(8,128)(2,1)S(1)}, bf16[2048,128]{1,0:T(8,128)(2,1)}, u32[]{:S(2)}) copy-start(bf16[2048,128]{1,0:T(8,128)(2,1)} %get-tuple-element.24.tail.refs_2_.refs_1_) | copy-start | bytes 1572868
  35.5 35.6 %collective-permute-start.12 = (bf16[3072,128]{1,0:T(8,128)(2,1)S(1)}, bf16[3072,128]{1,0:T(8,128)(2,1)S(1)}, u32[]{:S(2)}, u32[]{:S(2)}) collective-permute-start(bf16[3072,128]{1,0:T(8,128)(2,1)S(1)} %pick_rows.10.refs_3_), channel_id=1, source_target_pairs={{0,4},{4,0},{8,12},{12,8},{16,20},{20,16},{24,28},{28,24},{1,5},{5... | collective-permute-start | bytes 2359304 | tf_op jit(solution)/shard_map/ppermute | solution.py:367
  44.4 2.8 %copy-start = (bf16[1,1,8,8,128,128]{5,4,3,2,1,0:T(8,128)(2,1)S(1)}, bf16[1,1,8,8,128,128]{5,4,3,2,1,0:T(8,128)(2,1)}, u32[]{:S(2)}) copy-start(bf16[1,1,8,8,128,128]{5,4,3,2,1,0:T(8,128)(2,1)} %param.6) | copy-start | bytes 6291460
  44.4 2.8 %copy-start.2 = (bf16[4112,128]{1,0:T(8,128)(2,1)S(1)}, bf16[4112,128]{1,0:T(8,128)(2,1)}, u32[]{:S(2)}) copy-start(bf16[4112,128]{1,0:T(8,128)(2,1)} %get-tuple-element.23.head.refs_1_.refs_0_) | copy-start | bytes 3158020
  44.4 2.8 %copy-start.6 = (s32[1,1,8,8]{3,2,1,0:T(8,128)S(1)}, s32[1,1,8,8]{3,2,1,0:T(8,128)}, u32[]{:S(2)}) copy-start(s32[1,1,8,8]{3,2,1,0:T(8,128)} %param.7) | copy-start | bytes 772
  44.4 2.8 %copy-start.7 = (s32[1,1,8]{2,1,0:T(1,128)S(1)}, s32[1,1,8]{2,1,0:T(1,128)}, u32[]{:S(2)}) copy-start(s32[1,1,8]{2,1,0:T(1,128)} %param.9) | copy-start | bytes 100
  44.4 26.7 %collective-permute-start.11 = (bf16[3072,128]{1,0:T(8,128)(2,1)S(1)}, bf16[3072,128]{1,0:T(8,128)(2,1)S(1)}, u32[]{:S(2)}, u32[]{:S(2)}) collective-permute-start(bf16[3072,128]{1,0:T(8,128)(2,1)S(1)} %pick_rows.11.refs_3_), channel_id=1, source_target_pairs={{8,4},{12,0},{16,28},{20,24},{9,5},{13,1},{17,29},{21,25},{10,6},{... | collective-permute-start | bytes 2359304 | tf_op jit(solution)/shard_map/ppermute | solution.py:367
  46.5 9.3 %collective-permute-start.7 = (bf16[2048,128]{1,0:T(8,128)(2,1)S(1)}, bf16[2048,128]{1,0:T(8,128)(2,1)S(1)}, u32[]{:S(2)}, u32[]{:S(2)}) collective-permute-start(bf16[2048,128]{1,0:T(8,128)(2,1)S(1)} %collective-permute-done.6.refs_3_.refs_2_), channel_id=1, source_target_pairs={{9,17},{13,21},{17,9},{21,13},{10,18},{14,22},{18,10},{22,14}} | collective-permute-start | bytes 1572872 | tf_op jit(solution)/shard_map/ppermute | solution.py:367
  53.1 22.8 %collective-permute-start.10 = (bf16[2048,128]{1,0:T(8,128)(2,1)S(1)}, bf16[2048,128]{1,0:T(8,128)(2,1)S(1)}, u32[]{:S(2)}, u32[]{:S(2)}) collective-permute-start(bf16[2048,128]{1,0:T(8,128)(2,1)S(1)} %get-tuple-element.28.refs_7_), channel_id=1, source_target_pairs={{8,0},{12,4},{16,24},{20,28},{9,1},{13,5},{17,25},{21,29},{10,2},{... | collective-permute-start | bytes 1572872 | tf_op jit(solution)/shard_map/ppermute | solution.py:367
  55.1 27.0 %collective-permute-start.17 = (bf16[3072,128]{1,0:T(8,128)(2,1)S(1)}, bf16[3072,128]{1,0:T(8,128)(2,1)S(1)}, u32[]{:S(2)}, u32[]{:S(2)}) collective-permute-start(bf16[3072,128]{1,0:T(8,128)(2,1)S(1)} %pick_rows.13), channel_id=1, source_target_pairs={{8,12},{12,8},{16,20},{20,16},{9,13},{13,9},{17,21},{21,17},{10,14... | collective-permute-start | bytes 2359304 | tf_op jit(solution)/shard_map/ppermute | solution.py:367
  77.5 25.6 %collective-permute-start.14 = (bf16[3072,128]{1,0:T(8,128)(2,1)S(1)}, bf16[3072,128]{1,0:T(8,128)(2,1)S(1)}, u32[]{:S(2)}, u32[]{:S(2)}) collective-permute-start(bf16[3072,128]{1,0:T(8,128)(2,1)S(1)} %get-tuple-element.31), channel_id=1, source_target_pairs={{8,12},{12,8},{16,20},{20,16},{9,13},{13,9},{17,21},{21,17},{10,14... | collective-permute-start | bytes 2359304 | tf_op jit(solution)/shard_map/ppermute | solution.py:367
  78.2 13.4 %collective-permute-start.15 = (bf16[2048,128]{1,0:T(8,128)(2,1)S(1)}, bf16[2048,128]{1,0:T(8,128)(2,1)S(1)}, u32[]{:S(2)}, u32[]{:S(2)}) collective-permute-start(bf16[2048,128]{1,0:T(8,128)(2,1)S(1)} %get-tuple-element.29.refs_8_), channel_id=1, source_target_pairs={{8,4},{12,0},{16,28},{20,24},{9,5},{13,1},{17,29},{21,25},{10,6},{... | collective-permute-start | bytes 1572872 | tf_op jit(solution)/shard_map/ppermute | solution.py:367
  79.5 23.6 %collective-permute-start.13 = (bf16[2048,128]{1,0:T(8,128)(2,1)S(1)}, bf16[2048,128]{1,0:T(8,128)(2,1)S(1)}, u32[]{:S(2)}, u32[]{:S(2)}) collective-permute-start(bf16[2048,128]{1,0:T(8,128)(2,1)S(1)} %get-tuple-element.30), channel_id=1, source_target_pairs={{9,1},{13,5},{17,25},{21,29},{10,2},{14,6},{18,26},{22,30}} | collective-permute-start | bytes 1572872 | tf_op jit(solution)/shard_map/ppermute | solution.py:367
  80.8 22.3 %collective-permute-start.16 = (bf16[1024,128]{1,0:T(8,128)(2,1)S(1)}, bf16[1024,128]{1,0:T(8,128)(2,1)S(1)}, u32[]{:S(2)}, u32[]{:S(2)}) collective-permute-start(bf16[1024,128]{1,0:T(8,128)(2,1)S(1)} %get-tuple-element.32), channel_id=1, source_target_pairs={{9,5},{13,1},{17,29},{21,25},{10,6},{14,2},{18,30},{22,26}} | collective-permute-start | bytes 786440 | tf_op jit(solution)/shard_map/ppermute | solution.py:367
  105.8 16.0 %collective-permute-start.18 = (bf16[8,3,128,128]{3,2,1,0:T(8,128)(2,1)S(1)}, bf16[8,3,128,128]{3,2,1,0:T(8,128)(2,1)S(1)}, u32[]{:S(2)}, u32[]{:S(2)}) collective-permute-start(bf16[8,3,128,128]{3,2,1,0:T(8,128)(2,1)S(1)} %get-tuple-element.39), channel_id=1, source_target_pairs={{0,1},{1,2},{2,3},{4,5},{5,6},{6,7},{8,9},{9,10},{10,11},{12,13},{... | collective-permute-start | bytes 2359304 | tf_op jit(solution)/shard_map/ppermute | solution.py:376
  112.9 13.3 %collective-permute-start.19 = (bf16[8,3,128,128]{3,2,1,0:T(8,128)(2,1)S(1)}, bf16[8,3,128,128]{3,2,1,0:T(8,128)(2,1)S(1)}, u32[]{:S(2)}, u32[]{:S(2)}) collective-permute-start(bf16[8,3,128,128]{3,2,1,0:T(8,128)(2,1)S(1)} %get-tuple-element.40), channel_id=1, source_target_pairs={{1,0},{2,1},{3,2},{5,4},{6,5},{7,6},{9,8},{10,9},{11,10},{13,12},{... | collective-permute-start | bytes 2359304 | tf_op jit(solution)/shard_map/ppermute | solution.py:377

commit v17 on v16

--- a/solution.py
+++ b/solution.py
@@ -445,13 +445,14 @@
     sources = []
     for i in range(count):
         sources += [half_crossed[i], other_crossed[i], end_crossed[i]]
-    parts = stage(grid, grid.work_middle, lists, turned, matrix, sources, parts, ())
+    parts = stage(grid, grid.work_middle, lists, turned, matrix, sources, parts, far_tails)
+    first = exchange(parts)
 
     sources = [other, ((end_heads[0], 2), (end_tail, 1, 0)), far, ((far_heads[0], 2), (end_tail, 1, cap))]
     for i in range(count):
         sources += [far_crossed[i], ((far_heads[1 + i], 2), (far_tails[i], 1))]
-    parts = stage(grid, grid.work_far, lists, turned, matrix, sources, parts)
-    return assemble(grid, ((grid.work_near, grid.work_middle, grid.work_far),), [exchange(parts)])[None, None]
+    last = exchange(stage(grid, grid.work_far, lists, turned, matrix, sources, (), first[1:2]))
+    return assemble(grid, ((grid.work_near, grid.work_middle), (grid.work_far,)), [first, last])[None, None]
 
 
 def solution(mesh):

time: 129 us -> 125 us (0.969)
  waiting for transfers between devices: 70.4 us -> 54.7 us
  starting transfers between devices: 32.8 us -> 44.7 us
    ppermute x18, waiting for transfers between devices: 59 us -> 46.1 us  [move(): return lax.ppermute(x, ('blk', 'rows'), perm) if perm else jnp.zeros_like(x)]
    ppermute x1 -> x2, starting transfers between devices: 7.03 us -> 15.9 us  [exchange(): lax.ppermute(parts[1], 'rows', [(g, g + 1) for g in range(groups - 1)])]
    ppermute x1 -> x2, waiting for transfers between devices: 6.98 us -> 4.21 us  [exchange(): lax.ppermute(parts[1], 'rows', [(g, g + 1) for g in range(groups - 1)])]
    ppermute x1 -> x2, starting transfers between devices: 1.92 us -> 3.84 us  [exchange(): lax.ppermute(parts[2], 'rows', [(g + 1, g) for g in range(groups - 1)])]
    ppermute x1 -> x2, waiting for transfers between devices: 4.4 us -> 4.4 us  [exchange(): lax.ppermute(parts[2], 'rows', [(g + 1, g) for g in range(groups - 1)])]
  transfers between devices with their start and end apart: 20 -> 22, of which waited for: 9 -> 10; matrix products, arithmetic and copies ran while one was open for 0% -> 0% of each run, Pallas kernels for 12% -> 14%
where the time goes in v17:
time: 125 us
  waiting for transfers between devices  54.7 us (44%)
  starting transfers between devices  44.7 us (36%)
  Pallas kernels  23 us (18%)
  local copies, waits for them, and re-layouts  2.3 us (2%)
    ppermute x18, waiting for transfers between devices, move(): return lax.ppermute(x, ('blk', 'rows'), perm) if perm else jnp.zeros_like(x)  46.1 us
    ppermute x18, starting transfers between devices, move(): return lax.ppermute(x, ('blk', 'rows'), perm) if perm else jnp.zeros_like(x)  24.9 us
    ppermute x2, starting transfers between devices, exchange(): lax.ppermute(parts[1], 'rows', [(g, g + 1) for g in range(groups - 1)])  15.9 us
    pallas_call x3, Pallas kernels, stage(): pl.pallas_call(functools.partial(stage_kernel, grid, plan, layout, carrie...  11.5 us
    pallas_call x7, Pallas kernels, pick(): pl.pallas_call(functools.partial(pick_kernel, grid, plan, layout, carry,...  5.92 us
    ppermute x2, waiting for transfers between devices, exchange(): lax.ppermute(parts[2], 'rows', [(g + 1, g) for g in range(groups - 1)])  4.4 us
    ppermute x2, waiting for transfers between devices, exchange(): lax.ppermute(parts[1], 'rows', [(g, g + 1) for g in range(groups - 1)])  4.21 us
    ppermute x2, starting transfers between devices, exchange(): lax.ppermute(parts[2], 'rows', [(g + 1, g) for g in range(groups - 1)])  3.84 us
  transfers between devices with their start and end apart: 22, of which 10 were waited for; matrix products, arithmetic and copies ran while one was open for 0% of the time, Pallas kernels for 14%

profile of v17, /device:TPU:1, one launch (start us, length us, event | category | flops | bytes accessed | tf_op | source)
XLA Modules:
  0.0 125.1 jit_solution(17388288497714132474)
XLA Ops:
  0.0 2.6 %pack_rows.1 = (bf16[4112,128]{1,0:T(8,128)(2,1)}, bf16[2048,128]{1,0:T(8,128)(2,1)}) custom-call(s32[3,1,16]{2,1,0:T(1,128)} %bitcast.26, s32[8,8]{1,0:T(8,128)} %bitcast.14, bf16[16,128,384]{2,1,0:T(8,128)(2,1)} %bitcast.25), custom_call_target="tpu_custom_call" | custom-call | flops 1024 | bytes 1024 | tf_op jit(solution)/shard_map/pack_rows/pallas_call | solution.py:131
  2.6 2.2 %collective-permute-start.1 = (bf16[4112,128]{1,0:T(8,128)(2,1)}, bf16[4112,128]{1,0:T(8,128)(2,1)S(1)}, u32[]{:S(2)}, u32[]{:S(2)}) collective-permute-start(bf16[4112,128]{1,0:T(8,128)(2,1)} %get-tuple-element.23.head.refs_1_.refs_0_), channel_id=1, source_target_pairs={{0,8},{4,12},{16,24},{20,28},{8,0},{12,4},{24,16},{28,20},{1,9},{5... | collective-permute-start | bytes 3158024 | tf_op jit(solution)/shard_map/ppermute | solution.py:367
  4.8 0.7 collective-permute-start.5
  5.6 1.3 %collective-permute-start = (s32[8,8]{1,0:T(8,128)S(1)}, s32[8,8]{1,0:T(8,128)S(1)}, u32[]{:S(2)}, u32[]{:S(2)}) collective-permute-start(s32[8,8]{1,0:T(8,128)S(1)} %bitcast.15), channel_id=1, source_target_pairs={{4,0},{0,4},{12,8},{8,12},{20,16},{16,20},{28,24},{24,28},{5,1},{1... | collective-permute-start | bytes 776 | tf_op jit(solution)/shard_map/ppermute | solution.py:367
  6.9 0.7 collective-permute-start.6
  7.6 6.9 %collective-permute-start.2 = (bf16[2048,128]{1,0:T(8,128)(2,1)}, bf16[2048,128]{1,0:T(8,128)(2,1)S(1)}, u32[]{:S(2)}, u32[]{:S(2)}) collective-permute-start(bf16[2048,128]{1,0:T(8,128)(2,1)} %get-tuple-element.24.tail.refs_2_.refs_1_), channel_id=1, source_target_pairs={{1,9},{5,13},{17,25},{21,29},{9,1},{13,5},{25,17},{29,21},{2,10},{... | collective-permute-start | bytes 1572872 | tf_op jit(solution)/shard_map/ppermute | solution.py:367
  14.5 0.0 collective-permute-done.refs_0_
  14.5 0.0 copy-start.1
  14.5 1.2 copy-done.1
  15.7 1.0 copy-done.3
  16.8 0.7 pick_rows.7
  17.4 0.3 collective-permute-start.3
  17.7 10.3 %collective-permute-done.1.refs_1_.refs_2_.refs_5_ = bf16[4112,128]{1,0:T(8,128)(2,1)S(1)} collective-permute-done((bf16[4112,128]{1,0:T(8,128)(2,1)}, bf16[4112,128]{1,0:T(8,128)(2,1)S(1)}, u32[]{:S(2)}, u32[]{:S(2)}) %collective-permute-start.1) | collective-permute-done | bytes 1052704 | tf_op jit(solution)/shard_map/ppermute | solution.py:367
  28.0 0.7 collective-permute-start.11
  28.7 0.0 collective-permute-done.5.refs_0_.refs_1_
  28.8 0.7 pick_rows.9
  29.5 1.3 %collective-permute-start.8 = (bf16[2048,128]{1,0:T(8,128)(2,1)S(1)}, bf16[2048,128]{1,0:T(8,128)(2,1)S(1)}, u32[]{:S(2)}, u32[]{:S(2)}) collective-permute-start(bf16[2048,128]{1,0:T(8,128)(2,1)S(1)} %get-tuple-element.26), channel_id=1, source_target_pairs={{8,0},{12,4},{16,24},{20,28},{9,1},{13,5},{17,25},{21,29},{10,2},{... | collective-permute-start | bytes 1572872 | tf_op jit(solution)/shard_map/ppermute | solution.py:367
  30.8 3.4 %collective-permute-done.2.refs_2_.refs_3_ = bf16[2048,128]{1,0:T(8,128)(2,1)S(1)} collective-permute-done((bf16[2048,128]{1,0:T(8,128)(2,1)}, bf16[2048,128]{1,0:T(8,128)(2,1)S(1)}, u32[]{:S(2)}, u32[]{:S(2)}) %collective-permute-start.2) | collective-permute-done | bytes 524320 | tf_op jit(solution)/shard_map/ppermute | solution.py:367
  34.2 0.7 collective-permute-start.7
  34.8 0.0 collective-permute-done.3.refs_3_.refs_4_
  34.8 0.7 pick_rows.8.refs_3_
  35.5 0.0 copy-start.2
  35.6 1.5 %collective-permute-start.4 = (bf16[3072,128]{1,0:T(8,128)(2,1)S(1)}, bf16[3072,128]{1,0:T(8,128)(2,1)S(1)}, u32[]{:S(2)}, u32[]{:S(2)}) collective-permute-start(bf16[3072,128]{1,0:T(8,128)(2,1)S(1)} %pick_rows.8.refs_3_), channel_id=1, source_target_pairs={{0,4},{4,0},{8,12},{12,8},{16,20},{20,16},{24,28},{28,24},{1,5},{5... | collective-permute-start | bytes 2359304 | tf_op jit(solution)/shard_map/ppermute | solution.py:367
  37.0 0.0 collective-permute-done.6.refs_1_.refs_2_.refs_3_
  37.0 0.0 collective-permute-done.7.refs_2_.refs_6_
  37.0 6.6 %collective-permute-done.8.refs_4_.refs_10_.refs_2_ = bf16[2048,128]{1,0:T(8,128)(2,1)S(1)} collective-permute-done((bf16[2048,128]{1,0:T(8,128)(2,1)S(1)}, bf16[2048,128]{1,0:T(8,128)(2,1)S(1)}, u32[]{:S(2)}, u32[]{:S(2)}) %collective-permute-start.8) | collective-permute-done | bytes 524320 | tf_op jit(solution)/shard_map/ppermute | solution.py:367
  43.6 0.7 pick_rows.10.refs_3_
  44.4 0.0 copy-start
  44.4 0.0 copy-start.6
  44.4 0.0 copy-start.7
  44.4 1.4 %collective-permute-start.10 = (bf16[3072,128]{1,0:T(8,128)(2,1)S(1)}, bf16[3072,128]{1,0:T(8,128)(2,1)S(1)}, u32[]{:S(2)}, u32[]{:S(2)}) collective-permute-start(bf16[3072,128]{1,0:T(8,128)(2,1)S(1)} %pick_rows.10.refs_3_), channel_id=1, source_target_pairs={{8,4},{12,0},{16,28},{20,24},{9,5},{13,1},{17,29},{21,25},{10,6},{... | collective-permute-start | bytes 2359304 | tf_op jit(solution)/shard_map/ppermute | solution.py:367
  45.9 0.5 turn_rows.1.turned
  46.4 0.7 collective-permute-start.12
  47.1 4.9 %stage_products.3 = (bf16[3,3,128,128]{3,2,1,0:T(8,128)(2,1)S(1)}, bf16[3,3,128,128]{3,2,1,0:T(8,128)(2,1)S(1)}, bf16[3,3,128,128]{3,2,1,0:T(8,128)(2,1)S(1)}) custom-call(s32[8,8]{1,0:T(8,128)S(1)} %bitcast.19, s32[8,8]{1,0:T(8,128)S(1)} %bitcast.16, s32[1,8]{1,0:T(1,128)S(1)} %bitcast.22, bf16[16,384,128]{2,1,0:T(8,128)(2,1)S(1)} %turn_rows.1.turned, ...), custom_call_target="tpu_custom_call" | custom-call | flops 1024 | bytes 1024 | tf_op jit(solution)/shard_map/stage_products/pallas_call | solution.py:302
  52.0 0.0 collective-permute-done.11.refs_0_.refs_1_.refs_4_
  52.0 0.9 pick_rows.12
  52.9 1.3 %collective-permute-start.13 = (bf16[2048,128]{1,0:T(8,128)(2,1)S(1)}, bf16[2048,128]{1,0:T(8,128)(2,1)S(1)}, u32[]{:S(2)}, u32[]{:S(2)}) collective-permute-start(bf16[2048,128]{1,0:T(8,128)(2,1)S(1)} %get-tuple-element.30.refs_7_), channel_id=1, source_target_pairs={{8,0},{12,4},{16,24},{20,28},{9,1},{13,5},{17,25},{21,29},{10,2},{... | collective-permute-start | bytes 1572872 | tf_op jit(solution)/shard_map/ppermute | solution.py:367
  54.2 0.7 pick_rows.11
  54.8 0.7 collective-permute-start.9
  55.6 0.0 collective-permute-done.12.refs_2_.refs_4_.refs_5_
  55.6 15.6 %collective-permute-done.4.refs_12_.refs_0_ = bf16[3072,128]{1,0:T(8,128)(2,1)S(1)} collective-permute-done((bf16[3072,128]{1,0:T(8,128)(2,1)S(1)}, bf16[3072,128]{1,0:T(8,128)(2,1)S(1)}, u32[]{:S(2)}, u32[]{:S(2)}) %collective-permute-start.4) | collective-permute-done | bytes 786464 | tf_op jit(solution)/shard_map/ppermute | solution.py:367
  71.2 0.0 collective-permute-done.10.refs_11_.refs_2_
  71.2 4.7 %collective-permute-done.13.refs_9_.refs_6_ = bf16[2048,128]{1,0:T(8,128)(2,1)S(1)} collective-permute-done((bf16[2048,128]{1,0:T(8,128)(2,1)S(1)}, bf16[2048,128]{1,0:T(8,128)(2,1)S(1)}, u32[]{:S(2)}, u32[]{:S(2)}) %collective-permute-start.13) | collective-permute-done | bytes 524320 | tf_op jit(solution)/shard_map/ppermute | solution.py:367
  75.9 1.5 %pick_rows.13 = (bf16[3072,128]{1,0:T(8,128)(2,1)S(1)}, bf16[2048,128]{1,0:T(8,128)(2,1)S(1)}, bf16[1024,128]{1,0:T(8,128)(2,1)S(1)}) custom-call(s32[8,8]{1,0:T(8,128)S(1)} %collective-permute-done.refs_0_, bf16[4112,128]{1,0:T(8,128)(2,1)S(1)} %collective-permute-done.11.refs_0_.refs_1_.refs_4_, ...), custom_call_target="tpu_custom_call" | custom-call | flops 1024 | bytes 1024 | tf_op jit(solution)/shard_map/pick_rows/pallas_call | solution.py:223
  77.5 0.7 collective-permute-start.18
  78.2 1.3 %collective-permute-start.14 = (bf16[1024,128]{1,0:T(8,128)(2,1)S(1)}, bf16[1024,128]{1,0:T(8,128)(2,1)S(1)}, u32[]{:S(2)}, u32[]{:S(2)}) collective-permute-start(bf16[1024,128]{1,0:T(8,128)(2,1)S(1)} %get-tuple-element.32), channel_id=1, source_target_pairs={{9,5},{13,1},{17,29},{21,25},{10,6},{14,2},{18,30},{22,26}} | collective-permute-start | bytes 786440 | tf_op jit(solution)/shard_map/ppermute | solution.py:367
  79.5 1.3 %collective-permute-start.19 = (bf16[2048,128]{1,0:T(8,128)(2,1)S(1)}, bf16[2048,128]{1,0:T(8,128)(2,1)S(1)}, u32[]{:S(2)}, u32[]{:S(2)}) collective-permute-start(bf16[2048,128]{1,0:T(8,128)(2,1)S(1)} %get-tuple-element.31.refs_8_), channel_id=1, source_target_pairs={{8,4},{12,0},{16,28},{20,24},{9,5},{13,1},{17,29},{21,25},{10,6},{... | collective-permute-start | bytes 1572872 | tf_op jit(solution)/shard_map/ppermute | solution.py:367
  80.8 1.3 %collective-permute-start.17 = (bf16[2048,128]{1,0:T(8,128)(2,1)S(1)}, bf16[2048,128]{1,0:T(8,128)(2,1)S(1)}, u32[]{:S(2)}, u32[]{:S(2)}) collective-permute-start(bf16[2048,128]{1,0:T(8,128)(2,1)S(1)} %get-tuple-element.36), channel_id=1, source_target_pairs={{9,1},{13,5},{17,25},{21,29},{10,2},{14,6},{18,26},{22,30}} | collective-permute-start | bytes 1572872 | tf_op jit(solution)/shard_map/ppermute | solution.py:367
  82.1 0.0 collective-permute-done.9.refs_1_
  82.1 4.1 %collective-permute-done.14.refs_6_.refs_10_ = bf16[1024,128]{1,0:T(8,128)(2,1)S(1)} collective-permute-done((bf16[1024,128]{1,0:T(8,128)(2,1)S(1)}, bf16[1024,128]{1,0:T(8,128)(2,1)S(1)}, u32[]{:S(2)}, u32[]{:S(2)}) %collective-permute-start.14) | collective-permute-done | bytes 262176 | tf_op jit(solution)/shard_map/ppermute | solution.py:367
  86.2 2.2 %stage_products.4 = (bf16[5,3,128,128]{3,2,1,0:T(8,128)(2,1)S(1)}, bf16[5,3,128,128]{3,2,1,0:T(8,128)(2,1)S(1)}, bf16[5,3,128,128]{3,2,1,0:T(8,128)(2,1)S(1)}) custom-call(s32[8,8]{1,0:T(8,128)S(1)} %bitcast.20, s32[8,8]{1,0:T(8,128)S(1)} %bitcast.17, s32[1,8]{1,0:T(1,128)S(1)} %bitcast.23, bf16[16,384,128]{2,1,0:T(8,128)(2,1)S(1)} %turn_rows.1.turned, ...), custom_call_target="tpu_custom_call" | custom-call | flops 1024 | bytes 1024 | tf_op jit(solution)/shard_map/stage_products/pallas_call | solution.py:302
  88.4 11.5 %collective-permute-start.15 = (bf16[5,3,128,128]{3,2,1,0:T(8,128)(2,1)S(1)}, bf16[5,3,128,128]{3,2,1,0:T(8,128)(2,1)S(1)}, u32[]{:S(2)}, u32[]{:S(2)}) collective-permute-start(bf16[5,3,128,128]{3,2,1,0:T(8,128)(2,1)S(1)} %get-tuple-element.34), channel_id=1, source_target_pairs={{0,1},{1,2},{2,3},{4,5},{5,6},{6,7},{8,9},{9,10},{10,11},{12,13},{... | collective-permute-start | bytes 1474568 | tf_op jit(solution)/shard_map/ppermute | solution.py:376
  99.9 1.9 %collective-permute-start.16 = (bf16[5,3,128,128]{3,2,1,0:T(8,128)(2,1)S(1)}, bf16[5,3,128,128]{3,2,1,0:T(8,128)(2,1)S(1)}, u32[]{:S(2)}, u32[]{:S(2)}) collective-permute-start(bf16[5,3,128,128]{3,2,1,0:T(8,128)(2,1)S(1)} %get-tuple-element.35), channel_id=1, source_target_pairs={{1,0},{2,1},{3,2},{5,4},{6,5},{7,6},{9,8},{10,9},{11,10},{13,12},{... | collective-permute-start | bytes 1474568 | tf_op jit(solution)/shard_map/ppermute | solution.py:377
  101.8 0.0 collective-permute-done.19.refs_9_
  101.8 1.3 %collective-permute-done.17.refs_3_.refs_7_ = bf16[2048,128]{1,0:T(8,128)(2,1)S(1)} collective-permute-done((bf16[2048,128]{1,0:T(8,128)(2,1)S(1)}, bf16[2048,128]{1,0:T(8,128)(2,1)S(1)}, u32[]{:S(2)}, u32[]{:S(2)}) %collective-permute-start.17) | collective-permute-done | bytes 524320 | tf_op jit(solution)/shard_map/ppermute | solution.py:367
  103.1 2.5 %collective-permute-done.15.refs_11_.refs_1_ = bf16[5,3,128,128]{3,2,1,0:T(8,128)(2,1)S(1)} collective-permute-done((bf16[5,3,128,128]{3,2,1,0:T(8,128)(2,1)S(1)}, bf16[5,3,128,128]{3,2,1,0:T(8,128)(2,1)S(1)}, u32[]{:S(2)}, u32[]{:S(2)}) %collective-permute-start.15) | collective-permute-done | bytes 491552 | tf_op jit(solution)/shard_map/ppermute | solution.py:376
  105.6 0.0 collective-permute-done.18.refs_8_
  105.6 4.4 %stage_products.5 = (bf16[3,3,128,128]{3,2,1,0:T(8,128)(2,1)S(1)}, bf16[3,3,128,128]{3,2,1,0:T(8,128)(2,1)S(1)}, bf16[3,3,128,128]{3,2,1,0:T(8,128)(2,1)S(1)}) custom-call(s32[8,8]{1,0:T(8,128)S(1)} %bitcast.21, s32[8,8]{1,0:T(8,128)S(1)} %bitcast.18, s32[1,8]{1,0:T(1,128)S(1)} %bitcast.24, bf16[16,384,128]{2,1,0:T(8,128)(2,1)S(1)} %turn_rows.1.turned, ...), custom_call_target="tpu_custom_call" | custom-call | flops 1024 | bytes 1024 | tf_op jit(solution)/shard_map/stage_products/pallas_call | solution.py:302
  110.1 4.5 %collective-permute-start.20 = (bf16[3,3,128,128]{3,2,1,0:T(8,128)(2,1)S(1)}, bf16[3,3,128,128]{3,2,1,0:T(8,128)(2,1)S(1)}, u32[]{:S(2)}, u32[]{:S(2)}) collective-permute-start(bf16[3,3,128,128]{3,2,1,0:T(8,128)(2,1)S(1)} %get-tuple-element.39), channel_id=1, source_target_pairs={{0,1},{1,2},{2,3},{4,5},{5,6},{6,7},{8,9},{9,10},{10,11},{12,13},{... | collective-permute-start | bytes 884744 | tf_op jit(solution)/shard_map/ppermute | solution.py:376
  114.5 1.9 %collective-permute-start.21 = (bf16[3,3,128,128]{3,2,1,0:T(8,128)(2,1)S(1)}, bf16[3,3,128,128]{3,2,1,0:T(8,128)(2,1)S(1)}, u32[]{:S(2)}, u32[]{:S(2)}) collective-permute-start(bf16[3,3,128,128]{3,2,1,0:T(8,128)(2,1)S(1)} %get-tuple-element.40), channel_id=1, source_target_pairs={{1,0},{2,1},{3,2},{5,4},{6,5},{7,6},{9,8},{10,9},{11,10},{13,12},{... | collective-permute-start | bytes 884744 | tf_op jit(solution)/shard_map/ppermute | solution.py:377
  116.5 0.0 collective-permute-done.16.refs_2_
  116.5 1.7 %collective-permute-done.20.refs_4_ = bf16[3,3,128,128]{3,2,1,0:T(8,128)(2,1)S(1)} collective-permute-done((bf16[3,3,128,128]{3,2,1,0:T(8,128)(2,1)S(1)}, bf16[3,3,128,128]{3,2,1,0:T(8,128)(2,1)S(1)}, u32[]{:S(2)}, u32[]{:S(2)}) %collective-permute-start.20) | collective-permute-done | bytes 294944 | tf_op jit(solution)/shard_map/ppermute | solution.py:376
  118.2 4.4 %collective-permute-done.21.refs_5_ = bf16[3,3,128,128]{3,2,1,0:T(8,128)(2,1)S(1)} collective-permute-done((bf16[3,3,128,128]{3,2,1,0:T(8,128)(2,1)S(1)}, bf16[3,3,128,128]{3,2,1,0:T(8,128)(2,1)S(1)}, u32[]{:S(2)}, u32[]{:S(2)}) %collective-permute-start.21) | collective-permute-done | bytes 294944 | tf_op jit(solution)/shard_map/ppermute | solution.py:377
  122.6 2.5 %assemble_coarse.1 = f32[5120,128]{1,0:T(8,128)} custom-call(bf16[5,3,128,128]{3,2,1,0:T(8,128)(2,1)S(1)} %get-tuple-element.33.refs_0_, bf16[5,3,128,128]{3,2,1,0:T(8,128)(2,1)S(1)} %collective-permute-done.15.refs_11_.refs_1_, bf16[5,3,128,128]{3,2,1,0:T(8,128)(2,1)S(1)} %collective-permute-done.16.refs_2_, ...), custom_call_target="tpu_custom_call" | custom-call | flops 1024 | bytes 1024 | tf_op jit(solution)/shard_map/assemble_coarse/pallas_call | solution.py:343
  (9 shorter events, 0.0 us)
Async XLA Ops:
  0.0 5.6 %copy-start.5 = (s32[1,1,8,8]{3,2,1,0:T(8,128)S(1)}, s32[1,1,8,8]{3,2,1,0:T(8,128)}, u32[]{:S(2)}) copy-start(s32[1,1,8,8]{3,2,1,0:T(8,128)} %param.8) | copy-start | bytes 772
  2.6 25.4 %collective-permute-start.1 = (bf16[4112,128]{1,0:T(8,128)(2,1)}, bf16[4112,128]{1,0:T(8,128)(2,1)S(1)}, u32[]{:S(2)}, u32[]{:S(2)}) collective-permute-start(bf16[4112,128]{1,0:T(8,128)(2,1)} %get-tuple-element.23.head.refs_1_.refs_0_), channel_id=1, source_target_pairs={{0,8},{4,12},{16,24},{20,28},{8,0},{12,4},{24,16},{28,20},{1,9},{5... | collective-permute-start | bytes 3158024 | tf_op jit(solution)/shard_map/ppermute | solution.py:367
  4.8 23.9 %collective-permute-start.5 = (bf16[4112,128]{1,0:T(8,128)(2,1)}, bf16[4112,128]{1,0:T(8,128)(2,1)S(1)}, u32[]{:S(2)}, u32[]{:S(2)}) collective-permute-start(bf16[4112,128]{1,0:T(8,128)(2,1)} %get-tuple-element.23.head.refs_1_.refs_0_), channel_id=1, source_target_pairs={{8,16},{12,20},{16,8},{20,12},{9,17},{13,21},{17,9},{21,13},{10,18... | collective-permute-start | bytes 3158024 | tf_op jit(solution)/shard_map/ppermute | solution.py:367
  5.6 8.9 %collective-permute-start = (s32[8,8]{1,0:T(8,128)S(1)}, s32[8,8]{1,0:T(8,128)S(1)}, u32[]{:S(2)}, u32[]{:S(2)}) collective-permute-start(s32[8,8]{1,0:T(8,128)S(1)} %bitcast.15), channel_id=1, source_target_pairs={{4,0},{0,4},{12,8},{8,12},{20,16},{16,20},{28,24},{24,28},{5,1},{1... | collective-permute-start | bytes 776 | tf_op jit(solution)/shard_map/ppermute | solution.py:367
  6.9 30.2 %collective-permute-start.6 = (bf16[2048,128]{1,0:T(8,128)(2,1)}, bf16[2048,128]{1,0:T(8,128)(2,1)S(1)}, u32[]{:S(2)}, u32[]{:S(2)}) collective-permute-start(bf16[2048,128]{1,0:T(8,128)(2,1)} %get-tuple-element.24.tail.refs_2_.refs_1_), channel_id=1, source_target_pairs={{9,17},{13,21},{17,9},{21,13},{10,18},{14,22},{18,10},{22,14}} | collective-permute-start | bytes 1572872 | tf_op jit(solution)/shard_map/ppermute | solution.py:367
  7.6 26.6 %collective-permute-start.2 = (bf16[2048,128]{1,0:T(8,128)(2,1)}, bf16[2048,128]{1,0:T(8,128)(2,1)S(1)}, u32[]{:S(2)}, u32[]{:S(2)}) collective-permute-start(bf16[2048,128]{1,0:T(8,128)(2,1)} %get-tuple-element.24.tail.refs_2_.refs_1_), channel_id=1, source_target_pairs={{1,9},{5,13},{17,25},{21,29},{9,1},{13,5},{25,17},{29,21},{2,10},{... | collective-permute-start | bytes 1572872 | tf_op jit(solution)/shard_map/ppermute | solution.py:367
  14.5 1.2 copy-start.1
  15.7 1.0 copy-start.3
  17.4 17.4 %collective-permute-start.3 = (bf16[3072,128]{1,0:T(8,128)(2,1)S(1)}, bf16[3072,128]{1,0:T(8,128)(2,1)S(1)}, u32[]{:S(2)}, u32[]{:S(2)}) collective-permute-start(bf16[3072,128]{1,0:T(8,128)(2,1)S(1)} %pick_rows.7), channel_id=1, source_target_pairs={{0,4},{4,0},{8,12},{12,8},{16,20},{20,16},{24,28},{28,24},{1,5},{5... | collective-permute-start | bytes 2359304 | tf_op jit(solution)/shard_map/ppermute | solution.py:367
  28.0 23.9 %collective-permute-start.11 = (bf16[4112,128]{1,0:T(8,128)(2,1)S(1)}, bf16[4112,128]{1,0:T(8,128)(2,1)S(1)}, u32[]{:S(2)}, u32[]{:S(2)}) collective-permute-start(bf16[4112,128]{1,0:T(8,128)(2,1)S(1)} %collective-permute-done.1.refs_1_.refs_2_.refs_5_), channel_id=1, source_target_pairs={{8,16},{12,20},{16,8},{20,12},{9,17},{13,21},{17,9},{21,13},{10,18... | collective-permute-start | bytes 3158024 | tf_op jit(solution)/shard_map/ppermute | solution.py:367
  29.5 14.2 %collective-permute-start.8 = (bf16[2048,128]{1,0:T(8,128)(2,1)S(1)}, bf16[2048,128]{1,0:T(8,128)(2,1)S(1)}, u32[]{:S(2)}, u32[]{:S(2)}) collective-permute-start(bf16[2048,128]{1,0:T(8,128)(2,1)S(1)} %get-tuple-element.26), channel_id=1, source_target_pairs={{8,0},{12,4},{16,24},{20,28},{9,1},{13,5},{17,25},{21,29},{10,2},{... | collective-permute-start | bytes 1572872 | tf_op jit(solution)/shard_map/ppermute | solution.py:367
  34.2 2.9 %collective-permute-start.7 = (bf16[16,128]{1,0:T(8,128)(2,1)S(1)}, bf16[16,128]{1,0:T(8,128)(2,1)S(1)}, u32[]{:S(2)}, u32[]{:S(2)}) collective-permute-start(bf16[16,128]{1,0:T(8,128)(2,1)S(1)} %get-tuple-element.25), channel_id=1, source_target_pairs={{12,8},{8,12},{20,16},{16,20},{13,9},{9,13},{21,17},{17,21},{14,10... | collective-permute-start | bytes 12296 | tf_op jit(solution)/shard_map/ppermute | solution.py:367
  35.5 10.3 %copy-start.2 = (bf16[4112,128]{1,0:T(8,128)(2,1)S(1)}, bf16[4112,128]{1,0:T(8,128)(2,1)}, u32[]{:S(2)}) copy-start(bf16[4112,128]{1,0:T(8,128)(2,1)} %get-tuple-element.23.head.refs_1_.refs_0_) | copy-start | bytes 3158020
  35.5 10.3 %copy-start.4 = (bf16[2048,128]{1,0:T(8,128)(2,1)S(1)}, bf16[2048,128]{1,0:T(8,128)(2,1)}, u32[]{:S(2)}) copy-start(bf16[2048,128]{1,0:T(8,128)(2,1)} %get-tuple-element.24.tail.refs_2_.refs_1_) | copy-start | bytes 1572868
  35.6 35.6 %collective-permute-start.4 = (bf16[3072,128]{1,0:T(8,128)(2,1)S(1)}, bf16[3072,128]{1,0:T(8,128)(2,1)S(1)}, u32[]{:S(2)}, u32[]{:S(2)}) collective-permute-start(bf16[3072,128]{1,0:T(8,128)(2,1)S(1)} %pick_rows.8.refs_3_), channel_id=1, source_target_pairs={{0,4},{4,0},{8,12},{12,8},{16,20},{20,16},{24,28},{28,24},{1,5},{5... | collective-permute-start | bytes 2359304 | tf_op jit(solution)/shard_map/ppermute | solution.py:367
  44.4 2.7 %copy-start = (bf16[1,1,8,8,128,128]{5,4,3,2,1,0:T(8,128)(2,1)S(1)}, bf16[1,1,8,8,128,128]{5,4,3,2,1,0:T(8,128)(2,1)}, u32[]{:S(2)}) copy-start(bf16[1,1,8,8,128,128]{5,4,3,2,1,0:T(8,128)(2,1)} %param.6) | copy-start | bytes 6291460
  44.4 2.7 %copy-start.6 = (s32[1,1,8,8]{3,2,1,0:T(8,128)S(1)}, s32[1,1,8,8]{3,2,1,0:T(8,128)}, u32[]{:S(2)}) copy-start(s32[1,1,8,8]{3,2,1,0:T(8,128)} %param.7) | copy-start | bytes 772
  44.4 2.7 %copy-start.7 = (s32[1,1,8]{2,1,0:T(1,128)S(1)}, s32[1,1,8]{2,1,0:T(1,128)}, u32[]{:S(2)}) copy-start(s32[1,1,8]{2,1,0:T(1,128)} %param.9) | copy-start | bytes 100
  44.4 26.8 %collective-permute-start.10 = (bf16[3072,128]{1,0:T(8,128)(2,1)S(1)}, bf16[3072,128]{1,0:T(8,128)(2,1)S(1)}, u32[]{:S(2)}, u32[]{:S(2)}) collective-permute-start(bf16[3072,128]{1,0:T(8,128)(2,1)S(1)} %pick_rows.10.refs_3_), channel_id=1, source_target_pairs={{8,4},{12,0},{16,28},{20,24},{9,5},{13,1},{17,29},{21,25},{10,6},{... | collective-permute-start | bytes 2359304 | tf_op jit(solution)/shard_map/ppermute | solution.py:367
  46.4 9.2 %collective-permute-start.12 = (bf16[2048,128]{1,0:T(8,128)(2,1)S(1)}, bf16[2048,128]{1,0:T(8,128)(2,1)S(1)}, u32[]{:S(2)}, u32[]{:S(2)}) collective-permute-start(bf16[2048,128]{1,0:T(8,128)(2,1)S(1)} %collective-permute-done.2.refs_2_.refs_3_), channel_id=1, source_target_pairs={{9,17},{13,21},{17,9},{21,13},{10,18},{14,22},{18,10},{22,14}} | collective-permute-start | bytes 1572872 | tf_op jit(solution)/shard_map/ppermute | solution.py:367
  52.9 23.1 %collective-permute-start.13 = (bf16[2048,128]{1,0:T(8,128)(2,1)S(1)}, bf16[2048,128]{1,0:T(8,128)(2,1)S(1)}, u32[]{:S(2)}, u32[]{:S(2)}) collective-permute-start(bf16[2048,128]{1,0:T(8,128)(2,1)S(1)} %get-tuple-element.30.refs_7_), channel_id=1, source_target_pairs={{8,0},{12,4},{16,24},{20,28},{9,1},{13,5},{17,25},{21,29},{10,2},{... | collective-permute-start | bytes 1572872 | tf_op jit(solution)/shard_map/ppermute | solution.py:367
  54.8 27.2 %collective-permute-start.9 = (bf16[3072,128]{1,0:T(8,128)(2,1)S(1)}, bf16[3072,128]{1,0:T(8,128)(2,1)S(1)}, u32[]{:S(2)}, u32[]{:S(2)}) collective-permute-start(bf16[3072,128]{1,0:T(8,128)(2,1)S(1)} %pick_rows.11), channel_id=1, source_target_pairs={{8,12},{12,8},{16,20},{20,16},{9,13},{13,9},{17,21},{21,17},{10,14... | collective-permute-start | bytes 2359304 | tf_op jit(solution)/shard_map/ppermute | solution.py:367
  77.5 28.1 %collective-permute-start.18 = (bf16[3072,128]{1,0:T(8,128)(2,1)S(1)}, bf16[3072,128]{1,0:T(8,128)(2,1)S(1)}, u32[]{:S(2)}, u32[]{:S(2)}) collective-permute-start(bf16[3072,128]{1,0:T(8,128)(2,1)S(1)} %get-tuple-element.37), channel_id=1, source_target_pairs={{8,12},{12,8},{16,20},{20,16},{9,13},{13,9},{17,21},{21,17},{10,14... | collective-permute-start | bytes 2359304 | tf_op jit(solution)/shard_map/ppermute | solution.py:367
  78.2 8.0 %collective-permute-start.14 = (bf16[1024,128]{1,0:T(8,128)(2,1)S(1)}, bf16[1024,128]{1,0:T(8,128)(2,1)S(1)}, u32[]{:S(2)}, u32[]{:S(2)}) collective-permute-start(bf16[1024,128]{1,0:T(8,128)(2,1)S(1)} %get-tuple-element.32), channel_id=1, source_target_pairs={{9,5},{13,1},{17,29},{21,25},{10,6},{14,2},{18,30},{22,26}} | collective-permute-start | bytes 786440 | tf_op jit(solution)/shard_map/ppermute | solution.py:367
  79.5 22.3 %collective-permute-start.19 = (bf16[2048,128]{1,0:T(8,128)(2,1)S(1)}, bf16[2048,128]{1,0:T(8,128)(2,1)S(1)}, u32[]{:S(2)}, u32[]{:S(2)}) collective-permute-start(bf16[2048,128]{1,0:T(8,128)(2,1)S(1)} %get-tuple-element.31.refs_8_), channel_id=1, source_target_pairs={{8,4},{12,0},{16,28},{20,24},{9,5},{13,1},{17,29},{21,25},{10,6},{... | collective-permute-start | bytes 1572872 | tf_op jit(solution)/shard_map/ppermute | solution.py:367
  80.8 22.3 %collective-permute-start.17 = (bf16[2048,128]{1,0:T(8,128)(2,1)S(1)}, bf16[2048,128]{1,0:T(8,128)(2,1)S(1)}, u32[]{:S(2)}, u32[]{:S(2)}) collective-permute-start(bf16[2048,128]{1,0:T(8,128)(2,1)S(1)} %get-tuple-element.36), channel_id=1, source_target_pairs={{9,1},{13,5},{17,25},{21,29},{10,2},{14,6},{18,26},{22,30}} | collective-permute-start | bytes 1572872 | tf_op jit(solution)/shard_map/ppermute | solution.py:367
  88.4 17.2 %collective-permute-start.15 = (bf16[5,3,128,128]{3,2,1,0:T(8,128)(2,1)S(1)}, bf16[5,3,128,128]{3,2,1,0:T(8,128)(2,1)S(1)}, u32[]{:S(2)}, u32[]{:S(2)}) collective-permute-start(bf16[5,3,128,128]{3,2,1,0:T(8,128)(2,1)S(1)} %get-tuple-element.34), channel_id=1, source_target_pairs={{0,1},{1,2},{2,3},{4,5},{5,6},{6,7},{8,9},{9,10},{10,11},{12,13},{... | collective-permute-start | bytes 1474568 | tf_op jit(solution)/shard_map/ppermute | solution.py:376
  99.9 16.6 %collective-permute-start.16 = (bf16[5,3,128,128]{3,2,1,0:T(8,128)(2,1)S(1)}, bf16[5,3,128,128]{3,2,1,0:T(8,128)(2,1)S(1)}, u32[]{:S(2)}, u32[]{:S(2)}) collective-permute-start(bf16[5,3,128,128]{3,2,1,0:T(8,128)(2,1)S(1)} %get-tuple-element.35), channel_id=1, source_target_pairs={{1,0},{2,1},{3,2},{5,4},{6,5},{7,6},{9,8},{10,9},{11,10},{13,12},{... | collective-permute-start | bytes 1474568 | tf_op jit(solution)/shard_map/ppermute | solution.py:377
  110.1 8.1 %collective-permute-start.20 = (bf16[3,3,128,128]{3,2,1,0:T(8,128)(2,1)S(1)}, bf16[3,3,128,128]{3,2,1,0:T(8,128)(2,1)S(1)}, u32[]{:S(2)}, u32[]{:S(2)}) collective-permute-start(bf16[3,3,128,128]{3,2,1,0:T(8,128)(2,1)S(1)} %get-tuple-element.39), channel_id=1, source_target_pairs={{0,1},{1,2},{2,3},{4,5},{5,6},{6,7},{8,9},{9,10},{10,11},{12,13},{... | collective-permute-start | bytes 884744 | tf_op jit(solution)/shard_map/ppermute | solution.py:376
  114.5 8.0 %collective-permute-start.21 = (bf16[3,3,128,128]{3,2,1,0:T(8,128)(2,1)S(1)}, bf16[3,3,128,128]{3,2,1,0:T(8,128)(2,1)S(1)}, u32[]{:S(2)}, u32[]{:S(2)}) collective-permute-start(bf16[3,3,128,128]{3,2,1,0:T(8,128)(2,1)S(1)} %get-tuple-element.40), channel_id=1, source_target_pairs={{1,0},{2,1},{3,2},{5,4},{6,5},{7,6},{9,8},{10,9},{11,10},{13,12},{... | collective-permute-start | bytes 884744 | tf_op jit(solution)/shard_map/ppermute | solution.py:377

commit v18 on v15

--- a/solution.py
+++ b/solution.py
@@ -425,7 +425,7 @@
         return [(index, grid.panel(grid.lines(z)[2], y, 0), 0, index, 0) for index in range(columns)]
 
     far_picked = pick(grid, far_requests, [(2, cap)] * columns, [], [far[:1], *tables], tables=tuple(range(1, 2 + count)),
-                      after=[parts[0]], cost=COST)
+                      after=[parts[0], *picked], cost=COST)
     far_heads = [move(x, grid.ends(shift)) for shift, x in enumerate(far_picked)]
 
     def last_requests(z, y):
@@ -444,7 +444,7 @@
     sources = []
     for i in range(count):
         sources += [half_crossed[i], other_crossed[i], end_crossed[i]]
-    parts = stage(grid, grid.work_middle, lists, turned, matrix, sources, parts, far_heads[:1])
+    parts = stage(grid, grid.work_middle, lists, turned, matrix, sources, parts, [*far_heads[:1], *far_tails])
     first = exchange(parts)
 
     sources = [other, ((end_heads[0], 2), (end_tail, 1, 0)), far, ((far_heads[0], 2), (end_tail, 1, cap))]

time: 123 us -> 120 us (0.976)
  waiting for transfers between devices: 56.9 us -> 51.3 us
  starting transfers between devices: 37.3 us -> 39 us
    ppermute x18, waiting for transfers between devices: 50.8 us -> 44.9 us  [move(): return lax.ppermute(x, ('blk', 'rows'), perm) if perm else jnp.zeros_like(x)]
    ppermute x18, starting transfers between devices: 23.4 us -> 24.9 us  [move(): return lax.ppermute(x, ('blk', 'rows'), perm) if perm else jnp.zeros_like(x)]
  transfers between devices with their start and end apart: 22 -> 22, of which waited for: 8 -> 10; matrix products, arithmetic and copies ran while one was open for 0% -> 0% of each run, Pallas kernels for 17% -> 18%
where the time goes in v18:
time: 120 us; the launch traced here: 118 us
  waiting for transfers between devices  51.3 us (43%)
  starting transfers between devices  39 us (32%)
  Pallas kernels  25.8 us (22%)
  local copies, waits for them, and re-layouts  1.26 us (1%)
    ppermute x18, waiting for transfers between devices, move(): return lax.ppermute(x, ('blk', 'rows'), perm) if perm else jnp.zeros_like(x)  44.9 us
    ppermute x18, starting transfers between devices, move(): return lax.ppermute(x, ('blk', 'rows'), perm) if perm else jnp.zeros_like(x)  24.9 us
    pallas_call x3, Pallas kernels, stage(): pl.pallas_call(functools.partial(stage_kernel, grid, plan, layout, carrie...  12.2 us
    ppermute x2, starting transfers between devices, exchange(): lax.ppermute(parts[1], 'rows', [(g, g + 1) for g in range(groups - 1)])  10.3 us
    pallas_call x7, Pallas kernels, pick(): pl.pallas_call(functools.partial(pick_kernel, grid, plan, layout, carry,...  6.93 us
    ppermute x2, waiting for transfers between devices, exchange(): lax.ppermute(parts[2], 'rows', [(g + 1, g) for g in range(groups - 1)])  4.4 us
    ppermute x2, starting transfers between devices, exchange(): lax.ppermute(parts[2], 'rows', [(g + 1, g) for g in range(groups - 1)])  3.84 us
    pallas_call x1, Pallas kernels, pack(): pl.pallas_call(functools.partial(pack_kernel, grid), grid=(1,), in_specs=...  2.64 us
  transfers between devices with their start and end apart: 22, of which 10 were waited for; matrix products, arithmetic and copies ran while one was open for 0% of the time, Pallas kernels for 18%

profile of v18, /device:TPU:1, one launch (start us, length us, event | category | flops | bytes accessed | tf_op | source)
XLA Modules:
  0.0 117.7 jit_solution(18192455902716123535)
XLA Ops:
  0.0 2.6 %pack_rows.1 = (bf16[4112,128]{1,0:T(8,128)(2,1)}, bf16[2048,128]{1,0:T(8,128)(2,1)}) custom-call(s32[3,1,16]{2,1,0:T(1,128)} %bitcast.26, s32[8,8]{1,0:T(8,128)} %bitcast.14, bf16[16,128,384]{2,1,0:T(8,128)(2,1)} %bitcast.25), custom_call_target="tpu_custom_call" | custom-call | flops 1024 | bytes 1024 | tf_op jit(solution)/shard_map/pack_rows/pallas_call | solution.py:130
  2.6 2.2 %collective-permute-start.1 = (bf16[4112,128]{1,0:T(8,128)(2,1)}, bf16[4112,128]{1,0:T(8,128)(2,1)S(1)}, u32[]{:S(2)}, u32[]{:S(2)}) collective-permute-start(bf16[4112,128]{1,0:T(8,128)(2,1)} %get-tuple-element.23.head.refs_1_.refs_0_), channel_id=1, source_target_pairs={{0,8},{4,12},{16,24},{20,28},{8,0},{12,4},{24,16},{28,20},{1,9},{5... | collective-permute-start | bytes 3158024 | tf_op jit(solution)/shard_map/ppermute | solution.py:366
  4.8 0.7 collective-permute-start.5
  5.6 0.0 copy-done.3
  5.6 1.3 %collective-permute-start = (s32[8,8]{1,0:T(8,128)S(1)}, s32[8,8]{1,0:T(8,128)S(1)}, u32[]{:S(2)}, u32[]{:S(2)}) collective-permute-start(s32[8,8]{1,0:T(8,128)S(1)} %bitcast.15), channel_id=1, source_target_pairs={{4,0},{0,4},{12,8},{8,12},{20,16},{16,20},{28,24},{24,28},{5,1},{1... | collective-permute-start | bytes 776 | tf_op jit(solution)/shard_map/ppermute | solution.py:366
  6.9 1.5 %collective-permute-done.refs_0_ = s32[8,8]{1,0:T(8,128)S(1)} collective-permute-done((s32[8,8]{1,0:T(8,128)S(1)}, s32[8,8]{1,0:T(8,128)S(1)}, u32[]{:S(2)}, u32[]{:S(2)}) %collective-permute-start) | collective-permute-done | bytes 288 | tf_op jit(solution)/shard_map/ppermute | solution.py:366
  8.4 1.2 %copy-done.1 = bf16[4112,128]{1,0:T(8,128)(2,1)S(1)} copy-done((bf16[4112,128]{1,0:T(8,128)(2,1)S(1)}, bf16[4112,128]{1,0:T(8,128)(2,1)}, u32[]{:S(2)}) %copy-start.1) | copy-done | bytes 1052696
  9.6 1.7 %pick_rows.7 = bf16[3072,128]{1,0:T(8,128)(2,1)S(1)} custom-call(s32[8,8]{1,0:T(8,128)S(1)} %collective-permute-done.refs_0_, bf16[4112,128]{1,0:T(8,128)(2,1)S(1)} %copy-done.1, bf16[2048,128]{1,0:T(8,128)(2,1)} %get-tuple-element.24.tail.refs_2_.refs_1_), custom_call_target="tpu_custom_call" | custom-call | flops 1024 | bytes 1024 | tf_op jit(solution)/shard_map/pick_rows/pallas_call | solution.py:222
  11.3 1.3 %collective-permute-start.3 = (bf16[3072,128]{1,0:T(8,128)(2,1)S(1)}, bf16[3072,128]{1,0:T(8,128)(2,1)S(1)}, u32[]{:S(2)}, u32[]{:S(2)}) collective-permute-start(bf16[3072,128]{1,0:T(8,128)(2,1)S(1)} %pick_rows.7), channel_id=1, source_target_pairs={{0,4},{4,0},{8,12},{12,8},{16,20},{20,16},{24,28},{28,24},{1,5},{5... | collective-permute-start | bytes 2359304 | tf_op jit(solution)/shard_map/ppermute | solution.py:366
  12.6 5.7 %collective-permute-start.2 = (bf16[2048,128]{1,0:T(8,128)(2,1)}, bf16[2048,128]{1,0:T(8,128)(2,1)S(1)}, u32[]{:S(2)}, u32[]{:S(2)}) collective-permute-start(bf16[2048,128]{1,0:T(8,128)(2,1)} %get-tuple-element.24.tail.refs_2_.refs_1_), channel_id=1, source_target_pairs={{1,9},{5,13},{17,25},{21,29},{9,1},{13,5},{25,17},{29,21},{2,10},{... | collective-permute-start | bytes 1572872 | tf_op jit(solution)/shard_map/ppermute | solution.py:366
  18.3 0.7 collective-permute-start.6
  19.0 9.0 %collective-permute-done.1.refs_1_.refs_2_.refs_5_ = bf16[4112,128]{1,0:T(8,128)(2,1)S(1)} collective-permute-done((bf16[4112,128]{1,0:T(8,128)(2,1)}, bf16[4112,128]{1,0:T(8,128)(2,1)S(1)}, u32[]{:S(2)}, u32[]{:S(2)}) %collective-permute-start.1) | collective-permute-done | bytes 1052704 | tf_op jit(solution)/shard_map/ppermute | solution.py:366
  28.0 0.0 collective-permute-done.5.refs_0_.refs_1_
  28.0 0.7 pick_rows.9
  28.8 1.3 %collective-permute-start.8 = (bf16[2048,128]{1,0:T(8,128)(2,1)S(1)}, bf16[2048,128]{1,0:T(8,128)(2,1)S(1)}, u32[]{:S(2)}, u32[]{:S(2)}) collective-permute-start(bf16[2048,128]{1,0:T(8,128)(2,1)S(1)} %get-tuple-element.26), channel_id=1, source_target_pairs={{8,0},{12,4},{16,24},{20,28},{9,1},{13,5},{17,25},{21,29},{10,2},{... | collective-permute-start | bytes 1572872 | tf_op jit(solution)/shard_map/ppermute | solution.py:366
  30.1 0.7 collective-permute-start.11
  30.8 3.4 %collective-permute-done.2.refs_2_.refs_3_ = bf16[2048,128]{1,0:T(8,128)(2,1)S(1)} collective-permute-done((bf16[2048,128]{1,0:T(8,128)(2,1)}, bf16[2048,128]{1,0:T(8,128)(2,1)S(1)}, u32[]{:S(2)}, u32[]{:S(2)}) %collective-permute-start.2) | collective-permute-done | bytes 524320 | tf_op jit(solution)/shard_map/ppermute | solution.py:366
  34.2 0.7 collective-permute-start.7
  34.8 0.0 collective-permute-done.3.refs_3_.refs_4_
  34.8 0.7 pick_rows.8.refs_3_
  35.5 1.5 %collective-permute-start.4 = (bf16[3072,128]{1,0:T(8,128)(2,1)S(1)}, bf16[3072,128]{1,0:T(8,128)(2,1)S(1)}, u32[]{:S(2)}, u32[]{:S(2)}) collective-permute-start(bf16[3072,128]{1,0:T(8,128)(2,1)S(1)} %pick_rows.8.refs_3_), channel_id=1, source_target_pairs={{0,4},{4,0},{8,12},{12,8},{16,20},{20,16},{24,28},{28,24},{1,5},{5... | collective-permute-start | bytes 2359304 | tf_op jit(solution)/shard_map/ppermute | solution.py:366
  37.0 0.0 collective-permute-done.6.refs_1_.refs_2_.refs_3_
  37.0 0.0 collective-permute-done.7.refs_2_.refs_6_
  37.0 6.7 %collective-permute-done.8.refs_4_.refs_9_.refs_2_ = bf16[2048,128]{1,0:T(8,128)(2,1)S(1)} collective-permute-done((bf16[2048,128]{1,0:T(8,128)(2,1)S(1)}, bf16[2048,128]{1,0:T(8,128)(2,1)S(1)}, u32[]{:S(2)}, u32[]{:S(2)}) %collective-permute-start.8) | collective-permute-done | bytes 524320 | tf_op jit(solution)/shard_map/ppermute | solution.py:366
  43.7 0.7 pick_rows.10.refs_3_
  44.5 0.0 copy-start.2
  44.5 1.4 %collective-permute-start.10 = (bf16[3072,128]{1,0:T(8,128)(2,1)S(1)}, bf16[3072,128]{1,0:T(8,128)(2,1)S(1)}, u32[]{:S(2)}, u32[]{:S(2)}) collective-permute-start(bf16[3072,128]{1,0:T(8,128)(2,1)S(1)} %pick_rows.10.refs_3_), channel_id=1, source_target_pairs={{8,4},{12,0},{16,28},{20,24},{9,5},{13,1},{17,29},{21,25},{10,6},{... | collective-permute-start | bytes 2359304 | tf_op jit(solution)/shard_map/ppermute | solution.py:366
  45.9 0.7 collective-permute-start.13
  46.6 0.7 pick_rows.11.refs_4_
  47.3 0.0 copy-start
  47.3 0.0 copy-start.4
  47.3 0.0 copy-start.5
  47.3 0.8 collective-permute-start.9
  48.2 0.0 copy-done.2
  48.2 1.5 %turn_rows.1.turned = bf16[16,384,128]{2,1,0:T(8,128)(2,1)S(1)} custom-call(bf16[4112,128]{1,0:T(8,128)(2,1)S(1)} %copy-done.2, bf16[2048,128]{1,0:T(8,128)(2,1)} %get-tuple-element.24.tail.refs_2_.refs_1_), custom_call_target="tpu_custom_call" | custom-call | flops 1024 | bytes 1024 | tf_op jit(solution)/shard_map/turn_rows/pallas_call | solution.py:159
  49.7 5.0 %stage_products.3 = (bf16[3,3,128,128]{3,2,1,0:T(8,128)(2,1)S(1)}, bf16[3,3,128,128]{3,2,1,0:T(8,128)(2,1)S(1)}, bf16[3,3,128,128]{3,2,1,0:T(8,128)(2,1)S(1)}) custom-call(s32[8,8]{1,0:T(8,128)S(1)} %bitcast.19, s32[8,8]{1,0:T(8,128)S(1)} %bitcast.16, s32[1,8]{1,0:T(1,128)S(1)} %bitcast.22, bf16[16,384,128]{2,1,0:T(8,128)(2,1)S(1)} %turn_rows.1.turned, ...), custom_call_target="tpu_custom_call" | custom-call | flops 1024 | bytes 1024 | tf_op jit(solution)/shard_map/stage_products/pallas_call | solution.py:301
  54.7 0.0 collective-permute-done.11.refs_0_.refs_1_.refs_4_
  54.7 0.9 pick_rows.12
  55.6 1.3 %collective-permute-start.12 = (bf16[2048,128]{1,0:T(8,128)(2,1)S(1)}, bf16[2048,128]{1,0:T(8,128)(2,1)S(1)}, u32[]{:S(2)}, u32[]{:S(2)}) collective-permute-start(bf16[2048,128]{1,0:T(8,128)(2,1)S(1)} %get-tuple-element.30.refs_7_), channel_id=1, source_target_pairs={{8,0},{12,4},{16,24},{20,28},{9,1},{13,5},{17,25},{21,29},{10,2},{... | collective-permute-start | bytes 1572872 | tf_op jit(solution)/shard_map/ppermute | solution.py:366
  56.9 0.0 collective-permute-done.13.refs_2_.refs_4_.refs_5_
  57.0 14.2 %collective-permute-done.4.refs_11_.refs_0_ = bf16[3072,128]{1,0:T(8,128)(2,1)S(1)} collective-permute-done((bf16[3072,128]{1,0:T(8,128)(2,1)S(1)}, bf16[3072,128]{1,0:T(8,128)(2,1)S(1)}, u32[]{:S(2)}, u32[]{:S(2)}) %collective-permute-start.4) | collective-permute-done | bytes 786464 | tf_op jit(solution)/shard_map/ppermute | solution.py:366
  71.2 0.0 collective-permute-done.10.refs_10_.refs_2_
  71.2 1.5 %pick_rows.13 = (bf16[3072,128]{1,0:T(8,128)(2,1)S(1)}, bf16[2048,128]{1,0:T(8,128)(2,1)S(1)}, bf16[1024,128]{1,0:T(8,128)(2,1)S(1)}) custom-call(s32[8,8]{1,0:T(8,128)S(1)} %collective-permute-done.refs_0_, bf16[4112,128]{1,0:T(8,128)(2,1)S(1)} %collective-permute-done.11.refs_0_.refs_1_.refs_4_, ...), custom_call_target="tpu_custom_call" | custom-call | flops 1024 | bytes 1024 | tf_op jit(solution)/shard_map/pick_rows/pallas_call | solution.py:222
  72.7 0.7 collective-permute-start.18
  73.4 1.3 %collective-permute-start.14 = (bf16[1024,128]{1,0:T(8,128)(2,1)S(1)}, bf16[1024,128]{1,0:T(8,128)(2,1)S(1)}, u32[]{:S(2)}, u32[]{:S(2)}) collective-permute-start(bf16[1024,128]{1,0:T(8,128)(2,1)S(1)} %get-tuple-element.32), channel_id=1, source_target_pairs={{9,5},{13,1},{17,29},{21,25},{10,6},{14,2},{18,30},{22,26}} | collective-permute-start | bytes 786440 | tf_op jit(solution)/shard_map/ppermute | solution.py:366
  74.7 1.3 %collective-permute-start.19 = (bf16[2048,128]{1,0:T(8,128)(2,1)S(1)}, bf16[2048,128]{1,0:T(8,128)(2,1)S(1)}, u32[]{:S(2)}, u32[]{:S(2)}) collective-permute-start(bf16[2048,128]{1,0:T(8,128)(2,1)S(1)} %get-tuple-element.31.refs_8_), channel_id=1, source_target_pairs={{8,4},{12,0},{16,28},{20,24},{9,5},{13,1},{17,29},{21,25},{10,6},{... | collective-permute-start | bytes 1572872 | tf_op jit(solution)/shard_map/ppermute | solution.py:366
  76.0 0.0 collective-permute-done.9.refs_1_
  76.0 1.3 %collective-permute-start.17 = (bf16[2048,128]{1,0:T(8,128)(2,1)S(1)}, bf16[2048,128]{1,0:T(8,128)(2,1)S(1)}, u32[]{:S(2)}, u32[]{:S(2)}) collective-permute-start(bf16[2048,128]{1,0:T(8,128)(2,1)S(1)} %get-tuple-element.36), channel_id=1, source_target_pairs={{9,1},{13,5},{17,25},{21,29},{10,2},{14,6},{18,26},{22,30}} | collective-permute-start | bytes 1572872 | tf_op jit(solution)/shard_map/ppermute | solution.py:366
  77.3 6.5 %collective-permute-done.14.refs_7_.refs_10_ = bf16[1024,128]{1,0:T(8,128)(2,1)S(1)} collective-permute-done((bf16[1024,128]{1,0:T(8,128)(2,1)S(1)}, bf16[1024,128]{1,0:T(8,128)(2,1)S(1)}, u32[]{:S(2)}, u32[]{:S(2)}) %collective-permute-start.14) | collective-permute-done | bytes 262176 | tf_op jit(solution)/shard_map/ppermute | solution.py:366
  83.9 0.0 collective-permute-done.12.refs_6_
  83.9 3.1 %stage_products.4 = (bf16[5,3,128,128]{3,2,1,0:T(8,128)(2,1)S(1)}, bf16[5,3,128,128]{3,2,1,0:T(8,128)(2,1)S(1)}, bf16[5,3,128,128]{3,2,1,0:T(8,128)(2,1)S(1)}) custom-call(s32[8,8]{1,0:T(8,128)S(1)} %bitcast.20, s32[8,8]{1,0:T(8,128)S(1)} %bitcast.17, s32[1,8]{1,0:T(1,128)S(1)} %bitcast.23, bf16[16,384,128]{2,1,0:T(8,128)(2,1)S(1)} %turn_rows.1.turned, ...), custom_call_target="tpu_custom_call" | custom-call | flops 1024 | bytes 1024 | tf_op jit(solution)/shard_map/stage_products/pallas_call | solution.py:301
  87.0 6.4 %collective-permute-start.15 = (bf16[5,3,128,128]{3,2,1,0:T(8,128)(2,1)S(1)}, bf16[5,3,128,128]{3,2,1,0:T(8,128)(2,1)S(1)}, u32[]{:S(2)}, u32[]{:S(2)}) collective-permute-start(bf16[5,3,128,128]{3,2,1,0:T(8,128)(2,1)S(1)} %get-tuple-element.34), channel_id=1, source_target_pairs={{0,1},{1,2},{2,3},{4,5},{5,6},{6,7},{8,9},{9,10},{10,11},{12,13},{... | collective-permute-start | bytes 1474568 | tf_op jit(solution)/shard_map/ppermute | solution.py:375
  93.4 1.9 %collective-permute-start.16 = (bf16[5,3,128,128]{3,2,1,0:T(8,128)(2,1)S(1)}, bf16[5,3,128,128]{3,2,1,0:T(8,128)(2,1)S(1)}, u32[]{:S(2)}, u32[]{:S(2)}) collective-permute-start(bf16[5,3,128,128]{3,2,1,0:T(8,128)(2,1)S(1)} %get-tuple-element.35), channel_id=1, source_target_pairs={{1,0},{2,1},{3,2},{5,4},{6,5},{7,6},{9,8},{10,9},{11,10},{13,12},{... | collective-permute-start | bytes 1474568 | tf_op jit(solution)/shard_map/ppermute | solution.py:376
  95.4 0.0 collective-permute-done.19.refs_9_
  95.4 3.5 %collective-permute-done.17.refs_3_.refs_7_ = bf16[2048,128]{1,0:T(8,128)(2,1)S(1)} collective-permute-done((bf16[2048,128]{1,0:T(8,128)(2,1)S(1)}, bf16[2048,128]{1,0:T(8,128)(2,1)S(1)}, u32[]{:S(2)}, u32[]{:S(2)}) %collective-permute-start.17) | collective-permute-done | bytes 524320 | tf_op jit(solution)/shard_map/ppermute | solution.py:366
  98.8 0.4 collective-permute-done.15.refs_11_.refs_1_
  99.2 0.0 collective-permute-done.18.refs_8_
  99.2 4.1 %stage_products.5 = (bf16[3,3,128,128]{3,2,1,0:T(8,128)(2,1)S(1)}, bf16[3,3,128,128]{3,2,1,0:T(8,128)(2,1)S(1)}, bf16[3,3,128,128]{3,2,1,0:T(8,128)(2,1)S(1)}) custom-call(s32[8,8]{1,0:T(8,128)S(1)} %bitcast.21, s32[8,8]{1,0:T(8,128)S(1)} %bitcast.18, s32[1,8]{1,0:T(1,128)S(1)} %bitcast.24, bf16[16,384,128]{2,1,0:T(8,128)(2,1)S(1)} %turn_rows.1.turned, ...), custom_call_target="tpu_custom_call" | custom-call | flops 1024 | bytes 1024 | tf_op jit(solution)/shard_map/stage_products/pallas_call | solution.py:301
  103.3 3.9 %collective-permute-start.20 = (bf16[3,3,128,128]{3,2,1,0:T(8,128)(2,1)S(1)}, bf16[3,3,128,128]{3,2,1,0:T(8,128)(2,1)S(1)}, u32[]{:S(2)}, u32[]{:S(2)}) collective-permute-start(bf16[3,3,128,128]{3,2,1,0:T(8,128)(2,1)S(1)} %get-tuple-element.39), channel_id=1, source_target_pairs={{0,1},{1,2},{2,3},{4,5},{5,6},{6,7},{8,9},{9,10},{10,11},{12,13},{... | collective-permute-start | bytes 884744 | tf_op jit(solution)/shard_map/ppermute | solution.py:375
  107.2 1.9 %collective-permute-start.21 = (bf16[3,3,128,128]{3,2,1,0:T(8,128)(2,1)S(1)}, bf16[3,3,128,128]{3,2,1,0:T(8,128)(2,1)S(1)}, u32[]{:S(2)}, u32[]{:S(2)}) collective-permute-start(bf16[3,3,128,128]{3,2,1,0:T(8,128)(2,1)S(1)} %get-tuple-element.40), channel_id=1, source_target_pairs={{1,0},{2,1},{3,2},{5,4},{6,5},{7,6},{9,8},{10,9},{11,10},{13,12},{... | collective-permute-start | bytes 884744 | tf_op jit(solution)/shard_map/ppermute | solution.py:376
  109.1 0.0 collective-permute-done.16.refs_2_
  109.2 1.7 %collective-permute-done.20.refs_4_ = bf16[3,3,128,128]{3,2,1,0:T(8,128)(2,1)S(1)} collective-permute-done((bf16[3,3,128,128]{3,2,1,0:T(8,128)(2,1)S(1)}, bf16[3,3,128,128]{3,2,1,0:T(8,128)(2,1)S(1)}, u32[]{:S(2)}, u32[]{:S(2)}) %collective-permute-start.20) | collective-permute-done | bytes 294944 | tf_op jit(solution)/shard_map/ppermute | solution.py:375
  110.9 4.4 %collective-permute-done.21.refs_5_ = bf16[3,3,128,128]{3,2,1,0:T(8,128)(2,1)S(1)} collective-permute-done((bf16[3,3,128,128]{3,2,1,0:T(8,128)(2,1)S(1)}, bf16[3,3,128,128]{3,2,1,0:T(8,128)(2,1)S(1)}, u32[]{:S(2)}, u32[]{:S(2)}) %collective-permute-start.21) | collective-permute-done | bytes 294944 | tf_op jit(solution)/shard_map/ppermute | solution.py:376
  115.3 2.5 %assemble_coarse.1 = f32[5120,128]{1,0:T(8,128)} custom-call(bf16[5,3,128,128]{3,2,1,0:T(8,128)(2,1)S(1)} %get-tuple-element.33.refs_0_, bf16[5,3,128,128]{3,2,1,0:T(8,128)(2,1)S(1)} %collective-permute-done.15.refs_11_.refs_1_, bf16[5,3,128,128]{3,2,1,0:T(8,128)(2,1)S(1)} %collective-permute-done.16.refs_2_, ...), custom_call_target="tpu_custom_call" | custom-call | flops 1024 | bytes 1024 | tf_op jit(solution)/shard_map/assemble_coarse/pallas_call | solution.py:342
  (5 shorter events, 0.0 us)
Async XLA Ops:
  0.0 5.6 %copy-start.3 = (s32[1,1,8,8]{3,2,1,0:T(8,128)S(1)}, s32[1,1,8,8]{3,2,1,0:T(8,128)}, u32[]{:S(2)}) copy-start(s32[1,1,8,8]{3,2,1,0:T(8,128)} %param.8) | copy-start | bytes 772
  2.6 25.4 %collective-permute-start.1 = (bf16[4112,128]{1,0:T(8,128)(2,1)}, bf16[4112,128]{1,0:T(8,128)(2,1)S(1)}, u32[]{:S(2)}, u32[]{:S(2)}) collective-permute-start(bf16[4112,128]{1,0:T(8,128)(2,1)} %get-tuple-element.23.head.refs_1_.refs_0_), channel_id=1, source_target_pairs={{0,8},{4,12},{16,24},{20,28},{8,0},{12,4},{24,16},{28,20},{1,9},{5... | collective-permute-start | bytes 3158024 | tf_op jit(solution)/shard_map/ppermute | solution.py:366
  4.8 23.2 %collective-permute-start.5 = (bf16[4112,128]{1,0:T(8,128)(2,1)}, bf16[4112,128]{1,0:T(8,128)(2,1)S(1)}, u32[]{:S(2)}, u32[]{:S(2)}) collective-permute-start(bf16[4112,128]{1,0:T(8,128)(2,1)} %get-tuple-element.23.head.refs_1_.refs_0_), channel_id=1, source_target_pairs={{8,16},{12,20},{16,8},{20,12},{9,17},{13,21},{17,9},{21,13},{10,18... | collective-permute-start | bytes 3158024 | tf_op jit(solution)/shard_map/ppermute | solution.py:366
  5.6 2.8 %collective-permute-start = (s32[8,8]{1,0:T(8,128)S(1)}, s32[8,8]{1,0:T(8,128)S(1)}, u32[]{:S(2)}, u32[]{:S(2)}) collective-permute-start(s32[8,8]{1,0:T(8,128)S(1)} %bitcast.15), channel_id=1, source_target_pairs={{4,0},{0,4},{12,8},{8,12},{20,16},{16,20},{28,24},{24,28},{5,1},{1... | collective-permute-start | bytes 776 | tf_op jit(solution)/shard_map/ppermute | solution.py:366
  8.4 1.2 %copy-start.1 = (bf16[4112,128]{1,0:T(8,128)(2,1)S(1)}, bf16[4112,128]{1,0:T(8,128)(2,1)}, u32[]{:S(2)}) copy-start(bf16[4112,128]{1,0:T(8,128)(2,1)} %get-tuple-element.23.head.refs_1_.refs_0_) | copy-start | bytes 3158020
  11.3 23.5 %collective-permute-start.3 = (bf16[3072,128]{1,0:T(8,128)(2,1)S(1)}, bf16[3072,128]{1,0:T(8,128)(2,1)S(1)}, u32[]{:S(2)}, u32[]{:S(2)}) collective-permute-start(bf16[3072,128]{1,0:T(8,128)(2,1)S(1)} %pick_rows.7), channel_id=1, source_target_pairs={{0,4},{4,0},{8,12},{12,8},{16,20},{20,16},{24,28},{28,24},{1,5},{5... | collective-permute-start | bytes 2359304 | tf_op jit(solution)/shard_map/ppermute | solution.py:366
  12.6 21.6 %collective-permute-start.2 = (bf16[2048,128]{1,0:T(8,128)(2,1)}, bf16[2048,128]{1,0:T(8,128)(2,1)S(1)}, u32[]{:S(2)}, u32[]{:S(2)}) collective-permute-start(bf16[2048,128]{1,0:T(8,128)(2,1)} %get-tuple-element.24.tail.refs_2_.refs_1_), channel_id=1, source_target_pairs={{1,9},{5,13},{17,25},{21,29},{9,1},{13,5},{25,17},{29,21},{2,10},{... | collective-permute-start | bytes 1572872 | tf_op jit(solution)/shard_map/ppermute | solution.py:366
  18.3 18.7 %collective-permute-start.6 = (bf16[2048,128]{1,0:T(8,128)(2,1)}, bf16[2048,128]{1,0:T(8,128)(2,1)S(1)}, u32[]{:S(2)}, u32[]{:S(2)}) collective-permute-start(bf16[2048,128]{1,0:T(8,128)(2,1)} %get-tuple-element.24.tail.refs_2_.refs_1_), channel_id=1, source_target_pairs={{9,17},{13,21},{17,9},{21,13},{10,18},{14,22},{18,10},{22,14}} | collective-permute-start | bytes 1572872 | tf_op jit(solution)/shard_map/ppermute | solution.py:366
  28.8 15.0 %collective-permute-start.8 = (bf16[2048,128]{1,0:T(8,128)(2,1)S(1)}, bf16[2048,128]{1,0:T(8,128)(2,1)S(1)}, u32[]{:S(2)}, u32[]{:S(2)}) collective-permute-start(bf16[2048,128]{1,0:T(8,128)(2,1)S(1)} %get-tuple-element.26), channel_id=1, source_target_pairs={{8,0},{12,4},{16,24},{20,28},{9,1},{13,5},{17,25},{21,29},{10,2},{... | collective-permute-start | bytes 1572872 | tf_op jit(solution)/shard_map/ppermute | solution.py:366
  30.1 24.7 %collective-permute-start.11 = (bf16[4112,128]{1,0:T(8,128)(2,1)S(1)}, bf16[4112,128]{1,0:T(8,128)(2,1)S(1)}, u32[]{:S(2)}, u32[]{:S(2)}) collective-permute-start(bf16[4112,128]{1,0:T(8,128)(2,1)S(1)} %collective-permute-done.1.refs_1_.refs_2_.refs_5_), channel_id=1, source_target_pairs={{8,16},{12,20},{16,8},{20,12},{9,17},{13,21},{17,9},{21,13},{10,18... | collective-permute-start | bytes 3158024 | tf_op jit(solution)/shard_map/ppermute | solution.py:366
  34.2 2.8 %collective-permute-start.7 = (bf16[16,128]{1,0:T(8,128)(2,1)S(1)}, bf16[16,128]{1,0:T(8,128)(2,1)S(1)}, u32[]{:S(2)}, u32[]{:S(2)}) collective-permute-start(bf16[16,128]{1,0:T(8,128)(2,1)S(1)} %get-tuple-element.25), channel_id=1, source_target_pairs={{12,8},{8,12},{20,16},{16,20},{13,9},{9,13},{21,17},{17,21},{14,10... | collective-permute-start | bytes 12296 | tf_op jit(solution)/shard_map/ppermute | solution.py:366
  35.5 35.6 %collective-permute-start.4 = (bf16[3072,128]{1,0:T(8,128)(2,1)S(1)}, bf16[3072,128]{1,0:T(8,128)(2,1)S(1)}, u32[]{:S(2)}, u32[]{:S(2)}) collective-permute-start(bf16[3072,128]{1,0:T(8,128)(2,1)S(1)} %pick_rows.8.refs_3_), channel_id=1, source_target_pairs={{0,4},{4,0},{8,12},{12,8},{16,20},{20,16},{24,28},{28,24},{1,5},{5... | collective-permute-start | bytes 2359304 | tf_op jit(solution)/shard_map/ppermute | solution.py:366
  44.5 3.7 %copy-start.2 = (bf16[4112,128]{1,0:T(8,128)(2,1)S(1)}, bf16[4112,128]{1,0:T(8,128)(2,1)}, u32[]{:S(2)}) copy-start(bf16[4112,128]{1,0:T(8,128)(2,1)} %get-tuple-element.23.head.refs_1_.refs_0_) | copy-start | bytes 3158020
  44.5 26.7 %collective-permute-start.10 = (bf16[3072,128]{1,0:T(8,128)(2,1)S(1)}, bf16[3072,128]{1,0:T(8,128)(2,1)S(1)}, u32[]{:S(2)}, u32[]{:S(2)}) collective-permute-start(bf16[3072,128]{1,0:T(8,128)(2,1)S(1)} %pick_rows.10.refs_3_), channel_id=1, source_target_pairs={{8,4},{12,0},{16,28},{20,24},{9,5},{13,1},{17,29},{21,25},{10,6},{... | collective-permute-start | bytes 2359304 | tf_op jit(solution)/shard_map/ppermute | solution.py:366
  45.9 11.0 %collective-permute-start.13 = (bf16[2048,128]{1,0:T(8,128)(2,1)S(1)}, bf16[2048,128]{1,0:T(8,128)(2,1)S(1)}, u32[]{:S(2)}, u32[]{:S(2)}) collective-permute-start(bf16[2048,128]{1,0:T(8,128)(2,1)S(1)} %collective-permute-done.2.refs_2_.refs_3_), channel_id=1, source_target_pairs={{9,17},{13,21},{17,9},{21,13},{10,18},{14,22},{18,10},{22,14}} | collective-permute-start | bytes 1572872 | tf_op jit(solution)/shard_map/ppermute | solution.py:366
  47.3 2.4 %copy-start = (bf16[1,1,8,8,128,128]{5,4,3,2,1,0:T(8,128)(2,1)S(1)}, bf16[1,1,8,8,128,128]{5,4,3,2,1,0:T(8,128)(2,1)}, u32[]{:S(2)}) copy-start(bf16[1,1,8,8,128,128]{5,4,3,2,1,0:T(8,128)(2,1)} %param.6) | copy-start | bytes 6291460
  47.3 2.4 %copy-start.4 = (s32[1,1,8,8]{3,2,1,0:T(8,128)S(1)}, s32[1,1,8,8]{3,2,1,0:T(8,128)}, u32[]{:S(2)}) copy-start(s32[1,1,8,8]{3,2,1,0:T(8,128)} %param.7) | copy-start | bytes 772
  47.3 2.4 %copy-start.5 = (s32[1,1,8]{2,1,0:T(1,128)S(1)}, s32[1,1,8]{2,1,0:T(1,128)}, u32[]{:S(2)}) copy-start(s32[1,1,8]{2,1,0:T(1,128)} %param.9) | copy-start | bytes 100
  47.3 28.7 %collective-permute-start.9 = (bf16[3072,128]{1,0:T(8,128)(2,1)S(1)}, bf16[3072,128]{1,0:T(8,128)(2,1)S(1)}, u32[]{:S(2)}, u32[]{:S(2)}) collective-permute-start(bf16[3072,128]{1,0:T(8,128)(2,1)S(1)} %pick_rows.11.refs_4_), channel_id=1, source_target_pairs={{8,12},{12,8},{16,20},{20,16},{9,13},{13,9},{17,21},{21,17},{10,14... | collective-permute-start | bytes 2359304 | tf_op jit(solution)/shard_map/ppermute | solution.py:366
  55.6 28.2 %collective-permute-start.12 = (bf16[2048,128]{1,0:T(8,128)(2,1)S(1)}, bf16[2048,128]{1,0:T(8,128)(2,1)S(1)}, u32[]{:S(2)}, u32[]{:S(2)}) collective-permute-start(bf16[2048,128]{1,0:T(8,128)(2,1)S(1)} %get-tuple-element.30.refs_7_), channel_id=1, source_target_pairs={{8,0},{12,4},{16,24},{20,28},{9,1},{13,5},{17,25},{21,29},{10,2},{... | collective-permute-start | bytes 1572872 | tf_op jit(solution)/shard_map/ppermute | solution.py:366
  72.7 26.5 %collective-permute-start.18 = (bf16[3072,128]{1,0:T(8,128)(2,1)S(1)}, bf16[3072,128]{1,0:T(8,128)(2,1)S(1)}, u32[]{:S(2)}, u32[]{:S(2)}) collective-permute-start(bf16[3072,128]{1,0:T(8,128)(2,1)S(1)} %get-tuple-element.37), channel_id=1, source_target_pairs={{8,12},{12,8},{16,20},{20,16},{9,13},{13,9},{17,21},{21,17},{10,14... | collective-permute-start | bytes 2359304 | tf_op jit(solution)/shard_map/ppermute | solution.py:366
  73.4 10.4 %collective-permute-start.14 = (bf16[1024,128]{1,0:T(8,128)(2,1)S(1)}, bf16[1024,128]{1,0:T(8,128)(2,1)S(1)}, u32[]{:S(2)}, u32[]{:S(2)}) collective-permute-start(bf16[1024,128]{1,0:T(8,128)(2,1)S(1)} %get-tuple-element.32), channel_id=1, source_target_pairs={{9,5},{13,1},{17,29},{21,25},{10,6},{14,2},{18,30},{22,26}} | collective-permute-start | bytes 786440 | tf_op jit(solution)/shard_map/ppermute | solution.py:366
  74.7 20.6 %collective-permute-start.19 = (bf16[2048,128]{1,0:T(8,128)(2,1)S(1)}, bf16[2048,128]{1,0:T(8,128)(2,1)S(1)}, u32[]{:S(2)}, u32[]{:S(2)}) collective-permute-start(bf16[2048,128]{1,0:T(8,128)(2,1)S(1)} %get-tuple-element.31.refs_8_), channel_id=1, source_target_pairs={{8,4},{12,0},{16,28},{20,24},{9,5},{13,1},{17,29},{21,25},{10,6},{... | collective-permute-start | bytes 1572872 | tf_op jit(solution)/shard_map/ppermute | solution.py:366
  76.0 22.8 %collective-permute-start.17 = (bf16[2048,128]{1,0:T(8,128)(2,1)S(1)}, bf16[2048,128]{1,0:T(8,128)(2,1)S(1)}, u32[]{:S(2)}, u32[]{:S(2)}) collective-permute-start(bf16[2048,128]{1,0:T(8,128)(2,1)S(1)} %get-tuple-element.36), channel_id=1, source_target_pairs={{9,1},{13,5},{17,25},{21,29},{10,2},{14,6},{18,26},{22,30}} | collective-permute-start | bytes 1572872 | tf_op jit(solution)/shard_map/ppermute | solution.py:366
  87.0 12.2 %collective-permute-start.15 = (bf16[5,3,128,128]{3,2,1,0:T(8,128)(2,1)S(1)}, bf16[5,3,128,128]{3,2,1,0:T(8,128)(2,1)S(1)}, u32[]{:S(2)}, u32[]{:S(2)}) collective-permute-start(bf16[5,3,128,128]{3,2,1,0:T(8,128)(2,1)S(1)} %get-tuple-element.34), channel_id=1, source_target_pairs={{0,1},{1,2},{2,3},{4,5},{5,6},{6,7},{8,9},{9,10},{10,11},{12,13},{... | collective-permute-start | bytes 1474568 | tf_op jit(solution)/shard_map/ppermute | solution.py:375
  93.4 15.7 %collective-permute-start.16 = (bf16[5,3,128,128]{3,2,1,0:T(8,128)(2,1)S(1)}, bf16[5,3,128,128]{3,2,1,0:T(8,128)(2,1)S(1)}, u32[]{:S(2)}, u32[]{:S(2)}) collective-permute-start(bf16[5,3,128,128]{3,2,1,0:T(8,128)(2,1)S(1)} %get-tuple-element.35), channel_id=1, source_target_pairs={{1,0},{2,1},{3,2},{5,4},{6,5},{7,6},{9,8},{10,9},{11,10},{13,12},{... | collective-permute-start | bytes 1474568 | tf_op jit(solution)/shard_map/ppermute | solution.py:376
  103.3 7.5 %collective-permute-start.20 = (bf16[3,3,128,128]{3,2,1,0:T(8,128)(2,1)S(1)}, bf16[3,3,128,128]{3,2,1,0:T(8,128)(2,1)S(1)}, u32[]{:S(2)}, u32[]{:S(2)}) collective-permute-start(bf16[3,3,128,128]{3,2,1,0:T(8,128)(2,1)S(1)} %get-tuple-element.39), channel_id=1, source_target_pairs={{0,1},{1,2},{2,3},{4,5},{5,6},{6,7},{8,9},{9,10},{10,11},{12,13},{... | collective-permute-start | bytes 884744 | tf_op jit(solution)/shard_map/ppermute | solution.py:375
  107.2 8.0 %collective-permute-start.21 = (bf16[3,3,128,128]{3,2,1,0:T(8,128)(2,1)S(1)}, bf16[3,3,128,128]{3,2,1,0:T(8,128)(2,1)S(1)}, u32[]{:S(2)}, u32[]{:S(2)}) collective-permute-start(bf16[3,3,128,128]{3,2,1,0:T(8,128)(2,1)S(1)} %get-tuple-element.40), channel_id=1, source_target_pairs={{1,0},{2,1},{3,2},{5,4},{6,5},{7,6},{9,8},{10,9},{11,10},{13,12},{... | collective-permute-start | bytes 884744 | tf_op jit(solution)/shard_map/ppermute | solution.py:376

commit v19 on v18

--- a/solution.py
+++ b/solution.py
@@ -241,7 +241,8 @@
         arrays.append([(refs[at + i], k, base) for i, (k, base) in enumerate(blocks)])
         at += len(blocks)
     earlier = refs[at:at + 3] if carried else ()
-    own, up, down, total = refs[-4:]
+    own, up, down, total, values, lefts = refs[-6:]
+    cap = matrix.shape[1]
     width = own.shape[-1]
     first_group = lax.axis_index("rows") == 0
     for old, new in zip(earlier, (own, up, down)):
@@ -250,39 +251,24 @@
                 new[slot, f] = old[slot, f]
     z, y = grid.spot()
     for slot, (panel, sources) in enumerate(plan(z, y), start=carried):
-        total[...] = jnp.zeros_like(total)
-        for array, whole, present in sources:
-            live = slot_counts[0, panel]
-            if present is not True:
-                live = jnp.where(present, live, 0)
-            parts = arrays[array]
-
-            def product(entry, whole=whole, parts=parts, panel=panel):
+        live = 0
+        for _, _, present in sources:
+            live = live + (slot_counts[0, panel] if present is True else jnp.where(present, slot_counts[0, panel], 0))
+        for entry in range(cap):
+            right = None
+            for array, whole, present in sources:
                 pick = slot_cols[panel, entry] if whole else entry
-                right = jnp.concatenate(
-                    [grid.part(x, blocks, base + pick, block)[...] for x, blocks, base in parts for block in range(blocks)],
-                    axis=1)
-                return jnp.dot(matrix[panel, entry], right, preferred_element_type=jnp.float32)
-
-            def add(left, value):
-                result = jnp.dot(left, value, preferred_element_type=jnp.float32)
-                for k in range(3):
-                    total[k] += result[:, k * width:(k + 1) * width]
-
-            def two(u, carry, product=product, panel=panel):
-                first, second = 2 * u, 2 * u + 1
-                left = jnp.concatenate(
-                    [turned[slot_rows[panel, first]], turned[slot_rows[panel, second]]], axis=1)
-                value = jnp.concatenate([product(first), product(second)], axis=0).astype(jnp.bfloat16)
-                add(left, value)
-                return carry
-
-            lax.fori_loop(0, live // 2, two, 0)
-
-            @pl.when(live % 2 == 1)
-            def _(live=live, product=product, panel=panel):
-                add(turned[slot_rows[panel, live - 1]], product(live - 1).astype(jnp.bfloat16))
-
+                part = jnp.concatenate(
+                    [grid.part(x, blocks, base + pick, block)[...]
+                     for x, blocks, base in arrays[array] for block in range(blocks)], axis=1)
+                right = part if right is None else jnp.where(present, part, right)
+            product = jnp.dot(matrix[panel, entry], right, preferred_element_type=jnp.float32)
+            place = slice(entry * grid.pores, (entry + 1) * grid.pores)
+            values[place, :] = jnp.where(entry < live, product, 0.0).astype(values.dtype)
+            lefts[:, place] = turned[slot_rows[panel, entry]]
+        result = jnp.dot(lefts[...], values[...], preferred_element_type=jnp.float32)
+        for k in range(3):
+            total[k] = result[:, k * width:(k + 1) * width]
         begin = jnp.where(first_group, 0, width)
         for f in range(3):
             k = jnp.where(first_group, (f + 2) % 3, f)
@@ -305,7 +291,11 @@
             grid=(1,),
             in_specs=[*map(resident, (turned, matrix, *flat, *earlier)), *([ANYWHERE] * len(after))],
             out_specs=[resident(out)] * 3,
-            scratch_shapes=[pltpu.VMEM((3, 3 * width, width), jnp.float32)],
+            scratch_shapes=[
+                pltpu.VMEM((3, 3 * width, width), jnp.float32),
+                pltpu.VMEM((matrix.shape[1] * grid.pores, 3 * width), jnp.bfloat16),
+                pltpu.VMEM((3 * width, matrix.shape[1] * grid.pores), jnp.bfloat16),
+            ],
         ),
         out_shape=[out] * 3,
         compiler_params=PARAMS,

time: 120 us -> 118 us (0.983); the launches traced: 118 us -> 118 us
  Pallas kernels: 25.8 us -> 23.7 us
  starting transfers between devices: 39 us -> 40.3 us
    pallas_call x3, Pallas kernels: 12.2 us -> 10.1 us  [stage(): pl.pallas_call(functools.partial(stage_kernel, grid, plan, layout, carrie...]
    ppermute x2, starting transfers between devices: 10.3 us -> 11.6 us  [exchange(): lax.ppermute(parts[1], 'rows', [(g, g + 1) for g in range(groups - 1)])]
  transfers between devices with their start and end apart: 22 -> 22, of which waited for: 10 -> 10; matrix products, arithmetic and copies ran while one was open for 0% -> 0% of each run, Pallas kernels for 18% -> 16%
where the time goes in v19:
time: 118 us
  waiting for transfers between devices  52 us (44%)
  starting transfers between devices  40.3 us (34%)
  Pallas kernels  23.7 us (20%)
  local copies, waits for them, and re-layouts  1.26 us (1%)
    ppermute x18, waiting for transfers between devices, move(): return lax.ppermute(x, ('blk', 'rows'), perm) if perm else jnp.zeros_like(x)  45.4 us
    ppermute x18, starting transfers between devices, move(): return lax.ppermute(x, ('blk', 'rows'), perm) if perm else jnp.zeros_like(x)  24.9 us
    ppermute x2, starting transfers between devices, exchange(): lax.ppermute(parts[1], 'rows', [(g, g + 1) for g in range(groups - 1)])  11.6 us
    pallas_call x3, Pallas kernels, stage(): pl.pallas_call(functools.partial(stage_kernel, grid, plan, layout, carrie...  10.1 us
    pallas_call x7, Pallas kernels, pick(): pl.pallas_call(functools.partial(pick_kernel, grid, plan, layout, carry,...  6.93 us
    ppermute x2, waiting for transfers between devices, exchange(): lax.ppermute(parts[2], 'rows', [(g + 1, g) for g in range(groups - 1)])  4.4 us
    ppermute x2, starting transfers between devices, exchange(): lax.ppermute(parts[2], 'rows', [(g + 1, g) for g in range(groups - 1)])  3.84 us
    pallas_call x1, Pallas kernels, pack(): pl.pallas_call(functools.partial(pack_kernel, grid), grid=(1,), in_specs=...  2.64 us
  transfers between devices with their start and end apart: 22, of which 10 were waited for; matrix products, arithmetic and copies ran while one was open for 0% of the time, Pallas kernels for 16%

profile of v19, /device:TPU:1, one launch (start us, length us, event | category | flops | bytes accessed | tf_op | source)
XLA Modules:
  0.0 117.6 jit_solution(5246681823428970830)
XLA Ops:
  0.0 2.6 %pack_rows.1 = (bf16[4112,128]{1,0:T(8,128)(2,1)}, bf16[2048,128]{1,0:T(8,128)(2,1)}) custom-call(s32[3,1,16]{2,1,0:T(1,128)} %bitcast.26, s32[8,8]{1,0:T(8,128)} %bitcast.14, bf16[16,128,384]{2,1,0:T(8,128)(2,1)} %bitcast.25), custom_call_target="tpu_custom_call" | custom-call | flops 1024 | bytes 1024 | tf_op jit(solution)/shard_map/pack_rows/pallas_call | solution.py:130
  2.6 2.2 %collective-permute-start.1 = (bf16[4112,128]{1,0:T(8,128)(2,1)}, bf16[4112,128]{1,0:T(8,128)(2,1)S(1)}, u32[]{:S(2)}, u32[]{:S(2)}) collective-permute-start(bf16[4112,128]{1,0:T(8,128)(2,1)} %get-tuple-element.23.head.refs_1_.refs_0_), channel_id=1, source_target_pairs={{0,8},{4,12},{16,24},{20,28},{8,0},{12,4},{24,16},{28,20},{1,9},{5... | collective-permute-start | bytes 3158024 | tf_op jit(solution)/shard_map/ppermute | solution.py:356
  4.8 0.7 collective-permute-start.5
  5.6 0.0 copy-done.3
  5.6 1.3 %collective-permute-start = (s32[8,8]{1,0:T(8,128)S(1)}, s32[8,8]{1,0:T(8,128)S(1)}, u32[]{:S(2)}, u32[]{:S(2)}) collective-permute-start(s32[8,8]{1,0:T(8,128)S(1)} %bitcast.15), channel_id=1, source_target_pairs={{4,0},{0,4},{12,8},{8,12},{20,16},{16,20},{28,24},{24,28},{5,1},{1... | collective-permute-start | bytes 776 | tf_op jit(solution)/shard_map/ppermute | solution.py:356
  6.9 1.5 %collective-permute-done.refs_0_ = s32[8,8]{1,0:T(8,128)S(1)} collective-permute-done((s32[8,8]{1,0:T(8,128)S(1)}, s32[8,8]{1,0:T(8,128)S(1)}, u32[]{:S(2)}, u32[]{:S(2)}) %collective-permute-start) | collective-permute-done | bytes 288 | tf_op jit(solution)/shard_map/ppermute | solution.py:356
  8.4 1.2 %copy-done.1 = bf16[4112,128]{1,0:T(8,128)(2,1)S(1)} copy-done((bf16[4112,128]{1,0:T(8,128)(2,1)S(1)}, bf16[4112,128]{1,0:T(8,128)(2,1)}, u32[]{:S(2)}) %copy-start.1) | copy-done | bytes 1052696
  9.6 1.7 %pick_rows.7 = bf16[3072,128]{1,0:T(8,128)(2,1)S(1)} custom-call(s32[8,8]{1,0:T(8,128)S(1)} %collective-permute-done.refs_0_, bf16[4112,128]{1,0:T(8,128)(2,1)S(1)} %copy-done.1, bf16[2048,128]{1,0:T(8,128)(2,1)} %get-tuple-element.24.tail.refs_2_.refs_1_), custom_call_target="tpu_custom_call" | custom-call | flops 1024 | bytes 1024 | tf_op jit(solution)/shard_map/pick_rows/pallas_call | solution.py:222
  11.3 1.3 %collective-permute-start.3 = (bf16[3072,128]{1,0:T(8,128)(2,1)S(1)}, bf16[3072,128]{1,0:T(8,128)(2,1)S(1)}, u32[]{:S(2)}, u32[]{:S(2)}) collective-permute-start(bf16[3072,128]{1,0:T(8,128)(2,1)S(1)} %pick_rows.7), channel_id=1, source_target_pairs={{0,4},{4,0},{8,12},{12,8},{16,20},{20,16},{24,28},{28,24},{1,5},{5... | collective-permute-start | bytes 2359304 | tf_op jit(solution)/shard_map/ppermute | solution.py:356
  12.6 5.7 %collective-permute-start.2 = (bf16[2048,128]{1,0:T(8,128)(2,1)}, bf16[2048,128]{1,0:T(8,128)(2,1)S(1)}, u32[]{:S(2)}, u32[]{:S(2)}) collective-permute-start(bf16[2048,128]{1,0:T(8,128)(2,1)} %get-tuple-element.24.tail.refs_2_.refs_1_), channel_id=1, source_target_pairs={{1,9},{5,13},{17,25},{21,29},{9,1},{13,5},{25,17},{29,21},{2,10},{... | collective-permute-start | bytes 1572872 | tf_op jit(solution)/shard_map/ppermute | solution.py:356
  18.3 0.7 collective-permute-start.6
  19.0 9.0 %collective-permute-done.1.refs_1_.refs_2_.refs_5_ = bf16[4112,128]{1,0:T(8,128)(2,1)S(1)} collective-permute-done((bf16[4112,128]{1,0:T(8,128)(2,1)}, bf16[4112,128]{1,0:T(8,128)(2,1)S(1)}, u32[]{:S(2)}, u32[]{:S(2)}) %collective-permute-start.1) | collective-permute-done | bytes 1052704 | tf_op jit(solution)/shard_map/ppermute | solution.py:356
  28.0 0.0 collective-permute-done.5.refs_0_.refs_1_
  28.0 0.7 pick_rows.9
  28.8 1.3 %collective-permute-start.8 = (bf16[2048,128]{1,0:T(8,128)(2,1)S(1)}, bf16[2048,128]{1,0:T(8,128)(2,1)S(1)}, u32[]{:S(2)}, u32[]{:S(2)}) collective-permute-start(bf16[2048,128]{1,0:T(8,128)(2,1)S(1)} %get-tuple-element.26), channel_id=1, source_target_pairs={{8,0},{12,4},{16,24},{20,28},{9,1},{13,5},{17,25},{21,29},{10,2},{... | collective-permute-start | bytes 1572872 | tf_op jit(solution)/shard_map/ppermute | solution.py:356
  30.1 0.7 collective-permute-start.11
  30.8 3.4 %collective-permute-done.2.refs_2_.refs_3_ = bf16[2048,128]{1,0:T(8,128)(2,1)S(1)} collective-permute-done((bf16[2048,128]{1,0:T(8,128)(2,1)}, bf16[2048,128]{1,0:T(8,128)(2,1)S(1)}, u32[]{:S(2)}, u32[]{:S(2)}) %collective-permute-start.2) | collective-permute-done | bytes 524320 | tf_op jit(solution)/shard_map/ppermute | solution.py:356
  34.2 0.7 collective-permute-start.7
  34.8 0.0 collective-permute-done.3.refs_3_.refs_4_
  34.8 0.7 pick_rows.8.refs_3_
  35.5 1.5 %collective-permute-start.4 = (bf16[3072,128]{1,0:T(8,128)(2,1)S(1)}, bf16[3072,128]{1,0:T(8,128)(2,1)S(1)}, u32[]{:S(2)}, u32[]{:S(2)}) collective-permute-start(bf16[3072,128]{1,0:T(8,128)(2,1)S(1)} %pick_rows.8.refs_3_), channel_id=1, source_target_pairs={{0,4},{4,0},{8,12},{12,8},{16,20},{20,16},{24,28},{28,24},{1,5},{5... | collective-permute-start | bytes 2359304 | tf_op jit(solution)/shard_map/ppermute | solution.py:356
  37.0 0.0 collective-permute-done.6.refs_1_.refs_2_.refs_3_
  37.0 0.0 collective-permute-done.7.refs_2_.refs_6_
  37.0 6.7 %collective-permute-done.8.refs_4_.refs_9_.refs_2_ = bf16[2048,128]{1,0:T(8,128)(2,1)S(1)} collective-permute-done((bf16[2048,128]{1,0:T(8,128)(2,1)S(1)}, bf16[2048,128]{1,0:T(8,128)(2,1)S(1)}, u32[]{:S(2)}, u32[]{:S(2)}) %collective-permute-start.8) | collective-permute-done | bytes 524320 | tf_op jit(solution)/shard_map/ppermute | solution.py:356
  43.7 0.7 pick_rows.10.refs_3_
  44.5 0.0 copy-start.2
  44.5 1.4 %collective-permute-start.10 = (bf16[3072,128]{1,0:T(8,128)(2,1)S(1)}, bf16[3072,128]{1,0:T(8,128)(2,1)S(1)}, u32[]{:S(2)}, u32[]{:S(2)}) collective-permute-start(bf16[3072,128]{1,0:T(8,128)(2,1)S(1)} %pick_rows.10.refs_3_), channel_id=1, source_target_pairs={{8,4},{12,0},{16,28},{20,24},{9,5},{13,1},{17,29},{21,25},{10,6},{... | collective-permute-start | bytes 2359304 | tf_op jit(solution)/shard_map/ppermute | solution.py:356
  45.9 0.7 collective-permute-start.13
  46.6 0.7 pick_rows.11.refs_4_
  47.3 0.0 copy-start
  47.3 0.0 copy-start.4
  47.3 0.0 copy-start.5
  47.3 0.8 collective-permute-start.9
  48.2 0.0 copy-done.2
  48.2 1.5 %turn_rows.1.turned = bf16[16,384,128]{2,1,0:T(8,128)(2,1)S(1)} custom-call(bf16[4112,128]{1,0:T(8,128)(2,1)S(1)} %copy-done.2, bf16[2048,128]{1,0:T(8,128)(2,1)} %get-tuple-element.24.tail.refs_2_.refs_1_), custom_call_target="tpu_custom_call" | custom-call | flops 1024 | bytes 1024 | tf_op jit(solution)/shard_map/turn_rows/pallas_call | solution.py:159
  49.7 4.3 %stage_products.3 = (bf16[3,3,128,128]{3,2,1,0:T(8,128)(2,1)S(1)}, bf16[3,3,128,128]{3,2,1,0:T(8,128)(2,1)S(1)}, bf16[3,3,128,128]{3,2,1,0:T(8,128)(2,1)S(1)}) custom-call(s32[8,8]{1,0:T(8,128)S(1)} %bitcast.19, s32[8,8]{1,0:T(8,128)S(1)} %bitcast.16, s32[1,8]{1,0:T(1,128)S(1)} %bitcast.22, bf16[16,384,128]{2,1,0:T(8,128)(2,1)S(1)} %turn_rows.1.turned, ...), custom_call_target="tpu_custom_call" | custom-call | flops 1024 | bytes 1024 | tf_op jit(solution)/shard_map/stage_products/pallas_call | solution.py:287
  54.1 0.0 collective-permute-done.11.refs_0_.refs_1_.refs_4_
  54.1 0.9 pick_rows.12
  55.0 1.3 %collective-permute-start.12 = (bf16[2048,128]{1,0:T(8,128)(2,1)S(1)}, bf16[2048,128]{1,0:T(8,128)(2,1)S(1)}, u32[]{:S(2)}, u32[]{:S(2)}) collective-permute-start(bf16[2048,128]{1,0:T(8,128)(2,1)S(1)} %get-tuple-element.30.refs_7_), channel_id=1, source_target_pairs={{8,0},{12,4},{16,24},{20,28},{9,1},{13,5},{17,25},{21,29},{10,2},{... | collective-permute-start | bytes 1572872 | tf_op jit(solution)/shard_map/ppermute | solution.py:356
  56.3 0.0 collective-permute-done.13.refs_2_.refs_4_.refs_5_
  56.3 14.9 %collective-permute-done.4.refs_11_.refs_0_ = bf16[3072,128]{1,0:T(8,128)(2,1)S(1)} collective-permute-done((bf16[3072,128]{1,0:T(8,128)(2,1)S(1)}, bf16[3072,128]{1,0:T(8,128)(2,1)S(1)}, u32[]{:S(2)}, u32[]{:S(2)}) %collective-permute-start.4) | collective-permute-done | bytes 786464 | tf_op jit(solution)/shard_map/ppermute | solution.py:356
  71.2 0.0 collective-permute-done.10.refs_10_.refs_2_
  71.2 1.5 %pick_rows.13 = (bf16[3072,128]{1,0:T(8,128)(2,1)S(1)}, bf16[2048,128]{1,0:T(8,128)(2,1)S(1)}, bf16[1024,128]{1,0:T(8,128)(2,1)S(1)}) custom-call(s32[8,8]{1,0:T(8,128)S(1)} %collective-permute-done.refs_0_, bf16[4112,128]{1,0:T(8,128)(2,1)S(1)} %collective-permute-done.11.refs_0_.refs_1_.refs_4_, ...), custom_call_target="tpu_custom_call" | custom-call | flops 1024 | bytes 1024 | tf_op jit(solution)/shard_map/pick_rows/pallas_call | solution.py:222
  72.7 0.7 collective-permute-start.18
  73.4 1.3 %collective-permute-start.14 = (bf16[1024,128]{1,0:T(8,128)(2,1)S(1)}, bf16[1024,128]{1,0:T(8,128)(2,1)S(1)}, u32[]{:S(2)}, u32[]{:S(2)}) collective-permute-start(bf16[1024,128]{1,0:T(8,128)(2,1)S(1)} %get-tuple-element.32), channel_id=1, source_target_pairs={{9,5},{13,1},{17,29},{21,25},{10,6},{14,2},{18,30},{22,26}} | collective-permute-start | bytes 786440 | tf_op jit(solution)/shard_map/ppermute | solution.py:356
  74.7 1.3 %collective-permute-start.19 = (bf16[2048,128]{1,0:T(8,128)(2,1)S(1)}, bf16[2048,128]{1,0:T(8,128)(2,1)S(1)}, u32[]{:S(2)}, u32[]{:S(2)}) collective-permute-start(bf16[2048,128]{1,0:T(8,128)(2,1)S(1)} %get-tuple-element.31.refs_8_), channel_id=1, source_target_pairs={{8,4},{12,0},{16,28},{20,24},{9,5},{13,1},{17,29},{21,25},{10,6},{... | collective-permute-start | bytes 1572872 | tf_op jit(solution)/shard_map/ppermute | solution.py:356
  76.0 0.0 collective-permute-done.9.refs_1_
  76.0 1.3 %collective-permute-start.17 = (bf16[2048,128]{1,0:T(8,128)(2,1)S(1)}, bf16[2048,128]{1,0:T(8,128)(2,1)S(1)}, u32[]{:S(2)}, u32[]{:S(2)}) collective-permute-start(bf16[2048,128]{1,0:T(8,128)(2,1)S(1)} %get-tuple-element.36), channel_id=1, source_target_pairs={{9,1},{13,5},{17,25},{21,29},{10,2},{14,6},{18,26},{22,30}} | collective-permute-start | bytes 1572872 | tf_op jit(solution)/shard_map/ppermute | solution.py:356
  77.3 6.5 %collective-permute-done.14.refs_7_.refs_10_ = bf16[1024,128]{1,0:T(8,128)(2,1)S(1)} collective-permute-done((bf16[1024,128]{1,0:T(8,128)(2,1)S(1)}, bf16[1024,128]{1,0:T(8,128)(2,1)S(1)}, u32[]{:S(2)}, u32[]{:S(2)}) %collective-permute-start.14) | collective-permute-done | bytes 262176 | tf_op jit(solution)/shard_map/ppermute | solution.py:356
  83.9 0.0 collective-permute-done.12.refs_6_
  83.9 2.5 %stage_products.4 = (bf16[5,3,128,128]{3,2,1,0:T(8,128)(2,1)S(1)}, bf16[5,3,128,128]{3,2,1,0:T(8,128)(2,1)S(1)}, bf16[5,3,128,128]{3,2,1,0:T(8,128)(2,1)S(1)}) custom-call(s32[8,8]{1,0:T(8,128)S(1)} %bitcast.20, s32[8,8]{1,0:T(8,128)S(1)} %bitcast.17, s32[1,8]{1,0:T(1,128)S(1)} %bitcast.23, bf16[16,384,128]{2,1,0:T(8,128)(2,1)S(1)} %turn_rows.1.turned, ...), custom_call_target="tpu_custom_call" | custom-call | flops 1024 | bytes 1024 | tf_op jit(solution)/shard_map/stage_products/pallas_call | solution.py:287
  86.4 7.2 %collective-permute-start.15 = (bf16[5,3,128,128]{3,2,1,0:T(8,128)(2,1)S(1)}, bf16[5,3,128,128]{3,2,1,0:T(8,128)(2,1)S(1)}, u32[]{:S(2)}, u32[]{:S(2)}) collective-permute-start(bf16[5,3,128,128]{3,2,1,0:T(8,128)(2,1)S(1)} %get-tuple-element.34), channel_id=1, source_target_pairs={{0,1},{1,2},{2,3},{4,5},{5,6},{6,7},{8,9},{9,10},{10,11},{12,13},{... | collective-permute-start | bytes 1474568 | tf_op jit(solution)/shard_map/ppermute | solution.py:365
  93.6 1.9 %collective-permute-start.16 = (bf16[5,3,128,128]{3,2,1,0:T(8,128)(2,1)S(1)}, bf16[5,3,128,128]{3,2,1,0:T(8,128)(2,1)S(1)}, u32[]{:S(2)}, u32[]{:S(2)}) collective-permute-start(bf16[5,3,128,128]{3,2,1,0:T(8,128)(2,1)S(1)} %get-tuple-element.35), channel_id=1, source_target_pairs={{1,0},{2,1},{3,2},{5,4},{6,5},{7,6},{9,8},{10,9},{11,10},{13,12},{... | collective-permute-start | bytes 1474568 | tf_op jit(solution)/shard_map/ppermute | solution.py:366
  95.6 0.0 collective-permute-done.19.refs_9_
  95.6 3.3 %collective-permute-done.17.refs_3_.refs_7_ = bf16[2048,128]{1,0:T(8,128)(2,1)S(1)} collective-permute-done((bf16[2048,128]{1,0:T(8,128)(2,1)S(1)}, bf16[2048,128]{1,0:T(8,128)(2,1)S(1)}, u32[]{:S(2)}, u32[]{:S(2)}) %collective-permute-start.17) | collective-permute-done | bytes 524320 | tf_op jit(solution)/shard_map/ppermute | solution.py:356
  98.8 0.5 collective-permute-done.15.refs_11_.refs_1_
  99.4 0.0 collective-permute-done.18.refs_8_
  99.4 3.3 %stage_products.5 = (bf16[3,3,128,128]{3,2,1,0:T(8,128)(2,1)S(1)}, bf16[3,3,128,128]{3,2,1,0:T(8,128)(2,1)S(1)}, bf16[3,3,128,128]{3,2,1,0:T(8,128)(2,1)S(1)}) custom-call(s32[8,8]{1,0:T(8,128)S(1)} %bitcast.21, s32[8,8]{1,0:T(8,128)S(1)} %bitcast.18, s32[1,8]{1,0:T(1,128)S(1)} %bitcast.24, bf16[16,384,128]{2,1,0:T(8,128)(2,1)S(1)} %turn_rows.1.turned, ...), custom_call_target="tpu_custom_call" | custom-call | flops 1024 | bytes 1024 | tf_op jit(solution)/shard_map/stage_products/pallas_call | solution.py:287
  102.7 4.4 %collective-permute-start.20 = (bf16[3,3,128,128]{3,2,1,0:T(8,128)(2,1)S(1)}, bf16[3,3,128,128]{3,2,1,0:T(8,128)(2,1)S(1)}, u32[]{:S(2)}, u32[]{:S(2)}) collective-permute-start(bf16[3,3,128,128]{3,2,1,0:T(8,128)(2,1)S(1)} %get-tuple-element.39), channel_id=1, source_target_pairs={{0,1},{1,2},{2,3},{4,5},{5,6},{6,7},{8,9},{9,10},{10,11},{12,13},{... | collective-permute-start | bytes 884744 | tf_op jit(solution)/shard_map/ppermute | solution.py:365
  107.1 1.9 %collective-permute-start.21 = (bf16[3,3,128,128]{3,2,1,0:T(8,128)(2,1)S(1)}, bf16[3,3,128,128]{3,2,1,0:T(8,128)(2,1)S(1)}, u32[]{:S(2)}, u32[]{:S(2)}) collective-permute-start(bf16[3,3,128,128]{3,2,1,0:T(8,128)(2,1)S(1)} %get-tuple-element.40), channel_id=1, source_target_pairs={{1,0},{2,1},{3,2},{5,4},{6,5},{7,6},{9,8},{10,9},{11,10},{13,12},{... | collective-permute-start | bytes 884744 | tf_op jit(solution)/shard_map/ppermute | solution.py:366
  109.0 0.0 collective-permute-done.16.refs_2_
  109.0 1.7 %collective-permute-done.20.refs_4_ = bf16[3,3,128,128]{3,2,1,0:T(8,128)(2,1)S(1)} collective-permute-done((bf16[3,3,128,128]{3,2,1,0:T(8,128)(2,1)S(1)}, bf16[3,3,128,128]{3,2,1,0:T(8,128)(2,1)S(1)}, u32[]{:S(2)}, u32[]{:S(2)}) %collective-permute-start.20) | collective-permute-done | bytes 294944 | tf_op jit(solution)/shard_map/ppermute | solution.py:365
  110.7 4.4 %collective-permute-done.21.refs_5_ = bf16[3,3,128,128]{3,2,1,0:T(8,128)(2,1)S(1)} collective-permute-done((bf16[3,3,128,128]{3,2,1,0:T(8,128)(2,1)S(1)}, bf16[3,3,128,128]{3,2,1,0:T(8,128)(2,1)S(1)}, u32[]{:S(2)}, u32[]{:S(2)}) %collective-permute-start.21) | collective-permute-done | bytes 294944 | tf_op jit(solution)/shard_map/ppermute | solution.py:366
  115.1 2.5 %assemble_coarse.1 = f32[5120,128]{1,0:T(8,128)} custom-call(bf16[5,3,128,128]{3,2,1,0:T(8,128)(2,1)S(1)} %get-tuple-element.33.refs_0_, bf16[5,3,128,128]{3,2,1,0:T(8,128)(2,1)S(1)} %collective-permute-done.15.refs_11_.refs_1_, bf16[5,3,128,128]{3,2,1,0:T(8,128)(2,1)S(1)} %collective-permute-done.16.refs_2_, ...), custom_call_target="tpu_custom_call" | custom-call | flops 1024 | bytes 1024 | tf_op jit(solution)/shard_map/assemble_coarse/pallas_call | solution.py:332
  (5 shorter events, 0.0 us)
Async XLA Ops:
  0.0 5.6 %copy-start.3 = (s32[1,1,8,8]{3,2,1,0:T(8,128)S(1)}, s32[1,1,8,8]{3,2,1,0:T(8,128)}, u32[]{:S(2)}) copy-start(s32[1,1,8,8]{3,2,1,0:T(8,128)} %param.8) | copy-start | bytes 772
  2.6 25.4 %collective-permute-start.1 = (bf16[4112,128]{1,0:T(8,128)(2,1)}, bf16[4112,128]{1,0:T(8,128)(2,1)S(1)}, u32[]{:S(2)}, u32[]{:S(2)}) collective-permute-start(bf16[4112,128]{1,0:T(8,128)(2,1)} %get-tuple-element.23.head.refs_1_.refs_0_), channel_id=1, source_target_pairs={{0,8},{4,12},{16,24},{20,28},{8,0},{12,4},{24,16},{28,20},{1,9},{5... | collective-permute-start | bytes 3158024 | tf_op jit(solution)/shard_map/ppermute | solution.py:356
  4.8 23.2 %collective-permute-start.5 = (bf16[4112,128]{1,0:T(8,128)(2,1)}, bf16[4112,128]{1,0:T(8,128)(2,1)S(1)}, u32[]{:S(2)}, u32[]{:S(2)}) collective-permute-start(bf16[4112,128]{1,0:T(8,128)(2,1)} %get-tuple-element.23.head.refs_1_.refs_0_), channel_id=1, source_target_pairs={{8,16},{12,20},{16,8},{20,12},{9,17},{13,21},{17,9},{21,13},{10,18... | collective-permute-start | bytes 3158024 | tf_op jit(solution)/shard_map/ppermute | solution.py:356
  5.6 2.8 %collective-permute-start = (s32[8,8]{1,0:T(8,128)S(1)}, s32[8,8]{1,0:T(8,128)S(1)}, u32[]{:S(2)}, u32[]{:S(2)}) collective-permute-start(s32[8,8]{1,0:T(8,128)S(1)} %bitcast.15), channel_id=1, source_target_pairs={{4,0},{0,4},{12,8},{8,12},{20,16},{16,20},{28,24},{24,28},{5,1},{1... | collective-permute-start | bytes 776 | tf_op jit(solution)/shard_map/ppermute | solution.py:356
  8.4 1.2 %copy-start.1 = (bf16[4112,128]{1,0:T(8,128)(2,1)S(1)}, bf16[4112,128]{1,0:T(8,128)(2,1)}, u32[]{:S(2)}) copy-start(bf16[4112,128]{1,0:T(8,128)(2,1)} %get-tuple-element.23.head.refs_1_.refs_0_) | copy-start | bytes 3158020
  11.3 23.5 %collective-permute-start.3 = (bf16[3072,128]{1,0:T(8,128)(2,1)S(1)}, bf16[3072,128]{1,0:T(8,128)(2,1)S(1)}, u32[]{:S(2)}, u32[]{:S(2)}) collective-permute-start(bf16[3072,128]{1,0:T(8,128)(2,1)S(1)} %pick_rows.7), channel_id=1, source_target_pairs={{0,4},{4,0},{8,12},{12,8},{16,20},{20,16},{24,28},{28,24},{1,5},{5... | collective-permute-start | bytes 2359304 | tf_op jit(solution)/shard_map/ppermute | solution.py:356
  12.6 21.6 %collective-permute-start.2 = (bf16[2048,128]{1,0:T(8,128)(2,1)}, bf16[2048,128]{1,0:T(8,128)(2,1)S(1)}, u32[]{:S(2)}, u32[]{:S(2)}) collective-permute-start(bf16[2048,128]{1,0:T(8,128)(2,1)} %get-tuple-element.24.tail.refs_2_.refs_1_), channel_id=1, source_target_pairs={{1,9},{5,13},{17,25},{21,29},{9,1},{13,5},{25,17},{29,21},{2,10},{... | collective-permute-start | bytes 1572872 | tf_op jit(solution)/shard_map/ppermute | solution.py:356
  18.3 18.7 %collective-permute-start.6 = (bf16[2048,128]{1,0:T(8,128)(2,1)}, bf16[2048,128]{1,0:T(8,128)(2,1)S(1)}, u32[]{:S(2)}, u32[]{:S(2)}) collective-permute-start(bf16[2048,128]{1,0:T(8,128)(2,1)} %get-tuple-element.24.tail.refs_2_.refs_1_), channel_id=1, source_target_pairs={{9,17},{13,21},{17,9},{21,13},{10,18},{14,22},{18,10},{22,14}} | collective-permute-start | bytes 1572872 | tf_op jit(solution)/shard_map/ppermute | solution.py:356
  28.8 15.0 %collective-permute-start.8 = (bf16[2048,128]{1,0:T(8,128)(2,1)S(1)}, bf16[2048,128]{1,0:T(8,128)(2,1)S(1)}, u32[]{:S(2)}, u32[]{:S(2)}) collective-permute-start(bf16[2048,128]{1,0:T(8,128)(2,1)S(1)} %get-tuple-element.26), channel_id=1, source_target_pairs={{8,0},{12,4},{16,24},{20,28},{9,1},{13,5},{17,25},{21,29},{10,2},{... | collective-permute-start | bytes 1572872 | tf_op jit(solution)/shard_map/ppermute | solution.py:356
  30.1 24.0 %collective-permute-start.11 = (bf16[4112,128]{1,0:T(8,128)(2,1)S(1)}, bf16[4112,128]{1,0:T(8,128)(2,1)S(1)}, u32[]{:S(2)}, u32[]{:S(2)}) collective-permute-start(bf16[4112,128]{1,0:T(8,128)(2,1)S(1)} %collective-permute-done.1.refs_1_.refs_2_.refs_5_), channel_id=1, source_target_pairs={{8,16},{12,20},{16,8},{20,12},{9,17},{13,21},{17,9},{21,13},{10,18... | collective-permute-start | bytes 3158024 | tf_op jit(solution)/shard_map/ppermute | solution.py:356
  34.2 2.8 %collective-permute-start.7 = (bf16[16,128]{1,0:T(8,128)(2,1)S(1)}, bf16[16,128]{1,0:T(8,128)(2,1)S(1)}, u32[]{:S(2)}, u32[]{:S(2)}) collective-permute-start(bf16[16,128]{1,0:T(8,128)(2,1)S(1)} %get-tuple-element.25), channel_id=1, source_target_pairs={{12,8},{8,12},{20,16},{16,20},{13,9},{9,13},{21,17},{17,21},{14,10... | collective-permute-start | bytes 12296 | tf_op jit(solution)/shard_map/ppermute | solution.py:356
  35.5 35.6 %collective-permute-start.4 = (bf16[3072,128]{1,0:T(8,128)(2,1)S(1)}, bf16[3072,128]{1,0:T(8,128)(2,1)S(1)}, u32[]{:S(2)}, u32[]{:S(2)}) collective-permute-start(bf16[3072,128]{1,0:T(8,128)(2,1)S(1)} %pick_rows.8.refs_3_), channel_id=1, source_target_pairs={{0,4},{4,0},{8,12},{12,8},{16,20},{20,16},{24,28},{28,24},{1,5},{5... | collective-permute-start | bytes 2359304 | tf_op jit(solution)/shard_map/ppermute | solution.py:356
  44.5 3.7 %copy-start.2 = (bf16[4112,128]{1,0:T(8,128)(2,1)S(1)}, bf16[4112,128]{1,0:T(8,128)(2,1)}, u32[]{:S(2)}) copy-start(bf16[4112,128]{1,0:T(8,128)(2,1)} %get-tuple-element.23.head.refs_1_.refs_0_) | copy-start | bytes 3158020
  44.5 26.7 %collective-permute-start.10 = (bf16[3072,128]{1,0:T(8,128)(2,1)S(1)}, bf16[3072,128]{1,0:T(8,128)(2,1)S(1)}, u32[]{:S(2)}, u32[]{:S(2)}) collective-permute-start(bf16[3072,128]{1,0:T(8,128)(2,1)S(1)} %pick_rows.10.refs_3_), channel_id=1, source_target_pairs={{8,4},{12,0},{16,28},{20,24},{9,5},{13,1},{17,29},{21,25},{10,6},{... | collective-permute-start | bytes 2359304 | tf_op jit(solution)/shard_map/ppermute | solution.py:356
  45.9 10.4 %collective-permute-start.13 = (bf16[2048,128]{1,0:T(8,128)(2,1)S(1)}, bf16[2048,128]{1,0:T(8,128)(2,1)S(1)}, u32[]{:S(2)}, u32[]{:S(2)}) collective-permute-start(bf16[2048,128]{1,0:T(8,128)(2,1)S(1)} %collective-permute-done.2.refs_2_.refs_3_), channel_id=1, source_target_pairs={{9,17},{13,21},{17,9},{21,13},{10,18},{14,22},{18,10},{22,14}} | collective-permute-start | bytes 1572872 | tf_op jit(solution)/shard_map/ppermute | solution.py:356
  47.3 2.4 %copy-start = (bf16[1,1,8,8,128,128]{5,4,3,2,1,0:T(8,128)(2,1)S(1)}, bf16[1,1,8,8,128,128]{5,4,3,2,1,0:T(8,128)(2,1)}, u32[]{:S(2)}) copy-start(bf16[1,1,8,8,128,128]{5,4,3,2,1,0:T(8,128)(2,1)} %param.6) | copy-start | bytes 6291460
  47.3 2.4 %copy-start.4 = (s32[1,1,8,8]{3,2,1,0:T(8,128)S(1)}, s32[1,1,8,8]{3,2,1,0:T(8,128)}, u32[]{:S(2)}) copy-start(s32[1,1,8,8]{3,2,1,0:T(8,128)} %param.7) | copy-start | bytes 772
  47.3 2.4 %copy-start.5 = (s32[1,1,8]{2,1,0:T(1,128)S(1)}, s32[1,1,8]{2,1,0:T(1,128)}, u32[]{:S(2)}) copy-start(s32[1,1,8]{2,1,0:T(1,128)} %param.9) | copy-start | bytes 100
  47.3 28.7 %collective-permute-start.9 = (bf16[3072,128]{1,0:T(8,128)(2,1)S(1)}, bf16[3072,128]{1,0:T(8,128)(2,1)S(1)}, u32[]{:S(2)}, u32[]{:S(2)}) collective-permute-start(bf16[3072,128]{1,0:T(8,128)(2,1)S(1)} %pick_rows.11.refs_4_), channel_id=1, source_target_pairs={{8,12},{12,8},{16,20},{20,16},{9,13},{13,9},{17,21},{21,17},{10,14... | collective-permute-start | bytes 2359304 | tf_op jit(solution)/shard_map/ppermute | solution.py:356
  55.0 28.9 %collective-permute-start.12 = (bf16[2048,128]{1,0:T(8,128)(2,1)S(1)}, bf16[2048,128]{1,0:T(8,128)(2,1)S(1)}, u32[]{:S(2)}, u32[]{:S(2)}) collective-permute-start(bf16[2048,128]{1,0:T(8,128)(2,1)S(1)} %get-tuple-element.30.refs_7_), channel_id=1, source_target_pairs={{8,0},{12,4},{16,24},{20,28},{9,1},{13,5},{17,25},{21,29},{10,2},{... | collective-permute-start | bytes 1572872 | tf_op jit(solution)/shard_map/ppermute | solution.py:356
  72.7 26.7 %collective-permute-start.18 = (bf16[3072,128]{1,0:T(8,128)(2,1)S(1)}, bf16[3072,128]{1,0:T(8,128)(2,1)S(1)}, u32[]{:S(2)}, u32[]{:S(2)}) collective-permute-start(bf16[3072,128]{1,0:T(8,128)(2,1)S(1)} %get-tuple-element.37), channel_id=1, source_target_pairs={{8,12},{12,8},{16,20},{20,16},{9,13},{13,9},{17,21},{21,17},{10,14... | collective-permute-start | bytes 2359304 | tf_op jit(solution)/shard_map/ppermute | solution.py:356
  73.4 10.4 %collective-permute-start.14 = (bf16[1024,128]{1,0:T(8,128)(2,1)S(1)}, bf16[1024,128]{1,0:T(8,128)(2,1)S(1)}, u32[]{:S(2)}, u32[]{:S(2)}) collective-permute-start(bf16[1024,128]{1,0:T(8,128)(2,1)S(1)} %get-tuple-element.32), channel_id=1, source_target_pairs={{9,5},{13,1},{17,29},{21,25},{10,6},{14,2},{18,30},{22,26}} | collective-permute-start | bytes 786440 | tf_op jit(solution)/shard_map/ppermute | solution.py:356
  74.7 20.8 %collective-permute-start.19 = (bf16[2048,128]{1,0:T(8,128)(2,1)S(1)}, bf16[2048,128]{1,0:T(8,128)(2,1)S(1)}, u32[]{:S(2)}, u32[]{:S(2)}) collective-permute-start(bf16[2048,128]{1,0:T(8,128)(2,1)S(1)} %get-tuple-element.31.refs_8_), channel_id=1, source_target_pairs={{8,4},{12,0},{16,28},{20,24},{9,5},{13,1},{17,29},{21,25},{10,6},{... | collective-permute-start | bytes 1572872 | tf_op jit(solution)/shard_map/ppermute | solution.py:356
  76.0 22.8 %collective-permute-start.17 = (bf16[2048,128]{1,0:T(8,128)(2,1)S(1)}, bf16[2048,128]{1,0:T(8,128)(2,1)S(1)}, u32[]{:S(2)}, u32[]{:S(2)}) collective-permute-start(bf16[2048,128]{1,0:T(8,128)(2,1)S(1)} %get-tuple-element.36), channel_id=1, source_target_pairs={{9,1},{13,5},{17,25},{21,29},{10,2},{14,6},{18,26},{22,30}} | collective-permute-start | bytes 1572872 | tf_op jit(solution)/shard_map/ppermute | solution.py:356
  86.4 13.0 %collective-permute-start.15 = (bf16[5,3,128,128]{3,2,1,0:T(8,128)(2,1)S(1)}, bf16[5,3,128,128]{3,2,1,0:T(8,128)(2,1)S(1)}, u32[]{:S(2)}, u32[]{:S(2)}) collective-permute-start(bf16[5,3,128,128]{3,2,1,0:T(8,128)(2,1)S(1)} %get-tuple-element.34), channel_id=1, source_target_pairs={{0,1},{1,2},{2,3},{4,5},{5,6},{6,7},{8,9},{9,10},{10,11},{12,13},{... | collective-permute-start | bytes 1474568 | tf_op jit(solution)/shard_map/ppermute | solution.py:365
  93.6 15.4 %collective-permute-start.16 = (bf16[5,3,128,128]{3,2,1,0:T(8,128)(2,1)S(1)}, bf16[5,3,128,128]{3,2,1,0:T(8,128)(2,1)S(1)}, u32[]{:S(2)}, u32[]{:S(2)}) collective-permute-start(bf16[5,3,128,128]{3,2,1,0:T(8,128)(2,1)S(1)} %get-tuple-element.35), channel_id=1, source_target_pairs={{1,0},{2,1},{3,2},{5,4},{6,5},{7,6},{9,8},{10,9},{11,10},{13,12},{... | collective-permute-start | bytes 1474568 | tf_op jit(solution)/shard_map/ppermute | solution.py:366
  102.7 8.0 %collective-permute-start.20 = (bf16[3,3,128,128]{3,2,1,0:T(8,128)(2,1)S(1)}, bf16[3,3,128,128]{3,2,1,0:T(8,128)(2,1)S(1)}, u32[]{:S(2)}, u32[]{:S(2)}) collective-permute-start(bf16[3,3,128,128]{3,2,1,0:T(8,128)(2,1)S(1)} %get-tuple-element.39), channel_id=1, source_target_pairs={{0,1},{1,2},{2,3},{4,5},{5,6},{6,7},{8,9},{9,10},{10,11},{12,13},{... | collective-permute-start | bytes 884744 | tf_op jit(solution)/shard_map/ppermute | solution.py:365
  107.1 8.0 %collective-permute-start.21 = (bf16[3,3,128,128]{3,2,1,0:T(8,128)(2,1)S(1)}, bf16[3,3,128,128]{3,2,1,0:T(8,128)(2,1)S(1)}, u32[]{:S(2)}, u32[]{:S(2)}) collective-permute-start(bf16[3,3,128,128]{3,2,1,0:T(8,128)(2,1)S(1)} %get-tuple-element.40), channel_id=1, source_target_pairs={{1,0},{2,1},{3,2},{5,4},{6,5},{7,6},{9,8},{10,9},{11,10},{13,12},{... | collective-permute-start | bytes 884744 | tf_op jit(solution)/shard_map/ppermute | solution.py:366

commit v20 on v19

--- a/solution.py
+++ b/solution.py
@@ -426,7 +426,7 @@
                 [(count + 1 + index, row, 2, count + 1 + index, 0) for index in range(count)])
 
     picked = pick(grid, last_requests, [(3, cap)] * count + [(1, 2 * cap)] + [(1, cap)] * count, side_lists,
-                  [far, other[1:], far[1:], *tables], tables=tuple(range(3, 4 + count)), after=[*far_picked, end_heads[0], *[x for ((x, _),) in end_crossed], *[x for ((x, _),) in half_crossed]],
+                  [far, other[1:], far[1:], *tables], tables=tuple(range(3, 4 + count)), after=[*far_picked, end_heads[0], *[x for ((x, _),) in end_crossed]],
                   cost=COST)
     far_crossed = move_across(picked, mids)
     end_tail = move(picked[count], grid.ends(0), inner)

time: 118 us -> 125 us (1.059)
  waiting for transfers between devices: 52 us -> 59.6 us
    ppermute x18, waiting for transfers between devices: 45.4 us -> 53.5 us  [move(): return lax.ppermute(x, ('blk', 'rows'), perm) if perm else jnp.zeros_like(x)]
  transfers between devices with their start and end apart: 22 -> 22, of which waited for: 10 -> 10; matrix products, arithmetic and copies ran while one was open for 0% -> 0% of each run, Pallas kernels for 16% -> 15%
where the time goes in v20:
time: 125 us; the launch traced here: 124 us
  waiting for transfers between devices  59.6 us (48%)
  starting transfers between devices  39.5 us (32%)
  Pallas kernels  23.7 us (19%)
  local copies, waits for them, and re-layouts  1.26 us (1%)
    ppermute x18, waiting for transfers between devices, move(): return lax.ppermute(x, ('blk', 'rows'), perm) if perm else jnp.zeros_like(x)  53.5 us
    ppermute x18, starting transfers between devices, move(): return lax.ppermute(x, ('blk', 'rows'), perm) if perm else jnp.zeros_like(x)  24.7 us
    ppermute x2, starting transfers between devices, exchange(): lax.ppermute(parts[1], 'rows', [(g, g + 1) for g in range(groups - 1)])  11 us
    pallas_call x3, Pallas kernels, stage(): pl.pallas_call(functools.partial(stage_kernel, grid, plan, layout, carrie...  10.1 us
    pallas_call x7, Pallas kernels, pick(): pl.pallas_call(functools.partial(pick_kernel, grid, plan, layout, carry,...  6.93 us
    ppermute x2, waiting for transfers between devices, exchange(): lax.ppermute(parts[2], 'rows', [(g + 1, g) for g in range(groups - 1)])  4.4 us
    ppermute x2, starting transfers between devices, exchange(): lax.ppermute(parts[2], 'rows', [(g + 1, g) for g in range(groups - 1)])  3.84 us
    pallas_call x1, Pallas kernels, pack(): pl.pallas_call(functools.partial(pack_kernel, grid), grid=(1,), in_specs=...  2.64 us
  transfers between devices with their start and end apart: 22, of which 10 were waited for; matrix products, arithmetic and copies ran while one was open for 0% of the time, Pallas kernels for 15%

profile of v20, /device:TPU:1, one launch (start us, length us, event | category | flops | bytes accessed | tf_op | source)
XLA Modules:
  0.0 124.4 jit_solution(3358353084484074866)
XLA Ops:
  0.0 2.6 %pack_rows.1 = (bf16[4112,128]{1,0:T(8,128)(2,1)}, bf16[2048,128]{1,0:T(8,128)(2,1)}) custom-call(s32[3,1,16]{2,1,0:T(1,128)} %bitcast.26, s32[8,8]{1,0:T(8,128)} %bitcast.14, bf16[16,128,384]{2,1,0:T(8,128)(2,1)} %bitcast.25), custom_call_target="tpu_custom_call" | custom-call | flops 1024 | bytes 1024 | tf_op jit(solution)/shard_map/pack_rows/pallas_call | solution.py:130
  2.6 2.2 %collective-permute-start.1 = (bf16[4112,128]{1,0:T(8,128)(2,1)}, bf16[4112,128]{1,0:T(8,128)(2,1)S(1)}, u32[]{:S(2)}, u32[]{:S(2)}) collective-permute-start(bf16[4112,128]{1,0:T(8,128)(2,1)} %get-tuple-element.23.head.refs_1_.refs_0_), channel_id=1, source_target_pairs={{0,8},{4,12},{16,24},{20,28},{8,0},{12,4},{24,16},{28,20},{1,9},{5... | collective-permute-start | bytes 3158024 | tf_op jit(solution)/shard_map/ppermute | solution.py:356
  4.8 0.7 collective-permute-start.5
  5.6 0.0 copy-done.3
  5.6 1.3 %collective-permute-start = (s32[8,8]{1,0:T(8,128)S(1)}, s32[8,8]{1,0:T(8,128)S(1)}, u32[]{:S(2)}, u32[]{:S(2)}) collective-permute-start(s32[8,8]{1,0:T(8,128)S(1)} %bitcast.15), channel_id=1, source_target_pairs={{4,0},{0,4},{12,8},{8,12},{20,16},{16,20},{28,24},{24,28},{5,1},{1... | collective-permute-start | bytes 776 | tf_op jit(solution)/shard_map/ppermute | solution.py:356
  6.9 1.5 %collective-permute-done.refs_0_ = s32[8,8]{1,0:T(8,128)S(1)} collective-permute-done((s32[8,8]{1,0:T(8,128)S(1)}, s32[8,8]{1,0:T(8,128)S(1)}, u32[]{:S(2)}, u32[]{:S(2)}) %collective-permute-start) | collective-permute-done | bytes 288 | tf_op jit(solution)/shard_map/ppermute | solution.py:356
  8.4 1.2 copy-done.1
  9.6 1.7 %pick_rows.7 = bf16[3072,128]{1,0:T(8,128)(2,1)S(1)} custom-call(s32[8,8]{1,0:T(8,128)S(1)} %collective-permute-done.refs_0_, bf16[4112,128]{1,0:T(8,128)(2,1)S(1)} %copy-done.1, bf16[2048,128]{1,0:T(8,128)(2,1)} %get-tuple-element.24.tail.refs_2_.refs_1_), custom_call_target="tpu_custom_call" | custom-call | flops 1024 | bytes 1024 | tf_op jit(solution)/shard_map/pick_rows/pallas_call | solution.py:222
  11.3 1.3 %collective-permute-start.3 = (bf16[3072,128]{1,0:T(8,128)(2,1)S(1)}, bf16[3072,128]{1,0:T(8,128)(2,1)S(1)}, u32[]{:S(2)}, u32[]{:S(2)}) collective-permute-start(bf16[3072,128]{1,0:T(8,128)(2,1)S(1)} %pick_rows.7), channel_id=1, source_target_pairs={{0,4},{4,0},{8,12},{12,8},{16,20},{20,16},{24,28},{28,24},{1,5},{5... | collective-permute-start | bytes 2359304 | tf_op jit(solution)/shard_map/ppermute | solution.py:356
  12.6 5.7 %collective-permute-start.2 = (bf16[2048,128]{1,0:T(8,128)(2,1)}, bf16[2048,128]{1,0:T(8,128)(2,1)S(1)}, u32[]{:S(2)}, u32[]{:S(2)}) collective-permute-start(bf16[2048,128]{1,0:T(8,128)(2,1)} %get-tuple-element.24.tail.refs_2_.refs_1_), channel_id=1, source_target_pairs={{1,9},{5,13},{17,25},{21,29},{9,1},{13,5},{25,17},{29,21},{2,10},{... | collective-permute-start | bytes 1572872 | tf_op jit(solution)/shard_map/ppermute | solution.py:356
  18.3 0.7 collective-permute-start.6
  19.0 9.0 %collective-permute-done.1.refs_1_.refs_2_.refs_5_ = bf16[4112,128]{1,0:T(8,128)(2,1)S(1)} collective-permute-done((bf16[4112,128]{1,0:T(8,128)(2,1)}, bf16[4112,128]{1,0:T(8,128)(2,1)S(1)}, u32[]{:S(2)}, u32[]{:S(2)}) %collective-permute-start.1) | collective-permute-done | bytes 1052704 | tf_op jit(solution)/shard_map/ppermute | solution.py:356
  28.0 0.0 collective-permute-done.5.refs_0_.refs_1_
  28.0 0.7 pick_rows.9
  28.8 1.3 %collective-permute-start.8 = (bf16[2048,128]{1,0:T(8,128)(2,1)S(1)}, bf16[2048,128]{1,0:T(8,128)(2,1)S(1)}, u32[]{:S(2)}, u32[]{:S(2)}) collective-permute-start(bf16[2048,128]{1,0:T(8,128)(2,1)S(1)} %get-tuple-element.26), channel_id=1, source_target_pairs={{8,0},{12,4},{16,24},{20,28},{9,1},{13,5},{17,25},{21,29},{10,2},{... | collective-permute-start | bytes 1572872 | tf_op jit(solution)/shard_map/ppermute | solution.py:356
  30.1 0.7 collective-permute-start.11
  30.8 3.4 %collective-permute-done.2.refs_2_.refs_3_ = bf16[2048,128]{1,0:T(8,128)(2,1)S(1)} collective-permute-done((bf16[2048,128]{1,0:T(8,128)(2,1)}, bf16[2048,128]{1,0:T(8,128)(2,1)S(1)}, u32[]{:S(2)}, u32[]{:S(2)}) %collective-permute-start.2) | collective-permute-done | bytes 524320 | tf_op jit(solution)/shard_map/ppermute | solution.py:356
  34.2 0.7 collective-permute-start.7
  34.8 0.0 collective-permute-done.3.refs_3_.refs_4_
  34.8 0.7 pick_rows.8.refs_3_
  35.5 0.0 collective-permute-done.6.refs_1_.refs_2_.refs_3_
  35.5 0.0 collective-permute-done.7.refs_2_.refs_6_
  35.6 8.2 %collective-permute-done.8.refs_4_.refs_9_.refs_2_ = bf16[2048,128]{1,0:T(8,128)(2,1)S(1)} collective-permute-done((bf16[2048,128]{1,0:T(8,128)(2,1)S(1)}, bf16[2048,128]{1,0:T(8,128)(2,1)S(1)}, u32[]{:S(2)}, u32[]{:S(2)}) %collective-permute-start.8) | collective-permute-done | bytes 524320 | tf_op jit(solution)/shard_map/ppermute | solution.py:356
  43.7 0.7 pick_rows.10.refs_3_
  44.5 0.0 copy-start.2
  44.5 1.4 %collective-permute-start.10 = (bf16[3072,128]{1,0:T(8,128)(2,1)S(1)}, bf16[3072,128]{1,0:T(8,128)(2,1)S(1)}, u32[]{:S(2)}, u32[]{:S(2)}) collective-permute-start(bf16[3072,128]{1,0:T(8,128)(2,1)S(1)} %pick_rows.10.refs_3_), channel_id=1, source_target_pairs={{8,4},{12,0},{16,28},{20,24},{9,5},{13,1},{17,29},{21,25},{10,6},{... | collective-permute-start | bytes 2359304 | tf_op jit(solution)/shard_map/ppermute | solution.py:356
  45.9 1.3 %collective-permute-start.4 = (bf16[3072,128]{1,0:T(8,128)(2,1)S(1)}, bf16[3072,128]{1,0:T(8,128)(2,1)S(1)}, u32[]{:S(2)}, u32[]{:S(2)}) collective-permute-start(bf16[3072,128]{1,0:T(8,128)(2,1)S(1)} %pick_rows.8.refs_3_), channel_id=1, source_target_pairs={{0,4},{4,0},{8,12},{12,8},{16,20},{20,16},{24,28},{28,24},{1,5},{5... | collective-permute-start | bytes 2359304 | tf_op jit(solution)/shard_map/ppermute | solution.py:356
  47.2 0.7 collective-permute-start.13
  47.9 0.7 pick_rows.11.refs_4_
  48.6 0.0 copy-start
  48.6 0.0 copy-start.4
  48.6 0.0 copy-start.5
  48.6 0.8 collective-permute-start.9
  49.5 0.0 copy-done.2
  49.5 1.5 %turn_rows.1.turned = bf16[16,384,128]{2,1,0:T(8,128)(2,1)S(1)} custom-call(bf16[4112,128]{1,0:T(8,128)(2,1)S(1)} %copy-done.2, bf16[2048,128]{1,0:T(8,128)(2,1)} %get-tuple-element.24.tail.refs_2_.refs_1_), custom_call_target="tpu_custom_call" | custom-call | flops 1024 | bytes 1024 | tf_op jit(solution)/shard_map/turn_rows/pallas_call | solution.py:159
  51.0 4.3 %stage_products.3 = (bf16[3,3,128,128]{3,2,1,0:T(8,128)(2,1)S(1)}, bf16[3,3,128,128]{3,2,1,0:T(8,128)(2,1)S(1)}, bf16[3,3,128,128]{3,2,1,0:T(8,128)(2,1)S(1)}) custom-call(s32[8,8]{1,0:T(8,128)S(1)} %bitcast.19, s32[8,8]{1,0:T(8,128)S(1)} %bitcast.16, s32[1,8]{1,0:T(1,128)S(1)} %bitcast.22, bf16[16,384,128]{2,1,0:T(8,128)(2,1)S(1)} %turn_rows.1.turned, ...), custom_call_target="tpu_custom_call" | custom-call | flops 1024 | bytes 1024 | tf_op jit(solution)/shard_map/stage_products/pallas_call | solution.py:287
  55.4 0.0 collective-permute-done.11.refs_0_.refs_1_.refs_4_
  55.4 0.9 pick_rows.12
  56.3 1.3 %collective-permute-start.12 = (bf16[2048,128]{1,0:T(8,128)(2,1)S(1)}, bf16[2048,128]{1,0:T(8,128)(2,1)S(1)}, u32[]{:S(2)}, u32[]{:S(2)}) collective-permute-start(bf16[2048,128]{1,0:T(8,128)(2,1)S(1)} %get-tuple-element.30.refs_7_), channel_id=1, source_target_pairs={{8,0},{12,4},{16,24},{20,28},{9,1},{13,5},{17,25},{21,29},{10,2},{... | collective-permute-start | bytes 1572872 | tf_op jit(solution)/shard_map/ppermute | solution.py:356
  57.6 0.0 collective-permute-done.13.refs_2_.refs_4_.refs_5_
  57.6 5.6 %collective-permute-done.10.refs_10_.refs_2_ = bf16[3072,128]{1,0:T(8,128)(2,1)S(1)} collective-permute-done((bf16[3072,128]{1,0:T(8,128)(2,1)S(1)}, bf16[3072,128]{1,0:T(8,128)(2,1)S(1)}, u32[]{:S(2)}, u32[]{:S(2)}) %collective-permute-start.10) | collective-permute-done | bytes 786464 | tf_op jit(solution)/shard_map/ppermute | solution.py:356
  63.2 1.5 %pick_rows.13 = (bf16[3072,128]{1,0:T(8,128)(2,1)S(1)}, bf16[2048,128]{1,0:T(8,128)(2,1)S(1)}, bf16[1024,128]{1,0:T(8,128)(2,1)S(1)}) custom-call(s32[8,8]{1,0:T(8,128)S(1)} %collective-permute-done.refs_0_, bf16[4112,128]{1,0:T(8,128)(2,1)S(1)} %collective-permute-done.11.refs_0_.refs_1_.refs_4_, ...), custom_call_target="tpu_custom_call" | custom-call | flops 1024 | bytes 1024 | tf_op jit(solution)/shard_map/pick_rows/pallas_call | solution.py:222
  64.7 0.7 collective-permute-start.18
  65.5 1.3 %collective-permute-start.14 = (bf16[1024,128]{1,0:T(8,128)(2,1)S(1)}, bf16[1024,128]{1,0:T(8,128)(2,1)S(1)}, u32[]{:S(2)}, u32[]{:S(2)}) collective-permute-start(bf16[1024,128]{1,0:T(8,128)(2,1)S(1)} %get-tuple-element.32), channel_id=1, source_target_pairs={{9,5},{13,1},{17,29},{21,25},{10,6},{14,2},{18,30},{22,26}} | collective-permute-start | bytes 786440 | tf_op jit(solution)/shard_map/ppermute | solution.py:356
  66.8 16.9 %collective-permute-done.4.refs_0_ = bf16[3072,128]{1,0:T(8,128)(2,1)S(1)} collective-permute-done((bf16[3072,128]{1,0:T(8,128)(2,1)S(1)}, bf16[3072,128]{1,0:T(8,128)(2,1)S(1)}, u32[]{:S(2)}, u32[]{:S(2)}) %collective-permute-start.4) | collective-permute-done | bytes 786464 | tf_op jit(solution)/shard_map/ppermute | solution.py:356
  83.6 1.3 %collective-permute-start.19 = (bf16[2048,128]{1,0:T(8,128)(2,1)S(1)}, bf16[2048,128]{1,0:T(8,128)(2,1)S(1)}, u32[]{:S(2)}, u32[]{:S(2)}) collective-permute-start(bf16[2048,128]{1,0:T(8,128)(2,1)S(1)} %get-tuple-element.31.refs_8_), channel_id=1, source_target_pairs={{8,4},{12,0},{16,28},{20,24},{9,5},{13,1},{17,29},{21,25},{10,6},{... | collective-permute-start | bytes 1572872 | tf_op jit(solution)/shard_map/ppermute | solution.py:356
  84.9 0.0 collective-permute-done.9.refs_1_
  84.9 1.3 %collective-permute-start.17 = (bf16[2048,128]{1,0:T(8,128)(2,1)S(1)}, bf16[2048,128]{1,0:T(8,128)(2,1)S(1)}, u32[]{:S(2)}, u32[]{:S(2)}) collective-permute-start(bf16[2048,128]{1,0:T(8,128)(2,1)S(1)} %get-tuple-element.36), channel_id=1, source_target_pairs={{9,1},{13,5},{17,25},{21,29},{10,2},{14,6},{18,26},{22,30}} | collective-permute-start | bytes 1572872 | tf_op jit(solution)/shard_map/ppermute | solution.py:356
  86.2 0.0 collective-permute-done.14.refs_7_.refs_10_
  86.2 0.0 collective-permute-done.12.refs_6_
  86.2 2.5 %stage_products.4 = (bf16[5,3,128,128]{3,2,1,0:T(8,128)(2,1)S(1)}, bf16[5,3,128,128]{3,2,1,0:T(8,128)(2,1)S(1)}, bf16[5,3,128,128]{3,2,1,0:T(8,128)(2,1)S(1)}) custom-call(s32[8,8]{1,0:T(8,128)S(1)} %bitcast.20, s32[8,8]{1,0:T(8,128)S(1)} %bitcast.17, s32[1,8]{1,0:T(1,128)S(1)} %bitcast.23, bf16[16,384,128]{2,1,0:T(8,128)(2,1)S(1)} %turn_rows.1.turned, ...), custom_call_target="tpu_custom_call" | custom-call | flops 1024 | bytes 1024 | tf_op jit(solution)/shard_map/stage_products/pallas_call | solution.py:287
  88.8 6.1 %collective-permute-start.15 = (bf16[5,3,128,128]{3,2,1,0:T(8,128)(2,1)S(1)}, bf16[5,3,128,128]{3,2,1,0:T(8,128)(2,1)S(1)}, u32[]{:S(2)}, u32[]{:S(2)}) collective-permute-start(bf16[5,3,128,128]{3,2,1,0:T(8,128)(2,1)S(1)} %get-tuple-element.34), channel_id=1, source_target_pairs={{0,1},{1,2},{2,3},{4,5},{5,6},{6,7},{8,9},{9,10},{10,11},{12,13},{... | collective-permute-start | bytes 1474568 | tf_op jit(solution)/shard_map/ppermute | solution.py:365
  94.9 1.9 %collective-permute-start.16 = (bf16[5,3,128,128]{3,2,1,0:T(8,128)(2,1)S(1)}, bf16[5,3,128,128]{3,2,1,0:T(8,128)(2,1)S(1)}, u32[]{:S(2)}, u32[]{:S(2)}) collective-permute-start(bf16[5,3,128,128]{3,2,1,0:T(8,128)(2,1)S(1)} %get-tuple-element.35), channel_id=1, source_target_pairs={{1,0},{2,1},{3,2},{5,4},{6,5},{7,6},{9,8},{10,9},{11,10},{13,12},{... | collective-permute-start | bytes 1474568 | tf_op jit(solution)/shard_map/ppermute | solution.py:366
  96.8 1.0 collective-permute-done.19.refs_9_
  97.8 7.9 %collective-permute-done.17.refs_3_.refs_7_ = bf16[2048,128]{1,0:T(8,128)(2,1)S(1)} collective-permute-done((bf16[2048,128]{1,0:T(8,128)(2,1)S(1)}, bf16[2048,128]{1,0:T(8,128)(2,1)S(1)}, u32[]{:S(2)}, u32[]{:S(2)}) %collective-permute-start.17) | collective-permute-done | bytes 524320 | tf_op jit(solution)/shard_map/ppermute | solution.py:356
  105.7 0.0 collective-permute-done.15.refs_11_.refs_1_
  105.7 0.0 collective-permute-done.18.refs_8_
  105.7 3.3 %stage_products.5 = (bf16[3,3,128,128]{3,2,1,0:T(8,128)(2,1)S(1)}, bf16[3,3,128,128]{3,2,1,0:T(8,128)(2,1)S(1)}, bf16[3,3,128,128]{3,2,1,0:T(8,128)(2,1)S(1)}) custom-call(s32[8,8]{1,0:T(8,128)S(1)} %bitcast.21, s32[8,8]{1,0:T(8,128)S(1)} %bitcast.18, s32[1,8]{1,0:T(1,128)S(1)} %bitcast.24, bf16[16,384,128]{2,1,0:T(8,128)(2,1)S(1)} %turn_rows.1.turned, ...), custom_call_target="tpu_custom_call" | custom-call | flops 1024 | bytes 1024 | tf_op jit(solution)/shard_map/stage_products/pallas_call | solution.py:287
  109.0 4.8 %collective-permute-start.20 = (bf16[3,3,128,128]{3,2,1,0:T(8,128)(2,1)S(1)}, bf16[3,3,128,128]{3,2,1,0:T(8,128)(2,1)S(1)}, u32[]{:S(2)}, u32[]{:S(2)}) collective-permute-start(bf16[3,3,128,128]{3,2,1,0:T(8,128)(2,1)S(1)} %get-tuple-element.39), channel_id=1, source_target_pairs={{0,1},{1,2},{2,3},{4,5},{5,6},{6,7},{8,9},{9,10},{10,11},{12,13},{... | collective-permute-start | bytes 884744 | tf_op jit(solution)/shard_map/ppermute | solution.py:365
  113.9 1.9 %collective-permute-start.21 = (bf16[3,3,128,128]{3,2,1,0:T(8,128)(2,1)S(1)}, bf16[3,3,128,128]{3,2,1,0:T(8,128)(2,1)S(1)}, u32[]{:S(2)}, u32[]{:S(2)}) collective-permute-start(bf16[3,3,128,128]{3,2,1,0:T(8,128)(2,1)S(1)} %get-tuple-element.40), channel_id=1, source_target_pairs={{1,0},{2,1},{3,2},{5,4},{6,5},{7,6},{9,8},{10,9},{11,10},{13,12},{... | collective-permute-start | bytes 884744 | tf_op jit(solution)/shard_map/ppermute | solution.py:366
  115.8 0.0 collective-permute-done.16.refs_2_
  115.8 1.7 %collective-permute-done.20.refs_4_ = bf16[3,3,128,128]{3,2,1,0:T(8,128)(2,1)S(1)} collective-permute-done((bf16[3,3,128,128]{3,2,1,0:T(8,128)(2,1)S(1)}, bf16[3,3,128,128]{3,2,1,0:T(8,128)(2,1)S(1)}, u32[]{:S(2)}, u32[]{:S(2)}) %collective-permute-start.20) | collective-permute-done | bytes 294944 | tf_op jit(solution)/shard_map/ppermute | solution.py:365
  117.5 4.4 %collective-permute-done.21.refs_5_ = bf16[3,3,128,128]{3,2,1,0:T(8,128)(2,1)S(1)} collective-permute-done((bf16[3,3,128,128]{3,2,1,0:T(8,128)(2,1)S(1)}, bf16[3,3,128,128]{3,2,1,0:T(8,128)(2,1)S(1)}, u32[]{:S(2)}, u32[]{:S(2)}) %collective-permute-start.21) | collective-permute-done | bytes 294944 | tf_op jit(solution)/shard_map/ppermute | solution.py:366
  121.9 2.5 %assemble_coarse.1 = f32[5120,128]{1,0:T(8,128)} custom-call(bf16[5,3,128,128]{3,2,1,0:T(8,128)(2,1)S(1)} %get-tuple-element.33.refs_0_, bf16[5,3,128,128]{3,2,1,0:T(8,128)(2,1)S(1)} %collective-permute-done.15.refs_11_.refs_1_, bf16[5,3,128,128]{3,2,1,0:T(8,128)(2,1)S(1)} %collective-permute-done.16.refs_2_, ...), custom_call_target="tpu_custom_call" | custom-call | flops 1024 | bytes 1024 | tf_op jit(solution)/shard_map/assemble_coarse/pallas_call | solution.py:332
  (5 shorter events, 0.0 us)
Async XLA Ops:
  0.0 5.6 %copy-start.3 = (s32[1,1,8,8]{3,2,1,0:T(8,128)S(1)}, s32[1,1,8,8]{3,2,1,0:T(8,128)}, u32[]{:S(2)}) copy-start(s32[1,1,8,8]{3,2,1,0:T(8,128)} %param.8) | copy-start | bytes 772
  2.6 25.4 %collective-permute-start.1 = (bf16[4112,128]{1,0:T(8,128)(2,1)}, bf16[4112,128]{1,0:T(8,128)(2,1)S(1)}, u32[]{:S(2)}, u32[]{:S(2)}) collective-permute-start(bf16[4112,128]{1,0:T(8,128)(2,1)} %get-tuple-element.23.head.refs_1_.refs_0_), channel_id=1, source_target_pairs={{0,8},{4,12},{16,24},{20,28},{8,0},{12,4},{24,16},{28,20},{1,9},{5... | collective-permute-start | bytes 3158024 | tf_op jit(solution)/shard_map/ppermute | solution.py:356
  4.8 23.2 %collective-permute-start.5 = (bf16[4112,128]{1,0:T(8,128)(2,1)}, bf16[4112,128]{1,0:T(8,128)(2,1)S(1)}, u32[]{:S(2)}, u32[]{:S(2)}) collective-permute-start(bf16[4112,128]{1,0:T(8,128)(2,1)} %get-tuple-element.23.head.refs_1_.refs_0_), channel_id=1, source_target_pairs={{8,16},{12,20},{16,8},{20,12},{9,17},{13,21},{17,9},{21,13},{10,18... | collective-permute-start | bytes 3158024 | tf_op jit(solution)/shard_map/ppermute | solution.py:356
  5.6 2.8 %collective-permute-start = (s32[8,8]{1,0:T(8,128)S(1)}, s32[8,8]{1,0:T(8,128)S(1)}, u32[]{:S(2)}, u32[]{:S(2)}) collective-permute-start(s32[8,8]{1,0:T(8,128)S(1)} %bitcast.15), channel_id=1, source_target_pairs={{4,0},{0,4},{12,8},{8,12},{20,16},{16,20},{28,24},{24,28},{5,1},{1... | collective-permute-start | bytes 776 | tf_op jit(solution)/shard_map/ppermute | solution.py:356
  8.4 1.2 copy-start.1
  11.3 23.5 %collective-permute-start.3 = (bf16[3072,128]{1,0:T(8,128)(2,1)S(1)}, bf16[3072,128]{1,0:T(8,128)(2,1)S(1)}, u32[]{:S(2)}, u32[]{:S(2)}) collective-permute-start(bf16[3072,128]{1,0:T(8,128)(2,1)S(1)} %pick_rows.7), channel_id=1, source_target_pairs={{0,4},{4,0},{8,12},{12,8},{16,20},{20,16},{24,28},{28,24},{1,5},{5... | collective-permute-start | bytes 2359304 | tf_op jit(solution)/shard_map/ppermute | solution.py:356
  12.6 21.6 %collective-permute-start.2 = (bf16[2048,128]{1,0:T(8,128)(2,1)}, bf16[2048,128]{1,0:T(8,128)(2,1)S(1)}, u32[]{:S(2)}, u32[]{:S(2)}) collective-permute-start(bf16[2048,128]{1,0:T(8,128)(2,1)} %get-tuple-element.24.tail.refs_2_.refs_1_), channel_id=1, source_target_pairs={{1,9},{5,13},{17,25},{21,29},{9,1},{13,5},{25,17},{29,21},{2,10},{... | collective-permute-start | bytes 1572872 | tf_op jit(solution)/shard_map/ppermute | solution.py:356
  18.3 17.2 %collective-permute-start.6 = (bf16[2048,128]{1,0:T(8,128)(2,1)}, bf16[2048,128]{1,0:T(8,128)(2,1)S(1)}, u32[]{:S(2)}, u32[]{:S(2)}) collective-permute-start(bf16[2048,128]{1,0:T(8,128)(2,1)} %get-tuple-element.24.tail.refs_2_.refs_1_), channel_id=1, source_target_pairs={{9,17},{13,21},{17,9},{21,13},{10,18},{14,22},{18,10},{22,14}} | collective-permute-start | bytes 1572872 | tf_op jit(solution)/shard_map/ppermute | solution.py:356
  28.8 15.0 %collective-permute-start.8 = (bf16[2048,128]{1,0:T(8,128)(2,1)S(1)}, bf16[2048,128]{1,0:T(8,128)(2,1)S(1)}, u32[]{:S(2)}, u32[]{:S(2)}) collective-permute-start(bf16[2048,128]{1,0:T(8,128)(2,1)S(1)} %get-tuple-element.26), channel_id=1, source_target_pairs={{8,0},{12,4},{16,24},{20,28},{9,1},{13,5},{17,25},{21,29},{10,2},{... | collective-permute-start | bytes 1572872 | tf_op jit(solution)/shard_map/ppermute | solution.py:356
  30.1 25.3 %collective-permute-start.11 = (bf16[4112,128]{1,0:T(8,128)(2,1)S(1)}, bf16[4112,128]{1,0:T(8,128)(2,1)S(1)}, u32[]{:S(2)}, u32[]{:S(2)}) collective-permute-start(bf16[4112,128]{1,0:T(8,128)(2,1)S(1)} %collective-permute-done.1.refs_1_.refs_2_.refs_5_), channel_id=1, source_target_pairs={{8,16},{12,20},{16,8},{20,12},{9,17},{13,21},{17,9},{21,13},{10,18... | collective-permute-start | bytes 3158024 | tf_op jit(solution)/shard_map/ppermute | solution.py:356
  34.2 1.4 %collective-permute-start.7 = (bf16[16,128]{1,0:T(8,128)(2,1)S(1)}, bf16[16,128]{1,0:T(8,128)(2,1)S(1)}, u32[]{:S(2)}, u32[]{:S(2)}) collective-permute-start(bf16[16,128]{1,0:T(8,128)(2,1)S(1)} %get-tuple-element.25), channel_id=1, source_target_pairs={{12,8},{8,12},{20,16},{16,20},{13,9},{9,13},{21,17},{17,21},{14,10... | collective-permute-start | bytes 12296 | tf_op jit(solution)/shard_map/ppermute | solution.py:356
  44.5 5.0 %copy-start.2 = (bf16[4112,128]{1,0:T(8,128)(2,1)S(1)}, bf16[4112,128]{1,0:T(8,128)(2,1)}, u32[]{:S(2)}) copy-start(bf16[4112,128]{1,0:T(8,128)(2,1)} %get-tuple-element.23.head.refs_1_.refs_0_) | copy-start | bytes 3158020
  44.5 18.7 %collective-permute-start.10 = (bf16[3072,128]{1,0:T(8,128)(2,1)S(1)}, bf16[3072,128]{1,0:T(8,128)(2,1)S(1)}, u32[]{:S(2)}, u32[]{:S(2)}) collective-permute-start(bf16[3072,128]{1,0:T(8,128)(2,1)S(1)} %pick_rows.10.refs_3_), channel_id=1, source_target_pairs={{8,4},{12,0},{16,28},{20,24},{9,5},{13,1},{17,29},{21,25},{10,6},{... | collective-permute-start | bytes 2359304 | tf_op jit(solution)/shard_map/ppermute | solution.py:356
  45.9 37.7 %collective-permute-start.4 = (bf16[3072,128]{1,0:T(8,128)(2,1)S(1)}, bf16[3072,128]{1,0:T(8,128)(2,1)S(1)}, u32[]{:S(2)}, u32[]{:S(2)}) collective-permute-start(bf16[3072,128]{1,0:T(8,128)(2,1)S(1)} %pick_rows.8.refs_3_), channel_id=1, source_target_pairs={{0,4},{4,0},{8,12},{12,8},{16,20},{20,16},{24,28},{28,24},{1,5},{5... | collective-permute-start | bytes 2359304 | tf_op jit(solution)/shard_map/ppermute | solution.py:356
  47.2 10.3 %collective-permute-start.13 = (bf16[2048,128]{1,0:T(8,128)(2,1)S(1)}, bf16[2048,128]{1,0:T(8,128)(2,1)S(1)}, u32[]{:S(2)}, u32[]{:S(2)}) collective-permute-start(bf16[2048,128]{1,0:T(8,128)(2,1)S(1)} %collective-permute-done.2.refs_2_.refs_3_), channel_id=1, source_target_pairs={{9,17},{13,21},{17,9},{21,13},{10,18},{14,22},{18,10},{22,14}} | collective-permute-start | bytes 1572872 | tf_op jit(solution)/shard_map/ppermute | solution.py:356
  48.6 2.4 %copy-start = (bf16[1,1,8,8,128,128]{5,4,3,2,1,0:T(8,128)(2,1)S(1)}, bf16[1,1,8,8,128,128]{5,4,3,2,1,0:T(8,128)(2,1)}, u32[]{:S(2)}) copy-start(bf16[1,1,8,8,128,128]{5,4,3,2,1,0:T(8,128)(2,1)} %param.6) | copy-start | bytes 6291460
  48.6 2.4 %copy-start.4 = (s32[1,1,8,8]{3,2,1,0:T(8,128)S(1)}, s32[1,1,8,8]{3,2,1,0:T(8,128)}, u32[]{:S(2)}) copy-start(s32[1,1,8,8]{3,2,1,0:T(8,128)} %param.7) | copy-start | bytes 772
  48.6 2.4 %copy-start.5 = (s32[1,1,8]{2,1,0:T(1,128)S(1)}, s32[1,1,8]{2,1,0:T(1,128)}, u32[]{:S(2)}) copy-start(s32[1,1,8]{2,1,0:T(1,128)} %param.9) | copy-start | bytes 100
  48.6 36.3 %collective-permute-start.9 = (bf16[3072,128]{1,0:T(8,128)(2,1)S(1)}, bf16[3072,128]{1,0:T(8,128)(2,1)S(1)}, u32[]{:S(2)}, u32[]{:S(2)}) collective-permute-start(bf16[3072,128]{1,0:T(8,128)(2,1)S(1)} %pick_rows.11.refs_4_), channel_id=1, source_target_pairs={{8,12},{12,8},{16,20},{20,16},{9,13},{13,9},{17,21},{21,17},{10,14... | collective-permute-start | bytes 2359304 | tf_op jit(solution)/shard_map/ppermute | solution.py:356
  56.3 30.0 %collective-permute-start.12 = (bf16[2048,128]{1,0:T(8,128)(2,1)S(1)}, bf16[2048,128]{1,0:T(8,128)(2,1)S(1)}, u32[]{:S(2)}, u32[]{:S(2)}) collective-permute-start(bf16[2048,128]{1,0:T(8,128)(2,1)S(1)} %get-tuple-element.30.refs_7_), channel_id=1, source_target_pairs={{8,0},{12,4},{16,24},{20,28},{9,1},{13,5},{17,25},{21,29},{10,2},{... | collective-permute-start | bytes 1572872 | tf_op jit(solution)/shard_map/ppermute | solution.py:356
  64.7 41.0 %collective-permute-start.18 = (bf16[3072,128]{1,0:T(8,128)(2,1)S(1)}, bf16[3072,128]{1,0:T(8,128)(2,1)S(1)}, u32[]{:S(2)}, u32[]{:S(2)}) collective-permute-start(bf16[3072,128]{1,0:T(8,128)(2,1)S(1)} %get-tuple-element.37), channel_id=1, source_target_pairs={{8,12},{12,8},{16,20},{20,16},{9,13},{13,9},{17,21},{21,17},{10,14... | collective-permute-start | bytes 2359304 | tf_op jit(solution)/shard_map/ppermute | solution.py:356
  65.5 20.8 %collective-permute-start.14 = (bf16[1024,128]{1,0:T(8,128)(2,1)S(1)}, bf16[1024,128]{1,0:T(8,128)(2,1)S(1)}, u32[]{:S(2)}, u32[]{:S(2)}) collective-permute-start(bf16[1024,128]{1,0:T(8,128)(2,1)S(1)} %get-tuple-element.32), channel_id=1, source_target_pairs={{9,5},{13,1},{17,29},{21,25},{10,6},{14,2},{18,30},{22,26}} | collective-permute-start | bytes 786440 | tf_op jit(solution)/shard_map/ppermute | solution.py:356
  83.6 14.2 %collective-permute-start.19 = (bf16[2048,128]{1,0:T(8,128)(2,1)S(1)}, bf16[2048,128]{1,0:T(8,128)(2,1)S(1)}, u32[]{:S(2)}, u32[]{:S(2)}) collective-permute-start(bf16[2048,128]{1,0:T(8,128)(2,1)S(1)} %get-tuple-element.31.refs_8_), channel_id=1, source_target_pairs={{8,4},{12,0},{16,28},{20,24},{9,5},{13,1},{17,29},{21,25},{10,6},{... | collective-permute-start | bytes 1572872 | tf_op jit(solution)/shard_map/ppermute | solution.py:356
  84.9 20.8 %collective-permute-start.17 = (bf16[2048,128]{1,0:T(8,128)(2,1)S(1)}, bf16[2048,128]{1,0:T(8,128)(2,1)S(1)}, u32[]{:S(2)}, u32[]{:S(2)}) collective-permute-start(bf16[2048,128]{1,0:T(8,128)(2,1)S(1)} %get-tuple-element.36), channel_id=1, source_target_pairs={{9,1},{13,5},{17,25},{21,29},{10,2},{14,6},{18,26},{22,30}} | collective-permute-start | bytes 1572872 | tf_op jit(solution)/shard_map/ppermute | solution.py:356
  88.8 17.0 %collective-permute-start.15 = (bf16[5,3,128,128]{3,2,1,0:T(8,128)(2,1)S(1)}, bf16[5,3,128,128]{3,2,1,0:T(8,128)(2,1)S(1)}, u32[]{:S(2)}, u32[]{:S(2)}) collective-permute-start(bf16[5,3,128,128]{3,2,1,0:T(8,128)(2,1)S(1)} %get-tuple-element.34), channel_id=1, source_target_pairs={{0,1},{1,2},{2,3},{4,5},{5,6},{6,7},{8,9},{9,10},{10,11},{12,13},{... | collective-permute-start | bytes 1474568 | tf_op jit(solution)/shard_map/ppermute | solution.py:365
  94.9 20.9 %collective-permute-start.16 = (bf16[5,3,128,128]{3,2,1,0:T(8,128)(2,1)S(1)}, bf16[5,3,128,128]{3,2,1,0:T(8,128)(2,1)S(1)}, u32[]{:S(2)}, u32[]{:S(2)}) collective-permute-start(bf16[5,3,128,128]{3,2,1,0:T(8,128)(2,1)S(1)} %get-tuple-element.35), channel_id=1, source_target_pairs={{1,0},{2,1},{3,2},{5,4},{6,5},{7,6},{9,8},{10,9},{11,10},{13,12},{... | collective-permute-start | bytes 1474568 | tf_op jit(solution)/shard_map/ppermute | solution.py:366
  109.0 8.5 %collective-permute-start.20 = (bf16[3,3,128,128]{3,2,1,0:T(8,128)(2,1)S(1)}, bf16[3,3,128,128]{3,2,1,0:T(8,128)(2,1)S(1)}, u32[]{:S(2)}, u32[]{:S(2)}) collective-permute-start(bf16[3,3,128,128]{3,2,1,0:T(8,128)(2,1)S(1)} %get-tuple-element.39), channel_id=1, source_target_pairs={{0,1},{1,2},{2,3},{4,5},{5,6},{6,7},{8,9},{9,10},{10,11},{12,13},{... | collective-permute-start | bytes 884744 | tf_op jit(solution)/shard_map/ppermute | solution.py:365
  113.9 8.0 %collective-permute-start.21 = (bf16[3,3,128,128]{3,2,1,0:T(8,128)(2,1)S(1)}, bf16[3,3,128,128]{3,2,1,0:T(8,128)(2,1)S(1)}, u32[]{:S(2)}, u32[]{:S(2)}) collective-permute-start(bf16[3,3,128,128]{3,2,1,0:T(8,128)(2,1)S(1)} %get-tuple-element.40), channel_id=1, source_target_pairs={{1,0},{2,1},{3,2},{5,4},{6,5},{7,6},{9,8},{10,9},{11,10},{13,12},{... | collective-permute-start | bytes 884744 | tf_op jit(solution)/shard_map/ppermute | solution.py:366

commit v21 on v19

--- a/solution.py
+++ b/solution.py
@@ -327,7 +327,7 @@
 def assemble(grid, plans, pieces):
     panels = grid.panels
     width = pieces[0][0].shape[-1]
-    rows = width // 4
+    rows = width // 8
     flat = [x for piece in pieces for x in piece]
     result = pl.pallas_call(
         functools.partial(assemble_kernel, grid, plans),

time: 118 us -> 119 us (level)
  no operation moved by 1% of the time
where the time goes in v21:
time: 119 us
  waiting for transfers between devices  52 us (44%)
  starting transfers between devices  40.3 us (34%)
  Pallas kernels  24.8 us (21%)
  local copies, waits for them, and re-layouts  1.26 us (1%)
    ppermute x18, waiting for transfers between devices, move(): return lax.ppermute(x, ('blk', 'rows'), perm) if perm else jnp.zeros_like(x)  45.4 us
    ppermute x18, starting transfers between devices, move(): return lax.ppermute(x, ('blk', 'rows'), perm) if perm else jnp.zeros_like(x)  24.9 us
    ppermute x2, starting transfers between devices, exchange(): lax.ppermute(parts[1], 'rows', [(g, g + 1) for g in range(groups - 1)])  11.6 us
    pallas_call x3, Pallas kernels, stage(): pl.pallas_call(functools.partial(stage_kernel, grid, plan, layout, carrie...  10.1 us
    pallas_call x7, Pallas kernels, pick(): pl.pallas_call(functools.partial(pick_kernel, grid, plan, layout, carry,...  6.93 us
    ppermute x2, waiting for transfers between devices, exchange(): lax.ppermute(parts[2], 'rows', [(g + 1, g) for g in range(groups - 1)])  4.4 us
    ppermute x2, starting transfers between devices, exchange(): lax.ppermute(parts[2], 'rows', [(g + 1, g) for g in range(groups - 1)])  3.84 us
    pallas_call x1, Pallas kernels, assemble(): pl.pallas_call(functools.partial(assemble_kernel, grid, plans), grid=(wid...  3.64 us
  transfers between devices with their start and end apart: 22, of which 10 were waited for; matrix products, arithmetic and copies ran while one was open for 0% of the time, Pallas kernels for 16%

profile of v21, /device:TPU:1, one launch (start us, length us, event | category | flops | bytes accessed | tf_op | source)
XLA Modules:
  0.0 118.8 jit_solution(6028032222168639226)
XLA Ops:
  0.0 2.6 %pack_rows.1 = (bf16[4112,128]{1,0:T(8,128)(2,1)}, bf16[2048,128]{1,0:T(8,128)(2,1)}) custom-call(s32[3,1,16]{2,1,0:T(1,128)} %bitcast.26, s32[8,8]{1,0:T(8,128)} %bitcast.14, bf16[16,128,384]{2,1,0:T(8,128)(2,1)} %bitcast.25), custom_call_target="tpu_custom_call" | custom-call | flops 1024 | bytes 1024 | tf_op jit(solution)/shard_map/pack_rows/pallas_call | solution.py:130
  2.6 2.2 %collective-permute-start.1 = (bf16[4112,128]{1,0:T(8,128)(2,1)}, bf16[4112,128]{1,0:T(8,128)(2,1)S(1)}, u32[]{:S(2)}, u32[]{:S(2)}) collective-permute-start(bf16[4112,128]{1,0:T(8,128)(2,1)} %get-tuple-element.23.head.refs_1_.refs_0_), channel_id=1, source_target_pairs={{0,8},{4,12},{16,24},{20,28},{8,0},{12,4},{24,16},{28,20},{1,9},{5... | collective-permute-start | bytes 3158024 | tf_op jit(solution)/shard_map/ppermute | solution.py:356
  4.8 0.7 collective-permute-start.5
  5.6 0.0 copy-done.3
  5.6 1.3 %collective-permute-start = (s32[8,8]{1,0:T(8,128)S(1)}, s32[8,8]{1,0:T(8,128)S(1)}, u32[]{:S(2)}, u32[]{:S(2)}) collective-permute-start(s32[8,8]{1,0:T(8,128)S(1)} %bitcast.15), channel_id=1, source_target_pairs={{4,0},{0,4},{12,8},{8,12},{20,16},{16,20},{28,24},{24,28},{5,1},{1... | collective-permute-start | bytes 776 | tf_op jit(solution)/shard_map/ppermute | solution.py:356
  6.9 1.5 %collective-permute-done.refs_0_ = s32[8,8]{1,0:T(8,128)S(1)} collective-permute-done((s32[8,8]{1,0:T(8,128)S(1)}, s32[8,8]{1,0:T(8,128)S(1)}, u32[]{:S(2)}, u32[]{:S(2)}) %collective-permute-start) | collective-permute-done | bytes 288 | tf_op jit(solution)/shard_map/ppermute | solution.py:356
  8.4 1.2 %copy-done.1 = bf16[4112,128]{1,0:T(8,128)(2,1)S(1)} copy-done((bf16[4112,128]{1,0:T(8,128)(2,1)S(1)}, bf16[4112,128]{1,0:T(8,128)(2,1)}, u32[]{:S(2)}) %copy-start.1) | copy-done | bytes 1052696
  9.6 1.7 %pick_rows.7 = bf16[3072,128]{1,0:T(8,128)(2,1)S(1)} custom-call(s32[8,8]{1,0:T(8,128)S(1)} %collective-permute-done.refs_0_, bf16[4112,128]{1,0:T(8,128)(2,1)S(1)} %copy-done.1, bf16[2048,128]{1,0:T(8,128)(2,1)} %get-tuple-element.24.tail.refs_2_.refs_1_), custom_call_target="tpu_custom_call" | custom-call | flops 1024 | bytes 1024 | tf_op jit(solution)/shard_map/pick_rows/pallas_call | solution.py:222
  11.3 1.3 %collective-permute-start.3 = (bf16[3072,128]{1,0:T(8,128)(2,1)S(1)}, bf16[3072,128]{1,0:T(8,128)(2,1)S(1)}, u32[]{:S(2)}, u32[]{:S(2)}) collective-permute-start(bf16[3072,128]{1,0:T(8,128)(2,1)S(1)} %pick_rows.7), channel_id=1, source_target_pairs={{0,4},{4,0},{8,12},{12,8},{16,20},{20,16},{24,28},{28,24},{1,5},{5... | collective-permute-start | bytes 2359304 | tf_op jit(solution)/shard_map/ppermute | solution.py:356
  12.6 5.7 %collective-permute-start.2 = (bf16[2048,128]{1,0:T(8,128)(2,1)}, bf16[2048,128]{1,0:T(8,128)(2,1)S(1)}, u32[]{:S(2)}, u32[]{:S(2)}) collective-permute-start(bf16[2048,128]{1,0:T(8,128)(2,1)} %get-tuple-element.24.tail.refs_2_.refs_1_), channel_id=1, source_target_pairs={{1,9},{5,13},{17,25},{21,29},{9,1},{13,5},{25,17},{29,21},{2,10},{... | collective-permute-start | bytes 1572872 | tf_op jit(solution)/shard_map/ppermute | solution.py:356
  18.3 0.7 collective-permute-start.6
  19.0 9.0 %collective-permute-done.1.refs_1_.refs_2_.refs_5_ = bf16[4112,128]{1,0:T(8,128)(2,1)S(1)} collective-permute-done((bf16[4112,128]{1,0:T(8,128)(2,1)}, bf16[4112,128]{1,0:T(8,128)(2,1)S(1)}, u32[]{:S(2)}, u32[]{:S(2)}) %collective-permute-start.1) | collective-permute-done | bytes 1052704 | tf_op jit(solution)/shard_map/ppermute | solution.py:356
  28.0 0.0 collective-permute-done.5.refs_0_.refs_1_
  28.0 0.7 pick_rows.9
  28.8 1.3 %collective-permute-start.8 = (bf16[2048,128]{1,0:T(8,128)(2,1)S(1)}, bf16[2048,128]{1,0:T(8,128)(2,1)S(1)}, u32[]{:S(2)}, u32[]{:S(2)}) collective-permute-start(bf16[2048,128]{1,0:T(8,128)(2,1)S(1)} %get-tuple-element.26), channel_id=1, source_target_pairs={{8,0},{12,4},{16,24},{20,28},{9,1},{13,5},{17,25},{21,29},{10,2},{... | collective-permute-start | bytes 1572872 | tf_op jit(solution)/shard_map/ppermute | solution.py:356
  30.1 0.7 collective-permute-start.11
  30.8 3.4 %collective-permute-done.2.refs_2_.refs_3_ = bf16[2048,128]{1,0:T(8,128)(2,1)S(1)} collective-permute-done((bf16[2048,128]{1,0:T(8,128)(2,1)}, bf16[2048,128]{1,0:T(8,128)(2,1)S(1)}, u32[]{:S(2)}, u32[]{:S(2)}) %collective-permute-start.2) | collective-permute-done | bytes 524320 | tf_op jit(solution)/shard_map/ppermute | solution.py:356
  34.2 0.7 collective-permute-start.7
  34.8 0.0 collective-permute-done.3.refs_3_.refs_4_
  34.8 0.7 pick_rows.8.refs_3_
  35.5 1.5 %collective-permute-start.4 = (bf16[3072,128]{1,0:T(8,128)(2,1)S(1)}, bf16[3072,128]{1,0:T(8,128)(2,1)S(1)}, u32[]{:S(2)}, u32[]{:S(2)}) collective-permute-start(bf16[3072,128]{1,0:T(8,128)(2,1)S(1)} %pick_rows.8.refs_3_), channel_id=1, source_target_pairs={{0,4},{4,0},{8,12},{12,8},{16,20},{20,16},{24,28},{28,24},{1,5},{5... | collective-permute-start | bytes 2359304 | tf_op jit(solution)/shard_map/ppermute | solution.py:356
  37.0 0.0 collective-permute-done.6.refs_1_.refs_2_.refs_3_
  37.0 0.0 collective-permute-done.7.refs_2_.refs_6_
  37.0 6.7 %collective-permute-done.8.refs_4_.refs_9_.refs_2_ = bf16[2048,128]{1,0:T(8,128)(2,1)S(1)} collective-permute-done((bf16[2048,128]{1,0:T(8,128)(2,1)S(1)}, bf16[2048,128]{1,0:T(8,128)(2,1)S(1)}, u32[]{:S(2)}, u32[]{:S(2)}) %collective-permute-start.8) | collective-permute-done | bytes 524320 | tf_op jit(solution)/shard_map/ppermute | solution.py:356
  43.7 0.7 pick_rows.10.refs_3_
  44.5 0.0 copy-start.2
  44.5 1.4 %collective-permute-start.10 = (bf16[3072,128]{1,0:T(8,128)(2,1)S(1)}, bf16[3072,128]{1,0:T(8,128)(2,1)S(1)}, u32[]{:S(2)}, u32[]{:S(2)}) collective-permute-start(bf16[3072,128]{1,0:T(8,128)(2,1)S(1)} %pick_rows.10.refs_3_), channel_id=1, source_target_pairs={{8,4},{12,0},{16,28},{20,24},{9,5},{13,1},{17,29},{21,25},{10,6},{... | collective-permute-start | bytes 2359304 | tf_op jit(solution)/shard_map/ppermute | solution.py:356
  45.9 0.7 collective-permute-start.13
  46.6 0.7 pick_rows.11.refs_4_
  47.3 0.0 copy-start
  47.3 0.0 copy-start.4
  47.3 0.0 copy-start.5
  47.3 0.8 collective-permute-start.9
  48.2 0.0 copy-done.2
  48.2 1.5 %turn_rows.1.turned = bf16[16,384,128]{2,1,0:T(8,128)(2,1)S(1)} custom-call(bf16[4112,128]{1,0:T(8,128)(2,1)S(1)} %copy-done.2, bf16[2048,128]{1,0:T(8,128)(2,1)} %get-tuple-element.24.tail.refs_2_.refs_1_), custom_call_target="tpu_custom_call" | custom-call | flops 1024 | bytes 1024 | tf_op jit(solution)/shard_map/turn_rows/pallas_call | solution.py:159
  49.7 4.3 %stage_products.3 = (bf16[3,3,128,128]{3,2,1,0:T(8,128)(2,1)S(1)}, bf16[3,3,128,128]{3,2,1,0:T(8,128)(2,1)S(1)}, bf16[3,3,128,128]{3,2,1,0:T(8,128)(2,1)S(1)}) custom-call(s32[8,8]{1,0:T(8,128)S(1)} %bitcast.19, s32[8,8]{1,0:T(8,128)S(1)} %bitcast.16, s32[1,8]{1,0:T(1,128)S(1)} %bitcast.22, bf16[16,384,128]{2,1,0:T(8,128)(2,1)S(1)} %turn_rows.1.turned, ...), custom_call_target="tpu_custom_call" | custom-call | flops 1024 | bytes 1024 | tf_op jit(solution)/shard_map/stage_products/pallas_call | solution.py:287
  54.1 0.0 collective-permute-done.11.refs_0_.refs_1_.refs_4_
  54.1 0.9 pick_rows.12
  55.0 1.3 %collective-permute-start.12 = (bf16[2048,128]{1,0:T(8,128)(2,1)S(1)}, bf16[2048,128]{1,0:T(8,128)(2,1)S(1)}, u32[]{:S(2)}, u32[]{:S(2)}) collective-permute-start(bf16[2048,128]{1,0:T(8,128)(2,1)S(1)} %get-tuple-element.30.refs_7_), channel_id=1, source_target_pairs={{8,0},{12,4},{16,24},{20,28},{9,1},{13,5},{17,25},{21,29},{10,2},{... | collective-permute-start | bytes 1572872 | tf_op jit(solution)/shard_map/ppermute | solution.py:356
  56.3 0.0 collective-permute-done.13.refs_2_.refs_4_.refs_5_
  56.3 14.9 %collective-permute-done.4.refs_11_.refs_0_ = bf16[3072,128]{1,0:T(8,128)(2,1)S(1)} collective-permute-done((bf16[3072,128]{1,0:T(8,128)(2,1)S(1)}, bf16[3072,128]{1,0:T(8,128)(2,1)S(1)}, u32[]{:S(2)}, u32[]{:S(2)}) %collective-permute-start.4) | collective-permute-done | bytes 786464 | tf_op jit(solution)/shard_map/ppermute | solution.py:356
  71.2 0.0 collective-permute-done.10.refs_10_.refs_2_
  71.2 1.5 %pick_rows.13 = (bf16[3072,128]{1,0:T(8,128)(2,1)S(1)}, bf16[2048,128]{1,0:T(8,128)(2,1)S(1)}, bf16[1024,128]{1,0:T(8,128)(2,1)S(1)}) custom-call(s32[8,8]{1,0:T(8,128)S(1)} %collective-permute-done.refs_0_, bf16[4112,128]{1,0:T(8,128)(2,1)S(1)} %collective-permute-done.11.refs_0_.refs_1_.refs_4_, ...), custom_call_target="tpu_custom_call" | custom-call | flops 1024 | bytes 1024 | tf_op jit(solution)/shard_map/pick_rows/pallas_call | solution.py:222
  72.7 0.7 collective-permute-start.18
  73.4 1.3 %collective-permute-start.14 = (bf16[1024,128]{1,0:T(8,128)(2,1)S(1)}, bf16[1024,128]{1,0:T(8,128)(2,1)S(1)}, u32[]{:S(2)}, u32[]{:S(2)}) collective-permute-start(bf16[1024,128]{1,0:T(8,128)(2,1)S(1)} %get-tuple-element.32), channel_id=1, source_target_pairs={{9,5},{13,1},{17,29},{21,25},{10,6},{14,2},{18,30},{22,26}} | collective-permute-start | bytes 786440 | tf_op jit(solution)/shard_map/ppermute | solution.py:356
  74.7 1.3 %collective-permute-start.19 = (bf16[2048,128]{1,0:T(8,128)(2,1)S(1)}, bf16[2048,128]{1,0:T(8,128)(2,1)S(1)}, u32[]{:S(2)}, u32[]{:S(2)}) collective-permute-start(bf16[2048,128]{1,0:T(8,128)(2,1)S(1)} %get-tuple-element.31.refs_8_), channel_id=1, source_target_pairs={{8,4},{12,0},{16,28},{20,24},{9,5},{13,1},{17,29},{21,25},{10,6},{... | collective-permute-start | bytes 1572872 | tf_op jit(solution)/shard_map/ppermute | solution.py:356
  76.0 0.0 collective-permute-done.9.refs_1_
  76.0 1.3 %collective-permute-start.17 = (bf16[2048,128]{1,0:T(8,128)(2,1)S(1)}, bf16[2048,128]{1,0:T(8,128)(2,1)S(1)}, u32[]{:S(2)}, u32[]{:S(2)}) collective-permute-start(bf16[2048,128]{1,0:T(8,128)(2,1)S(1)} %get-tuple-element.36), channel_id=1, source_target_pairs={{9,1},{13,5},{17,25},{21,29},{10,2},{14,6},{18,26},{22,30}} | collective-permute-start | bytes 1572872 | tf_op jit(solution)/shard_map/ppermute | solution.py:356
  77.3 6.5 %collective-permute-done.14.refs_7_.refs_10_ = bf16[1024,128]{1,0:T(8,128)(2,1)S(1)} collective-permute-done((bf16[1024,128]{1,0:T(8,128)(2,1)S(1)}, bf16[1024,128]{1,0:T(8,128)(2,1)S(1)}, u32[]{:S(2)}, u32[]{:S(2)}) %collective-permute-start.14) | collective-permute-done | bytes 262176 | tf_op jit(solution)/shard_map/ppermute | solution.py:356
  83.9 0.0 collective-permute-done.12.refs_6_
  83.9 2.5 %stage_products.4 = (bf16[5,3,128,128]{3,2,1,0:T(8,128)(2,1)S(1)}, bf16[5,3,128,128]{3,2,1,0:T(8,128)(2,1)S(1)}, bf16[5,3,128,128]{3,2,1,0:T(8,128)(2,1)S(1)}) custom-call(s32[8,8]{1,0:T(8,128)S(1)} %bitcast.20, s32[8,8]{1,0:T(8,128)S(1)} %bitcast.17, s32[1,8]{1,0:T(1,128)S(1)} %bitcast.23, bf16[16,384,128]{2,1,0:T(8,128)(2,1)S(1)} %turn_rows.1.turned, ...), custom_call_target="tpu_custom_call" | custom-call | flops 1024 | bytes 1024 | tf_op jit(solution)/shard_map/stage_products/pallas_call | solution.py:287
  86.4 7.2 %collective-permute-start.15 = (bf16[5,3,128,128]{3,2,1,0:T(8,128)(2,1)S(1)}, bf16[5,3,128,128]{3,2,1,0:T(8,128)(2,1)S(1)}, u32[]{:S(2)}, u32[]{:S(2)}) collective-permute-start(bf16[5,3,128,128]{3,2,1,0:T(8,128)(2,1)S(1)} %get-tuple-element.34), channel_id=1, source_target_pairs={{0,1},{1,2},{2,3},{4,5},{5,6},{6,7},{8,9},{9,10},{10,11},{12,13},{... | collective-permute-start | bytes 1474568 | tf_op jit(solution)/shard_map/ppermute | solution.py:365
  93.6 1.9 %collective-permute-start.16 = (bf16[5,3,128,128]{3,2,1,0:T(8,128)(2,1)S(1)}, bf16[5,3,128,128]{3,2,1,0:T(8,128)(2,1)S(1)}, u32[]{:S(2)}, u32[]{:S(2)}) collective-permute-start(bf16[5,3,128,128]{3,2,1,0:T(8,128)(2,1)S(1)} %get-tuple-element.35), channel_id=1, source_target_pairs={{1,0},{2,1},{3,2},{5,4},{6,5},{7,6},{9,8},{10,9},{11,10},{13,12},{... | collective-permute-start | bytes 1474568 | tf_op jit(solution)/shard_map/ppermute | solution.py:366
  95.6 0.0 collective-permute-done.19.refs_9_
  95.6 3.3 %collective-permute-done.17.refs_3_.refs_7_ = bf16[2048,128]{1,0:T(8,128)(2,1)S(1)} collective-permute-done((bf16[2048,128]{1,0:T(8,128)(2,1)S(1)}, bf16[2048,128]{1,0:T(8,128)(2,1)S(1)}, u32[]{:S(2)}, u32[]{:S(2)}) %collective-permute-start.17) | collective-permute-done | bytes 524320 | tf_op jit(solution)/shard_map/ppermute | solution.py:356
  98.8 0.5 collective-permute-done.15.refs_11_.refs_1_
  99.4 0.0 collective-permute-done.18.refs_8_
  99.4 3.3 %stage_products.5 = (bf16[3,3,128,128]{3,2,1,0:T(8,128)(2,1)S(1)}, bf16[3,3,128,128]{3,2,1,0:T(8,128)(2,1)S(1)}, bf16[3,3,128,128]{3,2,1,0:T(8,128)(2,1)S(1)}) custom-call(s32[8,8]{1,0:T(8,128)S(1)} %bitcast.21, s32[8,8]{1,0:T(8,128)S(1)} %bitcast.18, s32[1,8]{1,0:T(1,128)S(1)} %bitcast.24, bf16[16,384,128]{2,1,0:T(8,128)(2,1)S(1)} %turn_rows.1.turned, ...), custom_call_target="tpu_custom_call" | custom-call | flops 1024 | bytes 1024 | tf_op jit(solution)/shard_map/stage_products/pallas_call | solution.py:287
  102.7 4.4 %collective-permute-start.20 = (bf16[3,3,128,128]{3,2,1,0:T(8,128)(2,1)S(1)}, bf16[3,3,128,128]{3,2,1,0:T(8,128)(2,1)S(1)}, u32[]{:S(2)}, u32[]{:S(2)}) collective-permute-start(bf16[3,3,128,128]{3,2,1,0:T(8,128)(2,1)S(1)} %get-tuple-element.39), channel_id=1, source_target_pairs={{0,1},{1,2},{2,3},{4,5},{5,6},{6,7},{8,9},{9,10},{10,11},{12,13},{... | collective-permute-start | bytes 884744 | tf_op jit(solution)/shard_map/ppermute | solution.py:365
  107.1 1.9 %collective-permute-start.21 = (bf16[3,3,128,128]{3,2,1,0:T(8,128)(2,1)S(1)}, bf16[3,3,128,128]{3,2,1,0:T(8,128)(2,1)S(1)}, u32[]{:S(2)}, u32[]{:S(2)}) collective-permute-start(bf16[3,3,128,128]{3,2,1,0:T(8,128)(2,1)S(1)} %get-tuple-element.40), channel_id=1, source_target_pairs={{1,0},{2,1},{3,2},{5,4},{6,5},{7,6},{9,8},{10,9},{11,10},{13,12},{... | collective-permute-start | bytes 884744 | tf_op jit(solution)/shard_map/ppermute | solution.py:366
  109.0 0.0 collective-permute-done.16.refs_2_
  109.0 1.7 %collective-permute-done.20.refs_4_ = bf16[3,3,128,128]{3,2,1,0:T(8,128)(2,1)S(1)} collective-permute-done((bf16[3,3,128,128]{3,2,1,0:T(8,128)(2,1)S(1)}, bf16[3,3,128,128]{3,2,1,0:T(8,128)(2,1)S(1)}, u32[]{:S(2)}, u32[]{:S(2)}) %collective-permute-start.20) | collective-permute-done | bytes 294944 | tf_op jit(solution)/shard_map/ppermute | solution.py:365
  110.7 4.4 %collective-permute-done.21.refs_5_ = bf16[3,3,128,128]{3,2,1,0:T(8,128)(2,1)S(1)} collective-permute-done((bf16[3,3,128,128]{3,2,1,0:T(8,128)(2,1)S(1)}, bf16[3,3,128,128]{3,2,1,0:T(8,128)(2,1)S(1)}, u32[]{:S(2)}, u32[]{:S(2)}) %collective-permute-start.21) | collective-permute-done | bytes 294944 | tf_op jit(solution)/shard_map/ppermute | solution.py:366
  115.1 3.6 %assemble_coarse.1 = f32[5120,128]{1,0:T(8,128)} custom-call(bf16[5,3,128,128]{3,2,1,0:T(8,128)(2,1)S(1)} %get-tuple-element.33.refs_0_, bf16[5,3,128,128]{3,2,1,0:T(8,128)(2,1)S(1)} %collective-permute-done.15.refs_11_.refs_1_, bf16[5,3,128,128]{3,2,1,0:T(8,128)(2,1)S(1)} %collective-permute-done.16.refs_2_, ...), custom_call_target="tpu_custom_call" | custom-call | flops 1024 | bytes 1024 | tf_op jit(solution)/shard_map/assemble_coarse/pallas_call | solution.py:332
  (5 shorter events, 0.0 us)
Async XLA Ops:
  0.0 5.6 %copy-start.3 = (s32[1,1,8,8]{3,2,1,0:T(8,128)S(1)}, s32[1,1,8,8]{3,2,1,0:T(8,128)}, u32[]{:S(2)}) copy-start(s32[1,1,8,8]{3,2,1,0:T(8,128)} %param.8) | copy-start | bytes 772
  2.6 25.4 %collective-permute-start.1 = (bf16[4112,128]{1,0:T(8,128)(2,1)}, bf16[4112,128]{1,0:T(8,128)(2,1)S(1)}, u32[]{:S(2)}, u32[]{:S(2)}) collective-permute-start(bf16[4112,128]{1,0:T(8,128)(2,1)} %get-tuple-element.23.head.refs_1_.refs_0_), channel_id=1, source_target_pairs={{0,8},{4,12},{16,24},{20,28},{8,0},{12,4},{24,16},{28,20},{1,9},{5... | collective-permute-start | bytes 3158024 | tf_op jit(solution)/shard_map/ppermute | solution.py:356
  4.8 23.2 %collective-permute-start.5 = (bf16[4112,128]{1,0:T(8,128)(2,1)}, bf16[4112,128]{1,0:T(8,128)(2,1)S(1)}, u32[]{:S(2)}, u32[]{:S(2)}) collective-permute-start(bf16[4112,128]{1,0:T(8,128)(2,1)} %get-tuple-element.23.head.refs_1_.refs_0_), channel_id=1, source_target_pairs={{8,16},{12,20},{16,8},{20,12},{9,17},{13,21},{17,9},{21,13},{10,18... | collective-permute-start | bytes 3158024 | tf_op jit(solution)/shard_map/ppermute | solution.py:356
  5.6 2.8 %collective-permute-start = (s32[8,8]{1,0:T(8,128)S(1)}, s32[8,8]{1,0:T(8,128)S(1)}, u32[]{:S(2)}, u32[]{:S(2)}) collective-permute-start(s32[8,8]{1,0:T(8,128)S(1)} %bitcast.15), channel_id=1, source_target_pairs={{4,0},{0,4},{12,8},{8,12},{20,16},{16,20},{28,24},{24,28},{5,1},{1... | collective-permute-start | bytes 776 | tf_op jit(solution)/shard_map/ppermute | solution.py:356
  8.4 1.2 %copy-start.1 = (bf16[4112,128]{1,0:T(8,128)(2,1)S(1)}, bf16[4112,128]{1,0:T(8,128)(2,1)}, u32[]{:S(2)}) copy-start(bf16[4112,128]{1,0:T(8,128)(2,1)} %get-tuple-element.23.head.refs_1_.refs_0_) | copy-start | bytes 3158020
  11.3 23.5 %collective-permute-start.3 = (bf16[3072,128]{1,0:T(8,128)(2,1)S(1)}, bf16[3072,128]{1,0:T(8,128)(2,1)S(1)}, u32[]{:S(2)}, u32[]{:S(2)}) collective-permute-start(bf16[3072,128]{1,0:T(8,128)(2,1)S(1)} %pick_rows.7), channel_id=1, source_target_pairs={{0,4},{4,0},{8,12},{12,8},{16,20},{20,16},{24,28},{28,24},{1,5},{5... | collective-permute-start | bytes 2359304 | tf_op jit(solution)/shard_map/ppermute | solution.py:356
  12.6 21.6 %collective-permute-start.2 = (bf16[2048,128]{1,0:T(8,128)(2,1)}, bf16[2048,128]{1,0:T(8,128)(2,1)S(1)}, u32[]{:S(2)}, u32[]{:S(2)}) collective-permute-start(bf16[2048,128]{1,0:T(8,128)(2,1)} %get-tuple-element.24.tail.refs_2_.refs_1_), channel_id=1, source_target_pairs={{1,9},{5,13},{17,25},{21,29},{9,1},{13,5},{25,17},{29,21},{2,10},{... | collective-permute-start | bytes 1572872 | tf_op jit(solution)/shard_map/ppermute | solution.py:356
  18.3 18.7 %collective-permute-start.6 = (bf16[2048,128]{1,0:T(8,128)(2,1)}, bf16[2048,128]{1,0:T(8,128)(2,1)S(1)}, u32[]{:S(2)}, u32[]{:S(2)}) collective-permute-start(bf16[2048,128]{1,0:T(8,128)(2,1)} %get-tuple-element.24.tail.refs_2_.refs_1_), channel_id=1, source_target_pairs={{9,17},{13,21},{17,9},{21,13},{10,18},{14,22},{18,10},{22,14}} | collective-permute-start | bytes 1572872 | tf_op jit(solution)/shard_map/ppermute | solution.py:356
  28.8 15.0 %collective-permute-start.8 = (bf16[2048,128]{1,0:T(8,128)(2,1)S(1)}, bf16[2048,128]{1,0:T(8,128)(2,1)S(1)}, u32[]{:S(2)}, u32[]{:S(2)}) collective-permute-start(bf16[2048,128]{1,0:T(8,128)(2,1)S(1)} %get-tuple-element.26), channel_id=1, source_target_pairs={{8,0},{12,4},{16,24},{20,28},{9,1},{13,5},{17,25},{21,29},{10,2},{... | collective-permute-start | bytes 1572872 | tf_op jit(solution)/shard_map/ppermute | solution.py:356
  30.1 24.0 %collective-permute-start.11 = (bf16[4112,128]{1,0:T(8,128)(2,1)S(1)}, bf16[4112,128]{1,0:T(8,128)(2,1)S(1)}, u32[]{:S(2)}, u32[]{:S(2)}) collective-permute-start(bf16[4112,128]{1,0:T(8,128)(2,1)S(1)} %collective-permute-done.1.refs_1_.refs_2_.refs_5_), channel_id=1, source_target_pairs={{8,16},{12,20},{16,8},{20,12},{9,17},{13,21},{17,9},{21,13},{10,18... | collective-permute-start | bytes 3158024 | tf_op jit(solution)/shard_map/ppermute | solution.py:356
  34.2 2.8 %collective-permute-start.7 = (bf16[16,128]{1,0:T(8,128)(2,1)S(1)}, bf16[16,128]{1,0:T(8,128)(2,1)S(1)}, u32[]{:S(2)}, u32[]{:S(2)}) collective-permute-start(bf16[16,128]{1,0:T(8,128)(2,1)S(1)} %get-tuple-element.25), channel_id=1, source_target_pairs={{12,8},{8,12},{20,16},{16,20},{13,9},{9,13},{21,17},{17,21},{14,10... | collective-permute-start | bytes 12296 | tf_op jit(solution)/shard_map/ppermute | solution.py:356
  35.5 35.6 %collective-permute-start.4 = (bf16[3072,128]{1,0:T(8,128)(2,1)S(1)}, bf16[3072,128]{1,0:T(8,128)(2,1)S(1)}, u32[]{:S(2)}, u32[]{:S(2)}) collective-permute-start(bf16[3072,128]{1,0:T(8,128)(2,1)S(1)} %pick_rows.8.refs_3_), channel_id=1, source_target_pairs={{0,4},{4,0},{8,12},{12,8},{16,20},{20,16},{24,28},{28,24},{1,5},{5... | collective-permute-start | bytes 2359304 | tf_op jit(solution)/shard_map/ppermute | solution.py:356
  44.5 3.7 %copy-start.2 = (bf16[4112,128]{1,0:T(8,128)(2,1)S(1)}, bf16[4112,128]{1,0:T(8,128)(2,1)}, u32[]{:S(2)}) copy-start(bf16[4112,128]{1,0:T(8,128)(2,1)} %get-tuple-element.23.head.refs_1_.refs_0_) | copy-start | bytes 3158020
  44.5 26.7 %collective-permute-start.10 = (bf16[3072,128]{1,0:T(8,128)(2,1)S(1)}, bf16[3072,128]{1,0:T(8,128)(2,1)S(1)}, u32[]{:S(2)}, u32[]{:S(2)}) collective-permute-start(bf16[3072,128]{1,0:T(8,128)(2,1)S(1)} %pick_rows.10.refs_3_), channel_id=1, source_target_pairs={{8,4},{12,0},{16,28},{20,24},{9,5},{13,1},{17,29},{21,25},{10,6},{... | collective-permute-start | bytes 2359304 | tf_op jit(solution)/shard_map/ppermute | solution.py:356
  45.9 10.4 %collective-permute-start.13 = (bf16[2048,128]{1,0:T(8,128)(2,1)S(1)}, bf16[2048,128]{1,0:T(8,128)(2,1)S(1)}, u32[]{:S(2)}, u32[]{:S(2)}) collective-permute-start(bf16[2048,128]{1,0:T(8,128)(2,1)S(1)} %collective-permute-done.2.refs_2_.refs_3_), channel_id=1, source_target_pairs={{9,17},{13,21},{17,9},{21,13},{10,18},{14,22},{18,10},{22,14}} | collective-permute-start | bytes 1572872 | tf_op jit(solution)/shard_map/ppermute | solution.py:356
  47.3 2.4 %copy-start = (bf16[1,1,8,8,128,128]{5,4,3,2,1,0:T(8,128)(2,1)S(1)}, bf16[1,1,8,8,128,128]{5,4,3,2,1,0:T(8,128)(2,1)}, u32[]{:S(2)}) copy-start(bf16[1,1,8,8,128,128]{5,4,3,2,1,0:T(8,128)(2,1)} %param.6) | copy-start | bytes 6291460
  47.3 2.4 %copy-start.4 = (s32[1,1,8,8]{3,2,1,0:T(8,128)S(1)}, s32[1,1,8,8]{3,2,1,0:T(8,128)}, u32[]{:S(2)}) copy-start(s32[1,1,8,8]{3,2,1,0:T(8,128)} %param.7) | copy-start | bytes 772
  47.3 2.4 %copy-start.5 = (s32[1,1,8]{2,1,0:T(1,128)S(1)}, s32[1,1,8]{2,1,0:T(1,128)}, u32[]{:S(2)}) copy-start(s32[1,1,8]{2,1,0:T(1,128)} %param.9) | copy-start | bytes 100
  47.3 28.7 %collective-permute-start.9 = (bf16[3072,128]{1,0:T(8,128)(2,1)S(1)}, bf16[3072,128]{1,0:T(8,128)(2,1)S(1)}, u32[]{:S(2)}, u32[]{:S(2)}) collective-permute-start(bf16[3072,128]{1,0:T(8,128)(2,1)S(1)} %pick_rows.11.refs_4_), channel_id=1, source_target_pairs={{8,12},{12,8},{16,20},{20,16},{9,13},{13,9},{17,21},{21,17},{10,14... | collective-permute-start | bytes 2359304 | tf_op jit(solution)/shard_map/ppermute | solution.py:356
  55.0 28.9 %collective-permute-start.12 = (bf16[2048,128]{1,0:T(8,128)(2,1)S(1)}, bf16[2048,128]{1,0:T(8,128)(2,1)S(1)}, u32[]{:S(2)}, u32[]{:S(2)}) collective-permute-start(bf16[2048,128]{1,0:T(8,128)(2,1)S(1)} %get-tuple-element.30.refs_7_), channel_id=1, source_target_pairs={{8,0},{12,4},{16,24},{20,28},{9,1},{13,5},{17,25},{21,29},{10,2},{... | collective-permute-start | bytes 1572872 | tf_op jit(solution)/shard_map/ppermute | solution.py:356
  72.7 26.7 %collective-permute-start.18 = (bf16[3072,128]{1,0:T(8,128)(2,1)S(1)}, bf16[3072,128]{1,0:T(8,128)(2,1)S(1)}, u32[]{:S(2)}, u32[]{:S(2)}) collective-permute-start(bf16[3072,128]{1,0:T(8,128)(2,1)S(1)} %get-tuple-element.37), channel_id=1, source_target_pairs={{8,12},{12,8},{16,20},{20,16},{9,13},{13,9},{17,21},{21,17},{10,14... | collective-permute-start | bytes 2359304 | tf_op jit(solution)/shard_map/ppermute | solution.py:356
  73.4 10.4 %collective-permute-start.14 = (bf16[1024,128]{1,0:T(8,128)(2,1)S(1)}, bf16[1024,128]{1,0:T(8,128)(2,1)S(1)}, u32[]{:S(2)}, u32[]{:S(2)}) collective-permute-start(bf16[1024,128]{1,0:T(8,128)(2,1)S(1)} %get-tuple-element.32), channel_id=1, source_target_pairs={{9,5},{13,1},{17,29},{21,25},{10,6},{14,2},{18,30},{22,26}} | collective-permute-start | bytes 786440 | tf_op jit(solution)/shard_map/ppermute | solution.py:356
  74.7 20.8 %collective-permute-start.19 = (bf16[2048,128]{1,0:T(8,128)(2,1)S(1)}, bf16[2048,128]{1,0:T(8,128)(2,1)S(1)}, u32[]{:S(2)}, u32[]{:S(2)}) collective-permute-start(bf16[2048,128]{1,0:T(8,128)(2,1)S(1)} %get-tuple-element.31.refs_8_), channel_id=1, source_target_pairs={{8,4},{12,0},{16,28},{20,24},{9,5},{13,1},{17,29},{21,25},{10,6},{... | collective-permute-start | bytes 1572872 | tf_op jit(solution)/shard_map/ppermute | solution.py:356
  76.0 22.8 %collective-permute-start.17 = (bf16[2048,128]{1,0:T(8,128)(2,1)S(1)}, bf16[2048,128]{1,0:T(8,128)(2,1)S(1)}, u32[]{:S(2)}, u32[]{:S(2)}) collective-permute-start(bf16[2048,128]{1,0:T(8,128)(2,1)S(1)} %get-tuple-element.36), channel_id=1, source_target_pairs={{9,1},{13,5},{17,25},{21,29},{10,2},{14,6},{18,26},{22,30}} | collective-permute-start | bytes 1572872 | tf_op jit(solution)/shard_map/ppermute | solution.py:356
  86.4 13.0 %collective-permute-start.15 = (bf16[5,3,128,128]{3,2,1,0:T(8,128)(2,1)S(1)}, bf16[5,3,128,128]{3,2,1,0:T(8,128)(2,1)S(1)}, u32[]{:S(2)}, u32[]{:S(2)}) collective-permute-start(bf16[5,3,128,128]{3,2,1,0:T(8,128)(2,1)S(1)} %get-tuple-element.34), channel_id=1, source_target_pairs={{0,1},{1,2},{2,3},{4,5},{5,6},{6,7},{8,9},{9,10},{10,11},{12,13},{... | collective-permute-start | bytes 1474568 | tf_op jit(solution)/shard_map/ppermute | solution.py:365
  93.6 15.4 %collective-permute-start.16 = (bf16[5,3,128,128]{3,2,1,0:T(8,128)(2,1)S(1)}, bf16[5,3,128,128]{3,2,1,0:T(8,128)(2,1)S(1)}, u32[]{:S(2)}, u32[]{:S(2)}) collective-permute-start(bf16[5,3,128,128]{3,2,1,0:T(8,128)(2,1)S(1)} %get-tuple-element.35), channel_id=1, source_target_pairs={{1,0},{2,1},{3,2},{5,4},{6,5},{7,6},{9,8},{10,9},{11,10},{13,12},{... | collective-permute-start | bytes 1474568 | tf_op jit(solution)/shard_map/ppermute | solution.py:366
  102.7 8.0 %collective-permute-start.20 = (bf16[3,3,128,128]{3,2,1,0:T(8,128)(2,1)S(1)}, bf16[3,3,128,128]{3,2,1,0:T(8,128)(2,1)S(1)}, u32[]{:S(2)}, u32[]{:S(2)}) collective-permute-start(bf16[3,3,128,128]{3,2,1,0:T(8,128)(2,1)S(1)} %get-tuple-element.39), channel_id=1, source_target_pairs={{0,1},{1,2},{2,3},{4,5},{5,6},{6,7},{8,9},{9,10},{10,11},{12,13},{... | collective-permute-start | bytes 884744 | tf_op jit(solution)/shard_map/ppermute | solution.py:365
  107.1 8.0 %collective-permute-start.21 = (bf16[3,3,128,128]{3,2,1,0:T(8,128)(2,1)S(1)}, bf16[3,3,128,128]{3,2,1,0:T(8,128)(2,1)S(1)}, u32[]{:S(2)}, u32[]{:S(2)}) collective-permute-start(bf16[3,3,128,128]{3,2,1,0:T(8,128)(2,1)S(1)} %get-tuple-element.40), channel_id=1, source_target_pairs={{1,0},{2,1},{3,2},{5,4},{6,5},{7,6},{9,8},{10,9},{11,10},{13,12},{... | collective-permute-start | bytes 884744 | tf_op jit(solution)/shard_map/ppermute | solution.py:366
